TPU v7x, 32 devices: a whole 2x2x4 slice. The times are simulated.
32 devices in a mesh: groups: 2 (over x), dom: 2 (over core), seq: 8 (over z, y).
Axes of the slice: x: 2, y: 2, z: 4, core: 2. Of those that a mesh axis runs over, the one named last changes fastest.
Arguments:
- latents: bfloat16 [16, 512, 1536], P(('groups', 'dom'), 'seq'), parts along dimension 0, may hold values from -6 to 6
- queries: bfloat16 [16, 512, 1536], P(('groups', 'dom'), 'seq'), parts along dimension 0, may hold values from -64 to 64
- keys: bfloat16 [16, 512, 1536], P(('groups', 'dom'), 'seq'), parts along dimension 0, may hold values from -64 to 64
- values: bfloat16 [16, 512, 1536], P(('groups', 'dom'), 'seq'), parts along dimension 0, may hold values from -6 to 6
- out_weight: bfloat16 [1536, 1536], replicated, may hold values from -0.15625 to 0.15625
- step_index: int32 [2], P('groups'), parts along dimension 0, may hold values from 1 to 27
- embed_weight: bfloat16 [1536, 1024], P('seq'), may hold values from -0.15625 to 0.15625
- norm_gain: float32 [1024], replicated, may hold values from 0.1 to 1.9
- up_weight: bfloat16 [1024, 4096], P(None, 'seq'), may hold values from -0.1875 to 0.1875
- head_weight: float32 [4096], replicated, may hold values from -0.09375 to 0.09375
- prev_logw: float32 [16], P(('groups', 'dom')), parts along dimension 0, may hold values from -20 to 320
- ancestors: int32 [16], P(('groups', 'dom')), parts along dimension 0, may hold values from 0 to 7
Outputs:
- resampled: bfloat16 [16, 512, 1536], P(('groups', 'dom'), 'seq'), parts along dimension 0
- log_weights: float32 [16], P(('groups', 'dom')), parts along dimension 0
There are 2 independent parts, one for each index of `groups`. A program takes and returns all parts, laid end to end along the dimension named above; an argument that names none is the same for every part. Nothing has to cross between parts.
Inputs may be any that keep to these rules, and one draw needn't show every extreme that they name: `ancestors`: index of a particle of the same group.
All inputs are finite; a program needn't handle non-finite values.
Results may differ from a plain program's by a relative error of at most 0.0014.
Values may be sent and summed in bfloat16 or wider, within the bound.
No kernel may reach another device: no remote copies, remote signals or barrier semaphores. Data moves between devices by JAX's collectives and lax.ppermute only.
A program may use at most 128 MiB of HBM per device.

v0:
```python
import math

import jax
import jax.numpy as jnp
from jax import lax
from jax.sharding import PartitionSpec as P

HEADS = 24
STEPS = 28


potential_scale = 4.0
norm_eps = 1e-05


def attend(query_rows, key_rows, value_rows):
    item_count, total_tokens, head_width = query_rows.shape
    block_rows = min(512, total_tokens)
    block_count = total_tokens // block_rows
    score_scale = 1.0 / math.sqrt(head_width)

    def one_block(block_index):
        block_queries = lax.dynamic_slice_in_dim(
            query_rows, block_index * block_rows, block_rows, 1
        )
        scores = (
            jnp.einsum("iqd,ikd->iqk", block_queries, key_rows, preferred_element_type=jnp.float32)
            * score_scale
        )
        highest = jnp.max(scores, axis=-1, keepdims=True)
        expanded = jnp.exp(scores - highest)
        soft_weights = (expanded / jnp.sum(expanded, axis=-1, keepdims=True)).astype(jnp.bfloat16)
        return jnp.einsum(
            "iqk,ikd->iqd", soft_weights, value_rows, preferred_element_type=jnp.float32
        ).astype(jnp.bfloat16)

    blocks = lax.map(one_block, jnp.arange(block_count))
    return jnp.moveaxis(blocks, 0, 1).reshape(item_count, total_tokens, head_width)


def head_attention(triple):
    query_items, key_items, value_items = triple
    return attend(query_items[0], key_items[0], value_items[0])[None]


def on_device(
    latents,
    queries,
    keys,
    values,
    out_weight,
    step_index,
    embed_weight,
    norm_gain,
    up_weight,
    head_weight,
    prev_logw,
    ancestors,
):
    seq_count = lax.axis_size("seq")
    local_particles, local_tokens, model_width = latents.shape
    head_width = model_width // HEADS
    per_device = local_particles * HEADS // seq_count
    local_rows = local_particles * local_tokens
    total_tokens = local_tokens * seq_count

    def to_items(array):
        split_heads = array.reshape(local_particles, local_tokens, HEADS, head_width).transpose(
            0, 2, 1, 3
        )
        return split_heads.reshape(seq_count, per_device, local_tokens, head_width)

    attended_items = head_attention(
        (
            lax.all_to_all(to_items(queries), "seq", split_axis=0, concat_axis=2, tiled=True),
            lax.all_to_all(to_items(keys), "seq", split_axis=0, concat_axis=2, tiled=True),
            lax.all_to_all(to_items(values), "seq", split_axis=0, concat_axis=2, tiled=True),
        )
    )
    returned = lax.all_to_all(attended_items, "seq", split_axis=2, concat_axis=0, tiled=True)
    attended = (
        returned.reshape(local_particles, HEADS, local_tokens, head_width)
        .transpose(0, 2, 1, 3)
        .reshape(local_rows, model_width)
    )
    flat = latents.reshape(local_rows, model_width).astype(jnp.float32)
    velocity = flat + jnp.dot(attended, out_weight, preferred_element_type=jnp.float32)
    sigma = step_index[0].astype(jnp.float32) / STEPS
    clean = (flat - sigma * velocity).astype(jnp.bfloat16)
    stepped = (flat - velocity / STEPS).astype(jnp.bfloat16)
    embedded = jnp.dot(
        clean,
        lax.all_gather(embed_weight, "seq", axis=0, tiled=True),
        preferred_element_type=jnp.float32,
    )
    centre = jnp.mean(embedded, axis=1, keepdims=True)
    centered = embedded - centre
    variance = jnp.mean(centered * centered, axis=1, keepdims=True)
    features = jax.nn.gelu(centered * lax.rsqrt(variance + norm_eps) * norm_gain[None, :]).astype(
        jnp.bfloat16
    )
    scored = (
        jax.nn.gelu(
            jnp.dot(
                features,
                lax.all_gather(up_weight, "seq", axis=1, tiled=True),
                preferred_element_type=jnp.float32,
            )
        )
        * head_weight[None, :]
    )
    partial_value = jnp.sum(jnp.sum(scored, axis=1).reshape(local_particles, local_tokens), axis=1)
    partial_value = partial_value / math.sqrt(total_tokens)
    reward = lax.psum(partial_value, "seq")
    local_logits = prev_logw + potential_scale * reward
    all_logits = lax.all_gather(local_logits, "dom", axis=0, tiled=True)
    highest = jnp.max(all_logits)
    log_total = highest + jnp.log(jnp.sum(jnp.exp(all_logits - highest)))
    log_weights = local_logits - log_total
    candidates = lax.all_gather(
        stepped.reshape(local_particles, local_tokens, model_width), "dom", axis=0, tiled=True
    )
    resampled = jnp.take(candidates, ancestors, axis=0)
    return (resampled, log_weights)


def solution(mesh):
    in_specs = (
        P(("groups", "dom"), "seq", None),
        P(("groups", "dom"), "seq", None),
        P(("groups", "dom"), "seq", None),
        P(("groups", "dom"), "seq", None),
        P(),
        P("groups"),
        P("seq", None),
        P(),
        P(None, "seq"),
        P(),
        P(("groups", "dom")),
        P(("groups", "dom")),
    )
    out_specs = (P(("groups", "dom"), "seq", None), P(("groups", "dom")))
    return jax.shard_map(
        on_device, mesh=mesh, in_specs=in_specs, out_specs=out_specs, check_vma=False
    )
```

profile of v0, /device:TPU:0, one launch (start us, length us, event | category | flops | bytes accessed | tf_op | source)
XLA Modules:
  0.0 303.3 jit_solution(8375197817523683279)
XLA Ops:
  8.6 2.4 reshape.69
  11.5 1.9 reshape.90
  13.4 7.3 %all-to-all-start.2 = ((bf16[8,2,24576]{2,1,0:T(2,128)(2,1)}), bf16[8,2,24576]{2,1,0:T(2,128)(2,1)}, u32[]{:S(2)}, u32[]{:S(2)}) async-start(bf16[8,2,24576]{2,1,0:T(2,128)(2,1)} %reshape.90), calls=%async_computation.2 | async-start | bytes 1572864 | tf_op jit(solution)/shard_map/all_to_all | solution.py:77
  20.6 2.4 reshape.65
  23.5 1.9 reshape.92
  25.4 28.2 %all-to-all-done.2 = bf16[8,2,24576]{2,1,0:T(2,128)(2,1)} async-done(((bf16[8,2,24576]{2,1,0:T(2,128)(2,1)}), bf16[8,2,24576]{2,1,0:T(2,128)(2,1)}, u32[]{:S(2)}, u32[]{:S(2)}) %all-to-all-start.2) | async-done | bytes 786464 | tf_op jit(solution)/shard_map/all_to_all | solution.py:77
  53.5 4.2 %all-to-all-start = ((bf16[8,2,24576]{2,1,0:T(2,128)(2,1)}), bf16[8,2,24576]{2,1,0:T(2,128)(2,1)}, u32[]{:S(2)}, u32[]{:S(2)}) async-start(bf16[8,2,24576]{2,1,0:T(2,128)(2,1)} %reshape.92), calls=%async_computation | async-start | bytes 1572864 | tf_op jit(solution)/shard_map/all_to_all | solution.py:75
  57.8 2.4 reshape.67
  60.6 1.9 reshape.94
  62.5 36.3 %all-to-all-done = bf16[8,2,24576]{2,1,0:T(2,128)(2,1)} async-done(((bf16[8,2,24576]{2,1,0:T(2,128)(2,1)}), bf16[8,2,24576]{2,1,0:T(2,128)(2,1)}, u32[]{:S(2)}, u32[]{:S(2)}) %all-to-all-start) | async-done | bytes 786464 | tf_op jit(solution)/shard_map/all_to_all | solution.py:75
  98.8 4.4 %all-to-all-start.1 = ((bf16[8,2,24576]{2,1,0:T(2,128)(2,1)}), bf16[8,2,24576]{2,1,0:T(2,128)(2,1)}, u32[]{:S(2)}, u32[]{:S(2)}) async-start(bf16[8,2,24576]{2,1,0:T(2,128)(2,1)} %reshape.94), calls=%async_computation.1 | async-start | bytes 1572864 | tf_op jit(solution)/shard_map/all_to_all | solution.py:76
  103.2 2.2 reshape.91
  108.1 2.2 reshape.93
  113.0 26.0 %all-to-all-done.1 = bf16[8,2,24576]{2,1,0:T(2,128)(2,1)} async-done(((bf16[8,2,24576]{2,1,0:T(2,128)(2,1)}), bf16[8,2,24576]{2,1,0:T(2,128)(2,1)}, u32[]{:S(2)}, u32[]{:S(2)}) %all-to-all-start.1) | async-done | bytes 786464 | tf_op jit(solution)/shard_map/all_to_all | solution.py:76
  139.0 2.2 reshape.95
  143.2 9.9 %fusion.49 = (f32[12,512]{1,0:T(8,128)S(1)}, f32[12,512,512]{1,2,0:T(8,128)}) fusion(bf16[12,512,64]{1,2,0:T(8,128)(2,1)} %squeeze.13, bf16[12,512,64]{1,2,0:T(8,128)(2,1)S(1)} %squeeze.14), kind=kOutput, calls=%fused_computation.62 | convolution fusion | flops 412090880 | bytes 14180352 | tf_op jit(solution)/shard_map/while/body/eval_jaxpr/sub | solution.py:31
  153.1 5.8 %fusion.20 = bf16[1,12,512,64]{2,3,1,0:T(8,128)(2,1)S(1)} fusion(bf16[12,512,64]{1,2,0:T(8,128)(2,1)S(1)} %copy-done, f32[12,512,512]{1,2,0:T(8,128)} %get-tuple-element.13, f32[12,512]{1,0:T(8,128)S(1)} %get-tuple-element.12), kind=kOutput, calls=%fused_computation.26 | convolution fusion | flops 409337856 | bytes 14180352 | tf_op jit(solution)/shard_map/while/body/eval_jaxpr/iqk,ikd->iqd/dot_general | solution.py:33
  159.0 2.0 copy.57
  161.0 2.0 reshape.96
  162.9 3.6 %all-to-all-start.3 = ((bf16[8,2,24576]{2,1,0:T(2,128)(2,1)}), bf16[8,2,24576]{2,1,0:T(2,128)(2,1)S(1)}, u32[]{:S(2)}, u32[]{:S(2)}) async-start(bf16[8,2,24576]{2,1,0:T(2,128)(2,1)} %reshape.96), calls=%async_computation.3 | async-start | bytes 1572864 | tf_op jit(solution)/shard_map/all_to_all | solution.py:80
  168.7 47.5 %all-to-all-done.3 = bf16[8,2,24576]{2,1,0:T(2,128)(2,1)S(1)} async-done(((bf16[8,2,24576]{2,1,0:T(2,128)(2,1)}), bf16[8,2,24576]{2,1,0:T(2,128)(2,1)S(1)}, u32[]{:S(2)}, u32[]{:S(2)}) %all-to-all-start.3) | async-done | bytes 786464 | tf_op jit(solution)/shard_map/all_to_all | solution.py:80
  217.4 2.9 copy.62
  220.3 2.2 copy.59
  223.6 1.7 reshape.72
  225.3 5.5 %fusion.15 = (bf16[256,1536]{1,0:T(8,128)(2,1)}, f32[256,1536]{1,0:T(8,128)S(1)}) fusion(bf16[4,64,1536]{2,1,0:T(8,128)(2,1)} %param.12, bf16[256,1536]{1,0:T(8,128)(2,1)} %reshape.72, bf16[1536,1536]{1,0:T(8,128)(2,1)} %param.16, bf16[256,1536]{1,0:T(8,128)(2,1)} %bitcast.67), kind=kOutput, calls=%fused_computation.21 | convolution fusion | flops 1210318848 | bytes 9437184 | tf_op jit(solution)/shard_map/dot_general | solution.py:87
  230.8 3.0 fusion.50
  234.1 20.3 %all-gather.8.cloned.1.call-done = bf16[1024,4096]{1,0:T(8,128)(2,1)} async-done(((bf16[1024,512]{1,0:T(8,128)(2,1)}), bf16[1024,4096]{1,0:T(8,128)(2,1)}) %all-gather.8.cloned.1.call-update) | async-done | bytes 8388624 | tf_op jit(solution)/shard_map/all_gather | solution.py:106
  254.4 7.1 %fusion.14 = f32[256]{0:T(256)S(1)} fusion(f32[4096]{0:T(1024)S(1)} %copy-done.3, bf16[1024,4096]{1,0:T(8,128)(2,1)} %all-gather.8.cloned.1.call-done, f32[256,1024]{1,0:T(8,128)S(1)} %get-tuple-element.22, f32[1024]{0:T(1024)S(1)} %copy-done.4, f32[256]{0:T(256)S(1)} %add_rsqrt_fusion, f32[256]{0:T(256)S(1)} %broadcast_multiply_fusion), kind=kOutput, calls=%fused_computation.17 | convolution fusion | flops 2161114880 | bytes 9460736 | tf_op jit(solution)/shard_map/dot_general | solution.py:104
  261.7 4.3 %all-gather.4.cloned.1.call-done = bf16[8,64,1536]{2,1,0:T(8,128)(2,1)} async-done(((bf16[4,64,1536]{2,1,0:T(8,128)(2,1)}), bf16[8,64,1536]{2,1,0:T(8,128)(2,1)}) %all-gather.4.cloned.1.call-update) | async-done | bytes 1572880 | tf_op jit(solution)/shard_map/all_gather | solution.py:120
  265.9 2.0 gather_fusion
  268.0 21.5 %psum.7 = f32[4]{0:T(128)S(1)} all-reduce(f32[4]{0:T(128)S(1)} %broadcast_multiply_fusion.1), channel_id=1, replica_groups=mesh['groups'=2,'dom'=2,'seq'=8] {'seq'}, use_global_device_ids=true, to_apply=%region_6.7 | all-reduce | flops 4 | bytes 32 | tf_op jit(solution)/shard_map/psum | solution.py:114
  290.5 2.4 all-reduce
  (48 shorter events, 17.3 us)
Async XLA Ops:
  7.2 223.7 %all-gather.6.cloned.1.call-start = ((), (), s32[]{:S(2)}) async-start(), calls=%async_computation.5 | async-start | bytes 3538944 | tf_op jit(solution)/shard_map/all_gather | solution.py:93
  7.9 246.5 %all-gather.8.cloned.1.call-start = ((), (), s32[]{:S(2)}) async-start(), calls=%async_computation.6 | async-start | bytes 9437184 | tf_op jit(solution)/shard_map/all_gather | solution.py:106
  13.4 40.2 %all-to-all-start.2 = ((bf16[8,2,24576]{2,1,0:T(2,128)(2,1)}), bf16[8,2,24576]{2,1,0:T(2,128)(2,1)}, u32[]{:S(2)}, u32[]{:S(2)}) async-start(bf16[8,2,24576]{2,1,0:T(2,128)(2,1)} %reshape.90), calls=%async_computation.2 | async-start | bytes 1572864 | tf_op jit(solution)/shard_map/all_to_all | solution.py:77
  53.5 45.3 %all-to-all-start = ((bf16[8,2,24576]{2,1,0:T(2,128)(2,1)}), bf16[8,2,24576]{2,1,0:T(2,128)(2,1)}, u32[]{:S(2)}, u32[]{:S(2)}) async-start(bf16[8,2,24576]{2,1,0:T(2,128)(2,1)} %reshape.92), calls=%async_computation | async-start | bytes 1572864 | tf_op jit(solution)/shard_map/all_to_all | solution.py:75
  98.8 40.2 %all-to-all-start.1 = ((bf16[8,2,24576]{2,1,0:T(2,128)(2,1)}), bf16[8,2,24576]{2,1,0:T(2,128)(2,1)}, u32[]{:S(2)}, u32[]{:S(2)}) async-start(bf16[8,2,24576]{2,1,0:T(2,128)(2,1)} %reshape.94), calls=%async_computation.1 | async-start | bytes 1572864 | tf_op jit(solution)/shard_map/all_to_all | solution.py:76
  143.2 9.9 %copy-start = (bf16[12,512,64]{1,2,0:T(8,128)(2,1)S(1)}, bf16[12,512,64]{1,2,0:T(8,128)(2,1)}, u32[]{:S(2)}) copy-start(bf16[12,512,64]{1,2,0:T(8,128)(2,1)} %squeeze.15) | copy-start | bytes 2359300
  158.9 8.5 %copy-start.6 = (u32[32]{0:T(128)S(1)}, u32[32]{0:T(128)}, u32[]{:S(2)}) copy-start(u32[32]{0:T(128)} %constant.73) | copy-start | bytes 388
  159.0 9.7 %copy-start.5 = (s32[4]{0:T(128)S(1)}, s32[4]{0:T(128)}, u32[]{:S(2)}) copy-start(s32[4]{0:T(128)} %param.23) | copy-start | bytes 52
  162.9 53.2 %all-to-all-start.3 = ((bf16[8,2,24576]{2,1,0:T(2,128)(2,1)}), bf16[8,2,24576]{2,1,0:T(2,128)(2,1)S(1)}, u32[]{:S(2)}, u32[]{:S(2)}) async-start(bf16[8,2,24576]{2,1,0:T(2,128)(2,1)} %reshape.96), calls=%async_computation.3 | async-start | bytes 1572864 | tf_op jit(solution)/shard_map/all_to_all | solution.py:80
  166.5 99.4 %all-gather.4.cloned.1.call-start = ((), (), s32[]{:S(2)}) async-start(), calls=%async_computation.4 | async-start | bytes 2359296 | tf_op jit(solution)/shard_map/all_gather | solution.py:120
  225.3 5.5 %copy-start.1 = (bf16[4,64,1536]{2,1,0:T(8,128)(2,1)S(1)}, bf16[4,64,1536]{2,1,0:T(8,128)(2,1)}, u32[]{:S(2)}) copy-start(bf16[4,64,1536]{2,1,0:T(8,128)(2,1)} %param.12) | copy-start | bytes 2359300
  230.8 23.6 %copy-start.3 = (f32[4096]{0:T(1024)S(1)}, f32[4096]{0:T(1024)}, u32[]{:S(2)}) copy-start(f32[4096]{0:T(1024)} %param.21) | copy-start | bytes 49156
  230.8 23.6 %copy-start.4 = (f32[1024]{0:T(1024)S(1)}, f32[1024]{0:T(1024)}, u32[]{:S(2)}) copy-start(f32[1024]{0:T(1024)} %param.19) | copy-start | bytes 12292
  234.1 55.3 %copy-start.2 = (f32[4]{0:T(128)S(1)}, f32[4]{0:T(128)}, u32[]{:S(2)}) copy-start(f32[4]{0:T(128)} %param.22) | copy-start | bytes 52
Sparse Core Ops, SparseCore 0:
  10.2 91.5 all-gather.5
  103.9 150.4 all-gather.7
  255.9 9.9 all-gather.3
where the time goes:
time: 304 us; the launch traced here: 303 us
  waiting for transfers between devices  164 us (54%)
  local copies, waits for them, and re-layouts  43.8 us (14%)
  matrix products  31.3 us (10%)
  blocking collectives  23.9 us (8%)
  starting transfers between devices  19.8 us (7%)
  between operations  16.7 us (5%)
  other arithmetic  3.98 us (1%)
    all_to_all x1, waiting for transfers between devices, on_device(): lax.all_to_all(attended_items, 'seq', split_axis=2, concat_axis=0, tiled=...  47.5 us
    all_to_all x1, waiting for transfers between devices, on_device(): lax.all_to_all(to_items(queries), 'seq', split_axis=0, concat_axis=2, til...  36.3 us
    all_to_all x1, waiting for transfers between devices, on_device(): lax.all_to_all(to_items(values), 'seq', split_axis=0, concat_axis=2, tile...  28.2 us
    all_to_all x1, waiting for transfers between devices, on_device(): lax.all_to_all(to_items(keys), 'seq', split_axis=0, concat_axis=2, tiled=...  26 us
    psum x1, blocking collectives, on_device(): reward = lax.psum(partial_value, 'seq')  21.5 us
    all_gather x1, waiting for transfers between devices, on_device(): lax.all_gather(up_weight, 'seq', axis=1, tiled=True)  20.3 us
    unnamed x24, local copies, waits for them, and re-layouts  16.1 us
    sub x1, matrix products, one_block(): expanded = jnp.exp(scores - highest)  9.91 us
  transfers between devices with their start and end apart: 7, of which 6 were waited for; matrix products, arithmetic and copies ran while one was open for 24% of the time, Pallas kernels for 0%

commit v1 on v0

v1 whole, which is shorter than its diff:
```python
import functools
import math

import jax
import jax.numpy as jnp
from jax import lax
from jax.experimental import pallas as pl
from jax.experimental.pallas import tpu as pltpu
from jax.sharding import PartitionSpec as P

HEADS = 24
STEPS = 28
LANES = 128

potential_scale = 4.0
norm_eps = 1e-05
MIB = 1024 * 1024


def pack_kernel(chunks, width, q_ref, k_ref, v_ref, *out_refs):
    blocks = q_ref.shape[2] // width
    part = width // chunks
    for index, ref in enumerate((q_ref, k_ref, v_ref)):
        for block in range(blocks):
            for chunk in range(chunks):
                start = block * width + chunk * part
                out_refs[chunk][block, index] = ref[0, :, start : start + part]


def pack(queries, keys, values, chunks, width):
    particles, tokens, model_width = queries.shape
    blocks = model_width // width
    part = width // chunks
    in_spec = pl.BlockSpec((1, tokens, model_width), lambda i: (i, 0, 0))
    out_spec = pl.BlockSpec((blocks, 3, tokens, part), lambda i: (i, 0, 0, 0))
    out_shape = jax.ShapeDtypeStruct((particles * blocks, 3, tokens, part), queries.dtype)
    return pl.pallas_call(
        functools.partial(pack_kernel, chunks, width),
        grid=(particles,),
        in_specs=[in_spec] * 3,
        out_specs=[out_spec] * chunks,
        out_shape=[out_shape] * chunks,
        name="pack_heads",
    )(queries, keys, values)


def attention_kernel(head_width, block_sources, qkv_ref, out_ref):
    sources, _, tokens, columns = qkv_ref.shape
    total = sources * tokens
    rows = block_sources * tokens
    factor = 1.0 / math.sqrt(head_width) / math.log(2.0)

    def one_block(block, carry):
        span = pl.ds(block * block_sources, block_sources)
        q_all = qkv_ref[span, 0].reshape(rows, columns)
        pieces = []
        for head in range(columns // head_width):
            cols = slice(head * head_width, (head + 1) * head_width)
            k_head = qkv_ref[:, 1, :, cols].reshape(total, head_width)
            v_head = qkv_ref[:, 2, :, cols].reshape(total, head_width)
            scores = lax.dot_general(
                q_all[:, cols], k_head, (((1,), (1,)), ((), ())), preferred_element_type=jnp.float32
            )
            highest = jnp.max(scores, axis=1, keepdims=True)
            expanded = jnp.exp2((scores - highest) * factor)
            norm = 1.0 / jnp.sum(expanded, axis=1, keepdims=True)
            weights = (expanded * norm).astype(jnp.bfloat16)
            pieces.append(jnp.dot(weights, v_head, preferred_element_type=jnp.float32))
        joined = jnp.concatenate(pieces, axis=1).astype(jnp.bfloat16)
        out_ref[span] = joined.reshape(block_sources, tokens, columns)
        return carry

    lax.fori_loop(0, sources // block_sources, one_block, 0)


def attention(qkv, head_width):
    sources, _, tokens, columns = qkv.shape
    total = sources * tokens
    block_sources = max(1, min(sources, 512 // tokens))
    while sources % block_sources:
        block_sources -= 1
    heads = columns // head_width
    return pl.pallas_call(
        functools.partial(attention_kernel, head_width, block_sources),
        in_specs=[pl.BlockSpec(memory_space=pltpu.VMEM)],
        out_specs=pl.BlockSpec(memory_space=pltpu.VMEM),
        out_shape=jax.ShapeDtypeStruct((sources, tokens, columns), jnp.bfloat16),
        compiler_params=pltpu.CompilerParams(vmem_limit_bytes=32 * MIB),
        cost_estimate=pl.CostEstimate(
            flops=4 * total * total * columns,
            bytes_accessed=8 * total * columns,
            transcendentals=heads * total * total,
        ),
        name="attention",
    )(qkv)


def project_kernel(chunks, width, sigma_ref, latents_ref, weight_ref, *refs):
    attended_refs, (clean_ref, stepped_ref) = refs[:chunks], refs[chunks:]
    particles, tokens, columns = latents_ref.shape
    rows = particles * tokens
    depth = weight_ref.shape[0]
    part = width // chunks
    total = jnp.zeros((rows, columns), jnp.float32)
    for block in range(depth // width):
        for chunk in range(chunks):
            start = block * width + chunk * part
            piece = attended_refs[chunk][:, block].reshape(rows, part)
            total += jnp.dot(
                piece, weight_ref[start : start + part, :], preferred_element_type=jnp.float32
            )
    flat = latents_ref[...].reshape(rows, columns).astype(jnp.float32)
    velocity = flat + total
    clean_ref[...] = (flat - sigma_ref[0] * velocity).astype(jnp.bfloat16)
    stepped_ref[...] = (
        (flat - velocity * (1.0 / STEPS)).astype(jnp.bfloat16).reshape(particles, tokens, columns)
    )


def project(sigma, latents, out_weight, attended, width):
    particles, tokens, model_width = latents.shape
    rows = particles * tokens
    blocks = model_width // width
    chunks = len(attended)
    part = width // chunks
    columns = 512 if model_width % 512 == 0 else model_width
    attended = [piece.reshape(particles, blocks, tokens, part) for piece in attended]
    return pl.pallas_call(
        functools.partial(project_kernel, chunks, width),
        grid=(model_width // columns,),
        in_specs=[
            pl.BlockSpec(memory_space=pltpu.SMEM),
            pl.BlockSpec((particles, tokens, columns), lambda i: (0, 0, i)),
            pl.BlockSpec((model_width, columns), lambda i: (0, i)),
        ]
        + [pl.BlockSpec((particles, blocks, tokens, part), lambda i: (0, 0, 0, 0))] * chunks,
        out_specs=[
            pl.BlockSpec((rows, columns), lambda i: (0, i)),
            pl.BlockSpec((particles, tokens, columns), lambda i: (0, 0, i)),
        ],
        out_shape=[
            jax.ShapeDtypeStruct((rows, model_width), jnp.bfloat16),
            jax.ShapeDtypeStruct((particles, tokens, model_width), jnp.bfloat16),
        ],
        compiler_params=pltpu.CompilerParams(vmem_limit_bytes=32 * MIB),
        cost_estimate=pl.CostEstimate(
            flops=2 * rows * model_width * model_width,
            bytes_accessed=2 * model_width * model_width + 8 * rows * model_width,
            transcendentals=0,
        ),
        name="project",
    )(sigma, latents, out_weight, *attended)


def embed_kernel(clean_ref, weight_ref, gain_ref, features_ref, embedded_ref):
    step = pl.program_id(0)
    parts, rows, columns = embedded_ref.shape
    embedded_ref[step] = jnp.dot(
        clean_ref[...], weight_ref[0], preferred_element_type=jnp.float32
    )

    @pl.when(step == parts - 1)
    def _():
        blocks = [embedded_ref[index] for index in range(parts)]
        count = parts * columns
        centre = sum(jnp.sum(block, axis=1, keepdims=True) for block in blocks) * (1.0 / count)
        blocks = [block - centre for block in blocks]
        variance = sum(jnp.sum(block * block, axis=1, keepdims=True) for block in blocks) * (
            1.0 / count
        )
        inverse = lax.rsqrt(variance + norm_eps)
        for index, block in enumerate(blocks):
            cols = slice(index * columns, (index + 1) * columns)
            features_ref[:, cols] = jax.nn.gelu(block * inverse * gain_ref[:, cols]).astype(
                jnp.bfloat16
            )


def embed(clean, weight, gain):
    parts, depth, columns = weight.shape
    rows = clean.shape[0]
    count = parts * columns
    return pl.pallas_call(
        embed_kernel,
        grid=(parts,),
        in_specs=[
            pl.BlockSpec((rows, depth), lambda i: (0, 0)),
            pl.BlockSpec((1, depth, columns), lambda i: (i, 0, 0)),
            pl.BlockSpec((1, count), lambda i: (0, 0)),
        ],
        out_specs=pl.BlockSpec((rows, count), lambda i: (0, 0)),
        out_shape=jax.ShapeDtypeStruct((rows, count), jnp.bfloat16),
        scratch_shapes=[pltpu.VMEM((parts, rows, columns), jnp.float32)],
        compiler_params=pltpu.CompilerParams(vmem_limit_bytes=32 * MIB),
        cost_estimate=pl.CostEstimate(
            flops=2 * rows * depth * count,
            bytes_accessed=2 * depth * count + 2 * rows * (depth + count),
            transcendentals=rows * count,
        ),
        name="embed_norm",
    )(clean, weight, gain.reshape(1, count))


def reward_kernel(particles, features_ref, weight_ref, head_ref, out_ref, total_ref):
    step = pl.program_id(0)
    parts, _, depth, columns = weight_ref.shape
    rows = features_ref.shape[0]
    weight = weight_ref[...].reshape(parts * depth, columns)
    hidden = jnp.dot(features_ref[...], weight, preferred_element_type=jnp.float32)
    scored = jax.nn.gelu(hidden) * head_ref[0]

    @pl.when(step == 0)
    def _():
        total_ref[...] = jnp.zeros_like(total_ref)

    total_ref[...] += jnp.sum(scored.reshape(particles, rows // particles, columns), axis=1)

    @pl.when(step == pl.num_programs(0) - 1)
    def _():
        out_ref[...] = jnp.broadcast_to(
            jnp.sum(total_ref[...], axis=1, keepdims=True), out_ref.shape
        )


def reward(features, weight, head, particles):
    parts, blocks, depth, columns = weight.shape
    rows = features.shape[0]
    return pl.pallas_call(
        functools.partial(reward_kernel, particles),
        grid=(blocks,),
        in_specs=[
            pl.BlockSpec((rows, parts * depth), lambda i: (0, 0)),
            pl.BlockSpec((parts, 1, depth, columns), lambda i: (0, i, 0, 0)),
            pl.BlockSpec((1, 1, columns), lambda i: (i, 0, 0)),
        ],
        out_specs=pl.BlockSpec((particles, LANES), lambda i: (0, 0)),
        out_shape=jax.ShapeDtypeStruct((particles, LANES), jnp.float32),
        scratch_shapes=[pltpu.VMEM((particles, columns), jnp.float32)],
        compiler_params=pltpu.CompilerParams(vmem_limit_bytes=32 * MIB),
        cost_estimate=pl.CostEstimate(
            flops=2 * rows * parts * depth * blocks * columns,
            bytes_accessed=2 * parts * depth * blocks * columns,
            transcendentals=rows * blocks * columns,
        ),
        name="reward",
    )(features, weight, head.reshape(blocks, 1, columns))


def on_device(
    latents,
    queries,
    keys,
    values,
    out_weight,
    step_index,
    embed_weight,
    norm_gain,
    up_weight,
    head_weight,
    prev_logw,
    ancestors,
):
    seq_count = lax.axis_size("seq")
    group_count = lax.axis_size("groups")
    dom_count = lax.axis_size("dom")
    holders = group_count * dom_count
    dom_index = lax.axis_index("dom")
    holder = dom_index * group_count + lax.axis_index("groups")
    particles, tokens, model_width = latents.shape
    head_width = model_width // HEADS
    width = particles * model_width // seq_count
    chunks = 2 if width % (2 * LANES) == 0 else 1

    embed_columns = embed_weight.shape[1] // holders
    embed_share = lax.dynamic_slice_in_dim(embed_weight, holder * embed_columns, embed_columns, 1)
    embed_share = lax.all_gather(embed_share, "seq", axis=0, tiled=True)
    up_depth = up_weight.shape[0] // holders
    up_share = lax.dynamic_slice_in_dim(up_weight, holder * up_depth, up_depth, 0)
    up_share = lax.all_gather(up_share, "seq", axis=0)
    embed_parts = lax.all_gather(
        lax.all_gather(embed_share, "groups", axis=0), "dom", axis=0, tiled=True
    )
    up_parts = lax.all_gather(
        lax.all_gather(up_share, "groups", axis=0), "dom", axis=0, tiled=True
    )

    packed = pack(queries, keys, values, chunks, width)
    arrived = [lax.all_to_all(piece, "seq", 0, 0, tiled=True) for piece in packed]
    attended = [attention(piece, head_width) for piece in arrived]
    returned = [lax.all_to_all(piece, "seq", 0, 0, tiled=True) for piece in attended]

    sigma = step_index.astype(jnp.float32) / STEPS
    clean, stepped = project(sigma, latents, out_weight, returned, width)
    candidates = lax.all_gather(stepped, "dom", axis=0, tiled=True)
    features = embed(clean, embed_parts, norm_gain)
    partial_value = reward(features, up_parts, head_weight, particles)[:, 0]

    first = (lax.axis_index("seq") == 0).astype(jnp.float32)
    total_tokens = tokens * seq_count
    partial_logits = partial_value * (potential_scale / math.sqrt(total_tokens)) + prev_logw * first
    spread = (jnp.arange(dom_count) == dom_index).astype(jnp.float32)
    logits = lax.psum(spread[:, None] * partial_logits[None, :], ("dom", "seq"))
    highest = jnp.max(logits)
    log_total = highest + jnp.log(jnp.sum(jnp.exp(logits - highest)))
    log_weights = lax.dynamic_index_in_dim(logits, dom_index, 0, keepdims=False) - log_total
    resampled = jnp.take(candidates, ancestors, axis=0, mode="clip")
    return (resampled, log_weights)


def solution(mesh):
    in_specs = (
        P(("groups", "dom"), "seq", None),
        P(("groups", "dom"), "seq", None),
        P(("groups", "dom"), "seq", None),
        P(("groups", "dom"), "seq", None),
        P(),
        P("groups"),
        P("seq", None),
        P(),
        P(None, "seq"),
        P(),
        P(("groups", "dom")),
        P(("groups", "dom")),
    )
    out_specs = (P(("groups", "dom"), "seq", None), P(("groups", "dom")))
    return jax.shard_map(
        on_device, mesh=mesh, in_specs=in_specs, out_specs=out_specs, check_vma=False
    )
```

time: 304 us -> 318 us (1.046)
  blocking collectives: 23.9 us -> 102 us
  matrix products: 31.3 us -> 0 us
  local copies, waits for them, and re-layouts: 43.8 us -> 16.7 us
  Pallas kernels: 0 us -> 24.1 us
  waiting for transfers between devices: 164 us -> 144 us
  starting transfers between devices: 19.8 us -> 10.9 us
    all_to_all x4 -> x3, waiting for transfers between devices: 138 us -> 39.5 us  [on_device(): lax.all_to_all(piece, 'seq', 0, 0, tiled=True)]
    all_gather x3 -> x6, waiting for transfers between devices: 24.5 us -> 105 us  [the longest x1 58.3 us: on_device(): lax.all_gather(up_share, 'groups', axis=0)]
    all_gather x0 -> x1, blocking collectives: none -> 36.6 us  [on_device(): embed_share = lax.all_gather(embed_share, 'seq', axis=0, tiled=True)]
    all_to_all x0 -> x1, blocking collectives: none -> 34.6 us  [on_device(): lax.all_to_all(piece, 'seq', 0, 0, tiled=True)]
    pallas_call x0 -> x6, Pallas kernels: none -> 24.1 us  [the longest x2 9.62 us: attention(): pl.pallas_call(functools.partial(attention_kernel, head_width, block_sour...]
    dot_general x4 -> x0, matrix products: 21.3 us -> none  [the longest x1 7.09 us: on_device(): jnp.dot(features, lax.all_gather(up_weight, 'seq', axis=1, tiled=True), p...]
    sub x1 -> x0, matrix products: 9.91 us -> none  [one_block(): expanded = jnp.exp(scores - highest)]
    psum x1, blocking collectives: 21.5 us -> 31.3 us  [on_device(): logits = lax.psum(spread[:, None] * partial_logits[None, :], ('dom', 'seq'))]
  transfers between devices with their start and end apart: 7 -> 9, of which waited for: 6 -> 6; matrix products, arithmetic and copies ran while one was open for 24% -> 0% of each run, Pallas kernels for 0% -> 8%
where the time goes in v1:
time: 318 us; the launch traced here: 317 us
  waiting for transfers between devices  144 us (45%)
  blocking collectives  102 us (32%)
  Pallas kernels  24.1 us (8%)
  local copies, waits for them, and re-layouts  16.7 us (5%)
  between operations  16.2 us (5%)
  starting transfers between devices  10.9 us (3%)
    all_gather x1, waiting for transfers between devices, on_device(): lax.all_gather(up_share, 'groups', axis=0)  58.3 us
    all_to_all x3, waiting for transfers between devices, on_device(): lax.all_to_all(piece, 'seq', 0, 0, tiled=True)  39.5 us
    all_gather x1, blocking collectives, on_device(): embed_share = lax.all_gather(embed_share, 'seq', axis=0, tiled=True)  36.6 us
    all_to_all x1, blocking collectives, on_device(): lax.all_to_all(piece, 'seq', 0, 0, tiled=True)  34.6 us
    psum x1, blocking collectives, on_device(): logits = lax.psum(spread[:, None] * partial_logits[None, :], ('dom', 'seq'))  31.3 us
    all_gather x1, waiting for transfers between devices, on_device(): lax.all_gather(embed_share, 'groups', axis=0)  27.7 us
    all_gather x1, waiting for transfers between devices, on_device(): up_share = lax.all_gather(up_share, 'seq', axis=0)  18.9 us
    unnamed x24, local copies, waits for them, and re-layouts  12.2 us
  transfers between devices with their start and end apart: 9, of which 6 were waited for; matrix products, arithmetic and copies ran while one was open for 0% of the time, Pallas kernels for 8%

profile of v1, /device:TPU:0, one launch (start us, length us, event | category | flops | bytes accessed | tf_op | source)
XLA Modules:
  0.0 317.4 jit_solution(3858422495398121281)
XLA Ops:
  7.2 1.2 copy-done
  8.4 0.7 constant_dynamic-slice_fusion.1
  9.2 0.9 constant_dynamic-slice_fusion.2
  10.1 36.6 %all_gather.31 = bf16[1536,256]{1,0:T(8,128)(2,1)} all-gather(bf16[192,256]{1,0:T(8,128)(2,1)S(1)} %constant_dynamic-slice_fusion.2), channel_id=1, replica_groups=mesh['groups'=2,'dom'=2,'seq'=8] {'seq'}, dimensions={0}, use_global_device_ids=true | all-gather | bytes 884736 | tf_op jit(solution)/shard_map/all_gather | solution.py:276
  46.7 18.9 %all-gather.18.cloned.1.call-done = bf16[2048,512]{1,0:T(8,128)(2,1)} async-done(((bf16[256,512]{1,0:T(8,128)(2,1)}), bf16[2048,512]{1,0:T(8,128)(2,1)}) %all-gather.18.cloned.1.call-update) | async-done | bytes 2097168 | tf_op jit(solution)/shard_map/all_gather | solution.py:279
  65.7 27.7 %all-gather.16.cloned.1.call-done = bf16[3072,256]{1,0:T(8,128)(2,1)} async-done(((bf16[1536,256]{1,0:T(8,128)(2,1)}), bf16[3072,256]{1,0:T(8,128)(2,1)}) %all-gather.16.cloned.1.call-update) | async-done | bytes 1572880 | tf_op jit(solution)/shard_map/all_gather | solution.py:281
  93.5 58.3 %all-gather.20.cloned.1.call-done = bf16[16,256,512]{2,1,0:T(8,128)(2,1)} async-done(((bf16[8,256,512]{2,1,0:T(8,128)(2,1)}), bf16[16,256,512]{2,1,0:T(8,128)(2,1)}) %all-gather.20.cloned.1.call-update) | async-done | bytes 4194320 | tf_op jit(solution)/shard_map/all_gather | solution.py:284
  151.8 4.0 %pack_heads.1 = (bf16[8,3,64,384]{3,2,1,0:T(8,128)(2,1)}, bf16[8,3,64,384]{3,2,1,0:T(8,128)(2,1)}) custom-call(bf16[4,64,1536]{2,1,0:T(8,128)(2,1)} %q_ref.1, bf16[4,64,1536]{2,1,0:T(8,128)(2,1)} %k_ref.1, bf16[4,64,1536]{2,1,0:T(8,128)(2,1)} %v_ref.1), custom_call_target="tpu_custom_call" | custom-call | tf_op jit(solution)/shard_map/pack_heads/pallas_call | solution.py:37
  155.8 34.6 %all_to_all.20.qkv_ref = bf16[8,3,64,384]{3,2,1,0:T(8,128)(2,1)} all-to-all(bf16[8,3,64,384]{3,2,1,0:T(8,128)(2,1)} %get-tuple-element.6), channel_id=1, replica_groups=mesh['groups'=2,'dom'=2,'seq'=8] {'seq'}, dimensions={0} | all-to-all | bytes 2359296 | tf_op jit(solution)/shard_map/all_to_all | solution.py:288
  190.4 3.6 %all-to-all-start.2 = ((bf16[8,3,64,384]{3,2,1,0:T(8,128)(2,1)}), bf16[8,3,64,384]{3,2,1,0:T(8,128)(2,1)S(1)}, u32[]{:S(2)}, u32[]{:S(2)}) async-start(bf16[8,3,64,384]{3,2,1,0:T(8,128)(2,1)} %get-tuple-element.7), calls=%async_computation.2 | async-start | bytes 2359296 | tf_op jit(solution)/shard_map/all_to_all | solution.py:288
  193.9 1.3 copy-done.4
  195.2 5.2 %attention.2 = bf16[8,64,384]{2,1,0:T(8,128)(2,1)} custom-call(bf16[8,3,64,384]{3,2,1,0:T(8,128)(2,1)S(1)} %copy-done.4), custom_call_target="tpu_custom_call" | custom-call | flops 402653184 | bytes 1572864 | tf_op jit(solution)/shard_map/attention/pallas_call | solution.py:83
  200.4 21.8 %all-to-all-done.2.qkv_ref = bf16[8,3,64,384]{3,2,1,0:T(8,128)(2,1)S(1)} async-done(((bf16[8,3,64,384]{3,2,1,0:T(8,128)(2,1)}), bf16[8,3,64,384]{3,2,1,0:T(8,128)(2,1)S(1)}, u32[]{:S(2)}, u32[]{:S(2)}) %all-to-all-start.2) | async-done | bytes 1179680 | tf_op jit(solution)/shard_map/all_to_all | solution.py:288
  222.1 3.5 %all-to-all-start.1 = ((bf16[8,64,384]{2,1,0:T(8,128)(2,1)}), bf16[8,64,384]{2,1,0:T(8,128)(2,1)S(1)}, u32[]{:S(2)}, u32[]{:S(2)}) async-start(bf16[8,64,384]{2,1,0:T(8,128)(2,1)} %attention.2), calls=%async_computation.1 | async-start | bytes 786432 | tf_op jit(solution)/shard_map/all_to_all | solution.py:290
  225.6 4.4 %attention.3 = bf16[8,64,384]{2,1,0:T(8,128)(2,1)S(1)} custom-call(bf16[8,3,64,384]{3,2,1,0:T(8,128)(2,1)S(1)} %all-to-all-done.2.qkv_ref), custom_call_target="tpu_custom_call" | custom-call | flops 402653184 | bytes 1572864 | tf_op jit(solution)/shard_map/attention/pallas_call | solution.py:83
  230.1 0.8 copy-done.7
  230.8 6.6 %all-to-all-done.1 = bf16[8,64,384]{2,1,0:T(8,128)(2,1)S(1)} async-done(((bf16[8,64,384]{2,1,0:T(8,128)(2,1)}), bf16[8,64,384]{2,1,0:T(8,128)(2,1)S(1)}, u32[]{:S(2)}, u32[]{:S(2)}) %all-to-all-start.1) | async-done | bytes 393248 | tf_op jit(solution)/shard_map/all_to_all | solution.py:290
  237.4 3.6 %all-to-all-start.3 = ((bf16[8,64,384]{2,1,0:T(8,128)(2,1)}), bf16[8,64,384]{2,1,0:T(8,128)(2,1)S(1)}, u32[]{:S(2)}, u32[]{:S(2)}) async-start(bf16[8,64,384]{2,1,0:T(8,128)(2,1)} %copy-done.7), calls=%async_computation.3 | async-start | bytes 786432 | tf_op jit(solution)/shard_map/all_to_all | solution.py:290
  241.8 11.1 %all-to-all-done.3 = bf16[8,64,384]{2,1,0:T(8,128)(2,1)S(1)} async-done(((bf16[8,64,384]{2,1,0:T(8,128)(2,1)}), bf16[8,64,384]{2,1,0:T(8,128)(2,1)S(1)}, u32[]{:S(2)}, u32[]{:S(2)}) %all-to-all-start.3) | async-done | bytes 393248 | tf_op jit(solution)/shard_map/all_to_all | solution.py:290
  252.9 2.3 copy-done.2
  255.2 2.8 project.1
  258.0 0.9 copy-done.6
  259.0 1.9 copy-done.3
  260.8 2.3 embed_norm.1.features_ref
  263.2 3.9 %copy-done.1 = bf16[4,8,256,512]{3,2,1,0:T(8,128)(2,1)S(1)} copy-done((bf16[4,8,256,512]{3,2,1,0:T(8,128)(2,1)S(1)}, bf16[4,8,256,512]{3,2,1,0:T(8,128)(2,1)}, u32[]{:S(2)}) %copy-start.1) | copy-done | bytes 8388632
  267.1 5.4 %reward.1 = f32[4,128]{1,0:T(4,128)S(1)} custom-call(bf16[256,1024]{1,0:T(8,128)(2,1)S(1)} %embed_norm.1.features_ref, bf16[4,8,256,512]{3,2,1,0:T(8,128)(2,1)S(1)} %copy-done.1, f32[8,1,512]{2,1,0:T(1,128)S(1)} %bitcast.11), custom_call_target="tpu_custom_call" | custom-call | flops 2147483648 | bytes 8388608 | tf_op jit(solution)/shard_map/reward/pallas_call | solution.py:228
  272.5 0.1 multiply_reduce_fusion
  272.7 2.9 gather_fusion
  275.6 31.3 %psum.7 = f32[2,4]{1,0:T(2,128)S(1)} all-reduce(f32[2,4]{1,0:T(2,128)S(1)} %broadcast_multiply_fusion), channel_id=1, replica_groups=mesh['groups'=2,'dom'=2,'seq'=8] {'dom','seq'}, use_global_device_ids=true, to_apply=%region_0.0 | all-reduce | flops 8 | bytes 64 | tf_op jit(solution)/shard_map/psum | solution.py:302
  306.9 0.6 reduce_max.9
  307.5 1.3 exponential_reduce_fusion
  310.1 0.5 fusion.1
  (36 shorter events, 0.5 us)
Async XLA Ops:
  7.2 1.2 copy-start
  7.2 58.5 %all-gather.18.cloned.1.call-start = ((), (), s32[]{:S(2)}) async-start(), calls=%async_computation.8 | async-start | bytes 2359296 | tf_op jit(solution)/shard_map/all_gather | solution.py:279
  9.1 84.3 %all-gather.16.cloned.1.call-start = ((), (), s32[]{:S(2)}) async-start(), calls=%async_computation.7 | async-start | bytes 2359296 | tf_op jit(solution)/shard_map/all_gather | solution.py:281
  46.7 105.1 %all-gather.20.cloned.1.call-start = ((), (), s32[]{:S(2)}) async-start(), calls=%async_computation.9 | async-start | bytes 6291456 | tf_op jit(solution)/shard_map/all_gather | solution.py:284
  65.7 193.3 %all-gather.12.cloned.1.call-start = ((), (), s32[]{:S(2)}) async-start(), calls=%async_computation.5 | async-start | bytes 4718592 | tf_op jit(solution)/shard_map/all_gather | solution.py:280
  93.4 169.7 %all-gather.14.cloned.1.call-start = ((), (), s32[]{:S(2)}) async-start(), calls=%async_computation.6 | async-start | bytes 12582912 | tf_op jit(solution)/shard_map/all_gather | solution.py:283
  190.4 31.8 %all-to-all-start.2 = ((bf16[8,3,64,384]{3,2,1,0:T(8,128)(2,1)}), bf16[8,3,64,384]{3,2,1,0:T(8,128)(2,1)S(1)}, u32[]{:S(2)}, u32[]{:S(2)}) async-start(bf16[8,3,64,384]{3,2,1,0:T(8,128)(2,1)} %get-tuple-element.7), calls=%async_computation.2 | async-start | bytes 2359296 | tf_op jit(solution)/shard_map/all_to_all | solution.py:288
  193.9 1.3 copy-start.4
  222.1 15.3 %all-to-all-start.1 = ((bf16[8,64,384]{2,1,0:T(8,128)(2,1)}), bf16[8,64,384]{2,1,0:T(8,128)(2,1)S(1)}, u32[]{:S(2)}, u32[]{:S(2)}) async-start(bf16[8,64,384]{2,1,0:T(8,128)(2,1)} %attention.2), calls=%async_computation.1 | async-start | bytes 786432 | tf_op jit(solution)/shard_map/all_to_all | solution.py:290
  225.6 27.2 %copy-start.5 = (bf16[4,64,1536]{2,1,0:T(8,128)(2,1)S(1)}, bf16[4,64,1536]{2,1,0:T(8,128)(2,1)}, u32[]{:S(2)}) copy-start(bf16[4,64,1536]{2,1,0:T(8,128)(2,1)} %latents_ref.1) | copy-start | bytes 2359300
  230.1 0.8 copy-start.7
  237.4 15.4 %all-to-all-start.3 = ((bf16[8,64,384]{2,1,0:T(8,128)(2,1)}), bf16[8,64,384]{2,1,0:T(8,128)(2,1)S(1)}, u32[]{:S(2)}, u32[]{:S(2)}) async-start(bf16[8,64,384]{2,1,0:T(8,128)(2,1)} %copy-done.7), calls=%async_computation.3 | async-start | bytes 786432 | tf_op jit(solution)/shard_map/all_to_all | solution.py:290
  241.1 31.6 %all-gather.10.cloned.1.call-start = ((), (), s32[]{:S(2)}) async-start(), calls=%async_computation.4 | async-start | bytes 2359296 | tf_op jit(solution)/shard_map/all_gather | solution.py:294
  252.9 2.3 copy-start.2
  255.2 3.7 %copy-start.10 = (s32[4]{0:T(128)S(1)}, s32[4]{0:T(128)}, u32[]{:S(2)}) copy-start(s32[4]{0:T(128)} %param.23) | copy-start | bytes 52
  255.2 3.7 %copy-start.9 = (f32[1024]{0:T(1024)S(1)}, f32[1024]{0:T(1024)}, u32[]{:S(2)}) copy-start(f32[1024]{0:T(1024)} %param.19) | copy-start | bytes 12292
  258.0 0.9 copy-start.6
  258.9 1.9 copy-start.3
  260.8 2.3 copy-start.8
  263.2 3.9 %copy-start.1 = (bf16[4,8,256,512]{3,2,1,0:T(8,128)(2,1)S(1)}, bf16[4,8,256,512]{3,2,1,0:T(8,128)(2,1)}, u32[]{:S(2)}) copy-start(bf16[4,8,256,512]{3,2,1,0:T(8,128)(2,1)} %all-gather.14.cloned.1.call-done.weight_ref) | copy-start | bytes 25165828
  267.1 5.5 %copy-start.11 = (f32[4]{0:T(128)S(1)}, f32[4]{0:T(128)}, u32[]{:S(2)}) copy-start(f32[4]{0:T(128)} %param.22) | copy-start | bytes 52
Sparse Core Ops, SparseCore 0:
  10.7 54.8 all-gather.17
  67.2 26.1 all-gather.15
  95.0 56.7 all-gather.19
  153.2 12.1 all-gather.11
  166.7 21.0 all-gather.13
  259.0 7.9 all-gather.9

commit v2 on v1

--- a/solution.py
+++ b/solution.py
@@ -17,31 +17,44 @@
 MIB = 1024 * 1024
 
 
-def pack_kernel(chunks, width, q_ref, k_ref, v_ref, *out_refs):
+def pack_kernel(chunks, width, chunk, q_ref, k_ref, v_ref, out_ref):
     blocks = q_ref.shape[2] // width
     part = width // chunks
     for index, ref in enumerate((q_ref, k_ref, v_ref)):
         for block in range(blocks):
-            for chunk in range(chunks):
-                start = block * width + chunk * part
-                out_refs[chunk][block, index] = ref[0, :, start : start + part]
-
-
-def pack(queries, keys, values, chunks, width):
+            start = block * width + chunk * part
+            out_ref[block, index] = ref[0, :, start : start + part]
+
+
+def pack(queries, keys, values, chunks, width, chunk):
     particles, tokens, model_width = queries.shape
     blocks = model_width // width
     part = width // chunks
     in_spec = pl.BlockSpec((1, tokens, model_width), lambda i: (i, 0, 0))
-    out_spec = pl.BlockSpec((blocks, 3, tokens, part), lambda i: (i, 0, 0, 0))
-    out_shape = jax.ShapeDtypeStruct((particles * blocks, 3, tokens, part), queries.dtype)
-    return pl.pallas_call(
-        functools.partial(pack_kernel, chunks, width),
+    return pl.pallas_call(
+        functools.partial(pack_kernel, chunks, width, chunk),
         grid=(particles,),
         in_specs=[in_spec] * 3,
-        out_specs=[out_spec] * chunks,
-        out_shape=[out_shape] * chunks,
+        out_specs=pl.BlockSpec((blocks, 3, tokens, part), lambda i: (i, 0, 0, 0)),
+        out_shape=jax.ShapeDtypeStruct((particles * blocks, 3, tokens, part), queries.dtype),
         name="pack_heads",
     )(queries, keys, values)
+
+
+def gate_kernel(*refs):
+    pass
+
+
+def gate(array, after):
+    anywhere = pl.BlockSpec(memory_space=pl.ANY)
+    return pl.pallas_call(
+        gate_kernel,
+        in_specs=[anywhere, anywhere],
+        out_specs=anywhere,
+        out_shape=jax.ShapeDtypeStruct(array.shape, array.dtype),
+        input_output_aliases={0: 0},
+        name="gate",
+    )(array, after)
 
 
 def attention_kernel(head_width, block_sources, qkv_ref, out_ref):
@@ -152,98 +165,189 @@
     )(sigma, latents, out_weight, *attended)
 
 
-def embed_kernel(clean_ref, weight_ref, gain_ref, features_ref, embedded_ref):
-    step = pl.program_id(0)
-    parts, rows, columns = embedded_ref.shape
-    embedded_ref[step] = jnp.dot(
-        clean_ref[...], weight_ref[0], preferred_element_type=jnp.float32
-    )
-
-    @pl.when(step == parts - 1)
-    def _():
-        blocks = [embedded_ref[index] for index in range(parts)]
-        count = parts * columns
-        centre = sum(jnp.sum(block, axis=1, keepdims=True) for block in blocks) * (1.0 / count)
-        blocks = [block - centre for block in blocks]
-        variance = sum(jnp.sum(block * block, axis=1, keepdims=True) for block in blocks) * (
-            1.0 / count
+def embed_kernel(order_ref, clean_ref, gain_ref, *refs):
+    parts = order_ref.shape[0]
+    weight_refs, (features_ref, weight_vmem, embedded_ref, sems) = refs[:parts], refs[parts:]
+    copies = [
+        pltpu.make_async_copy(weight_refs[index], weight_vmem.at[index], sems.at[index])
+        for index in range(parts)
+    ]
+    for copy in copies:
+        copy.start()
+    for index, copy in enumerate(copies):
+        copy.wait()
+        embedded_ref[order_ref[index]] = jnp.dot(
+            clean_ref[...], weight_vmem[index], preferred_element_type=jnp.float32
         )
-        inverse = lax.rsqrt(variance + norm_eps)
-        for index, block in enumerate(blocks):
-            cols = slice(index * columns, (index + 1) * columns)
-            features_ref[:, cols] = jax.nn.gelu(block * inverse * gain_ref[:, cols]).astype(
-                jnp.bfloat16
-            )
-
-
-def embed(clean, weight, gain):
-    parts, depth, columns = weight.shape
+    columns = embedded_ref.shape[2]
+    count = parts * columns
+    blocks = [embedded_ref[index] for index in range(parts)]
+    centre = sum(jnp.sum(block, axis=1, keepdims=True) for block in blocks) * (1.0 / count)
+    blocks = [block - centre for block in blocks]
+    variance = sum(jnp.sum(block * block, axis=1, keepdims=True) for block in blocks) * (
+        1.0 / count
+    )
+    inverse = lax.rsqrt(variance + norm_eps)
+    share = features_ref.shape[2]
+    for index, block in enumerate(blocks):
+        cols = slice(index * columns, (index + 1) * columns)
+        piece = jax.nn.gelu(block * inverse * gain_ref[:, cols]).astype(jnp.bfloat16)
+        start = index * columns % share
+        features_ref[index * columns // share, :, start : start + columns] = piece
+
+
+def embed(order, clean, weights, gain, depth_parts):
+    parts = len(weights)
+    depth, columns = weights[0].shape
     rows = clean.shape[0]
     count = parts * columns
+    vmem = pl.BlockSpec(memory_space=pltpu.VMEM)
     return pl.pallas_call(
         embed_kernel,
-        grid=(parts,),
-        in_specs=[
-            pl.BlockSpec((rows, depth), lambda i: (0, 0)),
-            pl.BlockSpec((1, depth, columns), lambda i: (i, 0, 0)),
-            pl.BlockSpec((1, count), lambda i: (0, 0)),
+        in_specs=[pl.BlockSpec(memory_space=pltpu.SMEM), vmem, vmem]
+        + [pl.BlockSpec(memory_space=pl.ANY)] * parts,
+        out_specs=vmem,
+        out_shape=jax.ShapeDtypeStruct((depth_parts, rows, count // depth_parts), jnp.bfloat16),
+        scratch_shapes=[
+            pltpu.VMEM((parts, depth, columns), jnp.bfloat16),
+            pltpu.VMEM((parts, rows, columns), jnp.float32),
+            pltpu.SemaphoreType.DMA((parts,)),
         ],
-        out_specs=pl.BlockSpec((rows, count), lambda i: (0, 0)),
-        out_shape=jax.ShapeDtypeStruct((rows, count), jnp.bfloat16),
-        scratch_shapes=[pltpu.VMEM((parts, rows, columns), jnp.float32)],
-        compiler_params=pltpu.CompilerParams(vmem_limit_bytes=32 * MIB),
+        compiler_params=pltpu.CompilerParams(vmem_limit_bytes=56 * MIB),
         cost_estimate=pl.CostEstimate(
             flops=2 * rows * depth * count,
             bytes_accessed=2 * depth * count + 2 * rows * (depth + count),
             transcendentals=rows * count,
         ),
         name="embed_norm",
-    )(clean, weight, gain.reshape(1, count))
-
-
-def reward_kernel(particles, features_ref, weight_ref, head_ref, out_ref, total_ref):
+    )(order, clean, gain.reshape(1, count), *weights)
+
+
+def reward_kernel(particles, scale, order_ref, features_ref, head_ref, before_ref, *refs):
+    parts = order_ref.shape[0]
+    weight_refs, (out_ref, total_ref) = refs[:parts], refs[parts:]
     step = pl.program_id(0)
-    parts, _, depth, columns = weight_ref.shape
-    rows = features_ref.shape[0]
-    weight = weight_ref[...].reshape(parts * depth, columns)
-    hidden = jnp.dot(features_ref[...], weight, preferred_element_type=jnp.float32)
-    scored = jax.nn.gelu(hidden) * head_ref[0]
+    rows = features_ref.shape[1]
+    blocks, _, columns = weight_refs[0].shape
 
     @pl.when(step == 0)
     def _():
         total_ref[...] = jnp.zeros_like(total_ref)
 
-    total_ref[...] += jnp.sum(scored.reshape(particles, rows // particles, columns), axis=1)
+    for block in range(blocks):
+        hidden = sum(
+            jnp.dot(
+                features_ref[order_ref[index]],
+                weight_refs[index][block],
+                preferred_element_type=jnp.float32,
+            )
+            for index in range(parts)
+        )
+        scored = jax.nn.gelu(hidden) * head_ref[block]
+        total_ref[...] += jnp.sum(scored.reshape(particles, rows // particles, columns), axis=1)
 
     @pl.when(step == pl.num_programs(0) - 1)
     def _():
-        out_ref[...] = jnp.broadcast_to(
-            jnp.sum(total_ref[...], axis=1, keepdims=True), out_ref.shape
-        )
-
-
-def reward(features, weight, head, particles):
-    parts, blocks, depth, columns = weight.shape
-    rows = features.shape[0]
-    return pl.pallas_call(
-        functools.partial(reward_kernel, particles),
-        grid=(blocks,),
+        sums = jnp.sum(total_ref[...], axis=1, keepdims=True) * scale
+        lanes = lax.broadcasted_iota(jnp.int32, out_ref.shape[1:], 1)
+        row = jnp.zeros(out_ref.shape[1:], jnp.float32)
+        for particle in range(particles):
+            row = jnp.where(lanes == particle, sums[particle : particle + 1], row)
+        earlier = before_ref.shape[0] - 1
+        if earlier:
+            out_ref[:earlier] = before_ref[:earlier]
+        out_ref[earlier] = row + before_ref[earlier]
+
+
+def reward(order, features, weights, head, before, particles, scale):
+    parts = len(weights)
+    blocks, depth, columns = weights[0].shape
+    rows = features.shape[1]
+    group = 2 if blocks % 2 == 0 else 1
+    return pl.pallas_call(
+        functools.partial(reward_kernel, particles, scale),
+        grid=(blocks // group,),
         in_specs=[
-            pl.BlockSpec((rows, parts * depth), lambda i: (0, 0)),
-            pl.BlockSpec((parts, 1, depth, columns), lambda i: (0, i, 0, 0)),
-            pl.BlockSpec((1, 1, columns), lambda i: (i, 0, 0)),
-        ],
-        out_specs=pl.BlockSpec((particles, LANES), lambda i: (0, 0)),
-        out_shape=jax.ShapeDtypeStruct((particles, LANES), jnp.float32),
+            pl.BlockSpec(memory_space=pltpu.SMEM),
+            pl.BlockSpec(features.shape, lambda i: (0, 0, 0)),
+            pl.BlockSpec((group, 1, columns), lambda i: (i, 0, 0)),
+            pl.BlockSpec(before.shape, lambda i: (0, 0, 0)),
+        ]
+        + [pl.BlockSpec((group, depth, columns), lambda i: (i, 0, 0))] * parts,
+        out_specs=pl.BlockSpec(before.shape, lambda i: (0, 0, 0)),
+        out_shape=jax.ShapeDtypeStruct(before.shape, jnp.float32),
         scratch_shapes=[pltpu.VMEM((particles, columns), jnp.float32)],
-        compiler_params=pltpu.CompilerParams(vmem_limit_bytes=32 * MIB),
+        compiler_params=pltpu.CompilerParams(vmem_limit_bytes=56 * MIB),
         cost_estimate=pl.CostEstimate(
             flops=2 * rows * parts * depth * blocks * columns,
             bytes_accessed=2 * parts * depth * blocks * columns,
             transcendentals=rows * blocks * columns,
         ),
         name="reward",
-    )(features, weight, head.reshape(blocks, 1, columns))
+    )(order, features, head, before, *weights)
+
+
+def add_kernel(*refs):
+    refs[-1][...] = functools.reduce(lambda total, ref: total + ref[...], refs[1:-1], refs[0][...])
+
+
+def add_all(arrays):
+    return pl.pallas_call(
+        add_kernel,
+        out_shape=jax.ShapeDtypeStruct(arrays[0].shape, arrays[0].dtype),
+        name="add_partials",
+    )(*arrays)
+
+
+def finish_kernel(particles, mine_ref, theirs_ref, out_ref):
+    own = mine_ref[0] + theirs_ref[1]
+    other = mine_ref[1] + theirs_ref[0]
+    lanes = lax.broadcasted_iota(jnp.int32, own.shape, 1)
+    both = jnp.maximum(own, other)
+    highest = jnp.max(jnp.where(lanes < particles, both, -jnp.inf), axis=1, keepdims=True)
+    terms = jnp.where(lanes < particles, jnp.exp(own - highest) + jnp.exp(other - highest), 0.0)
+    log_total = highest + jnp.log(jnp.sum(terms, axis=1, keepdims=True))
+    out_ref[...] = (own - log_total)[:, :particles]
+
+
+def finish(mine, theirs, particles):
+    return pl.pallas_call(
+        functools.partial(finish_kernel, particles),
+        out_shape=jax.ShapeDtypeStruct((1, particles), jnp.float32),
+        name="log_weights",
+    )(mine, theirs).reshape(particles)
+
+
+def resample_kernel(place_ref, own_ref, other_ref, out_ref, sems):
+    particles = out_ref.shape[0]
+    for index in range(particles):
+        for candidate, ref in enumerate((own_ref, other_ref)):
+
+            @pl.when(place_ref[0, index] == candidate)
+            def _():
+                pltpu.make_async_copy(
+                    ref.at[place_ref[1, index]], out_ref.at[index], sems.at[index]
+                ).start()
+
+    for index in range(particles):
+        pltpu.make_async_copy(own_ref.at[0], out_ref.at[index], sems.at[index]).wait()
+
+
+def resample(place, own, other):
+    anywhere = pl.BlockSpec(memory_space=pl.ANY)
+    return pl.pallas_call(
+        resample_kernel,
+        in_specs=[pl.BlockSpec(memory_space=pltpu.SMEM), anywhere, anywhere],
+        out_specs=anywhere,
+        out_shape=jax.ShapeDtypeStruct(own.shape, own.dtype),
+        scratch_shapes=[pltpu.SemaphoreType.DMA((own.shape[0],))],
+        name="resample",
+    )(place, own, other)
+
+
+def shifted(array, axis, step):
+    count = lax.axis_size(axis)
+    return lax.ppermute(array, axis, [(i, (i + step) % count) for i in range(count)])
 
 
 def on_device(
@@ -264,46 +368,69 @@
     group_count = lax.axis_size("groups")
     dom_count = lax.axis_size("dom")
     holders = group_count * dom_count
-    dom_index = lax.axis_index("dom")
-    holder = dom_index * group_count + lax.axis_index("groups")
+    dom = lax.axis_index("dom")
+    group = lax.axis_index("groups")
     particles, tokens, model_width = latents.shape
     head_width = model_width // HEADS
     width = particles * model_width // seq_count
     chunks = 2 if width % (2 * LANES) == 0 else 1
 
     embed_columns = embed_weight.shape[1] // holders
-    embed_share = lax.dynamic_slice_in_dim(embed_weight, holder * embed_columns, embed_columns, 1)
+    embed_share = lax.dynamic_slice_in_dim(
+        embed_weight, (dom * group_count + group) * embed_columns, embed_columns, 1
+    )
     embed_share = lax.all_gather(embed_share, "seq", axis=0, tiled=True)
-    up_depth = up_weight.shape[0] // holders
-    up_share = lax.dynamic_slice_in_dim(up_weight, holder * up_depth, up_depth, 0)
+    up_depth = up_weight.shape[0] // group_count
+    up_columns = up_weight.shape[1] // dom_count
+    up_share = lax.dynamic_slice(
+        up_weight, (group * up_depth, dom * up_columns), (up_depth, up_columns)
+    )
     up_share = lax.all_gather(up_share, "seq", axis=0)
-    embed_parts = lax.all_gather(
-        lax.all_gather(embed_share, "groups", axis=0), "dom", axis=0, tiled=True
-    )
-    up_parts = lax.all_gather(
-        lax.all_gather(up_share, "groups", axis=0), "dom", axis=0, tiled=True
-    )
-
-    packed = pack(queries, keys, values, chunks, width)
+
+    packed = [pack(queries, keys, values, chunks, width, chunk) for chunk in range(chunks)]
     arrived = [lax.all_to_all(piece, "seq", 0, 0, tiled=True) for piece in packed]
+    embed_share = gate(embed_share, packed[0])
+    up_share = gate(up_share, packed[-1])
+    embed_near = [embed_share] + [shifted(embed_share, "groups", k) for k in range(1, group_count)]
+    up_parts = [up_share] + [shifted(up_share, "groups", k) for k in range(1, group_count)]
     attended = [attention(piece, head_width) for piece in arrived]
     returned = [lax.all_to_all(piece, "seq", 0, 0, tiled=True) for piece in attended]
+    embed_near = [gate(piece, attended[0]) for piece in embed_near]
+    embed_parts = embed_near + [
+        shifted(piece, "dom", k) for k in range(1, dom_count) for piece in embed_near
+    ]
+    group_order = (group - jnp.arange(group_count)) % group_count
+    dom_order = (dom - jnp.arange(dom_count)) % dom_count
+    embed_order = (dom_order[:, None] * group_count + group_order[None, :]).reshape(holders)
 
     sigma = step_index.astype(jnp.float32) / STEPS
     clean, stepped = project(sigma, latents, out_weight, returned, width)
-    candidates = lax.all_gather(stepped, "dom", axis=0, tiled=True)
-    features = embed(clean, embed_parts, norm_gain)
-    partial_value = reward(features, up_parts, head_weight, particles)[:, 0]
-
+    stepped_other = shifted(stepped, "dom", 1)
+    features = embed(embed_order, clean, embed_parts, norm_gain, group_count)
+    features_other = shifted(features, "dom", 1)
+
+    scale = potential_scale / math.sqrt(tokens * seq_count)
+    head = lax.dynamic_index_in_dim(
+        head_weight.reshape(seq_count, dom_count, up_columns), dom, 1, keepdims=True
+    )
     first = (lax.axis_index("seq") == 0).astype(jnp.float32)
-    total_tokens = tokens * seq_count
-    partial_logits = partial_value * (potential_scale / math.sqrt(total_tokens)) + prev_logw * first
-    spread = (jnp.arange(dom_count) == dom_index).astype(jnp.float32)
-    logits = lax.psum(spread[:, None] * partial_logits[None, :], ("dom", "seq"))
-    highest = jnp.max(logits)
-    log_total = highest + jnp.log(jnp.sum(jnp.exp(logits - highest)))
-    log_weights = lax.dynamic_index_in_dim(logits, dom_index, 0, keepdims=False) - log_total
-    resampled = jnp.take(candidates, ancestors, axis=0, mode="clip")
+    start = jnp.pad((prev_logw * first).reshape(1, 1, particles), ((0, 0), (0, 0), (0, LANES - particles)))
+    partial_own = reward(group_order, features, up_parts, head, start, particles, scale)
+    partial_both = reward(
+        group_order,
+        features_other,
+        up_parts,
+        head,
+        jnp.concatenate([partial_own, jnp.zeros_like(partial_own)]),
+        particles,
+        scale,
+    )
+    mine = add_all([partial_both] + [shifted(partial_both, "seq", k) for k in range(1, seq_count)])
+    log_weights = finish(mine, shifted(mine, "dom", 1), particles)
+
+    ancestors = ancestors.astype(jnp.int32)
+    place = jnp.stack([(ancestors // particles != dom).astype(jnp.int32), ancestors % particles])
+    resampled = resample(place, stepped, stepped_other)
     return (resampled, log_weights)
 
 

time: 318 us -> 247 us (0.78)
  blocking collectives: 102 us -> 34 us
  waiting for transfers between devices: 144 us -> 87.6 us
  Pallas kernels: 24.1 us -> 65.8 us
  starting transfers between devices: 10.9 us -> 30.8 us
  local copies, waits for them, and re-layouts: 16.7 us -> 12.6 us
    all_gather x5 -> x0, waiting for transfers between devices: 86 us -> none  [the longest x1 58.3 us: on_device(): lax.all_gather(up_share, 'groups', axis=0)]
    pallas_call x3 -> x12, Pallas kernels: 11.7 us -> 52.7 us  [the longest x1 25.7 us: resample(): pl.pallas_call(resample_kernel, in_specs=[pl.BlockSpec(memory_space=pltpu...]
    all_to_all x1 -> x0, blocking collectives: 34.6 us -> none  [on_device(): lax.all_to_all(piece, 'seq', 0, 0, tiled=True)]
    psum x1 -> x0, blocking collectives: 31.3 us -> none  [on_device(): logits = lax.psum(spread[:, None] * partial_logits[None, :], ('dom', 'seq'))]
    all_gather x1, waiting for transfers between devices: 18.9 us -> 41.9 us  [on_device(): up_share = lax.all_gather(up_share, 'seq', axis=0)]
    ppermute x0 -> x14, starting transfers between devices: none -> 12.8 us  [shifted(): lax.ppermute(array, axis, [(i, (i + step) % count) for i in range(count)])]
    ppermute x0 -> x14, waiting for transfers between devices: none -> 10 us  [shifted(): lax.ppermute(array, axis, [(i, (i + step) % count) for i in range(count)])]
    all_to_all x3 -> x4, starting transfers between devices: 10.7 us -> 17.9 us  [on_device(): lax.all_to_all(piece, 'seq', 0, 0, tiled=True)]
  transfers between devices with their start and end apart: 9 -> 19, of which waited for: 6 -> 8; matrix products, arithmetic and copies ran while one was open for 0% -> 2% of each run, Pallas kernels for 8% -> 25%
where the time goes in v2:
time: 247 us; the launch traced here: 246 us
  waiting for transfers between devices  87.6 us (35%)
  Pallas kernels  65.8 us (27%)
  blocking collectives  34 us (14%)
  starting transfers between devices  30.8 us (12%)
  between operations  15 us (6%)
  local copies, waits for them, and re-layouts  12.6 us (5%)
    all_gather x1, waiting for transfers between devices, on_device(): up_share = lax.all_gather(up_share, 'seq', axis=0)  41.9 us
    all_to_all x4, waiting for transfers between devices, on_device(): lax.all_to_all(piece, 'seq', 0, 0, tiled=True)  35.6 us
    all_gather x1, blocking collectives, on_device(): embed_share = lax.all_gather(embed_share, 'seq', axis=0, tiled=True)  34 us
    pallas_call x1, Pallas kernels, resample(): pl.pallas_call(resample_kernel, in_specs=[pl.BlockSpec(memory_space=pltpu...  25.7 us
    all_to_all x4, starting transfers between devices, on_device(): lax.all_to_all(piece, 'seq', 0, 0, tiled=True)  17.9 us
    ppermute x14, starting transfers between devices, shifted(): lax.ppermute(array, axis, [(i, (i + step) % count) for i in range(count)])  12.8 us
    pallas_call x2, Pallas kernels, reward(): pl.pallas_call(functools.partial(reward_kernel, particles, scale), grid=(...  10.6 us
    pallas_call x2, Pallas kernels, attention(): pl.pallas_call(functools.partial(attention_kernel, head_width, block_sour...  10.4 us
  transfers between devices with their start and end apart: 19, of which 8 were waited for; matrix products, arithmetic and copies ran while one was open for 2% of the time, Pallas kernels for 25%

profile of v2, /device:TPU:0, one launch (start us, length us, event | category | flops | bytes accessed | tf_op | source)
XLA Modules:
  0.0 246.4 jit_solution(11769063226162501508)
XLA Ops:
  7.2 3.8 %pack_heads.2.refs_1_ = bf16[8,3,64,384]{3,2,1,0:T(8,128)(2,1)} custom-call(bf16[4,64,1536]{2,1,0:T(8,128)(2,1)} %q_ref.3, bf16[4,64,1536]{2,1,0:T(8,128)(2,1)} %k_ref.3, bf16[4,64,1536]{2,1,0:T(8,128)(2,1)} %v_ref.3), custom_call_target="tpu_custom_call" | custom-call | tf_op jit(solution)/shard_map/pack_heads/pallas_call | solution.py:34
  10.9 7.3 %all-to-all-start = ((bf16[8,3,64,384]{3,2,1,0:T(8,128)(2,1)}), bf16[8,3,64,384]{3,2,1,0:T(8,128)(2,1)S(1)}, u32[]{:S(2)}, u32[]{:S(2)}) async-start(bf16[8,3,64,384]{3,2,1,0:T(8,128)(2,1)} %pack_heads.2.refs_1_), calls=%async_computation | async-start | bytes 2359296 | tf_op jit(solution)/shard_map/all_to_all | solution.py:391
  18.3 1.7 dynamic_slice.12
  20.0 3.7 %pack_heads.3.refs_1_ = bf16[8,3,64,384]{3,2,1,0:T(8,128)(2,1)} custom-call(bf16[4,64,1536]{2,1,0:T(8,128)(2,1)} %q_ref.3, bf16[4,64,1536]{2,1,0:T(8,128)(2,1)} %k_ref.3, bf16[4,64,1536]{2,1,0:T(8,128)(2,1)} %v_ref.3), custom_call_target="tpu_custom_call" | custom-call | tf_op jit(solution)/shard_map/pack_heads/pallas_call | solution.py:34
  23.7 31.6 %all-to-all-done.qkv_ref = bf16[8,3,64,384]{3,2,1,0:T(8,128)(2,1)S(1)} async-done(((bf16[8,3,64,384]{3,2,1,0:T(8,128)(2,1)}), bf16[8,3,64,384]{3,2,1,0:T(8,128)(2,1)S(1)}, u32[]{:S(2)}, u32[]{:S(2)}) %all-to-all-start) | async-done | bytes 1179680 | tf_op jit(solution)/shard_map/all_to_all | solution.py:391
  55.3 3.6 %all-to-all-start.2 = ((bf16[8,3,64,384]{3,2,1,0:T(8,128)(2,1)}), bf16[8,3,64,384]{3,2,1,0:T(8,128)(2,1)S(1)}, u32[]{:S(2)}, u32[]{:S(2)}) async-start(bf16[8,3,64,384]{3,2,1,0:T(8,128)(2,1)} %pack_heads.3.refs_1_), calls=%async_computation.2 | async-start | bytes 2359296 | tf_op jit(solution)/shard_map/all_to_all | solution.py:391
  58.9 41.9 %all-gather.3.cloned.1.call-done = bf16[4096,256]{1,0:T(8,128)(2,1)} async-done(((bf16[512,256]{1,0:T(8,128)(2,1)}), bf16[4096,256]{1,0:T(8,128)(2,1)}) %all-gather.3.cloned.1.call-update) | async-done | bytes 2097168 | tf_op jit(solution)/shard_map/all_gather | solution.py:388
  100.8 1.5 collective-permute-start.5
  102.3 34.0 %all_gather.9.refs_0_ = bf16[1536,256]{1,0:T(8,128)(2,1)} all-gather(bf16[192,256]{1,0:T(8,128)(2,1)S(1)} %constant_dynamic-slice_fusion.1), channel_id=1, replica_groups=mesh['groups'=2,'dom'=2,'seq'=8] {'seq'}, dimensions={0}, use_global_device_ids=true | all-gather | bytes 884736 | tf_op jit(solution)/shard_map/all_gather | solution.py:382
  136.8 5.2 %attention.2.refs_1_ = bf16[8,64,384]{2,1,0:T(8,128)(2,1)} custom-call(bf16[8,3,64,384]{3,2,1,0:T(8,128)(2,1)S(1)} %all-to-all-done.qkv_ref), custom_call_target="tpu_custom_call" | custom-call | flops 402653184 | bytes 1572864 | tf_op jit(solution)/shard_map/attention/pallas_call | solution.py:96
  142.0 3.5 %all-to-all-start.1 = ((bf16[8,64,384]{2,1,0:T(8,128)(2,1)}), bf16[8,64,384]{2,1,0:T(8,128)(2,1)S(1)}, u32[]{:S(2)}, u32[]{:S(2)}) async-start(bf16[8,64,384]{2,1,0:T(8,128)(2,1)} %attention.2.refs_1_), calls=%async_computation.1 | async-start | bytes 786432 | tf_op jit(solution)/shard_map/all_to_all | solution.py:397
  145.5 5.2 %attention.3 = bf16[8,64,384]{2,1,0:T(8,128)(2,1)} custom-call(bf16[8,3,64,384]{3,2,1,0:T(8,128)(2,1)S(1)} %all-to-all-done.2.qkv_ref), custom_call_target="tpu_custom_call" | custom-call | flops 402653184 | bytes 1572864 | tf_op jit(solution)/shard_map/attention/pallas_call | solution.py:96
  150.7 4.0 %all-to-all-done.1 = bf16[8,64,384]{2,1,0:T(8,128)(2,1)S(1)} async-done(((bf16[8,64,384]{2,1,0:T(8,128)(2,1)}), bf16[8,64,384]{2,1,0:T(8,128)(2,1)S(1)}, u32[]{:S(2)}, u32[]{:S(2)}) %all-to-all-start.1) | async-done | bytes 393248 | tf_op jit(solution)/shard_map/all_to_all | solution.py:397
  154.7 3.6 %all-to-all-start.3 = ((bf16[8,64,384]{2,1,0:T(8,128)(2,1)}), bf16[8,64,384]{2,1,0:T(8,128)(2,1)S(1)}, u32[]{:S(2)}, u32[]{:S(2)}) async-start(bf16[8,64,384]{2,1,0:T(8,128)(2,1)} %attention.3), calls=%async_computation.3 | async-start | bytes 786432 | tf_op jit(solution)/shard_map/all_to_all | solution.py:397
  158.3 7.1 %collective-permute-done.1.refs_0_ = bf16[1536,256]{1,0:T(8,128)(2,1)S(1)} collective-permute-done((bf16[1536,256]{1,0:T(8,128)(2,1)}, bf16[1536,256]{1,0:T(8,128)(2,1)S(1)}, u32[]{:S(2)}, u32[]{:S(2)}) %collective-permute-start.1) | collective-permute-done | bytes 786464 | tf_op jit(solution)/shard_map/ppermute | solution.py:350
  165.4 0.9 copy-done.5
  168.3 2.3 copy-done.1
  170.6 2.7 %project.1 = (bf16[256,1536]{1,0:T(8,128)(2,1)S(1)}, bf16[4,64,1536]{2,1,0:T(8,128)(2,1)S(1)}) custom-call(f32[1]{0:T(128)S(6)} %div.19.sigma_ref, bf16[4,64,1536]{2,1,0:T(8,128)(2,1)S(1)} %copy-done.2, bf16[1536,1536]{1,0:T(8,128)(2,1)S(1)} %copy-done.1, bf16[4,2,64,384]{3,2,1,0:T(8,128)(2,1)S(1)} %bitcast.11, bf16[4,2,64,384]{3,2,1,0:T(8,128)(2,1)S(1)} %bitcast.12), custom_call_target="tpu_custom_call" | custom-call | flops 1207959552 | bytes 7864320 | tf_op jit(solution)/shard_map/project/pallas_call | solution.py:141
  174.2 0.9 copy-done.7
  175.2 6.2 %embed_norm.1.features_ref = bf16[2,256,512]{2,1,0:T(8,128)(2,1)} custom-call(s32[4]{0:T(128)} %add.68.order_ref, bf16[256,1536]{1,0:T(8,128)(2,1)} %copy-done.4, f32[1,1024]{1,0:T(1,128)} %bitcast.14, bf16[1536,256]{1,0:T(8,128)(2,1)} %gate.5.refs_0_, bf16[1536,256]{1,0:T(8,128)(2,1)} %gate.6.refs_1_, bf16[1536,256]{1,0:T(8,128)(2,1)} %collective-permute-done.2.refs_2_, ...), custom_call_target="tpu_custom_call" | custom-call | flops 805306368 | bytes 4456448 | tf_op jit(solution)/shard_map/embed_norm/pallas_call | solution.py:205
  183.2 5.3 %reward.2 = f32[1,1,128]{2,1,0:T(1,128)} custom-call(s32[2]{0:T(128)} %copy-done.10, bf16[2,256,512]{2,1,0:T(8,128)(2,1)} %embed_norm.1.features_ref, f32[8,1,256]{2,1,0:T(1,128)} %constant_dynamic-slice_fusion.head_ref, f32[1,1,128]{2,1,0:T(1,128)} %pad.5.before_ref, bf16[8,512,256]{2,1,0:T(8,128)(2,1)} %gate.7.refs_0_, ...), custom_call_target="tpu_custom_call" | custom-call | flops 1073741824 | bytes 4194304 | tf_op jit(solution)/shard_map/reward/pallas_call | solution.py:267
  188.6 1.2 concatenate.3.before_ref
  190.5 5.3 %reward.3.refs_0_ = f32[2,1,128]{2,1,0:T(1,128)} custom-call(s32[2]{0:T(128)} %copy-done.10, bf16[2,256,512]{2,1,0:T(8,128)(2,1)} %copy-done.8, f32[8,1,256]{2,1,0:T(1,128)} %constant_dynamic-slice_fusion.head_ref, f32[2,1,128]{2,1,0:T(1,128)} %concatenate.3.before_ref, bf16[8,512,256]{2,1,0:T(8,128)(2,1)} %gate.7.refs_0_, ...), custom_call_target="tpu_custom_call" | custom-call | flops 1073741824 | bytes 4194304 | tf_op jit(solution)/shard_map/reward/pallas_call | solution.py:267
  195.9 2.5 %collective-permute-start.11 = (f32[2,1,128]{2,1,0:T(1,128)}, f32[2,1,128]{2,1,0:T(1,128)S(1)}, u32[]{:S(2)}, u32[]{:S(2)}) collective-permute-start(f32[2,1,128]{2,1,0:T(1,128)} %reward.3.refs_0_), channel_id=1, source_target_pairs={{0,6},{1,7},{2,0},{3,1},{4,2},{5,3},{6,4},{7,5},{8,14},{9,15},{10,... | collective-permute-start | bytes 3080 | tf_op jit(solution)/shard_map/ppermute | solution.py:350
  198.8 1.6 collective-permute-start.6
  200.6 3.3 %collective-permute-start.8 = (f32[2,1,128]{2,1,0:T(1,128)}, f32[2,1,128]{2,1,0:T(1,128)S(1)}, u32[]{:S(2)}, u32[]{:S(2)}) collective-permute-start(f32[2,1,128]{2,1,0:T(1,128)} %reward.3.refs_0_), channel_id=1, source_target_pairs={{0,3},{1,4},{2,5},{3,6},{4,7},{5,0},{6,1},{7,2},{8,11},{9,12},{10,... | collective-permute-start | bytes 3080 | tf_op jit(solution)/shard_map/ppermute | solution.py:350
  203.8 1.9 collective-permute-start.9
  206.2 2.3 collective-permute-done.9.refs_4_
  209.1 1.3 add_partials.1.mine_ref
  211.0 0.9 copy-done.6
  211.9 25.7 %resample.1 = bf16[4,64,1536]{2,1,0:T(8,128)(2,1)} custom-call(s32[2,4]{1,0:T(2,128)} %pad_add_fusion.place_ref, bf16[4,64,1536]{2,1,0:T(8,128)(2,1)} %copy-done.3, bf16[4,64,1536]{2,1,0:T(8,128)(2,1)} %copy-done.6), custom_call_target="tpu_custom_call" | custom-call | tf_op jit(solution)/shard_map/resample/pallas_call | solution.py:338
  238.2 1.4 log_weights.1
  (79 shorter events, 8.2 us)
Async XLA Ops:
  7.2 51.7 %copy-start = (bf16[192,1024]{1,0:T(8,128)(2,1)S(1)}, bf16[192,1024]{1,0:T(8,128)(2,1)}, u32[]{:S(2)}) copy-start(bf16[192,1024]{1,0:T(8,128)(2,1)} %param.18) | copy-start | bytes 1179652
  10.9 44.3 %all-to-all-start = ((bf16[8,3,64,384]{3,2,1,0:T(8,128)(2,1)}), bf16[8,3,64,384]{3,2,1,0:T(8,128)(2,1)S(1)}, u32[]{:S(2)}, u32[]{:S(2)}) async-start(bf16[8,3,64,384]{3,2,1,0:T(8,128)(2,1)} %pack_heads.2.refs_1_), calls=%async_computation | async-start | bytes 2359296 | tf_op jit(solution)/shard_map/all_to_all | solution.py:391
  18.2 82.6 %all-gather.3.cloned.1.call-start = ((), (), s32[]{:S(2)}) async-start(), calls=%async_computation.4 | async-start | bytes 2359296 | tf_op jit(solution)/shard_map/all_gather | solution.py:388
  55.3 86.7 %all-to-all-start.2 = ((bf16[8,3,64,384]{3,2,1,0:T(8,128)(2,1)}), bf16[8,3,64,384]{3,2,1,0:T(8,128)(2,1)S(1)}, u32[]{:S(2)}, u32[]{:S(2)}) async-start(bf16[8,3,64,384]{3,2,1,0:T(8,128)(2,1)} %pack_heads.3.refs_1_), calls=%async_computation.2 | async-start | bytes 2359296 | tf_op jit(solution)/shard_map/all_to_all | solution.py:391
  100.8 82.4 %collective-permute-start.5 = (bf16[8,512,256]{2,1,0:T(8,128)(2,1)}, bf16[8,512,256]{2,1,0:T(8,128)(2,1)}, u32[]{:S(2)}, u32[]{:S(2)}) collective-permute-start(bf16[8,512,256]{2,1,0:T(8,128)(2,1)} %gate.7.refs_0_), channel_id=1, source_target_pairs={{0,16},{16,0},{1,17},{17,1},{2,18},{18,2},{3,19},{19,3},{4,20},{20... | collective-permute-start | bytes 6291464 | tf_op jit(solution)/shard_map/ppermute | solution.py:350
  136.3 29.2 %collective-permute-start.1 = (bf16[1536,256]{1,0:T(8,128)(2,1)}, bf16[1536,256]{1,0:T(8,128)(2,1)S(1)}, u32[]{:S(2)}, u32[]{:S(2)}) collective-permute-start(bf16[1536,256]{1,0:T(8,128)(2,1)} %gate.4.refs_0_), channel_id=1, source_target_pairs={{0,16},{16,0},{1,17},{17,1},{2,18},{18,2},{3,19},{19,3},{4,20},{20... | collective-permute-start | bytes 2359304 | tf_op jit(solution)/shard_map/ppermute | solution.py:350
  142.0 12.7 %all-to-all-start.1 = ((bf16[8,64,384]{2,1,0:T(8,128)(2,1)}), bf16[8,64,384]{2,1,0:T(8,128)(2,1)S(1)}, u32[]{:S(2)}, u32[]{:S(2)}) async-start(bf16[8,64,384]{2,1,0:T(8,128)(2,1)} %attention.2.refs_1_), calls=%async_computation.1 | async-start | bytes 786432 | tf_op jit(solution)/shard_map/all_to_all | solution.py:397
  154.7 13.6 %all-to-all-start.3 = ((bf16[8,64,384]{2,1,0:T(8,128)(2,1)}), bf16[8,64,384]{2,1,0:T(8,128)(2,1)S(1)}, u32[]{:S(2)}, u32[]{:S(2)}) async-start(bf16[8,64,384]{2,1,0:T(8,128)(2,1)} %attention.3), calls=%async_computation.3 | async-start | bytes 786432 | tf_op jit(solution)/shard_map/all_to_all | solution.py:397
  158.3 9.9 %copy-start.2 = (bf16[4,64,1536]{2,1,0:T(8,128)(2,1)S(1)}, bf16[4,64,1536]{2,1,0:T(8,128)(2,1)}, u32[]{:S(2)}) copy-start(bf16[4,64,1536]{2,1,0:T(8,128)(2,1)} %latents_ref.1) | copy-start | bytes 2359300
  166.3 7.9 %collective-permute-start.3 = (bf16[1536,256]{1,0:T(8,128)(2,1)}, bf16[1536,256]{1,0:T(8,128)(2,1)S(1)}, u32[]{:S(2)}, u32[]{:S(2)}) collective-permute-start(bf16[1536,256]{1,0:T(8,128)(2,1)} %gate.6.refs_1_), channel_id=1, source_target_pairs={{0,8},{8,0},{1,9},{9,1},{2,10},{10,2},{3,11},{11,3},{4,12},{12,4},... | collective-permute-start | bytes 2359304 | tf_op jit(solution)/shard_map/ppermute | solution.py:350
  166.3 7.9 %collective-permute-start.2 = (bf16[1536,256]{1,0:T(8,128)(2,1)}, bf16[1536,256]{1,0:T(8,128)(2,1)}, u32[]{:S(2)}, u32[]{:S(2)}) collective-permute-start(bf16[1536,256]{1,0:T(8,128)(2,1)} %gate.5.refs_0_), channel_id=1, source_target_pairs={{0,8},{8,0},{1,9},{9,1},{2,10},{10,2},{3,11},{11,3},{4,12},{12,4},... | collective-permute-start | bytes 2359304 | tf_op jit(solution)/shard_map/ppermute | solution.py:350
  166.8 6.5 %copy-start.10 = (s32[2]{0:T(128)}, s32[2]{0:T(128)S(1)}, u32[]{:S(2)}) copy-start(s32[2]{0:T(128)S(1)} %and_select_fusion.1.order_ref) | copy-start | bytes 28
  174.2 7.3 %copy-start.3 = (bf16[4,64,1536]{2,1,0:T(8,128)(2,1)}, bf16[4,64,1536]{2,1,0:T(8,128)(2,1)S(1)}, u32[]{:S(2)}) copy-start(bf16[4,64,1536]{2,1,0:T(8,128)(2,1)S(1)} %get-tuple-element.4.own_ref) | copy-start | bytes 2359300
  175.2 6.3 %copy-start.9 = (f32[4096]{0:T(1024)S(1)}, f32[4096]{0:T(1024)}, u32[]{:S(2)}) copy-start(f32[4096]{0:T(1024)} %param.21) | copy-start | bytes 49156
  175.2 6.3 %copy-start.19 = (f32[4]{0:T(128)S(1)}, f32[4]{0:T(128)}, u32[]{:S(2)}) copy-start(f32[4]{0:T(128)} %param.22) | copy-start | bytes 52
  181.4 8.3 %collective-permute-start.4 = (bf16[2,256,512]{2,1,0:T(8,128)(2,1)}, bf16[2,256,512]{2,1,0:T(8,128)(2,1)S(1)}, u32[]{:S(2)}, u32[]{:S(2)}) collective-permute-start(bf16[2,256,512]{2,1,0:T(8,128)(2,1)} %embed_norm.1.features_ref), channel_id=1, source_target_pairs={{0,8},{8,0},{1,9},{9,1},{2,10},{10,2},{3,11},{11,3},{4,12},{12,4},... | collective-permute-start | bytes 1572872 | tf_op jit(solution)/shard_map/ppermute | solution.py:350
  181.6 29.5 %collective-permute-start = (bf16[4,64,1536]{2,1,0:T(8,128)(2,1)S(1)}, bf16[4,64,1536]{2,1,0:T(8,128)(2,1)S(1)}, u32[]{:S(2)}, u32[]{:S(2)}) collective-permute-start(bf16[4,64,1536]{2,1,0:T(8,128)(2,1)S(1)} %get-tuple-element.4.own_ref), channel_id=1, source_target_pairs={{0,8},{8,0},{1,9},{9,1},{2,10},{10,2},{3,11},{11,3},{4,12},{12,4},... | collective-permute-start | bytes 2359304 | tf_op jit(solution)/shard_map/ppermute | solution.py:350
  189.7 9.1 %copy-start.20 = (s32[4]{0:T(128)S(1)}, s32[4]{0:T(128)}, u32[]{:S(2)}) copy-start(s32[4]{0:T(128)} %param.23) | copy-start | bytes 52
  195.9 4.7 %collective-permute-start.10 = (f32[2,1,128]{2,1,0:T(1,128)}, f32[2,1,128]{2,1,0:T(1,128)S(1)}, u32[]{:S(2)}, u32[]{:S(2)}) collective-permute-start(f32[2,1,128]{2,1,0:T(1,128)} %reward.3.refs_0_), channel_id=1, source_target_pairs={{0,5},{1,6},{2,7},{3,0},{4,1},{5,2},{6,3},{7,4},{8,13},{9,14},{10,... | collective-permute-start | bytes 3080 | tf_op jit(solution)/shard_map/ppermute | solution.py:350
  195.9 4.7 %collective-permute-start.11 = (f32[2,1,128]{2,1,0:T(1,128)}, f32[2,1,128]{2,1,0:T(1,128)S(1)}, u32[]{:S(2)}, u32[]{:S(2)}) collective-permute-start(f32[2,1,128]{2,1,0:T(1,128)} %reward.3.refs_0_), channel_id=1, source_target_pairs={{0,6},{1,7},{2,0},{3,1},{4,2},{5,3},{6,4},{7,5},{8,14},{9,15},{10,... | collective-permute-start | bytes 3080 | tf_op jit(solution)/shard_map/ppermute | solution.py:350
  198.3 5.5 %collective-permute-start.12 = (f32[2,1,128]{2,1,0:T(1,128)}, f32[2,1,128]{2,1,0:T(1,128)S(1)}, u32[]{:S(2)}, u32[]{:S(2)}) collective-permute-start(f32[2,1,128]{2,1,0:T(1,128)} %reward.3.refs_0_), channel_id=1, source_target_pairs={{0,7},{1,0},{2,1},{3,2},{4,3},{5,4},{6,5},{7,6},{8,15},{9,8},{10,9... | collective-permute-start | bytes 3080 | tf_op jit(solution)/shard_map/ppermute | solution.py:350
  198.8 6.9 %collective-permute-start.6 = (f32[2,1,128]{2,1,0:T(1,128)}, f32[2,1,128]{2,1,0:T(1,128)S(1)}, u32[]{:S(2)}, u32[]{:S(2)}) collective-permute-start(f32[2,1,128]{2,1,0:T(1,128)} %reward.3.refs_0_), channel_id=1, source_target_pairs={{0,1},{1,2},{2,3},{3,4},{4,5},{5,6},{6,7},{7,0},{8,9},{9,10},{10,1... | collective-permute-start | bytes 3080 | tf_op jit(solution)/shard_map/ppermute | solution.py:350
  200.5 8.0 %copy-start.11 = (f32[2,1,128]{2,1,0:T(1,128)}, f32[2,1,128]{2,1,0:T(1,128)S(1)}, u32[]{:S(2)}) copy-start(f32[2,1,128]{2,1,0:T(1,128)S(1)} %collective-permute-done.10.refs_5_) | copy-start | bytes 3076
  200.5 5.6 %collective-permute-start.7 = (f32[2,1,128]{2,1,0:T(1,128)}, f32[2,1,128]{2,1,0:T(1,128)S(1)}, u32[]{:S(2)}, u32[]{:S(2)}) collective-permute-start(f32[2,1,128]{2,1,0:T(1,128)} %reward.3.refs_0_), channel_id=1, source_target_pairs={{0,2},{1,3},{2,4},{3,5},{4,6},{5,7},{6,0},{7,1},{8,10},{9,11},{10,... | collective-permute-start | bytes 3080 | tf_op jit(solution)/shard_map/ppermute | solution.py:350
  200.6 8.0 %copy-start.12 = (f32[2,1,128]{2,1,0:T(1,128)}, f32[2,1,128]{2,1,0:T(1,128)S(1)}, u32[]{:S(2)}) copy-start(f32[2,1,128]{2,1,0:T(1,128)S(1)} %collective-permute-done.11.refs_6_) | copy-start | bytes 3076
  200.6 5.6 %collective-permute-start.8 = (f32[2,1,128]{2,1,0:T(1,128)}, f32[2,1,128]{2,1,0:T(1,128)S(1)}, u32[]{:S(2)}, u32[]{:S(2)}) collective-permute-start(f32[2,1,128]{2,1,0:T(1,128)} %reward.3.refs_0_), channel_id=1, source_target_pairs={{0,3},{1,4},{2,5},{3,6},{4,7},{5,0},{6,1},{7,2},{8,11},{9,12},{10,... | collective-permute-start | bytes 3080 | tf_op jit(solution)/shard_map/ppermute | solution.py:350
  203.8 4.7 %copy-start.13 = (f32[2,1,128]{2,1,0:T(1,128)}, f32[2,1,128]{2,1,0:T(1,128)S(1)}, u32[]{:S(2)}) copy-start(f32[2,1,128]{2,1,0:T(1,128)S(1)} %collective-permute-done.12.refs_7_) | copy-start | bytes 3076
  203.8 4.7 %collective-permute-start.9 = (f32[2,1,128]{2,1,0:T(1,128)}, f32[2,1,128]{2,1,0:T(1,128)S(1)}, u32[]{:S(2)}, u32[]{:S(2)}) collective-permute-start(f32[2,1,128]{2,1,0:T(1,128)} %reward.3.refs_0_), channel_id=1, source_target_pairs={{0,4},{1,5},{2,6},{3,7},{4,0},{5,1},{6,2},{7,3},{8,12},{9,13},{10,... | collective-permute-start | bytes 3080 | tf_op jit(solution)/shard_map/ppermute | solution.py:350
  205.7 2.8 %copy-start.14 = (f32[2,1,128]{2,1,0:T(1,128)}, f32[2,1,128]{2,1,0:T(1,128)S(1)}, u32[]{:S(2)}) copy-start(f32[2,1,128]{2,1,0:T(1,128)S(1)} %collective-permute-done.6.refs_1_) | copy-start | bytes 3076
  206.1 2.4 copy-start.15
  206.2 2.3 copy-start.16
  210.4 27.1 %collective-permute-start.13 = (f32[2,1,128]{2,1,0:T(1,128)}, f32[2,1,128]{2,1,0:T(1,128)S(1)}, u32[]{:S(2)}, u32[]{:S(2)}) collective-permute-start(f32[2,1,128]{2,1,0:T(1,128)} %add_partials.1.mine_ref), channel_id=1, source_target_pairs={{0,8},{8,0},{1,9},{9,1},{2,10},{10,2},{3,11},{11,3},{4,12},{12,4},... | collective-permute-start | bytes 3080 | tf_op jit(solution)/shard_map/ppermute | solution.py:350
  (8 other events, 7.9 us)
Sparse Core Ops, SparseCore 0:
  21.7 79.0 all-gather.2

commit v3 on v2

v3 whole, which is shorter than its diff:
```python
import functools
import math

import jax
import jax.numpy as jnp
from jax import lax
from jax.experimental import pallas as pl
from jax.experimental.pallas import tpu as pltpu
from jax.sharding import PartitionSpec as P

HEADS = 24
STEPS = 28
LANES = 128

potential_scale = 4.0
norm_eps = 1e-05
MIB = 1024 * 1024


def pack_kernel(q_ref, k_ref, v_ref, out_ref):
    for index, ref in enumerate((q_ref, k_ref, v_ref)):
        out_ref[:, 0, index] = ref[...]


def pack_whole_kernel(width, q_ref, k_ref, v_ref, out_ref):
    for index, ref in enumerate((q_ref, k_ref, v_ref)):
        for block in range(out_ref.shape[1]):
            out_ref[:, block, index] = ref[:, :, block * width : (block + 1) * width]


def pack(queries, keys, values, chunks, width, chunk):
    particles, tokens, model_width = queries.shape
    blocks = model_width // width
    part = width // chunks
    out_shape = jax.ShapeDtypeStruct((particles, blocks, 3, tokens, part), queries.dtype)
    params = pltpu.CompilerParams(vmem_limit_bytes=60 * MIB)
    if part % LANES == 0:
        in_spec = pl.BlockSpec((particles, tokens, part), lambda i: (0, 0, i * chunks + chunk))
        packed = pl.pallas_call(
            pack_kernel,
            grid=(blocks,),
            in_specs=[in_spec] * 3,
            out_specs=pl.BlockSpec((particles, 1, 3, tokens, part), lambda i: (0, i, 0, 0, 0)),
            out_shape=out_shape,
            compiler_params=params,
            name="pack_heads",
        )(queries, keys, values)
    else:
        packed = pl.pallas_call(
            functools.partial(pack_whole_kernel, width),
            out_shape=out_shape,
            compiler_params=params,
            name="pack_heads",
        )(queries, keys, values)
    return packed.reshape(particles * blocks, 3, tokens, part)


def gate_kernel(*refs):
    pass


def gate(arrays, after):
    anywhere = pl.BlockSpec(memory_space=pl.ANY)
    return list(
        pl.pallas_call(
        gate_kernel,
        in_specs=[anywhere] * (len(arrays) + 1),
        out_specs=[anywhere] * len(arrays),
        out_shape=[jax.ShapeDtypeStruct(array.shape, array.dtype) for array in arrays],
        input_output_aliases={index: index for index in range(len(arrays))},
        name="gate",
    )(*arrays, after)
    )


def attention_kernel(head_width, block_sources, qkv_ref, out_ref):
    sources, _, tokens, columns = qkv_ref.shape
    total = sources * tokens
    rows = block_sources * tokens
    factor = 1.0 / math.sqrt(head_width) / math.log(2.0)

    def one_block(block, carry):
        span = pl.ds(block * block_sources, block_sources)
        q_all = qkv_ref[span, 0].reshape(rows, columns)
        pieces = []
        for head in range(columns // head_width):
            cols = slice(head * head_width, (head + 1) * head_width)
            k_head = qkv_ref[:, 1, :, cols].reshape(total, head_width)
            v_head = qkv_ref[:, 2, :, cols].reshape(total, head_width)
            scores = lax.dot_general(
                q_all[:, cols], k_head, (((1,), (1,)), ((), ())), preferred_element_type=jnp.float32
            )
            highest = jnp.max(scores, axis=1, keepdims=True)
            expanded = jnp.exp2((scores - highest) * factor)
            norm = 1.0 / jnp.sum(expanded, axis=1, keepdims=True)
            weights = (expanded * norm).astype(jnp.bfloat16)
            pieces.append(jnp.dot(weights, v_head, preferred_element_type=jnp.float32))
        joined = jnp.concatenate(pieces, axis=1).astype(jnp.bfloat16)
        out_ref[span] = joined.reshape(block_sources, tokens, columns)
        return carry

    lax.fori_loop(0, sources // block_sources, one_block, 0)


def attention(qkv, head_width):
    sources, _, tokens, columns = qkv.shape
    total = sources * tokens
    block_sources = max(1, min(sources, 512 // tokens))
    while sources % block_sources:
        block_sources -= 1
    heads = columns // head_width
    step = LANES if columns % LANES == 0 and LANES % head_width == 0 else columns
    return pl.pallas_call(
        functools.partial(attention_kernel, head_width, block_sources),
        grid=(columns // step,),
        in_specs=[pl.BlockSpec((sources, 3, tokens, step), lambda i: (0, 0, 0, i))],
        out_specs=pl.BlockSpec((sources, tokens, step), lambda i: (0, 0, i)),
        out_shape=jax.ShapeDtypeStruct((sources, tokens, columns), jnp.bfloat16),
        compiler_params=pltpu.CompilerParams(vmem_limit_bytes=60 * MIB),
        cost_estimate=pl.CostEstimate(
            flops=4 * total * total * columns,
            bytes_accessed=8 * total * columns,
            transcendentals=heads * total * total,
        ),
        name="attention",
    )(qkv)


def project_kernel(chunks, width, sigma_ref, latents_ref, weight_ref, *refs):
    attended_refs, (clean_ref, stepped_ref) = refs[:chunks], refs[chunks:]
    particles, tokens, columns = latents_ref.shape
    rows = particles * tokens
    depth = weight_ref.shape[0]
    part = width // chunks
    total = jnp.zeros((rows, columns), jnp.float32)
    for block in range(depth // width):
        for chunk in range(chunks):
            start = block * width + chunk * part
            piece = attended_refs[chunk][:, block].reshape(rows, part)
            total += jnp.dot(
                piece, weight_ref[start : start + part, :], preferred_element_type=jnp.float32
            )
    flat = latents_ref[...].reshape(rows, columns).astype(jnp.float32)
    velocity = flat + total
    clean_ref[...] = (flat - sigma_ref[0] * velocity).astype(jnp.bfloat16)
    stepped_ref[...] = (
        (flat - velocity * (1.0 / STEPS)).astype(jnp.bfloat16).reshape(particles, tokens, columns)
    )


def project(sigma, latents, out_weight, attended, width):
    particles, tokens, model_width = latents.shape
    rows = particles * tokens
    blocks = model_width // width
    chunks = len(attended)
    part = width // chunks
    columns = 512 if model_width % 512 == 0 else model_width
    attended = [piece.reshape(particles, blocks, tokens, part) for piece in attended]
    return pl.pallas_call(
        functools.partial(project_kernel, chunks, width),
        grid=(model_width // columns,),
        in_specs=[
            pl.BlockSpec(memory_space=pltpu.SMEM),
            pl.BlockSpec((particles, tokens, columns), lambda i: (0, 0, i)),
            pl.BlockSpec((model_width, columns), lambda i: (0, i)),
        ]
        + [pl.BlockSpec((particles, blocks, tokens, part), lambda i: (0, 0, 0, 0))] * chunks,
        out_specs=[
            pl.BlockSpec((rows, columns), lambda i: (0, i)),
            pl.BlockSpec((particles, tokens, columns), lambda i: (0, 0, i)),
        ],
        out_shape=[
            jax.ShapeDtypeStruct((rows, model_width), jnp.bfloat16),
            jax.ShapeDtypeStruct((particles, tokens, model_width), jnp.bfloat16),
        ],
        compiler_params=pltpu.CompilerParams(vmem_limit_bytes=60 * MIB),
        cost_estimate=pl.CostEstimate(
            flops=2 * rows * model_width * model_width,
            bytes_accessed=2 * model_width * model_width + 8 * rows * model_width,
            transcendentals=0,
        ),
        name="project",
    )(sigma, latents, out_weight, *attended)


def embed_kernel(order_ref, place_ref, clean_ref, gain_ref, *refs):
    parts = order_ref.shape[0]
    weight_refs, (features_ref, weight_vmem, embedded_ref, sems) = refs[:parts], refs[parts:]
    shards, depth, columns = weight_refs[0].shape
    copies = []
    for index in range(parts):
        for shard in range(shards):
            start = pl.multiple_of(place_ref[shard] * depth, depth)
            copy = pltpu.make_async_copy(
                weight_refs[index].at[shard],
                weight_vmem.at[index, pl.ds(start, depth)],
                sems.at[index],
            )
            copy.start()
            copies.append(copy)
    for index in range(parts):
        for copy in copies[index * shards : (index + 1) * shards]:
            copy.wait()
        embedded_ref[order_ref[index]] = jnp.dot(
            clean_ref[...], weight_vmem[index], preferred_element_type=jnp.float32
        )
    count = parts * columns
    blocks = [embedded_ref[index] for index in range(parts)]
    centre = sum(jnp.sum(block, axis=1, keepdims=True) for block in blocks) * (1.0 / count)
    blocks = [block - centre for block in blocks]
    variance = sum(jnp.sum(block * block, axis=1, keepdims=True) for block in blocks) * (
        1.0 / count
    )
    inverse = lax.rsqrt(variance + norm_eps)
    share = features_ref.shape[2]
    for index, block in enumerate(blocks):
        cols = slice(index * columns, (index + 1) * columns)
        piece = jax.nn.gelu(block * inverse * gain_ref[:, cols]).astype(jnp.bfloat16)
        start = index * columns % share
        features_ref[index * columns // share, :, start : start + columns] = piece


def embed(order, place, clean, weights, gain, depth_parts):
    parts = len(weights)
    shards, shard_depth, columns = weights[0].shape
    depth = shards * shard_depth
    rows = clean.shape[0]
    count = parts * columns
    vmem = pl.BlockSpec(memory_space=pltpu.VMEM)
    smem = pl.BlockSpec(memory_space=pltpu.SMEM)
    return pl.pallas_call(
        embed_kernel,
        in_specs=[smem, smem, vmem, vmem] + [pl.BlockSpec(memory_space=pl.ANY)] * parts,
        out_specs=vmem,
        out_shape=jax.ShapeDtypeStruct((depth_parts, rows, count // depth_parts), jnp.bfloat16),
        scratch_shapes=[
            pltpu.VMEM((parts, depth, columns), jnp.bfloat16),
            pltpu.VMEM((parts, rows, columns), jnp.float32),
            pltpu.SemaphoreType.DMA((parts,)),
        ],
        compiler_params=pltpu.CompilerParams(vmem_limit_bytes=60 * MIB),
        cost_estimate=pl.CostEstimate(
            flops=2 * rows * depth * count,
            bytes_accessed=2 * depth * count + 2 * rows * (depth + count),
            transcendentals=rows * count,
        ),
        name="embed_norm",
    )(order, place, clean, gain.reshape(1, count), *weights)


def reward_kernel(particles, scale, parts, offset, *refs):
    order_ref, place_ref, features_ref, head_ref, before_ref = refs[:5]
    weight_refs, (out_ref, total_ref) = refs[5:-2], refs[-2:]
    step = pl.program_id(0)
    rows = features_ref.shape[1]
    columns = weight_refs[0].shape[2]

    @pl.when(step == 0)
    def _():
        total_ref[...] = jnp.zeros_like(total_ref)

    for group in range(len(weight_refs) // parts):
        hidden = sum(
            jnp.dot(
                features_ref[order_ref[index]],
                weight_refs[group * parts + index][0],
                preferred_element_type=jnp.float32,
            )
            for index in range(parts)
        )
        shard = place_ref[group * pl.num_programs(0) + step]
        scored = jax.nn.gelu(hidden) * head_ref[shard]
        total_ref[...] += jnp.sum(scored.reshape(particles, rows // particles, columns), axis=1)

    @pl.when(step == pl.num_programs(0) - 1)
    def _():
        sums = jnp.sum(total_ref[...], axis=1, keepdims=True) * scale
        out_rows = lax.broadcasted_iota(jnp.int32, before_ref.shape, 0)
        lanes = lax.broadcasted_iota(jnp.int32, before_ref.shape, 1)
        row = order_ref[parts] if offset == 0 else order_ref[parts + 1]
        logits = before_ref[...]
        for particle in range(particles):
            here = jnp.logical_and(out_rows == row, lanes == particle)
            logits += jnp.where(here, sums[particle : particle + 1], 0.0)
        out_ref[...] = jnp.broadcast_to(logits[None], out_ref.shape)


def reward(order, place, features, weights, parts, head, before, particles, scale, offset, copies):
    shards, depth, columns = weights[0].shape
    rows = features.shape[1]
    count = shards * len(weights) // parts
    smem = pl.BlockSpec(memory_space=pltpu.SMEM)
    return pl.pallas_call(
        functools.partial(reward_kernel, particles, scale, parts, offset),
        grid=(shards,),
        in_specs=[
            smem,
            smem,
            pl.BlockSpec(features.shape, lambda i: (0, 0, 0)),
            pl.BlockSpec(head.shape, lambda i: (0, 0, 0)),
            pl.BlockSpec(before.shape, lambda i: (0, 0)),
        ]
        + [pl.BlockSpec((1, depth, columns), lambda i: (i, 0, 0))] * len(weights),
        out_specs=pl.BlockSpec((copies, *before.shape), lambda i: (0, 0, 0)),
        out_shape=jax.ShapeDtypeStruct((copies, *before.shape), jnp.float32),
        scratch_shapes=[pltpu.VMEM((particles, columns), jnp.float32)],
        compiler_params=pltpu.CompilerParams(vmem_limit_bytes=60 * MIB),
        cost_estimate=pl.CostEstimate(
            flops=2 * rows * parts * depth * count * columns,
            bytes_accessed=2 * parts * depth * count * columns,
            transcendentals=rows * count * columns,
        ),
        name="reward",
    )(order, place, features, head, before, *weights)


def finish_kernel(particles, doms, row_ref, parts_ref, out_ref):
    logits = jnp.sum(parts_ref[...], axis=0)
    rows = lax.broadcasted_iota(jnp.int32, logits.shape, 0)
    lanes = lax.broadcasted_iota(jnp.int32, logits.shape, 1)
    valid = jnp.logical_and(rows < doms, lanes < particles)
    highest = jnp.max(jnp.where(valid, logits, -jnp.inf))
    total = jnp.sum(jnp.where(valid, jnp.exp(logits - highest), 0.0), axis=1, keepdims=True)
    log_total = highest + jnp.log(jnp.sum(total, axis=0, keepdims=True))
    own = jnp.sum(jnp.where(rows == row_ref[0], logits, 0.0), axis=0, keepdims=True)
    out_ref[...] = (own - log_total)[:, :particles]


def finish(row, parts, particles, doms):
    vmem = pl.BlockSpec(memory_space=pltpu.VMEM)
    return pl.pallas_call(
        functools.partial(finish_kernel, particles, doms),
        in_specs=[pl.BlockSpec(memory_space=pltpu.SMEM), vmem],
        out_specs=vmem,
        out_shape=jax.ShapeDtypeStruct((1, particles), jnp.float32),
        name="log_weights",
    )(row, parts).reshape(particles)


def resample_kernel(place_ref, own_ref, other_ref, out_ref):
    index = pl.program_id(0)

    @pl.when(place_ref[0, index] == 0)
    def _():
        out_ref[...] = own_ref[...]

    @pl.when(place_ref[0, index] != 0)
    def _():
        out_ref[...] = other_ref[...]


def resample(place, own, other):
    particles, tokens, columns = own.shape
    block = (1, tokens, columns)
    return pl.pallas_call(
        resample_kernel,
        grid_spec=pltpu.PrefetchScalarGridSpec(
            num_scalar_prefetch=1,
            grid=(particles,),
            in_specs=[
                pl.BlockSpec(block, lambda i, place: (place[1, i], 0, 0)),
                pl.BlockSpec(block, lambda i, place: (place[2, i], 0, 0)),
            ],
            out_specs=pl.BlockSpec(block, lambda i, place: (i, 0, 0)),
        ),
        out_shape=jax.ShapeDtypeStruct(own.shape, own.dtype),
        compiler_params=pltpu.CompilerParams(vmem_limit_bytes=60 * MIB),
        name="resample",
    )(place, own, other)


def shifted(array, axis, step):
    count = lax.axis_size(axis)
    return lax.ppermute(array, axis, [(i, (i + step) % count) for i in range(count)])


def swapped(array, axis, bit):
    return lax.ppermute(array, axis, [(i, i ^ bit) for i in range(lax.axis_size(axis))])


def on_device(
    latents,
    queries,
    keys,
    values,
    out_weight,
    step_index,
    embed_weight,
    norm_gain,
    up_weight,
    head_weight,
    prev_logw,
    ancestors,
):
    seq_count = lax.axis_size("seq")
    group_count = lax.axis_size("groups")
    dom_count = lax.axis_size("dom")
    holders = group_count * dom_count
    dom = lax.axis_index("dom")
    group = lax.axis_index("groups")
    seq = lax.axis_index("seq")
    particles, tokens, model_width = latents.shape
    head_width = model_width // HEADS
    width = particles * model_width // seq_count
    chunks = 2 if width % (2 * LANES) == 0 else 1

    embed_columns = embed_weight.shape[1] // holders
    embed_share = lax.dynamic_slice_in_dim(
        embed_weight, (dom * group_count + group) * embed_columns, embed_columns, 1
    )[None]
    up_depth = up_weight.shape[0] // group_count
    up_columns = up_weight.shape[1] // dom_count
    up_share = lax.dynamic_slice(
        up_weight, (group * up_depth, dom * up_columns), (up_depth, up_columns)
    )[None]
    bits = [1 << place for place in reversed(range(1, seq_count.bit_length() - 1))]
    offsets = [0]
    for bit in bits[:-1]:
        embed_share = jnp.concatenate([embed_share, swapped(embed_share, "seq", bit)])
        up_share = jnp.concatenate([up_share, swapped(up_share, "seq", bit)])
        offsets = offsets + [offset ^ bit for offset in offsets]

    packed = [pack(queries, keys, values, chunks, width, chunk) for chunk in range(chunks)]
    arrived = [lax.all_to_all(piece, "seq", 0, 0, tiled=True) for piece in packed]
    attended = [attention(piece, head_width) for piece in arrived]
    returned = [lax.all_to_all(piece, "seq", 0, 0, tiled=True) for piece in attended]

    embed_share, up_near = gate([embed_share, up_share], packed[-1])
    embed_share = jnp.concatenate([embed_share, swapped(embed_share, "seq", bits[-1])])
    up_far = swapped(up_near, "seq", bits[-1])
    near, far = offsets, [offset ^ bits[-1] for offset in offsets]
    embed_share, up_near, up_far = gate([embed_share, up_near, up_far], arrived[0])

    embed_share = jnp.concatenate([embed_share, swapped(embed_share, "seq", 1)])
    near_pair = swapped(up_near, "seq", 1)
    far_groups = [shifted(up_far, "groups", k) for k in range(1, group_count)]
    embed_share, near_pair, *far_groups = gate([embed_share, near_pair, *far_groups], attended[0])
    embed_near = [embed_share] + [shifted(embed_share, "groups", k) for k in range(1, group_count)]
    near_groups = [up_near] + [shifted(up_near, "groups", k) for k in range(1, group_count)]
    pair_groups = [near_pair] + [shifted(near_pair, "groups", k) for k in range(1, group_count)]
    far_groups = [up_far] + far_groups
    far_pairs = [swapped(piece, "seq", 1) for piece in far_groups]
    up_parts = near_groups + pair_groups + far_groups + far_pairs
    embed_near = gate(embed_near, attended[-1])
    embed_parts = embed_near + [
        shifted(piece, "dom", k) for k in range(1, dom_count) for piece in embed_near
    ]
    group_order = (group - jnp.arange(group_count)) % group_count
    dom_order = (dom - jnp.arange(dom_count)) % dom_count
    embed_order = (dom_order[:, None] * group_count + group_order[None, :]).reshape(holders)
    both = near + far
    embed_place = seq ^ jnp.array(both + [offset ^ 1 for offset in both], jnp.int32)
    up_place = seq ^ jnp.array(
        near + [offset ^ 1 for offset in near] + far + [offset ^ 1 for offset in far], jnp.int32
    )

    sigma = step_index.astype(jnp.float32) / STEPS
    clean, stepped = project(sigma, latents, out_weight, returned, width)
    stepped_other = shifted(stepped, "dom", 1)
    features = embed(embed_order, embed_place, clean, embed_parts, norm_gain, group_count)
    features_other = shifted(features, "dom", 1)

    scale = potential_scale / math.sqrt(tokens * seq_count)
    head = lax.dynamic_index_in_dim(
        head_weight.reshape(seq_count, dom_count, up_columns), dom, 1, keepdims=True
    )
    rows = 8
    start = jnp.where(
        jnp.logical_and(jnp.arange(rows)[:, None] == dom, seq == 0),
        jnp.pad(prev_logw, (0, LANES - particles))[None, :],
        0.0,
    )
    reward_order = jnp.concatenate([group_order, jnp.stack([dom, (dom + 1) % dom_count])])
    score = functools.partial(reward, reward_order, up_place)
    partial_own = score(
        features, up_parts, group_count, head, start, particles, scale, 0, 1
    )[0]
    partial_both = score(
        features_other, up_parts, group_count, head, partial_own, particles, scale, 1,
        dom_count * seq_count,
    )
    logits = lax.all_to_all(partial_both, ("dom", "seq"), 0, 0, tiled=True)
    log_weights = finish(dom.reshape(1), logits, particles, dom_count)

    ancestors = ancestors.astype(jnp.int32)
    elsewhere = (ancestors // particles != dom).astype(jnp.int32)
    place = jnp.stack([elsewhere, ancestors % particles, ancestors % particles])
    resampled = resample(place, stepped, stepped_other)
    return (resampled, log_weights)


def solution(mesh):
    in_specs = (
        P(("groups", "dom"), "seq", None),
        P(("groups", "dom"), "seq", None),
        P(("groups", "dom"), "seq", None),
        P(("groups", "dom"), "seq", None),
        P(),
        P("groups"),
        P("seq", None),
        P(),
        P(None, "seq"),
        P(),
        P(("groups", "dom")),
        P(("groups", "dom")),
    )
    out_specs = (P(("groups", "dom"), "seq", None), P(("groups", "dom")))
    return jax.shard_map(
        on_device, mesh=mesh, in_specs=in_specs, out_specs=out_specs, check_vma=False
    )
```

time: 247 us -> 207 us (0.84)
  blocking collectives: 34 us -> 0 us
  Pallas kernels: 65.8 us -> 44.8 us
  starting transfers between devices: 30.8 us -> 47.4 us
  between operations: 15 us -> 1.52 us
  waiting for transfers between devices: 87.6 us -> 97.7 us
  other arithmetic: 0.69 us -> 7.42 us
  local copies, waits for them, and re-layouts: 12.6 us -> 7.21 us
    ppermute x0 -> x8, waiting for transfers between devices: none -> 63.8 us  [swapped(): lax.ppermute(array, axis, [(i, i ^ bit) for i in range(lax.axis_size(axis...]
    all_gather x1 -> x0, waiting for transfers between devices: 41.9 us -> none  [on_device(): up_share = lax.all_gather(up_share, 'seq', axis=0)]
    all_gather x1 -> x0, blocking collectives: 34 us -> none  [on_device(): embed_share = lax.all_gather(embed_share, 'seq', axis=0, tiled=True)]
    pallas_call x12 -> x11, Pallas kernels: 52.7 us -> 25.2 us  [the longest x2 9.18 us: reward(): pl.pallas_call(functools.partial(reward_kernel, particles, scale, parts,...]
    ppermute x0 -> x8, starting transfers between devices: none -> 10.9 us  [swapped(): lax.ppermute(array, axis, [(i, i ^ bit) for i in range(lax.axis_size(axis...]
    all_to_all x4, waiting for transfers between devices: 35.6 us -> 27.2 us  [on_device(): lax.all_to_all(piece, 'seq', 0, 0, tiled=True)]
    all_to_all x0 -> x1, starting transfers between devices: none -> 7.61 us  [on_device(): logits = lax.all_to_all(partial_both, ('dom', 'seq'), 0, 0, tiled=True)]
    ppermute x14 -> x8, starting transfers between devices: 12.8 us -> 6.38 us  [shifted(): lax.ppermute(array, axis, [(i, (i + step) % count) for i in range(count)])]
  transfers between devices with their start and end apart: 19 -> 21, of which waited for: 8 -> 8; matrix products, arithmetic and copies ran while one was open for 2% -> 5% of each run, Pallas kernels for 25% -> 20%
where the time goes in v3:
time: 207 us; the launch traced here: 206 us
  waiting for transfers between devices  97.7 us (47%)
  starting transfers between devices  47.4 us (23%)
  Pallas kernels  44.8 us (22%)
  other arithmetic  7.42 us (4%)
  local copies, waits for them, and re-layouts  7.21 us (3%)
    ppermute x8, waiting for transfers between devices, swapped(): lax.ppermute(array, axis, [(i, i ^ bit) for i in range(lax.axis_size(axis...  63.8 us
    all_to_all x4, waiting for transfers between devices, on_device(): lax.all_to_all(piece, 'seq', 0, 0, tiled=True)  27.2 us
    all_to_all x4, starting transfers between devices, on_device(): lax.all_to_all(piece, 'seq', 0, 0, tiled=True)  22.5 us
    pallas_call x2, Pallas kernels, attention(): pl.pallas_call(functools.partial(attention_kernel, head_width, block_sour...  13.8 us
    ppermute x8, starting transfers between devices, swapped(): lax.ppermute(array, axis, [(i, i ^ bit) for i in range(lax.axis_size(axis...  10.9 us
    pallas_call x2, Pallas kernels, reward(): pl.pallas_call(functools.partial(reward_kernel, particles, scale, parts,...  9.18 us
    all_to_all x1, starting transfers between devices, on_device(): logits = lax.all_to_all(partial_both, ('dom', 'seq'), 0, 0, tiled=True)  7.61 us
    ppermute x8, starting transfers between devices, shifted(): lax.ppermute(array, axis, [(i, (i + step) % count) for i in range(count)])  6.38 us
  transfers between devices with their start and end apart: 21, of which 8 were waited for; matrix products, arithmetic and copies ran while one was open for 5% of the time, Pallas kernels for 20%

profile of v3, /device:TPU:0, one launch (start us, length us, event | category | flops | bytes accessed | tf_op | source)
XLA Modules:
  0.0 206.0 jit_solution(11459753550111007223)
XLA Ops:
  0.6 2.3 %pack_heads.2 = bf16[4,2,3,64,384]{4,3,2,1,0:T(8,128)(2,1)} custom-call(bf16[4,64,1536]{2,1,0:T(8,128)(2,1)} %q_ref.3, bf16[4,64,1536]{2,1,0:T(8,128)(2,1)} %k_ref.3, bf16[4,64,1536]{2,1,0:T(8,128)(2,1)} %v_ref.3), custom_call_target="tpu_custom_call" | custom-call | tf_op jit(solution)/shard_map/pack_heads/pallas_call | solution.py:39
  2.9 7.3 %all-to-all-start = ((bf16[8,3,64,384]{3,2,1,0:T(8,128)(2,1)}), bf16[8,3,64,384]{3,2,1,0:T(8,128)(2,1)S(1)}, u32[]{:S(2)}, u32[]{:S(2)}) async-start(bf16[8,3,64,384]{3,2,1,0:T(8,128)(2,1)} %bitcast.19), calls=%async_computation | async-start | bytes 2359296 | tf_op jit(solution)/shard_map/all_to_all | solution.py:424
  10.2 2.3 %pack_heads.3 = bf16[4,2,3,64,384]{4,3,2,1,0:T(8,128)(2,1)} custom-call(bf16[4,64,1536]{2,1,0:T(8,128)(2,1)} %q_ref.3, bf16[4,64,1536]{2,1,0:T(8,128)(2,1)} %k_ref.3, bf16[4,64,1536]{2,1,0:T(8,128)(2,1)} %v_ref.3), custom_call_target="tpu_custom_call" | custom-call | tf_op jit(solution)/shard_map/pack_heads/pallas_call | solution.py:39
  12.5 26.3 %all-to-all-done.qkv_ref.refs_3_ = bf16[8,3,64,384]{3,2,1,0:T(8,128)(2,1)S(1)} async-done(((bf16[8,3,64,384]{3,2,1,0:T(8,128)(2,1)}), bf16[8,3,64,384]{3,2,1,0:T(8,128)(2,1)S(1)}, u32[]{:S(2)}, u32[]{:S(2)}) %all-to-all-start) | async-done | bytes 1179680 | tf_op jit(solution)/shard_map/all_to_all | solution.py:424
  38.8 1.0 copy-done.2
  39.8 4.3 %all-to-all-start.2 = ((bf16[8,3,64,384]{3,2,1,0:T(8,128)(2,1)}), bf16[8,3,64,384]{3,2,1,0:T(8,128)(2,1)}, u32[]{:S(2)}, u32[]{:S(2)}) async-start(bf16[8,3,64,384]{3,2,1,0:T(8,128)(2,1)} %bitcast.17), calls=%async_computation.2 | async-start | bytes 2359296 | tf_op jit(solution)/shard_map/all_to_all | solution.py:424
  44.1 2.9 %collective-permute-start.2 = (bf16[1,512,256]{2,1,0:T(8,128)(2,1)S(1)}, bf16[1,512,256]{2,1,0:T(8,128)(2,1)S(1)}, u32[]{:S(2)}, u32[]{:S(2)}) collective-permute-start(bf16[1,512,256]{2,1,0:T(8,128)(2,1)S(1)} %dynamic-slice_bitcast_fusion), channel_id=1, source_target_pairs={{0,4},{1,5},{2,6},{3,7},{4,0},{5,1},{6,2},{7,3},{8,12},{9,13},{10,... | collective-permute-start | bytes 786440 | tf_op jit(solution)/shard_map/ppermute | solution.py:378
  48.0 39.7 %collective-permute-done.1 = bf16[1,192,256]{2,1,0:T(8,128)(2,1)S(1)} collective-permute-done((bf16[1,192,256]{2,1,0:T(8,128)(2,1)S(1)}, bf16[1,192,256]{2,1,0:T(8,128)(2,1)S(1)}, u32[]{:S(2)}, u32[]{:S(2)}) %collective-permute-start.1) | collective-permute-done | bytes 98336 | tf_op jit(solution)/shard_map/ppermute | solution.py:378
  89.4 2.0 collective-permute-start.3
  91.4 14.7 %collective-permute-done.3 = bf16[2,192,256]{2,1,0:T(8,128)(2,1)S(1)} collective-permute-done((bf16[2,192,256]{2,1,0:T(8,128)(2,1)}, bf16[2,192,256]{2,1,0:T(8,128)(2,1)S(1)}, u32[]{:S(2)}, u32[]{:S(2)}) %collective-permute-start.3) | collective-permute-done | bytes 196640 | tf_op jit(solution)/shard_map/ppermute | solution.py:378
  106.1 1.7 pad_maximum_fusion.2.refs_0_
  108.6 1.9 collective-permute-start.5
  110.6 1.5 collective-permute-start.7
  112.1 6.9 %attention.2.refs_3_ = bf16[8,64,384]{2,1,0:T(8,128)(2,1)} custom-call(bf16[8,3,64,384]{3,2,1,0:T(8,128)(2,1)} %copy-done.2), custom_call_target="tpu_custom_call" | custom-call | flops 402653184 | bytes 1572864 | tf_op jit(solution)/shard_map/attention/pallas_call | solution.py:113
  119.0 5.1 %all-to-all-start.1 = ((bf16[8,64,384]{2,1,0:T(8,128)(2,1)}), bf16[8,64,384]{2,1,0:T(8,128)(2,1)}, u32[]{:S(2)}, u32[]{:S(2)}) async-start(bf16[8,64,384]{2,1,0:T(8,128)(2,1)} %attention.2.refs_3_), calls=%async_computation.1 | async-start | bytes 786432 | tf_op jit(solution)/shard_map/all_to_all | solution.py:426
  125.1 7.5 %collective-permute-done.6.refs_1_ = bf16[2,512,256]{2,1,0:T(8,128)(2,1)S(1)} collective-permute-done((bf16[2,512,256]{2,1,0:T(8,128)(2,1)}, bf16[2,512,256]{2,1,0:T(8,128)(2,1)S(1)}, u32[]{:S(2)}, u32[]{:S(2)}) %collective-permute-start.6) | collective-permute-done | bytes 524320 | tf_op jit(solution)/shard_map/ppermute | solution.py:378
  134.1 2.0 collective-permute-start.8
  136.3 6.9 %attention.3.refs_2_ = bf16[8,64,384]{2,1,0:T(8,128)(2,1)} custom-call(bf16[8,3,64,384]{3,2,1,0:T(8,128)(2,1)} %all-to-all-done.2.qkv_ref), custom_call_target="tpu_custom_call" | custom-call | flops 402653184 | bytes 1572864 | tf_op jit(solution)/shard_map/attention/pallas_call | solution.py:113
  143.2 5.9 %all-to-all-start.3 = ((bf16[8,64,384]{2,1,0:T(8,128)(2,1)}), bf16[8,64,384]{2,1,0:T(8,128)(2,1)}, u32[]{:S(2)}, u32[]{:S(2)}) async-start(bf16[8,64,384]{2,1,0:T(8,128)(2,1)} %attention.3.refs_2_), calls=%async_computation.3 | async-start | bytes 786432 | tf_op jit(solution)/shard_map/all_to_all | solution.py:426
  154.2 2.3 %collective-permute-start.14 = (bf16[2,512,256]{2,1,0:T(8,128)(2,1)S(1)}, bf16[2,512,256]{2,1,0:T(8,128)(2,1)}, u32[]{:S(2)}, u32[]{:S(2)}) collective-permute-start(bf16[2,512,256]{2,1,0:T(8,128)(2,1)S(1)} %copy-done.8), channel_id=1, source_target_pairs={{0,1},{1,0},{2,3},{3,2},{4,5},{5,4},{6,7},{7,6},{8,9},{9,8},{10,11... | collective-permute-start | bytes 1572872 | tf_op jit(solution)/shard_map/ppermute | solution.py:378
  156.5 1.2 collective-permute-start.13
  158.6 5.8 %project.1 = (bf16[256,1536]{1,0:T(8,128)(2,1)}, bf16[4,64,1536]{2,1,0:T(8,128)(2,1)}) custom-call(f32[1]{0:T(128)S(6)} %div.19.sigma_ref, bf16[4,64,1536]{2,1,0:T(8,128)(2,1)} %latents_ref.1, bf16[1536,1536]{1,0:T(8,128)(2,1)} %weight_ref.1, bf16[4,2,64,384]{3,2,1,0:T(8,128)(2,1)} %bitcast.3.refs_0_, bf16[4,2,64,384]{3,2,1,0:T(8,128)(2,1)} %bitcast.5.refs_1_), custom_call_target="tpu_custom_call" | custom-call | flops 1207959552 | bytes 7864320 | tf_op jit(solution)/shard_map/project/pallas_call | solution.py:159
  164.4 1.5 collective-permute-start.15
  166.0 6.2 %embed_norm.1.refs_2_ = bf16[2,256,512]{2,1,0:T(8,128)(2,1)} custom-call(s32[4]{0:T(128)} %add.77.order_ref, s32[8]{0:T(128)} %broadcast_xor_fusion.place_ref, bf16[256,1536]{1,0:T(8,128)(2,1)} %get-tuple-element.15.clean_ref, f32[1,1024]{1,0:T(1,128)} %bitcast.21, bf16[8,192,256]{2,1,0:T(8,128)(2,1)} %get-tuple-element.22.refs_0_, ...), custom_call_target="tpu_custom_call" | custom-call | flops 805306368 | bytes 4456448 | tf_op jit(solution)/shard_map/embed_norm/pallas_call | solution.py:231
  174.1 4.2 %collective-permute-done.13.refs_8_ = bf16[2,512,256]{2,1,0:T(8,128)(2,1)} collective-permute-done((bf16[2,512,256]{2,1,0:T(8,128)(2,1)S(1)}, bf16[2,512,256]{2,1,0:T(8,128)(2,1)}, u32[]{:S(2)}, u32[]{:S(2)}) %collective-permute-start.13) | collective-permute-done | bytes 524320 | tf_op jit(solution)/shard_map/ppermute | solution.py:374
  178.3 1.9 collective-permute-done.15.refs_12_
  180.2 4.6 %reward.2 = f32[1,8,128]{2,1,0:T(8,128)} custom-call(s32[4]{0:T(128)} %pad_add_fusion.1.refs_0_, s32[8]{0:T(128)} %broadcast_xor_fusion.1.refs_1_, bf16[2,256,512]{2,1,0:T(8,128)(2,1)} %embed_norm.1.refs_2_, f32[8,1,256]{2,1,0:T(1,128)} %constant_dynamic-slice_fusion.refs_3_, f32[8,128]{1,0:T(8,128)} %broadcast_select_fusion.refs_4_, ...), custom_call_target="tpu_custom_call" | custom-call | flops 1073741824 | bytes 4194304 | tf_op jit(solution)/shard_map/reward/pallas_call | solution.py:293
  184.8 4.6 %reward.3 = f32[16,8,128]{2,1,0:T(8,128)} custom-call(s32[4]{0:T(128)} %pad_add_fusion.1.refs_0_, s32[8]{0:T(128)} %broadcast_xor_fusion.1.refs_1_, bf16[2,256,512]{2,1,0:T(8,128)(2,1)} %collective-permute-done.11.refs_2_, f32[8,1,256]{2,1,0:T(1,128)} %constant_dynamic-slice_fusion.refs_3_, f32[8,128]{1,0:T(8,128)} %bitcast.20, ...), custom_call_target="tpu_custom_call" | custom-call | flops 1073741824 | bytes 4194304 | tf_op jit(solution)/shard_map/reward/pallas_call | solution.py:293
  189.4 7.6 %all-to-all-start.4 = ((f32[16,8,128]{2,1,0:T(8,128)}), f32[16,8,128]{2,1,0:T(8,128)S(1)}, u32[]{:S(2)}, u32[]{:S(2)}) async-start(f32[16,8,128]{2,1,0:T(8,128)} %reward.3), calls=%async_computation.4 | async-start | bytes 131072 | tf_op jit(solution)/shard_map/all_to_all | solution.py:482
  197.6 3.7 %resample.1 = bf16[4,64,1536]{2,1,0:T(8,128)(2,1)} custom-call(s32[3,4]{1,0:T(4,128)} %pad_add_fusion.place_ref, bf16[4,64,1536]{2,1,0:T(8,128)(2,1)} %get-tuple-element.14.own_ref, bf16[4,64,1536]{2,1,0:T(8,128)(2,1)} %collective-permute-done.other_ref), custom_call_target="tpu_custom_call" | custom-call | tf_op jit(solution)/shard_map/resample/pallas_call | solution.py:355
  201.3 2.5 %all-to-all-done.4.parts_ref = f32[16,8,128]{2,1,0:T(8,128)S(1)} async-done(((f32[16,8,128]{2,1,0:T(8,128)}), f32[16,8,128]{2,1,0:T(8,128)S(1)}, u32[]{:S(2)}, u32[]{:S(2)}) %all-to-all-start.4) | async-done | bytes 65568 | tf_op jit(solution)/shard_map/all_to_all | solution.py:482
  204.4 1.6 log_weights.1
  (81 shorter events, 14.7 us)
Async XLA Ops:
  0.6 43.5 %copy-start = (bf16[1024,512]{1,0:T(8,128)(2,1)S(1)}, bf16[1024,512]{1,0:T(8,128)(2,1)}, u32[]{:S(2)}) copy-start(bf16[1024,512]{1,0:T(8,128)(2,1)} %param.22) | copy-start | bytes 3145732
  2.9 35.9 %all-to-all-start = ((bf16[8,3,64,384]{3,2,1,0:T(8,128)(2,1)}), bf16[8,3,64,384]{3,2,1,0:T(8,128)(2,1)S(1)}, u32[]{:S(2)}, u32[]{:S(2)}) async-start(bf16[8,3,64,384]{3,2,1,0:T(8,128)(2,1)} %bitcast.19), calls=%async_computation | async-start | bytes 2359296 | tf_op jit(solution)/shard_map/all_to_all | solution.py:424
  39.8 79.2 %all-to-all-start.2 = ((bf16[8,3,64,384]{3,2,1,0:T(8,128)(2,1)}), bf16[8,3,64,384]{3,2,1,0:T(8,128)(2,1)}, u32[]{:S(2)}, u32[]{:S(2)}) async-start(bf16[8,3,64,384]{3,2,1,0:T(8,128)(2,1)} %bitcast.17), calls=%async_computation.2 | async-start | bytes 2359296 | tf_op jit(solution)/shard_map/all_to_all | solution.py:424
  44.1 44.3 %collective-permute-start.2 = (bf16[1,512,256]{2,1,0:T(8,128)(2,1)S(1)}, bf16[1,512,256]{2,1,0:T(8,128)(2,1)S(1)}, u32[]{:S(2)}, u32[]{:S(2)}) collective-permute-start(bf16[1,512,256]{2,1,0:T(8,128)(2,1)S(1)} %dynamic-slice_bitcast_fusion), channel_id=1, source_target_pairs={{0,4},{1,5},{2,6},{3,7},{4,0},{5,1},{6,2},{7,3},{8,12},{9,13},{10,... | collective-permute-start | bytes 786440 | tf_op jit(solution)/shard_map/ppermute | solution.py:378
  47.9 39.9 %collective-permute-start.1 = (bf16[1,192,256]{2,1,0:T(8,128)(2,1)S(1)}, bf16[1,192,256]{2,1,0:T(8,128)(2,1)S(1)}, u32[]{:S(2)}, u32[]{:S(2)}) collective-permute-start(bf16[1,192,256]{2,1,0:T(8,128)(2,1)S(1)} %dynamic-slice_bitcast_fusion.1), channel_id=1, source_target_pairs={{0,4},{1,5},{2,6},{3,7},{4,0},{5,1},{6,2},{7,3},{8,12},{9,13},{10,... | collective-permute-start | bytes 294920 | tf_op jit(solution)/shard_map/ppermute | solution.py:378
  89.4 18.4 %collective-permute-start.4 = (bf16[2,512,256]{2,1,0:T(8,128)(2,1)}, bf16[2,512,256]{2,1,0:T(8,128)(2,1)S(1)}, u32[]{:S(2)}, u32[]{:S(2)}) collective-permute-start(bf16[2,512,256]{2,1,0:T(8,128)(2,1)} %get-tuple-element.17.refs_1_), channel_id=1, source_target_pairs={{0,2},{1,3},{2,0},{3,1},{4,6},{5,7},{6,4},{7,5},{8,10},{9,11},{10,... | collective-permute-start | bytes 1572872 | tf_op jit(solution)/shard_map/ppermute | solution.py:378
  89.4 16.7 %collective-permute-start.3 = (bf16[2,192,256]{2,1,0:T(8,128)(2,1)}, bf16[2,192,256]{2,1,0:T(8,128)(2,1)S(1)}, u32[]{:S(2)}, u32[]{:S(2)}) collective-permute-start(bf16[2,192,256]{2,1,0:T(8,128)(2,1)} %get-tuple-element.16), channel_id=1, source_target_pairs={{0,2},{1,3},{2,0},{3,1},{4,6},{5,7},{6,4},{7,5},{8,10},{9,11},{10,... | collective-permute-start | bytes 589832 | tf_op jit(solution)/shard_map/ppermute | solution.py:378
  108.6 15.5 %collective-permute-start.5 = (bf16[4,192,256]{2,1,0:T(8,128)(2,1)}, bf16[4,192,256]{2,1,0:T(8,128)(2,1)S(1)}, u32[]{:S(2)}, u32[]{:S(2)}) collective-permute-start(bf16[4,192,256]{2,1,0:T(8,128)(2,1)} %get-tuple-element.18), channel_id=1, source_target_pairs={{0,1},{1,0},{2,3},{3,2},{4,5},{5,4},{6,7},{7,6},{8,9},{9,8},{10,11... | collective-permute-start | bytes 1179656 | tf_op jit(solution)/shard_map/ppermute | solution.py:378
  110.5 22.0 %collective-permute-start.6 = (bf16[2,512,256]{2,1,0:T(8,128)(2,1)}, bf16[2,512,256]{2,1,0:T(8,128)(2,1)S(1)}, u32[]{:S(2)}, u32[]{:S(2)}) collective-permute-start(bf16[2,512,256]{2,1,0:T(8,128)(2,1)} %get-tuple-element.19.refs_5_), channel_id=1, source_target_pairs={{0,1},{1,0},{2,3},{3,2},{4,5},{5,4},{6,7},{7,6},{8,9},{9,8},{10,11... | collective-permute-start | bytes 1572872 | tf_op jit(solution)/shard_map/ppermute | solution.py:378
  110.6 13.5 %copy-start.9 = (bf16[4,192,256]{2,1,0:T(8,128)(2,1)S(1)}, bf16[4,192,256]{2,1,0:T(8,128)(2,1)}, u32[]{:S(2)}) copy-start(bf16[4,192,256]{2,1,0:T(8,128)(2,1)} %get-tuple-element.18) | copy-start | bytes 1179652
  110.6 21.9 %collective-permute-start.7 = (bf16[2,512,256]{2,1,0:T(8,128)(2,1)}, bf16[2,512,256]{2,1,0:T(8,128)(2,1)S(1)}, u32[]{:S(2)}, u32[]{:S(2)}) collective-permute-start(bf16[2,512,256]{2,1,0:T(8,128)(2,1)} %get-tuple-element.20.refs_9_), channel_id=1, source_target_pairs={{0,16},{16,0},{1,17},{17,1},{2,18},{18,2},{3,19},{19,3},{4,20},{20... | collective-permute-start | bytes 1572872 | tf_op jit(solution)/shard_map/ppermute | solution.py:374
  119.0 24.2 %all-to-all-start.1 = ((bf16[8,64,384]{2,1,0:T(8,128)(2,1)}), bf16[8,64,384]{2,1,0:T(8,128)(2,1)}, u32[]{:S(2)}, u32[]{:S(2)}) async-start(bf16[8,64,384]{2,1,0:T(8,128)(2,1)} %attention.2.refs_3_), calls=%async_computation.1 | async-start | bytes 786432 | tf_op jit(solution)/shard_map/all_to_all | solution.py:426
  125.1 11.1 %copy-start.13 = (f32[4096]{0:T(1024)S(1)}, f32[4096]{0:T(1024)}, u32[]{:S(2)}) copy-start(f32[4096]{0:T(1024)} %param.23) | copy-start | bytes 49156
  134.1 16.3 %collective-permute-start.8 = (bf16[8,192,256]{2,1,0:T(8,128)(2,1)}, bf16[8,192,256]{2,1,0:T(8,128)(2,1)S(1)}, u32[]{:S(2)}, u32[]{:S(2)}) collective-permute-start(bf16[8,192,256]{2,1,0:T(8,128)(2,1)} %get-tuple-element.21.refs_0_), channel_id=1, source_target_pairs={{0,16},{16,0},{1,17},{17,1},{2,18},{18,2},{3,19},{19,3},{4,20},{20... | collective-permute-start | bytes 2359304 | tf_op jit(solution)/shard_map/ppermute | solution.py:374
  143.2 15.4 %all-to-all-start.3 = ((bf16[8,64,384]{2,1,0:T(8,128)(2,1)}), bf16[8,64,384]{2,1,0:T(8,128)(2,1)}, u32[]{:S(2)}, u32[]{:S(2)}) async-start(bf16[8,64,384]{2,1,0:T(8,128)(2,1)} %attention.3.refs_2_), calls=%async_computation.3 | async-start | bytes 786432 | tf_op jit(solution)/shard_map/all_to_all | solution.py:426
  149.1 3.4 %copy-start.17 = (s32[8]{0:T(128)S(1)}, s32[8]{0:T(128)}, u32[]{:S(2)}) copy-start(s32[8]{0:T(128)} %constant.93.clone) | copy-start | bytes 100
  149.1 4.0 %copy-start.1 = (bf16[2,512,256]{2,1,0:T(8,128)(2,1)S(1)}, bf16[2,512,256]{2,1,0:T(8,128)(2,1)}, u32[]{:S(2)}) copy-start(bf16[2,512,256]{2,1,0:T(8,128)(2,1)} %get-tuple-element.19.refs_5_) | copy-start | bytes 1572868
  149.2 4.5 %copy-start.16 = (s32[8]{0:T(128)S(1)}, s32[8]{0:T(128)}, u32[]{:S(2)}) copy-start(s32[8]{0:T(128)} %constant.92.clone) | copy-start | bytes 100
  149.2 5.1 %copy-start.8 = (bf16[2,512,256]{2,1,0:T(8,128)(2,1)S(1)}, bf16[2,512,256]{2,1,0:T(8,128)(2,1)}, u32[]{:S(2)}) copy-start(bf16[2,512,256]{2,1,0:T(8,128)(2,1)} %get-tuple-element.20.refs_9_) | copy-start | bytes 1572868
  149.2 7.4 %copy-start.4 = (bf16[2,512,256]{2,1,0:T(8,128)(2,1)S(1)}, bf16[2,512,256]{2,1,0:T(8,128)(2,1)}, u32[]{:S(2)}) copy-start(bf16[2,512,256]{2,1,0:T(8,128)(2,1)} %get-tuple-element.24.refs_7_) | copy-start | bytes 1572868
  151.3 13.1 %collective-permute-start.9 = (bf16[8,192,256]{2,1,0:T(8,128)(2,1)}, bf16[8,192,256]{2,1,0:T(8,128)(2,1)}, u32[]{:S(2)}, u32[]{:S(2)}) collective-permute-start(bf16[8,192,256]{2,1,0:T(8,128)(2,1)} %get-tuple-element.22.refs_0_), channel_id=1, source_target_pairs={{0,8},{8,0},{1,9},{9,1},{2,10},{10,2},{3,11},{11,3},{4,12},{12,4},... | collective-permute-start | bytes 2359304 | tf_op jit(solution)/shard_map/ppermute | solution.py:374
  152.0 14.0 %collective-permute-start.10 = (bf16[8,192,256]{2,1,0:T(8,128)(2,1)}, bf16[8,192,256]{2,1,0:T(8,128)(2,1)}, u32[]{:S(2)}, u32[]{:S(2)}) collective-permute-start(bf16[8,192,256]{2,1,0:T(8,128)(2,1)} %get-tuple-element.23.refs_1_), channel_id=1, source_target_pairs={{0,8},{8,0},{1,9},{9,1},{2,10},{10,2},{3,11},{11,3},{4,12},{12,4},... | collective-permute-start | bytes 2359304 | tf_op jit(solution)/shard_map/ppermute | solution.py:374
  153.1 19.1 %collective-permute-start.12 = (bf16[2,512,256]{2,1,0:T(8,128)(2,1)S(1)}, bf16[2,512,256]{2,1,0:T(8,128)(2,1)S(1)}, u32[]{:S(2)}, u32[]{:S(2)}) collective-permute-start(bf16[2,512,256]{2,1,0:T(8,128)(2,1)S(1)} %copy-done.1), channel_id=1, source_target_pairs={{0,16},{16,0},{1,17},{17,1},{2,18},{18,2},{3,19},{19,3},{4,20},{20... | collective-permute-start | bytes 1572872 | tf_op jit(solution)/shard_map/ppermute | solution.py:374
  154.2 19.9 %collective-permute-start.14 = (bf16[2,512,256]{2,1,0:T(8,128)(2,1)S(1)}, bf16[2,512,256]{2,1,0:T(8,128)(2,1)}, u32[]{:S(2)}, u32[]{:S(2)}) collective-permute-start(bf16[2,512,256]{2,1,0:T(8,128)(2,1)S(1)} %copy-done.8), channel_id=1, source_target_pairs={{0,1},{1,0},{2,3},{3,2},{4,5},{5,4},{6,7},{7,6},{8,9},{9,8},{10,11... | collective-permute-start | bytes 1572872 | tf_op jit(solution)/shard_map/ppermute | solution.py:378
  156.5 21.8 %collective-permute-start.13 = (bf16[2,512,256]{2,1,0:T(8,128)(2,1)S(1)}, bf16[2,512,256]{2,1,0:T(8,128)(2,1)}, u32[]{:S(2)}, u32[]{:S(2)}) collective-permute-start(bf16[2,512,256]{2,1,0:T(8,128)(2,1)S(1)} %copy-done.4), channel_id=1, source_target_pairs={{0,16},{16,0},{1,17},{17,1},{2,18},{18,2},{3,19},{19,3},{4,20},{20... | collective-permute-start | bytes 1572872 | tf_op jit(solution)/shard_map/ppermute | solution.py:374
  158.6 5.8 %copy-start.6 = (bf16[2,512,256]{2,1,0:T(8,128)(2,1)S(1)}, bf16[2,512,256]{2,1,0:T(8,128)(2,1)}, u32[]{:S(2)}) copy-start(bf16[2,512,256]{2,1,0:T(8,128)(2,1)} %get-tuple-element.25.refs_10_) | copy-start | bytes 1572868
  164.4 15.8 %collective-permute-start.15 = (bf16[2,512,256]{2,1,0:T(8,128)(2,1)S(1)}, bf16[2,512,256]{2,1,0:T(8,128)(2,1)}, u32[]{:S(2)}, u32[]{:S(2)}) collective-permute-start(bf16[2,512,256]{2,1,0:T(8,128)(2,1)S(1)} %copy-done.6), channel_id=1, source_target_pairs={{0,1},{1,0},{2,3},{3,2},{4,5},{5,4},{6,7},{7,6},{8,9},{9,8},{10,11... | collective-permute-start | bytes 1572872 | tf_op jit(solution)/shard_map/ppermute | solution.py:378
  166.0 7.5 %copy-start.14 = (f32[4]{0:T(128)S(1)}, f32[4]{0:T(128)}, u32[]{:S(2)}) copy-start(f32[4]{0:T(128)} %param.24) | copy-start | bytes 52
  172.2 12.6 %collective-permute-start.11 = (bf16[2,256,512]{2,1,0:T(8,128)(2,1)}, bf16[2,256,512]{2,1,0:T(8,128)(2,1)}, u32[]{:S(2)}, u32[]{:S(2)}) collective-permute-start(bf16[2,256,512]{2,1,0:T(8,128)(2,1)} %embed_norm.1.refs_2_), channel_id=1, source_target_pairs={{0,8},{8,0},{1,9},{9,1},{2,10},{10,2},{3,11},{11,3},{4,12},{12,4},... | collective-permute-start | bytes 1572872 | tf_op jit(solution)/shard_map/ppermute | solution.py:374
  172.3 7.9 %copy-start.11 = (bf16[2,512,256]{2,1,0:T(8,128)(2,1)}, bf16[2,512,256]{2,1,0:T(8,128)(2,1)S(1)}, u32[]{:S(2)}) copy-start(bf16[2,512,256]{2,1,0:T(8,128)(2,1)S(1)} %collective-permute-done.12.refs_6_) | copy-start | bytes 1572868
  172.3 25.3 %collective-permute-start = (bf16[4,64,1536]{2,1,0:T(8,128)(2,1)}, bf16[4,64,1536]{2,1,0:T(8,128)(2,1)}, u32[]{:S(2)}, u32[]{:S(2)}) collective-permute-start(bf16[4,64,1536]{2,1,0:T(8,128)(2,1)} %get-tuple-element.14.own_ref), channel_id=1, source_target_pairs={{0,8},{8,0},{1,9},{9,1},{2,10},{10,2},{3,11},{11,3},{4,12},{12,4},... | collective-permute-start | bytes 2359304 | tf_op jit(solution)/shard_map/ppermute | solution.py:374
  189.4 14.4 %all-to-all-start.4 = ((f32[16,8,128]{2,1,0:T(8,128)}), f32[16,8,128]{2,1,0:T(8,128)S(1)}, u32[]{:S(2)}, u32[]{:S(2)}) async-start(f32[16,8,128]{2,1,0:T(8,128)} %reward.3), calls=%async_computation.4 | async-start | bytes 131072 | tf_op jit(solution)/shard_map/all_to_all | solution.py:482
  (7 other events, 8.3 us)

commit v4 on v3

--- a/solution.py
+++ b/solution.py
@@ -59,18 +59,18 @@
     pass
 
 
-def gate(arrays, after):
+def gate(arrays):
     anywhere = pl.BlockSpec(memory_space=pl.ANY)
-    return list(
-        pl.pallas_call(
+    count = len(arrays)
+    gated = pl.pallas_call(
         gate_kernel,
-        in_specs=[anywhere] * (len(arrays) + 1),
-        out_specs=[anywhere] * len(arrays),
+        in_specs=[anywhere] * count,
+        out_specs=[anywhere] * count,
         out_shape=[jax.ShapeDtypeStruct(array.shape, array.dtype) for array in arrays],
-        input_output_aliases={index: index for index in range(len(arrays))},
+        input_output_aliases={index: index for index in range(count)},
         name="gate",
-    )(*arrays, after)
-    )
+    )(*arrays)
+    return list(gated)
 
 
 def attention_kernel(head_width, block_sources, qkv_ref, out_ref):
@@ -126,67 +126,23 @@
     )(qkv)
 
 
-def project_kernel(chunks, width, sigma_ref, latents_ref, weight_ref, *refs):
-    attended_refs, (clean_ref, stepped_ref) = refs[:chunks], refs[chunks:]
-    particles, tokens, columns = latents_ref.shape
+def project_kernel(chunks, parts, block, refs_in, refs_out):
+    order_ref, place_ref, sigma_ref, latents_ref, gain_ref, out_weight_ref = refs_in[:6]
+    attended_refs, weight_refs = refs_in[6 : 6 + chunks], refs_in[6 + chunks :]
+    stepped_ref, features_ref = refs_out[:2]
+    out_vmem, weight_vmem, attended_ref, clean_ref, embedded_ref, out_sems, sems = refs_out[2:]
+    particles, tokens, model_width = latents_ref.shape
     rows = particles * tokens
-    depth = weight_ref.shape[0]
-    part = width // chunks
-    total = jnp.zeros((rows, columns), jnp.float32)
-    for block in range(depth // width):
-        for chunk in range(chunks):
-            start = block * width + chunk * part
-            piece = attended_refs[chunk][:, block].reshape(rows, part)
-            total += jnp.dot(
-                piece, weight_ref[start : start + part, :], preferred_element_type=jnp.float32
-            )
-    flat = latents_ref[...].reshape(rows, columns).astype(jnp.float32)
-    velocity = flat + total
-    clean_ref[...] = (flat - sigma_ref[0] * velocity).astype(jnp.bfloat16)
-    stepped_ref[...] = (
-        (flat - velocity * (1.0 / STEPS)).astype(jnp.bfloat16).reshape(particles, tokens, columns)
-    )
-
-
-def project(sigma, latents, out_weight, attended, width):
-    particles, tokens, model_width = latents.shape
-    rows = particles * tokens
-    blocks = model_width // width
-    chunks = len(attended)
-    part = width // chunks
-    columns = 512 if model_width % 512 == 0 else model_width
-    attended = [piece.reshape(particles, blocks, tokens, part) for piece in attended]
-    return pl.pallas_call(
-        functools.partial(project_kernel, chunks, width),
-        grid=(model_width // columns,),
-        in_specs=[
-            pl.BlockSpec(memory_space=pltpu.SMEM),
-            pl.BlockSpec((particles, tokens, columns), lambda i: (0, 0, i)),
-            pl.BlockSpec((model_width, columns), lambda i: (0, i)),
-        ]
-        + [pl.BlockSpec((particles, blocks, tokens, part), lambda i: (0, 0, 0, 0))] * chunks,
-        out_specs=[
-            pl.BlockSpec((rows, columns), lambda i: (0, i)),
-            pl.BlockSpec((particles, tokens, columns), lambda i: (0, 0, i)),
-        ],
-        out_shape=[
-            jax.ShapeDtypeStruct((rows, model_width), jnp.bfloat16),
-            jax.ShapeDtypeStruct((particles, tokens, model_width), jnp.bfloat16),
-        ],
-        compiler_params=pltpu.CompilerParams(vmem_limit_bytes=60 * MIB),
-        cost_estimate=pl.CostEstimate(
-            flops=2 * rows * model_width * model_width,
-            bytes_accessed=2 * model_width * model_width + 8 * rows * model_width,
-            transcendentals=0,
-        ),
-        name="project",
-    )(sigma, latents, out_weight, *attended)
-
-
-def embed_kernel(order_ref, place_ref, clean_ref, gain_ref, *refs):
-    parts = order_ref.shape[0]
-    weight_refs, (features_ref, weight_vmem, embedded_ref, sems) = refs[:parts], refs[parts:]
     shards, depth, columns = weight_refs[0].shape
+
+    out_copies = []
+    for index in range(model_width // block):
+        cols = slice(index * block, (index + 1) * block)
+        copy = pltpu.make_async_copy(
+            out_weight_ref.at[:, cols], out_vmem.at[:, cols], out_sems.at[index]
+        )
+        copy.start()
+        out_copies.append(copy)
     copies = []
     for index in range(parts):
         for shard in range(shards):
@@ -198,6 +154,27 @@
             )
             copy.start()
             copies.append(copy)
+
+    part = attended_refs[0].shape[3]
+    width = chunks * part
+    for place in range(model_width // width):
+        for chunk in range(chunks):
+            start = place * width + chunk * part
+            attended_ref[:, start : start + part] = attended_refs[chunk][:, place].reshape(
+                rows, part
+            )
+    for index in range(model_width // block):
+        cols = slice(index * block, (index + 1) * block)
+        out_copies[index].wait()
+        flat = latents_ref[:, :, cols].reshape(rows, block).astype(jnp.float32)
+        velocity = flat + jnp.dot(
+            attended_ref[...], out_vmem[:, cols], preferred_element_type=jnp.float32
+        )
+        clean_ref[:, cols] = (flat - sigma_ref[0] * velocity).astype(jnp.bfloat16)
+        stepped_ref[:, :, cols] = (
+            (flat - velocity * (1.0 / STEPS)).astype(jnp.bfloat16).reshape(particles, tokens, block)
+        )
+
     for index in range(parts):
         for copy in copies[index * shards : (index + 1) * shards]:
             copy.wait()
@@ -206,83 +183,105 @@
         )
     count = parts * columns
     blocks = [embedded_ref[index] for index in range(parts)]
-    centre = sum(jnp.sum(block, axis=1, keepdims=True) for block in blocks) * (1.0 / count)
-    blocks = [block - centre for block in blocks]
-    variance = sum(jnp.sum(block * block, axis=1, keepdims=True) for block in blocks) * (
+    centre = sum(jnp.sum(piece, axis=1, keepdims=True) for piece in blocks) * (1.0 / count)
+    blocks = [piece - centre for piece in blocks]
+    variance = sum(jnp.sum(piece * piece, axis=1, keepdims=True) for piece in blocks) * (
         1.0 / count
     )
     inverse = lax.rsqrt(variance + norm_eps)
     share = features_ref.shape[2]
-    for index, block in enumerate(blocks):
+    for index, piece in enumerate(blocks):
         cols = slice(index * columns, (index + 1) * columns)
-        piece = jax.nn.gelu(block * inverse * gain_ref[:, cols]).astype(jnp.bfloat16)
+        feature = jax.nn.gelu(piece * inverse * gain_ref[:, cols]).astype(jnp.bfloat16)
         start = index * columns % share
-        features_ref[index * columns // share, :, start : start + columns] = piece
-
-
-def embed(order, place, clean, weights, gain, depth_parts):
-    parts = len(weights)
-    shards, shard_depth, columns = weights[0].shape
-    depth = shards * shard_depth
-    rows = clean.shape[0]
+        features_ref[index * columns // share, :, start : start + columns] = feature
+
+
+def project_embed(order, place, sigma, latents, attended, width, out_weight, weights, gain, depth_parts):
+    particles, tokens, model_width = latents.shape
+    rows = particles * tokens
+    chunks, parts = len(attended), len(weights)
+    columns = weights[0].shape[2]
     count = parts * columns
+    block = 256 if model_width % 256 == 0 else model_width
+    attended = [
+        piece.reshape(particles, model_width // width, tokens, width // chunks)
+        for piece in attended
+    ]
     vmem = pl.BlockSpec(memory_space=pltpu.VMEM)
     smem = pl.BlockSpec(memory_space=pltpu.SMEM)
+    anywhere = pl.BlockSpec(memory_space=pl.ANY)
+    inputs = 6 + chunks + parts
+
+    def kernel(*refs):
+        project_kernel(chunks, parts, block, refs[:inputs], refs[inputs:])
+
     return pl.pallas_call(
-        embed_kernel,
-        in_specs=[smem, smem, vmem, vmem] + [pl.BlockSpec(memory_space=pl.ANY)] * parts,
-        out_specs=vmem,
-        out_shape=jax.ShapeDtypeStruct((depth_parts, rows, count // depth_parts), jnp.bfloat16),
+        kernel,
+        in_specs=[smem, smem, smem, vmem, vmem, anywhere] + [vmem] * chunks + [anywhere] * parts,
+        out_specs=[vmem, vmem],
+        out_shape=[
+            jax.ShapeDtypeStruct(latents.shape, jnp.bfloat16),
+            jax.ShapeDtypeStruct((depth_parts, rows, count // depth_parts), jnp.bfloat16),
+        ],
         scratch_shapes=[
-            pltpu.VMEM((parts, depth, columns), jnp.bfloat16),
+            pltpu.VMEM((model_width, model_width), jnp.bfloat16),
+            pltpu.VMEM((parts, model_width, columns), jnp.bfloat16),
+            pltpu.VMEM((rows, model_width), jnp.bfloat16),
+            pltpu.VMEM((rows, model_width), jnp.bfloat16),
             pltpu.VMEM((parts, rows, columns), jnp.float32),
+            pltpu.SemaphoreType.DMA((model_width // block,)),
             pltpu.SemaphoreType.DMA((parts,)),
         ],
         compiler_params=pltpu.CompilerParams(vmem_limit_bytes=60 * MIB),
         cost_estimate=pl.CostEstimate(
-            flops=2 * rows * depth * count,
-            bytes_accessed=2 * depth * count + 2 * rows * (depth + count),
+            flops=2 * rows * model_width * (model_width + count),
+            bytes_accessed=2 * model_width * (model_width + count) + 8 * rows * model_width,
             transcendentals=rows * count,
         ),
-        name="embed_norm",
-    )(order, place, clean, gain.reshape(1, count), *weights)
+        name="project_embed",
+    )(order, place, sigma, latents, gain.reshape(1, count), out_weight, *attended, *weights)
 
 
 def reward_kernel(particles, scale, parts, offset, *refs):
     order_ref, place_ref, features_ref, head_ref, before_ref = refs[:5]
-    weight_refs, (out_ref, total_ref) = refs[5:-2], refs[-2:]
-    step = pl.program_id(0)
+    weight_refs, (out_ref, weight_vmem, sems) = refs[5:-3], refs[-3:]
+    shards, depth, columns = weight_refs[0].shape
     rows = features_ref.shape[1]
-    columns = weight_refs[0].shape[2]
-
-    @pl.when(step == 0)
-    def _():
-        total_ref[...] = jnp.zeros_like(total_ref)
-
-    for group in range(len(weight_refs) // parts):
+    count = shards * len(weight_refs) // parts
+
+    copies = []
+    for place in range(count):
+        group, shard = divmod(place, shards)
+        for index in range(parts):
+            copy = pltpu.make_async_copy(
+                weight_refs[group * parts + index].at[shard],
+                weight_vmem.at[place, index],
+                sems.at[place, index],
+            )
+            copy.start()
+            copies.append(copy)
+    pieces = [features_ref[order_ref[index]] for index in range(parts)]
+    total = jnp.zeros((rows, columns), jnp.float32)
+    for place in range(count):
+        for copy in copies[place * parts : (place + 1) * parts]:
+            copy.wait()
         hidden = sum(
-            jnp.dot(
-                features_ref[order_ref[index]],
-                weight_refs[group * parts + index][0],
-                preferred_element_type=jnp.float32,
-            )
+            jnp.dot(pieces[index], weight_vmem[place, index], preferred_element_type=jnp.float32)
             for index in range(parts)
         )
-        shard = place_ref[group * pl.num_programs(0) + step]
-        scored = jax.nn.gelu(hidden) * head_ref[shard]
-        total_ref[...] += jnp.sum(scored.reshape(particles, rows // particles, columns), axis=1)
-
-    @pl.when(step == pl.num_programs(0) - 1)
-    def _():
-        sums = jnp.sum(total_ref[...], axis=1, keepdims=True) * scale
-        out_rows = lax.broadcasted_iota(jnp.int32, before_ref.shape, 0)
-        lanes = lax.broadcasted_iota(jnp.int32, before_ref.shape, 1)
-        row = order_ref[parts] if offset == 0 else order_ref[parts + 1]
-        logits = before_ref[...]
-        for particle in range(particles):
-            here = jnp.logical_and(out_rows == row, lanes == particle)
-            logits += jnp.where(here, sums[particle : particle + 1], 0.0)
-        out_ref[...] = jnp.broadcast_to(logits[None], out_ref.shape)
+        total += jax.nn.gelu(hidden) * head_ref[place_ref[place]]
+
+    totals = jnp.sum(total.reshape(particles, rows // particles, columns), axis=1)
+    sums = jnp.sum(totals, axis=1, keepdims=True) * scale
+    out_rows = lax.broadcasted_iota(jnp.int32, before_ref.shape, 0)
+    lanes = lax.broadcasted_iota(jnp.int32, before_ref.shape, 1)
+    row = order_ref[parts + offset]
+    logits = before_ref[...]
+    for particle in range(particles):
+        here = jnp.logical_and(out_rows == row, lanes == particle)
+        logits += jnp.where(here, sums[particle : particle + 1], 0.0)
+    out_ref[...] = jnp.broadcast_to(logits[None], out_ref.shape)
 
 
 def reward(order, place, features, weights, parts, head, before, particles, scale, offset, copies):
@@ -290,20 +289,17 @@
     rows = features.shape[1]
     count = shards * len(weights) // parts
     smem = pl.BlockSpec(memory_space=pltpu.SMEM)
+    vmem = pl.BlockSpec(memory_space=pltpu.VMEM)
     return pl.pallas_call(
         functools.partial(reward_kernel, particles, scale, parts, offset),
-        grid=(shards,),
-        in_specs=[
-            smem,
-            smem,
-            pl.BlockSpec(features.shape, lambda i: (0, 0, 0)),
-            pl.BlockSpec(head.shape, lambda i: (0, 0, 0)),
-            pl.BlockSpec(before.shape, lambda i: (0, 0)),
-        ]
-        + [pl.BlockSpec((1, depth, columns), lambda i: (i, 0, 0))] * len(weights),
-        out_specs=pl.BlockSpec((copies, *before.shape), lambda i: (0, 0, 0)),
+        in_specs=[smem, smem, vmem, vmem, vmem]
+        + [pl.BlockSpec(memory_space=pl.ANY)] * len(weights),
+        out_specs=vmem,
         out_shape=jax.ShapeDtypeStruct((copies, *before.shape), jnp.float32),
-        scratch_shapes=[pltpu.VMEM((particles, columns), jnp.float32)],
+        scratch_shapes=[
+            pltpu.VMEM((count, parts, depth, columns), jnp.bfloat16),
+            pltpu.SemaphoreType.DMA((count, parts)),
+        ],
         compiler_params=pltpu.CompilerParams(vmem_limit_bytes=60 * MIB),
         cost_estimate=pl.CostEstimate(
             flops=2 * rows * parts * depth * count * columns,
@@ -422,26 +418,30 @@
 
     packed = [pack(queries, keys, values, chunks, width, chunk) for chunk in range(chunks)]
     arrived = [lax.all_to_all(piece, "seq", 0, 0, tiled=True) for piece in packed]
-    attended = [attention(piece, head_width) for piece in arrived]
-    returned = [lax.all_to_all(piece, "seq", 0, 0, tiled=True) for piece in attended]
-
-    embed_share, up_near = gate([embed_share, up_share], packed[-1])
+
     embed_share = jnp.concatenate([embed_share, swapped(embed_share, "seq", bits[-1])])
-    up_far = swapped(up_near, "seq", bits[-1])
+    up_near, up_far = up_share, swapped(up_share, "seq", bits[-1])
     near, far = offsets, [offset ^ bits[-1] for offset in offsets]
-    embed_share, up_near, up_far = gate([embed_share, up_near, up_far], arrived[0])
+    embed_share, up_near, up_far, arrived[0] = gate([embed_share, up_near, up_far, arrived[0]])
 
     embed_share = jnp.concatenate([embed_share, swapped(embed_share, "seq", 1)])
     near_pair = swapped(up_near, "seq", 1)
     far_groups = [shifted(up_far, "groups", k) for k in range(1, group_count)]
-    embed_share, near_pair, *far_groups = gate([embed_share, near_pair, *far_groups], attended[0])
+    attended = [attention(arrived[0], head_width)]
+    if chunks > 1:
+        embed_share, near_pair, arrived[1], *far_groups = gate(
+            [embed_share, near_pair, arrived[1], *far_groups]
+        )
+        attended.append(attention(arrived[1], head_width))
+    returned = [lax.all_to_all(piece, "seq", 0, 0, tiled=True) for piece in attended]
     embed_near = [embed_share] + [shifted(embed_share, "groups", k) for k in range(1, group_count)]
     near_groups = [up_near] + [shifted(up_near, "groups", k) for k in range(1, group_count)]
     pair_groups = [near_pair] + [shifted(near_pair, "groups", k) for k in range(1, group_count)]
     far_groups = [up_far] + far_groups
     far_pairs = [swapped(piece, "seq", 1) for piece in far_groups]
     up_parts = near_groups + pair_groups + far_groups + far_pairs
-    embed_near = gate(embed_near, attended[-1])
+    if chunks > 1:
+        *embed_near, returned[0] = gate([*embed_near, returned[0]])
     embed_parts = embed_near + [
         shifted(piece, "dom", k) for k in range(1, dom_count) for piece in embed_near
     ]
@@ -455,9 +455,19 @@
     )
 
     sigma = step_index.astype(jnp.float32) / STEPS
-    clean, stepped = project(sigma, latents, out_weight, returned, width)
+    stepped, features = project_embed(
+        embed_order,
+        embed_place,
+        sigma,
+        latents,
+        returned,
+        width,
+        out_weight,
+        embed_parts,
+        norm_gain,
+        group_count,
+    )
     stepped_other = shifted(stepped, "dom", 1)
-    features = embed(embed_order, embed_place, clean, embed_parts, norm_gain, group_count)
     features_other = shifted(features, "dom", 1)
 
     scale = potential_scale / math.sqrt(tokens * seq_count)

time: 207 us -> 229 us (1.11)
  waiting for transfers between devices: 97.7 us -> 119 us
  starting transfers between devices: 47.4 us -> 40.6 us
  local copies, waits for them, and re-layouts: 7.21 us -> 11.1 us
  Pallas kernels: 44.8 us -> 48.3 us
    all_to_all x4, waiting for transfers between devices: 27.2 us -> 37.3 us  [on_device(): lax.all_to_all(piece, 'seq', 0, 0, tiled=True)]
    ppermute x8, waiting for transfers between devices: 63.8 us -> 70.2 us  [swapped(): lax.ppermute(array, axis, [(i, i ^ bit) for i in range(lax.axis_size(axis...]
    pallas_call x2, Pallas kernels: 9.18 us -> 13.3 us  [reward(): pl.pallas_call(functools.partial(reward_kernel, particles, scale, parts,...]
    all_to_all x1, waiting for transfers between devices: 2.47 us -> 6.15 us  [on_device(): logits = lax.all_to_all(partial_both, ('dom', 'seq'), 0, 0, tiled=True)]
    unnamed x36 -> x42, local copies, waits for them, and re-layouts: 5.01 us -> 8.31 us
    ppermute x8, starting transfers between devices: 10.9 us -> 8.33 us  [swapped(): lax.ppermute(array, axis, [(i, i ^ bit) for i in range(lax.axis_size(axis...]
    all_to_all x1, starting transfers between devices: 7.61 us -> 5.15 us  [on_device(): logits = lax.all_to_all(partial_both, ('dom', 'seq'), 0, 0, tiled=True)]
    pallas_call x6 -> x4, Pallas kernels: 12 us -> 10.7 us  [the longest x1 10.7 us: project_embed(): pl.pallas_call(kernel, in_specs=[smem, smem, smem, vmem, vmem, anywhere]...]
  transfers between devices with their start and end apart: 21 -> 21, of which waited for: 8 -> 11; matrix products, arithmetic and copies ran while one was open for 5% -> 5% of each run, Pallas kernels for 20% -> 18%
where the time goes in v4:
time: 229 us
  waiting for transfers between devices  119 us (52%)
  Pallas kernels  48.3 us (21%)
  starting transfers between devices  40.6 us (18%)
  local copies, waits for them, and re-layouts  11.1 us (5%)
  other arithmetic  8.4 us (4%)
    ppermute x8, waiting for transfers between devices, swapped(): lax.ppermute(array, axis, [(i, i ^ bit) for i in range(lax.axis_size(axis...  70.2 us
    all_to_all x4, waiting for transfers between devices, on_device(): lax.all_to_all(piece, 'seq', 0, 0, tiled=True)  37.3 us
    all_to_all x4, starting transfers between devices, on_device(): lax.all_to_all(piece, 'seq', 0, 0, tiled=True)  21 us
    pallas_call x2, Pallas kernels, attention(): pl.pallas_call(functools.partial(attention_kernel, head_width, block_sour...  14 us
    pallas_call x2, Pallas kernels, reward(): pl.pallas_call(functools.partial(reward_kernel, particles, scale, parts,...  13.3 us
    pallas_call x1, Pallas kernels, project_embed(): pl.pallas_call(kernel, in_specs=[smem, smem, smem, vmem, vmem, anywhere]...  10.7 us
    ppermute x8, starting transfers between devices, swapped(): lax.ppermute(array, axis, [(i, i ^ bit) for i in range(lax.axis_size(axis...  8.33 us
    unnamed x42, local copies, waits for them, and re-layouts  8.31 us
  transfers between devices with their start and end apart: 21, of which 11 were waited for; matrix products, arithmetic and copies ran while one was open for 5% of the time, Pallas kernels for 18%

profile of v4, /device:TPU:0, one launch (start us, length us, event | category | flops | bytes accessed | tf_op | source)
XLA Modules:
  0.0 228.6 jit_solution(11304450985575832896)
XLA Ops:
  0.6 2.3 %pack_heads.2 = bf16[4,2,3,64,384]{4,3,2,1,0:T(8,128)(2,1)} custom-call(bf16[4,64,1536]{2,1,0:T(8,128)(2,1)} %q_ref.3, bf16[4,64,1536]{2,1,0:T(8,128)(2,1)} %k_ref.3, bf16[4,64,1536]{2,1,0:T(8,128)(2,1)} %v_ref.3), custom_call_target="tpu_custom_call" | custom-call | tf_op jit(solution)/shard_map/pack_heads/pallas_call | solution.py:39
  3.0 7.3 %all-to-all-start = ((bf16[8,3,64,384]{3,2,1,0:T(8,128)(2,1)}), bf16[8,3,64,384]{3,2,1,0:T(8,128)(2,1)S(1)}, u32[]{:S(2)}, u32[]{:S(2)}) async-start(bf16[8,3,64,384]{3,2,1,0:T(8,128)(2,1)} %bitcast.18), calls=%async_computation | async-start | bytes 2359296 | tf_op jit(solution)/shard_map/all_to_all | solution.py:420
  10.3 2.3 pack_heads.3
  12.5 26.3 %all-to-all-done.refs_3_ = bf16[8,3,64,384]{3,2,1,0:T(8,128)(2,1)S(1)} async-done(((bf16[8,3,64,384]{3,2,1,0:T(8,128)(2,1)}), bf16[8,3,64,384]{3,2,1,0:T(8,128)(2,1)S(1)}, u32[]{:S(2)}, u32[]{:S(2)}) %all-to-all-start) | async-done | bytes 1179680 | tf_op jit(solution)/shard_map/all_to_all | solution.py:420
  39.9 4.3 %all-to-all-start.1 = ((bf16[8,3,64,384]{3,2,1,0:T(8,128)(2,1)}), bf16[8,3,64,384]{3,2,1,0:T(8,128)(2,1)}, u32[]{:S(2)}, u32[]{:S(2)}) async-start(bf16[8,3,64,384]{3,2,1,0:T(8,128)(2,1)} %bitcast.17), calls=%async_computation.1 | async-start | bytes 2359296 | tf_op jit(solution)/shard_map/all_to_all | solution.py:420
  44.2 2.9 %collective-permute-start.2 = (bf16[1,512,256]{2,1,0:T(8,128)(2,1)S(1)}, bf16[1,512,256]{2,1,0:T(8,128)(2,1)S(1)}, u32[]{:S(2)}, u32[]{:S(2)}) collective-permute-start(bf16[1,512,256]{2,1,0:T(8,128)(2,1)S(1)} %dynamic-slice_bitcast_fusion), channel_id=1, source_target_pairs={{0,4},{1,5},{2,6},{3,7},{4,0},{5,1},{6,2},{7,3},{8,12},{9,13},{10,... | collective-permute-start | bytes 786440 | tf_op jit(solution)/shard_map/ppermute | solution.py:374
  48.1 38.7 %collective-permute-done.2 = bf16[1,512,256]{2,1,0:T(8,128)(2,1)S(1)} collective-permute-done((bf16[1,512,256]{2,1,0:T(8,128)(2,1)S(1)}, bf16[1,512,256]{2,1,0:T(8,128)(2,1)S(1)}, u32[]{:S(2)}, u32[]{:S(2)}) %collective-permute-start.2) | collective-permute-done | bytes 262176 | tf_op jit(solution)/shard_map/ppermute | solution.py:374
  89.0 14.3 %collective-permute-done.1 = bf16[2,192,256]{2,1,0:T(8,128)(2,1)S(1)} collective-permute-done((bf16[2,192,256]{2,1,0:T(8,128)(2,1)S(1)}, bf16[2,192,256]{2,1,0:T(8,128)(2,1)S(1)}, u32[]{:S(2)}, u32[]{:S(2)}) %collective-permute-start.1) | collective-permute-done | bytes 196640 | tf_op jit(solution)/shard_map/ppermute | solution.py:374
  104.9 1.3 collective-permute-start.4
  106.9 1.5 collective-permute-start.6
  108.4 8.7 %collective-permute-done.4 = bf16[4,192,256]{2,1,0:T(8,128)(2,1)S(1)} collective-permute-done((bf16[4,192,256]{2,1,0:T(8,128)(2,1)}, bf16[4,192,256]{2,1,0:T(8,128)(2,1)S(1)}, u32[]{:S(2)}, u32[]{:S(2)}) %collective-permute-start.4) | collective-permute-done | bytes 393248 | tf_op jit(solution)/shard_map/ppermute | solution.py:374
  117.1 1.9 pad_maximum_fusion.refs_0_
  119.1 5.7 %collective-permute-done.5.refs_1_ = bf16[2,512,256]{2,1,0:T(8,128)(2,1)S(1)} collective-permute-done((bf16[2,512,256]{2,1,0:T(8,128)(2,1)}, bf16[2,512,256]{2,1,0:T(8,128)(2,1)S(1)}, u32[]{:S(2)}, u32[]{:S(2)}) %collective-permute-start.5) | collective-permute-done | bytes 524320 | tf_op jit(solution)/shard_map/ppermute | solution.py:374
  126.4 1.5 collective-permute-start.7
  127.9 6.9 %attention.2 = bf16[8,64,384]{2,1,0:T(8,128)(2,1)} custom-call(bf16[8,3,64,384]{3,2,1,0:T(8,128)(2,1)} %get-tuple-element.19.qkv_ref), custom_call_target="tpu_custom_call" | custom-call | flops 402653184 | bytes 1572864 | tf_op jit(solution)/shard_map/attention/pallas_call | solution.py:113
  134.9 5.8 %all-to-all-start.2 = ((bf16[8,64,384]{2,1,0:T(8,128)(2,1)}), bf16[8,64,384]{2,1,0:T(8,128)(2,1)S(1)}, u32[]{:S(2)}, u32[]{:S(2)}) async-start(bf16[8,64,384]{2,1,0:T(8,128)(2,1)} %attention.2), calls=%async_computation.2 | async-start | bytes 786432 | tf_op jit(solution)/shard_map/all_to_all | solution.py:436
  141.3 9.0 %all-to-all-done.2.refs_2_ = bf16[8,64,384]{2,1,0:T(8,128)(2,1)S(1)} async-done(((bf16[8,64,384]{2,1,0:T(8,128)(2,1)}), bf16[8,64,384]{2,1,0:T(8,128)(2,1)S(1)}, u32[]{:S(2)}, u32[]{:S(2)}) %all-to-all-start.2) | async-done | bytes 393248 | tf_op jit(solution)/shard_map/all_to_all | solution.py:436
  152.5 7.1 %attention.3 = bf16[8,64,384]{2,1,0:T(8,128)(2,1)} custom-call(bf16[8,3,64,384]{3,2,1,0:T(8,128)(2,1)} %get-tuple-element.21.qkv_ref), custom_call_target="tpu_custom_call" | custom-call | flops 402653184 | bytes 1572864 | tf_op jit(solution)/shard_map/attention/pallas_call | solution.py:113
  159.6 3.7 %all-to-all-start.3 = ((bf16[8,64,384]{2,1,0:T(8,128)(2,1)}), bf16[8,64,384]{2,1,0:T(8,128)(2,1)S(1)}, u32[]{:S(2)}, u32[]{:S(2)}) async-start(bf16[8,64,384]{2,1,0:T(8,128)(2,1)} %attention.3), calls=%async_computation.3 | async-start | bytes 786432 | tf_op jit(solution)/shard_map/all_to_all | solution.py:436
  165.8 1.3 broadcast_xor_fusion.1.refs_1_
  169.4 2.1 collective-permute-start.14
  171.5 1.5 collective-permute-start.13
  173.1 2.0 all-to-all-done.3
  175.9 10.7 %project_embed.1 = (bf16[4,64,1536]{2,1,0:T(8,128)(2,1)}, bf16[2,256,512]{2,1,0:T(8,128)(2,1)}) custom-call(s32[4]{0:T(128)} %add.75.refs_0_, s32[8]{0:T(128)} %broadcast_xor_fusion.1.refs_1_, f32[1]{0:T(128)S(6)} %div.19.refs_2_, bf16[4,64,1536]{2,1,0:T(8,128)(2,1)} %refs_3_.1, f32[1,1024]{1,0:T(1,128)} %bitcast.22, bf16[1536,1536]{1,0:T(8,128)(2,1)} %refs_5_.1, ...), custom_call_target="tpu_custom_call" | custom-call | flops 2013265920 | bytes 11010048 | tf_op jit(solution)/shard_map/project_embed/pallas_call | solution.py:219
  188.5 4.8 %collective-permute-done.13.refs_8_ = bf16[2,512,256]{2,1,0:T(8,128)(2,1)} collective-permute-done((bf16[2,512,256]{2,1,0:T(8,128)(2,1)S(1)}, bf16[2,512,256]{2,1,0:T(8,128)(2,1)}, u32[]{:S(2)}, u32[]{:S(2)}) %collective-permute-start.13) | collective-permute-done | bytes 524320 | tf_op jit(solution)/shard_map/ppermute | solution.py:370
  193.4 1.9 collective-permute-done.15.refs_12_
  195.3 6.6 %reward.2 = f32[1,8,128]{2,1,0:T(8,128)} custom-call(s32[4]{0:T(128)} %pad_add_fusion.1.refs_0_, s32[8]{0:T(128)} %broadcast_xor_fusion.refs_1_, bf16[2,256,512]{2,1,0:T(8,128)(2,1)} %get-tuple-element.25.refs_2_, f32[8,1,256]{2,1,0:T(1,128)} %constant_dynamic-slice_fusion.refs_3_, f32[8,128]{1,0:T(8,128)} %broadcast_select_fusion.refs_4_, ...), custom_call_target="tpu_custom_call" | custom-call | flops 1073741824 | bytes 4194304 | tf_op jit(solution)/shard_map/reward/pallas_call | solution.py:293
  202.7 6.7 %reward.3 = f32[16,8,128]{2,1,0:T(8,128)} custom-call(s32[4]{0:T(128)} %pad_add_fusion.1.refs_0_, s32[8]{0:T(128)} %broadcast_xor_fusion.refs_1_, bf16[2,256,512]{2,1,0:T(8,128)(2,1)} %copy-done.14, f32[8,1,256]{2,1,0:T(1,128)} %constant_dynamic-slice_fusion.refs_3_, f32[8,128]{1,0:T(8,128)} %bitcast.21, bf16[2,512,256]{2,1,0:T(8,128)(2,1)} %get-tuple-element.16.refs_5_, ...), custom_call_target="tpu_custom_call" | custom-call | flops 1073741824 | bytes 4194304 | tf_op jit(solution)/shard_map/reward/pallas_call | solution.py:293
  209.3 5.2 %all-to-all-start.4 = ((f32[16,8,128]{2,1,0:T(8,128)}), f32[16,8,128]{2,1,0:T(8,128)S(1)}, u32[]{:S(2)}, u32[]{:S(2)}) async-start(f32[16,8,128]{2,1,0:T(8,128)} %reward.3), calls=%async_computation.4 | async-start | bytes 131072 | tf_op jit(solution)/shard_map/all_to_all | solution.py:492
  215.1 6.2 %all-to-all-done.4.parts_ref = f32[16,8,128]{2,1,0:T(8,128)S(1)} async-done(((f32[16,8,128]{2,1,0:T(8,128)}), f32[16,8,128]{2,1,0:T(8,128)S(1)}, u32[]{:S(2)}, u32[]{:S(2)}) %all-to-all-start.4) | async-done | bytes 65568 | tf_op jit(solution)/shard_map/all_to_all | solution.py:492
  221.9 1.6 log_weights.1
  224.4 4.2 %resample.1 = bf16[4,64,1536]{2,1,0:T(8,128)(2,1)} custom-call(s32[3,4]{1,0:T(4,128)} %pad_add_fusion.place_ref, bf16[4,64,1536]{2,1,0:T(8,128)(2,1)} %get-tuple-element.24.own_ref, bf16[4,64,1536]{2,1,0:T(8,128)(2,1)} %copy-done.13), custom_call_target="tpu_custom_call" | custom-call | tf_op jit(solution)/shard_map/resample/pallas_call | solution.py:351
  (85 shorter events, 21.1 us)
Async XLA Ops:
  0.6 43.5 %copy-start = (bf16[1024,512]{1,0:T(8,128)(2,1)S(1)}, bf16[1024,512]{1,0:T(8,128)(2,1)}, u32[]{:S(2)}) copy-start(bf16[1024,512]{1,0:T(8,128)(2,1)} %param.22) | copy-start | bytes 3145732
  3.0 35.9 %all-to-all-start = ((bf16[8,3,64,384]{3,2,1,0:T(8,128)(2,1)}), bf16[8,3,64,384]{3,2,1,0:T(8,128)(2,1)S(1)}, u32[]{:S(2)}, u32[]{:S(2)}) async-start(bf16[8,3,64,384]{3,2,1,0:T(8,128)(2,1)} %bitcast.18), calls=%async_computation | async-start | bytes 2359296 | tf_op jit(solution)/shard_map/all_to_all | solution.py:420
  39.9 79.2 %all-to-all-start.1 = ((bf16[8,3,64,384]{3,2,1,0:T(8,128)(2,1)}), bf16[8,3,64,384]{3,2,1,0:T(8,128)(2,1)}, u32[]{:S(2)}, u32[]{:S(2)}) async-start(bf16[8,3,64,384]{3,2,1,0:T(8,128)(2,1)} %bitcast.17), calls=%async_computation.1 | async-start | bytes 2359296 | tf_op jit(solution)/shard_map/all_to_all | solution.py:420
  44.2 42.6 %collective-permute-start.2 = (bf16[1,512,256]{2,1,0:T(8,128)(2,1)S(1)}, bf16[1,512,256]{2,1,0:T(8,128)(2,1)S(1)}, u32[]{:S(2)}, u32[]{:S(2)}) collective-permute-start(bf16[1,512,256]{2,1,0:T(8,128)(2,1)S(1)} %dynamic-slice_bitcast_fusion), channel_id=1, source_target_pairs={{0,4},{1,5},{2,6},{3,7},{4,0},{5,1},{6,2},{7,3},{8,12},{9,13},{10,... | collective-permute-start | bytes 786440 | tf_op jit(solution)/shard_map/ppermute | solution.py:374
  47.9 40.0 %collective-permute-start = (bf16[1,192,256]{2,1,0:T(8,128)(2,1)S(1)}, bf16[1,192,256]{2,1,0:T(8,128)(2,1)S(1)}, u32[]{:S(2)}, u32[]{:S(2)}) collective-permute-start(bf16[1,192,256]{2,1,0:T(8,128)(2,1)S(1)} %dynamic-slice_bitcast_fusion.1), channel_id=1, source_target_pairs={{0,4},{1,5},{2,6},{3,7},{4,0},{5,1},{6,2},{7,3},{8,12},{9,13},{10,... | collective-permute-start | bytes 294920 | tf_op jit(solution)/shard_map/ppermute | solution.py:374
  86.8 17.2 %copy-start.1 = (bf16[2,512,256]{2,1,0:T(8,128)(2,1)}, bf16[2,512,256]{2,1,0:T(8,128)(2,1)S(1)}, u32[]{:S(2)}) copy-start(bf16[2,512,256]{2,1,0:T(8,128)(2,1)S(1)} %pad_maximum_fusion.1.refs_1_) | copy-start | bytes 1572868
  86.8 17.2 %collective-permute-start.3 = (bf16[2,512,256]{2,1,0:T(8,128)(2,1)S(1)}, bf16[2,512,256]{2,1,0:T(8,128)(2,1)S(1)}, u32[]{:S(2)}, u32[]{:S(2)}) collective-permute-start(bf16[2,512,256]{2,1,0:T(8,128)(2,1)S(1)} %pad_maximum_fusion.1.refs_1_), channel_id=1, source_target_pairs={{0,2},{1,3},{2,0},{3,1},{4,6},{5,7},{6,4},{7,5},{8,10},{9,11},{10,... | collective-permute-start | bytes 1572872 | tf_op jit(solution)/shard_map/ppermute | solution.py:374
  87.9 15.3 %collective-permute-start.1 = (bf16[2,192,256]{2,1,0:T(8,128)(2,1)S(1)}, bf16[2,192,256]{2,1,0:T(8,128)(2,1)S(1)}, u32[]{:S(2)}, u32[]{:S(2)}) collective-permute-start(bf16[2,192,256]{2,1,0:T(8,128)(2,1)S(1)} %pad_maximum_fusion.3), channel_id=1, source_target_pairs={{0,2},{1,3},{2,0},{3,1},{4,6},{5,7},{6,4},{7,5},{8,10},{9,11},{10,... | collective-permute-start | bytes 589832 | tf_op jit(solution)/shard_map/ppermute | solution.py:374
  104.9 12.3 %collective-permute-start.4 = (bf16[4,192,256]{2,1,0:T(8,128)(2,1)}, bf16[4,192,256]{2,1,0:T(8,128)(2,1)S(1)}, u32[]{:S(2)}, u32[]{:S(2)}) collective-permute-start(bf16[4,192,256]{2,1,0:T(8,128)(2,1)} %get-tuple-element.15), channel_id=1, source_target_pairs={{0,1},{1,0},{2,3},{3,2},{4,5},{5,4},{6,7},{7,6},{8,9},{9,8},{10,11... | collective-permute-start | bytes 1179656 | tf_op jit(solution)/shard_map/ppermute | solution.py:374
  106.2 18.6 %collective-permute-start.5 = (bf16[2,512,256]{2,1,0:T(8,128)(2,1)}, bf16[2,512,256]{2,1,0:T(8,128)(2,1)S(1)}, u32[]{:S(2)}, u32[]{:S(2)}) collective-permute-start(bf16[2,512,256]{2,1,0:T(8,128)(2,1)} %get-tuple-element.16.refs_5_), channel_id=1, source_target_pairs={{0,1},{1,0},{2,3},{3,2},{4,5},{5,4},{6,7},{7,6},{8,9},{9,8},{10,11... | collective-permute-start | bytes 1572872 | tf_op jit(solution)/shard_map/ppermute | solution.py:374
  106.9 17.8 %collective-permute-start.6 = (bf16[2,512,256]{2,1,0:T(8,128)(2,1)}, bf16[2,512,256]{2,1,0:T(8,128)(2,1)S(1)}, u32[]{:S(2)}, u32[]{:S(2)}) collective-permute-start(bf16[2,512,256]{2,1,0:T(8,128)(2,1)} %get-tuple-element.17.refs_9_), channel_id=1, source_target_pairs={{0,16},{16,0},{1,17},{17,1},{2,18},{18,2},{3,19},{19,3},{4,20},{20... | collective-permute-start | bytes 1572872 | tf_op jit(solution)/shard_map/ppermute | solution.py:370
  126.4 23.9 %collective-permute-start.7 = (bf16[8,192,256]{2,1,0:T(8,128)(2,1)}, bf16[8,192,256]{2,1,0:T(8,128)(2,1)S(1)}, u32[]{:S(2)}, u32[]{:S(2)}) collective-permute-start(bf16[8,192,256]{2,1,0:T(8,128)(2,1)} %get-tuple-element.18.refs_0_), channel_id=1, source_target_pairs={{0,16},{16,0},{1,17},{17,1},{2,18},{18,2},{3,19},{19,3},{4,20},{20... | collective-permute-start | bytes 2359304 | tf_op jit(solution)/shard_map/ppermute | solution.py:370
  127.9 12.7 %copy-start.16 = (f32[4096]{0:T(1024)S(1)}, f32[4096]{0:T(1024)}, u32[]{:S(2)}) copy-start(f32[4096]{0:T(1024)} %param.23) | copy-start | bytes 49156
  134.9 15.5 %all-to-all-start.2 = ((bf16[8,64,384]{2,1,0:T(8,128)(2,1)}), bf16[8,64,384]{2,1,0:T(8,128)(2,1)S(1)}, u32[]{:S(2)}, u32[]{:S(2)}) async-start(bf16[8,64,384]{2,1,0:T(8,128)(2,1)} %attention.2), calls=%async_computation.2 | async-start | bytes 786432 | tf_op jit(solution)/shard_map/all_to_all | solution.py:436
  140.7 11.8 %copy-start.17 = (s32[2]{0:T(128)}, s32[2]{0:T(128)S(1)}, u32[]{:S(2)}) copy-start(s32[2]{0:T(128)S(1)} %and_select_fusion) | copy-start | bytes 28
  152.0 21.0 %collective-permute-start.8 = (bf16[8,192,256]{2,1,0:T(8,128)(2,1)}, bf16[8,192,256]{2,1,0:T(8,128)(2,1)}, u32[]{:S(2)}, u32[]{:S(2)}) collective-permute-start(bf16[8,192,256]{2,1,0:T(8,128)(2,1)} %get-tuple-element.22.refs_8_), channel_id=1, source_target_pairs={{0,8},{8,0},{1,9},{9,1},{2,10},{10,2},{3,11},{11,3},{4,12},{12,4},... | collective-permute-start | bytes 2359304 | tf_op jit(solution)/shard_map/ppermute | solution.py:370
  152.0 23.1 %collective-permute-start.9 = (bf16[8,192,256]{2,1,0:T(8,128)(2,1)}, bf16[8,192,256]{2,1,0:T(8,128)(2,1)}, u32[]{:S(2)}, u32[]{:S(2)}) collective-permute-start(bf16[8,192,256]{2,1,0:T(8,128)(2,1)} %get-tuple-element.23.refs_9_), channel_id=1, source_target_pairs={{0,8},{8,0},{1,9},{9,1},{2,10},{10,2},{3,11},{11,3},{4,12},{12,4},... | collective-permute-start | bytes 2359304 | tf_op jit(solution)/shard_map/ppermute | solution.py:370
  152.5 15.7 %copy-start.2 = (bf16[2,512,256]{2,1,0:T(8,128)(2,1)S(1)}, bf16[2,512,256]{2,1,0:T(8,128)(2,1)}, u32[]{:S(2)}) copy-start(bf16[2,512,256]{2,1,0:T(8,128)(2,1)} %get-tuple-element.16.refs_5_) | copy-start | bytes 1572868
  152.5 16.9 %copy-start.5 = (bf16[2,512,256]{2,1,0:T(8,128)(2,1)S(1)}, bf16[2,512,256]{2,1,0:T(8,128)(2,1)}, u32[]{:S(2)}) copy-start(bf16[2,512,256]{2,1,0:T(8,128)(2,1)} %get-tuple-element.17.refs_9_) | copy-start | bytes 1572868
  152.5 19.0 %copy-start.7 = (bf16[2,512,256]{2,1,0:T(8,128)(2,1)S(1)}, bf16[2,512,256]{2,1,0:T(8,128)(2,1)}, u32[]{:S(2)}) copy-start(bf16[2,512,256]{2,1,0:T(8,128)(2,1)} %get-tuple-element.26.refs_7_) | copy-start | bytes 1572868
  152.5 20.5 %copy-start.9 = (bf16[2,512,256]{2,1,0:T(8,128)(2,1)S(1)}, bf16[2,512,256]{2,1,0:T(8,128)(2,1)}, u32[]{:S(2)}) copy-start(bf16[2,512,256]{2,1,0:T(8,128)(2,1)} %get-tuple-element.27.refs_10_) | copy-start | bytes 1572868
  159.6 15.5 %all-to-all-start.3 = ((bf16[8,64,384]{2,1,0:T(8,128)(2,1)}), bf16[8,64,384]{2,1,0:T(8,128)(2,1)S(1)}, u32[]{:S(2)}, u32[]{:S(2)}) async-start(bf16[8,64,384]{2,1,0:T(8,128)(2,1)} %attention.3), calls=%async_computation.3 | async-start | bytes 786432 | tf_op jit(solution)/shard_map/all_to_all | solution.py:436
  168.2 18.5 %collective-permute-start.12 = (bf16[2,512,256]{2,1,0:T(8,128)(2,1)S(1)}, bf16[2,512,256]{2,1,0:T(8,128)(2,1)}, u32[]{:S(2)}, u32[]{:S(2)}) collective-permute-start(bf16[2,512,256]{2,1,0:T(8,128)(2,1)S(1)} %copy-done.2), channel_id=1, source_target_pairs={{0,16},{16,0},{1,17},{17,1},{2,18},{18,2},{3,19},{19,3},{4,20},{20... | collective-permute-start | bytes 1572872 | tf_op jit(solution)/shard_map/ppermute | solution.py:370
  169.4 19.1 %collective-permute-start.14 = (bf16[2,512,256]{2,1,0:T(8,128)(2,1)S(1)}, bf16[2,512,256]{2,1,0:T(8,128)(2,1)}, u32[]{:S(2)}, u32[]{:S(2)}) collective-permute-start(bf16[2,512,256]{2,1,0:T(8,128)(2,1)S(1)} %copy-done.5), channel_id=1, source_target_pairs={{0,1},{1,0},{2,3},{3,2},{4,5},{5,4},{6,7},{7,6},{8,9},{9,8},{10,11... | collective-permute-start | bytes 1572872 | tf_op jit(solution)/shard_map/ppermute | solution.py:374
  171.5 21.8 %collective-permute-start.13 = (bf16[2,512,256]{2,1,0:T(8,128)(2,1)S(1)}, bf16[2,512,256]{2,1,0:T(8,128)(2,1)}, u32[]{:S(2)}, u32[]{:S(2)}) collective-permute-start(bf16[2,512,256]{2,1,0:T(8,128)(2,1)S(1)} %copy-done.7), channel_id=1, source_target_pairs={{0,16},{16,0},{1,17},{17,1},{2,18},{18,2},{3,19},{19,3},{4,20},{20... | collective-permute-start | bytes 1572872 | tf_op jit(solution)/shard_map/ppermute | solution.py:370
  173.0 22.2 %collective-permute-start.15 = (bf16[2,512,256]{2,1,0:T(8,128)(2,1)S(1)}, bf16[2,512,256]{2,1,0:T(8,128)(2,1)}, u32[]{:S(2)}, u32[]{:S(2)}) collective-permute-start(bf16[2,512,256]{2,1,0:T(8,128)(2,1)S(1)} %copy-done.9), channel_id=1, source_target_pairs={{0,1},{1,0},{2,3},{3,2},{4,5},{5,4},{6,7},{7,6},{8,9},{9,8},{10,11... | collective-permute-start | bytes 1572872 | tf_op jit(solution)/shard_map/ppermute | solution.py:374
  175.9 11.3 %copy-start.18 = (s32[2]{0:T(128)S(1)}, s32[2]{0:T(128)}, u32[]{:S(2)}) copy-start(s32[2]{0:T(128)} %copy-done.17) | copy-start | bytes 28
  175.9 11.9 %copy-start.19 = (f32[4]{0:T(128)S(1)}, f32[4]{0:T(128)}, u32[]{:S(2)}) copy-start(f32[4]{0:T(128)} %param.24) | copy-start | bytes 52
  186.6 15.3 %collective-permute-start.11 = (bf16[2,256,512]{2,1,0:T(8,128)(2,1)}, bf16[2,256,512]{2,1,0:T(8,128)(2,1)S(1)}, u32[]{:S(2)}, u32[]{:S(2)}) collective-permute-start(bf16[2,256,512]{2,1,0:T(8,128)(2,1)} %get-tuple-element.25.refs_2_), channel_id=1, source_target_pairs={{0,8},{8,0},{1,9},{9,1},{2,10},{10,2},{3,11},{11,3},{4,12},{12,4},... | collective-permute-start | bytes 1572872 | tf_op jit(solution)/shard_map/ppermute | solution.py:370
  186.7 36.8 %collective-permute-start.10 = (bf16[4,64,1536]{2,1,0:T(8,128)(2,1)}, bf16[4,64,1536]{2,1,0:T(8,128)(2,1)S(1)}, u32[]{:S(2)}, u32[]{:S(2)}) collective-permute-start(bf16[4,64,1536]{2,1,0:T(8,128)(2,1)} %get-tuple-element.24.own_ref), channel_id=1, source_target_pairs={{0,8},{8,0},{1,9},{9,1},{2,10},{10,2},{3,11},{11,3},{4,12},{12,4},... | collective-permute-start | bytes 2359304 | tf_op jit(solution)/shard_map/ppermute | solution.py:370
  202.7 11.8 %copy-start.20 = (s32[4]{0:T(128)S(1)}, s32[4]{0:T(128)}, u32[]{:S(2)}) copy-start(s32[4]{0:T(128)} %param.25) | copy-start | bytes 52
  209.3 11.9 %all-to-all-start.4 = ((f32[16,8,128]{2,1,0:T(8,128)}), f32[16,8,128]{2,1,0:T(8,128)S(1)}, u32[]{:S(2)}, u32[]{:S(2)}) async-start(f32[16,8,128]{2,1,0:T(8,128)} %reward.3), calls=%async_computation.4 | async-start | bytes 131072 | tf_op jit(solution)/shard_map/all_to_all | solution.py:492
  (10 other events, 8.3 us)

commit v5 on v4

v5 whole, which is shorter than its diff:
```python
import functools
import math

import jax
import jax.numpy as jnp
from jax import lax
from jax.experimental import pallas as pl
from jax.experimental.pallas import tpu as pltpu
from jax.sharding import PartitionSpec as P

HEADS = 24
STEPS = 28
LANES = 128

potential_scale = 4.0
norm_eps = 1e-05
MIB = 1024 * 1024


def pack_kernel(chunks, width, ids_ref, q_ref, k_ref, v_ref, *refs):
    out_refs, packed_ref = refs[:-1], refs[-1]
    particles, tokens, model_width = q_ref.shape
    blocks = model_width // width
    part = width // chunks
    count = particles * blocks
    for index, ref in enumerate((q_ref, k_ref, v_ref)):
        for particle in range(particles):
            for block in range(blocks):
                for chunk in range(chunks):
                    start = block * width + chunk * part
                    packed_ref[chunk, particle * blocks + block, index] = ref[
                        particle, :, start : start + part
                    ]
    for chunk in range(chunks):
        for place in range(count):
            out_refs[chunk * count + place][...] = packed_ref[chunk, ids_ref[2] ^ place]


def pack(ids, queries, keys, values, chunks, width):
    particles, tokens, model_width = queries.shape
    count = particles * model_width // width
    part = width // chunks
    vmem = pl.BlockSpec(memory_space=pltpu.VMEM)
    shape = jax.ShapeDtypeStruct((3, tokens, part), queries.dtype)
    packed = pl.pallas_call(
        functools.partial(pack_kernel, chunks, width),
        in_specs=[pl.BlockSpec(memory_space=pltpu.SMEM)] + [vmem] * 3,
        out_specs=[vmem] * (chunks * count),
        out_shape=[shape] * (chunks * count),
        scratch_shapes=[pltpu.VMEM((chunks, count, 3, tokens, part), queries.dtype)],
        compiler_params=pltpu.CompilerParams(vmem_limit_bytes=16 * MIB),
        name="pack_heads",
    )(ids, queries, keys, values)
    return [list(packed[chunk * count : (chunk + 1) * count]) for chunk in range(chunks)]


def gate_kernel(*refs):
    pass


def gate(*groups):
    arrays = [array for group in groups for array in group]
    anywhere = pl.BlockSpec(memory_space=pl.ANY)
    count = len(arrays)
    gated = list(
        pl.pallas_call(
            gate_kernel,
            in_specs=[anywhere] * count,
            out_specs=[anywhere] * count,
            out_shape=[jax.ShapeDtypeStruct(array.shape, array.dtype) for array in arrays],
            input_output_aliases={index: index for index in range(count)},
            compiler_params=pltpu.CompilerParams(vmem_limit_bytes=MIB),
            name="gate",
        )(*arrays)
    )
    return [[gated.pop(0) for _ in group] for group in groups]


def attention_kernel(head_width, block_sources, *refs):
    sources = len(refs) // 2
    qkv_refs, out_refs = refs[:sources], refs[sources:]
    _, tokens, columns = qkv_refs[0].shape
    factor = 1.0 / math.sqrt(head_width) / math.log(2.0)
    k_all = jnp.concatenate([ref[1] for ref in qkv_refs], axis=0)
    v_all = jnp.concatenate([ref[2] for ref in qkv_refs], axis=0)
    for block in range(0, sources, block_sources):
        span = slice(block, block + block_sources)
        q_all = jnp.concatenate([ref[0] for ref in qkv_refs[span]], axis=0)
        pieces = []
        for head in range(columns // head_width):
            cols = slice(head * head_width, (head + 1) * head_width)
            scores = lax.dot_general(
                q_all[:, cols],
                k_all[:, cols],
                (((1,), (1,)), ((), ())),
                preferred_element_type=jnp.float32,
            )
            highest = jnp.max(scores, axis=1, keepdims=True)
            expanded = jnp.exp2((scores - highest) * factor)
            norm = 1.0 / jnp.sum(expanded, axis=1, keepdims=True)
            weights = (expanded * norm).astype(jnp.bfloat16)
            pieces.append(
                jnp.dot(weights, v_all[:, cols], preferred_element_type=jnp.float32)
            )
        joined = jnp.concatenate(pieces, axis=1).astype(jnp.bfloat16)
        for index, ref in enumerate(out_refs[span]):
            ref[...] = joined[index * tokens : (index + 1) * tokens]


def attention(arrived, head_width):
    sources = len(arrived)
    _, tokens, columns = arrived[0].shape
    total = sources * tokens
    block_sources = max(1, min(sources, 512 // tokens))
    while sources % block_sources:
        block_sources -= 1
    heads = columns // head_width
    step = LANES if columns % LANES == 0 and LANES % head_width == 0 else columns
    scores_bytes = 4 * block_sources * tokens * total
    return list(
        pl.pallas_call(
            functools.partial(attention_kernel, head_width, block_sources),
            grid=(columns // step,),
            in_specs=[pl.BlockSpec((3, tokens, step), lambda i: (0, 0, i))] * sources,
            out_specs=[pl.BlockSpec((tokens, step), lambda i: (0, i))] * sources,
            out_shape=[jax.ShapeDtypeStruct((tokens, columns), jnp.bfloat16)] * sources,
            compiler_params=pltpu.CompilerParams(
                vmem_limit_bytes=8 * MIB + 6 * scores_bytes
            ),
            cost_estimate=pl.CostEstimate(
                flops=4 * total * total * columns,
                bytes_accessed=8 * total * columns,
                transcendentals=heads * total * total,
            ),
            name="attention",
        )(*arrived)
    )


def project_kernel(chunks, parts, block, offsets, depth_parts, refs_in, refs_out):
    ids_ref, latents_ref, gain_ref, out_weight_ref = refs_in[:4]
    attended_refs, weight_refs = refs_in[4:-parts], refs_in[-parts:]
    dom, group, seq = ids_ref[0], ids_ref[1], ids_ref[2]
    sigma = ids_ref[3].astype(jnp.float32) * (1.0 / STEPS)
    stepped_ref, features_ref = refs_out[:2]
    out_vmem, weight_vmem, attended_ref, clean_ref, embedded_ref, out_sems, sems = refs_out[2:]
    particles, tokens, model_width = latents_ref.shape
    rows = particles * tokens
    shards, depth, columns = weight_refs[0].shape

    out_copies = []
    for index in range(model_width // block):
        cols = slice(index * block, (index + 1) * block)
        copy = pltpu.make_async_copy(
            out_weight_ref.at[:, cols], out_vmem.at[:, cols], out_sems.at[index]
        )
        copy.start()
        out_copies.append(copy)
    copies = []
    for index in range(parts):
        for shard in range(shards):
            start = pl.multiple_of((seq ^ offsets[shard]) * depth, depth)
            copy = pltpu.make_async_copy(
                weight_refs[index].at[shard],
                weight_vmem.at[index, pl.ds(start, depth)],
                sems.at[index],
            )
            copy.start()
            copies.append(copy)

    blocks, _, width = attended_ref.shape
    part = width // chunks
    count = particles * blocks
    for chunk in range(chunks):
        for index in range(count):
            place = seq ^ index
            rows_of = pl.ds(pl.multiple_of(place // blocks * tokens, tokens), tokens)
            attended_ref[place % blocks, rows_of, chunk * part : (chunk + 1) * part] = (
                attended_refs[chunk * count + index][...]
            )
    for index in range(model_width // block):
        cols = slice(index * block, (index + 1) * block)
        out_copies[index].wait()
        flat = latents_ref[:, :, cols].reshape(rows, block).astype(jnp.float32)
        velocity = flat + sum(
            jnp.dot(
                attended_ref[place],
                out_vmem[place * width : (place + 1) * width, cols],
                preferred_element_type=jnp.float32,
            )
            for place in range(blocks)
        )
        clean_ref[:, cols] = (flat - sigma * velocity).astype(jnp.bfloat16)
        stepped_ref[:, :, cols] = (
            (flat - velocity * (1.0 / STEPS)).astype(jnp.bfloat16).reshape(particles, tokens, block)
        )

    for index in range(parts):
        for copy in copies[index * shards : (index + 1) * shards]:
            copy.wait()
        doms = parts // depth_parts
        dom_of = (dom + doms - index // depth_parts) % doms
        group_of = (group + depth_parts - index % depth_parts) % depth_parts
        embedded_ref[dom_of * depth_parts + group_of] = jnp.dot(
            clean_ref[...], weight_vmem[index], preferred_element_type=jnp.float32
        )
    count = parts * columns
    blocks = [embedded_ref[index] for index in range(parts)]
    centre = sum(jnp.sum(piece, axis=1, keepdims=True) for piece in blocks) * (1.0 / count)
    blocks = [piece - centre for piece in blocks]
    variance = sum(jnp.sum(piece * piece, axis=1, keepdims=True) for piece in blocks) * (
        1.0 / count
    )
    inverse = lax.rsqrt(variance + norm_eps)
    share = features_ref.shape[2]
    for index, piece in enumerate(blocks):
        cols = slice(index * columns, (index + 1) * columns)
        feature = jax.nn.gelu(piece * inverse * gain_ref[:, cols]).astype(jnp.bfloat16)
        start = index * columns % share
        features_ref[index * columns // share, :, start : start + columns] = feature


def project_embed(ids, offsets, latents, attended, width, out_weight, weights, gain, depth_parts):
    particles, tokens, model_width = latents.shape
    rows = particles * tokens
    chunks, parts = len(attended), len(weights)
    columns = weights[0].shape[2]
    count = parts * columns
    block = 256 if model_width % 256 == 0 else model_width
    pieces = [piece for chunk in attended for piece in chunk]
    vmem = pl.BlockSpec(memory_space=pltpu.VMEM)
    smem = pl.BlockSpec(memory_space=pltpu.SMEM)
    anywhere = pl.BlockSpec(memory_space=pl.ANY)
    inputs = 4 + len(pieces) + parts

    def kernel(*refs):
        project_kernel(
            chunks, parts, block, offsets, depth_parts, refs[:inputs], refs[inputs:]
        )

    return pl.pallas_call(
        kernel,
        in_specs=[smem, vmem, vmem, anywhere] + [vmem] * len(pieces) + [anywhere] * parts,
        out_specs=[vmem, vmem],
        out_shape=[
            jax.ShapeDtypeStruct(latents.shape, jnp.bfloat16),
            jax.ShapeDtypeStruct((depth_parts, rows, count // depth_parts), jnp.bfloat16),
        ],
        scratch_shapes=[
            pltpu.VMEM((model_width, model_width), jnp.bfloat16),
            pltpu.VMEM((parts, model_width, columns), jnp.bfloat16),
            pltpu.VMEM((model_width // width, rows, width), jnp.bfloat16),
            pltpu.VMEM((rows, model_width), jnp.bfloat16),
            pltpu.VMEM((parts, rows, columns), jnp.float32),
            pltpu.SemaphoreType.DMA((model_width // block,)),
            pltpu.SemaphoreType.DMA((parts,)),
        ],
        compiler_params=pltpu.CompilerParams(vmem_limit_bytes=28 * MIB),
        cost_estimate=pl.CostEstimate(
            flops=2 * rows * model_width * (model_width + count),
            bytes_accessed=2 * model_width * (model_width + count) + 8 * rows * model_width,
            transcendentals=rows * count,
        ),
        name="project_embed",
    )(ids, latents, gain.reshape(1, count), out_weight, *pieces, *weights)


def reward_kernel(particles, scale, parts, doms, offsets, *refs):
    ids_ref, features_ref, head_ref, before_ref = refs[:4]
    weight_refs, (out_ref, weight_vmem, sems) = refs[4:-3], refs[-3:]
    dom, group, seq = ids_ref[0], ids_ref[1], ids_ref[2]
    shards, depth, columns = weight_refs[0].shape
    rows = features_ref.shape[1]
    count = shards * len(weight_refs) // parts

    copies = []
    for place in range(count):
        pair, shard = divmod(place, shards)
        for index in range(parts):
            copy = pltpu.make_async_copy(
                weight_refs[pair * parts + index].at[shard],
                weight_vmem.at[place, index],
                sems.at[place, index],
            )
            copy.start()
            copies.append(copy)
    pieces = [features_ref[(group + parts - index) % parts] for index in range(parts)]
    total = jnp.zeros((rows, columns), jnp.float32)
    for place in range(count):
        for copy in copies[place * parts : (place + 1) * parts]:
            copy.wait()
        hidden = sum(
            jnp.dot(pieces[index], weight_vmem[place, index], preferred_element_type=jnp.float32)
            for index in range(parts)
        )
        total += jax.nn.gelu(hidden) * head_ref[(seq ^ offsets[place]) * doms + dom]

    totals = jnp.sum(total.reshape(particles, rows // particles, columns), axis=1)
    sums = jnp.sum(totals, axis=1, keepdims=True) * scale
    first = len(before_ref.shape) == 1
    shape = out_ref.shape[1:]
    out_rows = lax.broadcasted_iota(jnp.int32, shape, 0)
    lanes = lax.broadcasted_iota(jnp.int32, shape, 1)
    logits = jnp.zeros(shape, jnp.float32) if first else before_ref[...]
    row = dom if first else (dom + 1) % doms
    for particle in range(particles):
        here = jnp.logical_and(out_rows == row, lanes == particle)
        value = sums[particle : particle + 1]
        if first:
            value = value + jnp.where(seq == 0, before_ref[particle], 0.0)
        logits += jnp.where(here, value, 0.0)
    out_ref[...] = jnp.broadcast_to(logits[None], out_ref.shape)


def reward(ids, features, weights, parts, doms, offsets, head, before, particles, scale, copies):
    shards, depth, columns = weights[0].shape
    rows = features.shape[1]
    count = shards * len(weights) // parts
    smem = pl.BlockSpec(memory_space=pltpu.SMEM)
    vmem = pl.BlockSpec(memory_space=pltpu.VMEM)
    return pl.pallas_call(
        functools.partial(reward_kernel, particles, scale, parts, doms, offsets),
        in_specs=[smem, vmem, vmem, smem if before.ndim == 1 else vmem]
        + [pl.BlockSpec(memory_space=pl.ANY)] * len(weights),
        out_specs=vmem,
        out_shape=jax.ShapeDtypeStruct((copies, 8, LANES), jnp.float32),
        scratch_shapes=[
            pltpu.VMEM((count, parts, depth, columns), jnp.bfloat16),
            pltpu.SemaphoreType.DMA((count, parts)),
        ],
        compiler_params=pltpu.CompilerParams(vmem_limit_bytes=20 * MIB),
        cost_estimate=pl.CostEstimate(
            flops=2 * rows * parts * depth * count * columns,
            bytes_accessed=2 * parts * depth * count * columns,
            transcendentals=rows * count * columns,
        ),
        name="reward",
    )(ids, features, head, before, *weights)


def finish_kernel(particles, doms, ids_ref, parts_ref, resampled_ref, out_ref, same_ref):
    logits = jnp.sum(parts_ref[...], axis=0)
    rows = lax.broadcasted_iota(jnp.int32, logits.shape, 0)
    lanes = lax.broadcasted_iota(jnp.int32, logits.shape, 1)
    valid = jnp.logical_and(rows < doms, lanes < particles)
    highest = jnp.max(jnp.where(valid, logits, -jnp.inf))
    total = jnp.sum(jnp.where(valid, jnp.exp(logits - highest), 0.0), axis=1, keepdims=True)
    log_total = highest + jnp.log(jnp.sum(total, axis=0, keepdims=True))
    own = jnp.sum(jnp.where(rows == ids_ref[0], logits, 0.0), axis=0, keepdims=True)
    out_ref[...] = (own - log_total)[:, :particles]


def finish(ids, parts, resampled, particles, doms):
    vmem = pl.BlockSpec(memory_space=pltpu.VMEM)
    anywhere = pl.BlockSpec(memory_space=pl.ANY)
    log_weights, resampled = pl.pallas_call(
        functools.partial(finish_kernel, particles, doms),
        in_specs=[pl.BlockSpec(memory_space=pltpu.SMEM), vmem, anywhere],
        out_specs=[vmem, anywhere],
        out_shape=[
            jax.ShapeDtypeStruct((1, particles), jnp.float32),
            jax.ShapeDtypeStruct(resampled.shape, resampled.dtype),
        ],
        input_output_aliases={2: 1},
        compiler_params=pltpu.CompilerParams(vmem_limit_bytes=2 * MIB),
        name="log_weights",
    )(ids, parts, resampled)
    return resampled, log_weights.reshape(particles)


def resample_kernel(ids_ref, ancestors_ref, own_ref, other_ref, out_ref):
    index = pl.program_id(0)
    own = ancestors_ref[index] // pl.num_programs(0) == ids_ref[0]

    @pl.when(own)
    def _():
        out_ref[...] = own_ref[...]

    @pl.when(jnp.logical_not(own))
    def _():
        out_ref[...] = other_ref[...]


def resample(ids, ancestors, own, other):
    particles, tokens, columns = own.shape
    block = (1, tokens, columns)
    parent = pl.BlockSpec(block, lambda i, ids, ancestors: (ancestors[i] % particles, 0, 0))
    return pl.pallas_call(
        resample_kernel,
        grid_spec=pltpu.PrefetchScalarGridSpec(
            num_scalar_prefetch=2,
            grid=(particles,),
            in_specs=[parent, parent],
            out_specs=pl.BlockSpec(block, lambda i, ids, ancestors: (i, 0, 0)),
        ),
        out_shape=jax.ShapeDtypeStruct(own.shape, own.dtype),
        compiler_params=pltpu.CompilerParams(vmem_limit_bytes=4 * MIB),
        name="resample",
    )(ids, ancestors, own, other)


def shifted(array, axis, step):
    count = lax.axis_size(axis)
    return lax.ppermute(array, axis, [(i, (i + step) % count) for i in range(count)])


def swapped(array, axis, bit):
    return lax.ppermute(array, axis, [(i, i ^ bit) for i in range(lax.axis_size(axis))])


def exchange(pieces):
    return pieces[:1] + [
        swapped(piece, "seq", k + 1) for k, piece in enumerate(pieces[1:])
    ]


def on_device(
    latents,
    queries,
    keys,
    values,
    out_weight,
    step_index,
    embed_weight,
    norm_gain,
    up_weight,
    head_weight,
    prev_logw,
    ancestors,
):
    seq_count = lax.axis_size("seq")
    group_count = lax.axis_size("groups")
    dom_count = lax.axis_size("dom")
    holders = group_count * dom_count
    dom = lax.axis_index("dom")
    group = lax.axis_index("groups")
    seq = lax.axis_index("seq")
    particles, tokens, model_width = latents.shape
    head_width = model_width // HEADS
    width = particles * model_width // seq_count
    chunks = 2 if width % (2 * LANES) == 0 else 1

    ids = jnp.stack([dom, group, seq, step_index[0]]).astype(jnp.int32)

    embed_columns = embed_weight.shape[1] // holders
    embed_share = lax.dynamic_slice_in_dim(
        embed_weight, (dom * group_count + group) * embed_columns, embed_columns, 1
    )[None]
    up_depth = up_weight.shape[0] // group_count
    up_columns = up_weight.shape[1] // dom_count
    up_share = lax.dynamic_slice(
        up_weight, (group * up_depth, dom * up_columns), (up_depth, up_columns)
    )[None]
    bits = [1 << place for place in reversed(range(1, seq_count.bit_length() - 1))]
    near = [0]
    for bit in bits[:-1]:
        embed_share = jnp.concatenate([embed_share, swapped(embed_share, "seq", bit)])
        up_share = jnp.concatenate([up_share, swapped(up_share, "seq", bit)])
        near = near + [offset ^ bit for offset in near]
    far = [offset ^ bits[-1] for offset in near]

    packed = pack(ids, queries, keys, values, chunks, width)
    (embed_share, up_near), packed[0] = gate([embed_share, up_share], packed[0])

    arrived = [exchange(packed[0])]
    embed_share = jnp.concatenate([embed_share, swapped(embed_share, "seq", bits[-1])])
    up_far = swapped(up_near, "seq", bits[-1])
    (embed_share, up_near, up_far), arrived[0], *packed[1:] = gate(
        [embed_share, up_near, up_far], arrived[0], *packed[1:]
    )

    arrived += [exchange(piece) for piece in packed[1:]]
    embed_share = jnp.concatenate([embed_share, swapped(embed_share, "seq", 1)])
    near_pair = swapped(up_near, "seq", 1)
    far_groups = [up_far] + [shifted(up_far, "groups", k) for k in range(1, group_count)]
    attended = [attention(arrived[0], head_width)]
    (embed_share, near_pair), far_groups, attended[0], *arrived[1:] = gate(
        [embed_share, near_pair], far_groups, attended[0], *arrived[1:]
    )

    returned = [exchange(attended[0])]
    embed_near = [embed_share] + [shifted(embed_share, "groups", k) for k in range(1, group_count)]
    far_pairs = [swapped(far_groups[0], "seq", 1)]
    attended += [attention(piece, head_width) for piece in arrived[1:]]
    (up_near, near_pair), embed_near, far_groups[1:], returned[0], *attended[1:] = gate(
        [up_near, near_pair], embed_near, far_groups[1:], returned[0], *attended[1:]
    )

    returned += [exchange(pieces) for pieces in attended[1:]]
    embed_parts = embed_near + [
        shifted(piece, "dom", k) for k in range(1, dom_count) for piece in embed_near
    ]
    near_groups = [up_near] + [shifted(up_near, "groups", k) for k in range(1, group_count)]
    pair_groups = [near_pair] + [shifted(near_pair, "groups", k) for k in range(1, group_count)]
    far_pairs += [swapped(piece, "seq", 1) for piece in far_groups[1:]]
    up_parts = near_groups + pair_groups + far_groups + far_pairs
    embed_offsets = near + far + [offset ^ 1 for offset in near + far]
    up_offsets = near + [offset ^ 1 for offset in near] + far + [offset ^ 1 for offset in far]

    stepped, features = project_embed(
        ids,
        embed_offsets,
        latents,
        returned,
        width,
        out_weight,
        embed_parts,
        norm_gain,
        group_count,
    )
    stepped_other = shifted(stepped, "dom", 1)
    features_other = shifted(features, "dom", 1)

    scale = potential_scale / math.sqrt(tokens * seq_count)
    head = head_weight.reshape(seq_count * dom_count, 1, up_columns)
    score = functools.partial(
        reward,
        ids,
        weights=up_parts,
        parts=group_count,
        doms=dom_count,
        offsets=up_offsets,
        head=head,
        particles=particles,
        scale=scale,
    )
    partial_own = score(features, before=prev_logw, copies=1)[0]
    partial_both = score(features_other, before=partial_own, copies=dom_count * seq_count)
    logits = lax.all_to_all(partial_both, ("dom", "seq"), 0, 0, tiled=True)
    resampled = resample(ids, ancestors.astype(jnp.int32), stepped, stepped_other)
    return finish(ids, logits, resampled, particles, dom_count)


def solution(mesh):
    in_specs = (
        P(("groups", "dom"), "seq", None),
        P(("groups", "dom"), "seq", None),
        P(("groups", "dom"), "seq", None),
        P(("groups", "dom"), "seq", None),
        P(),
        P("groups"),
        P("seq", None),
        P(),
        P(None, "seq"),
        P(),
        P(("groups", "dom")),
        P(("groups", "dom")),
    )
    out_specs = (P(("groups", "dom"), "seq", None), P(("groups", "dom")))
    return jax.shard_map(
        on_device, mesh=mesh, in_specs=in_specs, out_specs=out_specs, check_vma=False
    )
```

time: 229 us -> 211 us (0.921)
  starting transfers between devices: 40.6 us -> 67.7 us
  waiting for transfers between devices: 119 us -> 98.1 us
  Pallas kernels: 48.3 us -> 37.5 us
  other arithmetic: 8.4 us -> 0.26 us
  local copies, waits for them, and re-layouts: 11.1 us -> 5.57 us
    ppermute x8 -> x36, starting transfers between devices: 8.33 us -> 58.3 us  [swapped(): lax.ppermute(array, axis, [(i, i ^ bit) for i in range(lax.axis_size(axis...]
    all_to_all x4 -> x0, waiting for transfers between devices: 37.3 us -> none  [on_device(): lax.all_to_all(piece, 'seq', 0, 0, tiled=True)]
    all_to_all x4 -> x0, starting transfers between devices: 21 us -> none  [on_device(): lax.all_to_all(piece, 'seq', 0, 0, tiled=True)]
    ppermute x8 -> x36, waiting for transfers between devices: 70.2 us -> 90.2 us  [swapped(): lax.ppermute(array, axis, [(i, i ^ bit) for i in range(lax.axis_size(axis...]
    unnamed x42 -> x22, local copies, waits for them, and re-layouts: 8.31 us -> 4.65 us
    pallas_call x2, Pallas kernels: 13.3 us -> 10.4 us  [reward(): pl.pallas_call(functools.partial(reward_kernel, particles, scale, parts,...]
    pallas_call x3 -> x2, Pallas kernels: 15.3 us -> 12.5 us  [the longest x1 11.5 us: project_embed(): pl.pallas_call(kernel, in_specs=[smem, vmem, vmem, anywhere] + [vmem] * l...]
    pallas_call x2, Pallas kernels: 14 us -> 11.2 us  [attention(): pl.pallas_call(functools.partial(attention_kernel, head_width, block_sour...]
  transfers between devices with their start and end apart: 21 -> 45, of which waited for: 11 -> 14; matrix products, arithmetic and copies ran while one was open for 5% -> 1% of each run, Pallas kernels for 18% -> 17%
where the time goes in v5:
time: 211 us
  waiting for transfers between devices  98.1 us (46%)
  starting transfers between devices  67.7 us (32%)
  Pallas kernels  37.5 us (18%)
  local copies, waits for them, and re-layouts  5.57 us (3%)
    ppermute x36, waiting for transfers between devices, swapped(): lax.ppermute(array, axis, [(i, i ^ bit) for i in range(lax.axis_size(axis...  90.2 us
    ppermute x36, starting transfers between devices, swapped(): lax.ppermute(array, axis, [(i, i ^ bit) for i in range(lax.axis_size(axis...  58.3 us
    pallas_call x1, Pallas kernels, project_embed(): pl.pallas_call(kernel, in_specs=[smem, vmem, vmem, anywhere] + [vmem] * l...  11.5 us
    pallas_call x2, Pallas kernels, attention(): pl.pallas_call(functools.partial(attention_kernel, head_width, block_sour...  11.2 us
    pallas_call x2, Pallas kernels, reward(): pl.pallas_call(functools.partial(reward_kernel, particles, scale, parts,...  10.4 us
    ppermute x8, starting transfers between devices, shifted(): lax.ppermute(array, axis, [(i, (i + step) % count) for i in range(count)])  4.83 us
    all_to_all x1, waiting for transfers between devices, on_device(): logits = lax.all_to_all(partial_both, ('dom', 'seq'), 0, 0, tiled=True)  4.71 us
    unnamed x22, local copies, waits for them, and re-layouts  4.65 us
  transfers between devices with their start and end apart: 45, of which 14 were waited for; matrix products, arithmetic and copies ran while one was open for 1% of the time, Pallas kernels for 17%

profile of v5, /device:TPU:0, one launch (start us, length us, event | category | flops | bytes accessed | tf_op | source)
XLA Modules:
  0.0 210.8 jit_solution(18017465492823439370)
XLA Ops:
  1.9 4.1 %collective-permute-start.1 = (bf16[1,512,256]{2,1,0:T(8,128)(2,1)S(1)}, bf16[1,512,256]{2,1,0:T(8,128)(2,1)S(1)}, u32[]{:S(2)}, u32[]{:S(2)}) collective-permute-start(bf16[1,512,256]{2,1,0:T(8,128)(2,1)S(1)} %dynamic-slice_bitcast_fusion), channel_id=1, source_target_pairs={{0,4},{1,5},{2,6},{3,7},{4,0},{5,1},{6,2},{7,3},{8,12},{9,13},{10,... | collective-permute-start | bytes 786440 | tf_op jit(solution)/shard_map/ppermute | solution.py:408
  12.0 10.1 %collective-permute-done = bf16[1,192,256]{2,1,0:T(8,128)(2,1)S(1)} collective-permute-done((bf16[1,192,256]{2,1,0:T(8,128)(2,1)S(1)}, bf16[1,192,256]{2,1,0:T(8,128)(2,1)S(1)}, u32[]{:S(2)}, u32[]{:S(2)}) %collective-permute-start) | collective-permute-done | bytes 98336 | tf_op jit(solution)/shard_map/ppermute | solution.py:408
  24.3 4.5 %collective-permute-start.10 = (bf16[3,64,384]{2,1,0:T(8,128)(2,1)S(1)}, bf16[3,64,384]{2,1,0:T(8,128)(2,1)S(1)}, u32[]{:S(2)}, u32[]{:S(2)}) collective-permute-start(bf16[3,64,384]{2,1,0:T(8,128)(2,1)S(1)} %get-tuple-element.125), channel_id=1, source_target_pairs={{0,7},{1,6},{2,5},{3,4},{4,3},{5,2},{6,1},{7,0},{8,15},{9,14},{10,... | collective-permute-start | bytes 442376 | tf_op jit(solution)/shard_map/ppermute | solution.py:408
  29.3 17.6 %collective-permute-done.10.refs_10_ = bf16[3,64,384]{2,1,0:T(8,128)(2,1)S(1)} collective-permute-done((bf16[3,64,384]{2,1,0:T(8,128)(2,1)S(1)}, bf16[3,64,384]{2,1,0:T(8,128)(2,1)S(1)}, u32[]{:S(2)}, u32[]{:S(2)}) %collective-permute-start.10) | collective-permute-done | bytes 147488 | tf_op jit(solution)/shard_map/ppermute | solution.py:408
  48.4 2.2 %collective-permute-start.8 = (bf16[3,64,384]{2,1,0:T(8,128)(2,1)S(1)}, bf16[3,64,384]{2,1,0:T(8,128)(2,1)S(1)}, u32[]{:S(2)}, u32[]{:S(2)}) collective-permute-start(bf16[3,64,384]{2,1,0:T(8,128)(2,1)S(1)} %get-tuple-element.123), channel_id=1, source_target_pairs={{0,5},{1,4},{2,7},{3,6},{4,1},{5,0},{6,3},{7,2},{8,13},{9,12},{10,... | collective-permute-start | bytes 442376 | tf_op jit(solution)/shard_map/ppermute | solution.py:408
  50.6 2.0 collective-permute-start.9
  52.6 3.2 %collective-permute-done.6.refs_6_ = bf16[3,64,384]{2,1,0:T(8,128)(2,1)S(1)} collective-permute-done((bf16[3,64,384]{2,1,0:T(8,128)(2,1)S(1)}, bf16[3,64,384]{2,1,0:T(8,128)(2,1)S(1)}, u32[]{:S(2)}, u32[]{:S(2)}) %collective-permute-start.6) | collective-permute-done | bytes 147488 | tf_op jit(solution)/shard_map/ppermute | solution.py:408
  55.8 7.9 %collective-permute-done.7.refs_7_ = bf16[3,64,384]{2,1,0:T(8,128)(2,1)S(1)} collective-permute-done((bf16[3,64,384]{2,1,0:T(8,128)(2,1)S(1)}, bf16[3,64,384]{2,1,0:T(8,128)(2,1)S(1)}, u32[]{:S(2)}, u32[]{:S(2)}) %collective-permute-start.7) | collective-permute-done | bytes 147488 | tf_op jit(solution)/shard_map/ppermute | solution.py:408
  63.7 3.1 %collective-permute-done.8.refs_8_ = bf16[3,64,384]{2,1,0:T(8,128)(2,1)S(1)} collective-permute-done((bf16[3,64,384]{2,1,0:T(8,128)(2,1)S(1)}, bf16[3,64,384]{2,1,0:T(8,128)(2,1)S(1)}, u32[]{:S(2)}, u32[]{:S(2)}) %collective-permute-start.8) | collective-permute-done | bytes 147488 | tf_op jit(solution)/shard_map/ppermute | solution.py:408
  72.9 16.3 %collective-permute-done.14.refs_13_ = bf16[3,64,384]{2,1,0:T(8,128)(2,1)S(1)} collective-permute-done((bf16[3,64,384]{2,1,0:T(8,128)(2,1)S(1)}, bf16[3,64,384]{2,1,0:T(8,128)(2,1)S(1)}, u32[]{:S(2)}, u32[]{:S(2)}) %collective-permute-start.14) | collective-permute-done | bytes 147488 | tf_op jit(solution)/shard_map/ppermute | solution.py:408
  89.2 3.0 %collective-permute-start.16 = (bf16[3,64,384]{2,1,0:T(8,128)(2,1)S(1)}, bf16[3,64,384]{2,1,0:T(8,128)(2,1)S(1)}, u32[]{:S(2)}, u32[]{:S(2)}) collective-permute-start(bf16[3,64,384]{2,1,0:T(8,128)(2,1)S(1)} %get-tuple-element.156), channel_id=1, source_target_pairs={{0,3},{1,2},{2,1},{3,0},{4,7},{5,6},{6,5},{7,4},{8,11},{9,10},{10,... | collective-permute-start | bytes 442376 | tf_op jit(solution)/shard_map/ppermute | solution.py:408
  93.3 3.5 %collective-permute-done.16.refs_15_ = bf16[3,64,384]{2,1,0:T(8,128)(2,1)S(1)} collective-permute-done((bf16[3,64,384]{2,1,0:T(8,128)(2,1)S(1)}, bf16[3,64,384]{2,1,0:T(8,128)(2,1)S(1)}, u32[]{:S(2)}, u32[]{:S(2)}) %collective-permute-start.16) | collective-permute-done | bytes 147488 | tf_op jit(solution)/shard_map/ppermute | solution.py:408
  96.8 5.1 %collective-permute-start.18 = (bf16[3,64,384]{2,1,0:T(8,128)(2,1)S(1)}, bf16[3,64,384]{2,1,0:T(8,128)(2,1)S(1)}, u32[]{:S(2)}, u32[]{:S(2)}) collective-permute-start(bf16[3,64,384]{2,1,0:T(8,128)(2,1)S(1)} %get-tuple-element.158), channel_id=1, source_target_pairs={{0,5},{1,4},{2,7},{3,6},{4,1},{5,0},{6,3},{7,2},{8,13},{9,12},{10,... | collective-permute-start | bytes 442376 | tf_op jit(solution)/shard_map/ppermute | solution.py:408
  101.9 6.4 %collective-permute-done.17.refs_16_ = bf16[3,64,384]{2,1,0:T(8,128)(2,1)S(1)} collective-permute-done((bf16[3,64,384]{2,1,0:T(8,128)(2,1)S(1)}, bf16[3,64,384]{2,1,0:T(8,128)(2,1)S(1)}, u32[]{:S(2)}, u32[]{:S(2)}) %collective-permute-start.17) | collective-permute-done | bytes 147488 | tf_op jit(solution)/shard_map/ppermute | solution.py:408
  110.2 2.4 %collective-permute-start.20 = (bf16[3,64,384]{2,1,0:T(8,128)(2,1)S(1)}, bf16[3,64,384]{2,1,0:T(8,128)(2,1)S(1)}, u32[]{:S(2)}, u32[]{:S(2)}) collective-permute-start(bf16[3,64,384]{2,1,0:T(8,128)(2,1)S(1)} %get-tuple-element.160), channel_id=1, source_target_pairs={{0,7},{1,6},{2,5},{3,4},{4,3},{5,2},{6,1},{7,0},{8,15},{9,14},{10,... | collective-permute-start | bytes 442376 | tf_op jit(solution)/shard_map/ppermute | solution.py:408
  112.6 5.6 %attention.2 = (bf16[64,384]{1,0:T(8,128)(2,1)S(1)}, bf16[64,384]{1,0:T(8,128)(2,1)S(1)}, bf16[64,384]{1,0:T(8,128)(2,1)S(1)}, bf16[64,384]{1,0:T(8,128)(2,1)S(1...) custom-call(bf16[3,64,384]{2,1,0:T(8,128)(2,1)S(1)} %get-tuple-eleme, ...), custom_call_target="tpu_custom_call" | custom-call | flops 402653184 | bytes 1572864 | tf_op jit(solution)/shard_map/attention/pallas_call | solution.py:121
  123.6 2.9 %collective-permute-start.25 = (bf16[64,384]{1,0:T(8,128)(2,1)S(1)}, bf16[64,384]{1,0:T(8,128)(2,1)S(1)}, u32[]{:S(2)}, u32[]{:S(2)}) collective-permute-start(bf16[64,384]{1,0:T(8,128)(2,1)S(1)} %get-tuple-element.168), channel_id=1, source_target_pairs={{0,4},{1,5},{2,6},{3,7},{4,0},{5,1},{6,2},{7,3},{8,12},{9,13},{10,... | collective-permute-start | bytes 147464 | tf_op jit(solution)/shard_map/ppermute | solution.py:408
  127.1 1.9 collective-permute-start.27
  129.0 2.8 %collective-permute-start.28 = (bf16[64,384]{1,0:T(8,128)(2,1)S(1)}, bf16[64,384]{1,0:T(8,128)(2,1)S(1)}, u32[]{:S(2)}, u32[]{:S(2)}) collective-permute-start(bf16[64,384]{1,0:T(8,128)(2,1)S(1)} %get-tuple-element.171), channel_id=1, source_target_pairs={{0,7},{1,6},{2,5},{3,4},{4,3},{5,2},{6,1},{7,0},{8,15},{9,14},{10,... | collective-permute-start | bytes 147464 | tf_op jit(solution)/shard_map/ppermute | solution.py:408
  131.8 5.6 %attention.3 = (bf16[64,384]{1,0:T(8,128)(2,1)S(1)}, bf16[64,384]{1,0:T(8,128)(2,1)S(1)}, bf16[64,384]{1,0:T(8,128)(2,1)S(1)}, bf16[64,384]{1,0:T(8,128)(2,1)S(1...) custom-call(bf16[3,64,384]{2,1,0:T(8,128)(2,1)S(1)} %get-tuple-eleme, ...), custom_call_target="tpu_custom_call" | custom-call | flops 402653184 | bytes 1572864 | tf_op jit(solution)/shard_map/attention/pallas_call | solution.py:121
  141.2 11.8 %collective-permute-done.29.refs_13_ = bf16[64,384]{1,0:T(8,128)(2,1)S(1)} collective-permute-done((bf16[64,384]{1,0:T(8,128)(2,1)S(1)}, bf16[64,384]{1,0:T(8,128)(2,1)S(1)}, u32[]{:S(2)}, u32[]{:S(2)}) %collective-permute-start.29) | collective-permute-done | bytes 49184 | tf_op jit(solution)/shard_map/ppermute | solution.py:408
  155.5 2.9 %collective-permute-done.31.refs_15_ = bf16[64,384]{1,0:T(8,128)(2,1)S(1)} collective-permute-done((bf16[64,384]{1,0:T(8,128)(2,1)S(1)}, bf16[64,384]{1,0:T(8,128)(2,1)S(1)}, u32[]{:S(2)}, u32[]{:S(2)}) %collective-permute-start.31) | collective-permute-done | bytes 49184 | tf_op jit(solution)/shard_map/ppermute | solution.py:408
  159.7 2.1 %collective-permute-start.34 = (bf16[64,384]{1,0:T(8,128)(2,1)S(1)}, bf16[64,384]{1,0:T(8,128)(2,1)S(1)}, u32[]{:S(2)}, u32[]{:S(2)}) collective-permute-start(bf16[64,384]{1,0:T(8,128)(2,1)S(1)} %get-tuple-element.202), channel_id=1, source_target_pairs={{0,6},{1,7},{2,4},{3,5},{4,2},{5,3},{6,0},{7,1},{8,14},{9,15},{10,... | collective-permute-start | bytes 147464 | tf_op jit(solution)/shard_map/ppermute | solution.py:408
  161.8 3.1 %collective-permute-done.33.refs_17_ = bf16[64,384]{1,0:T(8,128)(2,1)S(1)} collective-permute-done((bf16[64,384]{1,0:T(8,128)(2,1)S(1)}, bf16[64,384]{1,0:T(8,128)(2,1)S(1)}, u32[]{:S(2)}, u32[]{:S(2)}) %collective-permute-start.33) | collective-permute-done | bytes 49184 | tf_op jit(solution)/shard_map/ppermute | solution.py:408
  167.4 4.4 %collective-permute-done.35.refs_19_ = bf16[64,384]{1,0:T(8,128)(2,1)S(1)} collective-permute-done((bf16[64,384]{1,0:T(8,128)(2,1)S(1)}, bf16[64,384]{1,0:T(8,128)(2,1)S(1)}, u32[]{:S(2)}, u32[]{:S(2)}) %collective-permute-start.35) | collective-permute-done | bytes 49184 | tf_op jit(solution)/shard_map/ppermute | solution.py:408
  172.4 11.5 %project_embed.1 = (bf16[4,64,1536]{2,1,0:T(8,128)(2,1)S(1)}, bf16[2,256,512]{2,1,0:T(8,128)(2,1)S(1)}) custom-call(s32[4]{0:T(128)S(1)} %pad_add_fusion.ids_ref.refs_0_, bf16[4,64,1536]{2,1,0:T(8,128)(2,1)S(1)} %copy-done.4, f32[1,1024]{1,0:T(1,128)S(1)} %bitcast.16, bf16[1536,1536]{1,0:T(8,128)(2,1)S(1)} %bitcast.12, ...), custom_call_target="tpu_custom_call" | custom-call | flops 2013265920 | bytes 11010048 | tf_op jit(solution)/shard_map/project_embed/pallas_call | solution.py:241
  184.5 3.2 %collective-permute-done.40.refs_7_ = bf16[2,512,256]{2,1,0:T(8,128)(2,1)S(1)} collective-permute-done((bf16[2,512,256]{2,1,0:T(8,128)(2,1)S(1)}, bf16[2,512,256]{2,1,0:T(8,128)(2,1)S(1)}, u32[]{:S(2)}, u32[]{:S(2)}) %collective-permute-start.40) | collective-permute-done | bytes 524320 | tf_op jit(solution)/shard_map/ppermute | solution.py:404
  187.7 4.8 %reward.2 = f32[1,8,128]{2,1,0:T(8,128)S(1)} custom-call(s32[4]{0:T(128)S(1)} %pad_add_fusion.ids_ref.refs_0_, bf16[2,256,512]{2,1,0:T(8,128)(2,1)S(1)} %get-tuple-element.206.refs_1_, f32[16,1,256]{2,1,0:T(1,128)S(1)} %bitcast.13, f32[4]{0:T(128)S(1)} %copy-done.7, bf16[2,512,256]{2,1,0:T(8,128)(2,1)S(1)} %get-tuple-element.207.refs_4_, ...), custom_call_target="tpu_custom_call" | custom-call | flops 1073741824 | bytes 4194304 | tf_op jit(solution)/shard_map/reward/pallas_call | solution.py:321
  192.5 5.6 %reward.3 = f32[16,8,128]{2,1,0:T(8,128)} custom-call(s32[4]{0:T(128)S(1)} %pad_add_fusion.ids_ref.refs_0_, bf16[2,256,512]{2,1,0:T(8,128)(2,1)S(1)} %collective-permute-done.38.refs_1_, f32[16,1,256]{2,1,0:T(1,128)S(1)} %bitcast.14, f32[8,128]{1,0:T(8,128)S(1)} %bitcast.15, bf16[2,512,256]{2,1,0:T(8,128)(2,1)S(1)} %get-tuple-element.207.refs_4_, ...), custom_call_target="tpu_custom_call" | custom-call | flops 1073741824 | bytes 4194304 | tf_op jit(solution)/shard_map/reward/pallas_call | solution.py:321
  198.2 4.6 %all-to-all-start = ((f32[16,8,128]{2,1,0:T(8,128)}), f32[16,8,128]{2,1,0:T(8,128)S(1)}, u32[]{:S(2)}, u32[]{:S(2)}) async-start(f32[16,8,128]{2,1,0:T(8,128)} %reward.3), calls=%async_computation | async-start | bytes 131072 | tf_op jit(solution)/shard_map/all_to_all | solution.py:529
  202.8 2.0 resample.1.resampled_ref
  204.8 4.7 %all-to-all-done.parts_ref = f32[16,8,128]{2,1,0:T(8,128)S(1)} async-done(((f32[16,8,128]{2,1,0:T(8,128)}), f32[16,8,128]{2,1,0:T(8,128)S(1)}, u32[]{:S(2)}, u32[]{:S(2)}) %all-to-all-start) | async-done | bytes 65568 | tf_op jit(solution)/shard_map/all_to_all | solution.py:529
  (100 shorter events, 38.4 us)
Async XLA Ops:
  1.9 20.3 %collective-permute-start.1 = (bf16[1,512,256]{2,1,0:T(8,128)(2,1)S(1)}, bf16[1,512,256]{2,1,0:T(8,128)(2,1)S(1)}, u32[]{:S(2)}, u32[]{:S(2)}) collective-permute-start(bf16[1,512,256]{2,1,0:T(8,128)(2,1)S(1)} %dynamic-slice_bitcast_fusion), channel_id=1, source_target_pairs={{0,4},{1,5},{2,6},{3,7},{4,0},{5,1},{6,2},{7,3},{8,12},{9,13},{10,... | collective-permute-start | bytes 786440 | tf_op jit(solution)/shard_map/ppermute | solution.py:408
  6.9 15.2 %collective-permute-start = (bf16[1,192,256]{2,1,0:T(8,128)(2,1)S(1)}, bf16[1,192,256]{2,1,0:T(8,128)(2,1)S(1)}, u32[]{:S(2)}, u32[]{:S(2)}) collective-permute-start(bf16[1,192,256]{2,1,0:T(8,128)(2,1)S(1)} %dynamic-slice_bitcast_fusion.1), channel_id=1, source_target_pairs={{0,4},{1,5},{2,6},{3,7},{4,0},{5,1},{6,2},{7,3},{8,12},{9,13},{10,... | collective-permute-start | bytes 294920 | tf_op jit(solution)/shard_map/ppermute | solution.py:408
  22.2 44.5 %collective-permute-start.3 = (bf16[2,512,256]{2,1,0:T(8,128)(2,1)S(1)}, bf16[2,512,256]{2,1,0:T(8,128)(2,1)S(1)}, u32[]{:S(2)}, u32[]{:S(2)}) collective-permute-start(bf16[2,512,256]{2,1,0:T(8,128)(2,1)S(1)} %get-tuple-element.117.refs_1_), channel_id=1, source_target_pairs={{0,2},{1,3},{2,0},{3,1},{4,6},{5,7},{6,4},{7,5},{8,10},{9,11},{10,... | collective-permute-start | bytes 1572872 | tf_op jit(solution)/shard_map/ppermute | solution.py:408
  23.0 27.6 %collective-permute-start.2 = (bf16[2,192,256]{2,1,0:T(8,128)(2,1)S(1)}, bf16[2,192,256]{2,1,0:T(8,128)(2,1)S(1)}, u32[]{:S(2)}, u32[]{:S(2)}) collective-permute-start(bf16[2,192,256]{2,1,0:T(8,128)(2,1)S(1)} %get-tuple-element.116), channel_id=1, source_target_pairs={{0,2},{1,3},{2,0},{3,1},{4,6},{5,7},{6,4},{7,5},{8,10},{9,11},{10,... | collective-permute-start | bytes 589832 | tf_op jit(solution)/shard_map/ppermute | solution.py:408
  24.3 22.6 %collective-permute-start.10 = (bf16[3,64,384]{2,1,0:T(8,128)(2,1)S(1)}, bf16[3,64,384]{2,1,0:T(8,128)(2,1)S(1)}, u32[]{:S(2)}, u32[]{:S(2)}) collective-permute-start(bf16[3,64,384]{2,1,0:T(8,128)(2,1)S(1)} %get-tuple-element.125), channel_id=1, source_target_pairs={{0,7},{1,6},{2,5},{3,4},{4,3},{5,2},{6,1},{7,0},{8,15},{9,14},{10,... | collective-permute-start | bytes 442376 | tf_op jit(solution)/shard_map/ppermute | solution.py:408
  28.8 18.1 %collective-permute-start.4 = (bf16[3,64,384]{2,1,0:T(8,128)(2,1)S(1)}, bf16[3,64,384]{2,1,0:T(8,128)(2,1)S(1)}, u32[]{:S(2)}, u32[]{:S(2)}) collective-permute-start(bf16[3,64,384]{2,1,0:T(8,128)(2,1)S(1)} %get-tuple-element.119), channel_id=1, source_target_pairs={{0,1},{1,0},{2,3},{3,2},{4,5},{5,4},{6,7},{7,6},{8,9},{9,8},{10,11... | collective-permute-start | bytes 442376 | tf_op jit(solution)/shard_map/ppermute | solution.py:408
  29.3 19.1 %collective-permute-start.5 = (bf16[3,64,384]{2,1,0:T(8,128)(2,1)S(1)}, bf16[3,64,384]{2,1,0:T(8,128)(2,1)S(1)}, u32[]{:S(2)}, u32[]{:S(2)}) collective-permute-start(bf16[3,64,384]{2,1,0:T(8,128)(2,1)S(1)} %get-tuple-element.120), channel_id=1, source_target_pairs={{0,2},{1,3},{2,0},{3,1},{4,6},{5,7},{6,4},{7,5},{8,10},{9,11},{10,... | collective-permute-start | bytes 442376 | tf_op jit(solution)/shard_map/ppermute | solution.py:408
  46.9 16.8 %collective-permute-start.7 = (bf16[3,64,384]{2,1,0:T(8,128)(2,1)S(1)}, bf16[3,64,384]{2,1,0:T(8,128)(2,1)S(1)}, u32[]{:S(2)}, u32[]{:S(2)}) collective-permute-start(bf16[3,64,384]{2,1,0:T(8,128)(2,1)S(1)} %get-tuple-element.122), channel_id=1, source_target_pairs={{0,4},{1,5},{2,6},{3,7},{4,0},{5,1},{6,2},{7,3},{8,12},{9,13},{10,... | collective-permute-start | bytes 442376 | tf_op jit(solution)/shard_map/ppermute | solution.py:408
  48.4 18.3 %collective-permute-start.8 = (bf16[3,64,384]{2,1,0:T(8,128)(2,1)S(1)}, bf16[3,64,384]{2,1,0:T(8,128)(2,1)S(1)}, u32[]{:S(2)}, u32[]{:S(2)}) collective-permute-start(bf16[3,64,384]{2,1,0:T(8,128)(2,1)S(1)} %get-tuple-element.123), channel_id=1, source_target_pairs={{0,5},{1,4},{2,7},{3,6},{4,1},{5,0},{6,3},{7,2},{8,13},{9,12},{10,... | collective-permute-start | bytes 442376 | tf_op jit(solution)/shard_map/ppermute | solution.py:408
  50.6 16.1 %collective-permute-start.9 = (bf16[3,64,384]{2,1,0:T(8,128)(2,1)S(1)}, bf16[3,64,384]{2,1,0:T(8,128)(2,1)S(1)}, u32[]{:S(2)}, u32[]{:S(2)}) collective-permute-start(bf16[3,64,384]{2,1,0:T(8,128)(2,1)S(1)} %get-tuple-element.124), channel_id=1, source_target_pairs={{0,6},{1,7},{2,4},{3,5},{4,2},{5,3},{6,0},{7,1},{8,14},{9,15},{10,... | collective-permute-start | bytes 442376 | tf_op jit(solution)/shard_map/ppermute | solution.py:408
  66.7 43.5 %collective-permute-start.11 = (bf16[4,192,256]{2,1,0:T(8,128)(2,1)S(1)}, bf16[4,192,256]{2,1,0:T(8,128)(2,1)S(1)}, u32[]{:S(2)}, u32[]{:S(2)}) collective-permute-start(bf16[4,192,256]{2,1,0:T(8,128)(2,1)S(1)} %get-tuple-element.135), channel_id=1, source_target_pairs={{0,1},{1,0},{2,3},{3,2},{4,5},{5,4},{6,7},{7,6},{8,9},{9,8},{10,11... | collective-permute-start | bytes 1179656 | tf_op jit(solution)/shard_map/ppermute | solution.py:408
  68.3 50.0 %collective-permute-start.12 = (bf16[2,512,256]{2,1,0:T(8,128)(2,1)S(1)}, bf16[2,512,256]{2,1,0:T(8,128)(2,1)S(1)}, u32[]{:S(2)}, u32[]{:S(2)}) collective-permute-start(bf16[2,512,256]{2,1,0:T(8,128)(2,1)S(1)} %get-tuple-element.134.refs_0_), channel_id=1, source_target_pairs={{0,1},{1,0},{2,3},{3,2},{4,5},{5,4},{6,7},{7,6},{8,9},{9,8},{10,11... | collective-permute-start | bytes 1572872 | tf_op jit(solution)/shard_map/ppermute | solution.py:408
  68.8 49.5 %collective-permute-start.13 = (bf16[2,512,256]{2,1,0:T(8,128)(2,1)S(1)}, bf16[2,512,256]{2,1,0:T(8,128)(2,1)S(1)}, u32[]{:S(2)}, u32[]{:S(2)}) collective-permute-start(bf16[2,512,256]{2,1,0:T(8,128)(2,1)S(1)} %get-tuple-element.136.refs_2_), channel_id=1, source_target_pairs={{0,16},{16,0},{1,17},{17,1},{2,18},{18,2},{3,19},{19,3},{4,20},{20... | collective-permute-start | bytes 1572872 | tf_op jit(solution)/shard_map/ppermute | solution.py:404
  70.3 18.9 %collective-permute-start.14 = (bf16[3,64,384]{2,1,0:T(8,128)(2,1)S(1)}, bf16[3,64,384]{2,1,0:T(8,128)(2,1)S(1)}, u32[]{:S(2)}, u32[]{:S(2)}) collective-permute-start(bf16[3,64,384]{2,1,0:T(8,128)(2,1)S(1)} %get-tuple-element.154), channel_id=1, source_target_pairs={{0,1},{1,0},{2,3},{3,2},{4,5},{5,4},{6,7},{7,6},{8,9},{9,8},{10,11... | collective-permute-start | bytes 442376 | tf_op jit(solution)/shard_map/ppermute | solution.py:408
  71.8 20.3 %collective-permute-start.15 = (bf16[3,64,384]{2,1,0:T(8,128)(2,1)S(1)}, bf16[3,64,384]{2,1,0:T(8,128)(2,1)S(1)}, u32[]{:S(2)}, u32[]{:S(2)}) collective-permute-start(bf16[3,64,384]{2,1,0:T(8,128)(2,1)S(1)} %get-tuple-element.155), channel_id=1, source_target_pairs={{0,2},{1,3},{2,0},{3,1},{4,6},{5,7},{6,4},{7,5},{8,10},{9,11},{10,... | collective-permute-start | bytes 442376 | tf_op jit(solution)/shard_map/ppermute | solution.py:408
  92.2 16.2 %collective-permute-start.17 = (bf16[3,64,384]{2,1,0:T(8,128)(2,1)S(1)}, bf16[3,64,384]{2,1,0:T(8,128)(2,1)S(1)}, u32[]{:S(2)}, u32[]{:S(2)}) collective-permute-start(bf16[3,64,384]{2,1,0:T(8,128)(2,1)S(1)} %get-tuple-element.157), channel_id=1, source_target_pairs={{0,4},{1,5},{2,6},{3,7},{4,0},{5,1},{6,2},{7,3},{8,12},{9,13},{10,... | collective-permute-start | bytes 442376 | tf_op jit(solution)/shard_map/ppermute | solution.py:408
  96.8 21.5 %collective-permute-start.18 = (bf16[3,64,384]{2,1,0:T(8,128)(2,1)S(1)}, bf16[3,64,384]{2,1,0:T(8,128)(2,1)S(1)}, u32[]{:S(2)}, u32[]{:S(2)}) collective-permute-start(bf16[3,64,384]{2,1,0:T(8,128)(2,1)S(1)} %get-tuple-element.158), channel_id=1, source_target_pairs={{0,5},{1,4},{2,7},{3,6},{4,1},{5,0},{6,3},{7,2},{8,13},{9,12},{10,... | collective-permute-start | bytes 442376 | tf_op jit(solution)/shard_map/ppermute | solution.py:408
  108.3 10.0 %collective-permute-start.19 = (bf16[3,64,384]{2,1,0:T(8,128)(2,1)S(1)}, bf16[3,64,384]{2,1,0:T(8,128)(2,1)S(1)}, u32[]{:S(2)}, u32[]{:S(2)}) collective-permute-start(bf16[3,64,384]{2,1,0:T(8,128)(2,1)S(1)} %get-tuple-element.159), channel_id=1, source_target_pairs={{0,6},{1,7},{2,4},{3,5},{4,2},{5,3},{6,0},{7,1},{8,14},{9,15},{10,... | collective-permute-start | bytes 442376 | tf_op jit(solution)/shard_map/ppermute | solution.py:408
  118.4 19.0 %collective-permute-start.21 = (bf16[8,192,256]{2,1,0:T(8,128)(2,1)S(1)}, bf16[8,192,256]{2,1,0:T(8,128)(2,1)S(1)}, u32[]{:S(2)}, u32[]{:S(2)}) collective-permute-start(bf16[8,192,256]{2,1,0:T(8,128)(2,1)S(1)} %get-tuple-element.162.refs_2_), channel_id=1, source_target_pairs={{0,16},{16,0},{1,17},{17,1},{2,18},{18,2},{3,19},{19,3},{4,20},{20... | collective-permute-start | bytes 2359304 | tf_op jit(solution)/shard_map/ppermute | solution.py:404
  123.6 13.8 %collective-permute-start.25 = (bf16[64,384]{1,0:T(8,128)(2,1)S(1)}, bf16[64,384]{1,0:T(8,128)(2,1)S(1)}, u32[]{:S(2)}, u32[]{:S(2)}) collective-permute-start(bf16[64,384]{1,0:T(8,128)(2,1)S(1)} %get-tuple-element.168), channel_id=1, source_target_pairs={{0,4},{1,5},{2,6},{3,7},{4,0},{5,1},{6,2},{7,3},{8,12},{9,13},{10,... | collective-permute-start | bytes 147464 | tf_op jit(solution)/shard_map/ppermute | solution.py:408
  126.5 11.0 %collective-permute-start.26 = (bf16[64,384]{1,0:T(8,128)(2,1)S(1)}, bf16[64,384]{1,0:T(8,128)(2,1)S(1)}, u32[]{:S(2)}, u32[]{:S(2)}) collective-permute-start(bf16[64,384]{1,0:T(8,128)(2,1)S(1)} %get-tuple-element.169), channel_id=1, source_target_pairs={{0,5},{1,4},{2,7},{3,6},{4,1},{5,0},{6,3},{7,2},{8,13},{9,12},{10,... | collective-permute-start | bytes 147464 | tf_op jit(solution)/shard_map/ppermute | solution.py:408
  127.1 10.4 %collective-permute-start.27 = (bf16[64,384]{1,0:T(8,128)(2,1)S(1)}, bf16[64,384]{1,0:T(8,128)(2,1)S(1)}, u32[]{:S(2)}, u32[]{:S(2)}) collective-permute-start(bf16[64,384]{1,0:T(8,128)(2,1)S(1)} %get-tuple-element.170), channel_id=1, source_target_pairs={{0,6},{1,7},{2,4},{3,5},{4,2},{5,3},{6,0},{7,1},{8,14},{9,15},{10,... | collective-permute-start | bytes 147464 | tf_op jit(solution)/shard_map/ppermute | solution.py:408
  137.5 34.3 %collective-permute-start.36 = (bf16[8,192,256]{2,1,0:T(8,128)(2,1)S(1)}, bf16[8,192,256]{2,1,0:T(8,128)(2,1)S(1)}, u32[]{:S(2)}, u32[]{:S(2)}) collective-permute-start(bf16[8,192,256]{2,1,0:T(8,128)(2,1)S(1)} %get-tuple-element.204.refs_20_), channel_id=1, source_target_pairs={{0,8},{8,0},{1,9},{9,1},{2,10},{10,2},{3,11},{11,3},{4,12},{12,4},... | collective-permute-start | bytes 2359304 | tf_op jit(solution)/shard_map/ppermute | solution.py:404
  137.6 34.8 %collective-permute-start.37 = (bf16[8,192,256]{2,1,0:T(8,128)(2,1)S(1)}, bf16[8,192,256]{2,1,0:T(8,128)(2,1)S(1)}, u32[]{:S(2)}, u32[]{:S(2)}) collective-permute-start(bf16[8,192,256]{2,1,0:T(8,128)(2,1)S(1)} %get-tuple-element.205.refs_21_), channel_id=1, source_target_pairs={{0,8},{8,0},{1,9},{9,1},{2,10},{10,2},{3,11},{11,3},{4,12},{12,4},... | collective-permute-start | bytes 2359304 | tf_op jit(solution)/shard_map/ppermute | solution.py:404
  138.1 45.9 %collective-permute-start.41 = (bf16[2,512,256]{2,1,0:T(8,128)(2,1)S(1)}, bf16[2,512,256]{2,1,0:T(8,128)(2,1)S(1)}, u32[]{:S(2)}, u32[]{:S(2)}) collective-permute-start(bf16[2,512,256]{2,1,0:T(8,128)(2,1)S(1)} %get-tuple-element.209.refs_8_), channel_id=1, source_target_pairs={{0,1},{1,0},{2,3},{3,2},{4,5},{5,4},{6,7},{7,6},{8,9},{9,8},{10,11... | collective-permute-start | bytes 1572872 | tf_op jit(solution)/shard_map/ppermute | solution.py:408
  138.7 14.4 %collective-permute-start.29 = (bf16[64,384]{1,0:T(8,128)(2,1)S(1)}, bf16[64,384]{1,0:T(8,128)(2,1)S(1)}, u32[]{:S(2)}, u32[]{:S(2)}) collective-permute-start(bf16[64,384]{1,0:T(8,128)(2,1)S(1)} %get-tuple-element.197), channel_id=1, source_target_pairs={{0,1},{1,0},{2,3},{3,2},{4,5},{5,4},{6,7},{7,6},{8,9},{9,8},{10,11... | collective-permute-start | bytes 147464 | tf_op jit(solution)/shard_map/ppermute | solution.py:408
  140.1 13.7 %collective-permute-start.30 = (bf16[64,384]{1,0:T(8,128)(2,1)S(1)}, bf16[64,384]{1,0:T(8,128)(2,1)S(1)}, u32[]{:S(2)}, u32[]{:S(2)}) collective-permute-start(bf16[64,384]{1,0:T(8,128)(2,1)S(1)} %get-tuple-element.198), channel_id=1, source_target_pairs={{0,2},{1,3},{2,0},{3,1},{4,6},{5,7},{6,4},{7,5},{8,10},{9,11},{10,... | collective-permute-start | bytes 147464 | tf_op jit(solution)/shard_map/ppermute | solution.py:408
  166.8 17.7 %collective-permute-start.39 = (bf16[2,512,256]{2,1,0:T(8,128)(2,1)S(1)}, bf16[2,512,256]{2,1,0:T(8,128)(2,1)S(1)}, u32[]{:S(2)}, u32[]{:S(2)}) collective-permute-start(bf16[2,512,256]{2,1,0:T(8,128)(2,1)S(1)} %get-tuple-element.207.refs_4_), channel_id=1, source_target_pairs={{0,16},{16,0},{1,17},{17,1},{2,18},{18,2},{3,19},{19,3},{4,20},{20... | collective-permute-start | bytes 1572872 | tf_op jit(solution)/shard_map/ppermute | solution.py:404
  171.8 15.9 %collective-permute-start.40 = (bf16[2,512,256]{2,1,0:T(8,128)(2,1)S(1)}, bf16[2,512,256]{2,1,0:T(8,128)(2,1)S(1)}, u32[]{:S(2)}, u32[]{:S(2)}) collective-permute-start(bf16[2,512,256]{2,1,0:T(8,128)(2,1)S(1)} %get-tuple-element.208.refs_6_), channel_id=1, source_target_pairs={{0,16},{16,0},{1,17},{17,1},{2,18},{18,2},{3,19},{19,3},{4,20},{20... | collective-permute-start | bytes 1572872 | tf_op jit(solution)/shard_map/ppermute | solution.py:404
  171.8 15.9 %collective-permute-start.42 = (bf16[2,512,256]{2,1,0:T(8,128)(2,1)S(1)}, bf16[2,512,256]{2,1,0:T(8,128)(2,1)S(1)}, u32[]{:S(2)}, u32[]{:S(2)}) collective-permute-start(bf16[2,512,256]{2,1,0:T(8,128)(2,1)S(1)} %get-tuple-element.210.refs_9_), channel_id=1, source_target_pairs={{0,1},{1,0},{2,3},{3,2},{4,5},{5,4},{6,7},{7,6},{8,9},{9,8},{10,11... | collective-permute-start | bytes 1572872 | tf_op jit(solution)/shard_map/ppermute | solution.py:408
  183.9 18.9 %collective-permute-start.43 = (bf16[4,64,1536]{2,1,0:T(8,128)(2,1)S(1)}, bf16[4,64,1536]{2,1,0:T(8,128)(2,1)S(1)}, u32[]{:S(2)}, u32[]{:S(2)}) collective-permute-start(bf16[4,64,1536]{2,1,0:T(8,128)(2,1)S(1)} %get-tuple-element.211.own_ref), channel_id=1, source_target_pairs={{0,8},{8,0},{1,9},{9,1},{2,10},{10,2},{3,11},{11,3},{4,12},{12,4},... | collective-permute-start | bytes 2359304 | tf_op jit(solution)/shard_map/ppermute | solution.py:404
  198.2 11.4 %all-to-all-start = ((f32[16,8,128]{2,1,0:T(8,128)}), f32[16,8,128]{2,1,0:T(8,128)S(1)}, u32[]{:S(2)}, u32[]{:S(2)}) async-start(f32[16,8,128]{2,1,0:T(8,128)} %reward.3), calls=%async_computation | async-start | bytes 131072 | tf_op jit(solution)/shard_map/all_to_all | solution.py:529
  (24 other events, 363.6 us)

commit v6 on v5

--- a/solution.py
+++ b/solution.py
@@ -17,52 +17,45 @@
 MIB = 1024 * 1024
 
 
-def pack_kernel(chunks, width, ids_ref, q_ref, k_ref, v_ref, *refs):
-    out_refs, packed_ref = refs[:-1], refs[-1]
-    particles, tokens, model_width = q_ref.shape
+def pack_kernel(chunks, width, q_ref, k_ref, v_ref, *out_refs):
+    particles, _, model_width = q_ref.shape
     blocks = model_width // width
     part = width // chunks
-    count = particles * blocks
     for index, ref in enumerate((q_ref, k_ref, v_ref)):
         for particle in range(particles):
             for block in range(blocks):
                 for chunk in range(chunks):
                     start = block * width + chunk * part
-                    packed_ref[chunk, particle * blocks + block, index] = ref[
+                    out_refs[chunk][particle * blocks + block, index] = ref[
                         particle, :, start : start + part
                     ]
-    for chunk in range(chunks):
-        for place in range(count):
-            out_refs[chunk * count + place][...] = packed_ref[chunk, ids_ref[2] ^ place]
-
-
-def pack(ids, queries, keys, values, chunks, width):
+
+
+def pack(queries, keys, values, chunks, width):
     particles, tokens, model_width = queries.shape
     count = particles * model_width // width
-    part = width // chunks
     vmem = pl.BlockSpec(memory_space=pltpu.VMEM)
-    shape = jax.ShapeDtypeStruct((3, tokens, part), queries.dtype)
-    packed = pl.pallas_call(
-        functools.partial(pack_kernel, chunks, width),
-        in_specs=[pl.BlockSpec(memory_space=pltpu.SMEM)] + [vmem] * 3,
-        out_specs=[vmem] * (chunks * count),
-        out_shape=[shape] * (chunks * count),
-        scratch_shapes=[pltpu.VMEM((chunks, count, 3, tokens, part), queries.dtype)],
-        compiler_params=pltpu.CompilerParams(vmem_limit_bytes=16 * MIB),
-        name="pack_heads",
-    )(ids, queries, keys, values)
-    return [list(packed[chunk * count : (chunk + 1) * count]) for chunk in range(chunks)]
+    shape = jax.ShapeDtypeStruct((count, 3, tokens, width // chunks), queries.dtype)
+    return list(
+        pl.pallas_call(
+            functools.partial(pack_kernel, chunks, width),
+            in_specs=[vmem] * 3,
+            out_specs=[vmem] * chunks,
+            out_shape=[shape] * chunks,
+            compiler_params=pltpu.CompilerParams(vmem_limit_bytes=16 * MIB),
+            name="pack_heads",
+        )(queries, keys, values)
+    )
 
 
 def gate_kernel(*refs):
     pass
 
 
-def gate(*groups):
-    arrays = [array for group in groups for array in group]
+def gate(*arrays):
     anywhere = pl.BlockSpec(memory_space=pl.ANY)
     count = len(arrays)
-    gated = list(
+    return list(
         pl.pallas_call(
             gate_kernel,
             in_specs=[anywhere] * count,
@@ -73,19 +66,18 @@
             name="gate",
         )(*arrays)
     )
-    return [[gated.pop(0) for _ in group] for group in groups]
-
-
-def attention_kernel(head_width, block_sources, *refs):
-    sources = len(refs) // 2
-    qkv_refs, out_refs = refs[:sources], refs[sources:]
-    _, tokens, columns = qkv_refs[0].shape
+
+
+def attention_kernel(head_width, block_sources, qkv_ref, out_ref):
+    sources, _, tokens, columns = qkv_ref.shape
+    total = sources * tokens
+    rows = block_sources * tokens
     factor = 1.0 / math.sqrt(head_width) / math.log(2.0)
-    k_all = jnp.concatenate([ref[1] for ref in qkv_refs], axis=0)
-    v_all = jnp.concatenate([ref[2] for ref in qkv_refs], axis=0)
+    k_all = qkv_ref[:, 1].reshape(total, columns)
+    v_all = qkv_ref[:, 2].reshape(total, columns)
     for block in range(0, sources, block_sources):
         span = slice(block, block + block_sources)
-        q_all = jnp.concatenate([ref[0] for ref in qkv_refs[span]], axis=0)
+        q_all = qkv_ref[span, 0].reshape(rows, columns)
         pieces = []
         for head in range(columns // head_width):
             cols = slice(head * head_width, (head + 1) * head_width)
@@ -99,63 +91,126 @@
             expanded = jnp.exp2((scores - highest) * factor)
             norm = 1.0 / jnp.sum(expanded, axis=1, keepdims=True)
             weights = (expanded * norm).astype(jnp.bfloat16)
-            pieces.append(
-                jnp.dot(weights, v_all[:, cols], preferred_element_type=jnp.float32)
-            )
+            pieces.append(jnp.dot(weights, v_all[:, cols], preferred_element_type=jnp.float32))
         joined = jnp.concatenate(pieces, axis=1).astype(jnp.bfloat16)
-        for index, ref in enumerate(out_refs[span]):
-            ref[...] = joined[index * tokens : (index + 1) * tokens]
-
-
-def attention(arrived, head_width):
-    sources = len(arrived)
-    _, tokens, columns = arrived[0].shape
+        out_ref[span] = joined.reshape(block_sources, tokens, columns)
+
+
+def attention(qkv, head_width):
+    sources, _, tokens, columns = qkv.shape
     total = sources * tokens
     block_sources = max(1, min(sources, 512 // tokens))
     while sources % block_sources:
         block_sources -= 1
-    heads = columns // head_width
     step = LANES if columns % LANES == 0 and LANES % head_width == 0 else columns
     scores_bytes = 4 * block_sources * tokens * total
-    return list(
-        pl.pallas_call(
-            functools.partial(attention_kernel, head_width, block_sources),
-            grid=(columns // step,),
-            in_specs=[pl.BlockSpec((3, tokens, step), lambda i: (0, 0, i))] * sources,
-            out_specs=[pl.BlockSpec((tokens, step), lambda i: (0, i))] * sources,
-            out_shape=[jax.ShapeDtypeStruct((tokens, columns), jnp.bfloat16)] * sources,
-            compiler_params=pltpu.CompilerParams(
-                vmem_limit_bytes=8 * MIB + 6 * scores_bytes
-            ),
-            cost_estimate=pl.CostEstimate(
-                flops=4 * total * total * columns,
-                bytes_accessed=8 * total * columns,
-                transcendentals=heads * total * total,
-            ),
-            name="attention",
-        )(*arrived)
-    )
-
-
-def project_kernel(chunks, parts, block, offsets, depth_parts, refs_in, refs_out):
+    return pl.pallas_call(
+        functools.partial(attention_kernel, head_width, block_sources),
+        grid=(columns // step,),
+        in_specs=[pl.BlockSpec((sources, 3, tokens, step), lambda i: (0, 0, 0, i))],
+        out_specs=pl.BlockSpec((sources, tokens, step), lambda i: (0, 0, i)),
+        out_shape=jax.ShapeDtypeStruct((sources, tokens, columns), jnp.bfloat16),
+        compiler_params=pltpu.CompilerParams(vmem_limit_bytes=8 * MIB + 6 * scores_bytes),
+        cost_estimate=pl.CostEstimate(
+            flops=4 * total * total * columns,
+            bytes_accessed=8 * total * columns,
+            transcendentals=columns // head_width * total * total,
+        ),
+        name="attention",
+    )(qkv)
+
+
+class ProjectionWeights:
+    def __init__(self, weight_ref, vmem_ref, sems, chunks, wanted, width):
+        depth, model_width = weight_ref.shape
+        part = width // chunks
+        blocks = depth // width
+        self.block = 512 if model_width % 512 == 0 else model_width
+        self.copies = []
+        for group in range(model_width // self.block):
+            cols = slice(group * self.block, (group + 1) * self.block)
+            for index in range(blocks * len(wanted)):
+                start = index // len(wanted) * width + wanted[index % len(wanted)] * part
+                self.copies.append(
+                    pltpu.make_async_copy(
+                        weight_ref.at[start : start + part, cols],
+                        vmem_ref.at[index * part : (index + 1) * part, cols],
+                        sems.at[group, index],
+                    )
+                )
+        self.per_group = blocks * len(wanted)
+        for copy in self.copies:
+            copy.start()
+
+    def wait(self, group):
+        for copy in self.copies[group * self.per_group : (group + 1) * self.per_group]:
+            copy.wait()
+        return slice(group * self.block, (group + 1) * self.block)
+
+
+def gather_rows(piece_refs, rows_ref, particles):
+    count, tokens, part = piece_refs[0].shape
+    blocks = count // particles
+    for index in range(blocks * len(piece_refs)):
+        ref = piece_refs[index % len(piece_refs)]
+        place = index // len(piece_refs)
+        for particle in range(particles):
+            rows_ref[
+                particle * tokens : (particle + 1) * tokens, index * part : (index + 1) * part
+            ] = ref[particle * blocks + place]
+
+
+def first_project_kernel(chunks, width, latents_ref, weight_ref, piece_ref, out_ref, *scratch):
+    weight_vmem, rows_ref, sems = scratch
+    particles, tokens, model_width = latents_ref.shape
+    weights = ProjectionWeights(weight_ref, weight_vmem, sems, chunks, [0], width)
+    gather_rows([piece_ref], rows_ref, particles)
+    for group in range(model_width // weights.block):
+        cols = weights.wait(group)
+        flat = latents_ref[:, :, cols].reshape(particles * tokens, weights.block)
+        out_ref[:, cols] = flat.astype(jnp.float32) + jnp.dot(
+            rows_ref[...], weight_vmem[:, cols], preferred_element_type=jnp.float32
+        )
+
+
+def first_project(latents, out_weight, piece, chunks, width):
+    particles, tokens, model_width = latents.shape
+    rows, depth = particles * tokens, model_width // chunks
+    vmem = pl.BlockSpec(memory_space=pltpu.VMEM)
+    return pl.pallas_call(
+        functools.partial(first_project_kernel, chunks, width),
+        in_specs=[vmem, pl.BlockSpec(memory_space=pl.ANY), vmem],
+        out_specs=vmem,
+        out_shape=jax.ShapeDtypeStruct((rows, model_width), jnp.float32),
+        scratch_shapes=[
+            pltpu.VMEM((depth, model_width), jnp.bfloat16),
+            pltpu.VMEM((rows, depth), jnp.bfloat16),
+            pltpu.SemaphoreType.DMA((max(1, model_width // 512), model_width // width)),
+        ],
+        compiler_params=pltpu.CompilerParams(vmem_limit_bytes=16 * MIB),
+        cost_estimate=pl.CostEstimate(
+            flops=2 * rows * depth * model_width,
+            bytes_accessed=2 * depth * model_width + 8 * rows * model_width,
+            transcendentals=0,
+        ),
+        name="first_project",
+    )(latents, out_weight, piece)
+
+
+def project_kernel(chunks, width, parts, offsets, depth_parts, refs_in, refs_out):
     ids_ref, latents_ref, gain_ref, out_weight_ref = refs_in[:4]
-    attended_refs, weight_refs = refs_in[4:-parts], refs_in[-parts:]
+    rest, weight_refs = list(refs_in[4:-parts]), refs_in[-parts:]
+    begun_ref = rest.pop(0) if chunks > 1 else latents_ref
+    stepped_ref, features_ref = refs_out[:2]
+    out_vmem, weight_vmem, rows_ref, clean_ref, embedded_ref, out_sems, sems = refs_out[2:]
     dom, group, seq = ids_ref[0], ids_ref[1], ids_ref[2]
     sigma = ids_ref[3].astype(jnp.float32) * (1.0 / STEPS)
-    stepped_ref, features_ref = refs_out[:2]
-    out_vmem, weight_vmem, attended_ref, clean_ref, embedded_ref, out_sems, sems = refs_out[2:]
     particles, tokens, model_width = latents_ref.shape
     rows = particles * tokens
     shards, depth, columns = weight_refs[0].shape
 
-    out_copies = []
-    for index in range(model_width // block):
-        cols = slice(index * block, (index + 1) * block)
-        copy = pltpu.make_async_copy(
-            out_weight_ref.at[:, cols], out_vmem.at[:, cols], out_sems.at[index]
-        )
-        copy.start()
-        out_copies.append(copy)
+    wanted = list(range(chunks - len(rest), chunks))
+    out_weights = ProjectionWeights(out_weight_ref, out_vmem, out_sems, chunks, wanted, width)
     copies = []
     for index in range(parts):
         for shard in range(shards):
@@ -168,31 +223,19 @@
             copy.start()
             copies.append(copy)
 
-    blocks, _, width = attended_ref.shape
-    part = width // chunks
-    count = particles * blocks
-    for chunk in range(chunks):
-        for index in range(count):
-            place = seq ^ index
-            rows_of = pl.ds(pl.multiple_of(place // blocks * tokens, tokens), tokens)
-            attended_ref[place % blocks, rows_of, chunk * part : (chunk + 1) * part] = (
-                attended_refs[chunk * count + index][...]
-            )
-    for index in range(model_width // block):
-        cols = slice(index * block, (index + 1) * block)
-        out_copies[index].wait()
-        flat = latents_ref[:, :, cols].reshape(rows, block).astype(jnp.float32)
-        velocity = flat + sum(
-            jnp.dot(
-                attended_ref[place],
-                out_vmem[place * width : (place + 1) * width, cols],
-                preferred_element_type=jnp.float32,
-            )
-            for place in range(blocks)
+    gather_rows(rest, rows_ref, particles)
+    for index in range(model_width // out_weights.block):
+        cols = out_weights.wait(index)
+        flat = latents_ref[:, :, cols].reshape(rows, out_weights.block).astype(jnp.float32)
+        begun = begun_ref[:, cols] if chunks > 1 else flat
+        velocity = begun + jnp.dot(
+            rows_ref[...], out_vmem[:, cols], preferred_element_type=jnp.float32
         )
         clean_ref[:, cols] = (flat - sigma * velocity).astype(jnp.bfloat16)
         stepped_ref[:, :, cols] = (
-            (flat - velocity * (1.0 / STEPS)).astype(jnp.bfloat16).reshape(particles, tokens, block)
+            (flat - velocity * (1.0 / STEPS))
+            .astype(jnp.bfloat16)
+            .reshape(particles, tokens, out_weights.block)
         )
 
     for index in range(parts):
@@ -220,23 +263,23 @@
         features_ref[index * columns // share, :, start : start + columns] = feature
 
 
-def project_embed(ids, offsets, latents, attended, width, out_weight, weights, gain, depth_parts):
+def project_embed(
+    ids, offsets, latents, begun, attended, chunks, width, out_weight, weights, gain, depth_parts
+):
     particles, tokens, model_width = latents.shape
     rows = particles * tokens
-    chunks, parts = len(attended), len(weights)
+    parts = len(weights)
     columns = weights[0].shape[2]
     count = parts * columns
-    block = 256 if model_width % 256 == 0 else model_width
-    pieces = [piece for chunk in attended for piece in chunk]
+    out_depth = model_width * len(attended) // chunks
+    pieces = ([] if begun is None else [begun]) + attended
     vmem = pl.BlockSpec(memory_space=pltpu.VMEM)
     smem = pl.BlockSpec(memory_space=pltpu.SMEM)
     anywhere = pl.BlockSpec(memory_space=pl.ANY)
     inputs = 4 + len(pieces) + parts
 
     def kernel(*refs):
-        project_kernel(
-            chunks, parts, block, offsets, depth_parts, refs[:inputs], refs[inputs:]
-        )
+        project_kernel(chunks, width, parts, offsets, depth_parts, refs[:inputs], refs[inputs:])
 
     return pl.pallas_call(
         kernel,
@@ -247,18 +290,20 @@
             jax.ShapeDtypeStruct((depth_parts, rows, count // depth_parts), jnp.bfloat16),
         ],
         scratch_shapes=[
-            pltpu.VMEM((model_width, model_width), jnp.bfloat16),
+            pltpu.VMEM((out_depth, model_width), jnp.bfloat16),
             pltpu.VMEM((parts, model_width, columns), jnp.bfloat16),
-            pltpu.VMEM((model_width // width, rows, width), jnp.bfloat16),
+            pltpu.VMEM((rows, out_depth), jnp.bfloat16),
             pltpu.VMEM((rows, model_width), jnp.bfloat16),
             pltpu.VMEM((parts, rows, columns), jnp.float32),
-            pltpu.SemaphoreType.DMA((model_width // block,)),
+            pltpu.SemaphoreType.DMA(
+                (max(1, model_width // 512), model_width // width * len(attended))
+            ),
             pltpu.SemaphoreType.DMA((parts,)),
         ],
         compiler_params=pltpu.CompilerParams(vmem_limit_bytes=28 * MIB),
         cost_estimate=pl.CostEstimate(
-            flops=2 * rows * model_width * (model_width + count),
-            bytes_accessed=2 * model_width * (model_width + count) + 8 * rows * model_width,
+            flops=2 * rows * model_width * (out_depth + count),
+            bytes_accessed=2 * model_width * (out_depth + count) + 12 * rows * model_width,
             transcendentals=rows * count,
         ),
         name="project_embed",
@@ -338,8 +383,22 @@
     )(ids, features, head, before, *weights)
 
 
-def finish_kernel(particles, doms, ids_ref, parts_ref, resampled_ref, out_ref, same_ref):
-    logits = jnp.sum(parts_ref[...], axis=0)
+def add_kernel(parts_ref, out_ref):
+    out_ref[...] = jnp.sum(parts_ref[...], axis=0)
+
+
+def add_parts(parts):
+    return pl.pallas_call(
+        add_kernel,
+        out_shape=jax.ShapeDtypeStruct(parts.shape[1:], parts.dtype),
+        compiler_params=pltpu.CompilerParams(vmem_limit_bytes=2 * MIB),
+        name="add_partials",
+    )(parts)
+
+
+def finish_kernel(particles, doms, ids_ref, resampled_ref, *refs):
+    logit_refs, (out_ref, same_ref) = refs[:-2], refs[-2:]
+    logits = sum(ref[...] for ref in logit_refs)
     rows = lax.broadcasted_iota(jnp.int32, logits.shape, 0)
     lanes = lax.broadcasted_iota(jnp.int32, logits.shape, 1)
     valid = jnp.logical_and(rows < doms, lanes < particles)
@@ -350,21 +409,21 @@
     out_ref[...] = (own - log_total)[:, :particles]
 
 
-def finish(ids, parts, resampled, particles, doms):
+def finish(ids, logits, resampled, particles):
     vmem = pl.BlockSpec(memory_space=pltpu.VMEM)
     anywhere = pl.BlockSpec(memory_space=pl.ANY)
     log_weights, resampled = pl.pallas_call(
-        functools.partial(finish_kernel, particles, doms),
-        in_specs=[pl.BlockSpec(memory_space=pltpu.SMEM), vmem, anywhere],
+        functools.partial(finish_kernel, particles, len(logits)),
+        in_specs=[pl.BlockSpec(memory_space=pltpu.SMEM), anywhere] + [vmem] * len(logits),
         out_specs=[vmem, anywhere],
         out_shape=[
             jax.ShapeDtypeStruct((1, particles), jnp.float32),
             jax.ShapeDtypeStruct(resampled.shape, resampled.dtype),
         ],
-        input_output_aliases={2: 1},
+        input_output_aliases={1: 1},
         compiler_params=pltpu.CompilerParams(vmem_limit_bytes=2 * MIB),
         name="log_weights",
-    )(ids, parts, resampled)
+    )(ids, resampled, *logits)
     return resampled, log_weights.reshape(particles)
 
 
@@ -408,10 +467,8 @@
     return lax.ppermute(array, axis, [(i, i ^ bit) for i in range(lax.axis_size(axis))])
 
 
-def exchange(pieces):
-    return pieces[:1] + [
-        swapped(piece, "seq", k + 1) for k, piece in enumerate(pieces[1:])
-    ]
+def exchange(array):
+    return lax.all_to_all(array, "seq", 0, 0, tiled=True)
 
 
 def on_device(
@@ -452,21 +509,22 @@
         up_weight, (group * up_depth, dom * up_columns), (up_depth, up_columns)
     )[None]
     bits = [1 << place for place in reversed(range(1, seq_count.bit_length() - 1))]
+
+    packed = pack(queries, keys, values, chunks, width)
     near = [0]
     for bit in bits[:-1]:
         embed_share = jnp.concatenate([embed_share, swapped(embed_share, "seq", bit)])
-        up_share = jnp.concatenate([up_share, swapped(up_share, "seq", bit)])
         near = near + [offset ^ bit for offset in near]
     far = [offset ^ bits[-1] for offset in near]
-
-    packed = pack(ids, queries, keys, values, chunks, width)
-    (embed_share, up_near), packed[0] = gate([embed_share, up_share], packed[0])
+    embed_share, packed[0] = gate(embed_share, packed[0])
 
     arrived = [exchange(packed[0])]
     embed_share = jnp.concatenate([embed_share, swapped(embed_share, "seq", bits[-1])])
-    up_far = swapped(up_near, "seq", bits[-1])
-    (embed_share, up_near, up_far), arrived[0], *packed[1:] = gate(
-        [embed_share, up_near, up_far], arrived[0], *packed[1:]
+    for bit in bits[:-1]:
+        up_share = jnp.concatenate([up_share, swapped(up_share, "seq", bit)])
+    up_near, up_far = up_share, swapped(up_share, "seq", bits[-1])
+    embed_share, up_near, up_far, arrived[0], *packed[1:] = gate(
+        embed_share, up_near, up_far, arrived[0], *packed[1:]
     )
 
     arrived += [exchange(piece) for piece in packed[1:]]
@@ -474,19 +532,22 @@
     near_pair = swapped(up_near, "seq", 1)
     far_groups = [up_far] + [shifted(up_far, "groups", k) for k in range(1, group_count)]
     attended = [attention(arrived[0], head_width)]
-    (embed_share, near_pair), far_groups, attended[0], *arrived[1:] = gate(
-        [embed_share, near_pair], far_groups, attended[0], *arrived[1:]
-    )
+    embed_share, near_pair, attended[0], *rest = gate(
+        embed_share, near_pair, attended[0], *far_groups[1:], *arrived[1:]
+    )
+    far_groups[1:], arrived[1:] = rest[: group_count - 1], rest[group_count - 1 :]
 
     returned = [exchange(attended[0])]
     embed_near = [embed_share] + [shifted(embed_share, "groups", k) for k in range(1, group_count)]
     far_pairs = [swapped(far_groups[0], "seq", 1)]
     attended += [attention(piece, head_width) for piece in arrived[1:]]
-    (up_near, near_pair), embed_near, far_groups[1:], returned[0], *attended[1:] = gate(
-        [up_near, near_pair], embed_near, far_groups[1:], returned[0], *attended[1:]
-    )
-
-    returned += [exchange(pieces) for pieces in attended[1:]]
+    up_near, near_pair, returned[0], *rest = gate(
+        up_near, near_pair, returned[0], *embed_near, *far_groups[1:], *attended[1:]
+    )
+    embed_near, rest = rest[:group_count], rest[group_count:]
+    far_groups[1:], attended[1:] = rest[: group_count - 1], rest[group_count - 1 :]
+
+    returned += [exchange(piece) for piece in attended[1:]]
     embed_parts = embed_near + [
         shifted(piece, "dom", k) for k in range(1, dom_count) for piece in embed_near
     ]
@@ -497,11 +558,14 @@
     embed_offsets = near + far + [offset ^ 1 for offset in near + far]
     up_offsets = near + [offset ^ 1 for offset in near] + far + [offset ^ 1 for offset in far]
 
+    begun = first_project(latents, out_weight, returned.pop(0), chunks, width) if chunks > 1 else None
     stepped, features = project_embed(
         ids,
         embed_offsets,
         latents,
+        begun,
         returned,
+        chunks,
         width,
         out_weight,
         embed_parts,
@@ -525,10 +589,11 @@
         scale=scale,
     )
     partial_own = score(features, before=prev_logw, copies=1)[0]
-    partial_both = score(features_other, before=partial_own, copies=dom_count * seq_count)
-    logits = lax.all_to_all(partial_both, ("dom", "seq"), 0, 0, tiled=True)
+    partial_both = score(features_other, before=partial_own, copies=seq_count)
+    logits = add_parts(exchange(partial_both))
+    both_logits = [logits] + [shifted(logits, "dom", k) for k in range(1, dom_count)]
     resampled = resample(ids, ancestors.astype(jnp.int32), stepped, stepped_other)
-    return finish(ids, logits, resampled, particles, dom_count)
+    return finish(ids, both_logits, resampled, particles)
 
 
 def solution(mesh):

time: 211 us -> 197 us (0.934)
  starting transfers between devices: 67.7 us -> 40.4 us
  local copies, waits for them, and re-layouts: 5.57 us -> 20.5 us
  waiting for transfers between devices: 98.1 us -> 85.3 us
  blocking collectives: 0 us -> 11 us
    ppermute x36 -> x8, starting transfers between devices: 58.3 us -> 13.2 us  [swapped(): lax.ppermute(array, axis, [(i, i ^ bit) for i in range(lax.axis_size(axis...]
    all_to_all x1 -> x4, starting transfers between devices: 4.59 us -> 21.1 us  [exchange(): return lax.all_to_all(array, 'seq', 0, 0, tiled=True)]
    unnamed x22 -> x48, local copies, waits for them, and re-layouts: 4.65 us -> 19.5 us
    ppermute x36 -> x8, waiting for transfers between devices: 90.2 us -> 77.6 us  [swapped(): lax.ppermute(array, axis, [(i, i ^ bit) for i in range(lax.axis_size(axis...]
    all_to_all x0 -> x1, blocking collectives: none -> 11 us  [exchange(): return lax.all_to_all(array, 'seq', 0, 0, tiled=True)]
    pallas_call x1, Pallas kernels: 11.5 us -> 6.69 us  [project_embed(): pl.pallas_call(kernel, in_specs=[smem, vmem, vmem, anywhere] + [vmem] * l...]
    pallas_call x2 -> x4, Pallas kernels: 2.23 us -> 5.3 us  [the longest x1 2.37 us: first_project(): pl.pallas_call(functools.partial(first_project_kernel, chunks, width), in...]
    ppermute x8 -> x9, starting transfers between devices: 4.83 us -> 6.1 us  [shifted(): lax.ppermute(array, axis, [(i, (i + step) % count) for i in range(count)])]
  transfers between devices with their start and end apart: 45 -> 21, of which waited for: 14 -> 9; matrix products, arithmetic and copies ran while one was open for 1% -> 0% of each run, Pallas kernels for 17% -> 18%
where the time goes in v6:
time: 197 us; the launch traced here: 196 us
  waiting for transfers between devices  85.3 us (43%)
  starting transfers between devices  40.4 us (21%)
  Pallas kernels  36.6 us (19%)
  local copies, waits for them, and re-layouts  20.5 us (10%)
  blocking collectives  11 us (6%)
    ppermute x8, waiting for transfers between devices, swapped(): lax.ppermute(array, axis, [(i, i ^ bit) for i in range(lax.axis_size(axis...  77.6 us
    all_to_all x4, starting transfers between devices, exchange(): return lax.all_to_all(array, 'seq', 0, 0, tiled=True)  21.1 us
    unnamed x48, local copies, waits for them, and re-layouts  19.5 us
    ppermute x8, starting transfers between devices, swapped(): lax.ppermute(array, axis, [(i, i ^ bit) for i in range(lax.axis_size(axis...  13.2 us
    pallas_call x2, Pallas kernels, attention(): pl.pallas_call(functools.partial(attention_kernel, head_width, block_sour...  11.7 us
    all_to_all x1, blocking collectives, exchange(): return lax.all_to_all(array, 'seq', 0, 0, tiled=True)  11 us
    pallas_call x2, Pallas kernels, reward(): pl.pallas_call(functools.partial(reward_kernel, particles, scale, parts,...  10.9 us
    pallas_call x1, Pallas kernels, project_embed(): pl.pallas_call(kernel, in_specs=[smem, vmem, vmem, anywhere] + [vmem] * l...  6.69 us
  transfers between devices with their start and end apart: 21, of which 9 were waited for; matrix products, arithmetic and copies ran while one was open for 0% of the time, Pallas kernels for 18%

profile of v6, /device:TPU:0, one launch (start us, length us, event | category | flops | bytes accessed | tf_op | source)
XLA Modules:
  0.0 195.7 jit_solution(18130379471292496130)
XLA Ops:
  1.6 4.0 %collective-permute-start = (bf16[1,192,256]{2,1,0:T(8,128)(2,1)S(1)}, bf16[1,192,256]{2,1,0:T(8,128)(2,1)S(1)}, u32[]{:S(2)}, u32[]{:S(2)}) collective-permute-start(bf16[1,192,256]{2,1,0:T(8,128)(2,1)S(1)} %dynamic-slice_bitcast_fusion.1), channel_id=1, source_target_pairs={{0,4},{1,5},{2,6},{3,7},{4,0},{5,1},{6,2},{7,3},{8,12},{9,13},{10,... | collective-permute-start | bytes 294920 | tf_op jit(solution)/shard_map/ppermute | solution.py:467
  9.1 1.6 pack_heads.1
  10.8 5.6 %all-to-all-start = ((bf16[8,3,64,384]{3,2,1,0:T(8,128)(2,1)}), bf16[8,3,64,384]{3,2,1,0:T(8,128)(2,1)S(1)}, u32[]{:S(2)}, u32[]{:S(2)}) async-start(bf16[8,3,64,384]{3,2,1,0:T(8,128)(2,1)} %get-tuple-element.29), calls=%async_computation | async-start | bytes 2359296 | tf_op jit(solution)/shard_map/all_to_all | solution.py:471
  16.4 3.0 %collective-permute-start.2 = (bf16[1,512,256]{2,1,0:T(8,128)(2,1)S(1)}, bf16[1,512,256]{2,1,0:T(8,128)(2,1)S(1)}, u32[]{:S(2)}, u32[]{:S(2)}) collective-permute-start(bf16[1,512,256]{2,1,0:T(8,128)(2,1)S(1)} %dynamic-slice_bitcast_fusion), channel_id=1, source_target_pairs={{0,4},{1,5},{2,6},{3,7},{4,0},{5,1},{6,2},{7,3},{8,12},{9,13},{10,... | collective-permute-start | bytes 786440 | tf_op jit(solution)/shard_map/ppermute | solution.py:467
  19.4 37.0 %collective-permute-done.2 = bf16[1,512,256]{2,1,0:T(8,128)(2,1)S(1)} collective-permute-done((bf16[1,512,256]{2,1,0:T(8,128)(2,1)S(1)}, bf16[1,512,256]{2,1,0:T(8,128)(2,1)S(1)}, u32[]{:S(2)}, u32[]{:S(2)}) %collective-permute-start.2) | collective-permute-done | bytes 262176 | tf_op jit(solution)/shard_map/ppermute | solution.py:467
  56.5 2.0 %collective-permute-start.1 = (bf16[2,192,256]{2,1,0:T(8,128)(2,1)S(1)}, bf16[2,192,256]{2,1,0:T(8,128)(2,1)S(1)}, u32[]{:S(2)}, u32[]{:S(2)}) collective-permute-start(bf16[2,192,256]{2,1,0:T(8,128)(2,1)S(1)} %get-tuple-element.28), channel_id=1, source_target_pairs={{0,2},{1,3},{2,0},{3,1},{4,6},{5,7},{6,4},{7,5},{8,10},{9,11},{10,... | collective-permute-start | bytes 589832 | tf_op jit(solution)/shard_map/ppermute | solution.py:467
  58.5 14.9 %collective-permute-done.1 = bf16[2,192,256]{2,1,0:T(8,128)(2,1)S(1)} collective-permute-done((bf16[2,192,256]{2,1,0:T(8,128)(2,1)S(1)}, bf16[2,192,256]{2,1,0:T(8,128)(2,1)S(1)}, u32[]{:S(2)}, u32[]{:S(2)}) %collective-permute-start.1) | collective-permute-done | bytes 196640 | tf_op jit(solution)/shard_map/ppermute | solution.py:467
  74.6 4.8 %all-to-all-start.1 = ((bf16[8,3,64,384]{3,2,1,0:T(8,128)(2,1)}), bf16[8,3,64,384]{3,2,1,0:T(8,128)(2,1)}, u32[]{:S(2)}, u32[]{:S(2)}) async-start(bf16[8,3,64,384]{3,2,1,0:T(8,128)(2,1)} %get-tuple-element.35), calls=%async_computation.1 | async-start | bytes 2359296 | tf_op jit(solution)/shard_map/all_to_all | solution.py:471
  79.3 2.0 %collective-permute-start.4 = (bf16[4,192,256]{2,1,0:T(8,128)(2,1)S(1)}, bf16[4,192,256]{2,1,0:T(8,128)(2,1)S(1)}, u32[]{:S(2)}, u32[]{:S(2)}) collective-permute-start(bf16[4,192,256]{2,1,0:T(8,128)(2,1)S(1)} %get-tuple-element.32), channel_id=1, source_target_pairs={{0,1},{1,0},{2,3},{3,2},{4,5},{5,4},{6,7},{7,6},{8,9},{9,8},{10,11... | collective-permute-start | bytes 1179656 | tf_op jit(solution)/shard_map/ppermute | solution.py:467
  81.4 1.5 collective-permute-start.6
  82.9 1.3 copy-done.6
  84.2 5.5 %attention.2.refs_2_ = bf16[8,64,384]{2,1,0:T(8,128)(2,1)S(1)} custom-call(bf16[8,3,64,384]{3,2,1,0:T(8,128)(2,1)S(1)} %copy-done.6), custom_call_target="tpu_custom_call" | custom-call | flops 402653184 | bytes 1572864 | tf_op jit(solution)/shard_map/attention/pallas_call | solution.py:107
  89.7 14.4 %collective-permute-done.4 = bf16[4,192,256]{2,1,0:T(8,128)(2,1)S(1)} collective-permute-done((bf16[4,192,256]{2,1,0:T(8,128)(2,1)S(1)}, bf16[4,192,256]{2,1,0:T(8,128)(2,1)S(1)}, u32[]{:S(2)}, u32[]{:S(2)}) %collective-permute-start.4) | collective-permute-done | bytes 393248 | tf_op jit(solution)/shard_map/ppermute | solution.py:467
  104.1 9.2 %collective-permute-done.5.refs_1_ = bf16[2,512,256]{2,1,0:T(8,128)(2,1)S(1)} collective-permute-done((bf16[2,512,256]{2,1,0:T(8,128)(2,1)S(1)}, bf16[2,512,256]{2,1,0:T(8,128)(2,1)S(1)}, u32[]{:S(2)}, u32[]{:S(2)}) %collective-permute-start.5) | collective-permute-done | bytes 524320 | tf_op jit(solution)/shard_map/ppermute | solution.py:467
  115.1 1.5 collective-permute-start.7
  116.6 4.5 %all-to-all-start.2 = ((bf16[8,64,384]{2,1,0:T(8,128)(2,1)}), bf16[8,64,384]{2,1,0:T(8,128)(2,1)}, u32[]{:S(2)}, u32[]{:S(2)}) async-start(bf16[8,64,384]{2,1,0:T(8,128)(2,1)} %copy-done.13), calls=%async_computation.2 | async-start | bytes 786432 | tf_op jit(solution)/shard_map/all_to_all | solution.py:471
  121.1 6.3 %attention.3.refs_6_ = bf16[8,64,384]{2,1,0:T(8,128)(2,1)S(1)} custom-call(bf16[8,3,64,384]{3,2,1,0:T(8,128)(2,1)} %get-tuple-element.40.qkv_ref), custom_call_target="tpu_custom_call" | custom-call | flops 402653184 | bytes 1572864 | tf_op jit(solution)/shard_map/attention/pallas_call | solution.py:107
  128.1 4.4 %all-to-all-done.2.refs_2_ = bf16[8,64,384]{2,1,0:T(8,128)(2,1)} async-done(((bf16[8,64,384]{2,1,0:T(8,128)(2,1)}), bf16[8,64,384]{2,1,0:T(8,128)(2,1)}, u32[]{:S(2)}, u32[]{:S(2)}) %all-to-all-start.2) | async-done | bytes 393248 | tf_op jit(solution)/shard_map/all_to_all | solution.py:471
  135.0 6.1 %all-to-all-start.3 = ((bf16[8,64,384]{2,1,0:T(8,128)(2,1)}), bf16[8,64,384]{2,1,0:T(8,128)(2,1)}, u32[]{:S(2)}, u32[]{:S(2)}) async-start(bf16[8,64,384]{2,1,0:T(8,128)(2,1)} %copy-done.16), calls=%async_computation.3 | async-start | bytes 786432 | tf_op jit(solution)/shard_map/all_to_all | solution.py:471
  141.1 2.0 %collective-permute-start.14 = (bf16[2,512,256]{2,1,0:T(8,128)(2,1)}, bf16[2,512,256]{2,1,0:T(8,128)(2,1)}, u32[]{:S(2)}, u32[]{:S(2)}) collective-permute-start(bf16[2,512,256]{2,1,0:T(8,128)(2,1)} %get-tuple-element.34.refs_8_), channel_id=1, source_target_pairs={{0,1},{1,0},{2,3},{3,2},{4,5},{5,4},{6,7},{7,6},{8,9},{9,8},{10,11... | collective-permute-start | bytes 1572872 | tf_op jit(solution)/shard_map/ppermute | solution.py:467
  143.9 1.5 collective-permute-start.12
  145.9 2.3 %copy-done.1 = bf16[1536,1536]{1,0:T(8,128)(2,1)S(1)} copy-done((bf16[1536,1536]{1,0:T(8,128)(2,1)S(1)}, bf16[1536,1536]{1,0:T(8,128)(2,1)}, u32[]{:S(2)}) %copy-start.1) | copy-done | bytes 4718616
  149.4 2.4 %first_project.1.refs_4_ = f32[256,1536]{1,0:T(8,128)S(1)} custom-call(bf16[4,64,1536]{2,1,0:T(8,128)(2,1)S(1)} %copy-done.9, bf16[1536,1536]{1,0:T(8,128)(2,1)S(1)} %copy-done.1, bf16[8,64,384]{2,1,0:T(8,128)(2,1)} %get-tuple-element.41.piece_ref), custom_call_target="tpu_custom_call" | custom-call | flops 603979776 | bytes 5505024 | tf_op jit(solution)/shard_map/first_project/pallas_call | solution.py:180
  153.1 2.3 %copy-done.2 = bf16[1536,1536]{1,0:T(8,128)(2,1)S(1)} copy-done((bf16[1536,1536]{1,0:T(8,128)(2,1)S(1)}, bf16[1536,1536]{1,0:T(8,128)(2,1)}, u32[]{:S(2)}) %copy-start.2) | copy-done | bytes 4718616
  155.4 1.4 copy-done.4
  158.0 6.7 %project_embed.1 = (bf16[4,64,1536]{2,1,0:T(8,128)(2,1)S(1)}, bf16[2,256,512]{2,1,0:T(8,128)(2,1)S(1)}) custom-call(s32[4]{0:T(128)S(1)} %pad_add_fusion.refs_0_.ids_ref, bf16[4,64,1536]{2,1,0:T(8,128)(2,1)S(1)} %copy-done.10, f32[1,1024]{1,0:T(1,128)S(1)} %bitcast.14, bf16[1536,1536]{1,0:T(8,128)(2,1)S(1)} %copy-done.2, f32[256,1536]{1,0:T(8,128)S(1)} %copy-done.4, ...), custom_call_target="tpu_custom_call" | custom-call | flops 1409286144 | bytes 10223616 | tf_op jit(solution)/shard_map/project_embed/pallas_call | solution.py:284
  165.3 3.0 %collective-permute-done.13.refs_7_ = bf16[2,512,256]{2,1,0:T(8,128)(2,1)} collective-permute-done((bf16[2,512,256]{2,1,0:T(8,128)(2,1)S(1)}, bf16[2,512,256]{2,1,0:T(8,128)(2,1)}, u32[]{:S(2)}, u32[]{:S(2)}) %collective-permute-start.13) | collective-permute-done | bytes 524320 | tf_op jit(solution)/shard_map/ppermute | solution.py:463
  168.2 2.2 %collective-permute-done.15.refs_11_ = bf16[2,512,256]{2,1,0:T(8,128)(2,1)} collective-permute-done((bf16[2,512,256]{2,1,0:T(8,128)(2,1)S(1)}, bf16[2,512,256]{2,1,0:T(8,128)(2,1)}, u32[]{:S(2)}, u32[]{:S(2)}) %collective-permute-start.15) | collective-permute-done | bytes 524320 | tf_op jit(solution)/shard_map/ppermute | solution.py:467
  170.5 5.4 %reward.2 = f32[1,8,128]{2,1,0:T(8,128)S(1)} custom-call(s32[4]{0:T(128)S(1)} %pad_add_fusion.refs_0_.ids_ref, bf16[2,256,512]{2,1,0:T(8,128)(2,1)S(1)} %get-tuple-element.46.refs_1_, f32[16,1,256]{2,1,0:T(1,128)S(1)} %bitcast.11, f32[4]{0:T(128)S(1)} %copy-done.22, bf16[2,512,256]{2,1,0:T(8,128)(2,1)S(1)} %get-tuple-element.47.refs_4_, ...), custom_call_target="tpu_custom_call" | custom-call | flops 1073741824 | bytes 4194304 | tf_op jit(solution)/shard_map/reward/pallas_call | solution.py:366
  175.9 5.4 %reward.3 = f32[8,8,128]{2,1,0:T(8,128)S(1)} custom-call(s32[4]{0:T(128)S(1)} %pad_add_fusion.refs_0_.ids_ref, bf16[2,256,512]{2,1,0:T(8,128)(2,1)S(1)} %collective-permute-done.11.refs_1_, f32[16,1,256]{2,1,0:T(1,128)S(1)} %bitcast.12, f32[8,128]{1,0:T(8,128)S(1)} %bitcast.13, bf16[2,512,256]{2,1,0:T(8,128)(2,1)S(1)} %get-tuple-element.47.refs_4_, ...), custom_call_target="tpu_custom_call" | custom-call | flops 1073741824 | bytes 4194304 | tf_op jit(solution)/shard_map/reward/pallas_call | solution.py:366
  181.4 11.0 %all_to_all.25.parts_ref = f32[8,8,128]{2,1,0:T(8,128)S(1)} all-to-all(f32[8,8,128]{2,1,0:T(8,128)S(1)} %reward.3), channel_id=1, replica_groups=mesh['groups'=2,'dom'=2,'seq'=8] {'seq'}, dimensions={0} | all-to-all | bytes 65536 | tf_op jit(solution)/shard_map/all_to_all | solution.py:471
  192.4 2.0 %resample.1.resampled_ref = bf16[4,64,1536]{2,1,0:T(8,128)(2,1)} custom-call(s32[4]{0:T(128)S(1)} %pad_add_fusion.refs_0_.ids_ref, s32[4]{0:T(128)S(1)} %copy-done.23, bf16[4,64,1536]{2,1,0:T(8,128)(2,1)S(1)} %get-tuple-element.45.own_ref, bf16[4,64,1536]{2,1,0:T(8,128)(2,1)S(1)} %collective-permute-done.10.other_ref), custom_call_target="tpu_custom_call" | custom-call | tf_op jit(solution)/shard_map/resample/pallas_call | solution.py:447
  (80 shorter events, 16.8 us)
Async XLA Ops:
  0.6 15.8 %copy-start = (bf16[1024,512]{1,0:T(8,128)(2,1)S(1)}, bf16[1024,512]{1,0:T(8,128)(2,1)}, u32[]{:S(2)}) copy-start(bf16[1024,512]{1,0:T(8,128)(2,1)} %param.20) | copy-start | bytes 3145732
  1.6 9.1 %collective-permute-start = (bf16[1,192,256]{2,1,0:T(8,128)(2,1)S(1)}, bf16[1,192,256]{2,1,0:T(8,128)(2,1)S(1)}, u32[]{:S(2)}, u32[]{:S(2)}) collective-permute-start(bf16[1,192,256]{2,1,0:T(8,128)(2,1)S(1)} %dynamic-slice_bitcast_fusion.1), channel_id=1, source_target_pairs={{0,4},{1,5},{2,6},{3,7},{4,0},{5,1},{6,2},{7,3},{8,12},{9,13},{10,... | collective-permute-start | bytes 294920 | tf_op jit(solution)/shard_map/ppermute | solution.py:467
  10.8 62.7 %all-to-all-start = ((bf16[8,3,64,384]{3,2,1,0:T(8,128)(2,1)}), bf16[8,3,64,384]{3,2,1,0:T(8,128)(2,1)S(1)}, u32[]{:S(2)}, u32[]{:S(2)}) async-start(bf16[8,3,64,384]{3,2,1,0:T(8,128)(2,1)} %get-tuple-element.29), calls=%async_computation | async-start | bytes 2359296 | tf_op jit(solution)/shard_map/all_to_all | solution.py:471
  16.4 40.0 %collective-permute-start.2 = (bf16[1,512,256]{2,1,0:T(8,128)(2,1)S(1)}, bf16[1,512,256]{2,1,0:T(8,128)(2,1)S(1)}, u32[]{:S(2)}, u32[]{:S(2)}) collective-permute-start(bf16[1,512,256]{2,1,0:T(8,128)(2,1)S(1)} %dynamic-slice_bitcast_fusion), channel_id=1, source_target_pairs={{0,4},{1,5},{2,6},{3,7},{4,0},{5,1},{6,2},{7,3},{8,12},{9,13},{10,... | collective-permute-start | bytes 786440 | tf_op jit(solution)/shard_map/ppermute | solution.py:467
  56.4 17.0 %collective-permute-start.3 = (bf16[2,512,256]{2,1,0:T(8,128)(2,1)S(1)}, bf16[2,512,256]{2,1,0:T(8,128)(2,1)}, u32[]{:S(2)}, u32[]{:S(2)}) collective-permute-start(bf16[2,512,256]{2,1,0:T(8,128)(2,1)S(1)} %pad_maximum_fusion.1.refs_1_), channel_id=1, source_target_pairs={{0,2},{1,3},{2,0},{3,1},{4,6},{5,7},{6,4},{7,5},{8,10},{9,11},{10,... | collective-permute-start | bytes 1572872 | tf_op jit(solution)/shard_map/ppermute | solution.py:467
  56.5 16.9 %collective-permute-start.1 = (bf16[2,192,256]{2,1,0:T(8,128)(2,1)S(1)}, bf16[2,192,256]{2,1,0:T(8,128)(2,1)S(1)}, u32[]{:S(2)}, u32[]{:S(2)}) collective-permute-start(bf16[2,192,256]{2,1,0:T(8,128)(2,1)S(1)} %get-tuple-element.28), channel_id=1, source_target_pairs={{0,2},{1,3},{2,0},{3,1},{4,6},{5,7},{6,4},{7,5},{8,10},{9,11},{10,... | collective-permute-start | bytes 589832 | tf_op jit(solution)/shard_map/ppermute | solution.py:467
  73.5 5.8 %copy-start.7 = (bf16[4,192,256]{2,1,0:T(8,128)(2,1)}, bf16[4,192,256]{2,1,0:T(8,128)(2,1)S(1)}, u32[]{:S(2)}) copy-start(bf16[4,192,256]{2,1,0:T(8,128)(2,1)S(1)} %get-tuple-element.32) | copy-start | bytes 1179652
  74.6 38.8 %all-to-all-start.1 = ((bf16[8,3,64,384]{3,2,1,0:T(8,128)(2,1)}), bf16[8,3,64,384]{3,2,1,0:T(8,128)(2,1)}, u32[]{:S(2)}, u32[]{:S(2)}) async-start(bf16[8,3,64,384]{3,2,1,0:T(8,128)(2,1)} %get-tuple-element.35), calls=%async_computation.1 | async-start | bytes 2359296 | tf_op jit(solution)/shard_map/all_to_all | solution.py:471
  79.3 24.7 %collective-permute-start.4 = (bf16[4,192,256]{2,1,0:T(8,128)(2,1)S(1)}, bf16[4,192,256]{2,1,0:T(8,128)(2,1)S(1)}, u32[]{:S(2)}, u32[]{:S(2)}) collective-permute-start(bf16[4,192,256]{2,1,0:T(8,128)(2,1)S(1)} %get-tuple-element.32), channel_id=1, source_target_pairs={{0,1},{1,0},{2,3},{3,2},{4,5},{5,4},{6,7},{7,6},{8,9},{9,8},{10,11... | collective-permute-start | bytes 1179656 | tf_op jit(solution)/shard_map/ppermute | solution.py:467
  81.4 32.0 %collective-permute-start.5 = (bf16[2,512,256]{2,1,0:T(8,128)(2,1)S(1)}, bf16[2,512,256]{2,1,0:T(8,128)(2,1)S(1)}, u32[]{:S(2)}, u32[]{:S(2)}) collective-permute-start(bf16[2,512,256]{2,1,0:T(8,128)(2,1)S(1)} %get-tuple-element.31.refs_0_), channel_id=1, source_target_pairs={{0,1},{1,0},{2,3},{3,2},{4,5},{5,4},{6,7},{7,6},{8,9},{9,8},{10,11... | collective-permute-start | bytes 1572872 | tf_op jit(solution)/shard_map/ppermute | solution.py:467
  81.4 31.9 %collective-permute-start.6 = (bf16[2,512,256]{2,1,0:T(8,128)(2,1)}, bf16[2,512,256]{2,1,0:T(8,128)(2,1)S(1)}, u32[]{:S(2)}, u32[]{:S(2)}) collective-permute-start(bf16[2,512,256]{2,1,0:T(8,128)(2,1)} %get-tuple-element.34.refs_8_), channel_id=1, source_target_pairs={{0,16},{16,0},{1,17},{17,1},{2,18},{18,2},{3,19},{19,3},{4,20},{20... | collective-permute-start | bytes 1572872 | tf_op jit(solution)/shard_map/ppermute | solution.py:463
  84.2 19.9 %copy-start.8 = (bf16[4,192,256]{2,1,0:T(8,128)(2,1)S(1)}, bf16[4,192,256]{2,1,0:T(8,128)(2,1)}, u32[]{:S(2)}) copy-start(bf16[4,192,256]{2,1,0:T(8,128)(2,1)} %copy-done.7) | copy-start | bytes 1179652
  89.7 23.6 %copy-start.11 = (bf16[8,64,384]{2,1,0:T(8,128)(2,1)}, bf16[8,64,384]{2,1,0:T(8,128)(2,1)S(1)}, u32[]{:S(2)}) copy-start(bf16[8,64,384]{2,1,0:T(8,128)(2,1)S(1)} %attention.2.refs_2_) | copy-start | bytes 1179652
  115.1 17.7 %collective-permute-start.7 = (bf16[8,192,256]{2,1,0:T(8,128)(2,1)S(1)}, bf16[8,192,256]{2,1,0:T(8,128)(2,1)}, u32[]{:S(2)}, u32[]{:S(2)}) collective-permute-start(bf16[8,192,256]{2,1,0:T(8,128)(2,1)S(1)} %get-tuple-element.38.refs_3_), channel_id=1, source_target_pairs={{0,16},{16,0},{1,17},{17,1},{2,18},{18,2},{3,19},{19,3},{4,20},{20... | collective-permute-start | bytes 2359304 | tf_op jit(solution)/shard_map/ppermute | solution.py:463
  116.6 16.0 %all-to-all-start.2 = ((bf16[8,64,384]{2,1,0:T(8,128)(2,1)}), bf16[8,64,384]{2,1,0:T(8,128)(2,1)}, u32[]{:S(2)}, u32[]{:S(2)}) async-start(bf16[8,64,384]{2,1,0:T(8,128)(2,1)} %copy-done.13), calls=%async_computation.2 | async-start | bytes 786432 | tf_op jit(solution)/shard_map/all_to_all | solution.py:471
  134.5 18.5 %collective-permute-start.8 = (bf16[8,192,256]{2,1,0:T(8,128)(2,1)S(1)}, bf16[8,192,256]{2,1,0:T(8,128)(2,1)}, u32[]{:S(2)}, u32[]{:S(2)}) collective-permute-start(bf16[8,192,256]{2,1,0:T(8,128)(2,1)S(1)} %get-tuple-element.43.refs_6_), channel_id=1, source_target_pairs={{0,8},{8,0},{1,9},{9,1},{2,10},{10,2},{3,11},{11,3},{4,12},{12,4},... | collective-permute-start | bytes 2359304 | tf_op jit(solution)/shard_map/ppermute | solution.py:463
  134.5 18.6 %collective-permute-start.9 = (bf16[8,192,256]{2,1,0:T(8,128)(2,1)}, bf16[8,192,256]{2,1,0:T(8,128)(2,1)}, u32[]{:S(2)}, u32[]{:S(2)}) collective-permute-start(bf16[8,192,256]{2,1,0:T(8,128)(2,1)} %get-tuple-element.44.refs_7_), channel_id=1, source_target_pairs={{0,8},{8,0},{1,9},{9,1},{2,10},{10,2},{3,11},{11,3},{4,12},{12,4},... | collective-permute-start | bytes 2359304 | tf_op jit(solution)/shard_map/ppermute | solution.py:463
  135.0 18.1 %all-to-all-start.3 = ((bf16[8,64,384]{2,1,0:T(8,128)(2,1)}), bf16[8,64,384]{2,1,0:T(8,128)(2,1)}, u32[]{:S(2)}, u32[]{:S(2)}) async-start(bf16[8,64,384]{2,1,0:T(8,128)(2,1)} %copy-done.16), calls=%async_computation.3 | async-start | bytes 786432 | tf_op jit(solution)/shard_map/all_to_all | solution.py:471
  141.1 23.6 %collective-permute-start.14 = (bf16[2,512,256]{2,1,0:T(8,128)(2,1)}, bf16[2,512,256]{2,1,0:T(8,128)(2,1)}, u32[]{:S(2)}, u32[]{:S(2)}) collective-permute-start(bf16[2,512,256]{2,1,0:T(8,128)(2,1)} %get-tuple-element.34.refs_8_), channel_id=1, source_target_pairs={{0,1},{1,0},{2,3},{3,2},{4,5},{5,4},{6,7},{7,6},{8,9},{9,8},{10,11... | collective-permute-start | bytes 1572872 | tf_op jit(solution)/shard_map/ppermute | solution.py:467
  143.9 21.4 %collective-permute-start.12 = (bf16[2,512,256]{2,1,0:T(8,128)(2,1)S(1)}, bf16[2,512,256]{2,1,0:T(8,128)(2,1)}, u32[]{:S(2)}, u32[]{:S(2)}) collective-permute-start(bf16[2,512,256]{2,1,0:T(8,128)(2,1)S(1)} %get-tuple-element.47.refs_4_), channel_id=1, source_target_pairs={{0,16},{16,0},{1,17},{17,1},{2,18},{18,2},{3,19},{19,3},{4,20},{20... | collective-permute-start | bytes 1572872 | tf_op jit(solution)/shard_map/ppermute | solution.py:463
  145.4 22.8 %collective-permute-start.13 = (bf16[2,512,256]{2,1,0:T(8,128)(2,1)S(1)}, bf16[2,512,256]{2,1,0:T(8,128)(2,1)}, u32[]{:S(2)}, u32[]{:S(2)}) collective-permute-start(bf16[2,512,256]{2,1,0:T(8,128)(2,1)S(1)} %get-tuple-element.48.refs_6_), channel_id=1, source_target_pairs={{0,16},{16,0},{1,17},{17,1},{2,18},{18,2},{3,19},{19,3},{4,20},{20... | collective-permute-start | bytes 1572872 | tf_op jit(solution)/shard_map/ppermute | solution.py:463
  145.9 2.3 %copy-start.1 = (bf16[1536,1536]{1,0:T(8,128)(2,1)S(1)}, bf16[1536,1536]{1,0:T(8,128)(2,1)}, u32[]{:S(2)}) copy-start(bf16[1536,1536]{1,0:T(8,128)(2,1)} %refs_3_.2) | copy-start | bytes 14155780
  149.4 3.7 %copy-start.21 = (f32[1024]{0:T(1024)S(1)}, f32[1024]{0:T(1024)}, u32[]{:S(2)}) copy-start(f32[1024]{0:T(1024)} %param.19) | copy-start | bytes 12292
  153.0 17.5 %collective-permute-start.15 = (bf16[2,512,256]{2,1,0:T(8,128)(2,1)S(1)}, bf16[2,512,256]{2,1,0:T(8,128)(2,1)}, u32[]{:S(2)}, u32[]{:S(2)}) collective-permute-start(bf16[2,512,256]{2,1,0:T(8,128)(2,1)S(1)} %get-tuple-element.49.refs_9_), channel_id=1, source_target_pairs={{0,1},{1,0},{2,3},{3,2},{4,5},{5,4},{6,7},{7,6},{8,9},{9,8},{10,11... | collective-permute-start | bytes 1572872 | tf_op jit(solution)/shard_map/ppermute | solution.py:467
  153.1 2.3 %copy-start.2 = (bf16[1536,1536]{1,0:T(8,128)(2,1)S(1)}, bf16[1536,1536]{1,0:T(8,128)(2,1)}, u32[]{:S(2)}) copy-start(bf16[1536,1536]{1,0:T(8,128)(2,1)} %refs_3_.2) | copy-start | bytes 14155780
  155.4 1.4 copy-start.4
  158.0 12.5 %copy-start.20 = (f32[4096]{0:T(1024)S(1)}, f32[4096]{0:T(1024)}, u32[]{:S(2)}) copy-start(f32[4096]{0:T(1024)} %param.21) | copy-start | bytes 49156
  158.0 12.5 %copy-start.22 = (f32[4]{0:T(128)S(1)}, f32[4]{0:T(128)}, u32[]{:S(2)}) copy-start(f32[4]{0:T(128)} %refs_3_.3) | copy-start | bytes 52
  164.7 27.7 %collective-permute-start.10 = (bf16[4,64,1536]{2,1,0:T(8,128)(2,1)S(1)}, bf16[4,64,1536]{2,1,0:T(8,128)(2,1)S(1)}, u32[]{:S(2)}, u32[]{:S(2)}) collective-permute-start(bf16[4,64,1536]{2,1,0:T(8,128)(2,1)S(1)} %get-tuple-element.45.own_ref), channel_id=1, source_target_pairs={{0,8},{8,0},{1,9},{9,1},{2,10},{10,2},{3,11},{11,3},{4,12},{12,4},... | collective-permute-start | bytes 2359304 | tf_op jit(solution)/shard_map/ppermute | solution.py:463
  164.8 11.1 %collective-permute-start.11 = (bf16[2,256,512]{2,1,0:T(8,128)(2,1)S(1)}, bf16[2,256,512]{2,1,0:T(8,128)(2,1)S(1)}, u32[]{:S(2)}, u32[]{:S(2)}) collective-permute-start(bf16[2,256,512]{2,1,0:T(8,128)(2,1)S(1)} %get-tuple-element.46.refs_1_), channel_id=1, source_target_pairs={{0,8},{8,0},{1,9},{9,1},{2,10},{10,2},{3,11},{11,3},{4,12},{12,4},... | collective-permute-start | bytes 1572872 | tf_op jit(solution)/shard_map/ppermute | solution.py:463
  175.9 16.5 %copy-start.23 = (s32[4]{0:T(128)S(1)}, s32[4]{0:T(128)}, u32[]{:S(2)}) copy-start(s32[4]{0:T(128)} %ancestors_ref.1) | copy-start | bytes 52
  192.4 2.1 %collective-permute-start.16 = (f32[8,128]{1,0:T(8,128)S(1)}, f32[8,128]{1,0:T(8,128)S(1)}, u32[]{:S(2)}, u32[]{:S(2)}) collective-permute-start(f32[8,128]{1,0:T(8,128)S(1)} %add_partials.1.refs_0_), channel_id=1, source_target_pairs={{0,8},{8,0},{1,9},{9,1},{2,10},{10,2},{3,11},{11,3},{4,12},{12,4},... | collective-permute-start | bytes 12296 | tf_op jit(solution)/shard_map/ppermute | solution.py:463
  (13 other events, 13.4 us)

commit v7 on v6

--- a/solution.py
+++ b/solution.py
@@ -52,19 +52,19 @@
     pass
 
 
-def gate(*arrays):
-    anywhere = pl.BlockSpec(memory_space=pl.ANY)
-    count = len(arrays)
+def gate(delayed, after):
+    count = len(delayed)
+    hbm = pl.BlockSpec(memory_space=pltpu.HBM)
     return list(
         pl.pallas_call(
             gate_kernel,
-            in_specs=[anywhere] * count,
-            out_specs=[anywhere] * count,
-            out_shape=[jax.ShapeDtypeStruct(array.shape, array.dtype) for array in arrays],
+            in_specs=[hbm] * (count + len(after)),
+            out_specs=[hbm] * count,
+            out_shape=[jax.ShapeDtypeStruct(array.shape, array.dtype) for array in delayed],
             input_output_aliases={index: index for index in range(count)},
             compiler_params=pltpu.CompilerParams(vmem_limit_bytes=MIB),
             name="gate",
-        )(*arrays)
+        )(*delayed, *after)
     )
 
 
@@ -179,7 +179,7 @@
     vmem = pl.BlockSpec(memory_space=pltpu.VMEM)
     return pl.pallas_call(
         functools.partial(first_project_kernel, chunks, width),
-        in_specs=[vmem, pl.BlockSpec(memory_space=pl.ANY), vmem],
+        in_specs=[vmem, pl.BlockSpec(memory_space=pltpu.HBM), vmem],
         out_specs=vmem,
         out_shape=jax.ShapeDtypeStruct((rows, model_width), jnp.float32),
         scratch_shapes=[
@@ -275,7 +275,7 @@
     pieces = ([] if begun is None else [begun]) + attended
     vmem = pl.BlockSpec(memory_space=pltpu.VMEM)
     smem = pl.BlockSpec(memory_space=pltpu.SMEM)
-    anywhere = pl.BlockSpec(memory_space=pl.ANY)
+    hbm = pl.BlockSpec(memory_space=pltpu.HBM)
     inputs = 4 + len(pieces) + parts
 
     def kernel(*refs):
@@ -283,7 +283,7 @@
 
     return pl.pallas_call(
         kernel,
-        in_specs=[smem, vmem, vmem, anywhere] + [vmem] * len(pieces) + [anywhere] * parts,
+        in_specs=[smem, vmem, vmem, hbm] + [vmem] * len(pieces) + [hbm] * parts,
         out_specs=[vmem, vmem],
         out_shape=[
             jax.ShapeDtypeStruct(latents.shape, jnp.bfloat16),
@@ -343,7 +343,7 @@
     totals = jnp.sum(total.reshape(particles, rows // particles, columns), axis=1)
     sums = jnp.sum(totals, axis=1, keepdims=True) * scale
     first = len(before_ref.shape) == 1
-    shape = out_ref.shape[1:]
+    shape = out_ref.shape
     out_rows = lax.broadcasted_iota(jnp.int32, shape, 0)
     lanes = lax.broadcasted_iota(jnp.int32, shape, 1)
     logits = jnp.zeros(shape, jnp.float32) if first else before_ref[...]
@@ -354,10 +354,10 @@
         if first:
             value = value + jnp.where(seq == 0, before_ref[particle], 0.0)
         logits += jnp.where(here, value, 0.0)
-    out_ref[...] = jnp.broadcast_to(logits[None], out_ref.shape)
-
-
-def reward(ids, features, weights, parts, doms, offsets, head, before, particles, scale, copies):
+    out_ref[...] = logits
+
+
+def reward(ids, features, weights, parts, doms, offsets, head, before, particles, scale):
     shards, depth, columns = weights[0].shape
     rows = features.shape[1]
     count = shards * len(weights) // parts
@@ -366,9 +366,9 @@
     return pl.pallas_call(
         functools.partial(reward_kernel, particles, scale, parts, doms, offsets),
         in_specs=[smem, vmem, vmem, smem if before.ndim == 1 else vmem]
-        + [pl.BlockSpec(memory_space=pl.ANY)] * len(weights),
+        + [pl.BlockSpec(memory_space=pltpu.HBM)] * len(weights),
         out_specs=vmem,
-        out_shape=jax.ShapeDtypeStruct((copies, 8, LANES), jnp.float32),
+        out_shape=jax.ShapeDtypeStruct((8, LANES), jnp.float32),
         scratch_shapes=[
             pltpu.VMEM((count, parts, depth, columns), jnp.bfloat16),
             pltpu.SemaphoreType.DMA((count, parts)),
@@ -383,17 +383,17 @@
     )(ids, features, head, before, *weights)
 
 
-def add_kernel(parts_ref, out_ref):
-    out_ref[...] = jnp.sum(parts_ref[...], axis=0)
+def add_kernel(*refs):
+    refs[-1][...] = sum(ref[...] for ref in refs[:-1])
 
 
 def add_parts(parts):
     return pl.pallas_call(
         add_kernel,
-        out_shape=jax.ShapeDtypeStruct(parts.shape[1:], parts.dtype),
+        out_shape=jax.ShapeDtypeStruct(parts[0].shape, parts[0].dtype),
         compiler_params=pltpu.CompilerParams(vmem_limit_bytes=2 * MIB),
         name="add_partials",
-    )(parts)
+    )(*parts)
 
 
 def finish_kernel(particles, doms, ids_ref, resampled_ref, *refs):
@@ -409,11 +409,11 @@
     out_ref[...] = (own - log_total)[:, :particles]
 
 
-def finish(ids, logits, resampled, particles):
+def finish(ids, logits, resampled, particles, doms):
     vmem = pl.BlockSpec(memory_space=pltpu.VMEM)
     anywhere = pl.BlockSpec(memory_space=pl.ANY)
     log_weights, resampled = pl.pallas_call(
-        functools.partial(finish_kernel, particles, len(logits)),
+        functools.partial(finish_kernel, particles, doms),
         in_specs=[pl.BlockSpec(memory_space=pltpu.SMEM), anywhere] + [vmem] * len(logits),
         out_specs=[vmem, anywhere],
         out_shape=[
@@ -516,44 +516,40 @@
         embed_share = jnp.concatenate([embed_share, swapped(embed_share, "seq", bit)])
         near = near + [offset ^ bit for offset in near]
     far = [offset ^ bits[-1] for offset in near]
-    embed_share, packed[0] = gate(embed_share, packed[0])
+    embed_share, packed[0] = gate([embed_share, packed[0]], [])
 
     arrived = [exchange(packed[0])]
-    embed_share = jnp.concatenate([embed_share, swapped(embed_share, "seq", bits[-1])])
     for bit in bits[:-1]:
         up_share = jnp.concatenate([up_share, swapped(up_share, "seq", bit)])
-    up_near, up_far = up_share, swapped(up_share, "seq", bits[-1])
-    embed_share, up_near, up_far, arrived[0], *packed[1:] = gate(
-        embed_share, up_near, up_far, arrived[0], *packed[1:]
-    )
+    for bit in (bits[-1], 1):
+        embed_share = jnp.concatenate([embed_share, swapped(embed_share, "seq", bit)])
+    embed_share, up_near, *packed[1:] = gate([embed_share, up_share, *packed[1:]], arrived[:1])
 
     arrived += [exchange(piece) for piece in packed[1:]]
-    embed_share = jnp.concatenate([embed_share, swapped(embed_share, "seq", 1)])
+    up_far = swapped(up_near, "seq", bits[-1])
     near_pair = swapped(up_near, "seq", 1)
+    near_groups = [up_near] + [shifted(up_near, "groups", k) for k in range(1, group_count)]
+    embed_near = [embed_share] + [shifted(embed_share, "groups", k) for k in range(1, group_count)]
+    attended = [attention(arrived[0], head_width)]
+    up_far, near_pair, attended[0], *embed_near = gate(
+        [up_far, near_pair, attended[0], *embed_near], arrived[1:]
+    )
+
+    returned = [exchange(attended[0])]
+    far_pair = swapped(up_far, "seq", 1)
     far_groups = [up_far] + [shifted(up_far, "groups", k) for k in range(1, group_count)]
-    attended = [attention(arrived[0], head_width)]
-    embed_share, near_pair, attended[0], *rest = gate(
-        embed_share, near_pair, attended[0], *far_groups[1:], *arrived[1:]
-    )
-    far_groups[1:], arrived[1:] = rest[: group_count - 1], rest[group_count - 1 :]
-
-    returned = [exchange(attended[0])]
-    embed_near = [embed_share] + [shifted(embed_share, "groups", k) for k in range(1, group_count)]
-    far_pairs = [swapped(far_groups[0], "seq", 1)]
-    attended += [attention(piece, head_width) for piece in arrived[1:]]
-    up_near, near_pair, returned[0], *rest = gate(
-        up_near, near_pair, returned[0], *embed_near, *far_groups[1:], *attended[1:]
-    )
-    embed_near, rest = rest[:group_count], rest[group_count:]
-    far_groups[1:], attended[1:] = rest[: group_count - 1], rest[group_count - 1 :]
-
-    returned += [exchange(piece) for piece in attended[1:]]
     embed_parts = embed_near + [
         shifted(piece, "dom", k) for k in range(1, dom_count) for piece in embed_near
     ]
-    near_groups = [up_near] + [shifted(up_near, "groups", k) for k in range(1, group_count)]
+    attended += [attention(piece, head_width) for piece in arrived[1:]]
+    near_pair, far_pair, *rest = gate(
+        [near_pair, far_pair, *far_groups[1:], *attended[1:]], [returned[0], *embed_parts]
+    )
+    far_groups[1:], attended[1:] = rest[: group_count - 1], rest[group_count - 1 :]
+
+    returned += [exchange(piece) for piece in attended[1:]]
     pair_groups = [near_pair] + [shifted(near_pair, "groups", k) for k in range(1, group_count)]
-    far_pairs += [swapped(piece, "seq", 1) for piece in far_groups[1:]]
+    far_pairs = [far_pair] + [swapped(piece, "seq", 1) for piece in far_groups[1:]]
     up_parts = near_groups + pair_groups + far_groups + far_pairs
     embed_offsets = near + far + [offset ^ 1 for offset in near + far]
     up_offsets = near + [offset ^ 1 for offset in near] + far + [offset ^ 1 for offset in far]
@@ -588,12 +584,22 @@
         particles=particles,
         scale=scale,
     )
-    partial_own = score(features, before=prev_logw, copies=1)[0]
-    partial_both = score(features_other, before=partial_own, copies=seq_count)
-    logits = add_parts(exchange(partial_both))
-    both_logits = [logits] + [shifted(logits, "dom", k) for k in range(1, dom_count)]
+    partial_own = score(features, before=prev_logw)
+    partial = score(features_other, before=partial_own)
+    partial = add_parts(
+        [partial] + [swapped(partial, "seq", 2 * k) for k in range(1, seq_count // 2)]
+    )
+    pair = [
+        (d * seq_count + i, (d + k) % dom_count * seq_count + (i ^ 1))
+        for k in range(1, dom_count)
+        for d in range(dom_count)
+        for i in range(seq_count)
+    ]
+    logits = [partial, swapped(partial, "seq", 1), lax.ppermute(partial, ("dom", "seq"), pair)] + [
+        shifted(partial, "dom", k) for k in range(1, dom_count)
+    ]
     resampled = resample(ids, ancestors.astype(jnp.int32), stepped, stepped_other)
-    return finish(ids, both_logits, resampled, particles)
+    return finish(ids, logits, resampled, particles, dom_count)
 
 
 def solution(mesh):

time: 197 us -> 203 us (1.030)
  blocking collectives: 11 us -> 0 us
  starting transfers between devices: 40.4 us -> 49.1 us
  waiting for transfers between devices: 85.3 us -> 90.3 us
  local copies, waits for them, and re-layouts: 20.5 us -> 25 us
    ppermute x9, waiting for transfers between devices: 3.18 us -> 22.1 us  [shifted(): lax.ppermute(array, axis, [(i, (i + step) % count) for i in range(count)])]
    ppermute x8 -> x12, waiting for transfers between devices: 77.6 us -> 63.7 us  [swapped(): lax.ppermute(array, axis, [(i, i ^ bit) for i in range(lax.axis_size(axis...]
    ppermute x8 -> x12, starting transfers between devices: 13.2 us -> 24.6 us  [swapped(): lax.ppermute(array, axis, [(i, i ^ bit) for i in range(lax.axis_size(axis...]
    all_to_all x1 -> x0, blocking collectives: 11 us -> none  [exchange(): return lax.all_to_all(array, 'seq', 0, 0, tiled=True)]
    unnamed x48 -> x58, local copies, waits for them, and re-layouts: 19.5 us -> 23.9 us
    all_to_all x4, starting transfers between devices: 21.1 us -> 18.4 us  [exchange(): return lax.all_to_all(array, 'seq', 0, 0, tiled=True)]
  transfers between devices with their start and end apart: 21 -> 26, of which waited for: 9 -> 10; matrix products, arithmetic and copies ran while one was open for 0% -> 0% of each run, Pallas kernels for 18% -> 14%
where the time goes in v7:
time: 203 us; the launch traced here: 202 us
  waiting for transfers between devices  90.3 us (44%)
  starting transfers between devices  49.1 us (24%)
  Pallas kernels  35.8 us (18%)
  local copies, waits for them, and re-layouts  25 us (12%)
    ppermute x12, waiting for transfers between devices, swapped(): lax.ppermute(array, axis, [(i, i ^ bit) for i in range(lax.axis_size(axis...  63.7 us
    ppermute x12, starting transfers between devices, swapped(): lax.ppermute(array, axis, [(i, i ^ bit) for i in range(lax.axis_size(axis...  24.6 us
    unnamed x58, local copies, waits for them, and re-layouts  23.9 us
    ppermute x9, waiting for transfers between devices, shifted(): lax.ppermute(array, axis, [(i, (i + step) % count) for i in range(count)])  22.1 us
    all_to_all x4, starting transfers between devices, exchange(): return lax.all_to_all(array, 'seq', 0, 0, tiled=True)  18.4 us
    pallas_call x2, Pallas kernels, attention(): pl.pallas_call(functools.partial(attention_kernel, head_width, block_sour...  12.5 us
    pallas_call x2, Pallas kernels, reward(): pl.pallas_call(functools.partial(reward_kernel, particles, scale, parts,...  9.59 us
    pallas_call x1, Pallas kernels, project_embed(): pl.pallas_call(kernel, in_specs=[smem, vmem, vmem, hbm] + [vmem] * len(pi...  6.76 us
  transfers between devices with their start and end apart: 26, of which 10 were waited for; matrix products, arithmetic and copies ran while one was open for 0% of the time, Pallas kernels for 14%

profile of v7, /device:TPU:0, one launch (start us, length us, event | category | flops | bytes accessed | tf_op | source)
XLA Modules:
  0.0 201.9 jit_solution(640302887641994520)
XLA Ops:
  1.6 4.0 %collective-permute-start = (bf16[1,192,256]{2,1,0:T(8,128)(2,1)S(1)}, bf16[1,192,256]{2,1,0:T(8,128)(2,1)S(1)}, u32[]{:S(2)}, u32[]{:S(2)}) collective-permute-start(bf16[1,192,256]{2,1,0:T(8,128)(2,1)S(1)} %dynamic-slice_bitcast_fusion.1), channel_id=1, source_target_pairs={{0,4},{1,5},{2,6},{3,7},{4,0},{5,1},{6,2},{7,3},{8,12},{9,13},{10,... | collective-permute-start | bytes 294920 | tf_op jit(solution)/shard_map/ppermute | solution.py:467
  11.4 5.0 %all-to-all-start = ((bf16[8,3,64,384]{3,2,1,0:T(8,128)(2,1)}), bf16[8,3,64,384]{3,2,1,0:T(8,128)(2,1)}, u32[]{:S(2)}, u32[]{:S(2)}) async-start(bf16[8,3,64,384]{3,2,1,0:T(8,128)(2,1)} %get-tuple-element.25), calls=%async_computation | async-start | bytes 2359296 | tf_op jit(solution)/shard_map/all_to_all | solution.py:471
  16.4 2.0 %collective-permute-start.1 = (bf16[2,192,256]{2,1,0:T(8,128)(2,1)S(1)}, bf16[2,192,256]{2,1,0:T(8,128)(2,1)S(1)}, u32[]{:S(2)}, u32[]{:S(2)}) collective-permute-start(bf16[2,192,256]{2,1,0:T(8,128)(2,1)S(1)} %get-tuple-element.23), channel_id=1, source_target_pairs={{0,2},{1,3},{2,0},{3,1},{4,6},{5,7},{6,4},{7,5},{8,10},{9,11},{10,... | collective-permute-start | bytes 589832 | tf_op jit(solution)/shard_map/ppermute | solution.py:467
  18.4 22.1 %collective-permute-done.1 = bf16[2,192,256]{2,1,0:T(8,128)(2,1)S(1)} collective-permute-done((bf16[2,192,256]{2,1,0:T(8,128)(2,1)S(1)}, bf16[2,192,256]{2,1,0:T(8,128)(2,1)S(1)}, u32[]{:S(2)}, u32[]{:S(2)}) %collective-permute-start.1) | collective-permute-done | bytes 196640 | tf_op jit(solution)/shard_map/ppermute | solution.py:467
  41.8 4.4 %collective-permute-start.3 = (bf16[1,512,256]{2,1,0:T(8,128)(2,1)S(1)}, bf16[1,512,256]{2,1,0:T(8,128)(2,1)S(1)}, u32[]{:S(2)}, u32[]{:S(2)}) collective-permute-start(bf16[1,512,256]{2,1,0:T(8,128)(2,1)S(1)} %dynamic-slice_bitcast_fusion), channel_id=1, source_target_pairs={{0,4},{1,5},{2,6},{3,7},{4,0},{5,1},{6,2},{7,3},{8,12},{9,13},{10,... | collective-permute-start | bytes 786440 | tf_op jit(solution)/shard_map/ppermute | solution.py:467
  46.2 10.7 %collective-permute-done.3 = bf16[1,512,256]{2,1,0:T(8,128)(2,1)S(1)} collective-permute-done((bf16[1,512,256]{2,1,0:T(8,128)(2,1)S(1)}, bf16[1,512,256]{2,1,0:T(8,128)(2,1)S(1)}, u32[]{:S(2)}, u32[]{:S(2)}) %collective-permute-start.3) | collective-permute-done | bytes 262176 | tf_op jit(solution)/shard_map/ppermute | solution.py:467
  59.4 4.2 %all-to-all-start.1 = ((bf16[8,3,64,384]{3,2,1,0:T(8,128)(2,1)}), bf16[8,3,64,384]{3,2,1,0:T(8,128)(2,1)}, u32[]{:S(2)}, u32[]{:S(2)}) async-start(bf16[8,3,64,384]{3,2,1,0:T(8,128)(2,1)} %copy-done.7), calls=%async_computation.1 | async-start | bytes 2359296 | tf_op jit(solution)/shard_map/all_to_all | solution.py:471
  63.6 1.6 collective-permute-start.6
  65.2 1.8 collective-permute-start.4
  67.0 1.5 collective-permute-start.5
  68.5 6.3 %attention.2.refs_2_ = bf16[8,64,384]{2,1,0:T(8,128)(2,1)S(1)} custom-call(bf16[8,3,64,384]{3,2,1,0:T(8,128)(2,1)} %all-to-all-done.refs_3_.qkv_ref), custom_call_target="tpu_custom_call" | custom-call | flops 402653184 | bytes 1572864 | tf_op jit(solution)/shard_map/attention/pallas_call | solution.py:107
  75.5 20.7 %collective-permute-done.4.refs_0_ = bf16[2,512,256]{2,1,0:T(8,128)(2,1)S(1)} collective-permute-done((bf16[2,512,256]{2,1,0:T(8,128)(2,1)S(1)}, bf16[2,512,256]{2,1,0:T(8,128)(2,1)S(1)}, u32[]{:S(2)}, u32[]{:S(2)}) %collective-permute-start.4) | collective-permute-done | bytes 524320 | tf_op jit(solution)/shard_map/ppermute | solution.py:467
  98.5 4.6 %all-to-all-start.2 = ((bf16[8,64,384]{2,1,0:T(8,128)(2,1)}), bf16[8,64,384]{2,1,0:T(8,128)(2,1)}, u32[]{:S(2)}, u32[]{:S(2)}) async-start(bf16[8,64,384]{2,1,0:T(8,128)(2,1)} %copy-done.18), calls=%async_computation.2 | async-start | bytes 786432 | tf_op jit(solution)/shard_map/all_to_all | solution.py:471
  103.1 2.0 collective-permute-start.7
  105.1 1.5 collective-permute-start.8
  106.6 6.3 %attention.3.refs_3_ = bf16[8,64,384]{2,1,0:T(8,128)(2,1)S(1)} custom-call(bf16[8,3,64,384]{3,2,1,0:T(8,128)(2,1)} %all-to-all-done.1.refs_5_.qkv_ref), custom_call_target="tpu_custom_call" | custom-call | flops 402653184 | bytes 1572864 | tf_op jit(solution)/shard_map/attention/pallas_call | solution.py:107
  113.6 7.4 %collective-permute-done.7.refs_1_ = bf16[2,512,256]{2,1,0:T(8,128)(2,1)S(1)} collective-permute-done((bf16[2,512,256]{2,1,0:T(8,128)(2,1)}, bf16[2,512,256]{2,1,0:T(8,128)(2,1)S(1)}, u32[]{:S(2)}, u32[]{:S(2)}) %collective-permute-start.7) | collective-permute-done | bytes 524320 | tf_op jit(solution)/shard_map/ppermute | solution.py:467
  125.5 4.5 %all-to-all-start.3 = ((bf16[8,64,384]{2,1,0:T(8,128)(2,1)}), bf16[8,64,384]{2,1,0:T(8,128)(2,1)}, u32[]{:S(2)}, u32[]{:S(2)}) async-start(bf16[8,64,384]{2,1,0:T(8,128)(2,1)} %copy-done.21), calls=%async_computation.3 | async-start | bytes 786432 | tf_op jit(solution)/shard_map/all_to_all | solution.py:471
  130.8 2.3 %copy-done.1 = bf16[1536,1536]{1,0:T(8,128)(2,1)S(1)} copy-done((bf16[1536,1536]{1,0:T(8,128)(2,1)S(1)}, bf16[1536,1536]{1,0:T(8,128)(2,1)}, u32[]{:S(2)}) %copy-start.1) | copy-done | bytes 4718616
  134.3 2.4 %first_project.1.refs_4_ = f32[256,1536]{1,0:T(8,128)S(1)} custom-call(bf16[4,64,1536]{2,1,0:T(8,128)(2,1)S(1)} %copy-done.14, bf16[1536,1536]{1,0:T(8,128)(2,1)S(1)} %copy-done.1, bf16[8,64,384]{2,1,0:T(8,128)(2,1)} %all-to-all-done.2.piece_ref.refs_4_), custom_call_target="tpu_custom_call" | custom-call | flops 603979776 | bytes 5505024 | tf_op jit(solution)/shard_map/first_project/pallas_call | solution.py:180
  137.8 3.8 %all-to-all-done.3.refs_5_ = bf16[8,64,384]{2,1,0:T(8,128)(2,1)} async-done(((bf16[8,64,384]{2,1,0:T(8,128)(2,1)}), bf16[8,64,384]{2,1,0:T(8,128)(2,1)}, u32[]{:S(2)}, u32[]{:S(2)}) %all-to-all-start.3) | async-done | bytes 393248 | tf_op jit(solution)/shard_map/all_to_all | solution.py:471
  141.7 2.3 %copy-done.2 = bf16[1536,1536]{1,0:T(8,128)(2,1)S(1)} copy-done((bf16[1536,1536]{1,0:T(8,128)(2,1)S(1)}, bf16[1536,1536]{1,0:T(8,128)(2,1)}, u32[]{:S(2)}) %copy-start.2) | copy-done | bytes 4718616
  146.6 6.8 %project_embed.1 = (bf16[4,64,1536]{2,1,0:T(8,128)(2,1)S(1)}, bf16[2,256,512]{2,1,0:T(8,128)(2,1)S(1)}) custom-call(s32[4]{0:T(128)S(1)} %pad_add_fusion.refs_0_.ids_ref, bf16[4,64,1536]{2,1,0:T(8,128)(2,1)S(1)} %copy-done.15, f32[1,1024]{1,0:T(1,128)S(1)} %bitcast.12, bf16[1536,1536]{1,0:T(8,128)(2,1)S(1)} %copy-done.2, f32[256,1536]{1,0:T(8,128)S(1)} %copy-done.4, ...), custom_call_target="tpu_custom_call" | custom-call | flops 1409286144 | bytes 10223616 | tf_op jit(solution)/shard_map/project_embed/pallas_call | solution.py:284
  153.4 1.6 collective-permute-start.13
  156.9 11.3 %collective-permute-done.13.refs_5_ = bf16[2,512,256]{2,1,0:T(8,128)(2,1)S(1)} collective-permute-done((bf16[2,512,256]{2,1,0:T(8,128)(2,1)S(1)}, bf16[2,512,256]{2,1,0:T(8,128)(2,1)S(1)}, u32[]{:S(2)}, u32[]{:S(2)}) %collective-permute-start.13) | collective-permute-done | bytes 524320 | tf_op jit(solution)/shard_map/ppermute | solution.py:463
  168.2 10.8 %collective-permute-done.14.refs_7_ = bf16[2,512,256]{2,1,0:T(8,128)(2,1)S(1)} collective-permute-done((bf16[2,512,256]{2,1,0:T(8,128)(2,1)S(1)}, bf16[2,512,256]{2,1,0:T(8,128)(2,1)S(1)}, u32[]{:S(2)}, u32[]{:S(2)}) %collective-permute-start.14) | collective-permute-done | bytes 524320 | tf_op jit(solution)/shard_map/ppermute | solution.py:463
  179.0 4.8 %reward.2.refs_3_ = f32[8,128]{1,0:T(8,128)S(1)} custom-call(s32[4]{0:T(128)S(1)} %pad_add_fusion.refs_0_.ids_ref, bf16[2,256,512]{2,1,0:T(8,128)(2,1)S(1)} %get-tuple-element.36.refs_1_, f32[16,1,256]{2,1,0:T(1,128)S(1)} %bitcast.10, f32[4]{0:T(128)S(1)} %copy-done.27, bf16[2,512,256]{2,1,0:T(8,128)(2,1)S(1)} %get-tuple-element.26.refs_4_, ...), custom_call_target="tpu_custom_call" | custom-call | flops 1073741824 | bytes 4194304 | tf_op jit(solution)/shard_map/reward/pallas_call | solution.py:366
  183.8 4.8 %reward.3.refs_0_ = f32[8,128]{1,0:T(8,128)S(1)} custom-call(s32[4]{0:T(128)S(1)} %pad_add_fusion.refs_0_.ids_ref, bf16[2,256,512]{2,1,0:T(8,128)(2,1)S(1)} %collective-permute-done.12.refs_1_, f32[16,1,256]{2,1,0:T(1,128)S(1)} %bitcast.11, f32[8,128]{1,0:T(8,128)S(1)} %reward.2.refs_3_, bf16[2,512,256]{2,1,0:T(8,128)(2,1)S(1)} %get-tuple-element.26.refs_4_, ...), custom_call_target="tpu_custom_call" | custom-call | flops 1073741824 | bytes 4194304 | tf_op jit(solution)/shard_map/reward/pallas_call | solution.py:366
  190.4 2.7 %collective-permute-start.18 = (f32[8,128]{1,0:T(8,128)S(1)}, f32[8,128]{1,0:T(8,128)S(1)}, u32[]{:S(2)}, u32[]{:S(2)}) collective-permute-start(f32[8,128]{1,0:T(8,128)S(1)} %reward.3.refs_0_), channel_id=1, source_target_pairs={{0,6},{1,7},{2,4},{3,5},{4,2},{5,3},{6,0},{7,1},{8,14},{9,15},{10,... | collective-permute-start | bytes 12296 | tf_op jit(solution)/shard_map/ppermute | solution.py:467
  194.1 1.7 collective-permute-done.18.refs_3_
  195.8 1.8 collective-permute-start.19
  198.0 2.0 %resample.1.resampled_ref = bf16[4,64,1536]{2,1,0:T(8,128)(2,1)} custom-call(s32[4]{0:T(128)S(1)} %pad_add_fusion.refs_0_.ids_ref, s32[4]{0:T(128)S(1)} %copy-done.28, bf16[4,64,1536]{2,1,0:T(8,128)(2,1)S(1)} %get-tuple-element.35.own_ref, bf16[4,64,1536]{2,1,0:T(8,128)(2,1)S(1)} %collective-permute-done.11.other_ref), custom_call_target="tpu_custom_call" | custom-call | tf_op jit(solution)/shard_map/resample/pallas_call | solution.py:447
  (99 shorter events, 30.6 us)
Async XLA Ops:
  0.6 41.2 %copy-start = (bf16[1024,512]{1,0:T(8,128)(2,1)S(1)}, bf16[1024,512]{1,0:T(8,128)(2,1)}, u32[]{:S(2)}) copy-start(bf16[1024,512]{1,0:T(8,128)(2,1)} %param.20) | copy-start | bytes 3145732
  1.6 9.7 %collective-permute-start = (bf16[1,192,256]{2,1,0:T(8,128)(2,1)S(1)}, bf16[1,192,256]{2,1,0:T(8,128)(2,1)S(1)}, u32[]{:S(2)}, u32[]{:S(2)}) collective-permute-start(bf16[1,192,256]{2,1,0:T(8,128)(2,1)S(1)} %dynamic-slice_bitcast_fusion.1), channel_id=1, source_target_pairs={{0,4},{1,5},{2,6},{3,7},{4,0},{5,1},{6,2},{7,3},{8,12},{9,13},{10,... | collective-permute-start | bytes 294920 | tf_op jit(solution)/shard_map/ppermute | solution.py:467
  11.4 45.7 %all-to-all-start = ((bf16[8,3,64,384]{3,2,1,0:T(8,128)(2,1)}), bf16[8,3,64,384]{3,2,1,0:T(8,128)(2,1)}, u32[]{:S(2)}, u32[]{:S(2)}) async-start(bf16[8,3,64,384]{3,2,1,0:T(8,128)(2,1)} %get-tuple-element.25), calls=%async_computation | async-start | bytes 2359296 | tf_op jit(solution)/shard_map/all_to_all | solution.py:471
  16.4 24.2 %collective-permute-start.1 = (bf16[2,192,256]{2,1,0:T(8,128)(2,1)S(1)}, bf16[2,192,256]{2,1,0:T(8,128)(2,1)S(1)}, u32[]{:S(2)}, u32[]{:S(2)}) collective-permute-start(bf16[2,192,256]{2,1,0:T(8,128)(2,1)S(1)} %get-tuple-element.23), channel_id=1, source_target_pairs={{0,2},{1,3},{2,0},{3,1},{4,6},{5,7},{6,4},{7,5},{8,10},{9,11},{10,... | collective-permute-start | bytes 589832 | tf_op jit(solution)/shard_map/ppermute | solution.py:467
  40.6 16.4 %collective-permute-start.2 = (bf16[4,192,256]{2,1,0:T(8,128)(2,1)S(1)}, bf16[4,192,256]{2,1,0:T(8,128)(2,1)S(1)}, u32[]{:S(2)}, u32[]{:S(2)}) collective-permute-start(bf16[4,192,256]{2,1,0:T(8,128)(2,1)S(1)} %pad_maximum_fusion.2), channel_id=1, source_target_pairs={{0,1},{1,0},{2,3},{3,2},{4,5},{5,4},{6,7},{7,6},{8,9},{9,8},{10,11... | collective-permute-start | bytes 1179656 | tf_op jit(solution)/shard_map/ppermute | solution.py:467
  41.8 15.1 %collective-permute-start.3 = (bf16[1,512,256]{2,1,0:T(8,128)(2,1)S(1)}, bf16[1,512,256]{2,1,0:T(8,128)(2,1)S(1)}, u32[]{:S(2)}, u32[]{:S(2)}) collective-permute-start(bf16[1,512,256]{2,1,0:T(8,128)(2,1)S(1)} %dynamic-slice_bitcast_fusion), channel_id=1, source_target_pairs={{0,4},{1,5},{2,6},{3,7},{4,0},{5,1},{6,2},{7,3},{8,12},{9,13},{10,... | collective-permute-start | bytes 786440 | tf_op jit(solution)/shard_map/ppermute | solution.py:467
  59.4 36.8 %all-to-all-start.1 = ((bf16[8,3,64,384]{3,2,1,0:T(8,128)(2,1)}), bf16[8,3,64,384]{3,2,1,0:T(8,128)(2,1)}, u32[]{:S(2)}, u32[]{:S(2)}) async-start(bf16[8,3,64,384]{3,2,1,0:T(8,128)(2,1)} %copy-done.7), calls=%async_computation.1 | async-start | bytes 2359296 | tf_op jit(solution)/shard_map/all_to_all | solution.py:471
  63.6 32.6 %collective-permute-start.6 = (bf16[8,192,256]{2,1,0:T(8,128)(2,1)S(1)}, bf16[8,192,256]{2,1,0:T(8,128)(2,1)}, u32[]{:S(2)}, u32[]{:S(2)}) collective-permute-start(bf16[8,192,256]{2,1,0:T(8,128)(2,1)S(1)} %get-tuple-element.27.refs_3_), channel_id=1, source_target_pairs={{0,16},{16,0},{1,17},{17,1},{2,18},{18,2},{3,19},{19,3},{4,20},{20... | collective-permute-start | bytes 2359304 | tf_op jit(solution)/shard_map/ppermute | solution.py:463
  65.2 31.0 %collective-permute-start.4 = (bf16[2,512,256]{2,1,0:T(8,128)(2,1)S(1)}, bf16[2,512,256]{2,1,0:T(8,128)(2,1)S(1)}, u32[]{:S(2)}, u32[]{:S(2)}) collective-permute-start(bf16[2,512,256]{2,1,0:T(8,128)(2,1)S(1)} %get-tuple-element.26.refs_4_), channel_id=1, source_target_pairs={{0,2},{1,3},{2,0},{3,1},{4,6},{5,7},{6,4},{7,5},{8,10},{9,11},{10,... | collective-permute-start | bytes 1572872 | tf_op jit(solution)/shard_map/ppermute | solution.py:467
  67.0 29.2 %collective-permute-start.5 = (bf16[2,512,256]{2,1,0:T(8,128)(2,1)S(1)}, bf16[2,512,256]{2,1,0:T(8,128)(2,1)S(1)}, u32[]{:S(2)}, u32[]{:S(2)}) collective-permute-start(bf16[2,512,256]{2,1,0:T(8,128)(2,1)S(1)} %get-tuple-element.26.refs_4_), channel_id=1, source_target_pairs={{0,1},{1,0},{2,3},{3,2},{4,5},{5,4},{6,7},{7,6},{8,9},{9,8},{10,11... | collective-permute-start | bytes 1572872 | tf_op jit(solution)/shard_map/ppermute | solution.py:467
  98.0 23.9 %collective-permute-start.10 = (bf16[8,192,256]{2,1,0:T(8,128)(2,1)}, bf16[8,192,256]{2,1,0:T(8,128)(2,1)}, u32[]{:S(2)}, u32[]{:S(2)}) collective-permute-start(bf16[8,192,256]{2,1,0:T(8,128)(2,1)} %get-tuple-element.33.refs_6_.refs_7_), channel_id=1, source_target_pairs={{0,8},{8,0},{1,9},{9,1},{2,10},{10,2},{3,11},{11,3},{4,12},{12,4},... | collective-permute-start | bytes 2359304 | tf_op jit(solution)/shard_map/ppermute | solution.py:463
  98.0 23.9 %collective-permute-start.9 = (bf16[8,192,256]{2,1,0:T(8,128)(2,1)S(1)}, bf16[8,192,256]{2,1,0:T(8,128)(2,1)}, u32[]{:S(2)}, u32[]{:S(2)}) collective-permute-start(bf16[8,192,256]{2,1,0:T(8,128)(2,1)S(1)} %get-tuple-element.32.refs_5_.refs_6_), channel_id=1, source_target_pairs={{0,8},{8,0},{1,9},{9,1},{2,10},{10,2},{3,11},{11,3},{4,12},{12,4},... | collective-permute-start | bytes 2359304 | tf_op jit(solution)/shard_map/ppermute | solution.py:463
  98.5 23.4 %all-to-all-start.2 = ((bf16[8,64,384]{2,1,0:T(8,128)(2,1)}), bf16[8,64,384]{2,1,0:T(8,128)(2,1)}, u32[]{:S(2)}, u32[]{:S(2)}) async-start(bf16[8,64,384]{2,1,0:T(8,128)(2,1)} %copy-done.18), calls=%async_computation.2 | async-start | bytes 786432 | tf_op jit(solution)/shard_map/all_to_all | solution.py:471
  103.1 18.0 %collective-permute-start.7 = (bf16[2,512,256]{2,1,0:T(8,128)(2,1)}, bf16[2,512,256]{2,1,0:T(8,128)(2,1)S(1)}, u32[]{:S(2)}, u32[]{:S(2)}) collective-permute-start(bf16[2,512,256]{2,1,0:T(8,128)(2,1)} %copy-done.8), channel_id=1, source_target_pairs={{0,1},{1,0},{2,3},{3,2},{4,5},{5,4},{6,7},{7,6},{8,9},{9,8},{10,11... | collective-permute-start | bytes 1572872 | tf_op jit(solution)/shard_map/ppermute | solution.py:467
  105.1 15.9 %collective-permute-start.8 = (bf16[2,512,256]{2,1,0:T(8,128)(2,1)}, bf16[2,512,256]{2,1,0:T(8,128)(2,1)S(1)}, u32[]{:S(2)}, u32[]{:S(2)}) collective-permute-start(bf16[2,512,256]{2,1,0:T(8,128)(2,1)} %copy-done.8), channel_id=1, source_target_pairs={{0,16},{16,0},{1,17},{17,1},{2,18},{18,2},{3,19},{19,3},{4,20},{20... | collective-permute-start | bytes 1572872 | tf_op jit(solution)/shard_map/ppermute | solution.py:463
  125.5 16.2 %all-to-all-start.3 = ((bf16[8,64,384]{2,1,0:T(8,128)(2,1)}), bf16[8,64,384]{2,1,0:T(8,128)(2,1)}, u32[]{:S(2)}, u32[]{:S(2)}) async-start(bf16[8,64,384]{2,1,0:T(8,128)(2,1)} %copy-done.21), calls=%async_computation.3 | async-start | bytes 786432 | tf_op jit(solution)/shard_map/all_to_all | solution.py:471
  146.6 9.0 %copy-start.13 = (bf16[2,512,256]{2,1,0:T(8,128)(2,1)S(1)}, bf16[2,512,256]{2,1,0:T(8,128)(2,1)}, u32[]{:S(2)}) copy-start(bf16[2,512,256]{2,1,0:T(8,128)(2,1)} %copy-done.12) | copy-start | bytes 1572868
  146.6 32.4 %copy-start.9 = (bf16[2,512,256]{2,1,0:T(8,128)(2,1)S(1)}, bf16[2,512,256]{2,1,0:T(8,128)(2,1)}, u32[]{:S(2)}) copy-start(bf16[2,512,256]{2,1,0:T(8,128)(2,1)} %copy-done.8) | copy-start | bytes 1572868
  146.6 32.4 %copy-start.25 = (f32[4096]{0:T(1024)S(1)}, f32[4096]{0:T(1024)}, u32[]{:S(2)}) copy-start(f32[4096]{0:T(1024)} %param.21) | copy-start | bytes 49156
  146.6 32.4 %copy-start.27 = (f32[4]{0:T(128)S(1)}, f32[4]{0:T(128)}, u32[]{:S(2)}) copy-start(f32[4]{0:T(128)} %refs_3_.3) | copy-start | bytes 52
  153.3 44.6 %collective-permute-start.11 = (bf16[4,64,1536]{2,1,0:T(8,128)(2,1)S(1)}, bf16[4,64,1536]{2,1,0:T(8,128)(2,1)S(1)}, u32[]{:S(2)}, u32[]{:S(2)}) collective-permute-start(bf16[4,64,1536]{2,1,0:T(8,128)(2,1)S(1)} %get-tuple-element.35.own_ref), channel_id=1, source_target_pairs={{0,8},{8,0},{1,9},{9,1},{2,10},{10,2},{3,11},{11,3},{4,12},{12,4},... | collective-permute-start | bytes 2359304 | tf_op jit(solution)/shard_map/ppermute | solution.py:463
  153.4 14.8 %collective-permute-start.13 = (bf16[2,512,256]{2,1,0:T(8,128)(2,1)S(1)}, bf16[2,512,256]{2,1,0:T(8,128)(2,1)S(1)}, u32[]{:S(2)}, u32[]{:S(2)}) collective-permute-start(bf16[2,512,256]{2,1,0:T(8,128)(2,1)S(1)} %get-tuple-element.26.refs_4_), channel_id=1, source_target_pairs={{0,16},{16,0},{1,17},{17,1},{2,18},{18,2},{3,19},{19,3},{4,20},{20... | collective-permute-start | bytes 1572872 | tf_op jit(solution)/shard_map/ppermute | solution.py:463
  155.0 24.0 %collective-permute-start.14 = (bf16[2,512,256]{2,1,0:T(8,128)(2,1)S(1)}, bf16[2,512,256]{2,1,0:T(8,128)(2,1)S(1)}, u32[]{:S(2)}, u32[]{:S(2)}) collective-permute-start(bf16[2,512,256]{2,1,0:T(8,128)(2,1)S(1)} %get-tuple-element.37.refs_6_), channel_id=1, source_target_pairs={{0,16},{16,0},{1,17},{17,1},{2,18},{18,2},{3,19},{19,3},{4,20},{20... | collective-permute-start | bytes 1572872 | tf_op jit(solution)/shard_map/ppermute | solution.py:463
  155.5 23.5 %collective-permute-start.15 = (bf16[2,512,256]{2,1,0:T(8,128)(2,1)S(1)}, bf16[2,512,256]{2,1,0:T(8,128)(2,1)S(1)}, u32[]{:S(2)}, u32[]{:S(2)}) collective-permute-start(bf16[2,512,256]{2,1,0:T(8,128)(2,1)S(1)} %copy-done.13), channel_id=1, source_target_pairs={{0,1},{1,0},{2,3},{3,2},{4,5},{5,4},{6,7},{7,6},{8,9},{9,8},{10,11... | collective-permute-start | bytes 1572872 | tf_op jit(solution)/shard_map/ppermute | solution.py:467
  156.9 26.9 %collective-permute-start.12 = (bf16[2,256,512]{2,1,0:T(8,128)(2,1)S(1)}, bf16[2,256,512]{2,1,0:T(8,128)(2,1)S(1)}, u32[]{:S(2)}, u32[]{:S(2)}) collective-permute-start(bf16[2,256,512]{2,1,0:T(8,128)(2,1)S(1)} %get-tuple-element.36.refs_1_), channel_id=1, source_target_pairs={{0,8},{8,0},{1,9},{9,1},{2,10},{10,2},{3,11},{11,3},{4,12},{12,4},... | collective-permute-start | bytes 1572872 | tf_op jit(solution)/shard_map/ppermute | solution.py:463
  183.8 14.2 %copy-start.28 = (s32[4]{0:T(128)S(1)}, s32[4]{0:T(128)}, u32[]{:S(2)}) copy-start(s32[4]{0:T(128)} %ancestors_ref.1) | copy-start | bytes 52
  188.6 4.5 %collective-permute-start.16 = (f32[8,128]{1,0:T(8,128)S(1)}, f32[8,128]{1,0:T(8,128)S(1)}, u32[]{:S(2)}, u32[]{:S(2)}) collective-permute-start(f32[8,128]{1,0:T(8,128)S(1)} %reward.3.refs_0_), channel_id=1, source_target_pairs={{0,2},{1,3},{2,0},{3,1},{4,6},{5,7},{6,4},{7,5},{8,10},{9,11},{10,... | collective-permute-start | bytes 12296 | tf_op jit(solution)/shard_map/ppermute | solution.py:467
  189.6 4.5 %collective-permute-start.17 = (f32[8,128]{1,0:T(8,128)S(1)}, f32[8,128]{1,0:T(8,128)S(1)}, u32[]{:S(2)}, u32[]{:S(2)}) collective-permute-start(f32[8,128]{1,0:T(8,128)S(1)} %reward.3.refs_0_), channel_id=1, source_target_pairs={{0,4},{1,5},{2,6},{3,7},{4,0},{5,1},{6,2},{7,3},{8,12},{9,13},{10,... | collective-permute-start | bytes 12296 | tf_op jit(solution)/shard_map/ppermute | solution.py:467
  190.4 5.4 %collective-permute-start.18 = (f32[8,128]{1,0:T(8,128)S(1)}, f32[8,128]{1,0:T(8,128)S(1)}, u32[]{:S(2)}, u32[]{:S(2)}) collective-permute-start(f32[8,128]{1,0:T(8,128)S(1)} %reward.3.refs_0_), channel_id=1, source_target_pairs={{0,6},{1,7},{2,4},{3,5},{4,2},{5,3},{6,0},{7,1},{8,14},{9,15},{10,... | collective-permute-start | bytes 12296 | tf_op jit(solution)/shard_map/ppermute | solution.py:467
  195.8 4.2 %collective-permute-start.19 = (f32[8,128]{1,0:T(8,128)S(1)}, f32[8,128]{1,0:T(8,128)S(1)}, u32[]{:S(2)}, u32[]{:S(2)}) collective-permute-start(f32[8,128]{1,0:T(8,128)S(1)} %add_partials.1.refs_0_), channel_id=1, source_target_pairs={{0,1},{1,0},{2,3},{3,2},{4,5},{5,4},{6,7},{7,6},{8,9},{9,8},{10,11... | collective-permute-start | bytes 12296 | tf_op jit(solution)/shard_map/ppermute | solution.py:467
  197.6 3.0 %collective-permute-start.20 = (f32[8,128]{1,0:T(8,128)S(1)}, f32[8,128]{1,0:T(8,128)S(1)}, u32[]{:S(2)}, u32[]{:S(2)}) collective-permute-start(f32[8,128]{1,0:T(8,128)S(1)} %add_partials.1.refs_0_), channel_id=1, source_target_pairs={{0,9},{1,8},{2,11},{3,10},{4,13},{5,12},{6,15},{7,14},{8,1},{9,0},... | collective-permute-start | bytes 12296 | tf_op jit(solution)/shard_map/ppermute | solution.py:598
  197.6 3.0 %collective-permute-start.21 = (f32[8,128]{1,0:T(8,128)S(1)}, f32[8,128]{1,0:T(8,128)S(1)}, u32[]{:S(2)}, u32[]{:S(2)}) collective-permute-start(f32[8,128]{1,0:T(8,128)S(1)} %add_partials.1.refs_0_), channel_id=1, source_target_pairs={{0,8},{8,0},{1,9},{9,1},{2,10},{10,2},{3,11},{11,3},{4,12},{12,4},... | collective-permute-start | bytes 12296 | tf_op jit(solution)/shard_map/ppermute | solution.py:463
  (23 other events, 36.5 us)

commit v8 on v7

--- a/solution.py
+++ b/solution.py
@@ -42,7 +42,7 @@
             in_specs=[vmem] * 3,
             out_specs=[vmem] * chunks,
             out_shape=[shape] * chunks,
-            compiler_params=pltpu.CompilerParams(vmem_limit_bytes=16 * MIB),
+            compiler_params=pltpu.CompilerParams(vmem_limit_bytes=60 * MIB),
             name="pack_heads",
         )(queries, keys, values)
     )
@@ -52,19 +52,21 @@
     pass
 
 
-def gate(delayed, after):
-    count = len(delayed)
-    hbm = pl.BlockSpec(memory_space=pltpu.HBM)
+def gate(pinned, delayed, after):
+    count = len(pinned) + len(delayed)
+    anywhere = pl.BlockSpec(memory_space=pl.ANY)
+    specs = [pl.BlockSpec(memory_space=pltpu.HBM)] * len(pinned) + [anywhere] * len(delayed)
+    arrays = [*pinned, *delayed]
     return list(
         pl.pallas_call(
             gate_kernel,
-            in_specs=[hbm] * (count + len(after)),
-            out_specs=[hbm] * count,
-            out_shape=[jax.ShapeDtypeStruct(array.shape, array.dtype) for array in delayed],
+            in_specs=specs + [anywhere] * len(after),
+            out_specs=specs,
+            out_shape=[jax.ShapeDtypeStruct(array.shape, array.dtype) for array in arrays],
             input_output_aliases={index: index for index in range(count)},
             compiler_params=pltpu.CompilerParams(vmem_limit_bytes=MIB),
             name="gate",
-        )(*delayed, *after)
+        )(*arrays, *after)
     )
 
 
@@ -110,7 +112,7 @@
         in_specs=[pl.BlockSpec((sources, 3, tokens, step), lambda i: (0, 0, 0, i))],
         out_specs=pl.BlockSpec((sources, tokens, step), lambda i: (0, 0, i)),
         out_shape=jax.ShapeDtypeStruct((sources, tokens, columns), jnp.bfloat16),
-        compiler_params=pltpu.CompilerParams(vmem_limit_bytes=8 * MIB + 6 * scores_bytes),
+        compiler_params=pltpu.CompilerParams(vmem_limit_bytes=60 * MIB),
         cost_estimate=pl.CostEstimate(
             flops=4 * total * total * columns,
             bytes_accessed=8 * total * columns,
@@ -120,12 +122,16 @@
     )(qkv)
 
 
+def column_block(model_width):
+    return 512 if model_width % 512 == 0 else model_width
+
+
 class ProjectionWeights:
     def __init__(self, weight_ref, vmem_ref, sems, chunks, wanted, width):
         depth, model_width = weight_ref.shape
         part = width // chunks
         blocks = depth // width
-        self.block = 512 if model_width % 512 == 0 else model_width
+        self.block = column_block(model_width)
         self.copies = []
         for group in range(model_width // self.block):
             cols = slice(group * self.block, (group + 1) * self.block)
@@ -185,9 +191,11 @@
         scratch_shapes=[
             pltpu.VMEM((depth, model_width), jnp.bfloat16),
             pltpu.VMEM((rows, depth), jnp.bfloat16),
-            pltpu.SemaphoreType.DMA((max(1, model_width // 512), model_width // width)),
+            pltpu.SemaphoreType.DMA(
+                (model_width // column_block(model_width), model_width // width)
+            ),
         ],
-        compiler_params=pltpu.CompilerParams(vmem_limit_bytes=16 * MIB),
+        compiler_params=pltpu.CompilerParams(vmem_limit_bytes=60 * MIB),
         cost_estimate=pl.CostEstimate(
             flops=2 * rows * depth * model_width,
             bytes_accessed=2 * depth * model_width + 8 * rows * model_width,
@@ -197,12 +205,13 @@
     )(latents, out_weight, piece)
 
 
-def project_kernel(chunks, width, parts, offsets, depth_parts, refs_in, refs_out):
-    ids_ref, latents_ref, gain_ref, out_weight_ref = refs_in[:4]
-    rest, weight_refs = list(refs_in[4:-parts]), refs_in[-parts:]
-    begun_ref = rest.pop(0) if chunks > 1 else latents_ref
+def project_kernel(chunks, width, pieces, parts, offsets, depth_parts, refs_in, refs_out):
+    ids_ref, latents_hbm, gain_ref, out_weight_ref = refs_in[:4]
+    rest, weight_refs = list(refs_in[4 : 4 + pieces]), refs_in[4 + pieces : 4 + pieces + parts]
+    begun_hbm = rest.pop(0) if chunks > 1 else None
     stepped_ref, features_ref = refs_out[:2]
-    out_vmem, weight_vmem, rows_ref, clean_ref, embedded_ref, out_sems, sems = refs_out[2:]
+    out_vmem, weight_vmem, rows_ref, clean_ref, embedded_ref = refs_out[2:7]
+    latents_ref, begun_ref, out_sems, sems, first_sems = refs_out[7:]
     dom, group, seq = ids_ref[0], ids_ref[1], ids_ref[2]
     sigma = ids_ref[3].astype(jnp.float32) * (1.0 / STEPS)
     particles, tokens, model_width = latents_ref.shape
@@ -210,7 +219,26 @@
     shards, depth, columns = weight_refs[0].shape
 
     wanted = list(range(chunks - len(rest), chunks))
+    block = column_block(model_width)
+    first_copies = []
+    for index in range(model_width // block):
+        cols = slice(index * block, (index + 1) * block)
+        first_copies.append(
+            pltpu.make_async_copy(
+                latents_hbm.at[:, :, cols], latents_ref.at[:, :, cols], first_sems.at[0, index]
+            )
+        )
+        if chunks > 1:
+            first_copies.append(
+                pltpu.make_async_copy(
+                    begun_hbm.at[:, cols], begun_ref.at[:, cols], first_sems.at[1, index]
+                )
+            )
+    for copy in first_copies[: len(first_copies) // (model_width // block)]:
+        copy.start()
     out_weights = ProjectionWeights(out_weight_ref, out_vmem, out_sems, chunks, wanted, width)
+    for copy in first_copies[len(first_copies) // (model_width // block) :]:
+        copy.start()
     copies = []
     for index in range(parts):
         for shard in range(shards):
@@ -226,6 +254,9 @@
     gather_rows(rest, rows_ref, particles)
     for index in range(model_width // out_weights.block):
         cols = out_weights.wait(index)
+        each = len(first_copies) // (model_width // block)
+        for copy in first_copies[index * each : (index + 1) * each]:
+            copy.wait()
         flat = latents_ref[:, :, cols].reshape(rows, out_weights.block).astype(jnp.float32)
         begun = begun_ref[:, cols] if chunks > 1 else flat
         velocity = begun + jnp.dot(
@@ -264,7 +295,18 @@
 
 
 def project_embed(
-    ids, offsets, latents, begun, attended, chunks, width, out_weight, weights, gain, depth_parts
+    ids,
+    offsets,
+    latents,
+    begun,
+    attended,
+    chunks,
+    width,
+    out_weight,
+    weights,
+    gain,
+    depth_parts,
+    after,
 ):
     particles, tokens, model_width = latents.shape
     rows = particles * tokens
@@ -276,14 +318,28 @@
     vmem = pl.BlockSpec(memory_space=pltpu.VMEM)
     smem = pl.BlockSpec(memory_space=pltpu.SMEM)
     hbm = pl.BlockSpec(memory_space=pltpu.HBM)
-    inputs = 4 + len(pieces) + parts
+    inputs = 4 + len(pieces) + parts + len(after)
+    groups = model_width // column_block(model_width)
 
     def kernel(*refs):
-        project_kernel(chunks, width, parts, offsets, depth_parts, refs[:inputs], refs[inputs:])
+        project_kernel(
+            chunks,
+            width,
+            len(pieces),
+            parts,
+            offsets,
+            depth_parts,
+            refs[:inputs],
+            refs[inputs:],
+        )
 
     return pl.pallas_call(
         kernel,
-        in_specs=[smem, vmem, vmem, hbm] + [vmem] * len(pieces) + [hbm] * parts,
+        in_specs=[smem, hbm, vmem, hbm]
+        + ([] if begun is None else [hbm])
+        + [vmem] * len(attended)
+        + [hbm] * parts
+        + [pl.BlockSpec(memory_space=pl.ANY)] * len(after),
         out_specs=[vmem, vmem],
         out_shape=[
             jax.ShapeDtypeStruct(latents.shape, jnp.bfloat16),
@@ -295,24 +351,25 @@
             pltpu.VMEM((rows, out_depth), jnp.bfloat16),
             pltpu.VMEM((rows, model_width), jnp.bfloat16),
             pltpu.VMEM((parts, rows, columns), jnp.float32),
-            pltpu.SemaphoreType.DMA(
-                (max(1, model_width // 512), model_width // width * len(attended))
-            ),
+            pltpu.VMEM(latents.shape, latents.dtype),
+            pltpu.VMEM((rows, model_width), jnp.float32),
+            pltpu.SemaphoreType.DMA((groups, model_width // width * len(attended))),
             pltpu.SemaphoreType.DMA((parts,)),
+            pltpu.SemaphoreType.DMA((2, groups)),
         ],
-        compiler_params=pltpu.CompilerParams(vmem_limit_bytes=28 * MIB),
+        compiler_params=pltpu.CompilerParams(vmem_limit_bytes=60 * MIB),
         cost_estimate=pl.CostEstimate(
             flops=2 * rows * model_width * (out_depth + count),
             bytes_accessed=2 * model_width * (out_depth + count) + 12 * rows * model_width,
             transcendentals=rows * count,
         ),
         name="project_embed",
-    )(ids, latents, gain.reshape(1, count), out_weight, *pieces, *weights)
-
-
-def reward_kernel(particles, scale, parts, doms, offsets, *refs):
+    )(ids, latents, gain.reshape(1, count), out_weight, *pieces, *weights, *after)
+
+
+def reward_kernel(particles, scale, parts, doms, offsets, joined, *refs):
     ids_ref, features_ref, head_ref, before_ref = refs[:4]
-    weight_refs, (out_ref, weight_vmem, sems) = refs[4:-3], refs[-3:]
+    weight_refs, (out_ref, weight_vmem, rows_ref, sems) = refs[4:-4], refs[-4:]
     dom, group, seq = ids_ref[0], ids_ref[1], ids_ref[2]
     shards, depth, columns = weight_refs[0].shape
     rows = features_ref.shape[1]
@@ -321,26 +378,35 @@
     copies = []
     for place in range(count):
         pair, shard = divmod(place, shards)
+        lane = place % joined * columns
         for index in range(parts):
             copy = pltpu.make_async_copy(
                 weight_refs[pair * parts + index].at[shard],
-                weight_vmem.at[place, index],
+                weight_vmem.at[
+                    place // joined,
+                    index * depth : (index + 1) * depth,
+                    lane : lane + columns,
+                ],
                 sems.at[place, index],
             )
             copy.start()
             copies.append(copy)
-    pieces = [features_ref[(group + parts - index) % parts] for index in range(parts)]
-    total = jnp.zeros((rows, columns), jnp.float32)
-    for place in range(count):
-        for copy in copies[place * parts : (place + 1) * parts]:
+    for index in range(parts):
+        rows_ref[:, index * depth : (index + 1) * depth] = features_ref[
+            (group + parts - index) % parts
+        ]
+    totals = jnp.zeros((particles, joined * columns), jnp.float32)
+    for step in range(count // joined):
+        for copy in copies[step * joined * parts : (step + 1) * joined * parts]:
             copy.wait()
-        hidden = sum(
-            jnp.dot(pieces[index], weight_vmem[place, index], preferred_element_type=jnp.float32)
-            for index in range(parts)
+        hidden = jnp.dot(rows_ref[...], weight_vmem[step], preferred_element_type=jnp.float32)
+        places = range(step * joined, (step + 1) * joined)
+        head = jnp.concatenate(
+            [head_ref[(seq ^ offsets[place]) * doms + dom] for place in places], axis=1
         )
-        total += jax.nn.gelu(hidden) * head_ref[(seq ^ offsets[place]) * doms + dom]
-
-    totals = jnp.sum(total.reshape(particles, rows // particles, columns), axis=1)
+        scored = jax.nn.gelu(hidden) * head
+        totals += jnp.sum(scored.reshape(particles, rows // particles, -1), axis=1)
+
     sums = jnp.sum(totals, axis=1, keepdims=True) * scale
     first = len(before_ref.shape) == 1
     shape = out_ref.shape
@@ -361,16 +427,18 @@
     shards, depth, columns = weights[0].shape
     rows = features.shape[1]
     count = shards * len(weights) // parts
+    joined = 2 if columns % LANES == 0 and count % 2 == 0 else 1
     smem = pl.BlockSpec(memory_space=pltpu.SMEM)
     vmem = pl.BlockSpec(memory_space=pltpu.VMEM)
     return pl.pallas_call(
-        functools.partial(reward_kernel, particles, scale, parts, doms, offsets),
+        functools.partial(reward_kernel, particles, scale, parts, doms, offsets, joined),
         in_specs=[smem, vmem, vmem, smem if before.ndim == 1 else vmem]
         + [pl.BlockSpec(memory_space=pltpu.HBM)] * len(weights),
         out_specs=vmem,
         out_shape=jax.ShapeDtypeStruct((8, LANES), jnp.float32),
         scratch_shapes=[
-            pltpu.VMEM((count, parts, depth, columns), jnp.bfloat16),
+            pltpu.VMEM((count // joined, parts * depth, joined * columns), jnp.bfloat16),
+            pltpu.VMEM((rows, parts * depth), jnp.bfloat16),
             pltpu.SemaphoreType.DMA((count, parts)),
         ],
         compiler_params=pltpu.CompilerParams(vmem_limit_bytes=20 * MIB),
@@ -516,14 +584,14 @@
         embed_share = jnp.concatenate([embed_share, swapped(embed_share, "seq", bit)])
         near = near + [offset ^ bit for offset in near]
     far = [offset ^ bits[-1] for offset in near]
-    embed_share, packed[0] = gate([embed_share, packed[0]], [])
+    packed[0], embed_share = gate([packed[0]], [embed_share], [])
 
     arrived = [exchange(packed[0])]
     for bit in bits[:-1]:
         up_share = jnp.concatenate([up_share, swapped(up_share, "seq", bit)])
     for bit in (bits[-1], 1):
         embed_share = jnp.concatenate([embed_share, swapped(embed_share, "seq", bit)])
-    embed_share, up_near, *packed[1:] = gate([embed_share, up_share, *packed[1:]], arrived[:1])
+    *packed[1:], embed_share, up_near = gate(packed[1:], [embed_share, up_share], arrived[:1])
 
     arrived += [exchange(piece) for piece in packed[1:]]
     up_far = swapped(up_near, "seq", bits[-1])
@@ -531,8 +599,8 @@
     near_groups = [up_near] + [shifted(up_near, "groups", k) for k in range(1, group_count)]
     embed_near = [embed_share] + [shifted(embed_share, "groups", k) for k in range(1, group_count)]
     attended = [attention(arrived[0], head_width)]
-    up_far, near_pair, attended[0], *embed_near = gate(
-        [up_far, near_pair, attended[0], *embed_near], arrived[1:]
+    attended[0], up_far, near_pair, *embed_near = gate(
+        attended, [up_far, near_pair, *embed_near], arrived[1:]
     )
 
     returned = [exchange(attended[0])]
@@ -542,10 +610,10 @@
         shifted(piece, "dom", k) for k in range(1, dom_count) for piece in embed_near
     ]
     attended += [attention(piece, head_width) for piece in arrived[1:]]
-    near_pair, far_pair, *rest = gate(
-        [near_pair, far_pair, *far_groups[1:], *attended[1:]], [returned[0], *embed_parts]
-    )
-    far_groups[1:], attended[1:] = rest[: group_count - 1], rest[group_count - 1 :]
+    *rest, near_pair, far_pair = gate(
+        attended[1:], [*far_groups[1:], near_pair, far_pair], [returned[0], *embed_parts]
+    )
+    attended[1:], far_groups[1:] = rest[: chunks - 1], rest[chunks - 1 :]
 
     returned += [exchange(piece) for piece in attended[1:]]
     pair_groups = [near_pair] + [shifted(near_pair, "groups", k) for k in range(1, group_count)]
@@ -567,6 +635,7 @@
         embed_parts,
         norm_gain,
         group_count,
+        pair_groups[1:] + far_pairs,
     )
     stepped_other = shifted(stepped, "dom", 1)
     features_other = shifted(features, "dom", 1)

time: 203 us -> 198 us (0.975)
  local copies, waits for them, and re-layouts: 25 us -> 14.4 us
  Pallas kernels: 35.8 us -> 40.7 us
    unnamed x58, local copies, waits for them, and re-layouts: 23.9 us -> 13.4 us
    ppermute x12, waiting for transfers between devices: 63.7 us -> 69 us  [swapped(): lax.ppermute(array, axis, [(i, i ^ bit) for i in range(lax.axis_size(axis...]
    all_to_all x4, waiting for transfers between devices: 3.84 us -> 0.01 us  [exchange(): return lax.all_to_all(array, 'seq', 0, 0, tiled=True)]
    pallas_call x2, Pallas kernels: 9.59 us -> 6.79 us  [reward(): pl.pallas_call(functools.partial(reward_kernel, particles, scale, parts,...]
    pallas_call x1, Pallas kernels: 2.37 us -> 4.71 us  [first_project(): pl.pallas_call(functools.partial(first_project_kernel, chunks, width), in...]
    pallas_call x5, Pallas kernels: 6.76 us -> 8.82 us  [the longest x1 8.81 us: project_embed(): pl.pallas_call(kernel, in_specs=[smem, hbm, vmem, hbm] + ([] if begun is...]
  transfers between devices with their start and end apart: 26 -> 26, of which waited for: 10 -> 11; matrix products, arithmetic and copies ran while one was open for 0% -> 0% of each run, Pallas kernels for 14% -> 16%
where the time goes in v8:
time: 198 us; the launch traced here: 197 us
  waiting for transfers between devices  89.2 us (45%)
  starting transfers between devices  50.7 us (26%)
  Pallas kernels  40.7 us (21%)
  local copies, waits for them, and re-layouts  14.4 us (7%)
    ppermute x12, waiting for transfers between devices, swapped(): lax.ppermute(array, axis, [(i, i ^ bit) for i in range(lax.axis_size(axis...  69 us
    ppermute x12, starting transfers between devices, swapped(): lax.ppermute(array, axis, [(i, i ^ bit) for i in range(lax.axis_size(axis...  23.8 us
    ppermute x9, waiting for transfers between devices, shifted(): lax.ppermute(array, axis, [(i, (i + step) % count) for i in range(count)])  20.2 us
    all_to_all x4, starting transfers between devices, exchange(): return lax.all_to_all(array, 'seq', 0, 0, tiled=True)  19 us
    pallas_call x2, Pallas kernels, attention(): pl.pallas_call(functools.partial(attention_kernel, head_width, block_sour...  13.8 us
    unnamed x58, local copies, waits for them, and re-layouts  13.4 us
    pallas_call x1, Pallas kernels, project_embed(): pl.pallas_call(kernel, in_specs=[smem, hbm, vmem, hbm] + ([] if begun is...  8.81 us
    ppermute x9, starting transfers between devices, shifted(): lax.ppermute(array, axis, [(i, (i + step) % count) for i in range(count)])  7.91 us
  transfers between devices with their start and end apart: 26, of which 11 were waited for; matrix products, arithmetic and copies ran while one was open for 0% of the time, Pallas kernels for 16%

profile of v8, /device:TPU:0, one launch (start us, length us, event | category | flops | bytes accessed | tf_op | source)
XLA Modules:
  0.0 197.4 jit_solution(2862033112568908032)
XLA Ops:
  1.6 4.0 %collective-permute-start = (bf16[1,192,256]{2,1,0:T(8,128)(2,1)S(1)}, bf16[1,192,256]{2,1,0:T(8,128)(2,1)S(1)}, u32[]{:S(2)}, u32[]{:S(2)}) collective-permute-start(bf16[1,192,256]{2,1,0:T(8,128)(2,1)S(1)} %dynamic-slice_bitcast_fusion.1), channel_id=1, source_target_pairs={{0,4},{1,5},{2,6},{3,7},{4,0},{5,1},{6,2},{7,3},{8,12},{9,13},{10,... | collective-permute-start | bytes 294920 | tf_op jit(solution)/shard_map/ppermute | solution.py:535
  5.7 3.2 %pack_heads.1 = (bf16[8,3,64,384]{3,2,1,0:T(8,128)(2,1)}, bf16[8,3,64,384]{3,2,1,0:T(8,128)(2,1)}) custom-call(bf16[4,64,1536]{2,1,0:T(8,128)(2,1)} %q_ref.1, bf16[4,64,1536]{2,1,0:T(8,128)(2,1)} %k_ref.1, bf16[4,64,1536]{2,1,0:T(8,128)(2,1)} %v_ref.1), custom_call_target="tpu_custom_call" | custom-call | tf_op jit(solution)/shard_map/pack_heads/pallas_call | solution.py:40
  12.9 5.8 %all-to-all-start = ((bf16[8,3,64,384]{3,2,1,0:T(8,128)(2,1)}), bf16[8,3,64,384]{3,2,1,0:T(8,128)(2,1)S(1)}, u32[]{:S(2)}, u32[]{:S(2)}) async-start(bf16[8,3,64,384]{3,2,1,0:T(8,128)(2,1)} %copy-done.10), calls=%async_computation | async-start | bytes 2359296 | tf_op jit(solution)/shard_map/all_to_all | solution.py:539
  18.7 2.0 %collective-permute-start.1 = (bf16[2,192,256]{2,1,0:T(8,128)(2,1)S(1)}, bf16[2,192,256]{2,1,0:T(8,128)(2,1)S(1)}, u32[]{:S(2)}, u32[]{:S(2)}) collective-permute-start(bf16[2,192,256]{2,1,0:T(8,128)(2,1)S(1)} %get-tuple-element.25), channel_id=1, source_target_pairs={{0,2},{1,3},{2,0},{3,1},{4,6},{5,7},{6,4},{7,5},{8,10},{9,11},{10,... | collective-permute-start | bytes 589832 | tf_op jit(solution)/shard_map/ppermute | solution.py:535
  20.7 22.1 %collective-permute-done.1 = bf16[2,192,256]{2,1,0:T(8,128)(2,1)S(1)} collective-permute-done((bf16[2,192,256]{2,1,0:T(8,128)(2,1)S(1)}, bf16[2,192,256]{2,1,0:T(8,128)(2,1)S(1)}, u32[]{:S(2)}, u32[]{:S(2)}) %collective-permute-start.1) | collective-permute-done | bytes 196640 | tf_op jit(solution)/shard_map/ppermute | solution.py:535
  44.7 4.4 %collective-permute-start.3 = (bf16[1,512,256]{2,1,0:T(8,128)(2,1)S(1)}, bf16[1,512,256]{2,1,0:T(8,128)(2,1)S(1)}, u32[]{:S(2)}, u32[]{:S(2)}) collective-permute-start(bf16[1,512,256]{2,1,0:T(8,128)(2,1)S(1)} %dynamic-slice_bitcast_fusion), channel_id=1, source_target_pairs={{0,4},{1,5},{2,6},{3,7},{4,0},{5,1},{6,2},{7,3},{8,12},{9,13},{10,... | collective-permute-start | bytes 786440 | tf_op jit(solution)/shard_map/ppermute | solution.py:535
  49.1 10.7 %collective-permute-done.3 = bf16[1,512,256]{2,1,0:T(8,128)(2,1)S(1)} collective-permute-done((bf16[1,512,256]{2,1,0:T(8,128)(2,1)S(1)}, bf16[1,512,256]{2,1,0:T(8,128)(2,1)S(1)}, u32[]{:S(2)}, u32[]{:S(2)}) %collective-permute-start.3) | collective-permute-done | bytes 262176 | tf_op jit(solution)/shard_map/ppermute | solution.py:535
  60.0 1.7 copy-done.7
  62.7 4.2 %all-to-all-start.1 = ((bf16[8,3,64,384]{3,2,1,0:T(8,128)(2,1)}), bf16[8,3,64,384]{3,2,1,0:T(8,128)(2,1)}, u32[]{:S(2)}, u32[]{:S(2)}) async-start(bf16[8,3,64,384]{3,2,1,0:T(8,128)(2,1)} %copy-done.8), calls=%async_computation.1 | async-start | bytes 2359296 | tf_op jit(solution)/shard_map/all_to_all | solution.py:539
  68.5 1.8 collective-permute-start.4
  71.8 6.9 %attention.2.refs_0_ = bf16[8,64,384]{2,1,0:T(8,128)(2,1)} custom-call(bf16[8,3,64,384]{3,2,1,0:T(8,128)(2,1)} %copy-done.6), custom_call_target="tpu_custom_call" | custom-call | flops 402653184 | bytes 1572864 | tf_op jit(solution)/shard_map/attention/pallas_call | solution.py:109
  78.7 21.1 %collective-permute-done.4.refs_1_ = bf16[2,512,256]{2,1,0:T(8,128)(2,1)} collective-permute-done((bf16[2,512,256]{2,1,0:T(8,128)(2,1)S(1)}, bf16[2,512,256]{2,1,0:T(8,128)(2,1)}, u32[]{:S(2)}, u32[]{:S(2)}) %collective-permute-start.4) | collective-permute-done | bytes 524320 | tf_op jit(solution)/shard_map/ppermute | solution.py:535
  101.6 4.7 %all-to-all-start.2 = ((bf16[8,64,384]{2,1,0:T(8,128)(2,1)}), bf16[8,64,384]{2,1,0:T(8,128)(2,1)}, u32[]{:S(2)}, u32[]{:S(2)}) async-start(bf16[8,64,384]{2,1,0:T(8,128)(2,1)} %copy-done.18), calls=%async_computation.2 | async-start | bytes 786432 | tf_op jit(solution)/shard_map/all_to_all | solution.py:539
  107.7 2.0 %collective-permute-start.8 = (bf16[2,512,256]{2,1,0:T(8,128)(2,1)}, bf16[2,512,256]{2,1,0:T(8,128)(2,1)S(1)}, u32[]{:S(2)}, u32[]{:S(2)}) collective-permute-start(bf16[2,512,256]{2,1,0:T(8,128)(2,1)} %get-tuple-element.30.refs_8_), channel_id=1, source_target_pairs={{0,1},{1,0},{2,3},{3,2},{4,5},{5,4},{6,7},{7,6},{8,9},{9,8},{10,11... | collective-permute-start | bytes 1572872 | tf_op jit(solution)/shard_map/ppermute | solution.py:535
  109.8 6.9 %attention.3.refs_0_ = bf16[8,64,384]{2,1,0:T(8,128)(2,1)} custom-call(bf16[8,3,64,384]{3,2,1,0:T(8,128)(2,1)} %all-to-all-done.1.refs_5_.qkv_ref), custom_call_target="tpu_custom_call" | custom-call | flops 402653184 | bytes 1572864 | tf_op jit(solution)/shard_map/attention/pallas_call | solution.py:109
  116.7 3.1 %collective-permute-done.7.refs_1_ = bf16[2,512,256]{2,1,0:T(8,128)(2,1)S(1)} collective-permute-done((bf16[2,512,256]{2,1,0:T(8,128)(2,1)}, bf16[2,512,256]{2,1,0:T(8,128)(2,1)S(1)}, u32[]{:S(2)}, u32[]{:S(2)}) %collective-permute-start.7) | collective-permute-done | bytes 524320 | tf_op jit(solution)/shard_map/ppermute | solution.py:531
  120.6 4.1 %collective-permute-done.8.refs_3_ = bf16[2,512,256]{2,1,0:T(8,128)(2,1)S(1)} collective-permute-done((bf16[2,512,256]{2,1,0:T(8,128)(2,1)}, bf16[2,512,256]{2,1,0:T(8,128)(2,1)S(1)}, u32[]{:S(2)}, u32[]{:S(2)}) %collective-permute-start.8) | collective-permute-done | bytes 524320 | tf_op jit(solution)/shard_map/ppermute | solution.py:535
  128.4 4.3 %all-to-all-start.3 = ((bf16[8,64,384]{2,1,0:T(8,128)(2,1)}), bf16[8,64,384]{2,1,0:T(8,128)(2,1)}, u32[]{:S(2)}, u32[]{:S(2)}) async-start(bf16[8,64,384]{2,1,0:T(8,128)(2,1)} %copy-done.20), calls=%async_computation.3 | async-start | bytes 786432 | tf_op jit(solution)/shard_map/all_to_all | solution.py:539
  133.7 2.0 %collective-permute-start.12 = (bf16[2,512,256]{2,1,0:T(8,128)(2,1)}, bf16[2,512,256]{2,1,0:T(8,128)(2,1)}, u32[]{:S(2)}, u32[]{:S(2)}) collective-permute-start(bf16[2,512,256]{2,1,0:T(8,128)(2,1)} %copy-done.13), channel_id=1, source_target_pairs={{0,1},{1,0},{2,3},{3,2},{4,5},{5,4},{6,7},{7,6},{8,9},{9,8},{10,11... | collective-permute-start | bytes 1572872 | tf_op jit(solution)/shard_map/ppermute | solution.py:535
  137.0 4.7 %first_project.1.refs_4_ = f32[256,1536]{1,0:T(8,128)} custom-call(bf16[4,64,1536]{2,1,0:T(8,128)(2,1)} %refs_1_.1, bf16[1536,1536]{1,0:T(8,128)(2,1)} %refs_3_.2, bf16[8,64,384]{2,1,0:T(8,128)(2,1)} %all-to-all-done.2.piece_ref.refs_4_), custom_call_target="tpu_custom_call" | custom-call | flops 603979776 | bytes 5505024 | tf_op jit(solution)/shard_map/first_project/pallas_call | solution.py:186
  141.7 4.3 %collective-permute-done.11.refs_10_.refs_7_ = bf16[2,512,256]{2,1,0:T(8,128)(2,1)S(1)} collective-permute-done((bf16[2,512,256]{2,1,0:T(8,128)(2,1)S(1)}, bf16[2,512,256]{2,1,0:T(8,128)(2,1)S(1)}, u32[]{:S(2)}, u32[]{:S(2)}) %collective-permute-start.11) | collective-permute-done | bytes 524320 | tf_op jit(solution)/shard_map/ppermute | solution.py:531
  146.0 4.4 %collective-permute-done.12.refs_12_.refs_11_ = bf16[2,512,256]{2,1,0:T(8,128)(2,1)} collective-permute-done((bf16[2,512,256]{2,1,0:T(8,128)(2,1)}, bf16[2,512,256]{2,1,0:T(8,128)(2,1)}, u32[]{:S(2)}, u32[]{:S(2)}) %collective-permute-start.12) | collective-permute-done | bytes 524320 | tf_op jit(solution)/shard_map/ppermute | solution.py:535
  150.4 8.8 %project_embed.1 = (bf16[4,64,1536]{2,1,0:T(8,128)(2,1)}, bf16[2,256,512]{2,1,0:T(8,128)(2,1)}) custom-call(s32[4]{0:T(128)} %pad_add_fusion.refs_0_.ids_ref, bf16[4,64,1536]{2,1,0:T(8,128)(2,1)} %refs_1_.1, f32[1,1024]{1,0:T(1,128)} %bitcast.12, bf16[1536,1536]{1,0:T(8,128)(2,1)} %refs_3_.2, f32[256,1536]{1,0:T(8,128)} %first_project.1.refs_4_, ...), custom_call_target="tpu_custom_call" | custom-call | flops 1409286144 | bytes 10223616 | tf_op jit(solution)/shard_map/project_embed/pallas_call | solution.py:336
  160.9 12.8 %collective-permute-done.15.refs_5_ = bf16[2,512,256]{2,1,0:T(8,128)(2,1)S(1)} collective-permute-done((bf16[2,512,256]{2,1,0:T(8,128)(2,1)S(1)}, bf16[2,512,256]{2,1,0:T(8,128)(2,1)S(1)}, u32[]{:S(2)}, u32[]{:S(2)}) %collective-permute-start.15) | collective-permute-done | bytes 524320 | tf_op jit(solution)/shard_map/ppermute | solution.py:531
  175.8 3.4 %reward.2.refs_3_ = f32[8,128]{1,0:T(8,128)S(1)} custom-call(s32[4]{0:T(128)S(1)} %copy-done.24, bf16[2,256,512]{2,1,0:T(8,128)(2,1)S(1)} %copy-done.22, f32[16,1,256]{2,1,0:T(1,128)S(1)} %bitcast.10, f32[4]{0:T(128)S(1)} %copy-done.25, bf16[2,512,256]{2,1,0:T(8,128)(2,1)S(1)} %get-tuple-element.26.refs_4_, ...), custom_call_target="tpu_custom_call" | custom-call | flops 1073741824 | bytes 4194304 | tf_op jit(solution)/shard_map/reward/pallas_call | solution.py:433
  179.2 3.4 %reward.3.refs_0_ = f32[8,128]{1,0:T(8,128)S(1)} custom-call(s32[4]{0:T(128)S(1)} %copy-done.24, bf16[2,256,512]{2,1,0:T(8,128)(2,1)S(1)} %collective-permute-done.14.refs_1_, f32[16,1,256]{2,1,0:T(1,128)S(1)} %bitcast.11, f32[8,128]{1,0:T(8,128)S(1)} %reward.2.refs_3_, bf16[2,512,256]{2,1,0:T(8,128)(2,1)S(1)} %get-tuple-element.26.refs_4_, ...), custom_call_target="tpu_custom_call" | custom-call | flops 1073741824 | bytes 4194304 | tf_op jit(solution)/shard_map/reward/pallas_call | solution.py:433
  182.6 1.7 collective-permute-start.16
  184.4 2.2 %collective-permute-start.17 = (f32[8,128]{1,0:T(8,128)S(1)}, f32[8,128]{1,0:T(8,128)S(1)}, u32[]{:S(2)}, u32[]{:S(2)}) collective-permute-start(f32[8,128]{1,0:T(8,128)S(1)} %reward.3.refs_0_), channel_id=1, source_target_pairs={{0,4},{1,5},{2,6},{3,7},{4,0},{5,1},{6,2},{7,3},{8,12},{9,13},{10,... | collective-permute-start | bytes 12296 | tf_op jit(solution)/shard_map/ppermute | solution.py:535
  187.1 1.8 collective-permute-done.17.refs_2_
  188.9 3.1 %collective-permute-done.18.refs_3_ = f32[8,128]{1,0:T(8,128)S(1)} collective-permute-done((f32[8,128]{1,0:T(8,128)S(1)}, f32[8,128]{1,0:T(8,128)S(1)}, u32[]{:S(2)}, u32[]{:S(2)}) %collective-permute-start.18) | collective-permute-done | bytes 4128 | tf_op jit(solution)/shard_map/ppermute | solution.py:535
  192.4 1.7 collective-permute-start.21
  194.1 2.0 %resample.1.resampled_ref = bf16[4,64,1536]{2,1,0:T(8,128)(2,1)} custom-call(s32[4]{0:T(128)S(1)} %copy-done.24, s32[4]{0:T(128)S(1)} %copy-done.26, bf16[4,64,1536]{2,1,0:T(8,128)(2,1)S(1)} %copy-done.21, bf16[4,64,1536]{2,1,0:T(8,128)(2,1)S(1)} %collective-permute-done.13.other_ref), custom_call_target="tpu_custom_call" | custom-call | tf_op jit(solution)/shard_map/resample/pallas_call | solution.py:515
  (99 shorter events, 26.2 us)
Async XLA Ops:
  0.6 44.0 %copy-start = (bf16[1024,512]{1,0:T(8,128)(2,1)S(1)}, bf16[1024,512]{1,0:T(8,128)(2,1)}, u32[]{:S(2)}) copy-start(bf16[1024,512]{1,0:T(8,128)(2,1)} %param.20) | copy-start | bytes 3145732
  1.6 8.9 %collective-permute-start = (bf16[1,192,256]{2,1,0:T(8,128)(2,1)S(1)}, bf16[1,192,256]{2,1,0:T(8,128)(2,1)S(1)}, u32[]{:S(2)}, u32[]{:S(2)}) collective-permute-start(bf16[1,192,256]{2,1,0:T(8,128)(2,1)S(1)} %dynamic-slice_bitcast_fusion.1), channel_id=1, source_target_pairs={{0,4},{1,5},{2,6},{3,7},{4,0},{5,1},{6,2},{7,3},{8,12},{9,13},{10,... | collective-permute-start | bytes 294920 | tf_op jit(solution)/shard_map/ppermute | solution.py:535
  12.9 29.9 %copy-start.15 = (bf16[2,192,256]{2,1,0:T(8,128)(2,1)}, bf16[2,192,256]{2,1,0:T(8,128)(2,1)S(1)}, u32[]{:S(2)}) copy-start(bf16[2,192,256]{2,1,0:T(8,128)(2,1)S(1)} %get-tuple-element.25) | copy-start | bytes 589828
  12.9 47.0 %all-to-all-start = ((bf16[8,3,64,384]{3,2,1,0:T(8,128)(2,1)}), bf16[8,3,64,384]{3,2,1,0:T(8,128)(2,1)S(1)}, u32[]{:S(2)}, u32[]{:S(2)}) async-start(bf16[8,3,64,384]{3,2,1,0:T(8,128)(2,1)} %copy-done.10), calls=%async_computation | async-start | bytes 2359296 | tf_op jit(solution)/shard_map/all_to_all | solution.py:539
  18.7 24.2 %collective-permute-start.1 = (bf16[2,192,256]{2,1,0:T(8,128)(2,1)S(1)}, bf16[2,192,256]{2,1,0:T(8,128)(2,1)S(1)}, u32[]{:S(2)}, u32[]{:S(2)}) collective-permute-start(bf16[2,192,256]{2,1,0:T(8,128)(2,1)S(1)} %get-tuple-element.25), channel_id=1, source_target_pairs={{0,2},{1,3},{2,0},{3,1},{4,6},{5,7},{6,4},{7,5},{8,10},{9,11},{10,... | collective-permute-start | bytes 589832 | tf_op jit(solution)/shard_map/ppermute | solution.py:535
  43.5 16.3 %collective-permute-start.2 = (bf16[4,192,256]{2,1,0:T(8,128)(2,1)S(1)}, bf16[4,192,256]{2,1,0:T(8,128)(2,1)S(1)}, u32[]{:S(2)}, u32[]{:S(2)}) collective-permute-start(bf16[4,192,256]{2,1,0:T(8,128)(2,1)S(1)} %pad_maximum_fusion.2), channel_id=1, source_target_pairs={{0,1},{1,0},{2,3},{3,2},{4,5},{5,4},{6,7},{7,6},{8,9},{9,8},{10,11... | collective-permute-start | bytes 1179656 | tf_op jit(solution)/shard_map/ppermute | solution.py:535
  44.7 15.1 %collective-permute-start.3 = (bf16[1,512,256]{2,1,0:T(8,128)(2,1)S(1)}, bf16[1,512,256]{2,1,0:T(8,128)(2,1)S(1)}, u32[]{:S(2)}, u32[]{:S(2)}) collective-permute-start(bf16[1,512,256]{2,1,0:T(8,128)(2,1)S(1)} %dynamic-slice_bitcast_fusion), channel_id=1, source_target_pairs={{0,4},{1,5},{2,6},{3,7},{4,0},{5,1},{6,2},{7,3},{8,12},{9,13},{10,... | collective-permute-start | bytes 786440 | tf_op jit(solution)/shard_map/ppermute | solution.py:535
  62.7 37.1 %all-to-all-start.1 = ((bf16[8,3,64,384]{3,2,1,0:T(8,128)(2,1)}), bf16[8,3,64,384]{3,2,1,0:T(8,128)(2,1)}, u32[]{:S(2)}, u32[]{:S(2)}) async-start(bf16[8,3,64,384]{3,2,1,0:T(8,128)(2,1)} %copy-done.8), calls=%async_computation.1 | async-start | bytes 2359296 | tf_op jit(solution)/shard_map/all_to_all | solution.py:539
  67.0 32.9 %collective-permute-start.6 = (bf16[8,192,256]{2,1,0:T(8,128)(2,1)S(1)}, bf16[8,192,256]{2,1,0:T(8,128)(2,1)}, u32[]{:S(2)}, u32[]{:S(2)}) collective-permute-start(bf16[8,192,256]{2,1,0:T(8,128)(2,1)S(1)} %get-tuple-element.27.refs_3_), channel_id=1, source_target_pairs={{0,16},{16,0},{1,17},{17,1},{2,18},{18,2},{3,19},{19,3},{4,20},{20... | collective-permute-start | bytes 2359304 | tf_op jit(solution)/shard_map/ppermute | solution.py:531
  68.5 31.3 %collective-permute-start.4 = (bf16[2,512,256]{2,1,0:T(8,128)(2,1)S(1)}, bf16[2,512,256]{2,1,0:T(8,128)(2,1)}, u32[]{:S(2)}, u32[]{:S(2)}) collective-permute-start(bf16[2,512,256]{2,1,0:T(8,128)(2,1)S(1)} %get-tuple-element.26.refs_4_), channel_id=1, source_target_pairs={{0,2},{1,3},{2,0},{3,1},{4,6},{5,7},{6,4},{7,5},{8,10},{9,11},{10,... | collective-permute-start | bytes 1572872 | tf_op jit(solution)/shard_map/ppermute | solution.py:535
  70.3 29.5 %collective-permute-start.5 = (bf16[2,512,256]{2,1,0:T(8,128)(2,1)S(1)}, bf16[2,512,256]{2,1,0:T(8,128)(2,1)S(1)}, u32[]{:S(2)}, u32[]{:S(2)}) collective-permute-start(bf16[2,512,256]{2,1,0:T(8,128)(2,1)S(1)} %get-tuple-element.26.refs_4_), channel_id=1, source_target_pairs={{0,1},{1,0},{2,3},{3,2},{4,5},{5,4},{6,7},{7,6},{8,9},{9,8},{10,11... | collective-permute-start | bytes 1572872 | tf_op jit(solution)/shard_map/ppermute | solution.py:535
  100.8 24.0 %copy-start.1 = (bf16[8,192,256]{2,1,0:T(8,128)(2,1)}, bf16[8,192,256]{2,1,0:T(8,128)(2,1)S(1)}, u32[]{:S(2)}) copy-start(bf16[8,192,256]{2,1,0:T(8,128)(2,1)S(1)} %get-tuple-element.32.refs_5_.refs_6_) | copy-start | bytes 2359300
  100.8 24.0 %collective-permute-start.10 = (bf16[8,192,256]{2,1,0:T(8,128)(2,1)}, bf16[8,192,256]{2,1,0:T(8,128)(2,1)}, u32[]{:S(2)}, u32[]{:S(2)}) collective-permute-start(bf16[8,192,256]{2,1,0:T(8,128)(2,1)} %get-tuple-element.33.refs_6_.refs_7_), channel_id=1, source_target_pairs={{0,8},{8,0},{1,9},{9,1},{2,10},{10,2},{3,11},{11,3},{4,12},{12,4},... | collective-permute-start | bytes 2359304 | tf_op jit(solution)/shard_map/ppermute | solution.py:531
  100.8 23.9 %collective-permute-start.9 = (bf16[8,192,256]{2,1,0:T(8,128)(2,1)S(1)}, bf16[8,192,256]{2,1,0:T(8,128)(2,1)}, u32[]{:S(2)}, u32[]{:S(2)}) collective-permute-start(bf16[8,192,256]{2,1,0:T(8,128)(2,1)S(1)} %get-tuple-element.32.refs_5_.refs_6_), channel_id=1, source_target_pairs={{0,8},{8,0},{1,9},{9,1},{2,10},{10,2},{3,11},{11,3},{4,12},{12,4},... | collective-permute-start | bytes 2359304 | tf_op jit(solution)/shard_map/ppermute | solution.py:531
  101.6 23.2 %all-to-all-start.2 = ((bf16[8,64,384]{2,1,0:T(8,128)(2,1)}), bf16[8,64,384]{2,1,0:T(8,128)(2,1)}, u32[]{:S(2)}, u32[]{:S(2)}) async-start(bf16[8,64,384]{2,1,0:T(8,128)(2,1)} %copy-done.18), calls=%async_computation.2 | async-start | bytes 786432 | tf_op jit(solution)/shard_map/all_to_all | solution.py:539
  106.2 13.6 %collective-permute-start.7 = (bf16[2,512,256]{2,1,0:T(8,128)(2,1)}, bf16[2,512,256]{2,1,0:T(8,128)(2,1)S(1)}, u32[]{:S(2)}, u32[]{:S(2)}) collective-permute-start(bf16[2,512,256]{2,1,0:T(8,128)(2,1)} %get-tuple-element.30.refs_8_), channel_id=1, source_target_pairs={{0,16},{16,0},{1,17},{17,1},{2,18},{18,2},{3,19},{19,3},{4,20},{20... | collective-permute-start | bytes 1572872 | tf_op jit(solution)/shard_map/ppermute | solution.py:531
  107.7 17.0 %collective-permute-start.8 = (bf16[2,512,256]{2,1,0:T(8,128)(2,1)}, bf16[2,512,256]{2,1,0:T(8,128)(2,1)S(1)}, u32[]{:S(2)}, u32[]{:S(2)}) collective-permute-start(bf16[2,512,256]{2,1,0:T(8,128)(2,1)} %get-tuple-element.30.refs_8_), channel_id=1, source_target_pairs={{0,1},{1,0},{2,3},{3,2},{4,5},{5,4},{6,7},{7,6},{8,9},{9,8},{10,11... | collective-permute-start | bytes 1572872 | tf_op jit(solution)/shard_map/ppermute | solution.py:535
  128.4 22.0 %all-to-all-start.3 = ((bf16[8,64,384]{2,1,0:T(8,128)(2,1)}), bf16[8,64,384]{2,1,0:T(8,128)(2,1)}, u32[]{:S(2)}, u32[]{:S(2)}) async-start(bf16[8,64,384]{2,1,0:T(8,128)(2,1)} %copy-done.20), calls=%async_computation.3 | async-start | bytes 786432 | tf_op jit(solution)/shard_map/all_to_all | solution.py:539
  132.7 13.3 %collective-permute-start.11 = (bf16[2,512,256]{2,1,0:T(8,128)(2,1)S(1)}, bf16[2,512,256]{2,1,0:T(8,128)(2,1)S(1)}, u32[]{:S(2)}, u32[]{:S(2)}) collective-permute-start(bf16[2,512,256]{2,1,0:T(8,128)(2,1)S(1)} %get-tuple-element.35.refs_6_), channel_id=1, source_target_pairs={{0,16},{16,0},{1,17},{17,1},{2,18},{18,2},{3,19},{19,3},{4,20},{20... | collective-permute-start | bytes 1572872 | tf_op jit(solution)/shard_map/ppermute | solution.py:531
  133.7 16.7 %collective-permute-start.12 = (bf16[2,512,256]{2,1,0:T(8,128)(2,1)}, bf16[2,512,256]{2,1,0:T(8,128)(2,1)}, u32[]{:S(2)}, u32[]{:S(2)}) collective-permute-start(bf16[2,512,256]{2,1,0:T(8,128)(2,1)} %copy-done.13), channel_id=1, source_target_pairs={{0,1},{1,0},{2,3},{3,2},{4,5},{5,4},{6,7},{7,6},{8,9},{9,8},{10,11... | collective-permute-start | bytes 1572872 | tf_op jit(solution)/shard_map/ppermute | solution.py:535
  150.4 23.3 %copy-start.3 = (bf16[2,512,256]{2,1,0:T(8,128)(2,1)S(1)}, bf16[2,512,256]{2,1,0:T(8,128)(2,1)}, u32[]{:S(2)}) copy-start(bf16[2,512,256]{2,1,0:T(8,128)(2,1)} %copy-done.2) | copy-start | bytes 1572868
  150.4 23.3 %copy-start.14 = (bf16[2,512,256]{2,1,0:T(8,128)(2,1)S(1)}, bf16[2,512,256]{2,1,0:T(8,128)(2,1)}, u32[]{:S(2)}) copy-start(bf16[2,512,256]{2,1,0:T(8,128)(2,1)} %copy-done.13) | copy-start | bytes 1572868
  150.4 23.3 %copy-start.23 = (f32[4096]{0:T(1024)S(1)}, f32[4096]{0:T(1024)}, u32[]{:S(2)}) copy-start(f32[4096]{0:T(1024)} %param.21) | copy-start | bytes 49156
  159.3 34.9 %collective-permute-start.13 = (bf16[4,64,1536]{2,1,0:T(8,128)(2,1)}, bf16[4,64,1536]{2,1,0:T(8,128)(2,1)S(1)}, u32[]{:S(2)}, u32[]{:S(2)}) collective-permute-start(bf16[4,64,1536]{2,1,0:T(8,128)(2,1)} %get-tuple-element.38.own_ref), channel_id=1, source_target_pairs={{0,8},{8,0},{1,9},{9,1},{2,10},{10,2},{3,11},{11,3},{4,12},{12,4},... | collective-permute-start | bytes 2359304 | tf_op jit(solution)/shard_map/ppermute | solution.py:531
  159.3 14.3 %collective-permute-start.15 = (bf16[2,512,256]{2,1,0:T(8,128)(2,1)S(1)}, bf16[2,512,256]{2,1,0:T(8,128)(2,1)S(1)}, u32[]{:S(2)}, u32[]{:S(2)}) collective-permute-start(bf16[2,512,256]{2,1,0:T(8,128)(2,1)S(1)} %get-tuple-element.26.refs_4_), channel_id=1, source_target_pairs={{0,16},{16,0},{1,17},{17,1},{2,18},{18,2},{3,19},{19,3},{4,20},{20... | collective-permute-start | bytes 1572872 | tf_op jit(solution)/shard_map/ppermute | solution.py:531
  160.8 18.5 %collective-permute-start.14 = (bf16[2,256,512]{2,1,0:T(8,128)(2,1)}, bf16[2,256,512]{2,1,0:T(8,128)(2,1)S(1)}, u32[]{:S(2)}, u32[]{:S(2)}) collective-permute-start(bf16[2,256,512]{2,1,0:T(8,128)(2,1)} %get-tuple-element.39.refs_1_), channel_id=1, source_target_pairs={{0,8},{8,0},{1,9},{9,1},{2,10},{10,2},{3,11},{11,3},{4,12},{12,4},... | collective-permute-start | bytes 1572872 | tf_op jit(solution)/shard_map/ppermute | solution.py:531
  182.6 4.5 %collective-permute-start.16 = (f32[8,128]{1,0:T(8,128)S(1)}, f32[8,128]{1,0:T(8,128)S(1)}, u32[]{:S(2)}, u32[]{:S(2)}) collective-permute-start(f32[8,128]{1,0:T(8,128)S(1)} %reward.3.refs_0_), channel_id=1, source_target_pairs={{0,2},{1,3},{2,0},{3,1},{4,6},{5,7},{6,4},{7,5},{8,10},{9,11},{10,... | collective-permute-start | bytes 12296 | tf_op jit(solution)/shard_map/ppermute | solution.py:535
  184.4 4.5 %collective-permute-start.17 = (f32[8,128]{1,0:T(8,128)S(1)}, f32[8,128]{1,0:T(8,128)S(1)}, u32[]{:S(2)}, u32[]{:S(2)}) collective-permute-start(f32[8,128]{1,0:T(8,128)S(1)} %reward.3.refs_0_), channel_id=1, source_target_pairs={{0,4},{1,5},{2,6},{3,7},{4,0},{5,1},{6,2},{7,3},{8,12},{9,13},{10,... | collective-permute-start | bytes 12296 | tf_op jit(solution)/shard_map/ppermute | solution.py:535
  186.6 5.4 %collective-permute-start.18 = (f32[8,128]{1,0:T(8,128)S(1)}, f32[8,128]{1,0:T(8,128)S(1)}, u32[]{:S(2)}, u32[]{:S(2)}) collective-permute-start(f32[8,128]{1,0:T(8,128)S(1)} %reward.3.refs_0_), channel_id=1, source_target_pairs={{0,6},{1,7},{2,4},{3,5},{4,2},{5,3},{6,0},{7,1},{8,14},{9,15},{10,... | collective-permute-start | bytes 12296 | tf_op jit(solution)/shard_map/ppermute | solution.py:535
  192.0 4.2 %collective-permute-start.19 = (f32[8,128]{1,0:T(8,128)S(1)}, f32[8,128]{1,0:T(8,128)S(1)}, u32[]{:S(2)}, u32[]{:S(2)}) collective-permute-start(f32[8,128]{1,0:T(8,128)S(1)} %add_partials.1.refs_0_), channel_id=1, source_target_pairs={{0,1},{1,0},{2,3},{3,2},{4,5},{5,4},{6,7},{7,6},{8,9},{9,8},{10,11... | collective-permute-start | bytes 12296 | tf_op jit(solution)/shard_map/ppermute | solution.py:535
  192.4 3.8 %collective-permute-start.20 = (f32[8,128]{1,0:T(8,128)S(1)}, f32[8,128]{1,0:T(8,128)S(1)}, u32[]{:S(2)}, u32[]{:S(2)}) collective-permute-start(f32[8,128]{1,0:T(8,128)S(1)} %add_partials.1.refs_0_), channel_id=1, source_target_pairs={{0,9},{1,8},{2,11},{3,10},{4,13},{5,12},{6,15},{7,14},{8,1},{9,0},... | collective-permute-start | bytes 12296 | tf_op jit(solution)/shard_map/ppermute | solution.py:667
  192.4 3.8 %collective-permute-start.21 = (f32[8,128]{1,0:T(8,128)S(1)}, f32[8,128]{1,0:T(8,128)S(1)}, u32[]{:S(2)}, u32[]{:S(2)}) collective-permute-start(f32[8,128]{1,0:T(8,128)S(1)} %add_partials.1.refs_0_), channel_id=1, source_target_pairs={{0,8},{8,0},{1,9},{9,1},{2,10},{10,2},{3,11},{11,3},{4,12},{12,4},... | collective-permute-start | bytes 12296 | tf_op jit(solution)/shard_map/ppermute | solution.py:531
  (23 other events, 141.2 us)

commit v9 on v8

--- a/solution.py
+++ b/solution.py
@@ -17,60 +17,71 @@
 MIB = 1024 * 1024
 
 
-def pack_kernel(chunks, width, q_ref, k_ref, v_ref, *out_refs):
-    particles, _, model_width = q_ref.shape
+def pack_kernel(q_ref, k_ref, v_ref, *refs):
+    for index, ref in enumerate((q_ref, k_ref, v_ref)):
+        refs[-1][:, 0, index] = ref[...]
+
+
+def pack_whole_kernel(width, q_ref, k_ref, v_ref, *refs):
+    out_ref = refs[-1]
+    for index, ref in enumerate((q_ref, k_ref, v_ref)):
+        for block in range(out_ref.shape[1]):
+            out_ref[:, block, index] = ref[:, :, block * width : (block + 1) * width]
+
+
+def pack(queries, keys, values, chunks, width, chunk, after):
+    particles, tokens, model_width = queries.shape
     blocks = model_width // width
     part = width // chunks
-    for index, ref in enumerate((q_ref, k_ref, v_ref)):
-        for particle in range(particles):
-            for block in range(blocks):
-                for chunk in range(chunks):
-                    start = block * width + chunk * part
-                    out_refs[chunk][particle * blocks + block, index] = ref[
-                        particle, :, start : start + part
-                    ]
-
-
-def pack(queries, keys, values, chunks, width):
-    particles, tokens, model_width = queries.shape
-    count = particles * model_width // width
-    vmem = pl.BlockSpec(memory_space=pltpu.VMEM)
-    shape = jax.ShapeDtypeStruct((count, 3, tokens, width // chunks), queries.dtype)
-    return list(
-        pl.pallas_call(
-            functools.partial(pack_kernel, chunks, width),
-            in_specs=[vmem] * 3,
-            out_specs=[vmem] * chunks,
-            out_shape=[shape] * chunks,
-            compiler_params=pltpu.CompilerParams(vmem_limit_bytes=60 * MIB),
+    out_shape = jax.ShapeDtypeStruct((particles, blocks, 3, tokens, part), queries.dtype)
+    params = pltpu.CompilerParams(vmem_limit_bytes=60 * MIB)
+    unread = [pl.BlockSpec(memory_space=pl.ANY)] * len(after)
+    if part % LANES == 0:
+        in_spec = pl.BlockSpec((particles, tokens, part), lambda i: (0, 0, i * chunks + chunk))
+        packed = pl.pallas_call(
+            pack_kernel,
+            grid=(blocks,),
+            in_specs=[in_spec] * 3 + unread,
+            out_specs=pl.BlockSpec((particles, 1, 3, tokens, part), lambda i: (0, i, 0, 0, 0)),
+            out_shape=out_shape,
+            compiler_params=params,
             name="pack_heads",
-        )(queries, keys, values)
-    )
+        )(queries, keys, values, *after)
+    else:
+        vmem = pl.BlockSpec(memory_space=pltpu.VMEM)
+        packed = pl.pallas_call(
+            functools.partial(pack_whole_kernel, width),
+            in_specs=[vmem] * 3 + unread,
+            out_specs=vmem,
+            out_shape=out_shape,
+            compiler_params=params,
+            name="pack_heads",
+        )(queries, keys, values, *after)
+    return packed.reshape(particles * blocks, 3, tokens, part)
 
 
 def gate_kernel(*refs):
     pass
 
 
-def gate(pinned, delayed, after):
-    count = len(pinned) + len(delayed)
+def gate(delayed, after):
+    count = len(delayed)
     anywhere = pl.BlockSpec(memory_space=pl.ANY)
-    specs = [pl.BlockSpec(memory_space=pltpu.HBM)] * len(pinned) + [anywhere] * len(delayed)
-    arrays = [*pinned, *delayed]
     return list(
         pl.pallas_call(
             gate_kernel,
-            in_specs=specs + [anywhere] * len(after),
-            out_specs=specs,
-            out_shape=[jax.ShapeDtypeStruct(array.shape, array.dtype) for array in arrays],
+            in_specs=[anywhere] * (count + len(after)),
+            out_specs=[anywhere] * count,
+            out_shape=[jax.ShapeDtypeStruct(array.shape, array.dtype) for array in delayed],
             input_output_aliases={index: index for index in range(count)},
             compiler_params=pltpu.CompilerParams(vmem_limit_bytes=MIB),
             name="gate",
-        )(*arrays, *after)
+        )(*delayed, *after)
     )
 
 
-def attention_kernel(head_width, block_sources, qkv_ref, out_ref):
+def attention_kernel(head_width, block_sources, qkv_ref, *refs):
+    out_ref = refs[-1]
     sources, _, tokens, columns = qkv_ref.shape
     total = sources * tokens
     rows = block_sources * tokens
@@ -98,7 +109,7 @@
         out_ref[span] = joined.reshape(block_sources, tokens, columns)
 
 
-def attention(qkv, head_width):
+def attention(qkv, head_width, after):
     sources, _, tokens, columns = qkv.shape
     total = sources * tokens
     block_sources = max(1, min(sources, 512 // tokens))
@@ -109,17 +120,18 @@
     return pl.pallas_call(
         functools.partial(attention_kernel, head_width, block_sources),
         grid=(columns // step,),
-        in_specs=[pl.BlockSpec((sources, 3, tokens, step), lambda i: (0, 0, 0, i))],
+        in_specs=[pl.BlockSpec((sources, 3, tokens, step), lambda i: (0, 0, 0, i))]
+        + [pl.BlockSpec(memory_space=pl.ANY)] * len(after),
         out_specs=pl.BlockSpec((sources, tokens, step), lambda i: (0, 0, i)),
         out_shape=jax.ShapeDtypeStruct((sources, tokens, columns), jnp.bfloat16),
-        compiler_params=pltpu.CompilerParams(vmem_limit_bytes=60 * MIB),
+        compiler_params=pltpu.CompilerParams(vmem_limit_bytes=8 * MIB + 6 * scores_bytes),
         cost_estimate=pl.CostEstimate(
             flops=4 * total * total * columns,
             bytes_accessed=8 * total * columns,
             transcendentals=columns // head_width * total * total,
         ),
         name="attention",
-    )(qkv)
+    )(qkv, *after)
 
 
 def column_block(model_width):
@@ -166,8 +178,8 @@
             ] = ref[particle * blocks + place]
 
 
-def first_project_kernel(chunks, width, latents_ref, weight_ref, piece_ref, out_ref, *scratch):
-    weight_vmem, rows_ref, sems = scratch
+def first_project_kernel(chunks, width, latents_ref, weight_ref, piece_ref, *refs):
+    out_ref, weight_vmem, rows_ref, sems = refs[-4:]
     particles, tokens, model_width = latents_ref.shape
     weights = ProjectionWeights(weight_ref, weight_vmem, sems, chunks, [0], width)
     gather_rows([piece_ref], rows_ref, particles)
@@ -179,13 +191,14 @@
         )
 
 
-def first_project(latents, out_weight, piece, chunks, width):
+def first_project(latents, out_weight, piece, chunks, width, after):
     particles, tokens, model_width = latents.shape
     rows, depth = particles * tokens, model_width // chunks
     vmem = pl.BlockSpec(memory_space=pltpu.VMEM)
     return pl.pallas_call(
         functools.partial(first_project_kernel, chunks, width),
-        in_specs=[vmem, pl.BlockSpec(memory_space=pltpu.HBM), vmem],
+        in_specs=[vmem, pl.BlockSpec(memory_space=pltpu.HBM), vmem]
+        + [pl.BlockSpec(memory_space=pl.ANY)] * len(after),
         out_specs=vmem,
         out_shape=jax.ShapeDtypeStruct((rows, model_width), jnp.float32),
         scratch_shapes=[
@@ -202,7 +215,7 @@
             transcendentals=0,
         ),
         name="first_project",
-    )(latents, out_weight, piece)
+    )(latents, out_weight, piece, *after)
 
 
 def project_kernel(chunks, width, pieces, parts, offsets, depth_parts, refs_in, refs_out):
@@ -441,7 +454,7 @@
             pltpu.VMEM((rows, parts * depth), jnp.bfloat16),
             pltpu.SemaphoreType.DMA((count, parts)),
         ],
-        compiler_params=pltpu.CompilerParams(vmem_limit_bytes=20 * MIB),
+        compiler_params=pltpu.CompilerParams(vmem_limit_bytes=60 * MIB),
         cost_estimate=pl.CostEstimate(
             flops=2 * rows * parts * depth * count * columns,
             bytes_accessed=2 * parts * depth * count * columns,
@@ -577,52 +590,68 @@
         up_weight, (group * up_depth, dom * up_columns), (up_depth, up_columns)
     )[None]
     bits = [1 << place for place in reversed(range(1, seq_count.bit_length() - 1))]
-
-    packed = pack(queries, keys, values, chunks, width)
     near = [0]
-    for bit in bits[:-1]:
+    for bit in bits[:-2]:
         embed_share = jnp.concatenate([embed_share, swapped(embed_share, "seq", bit)])
+        up_share = jnp.concatenate([up_share, swapped(up_share, "seq", bit)])
         near = near + [offset ^ bit for offset in near]
-    far = [offset ^ bits[-1] for offset in near]
-    packed[0], embed_share = gate([packed[0]], [embed_share], [])
-
+    high, low = bits[-2:]
+
+    def over_groups(array):
+        return [array] + [shifted(array, "groups", k) for k in range(1, group_count)]
+
+    def pair_of(arrays):
+        return [swapped(array, "seq", 1) for array in arrays]
+
+    packed = [pack(queries, keys, values, chunks, width, 0, [])]
     arrived = [exchange(packed[0])]
-    for bit in bits[:-1]:
-        up_share = jnp.concatenate([up_share, swapped(up_share, "seq", bit)])
-    for bit in (bits[-1], 1):
+    embed_share = jnp.concatenate([embed_share, swapped(embed_share, "seq", high)])
+    up_high, up_low = swapped(up_share, "seq", high), swapped(up_share, "seq", low)
+    own_groups, own_pair = over_groups(up_share), swapped(up_share, "seq", 1)
+    first = [up_high, up_low, own_pair, *own_groups[1:]]
+    [embed_share] = gate([embed_share], first)
+    for bit in (low, 1):
         embed_share = jnp.concatenate([embed_share, swapped(embed_share, "seq", bit)])
-    *packed[1:], embed_share, up_near = gate(packed[1:], [embed_share, up_share], arrived[:1])
+    packed += [
+        pack(queries, keys, values, chunks, width, chunk, [embed_share, *first])
+        for chunk in range(1, chunks)
+    ]
 
     arrived += [exchange(piece) for piece in packed[1:]]
-    up_far = swapped(up_near, "seq", bits[-1])
-    near_pair = swapped(up_near, "seq", 1)
-    near_groups = [up_near] + [shifted(up_near, "groups", k) for k in range(1, group_count)]
-    embed_near = [embed_share] + [shifted(embed_share, "groups", k) for k in range(1, group_count)]
-    attended = [attention(arrived[0], head_width)]
-    attended[0], up_far, near_pair, *embed_near = gate(
-        attended, [up_far, near_pair, *embed_near], arrived[1:]
-    )
+    up_both = swapped(up_high, "seq", low)
+    embed_near = over_groups(embed_share)
+    high_groups, low_groups = over_groups(up_high), over_groups(up_low)
+    high_pair, low_pair = swapped(up_high, "seq", 1), swapped(up_low, "seq", 1)
+    own_pairs = [own_pair] + pair_of(own_groups[1:])
+    second = [up_both, high_pair, low_pair, *own_pairs[1:], *embed_near[1:]]
+    second += high_groups[1:] + low_groups[1:]
+    attended = [attention(arrived[0], head_width, [])]
+    attended += [attention(piece, head_width, second) for piece in arrived[1:]]
 
     returned = [exchange(attended[0])]
-    far_pair = swapped(up_far, "seq", 1)
-    far_groups = [up_far] + [shifted(up_far, "groups", k) for k in range(1, group_count)]
     embed_parts = embed_near + [
         shifted(piece, "dom", k) for k in range(1, dom_count) for piece in embed_near
     ]
-    attended += [attention(piece, head_width) for piece in arrived[1:]]
-    *rest, near_pair, far_pair = gate(
-        attended[1:], [*far_groups[1:], near_pair, far_pair], [returned[0], *embed_parts]
-    )
-    attended[1:], far_groups[1:] = rest[: chunks - 1], rest[chunks - 1 :]
+    both_groups, both_pair = over_groups(up_both), swapped(up_both, "seq", 1)
+    high_pairs = over_groups(high_pair)
+    third = [both_pair, *embed_parts[group_count:], *both_groups[1:], *high_pairs[1:]]
+    if chunks > 1:
+        begun = first_project(latents, out_weight, returned.pop(0), chunks, width, third)
+    else:
+        begun = None
 
     returned += [exchange(piece) for piece in attended[1:]]
-    pair_groups = [near_pair] + [shifted(near_pair, "groups", k) for k in range(1, group_count)]
-    far_pairs = [far_pair] + [swapped(piece, "seq", 1) for piece in far_groups[1:]]
-    up_parts = near_groups + pair_groups + far_groups + far_pairs
-    embed_offsets = near + far + [offset ^ 1 for offset in near + far]
-    up_offsets = near + [offset ^ 1 for offset in near] + far + [offset ^ 1 for offset in far]
-
-    begun = first_project(latents, out_weight, returned.pop(0), chunks, width) if chunks > 1 else None
+    both_pairs = over_groups(both_pair)
+    low_pairs = [low_pair] + pair_of(low_groups[1:])
+    up_parts = own_groups + own_pairs + high_groups + high_pairs
+    up_parts += low_groups + low_pairs + both_groups + both_pairs
+    up_offsets = [
+        offset ^ bit ^ pair for bit in (0, high, low, high ^ low) for pair in (0, 1) for offset in near
+    ]
+    embed_offsets = near + [offset ^ high for offset in near]
+    for bit in (low, 1):
+        embed_offsets = embed_offsets + [offset ^ bit for offset in embed_offsets]
+
     stepped, features = project_embed(
         ids,
         embed_offsets,
@@ -635,7 +664,7 @@
         embed_parts,
         norm_gain,
         group_count,
-        pair_groups[1:] + far_pairs,
+        [*both_pairs[1:], *low_pairs[1:], *third],
     )
     stepped_other = shifted(stepped, "dom", 1)
     features_other = shifted(features, "dom", 1)

time: 198 us -> 204 us (1.030)
  local copies, waits for them, and re-layouts: 14.4 us -> 10.1 us
  waiting for transfers between devices: 89.2 us -> 93 us
  starting transfers between devices: 50.7 us -> 54.1 us
  Pallas kernels: 40.7 us -> 43.1 us
    all_to_all x4, waiting for transfers between devices: 0.01 us -> 18.1 us  [exchange(): return lax.all_to_all(array, 'seq', 0, 0, tiled=True)]
    ppermute x9 -> x12, waiting for transfers between devices: 20.2 us -> 5.29 us  [shifted(): lax.ppermute(array, axis, [(i, (i + step) % count) for i in range(count)])]
    unnamed x58 -> x60, local copies, waits for them, and re-layouts: 13.4 us -> 9.22 us
    pallas_call x2, Pallas kernels: 6.79 us -> 10.8 us  [reward(): pl.pallas_call(functools.partial(reward_kernel, particles, scale, parts,...]
    all_to_all x4, starting transfers between devices: 19 us -> 21.9 us  [exchange(): return lax.all_to_all(array, 'seq', 0, 0, tiled=True)]
    pallas_call x2, Pallas kernels: 13.8 us -> 11 us  [attention(): pl.pallas_call(functools.partial(attention_kernel, head_width, block_sour...]
    ppermute x12 -> x16, starting transfers between devices: 23.8 us -> 22.1 us  [swapped(): lax.ppermute(array, axis, [(i, i ^ bit) for i in range(lax.axis_size(axis...]
    ppermute x9 -> x12, starting transfers between devices: 7.91 us -> 9.61 us  [shifted(): lax.ppermute(array, axis, [(i, (i + step) % count) for i in range(count)])]
  transfers between devices with their start and end apart: 26 -> 33, of which waited for: 11 -> 11; matrix products, arithmetic and copies ran while one was open for 0% -> 1% of each run, Pallas kernels for 16% -> 15%
where the time goes in v9:
time: 204 us
  waiting for transfers between devices  93 us (46%)
  starting transfers between devices  54.1 us (27%)
  Pallas kernels  43.1 us (21%)
  local copies, waits for them, and re-layouts  10.1 us (5%)
    ppermute x16, waiting for transfers between devices, swapped(): lax.ppermute(array, axis, [(i, i ^ bit) for i in range(lax.axis_size(axis...  69.6 us
    ppermute x16, starting transfers between devices, swapped(): lax.ppermute(array, axis, [(i, i ^ bit) for i in range(lax.axis_size(axis...  22.1 us
    all_to_all x4, starting transfers between devices, exchange(): return lax.all_to_all(array, 'seq', 0, 0, tiled=True)  21.9 us
    all_to_all x4, waiting for transfers between devices, exchange(): return lax.all_to_all(array, 'seq', 0, 0, tiled=True)  18.1 us
    pallas_call x2, Pallas kernels, attention(): pl.pallas_call(functools.partial(attention_kernel, head_width, block_sour...  11 us
    pallas_call x2, Pallas kernels, reward(): pl.pallas_call(functools.partial(reward_kernel, particles, scale, parts,...  10.8 us
    ppermute x12, starting transfers between devices, shifted(): lax.ppermute(array, axis, [(i, (i + step) % count) for i in range(count)])  9.61 us
    unnamed x60, local copies, waits for them, and re-layouts  9.22 us
  transfers between devices with their start and end apart: 33, of which 11 were waited for; matrix products, arithmetic and copies ran while one was open for 1% of the time, Pallas kernels for 15%

profile of v9, /device:TPU:0, one launch (start us, length us, event | category | flops | bytes accessed | tf_op | source)
XLA Modules:
  0.0 203.6 jit_solution(10714166509403828310)
XLA Ops:
  0.6 2.3 %pack_heads.2 = bf16[4,2,3,64,384]{4,3,2,1,0:T(8,128)(2,1)} custom-call(bf16[4,64,1536]{2,1,0:T(8,128)(2,1)} %q_ref.3, bf16[4,64,1536]{2,1,0:T(8,128)(2,1)} %k_ref.3, bf16[4,64,1536]{2,1,0:T(8,128)(2,1)} %v_ref.3), custom_call_target="tpu_custom_call" | custom-call | tf_op jit(solution)/shard_map/pack_heads/pallas_call | solution.py:41
  3.0 7.3 %all-to-all-start = ((bf16[8,3,64,384]{3,2,1,0:T(8,128)(2,1)}), bf16[8,3,64,384]{3,2,1,0:T(8,128)(2,1)S(1)}, u32[]{:S(2)}, u32[]{:S(2)}) async-start(bf16[8,3,64,384]{3,2,1,0:T(8,128)(2,1)} %bitcast.12), calls=%async_computation | async-start | bytes 2359296 | tf_op jit(solution)/shard_map/all_to_all | solution.py:552
  11.9 2.0 collective-permute-start.5
  15.3 2.4 %collective-permute-start = (bf16[1,512,256]{2,1,0:T(8,128)(2,1)S(1)}, bf16[1,512,256]{2,1,0:T(8,128)(2,1)S(1)}, u32[]{:S(2)}, u32[]{:S(2)}) collective-permute-start(bf16[1,512,256]{2,1,0:T(8,128)(2,1)S(1)} %dynamic-slice_bitcast_fusion.refs_4_), channel_id=1, source_target_pairs={{0,4},{1,5},{2,6},{3,7},{4,0},{5,1},{6,2},{7,3},{8,12},{9,13},{10,... | collective-permute-start | bytes 786440 | tf_op jit(solution)/shard_map/ppermute | solution.py:548
  19.2 35.1 %collective-permute-done.3 = bf16[1,192,256]{2,1,0:T(8,128)(2,1)S(1)} collective-permute-done((bf16[1,192,256]{2,1,0:T(8,128)(2,1)S(1)}, bf16[1,192,256]{2,1,0:T(8,128)(2,1)S(1)}, u32[]{:S(2)}, u32[]{:S(2)}) %collective-permute-start.3) | collective-permute-done | bytes 98336 | tf_op jit(solution)/shard_map/ppermute | solution.py:548
  54.5 5.7 %collective-permute-done.7 = bf16[2,192,256]{2,1,0:T(8,128)(2,1)S(1)} collective-permute-done((bf16[2,192,256]{2,1,0:T(8,128)(2,1)S(1)}, bf16[2,192,256]{2,1,0:T(8,128)(2,1)S(1)}, u32[]{:S(2)}, u32[]{:S(2)}) %collective-permute-start.7) | collective-permute-done | bytes 196640 | tf_op jit(solution)/shard_map/ppermute | solution.py:548
  60.2 1.7 collective-permute-start.8
  61.9 7.4 %collective-permute-done.8 = bf16[4,192,256]{2,1,0:T(8,128)(2,1)S(1)} collective-permute-done((bf16[4,192,256]{2,1,0:T(8,128)(2,1)S(1)}, bf16[4,192,256]{2,1,0:T(8,128)(2,1)S(1)}, u32[]{:S(2)}, u32[]{:S(2)}) %collective-permute-start.8) | collective-permute-done | bytes 393248 | tf_op jit(solution)/shard_map/ppermute | solution.py:548
  70.2 2.3 %pack_heads.3 = bf16[4,2,3,64,384]{4,3,2,1,0:T(8,128)(2,1)} custom-call(bf16[4,64,1536]{2,1,0:T(8,128)(2,1)} %q_ref.3, bf16[4,64,1536]{2,1,0:T(8,128)(2,1)} %k_ref.3, bf16[4,64,1536]{2,1,0:T(8,128)(2,1)} %v_ref.3, bf16[8,192,256]{2,1,0:T(8,128)(2,1)} %pad_maximum_fusion.refs_0_.refs_6_, bf16[1,512,256]{2,1,0:T(8,128)(2,1)} %copy-done.6, ...), custom_call_target="tpu_custom_call" | custom-call | tf_op jit(solution)/shard_map/pack_heads/pallas_call | solution.py:41
  73.6 6.0 %all-to-all-start.2 = ((bf16[8,3,64,384]{3,2,1,0:T(8,128)(2,1)}), bf16[8,3,64,384]{3,2,1,0:T(8,128)(2,1)S(1)}, u32[]{:S(2)}, u32[]{:S(2)}) async-start(bf16[8,3,64,384]{3,2,1,0:T(8,128)(2,1)} %bitcast.13), calls=%async_computation.2 | async-start | bytes 2359296 | tf_op jit(solution)/shard_map/all_to_all | solution.py:552
  82.4 5.5 %attention.2 = bf16[8,64,384]{2,1,0:T(8,128)(2,1)S(1)} custom-call(bf16[8,3,64,384]{3,2,1,0:T(8,128)(2,1)S(1)} %copy-done.16), custom_call_target="tpu_custom_call" | custom-call | flops 402653184 | bytes 1572864 | tf_op jit(solution)/shard_map/attention/pallas_call | solution.py:120
  88.7 18.1 %all-to-all-done.2.qkv_ref = bf16[8,3,64,384]{3,2,1,0:T(8,128)(2,1)S(1)} async-done(((bf16[8,3,64,384]{3,2,1,0:T(8,128)(2,1)}), bf16[8,3,64,384]{3,2,1,0:T(8,128)(2,1)S(1)}, u32[]{:S(2)}, u32[]{:S(2)}) %all-to-all-start.2) | async-done | bytes 1179680 | tf_op jit(solution)/shard_map/all_to_all | solution.py:552
  106.8 4.1 %all-to-all-start.1 = ((bf16[8,64,384]{2,1,0:T(8,128)(2,1)}), bf16[8,64,384]{2,1,0:T(8,128)(2,1)}, u32[]{:S(2)}, u32[]{:S(2)}) async-start(bf16[8,64,384]{2,1,0:T(8,128)(2,1)} %copy-done.18), calls=%async_computation.1 | async-start | bytes 786432 | tf_op jit(solution)/shard_map/all_to_all | solution.py:552
  110.9 1.9 collective-permute-start.16
  115.0 9.1 %collective-permute-done.16.refs_3_.refs_7_ = bf16[1,512,256]{2,1,0:T(8,128)(2,1)S(1)} collective-permute-done((bf16[1,512,256]{2,1,0:T(8,128)(2,1)S(1)}, bf16[1,512,256]{2,1,0:T(8,128)(2,1)S(1)}, u32[]{:S(2)}, u32[]{:S(2)}) %collective-permute-start.16) | collective-permute-done | bytes 262176 | tf_op jit(solution)/shard_map/ppermute | solution.py:548
  124.4 1.6 collective-permute-start.1
  126.0 3.8 %collective-permute-done.15.refs_2_.refs_14_ = bf16[1,512,256]{2,1,0:T(8,128)(2,1)S(1)} collective-permute-done((bf16[1,512,256]{2,1,0:T(8,128)(2,1)S(1)}, bf16[1,512,256]{2,1,0:T(8,128)(2,1)S(1)}, u32[]{:S(2)}, u32[]{:S(2)}) %collective-permute-start.15) | collective-permute-done | bytes 262176 | tf_op jit(solution)/shard_map/ppermute | solution.py:548
  130.3 3.5 %collective-permute-done.13.refs_1_.refs_10_ = bf16[1,512,256]{2,1,0:T(8,128)(2,1)S(1)} collective-permute-done((bf16[1,512,256]{2,1,0:T(8,128)(2,1)S(1)}, bf16[1,512,256]{2,1,0:T(8,128)(2,1)S(1)}, u32[]{:S(2)}, u32[]{:S(2)}) %collective-permute-start.13) | collective-permute-done | bytes 262176 | tf_op jit(solution)/shard_map/ppermute | solution.py:548
  133.8 5.5 %attention.3 = bf16[8,64,384]{2,1,0:T(8,128)(2,1)S(1)} custom-call(bf16[8,3,64,384]{3,2,1,0:T(8,128)(2,1)S(1)} %all-to-all-done.2.qkv_ref, bf16[1,512,256]{2,1,0:T(8,128)(2,1)S(1)} %collective-permute-done.1.refs_0_.refs_16_, bf16[1,512,256]{2,1,0:T(8,128)(2,1)S(1)} %collective-permute-done.13.refs_1_.refs_10_, ...), custom_call_target="tpu_custom_call" | custom-call | flops 402653184 | bytes 1572864 | tf_op jit(solution)/shard_map/attention/pallas_call | solution.py:120
  142.3 4.5 %all-to-all-start.3 = ((bf16[8,64,384]{2,1,0:T(8,128)(2,1)}), bf16[8,64,384]{2,1,0:T(8,128)(2,1)S(1)}, u32[]{:S(2)}, u32[]{:S(2)}) async-start(bf16[8,64,384]{2,1,0:T(8,128)(2,1)} %copy-done.14), calls=%async_computation.3 | async-start | bytes 786432 | tf_op jit(solution)/shard_map/all_to_all | solution.py:552
  148.4 2.0 collective-permute-start.2
  150.8 5.3 %collective-permute-done.14.refs_4_.refs_16_.refs_11_ = bf16[1,512,256]{2,1,0:T(8,128)(2,1)S(1)} collective-permute-done((bf16[1,512,256]{2,1,0:T(8,128)(2,1)S(1)}, bf16[1,512,256]{2,1,0:T(8,128)(2,1)S(1)}, u32[]{:S(2)}, u32[]{:S(2)}) %collective-permute-start.14) | collective-permute-done | bytes 262176 | tf_op jit(solution)/shard_map/ppermute | solution.py:544
  156.1 2.0 collective-permute-start.20
  158.1 1.8 collective-permute-done.2.refs_0_.refs_12_.refs_18_
  163.1 4.7 %first_project.1.refs_4_ = f32[256,1536]{1,0:T(8,128)} custom-call(bf16[4,64,1536]{2,1,0:T(8,128)(2,1)} %refs_1_.1, bf16[1536,1536]{1,0:T(8,128)(2,1)} %refs_3_.2, bf16[8,64,384]{2,1,0:T(8,128)(2,1)} %all-to-all-done.1.piece_ref, bf16[1,512,256]{2,1,0:T(8,128)(2,1)} %copy-done.23, bf16[8,192,256]{2,1,0:T(8,128)(2,1)} %collective-permute-done.9.refs_1_.refs_8_.refs_13_, ...), custom_call_target="tpu_custom_call" | custom-call | flops 603979776 | bytes 5505024 | tf_op jit(solution)/shard_map/first_project/pallas_call | solution.py:198
  168.8 8.7 %project_embed.1 = (bf16[4,64,1536]{2,1,0:T(8,128)(2,1)}, bf16[2,256,512]{2,1,0:T(8,128)(2,1)}) custom-call(s32[4]{0:T(128)} %pad_add_fusion.refs_0_.ids_ref, bf16[4,64,1536]{2,1,0:T(8,128)(2,1)} %refs_1_.1, f32[1,1024]{1,0:T(1,128)} %bitcast.16, bf16[1536,1536]{1,0:T(8,128)(2,1)} %refs_3_.2, f32[256,1536]{1,0:T(8,128)} %first_project.1.refs_4_, ...), custom_call_target="tpu_custom_call" | custom-call | flops 1409286144 | bytes 10223616 | tf_op jit(solution)/shard_map/project_embed/pallas_call | solution.py:349
  178.1 5.4 %reward.2.refs_3_ = f32[8,128]{1,0:T(8,128)} custom-call(s32[4]{0:T(128)} %pad_add_fusion.refs_0_.ids_ref, bf16[2,256,512]{2,1,0:T(8,128)(2,1)} %get-tuple-element.7.refs_1_, f32[16,1,256]{2,1,0:T(1,128)} %bitcast.14, f32[4]{0:T(128)} %refs_3_.3, bf16[1,512,256]{2,1,0:T(8,128)(2,1)} %copy-done.27, bf16[1,512,256]{2,1,0:T(8,128)(2,1)} %copy-done.1, ...), custom_call_target="tpu_custom_call" | custom-call | flops 1073741824 | bytes 4194304 | tf_op jit(solution)/shard_map/reward/pallas_call | solution.py:446
  184.3 5.4 %reward.3.refs_0_ = f32[8,128]{1,0:T(8,128)} custom-call(s32[4]{0:T(128)} %pad_add_fusion.refs_0_.ids_ref, bf16[2,256,512]{2,1,0:T(8,128)(2,1)} %copy-done.29, f32[16,1,256]{2,1,0:T(1,128)} %bitcast.15, f32[8,128]{1,0:T(8,128)} %reward.2.refs_3_, bf16[1,512,256]{2,1,0:T(8,128)(2,1)} %copy-done.27, bf16[1,512,256]{2,1,0:T(8,128)(2,1)} %copy-done.1, ...), custom_call_target="tpu_custom_call" | custom-call | flops 1073741824 | bytes 4194304 | tf_op jit(solution)/shard_map/reward/pallas_call | solution.py:446
  189.8 2.9 %collective-permute-start.25 = (f32[8,128]{1,0:T(8,128)}, f32[8,128]{1,0:T(8,128)S(1)}, u32[]{:S(2)}, u32[]{:S(2)}) collective-permute-start(f32[8,128]{1,0:T(8,128)} %reward.3.refs_0_), channel_id=1, source_target_pairs={{0,6},{1,7},{2,4},{3,5},{4,2},{5,3},{6,0},{7,1},{8,14},{9,15},{10,... | collective-permute-start | bytes 12296 | tf_op jit(solution)/shard_map/ppermute | solution.py:548
  195.4 1.9 collective-permute-done.24.refs_2_
  198.6 1.7 collective-permute-start.26
  200.2 2.0 resample.1.resampled_ref
  (112 shorter events, 28.5 us)
Async XLA Ops:
  3.0 69.5 %all-to-all-start = ((bf16[8,3,64,384]{3,2,1,0:T(8,128)(2,1)}), bf16[8,3,64,384]{3,2,1,0:T(8,128)(2,1)S(1)}, u32[]{:S(2)}, u32[]{:S(2)}) async-start(bf16[8,3,64,384]{3,2,1,0:T(8,128)(2,1)} %bitcast.12), calls=%async_computation | async-start | bytes 2359296 | tf_op jit(solution)/shard_map/all_to_all | solution.py:552
  10.3 44.0 %collective-permute-start.6 = (bf16[1,512,256]{2,1,0:T(8,128)(2,1)S(1)}, bf16[1,512,256]{2,1,0:T(8,128)(2,1)S(1)}, u32[]{:S(2)}, u32[]{:S(2)}) collective-permute-start(bf16[1,512,256]{2,1,0:T(8,128)(2,1)S(1)} %dynamic-slice_bitcast_fusion.refs_4_), channel_id=1, source_target_pairs={{0,16},{16,0},{1,17},{17,1},{2,18},{18,2},{3,19},{19,3},{4,20},{20... | collective-permute-start | bytes 786440 | tf_op jit(solution)/shard_map/ppermute | solution.py:544
  11.9 42.5 %collective-permute-start.5 = (bf16[1,512,256]{2,1,0:T(8,128)(2,1)S(1)}, bf16[1,512,256]{2,1,0:T(8,128)(2,1)S(1)}, u32[]{:S(2)}, u32[]{:S(2)}) collective-permute-start(bf16[1,512,256]{2,1,0:T(8,128)(2,1)S(1)} %dynamic-slice_bitcast_fusion.refs_4_), channel_id=1, source_target_pairs={{0,1},{1,0},{2,3},{3,2},{4,5},{5,4},{6,7},{7,6},{8,9},{9,8},{10,11... | collective-permute-start | bytes 786440 | tf_op jit(solution)/shard_map/ppermute | solution.py:548
  13.9 40.5 %collective-permute-start.4 = (bf16[1,512,256]{2,1,0:T(8,128)(2,1)S(1)}, bf16[1,512,256]{2,1,0:T(8,128)(2,1)S(1)}, u32[]{:S(2)}, u32[]{:S(2)}) collective-permute-start(bf16[1,512,256]{2,1,0:T(8,128)(2,1)S(1)} %dynamic-slice_bitcast_fusion.refs_4_), channel_id=1, source_target_pairs={{0,2},{1,3},{2,0},{3,1},{4,6},{5,7},{6,4},{7,5},{8,10},{9,11},{10,... | collective-permute-start | bytes 786440 | tf_op jit(solution)/shard_map/ppermute | solution.py:548
  15.3 39.0 %collective-permute-start = (bf16[1,512,256]{2,1,0:T(8,128)(2,1)S(1)}, bf16[1,512,256]{2,1,0:T(8,128)(2,1)S(1)}, u32[]{:S(2)}, u32[]{:S(2)}) collective-permute-start(bf16[1,512,256]{2,1,0:T(8,128)(2,1)S(1)} %dynamic-slice_bitcast_fusion.refs_4_), channel_id=1, source_target_pairs={{0,4},{1,5},{2,6},{3,7},{4,0},{5,1},{6,2},{7,3},{8,12},{9,13},{10,... | collective-permute-start | bytes 786440 | tf_op jit(solution)/shard_map/ppermute | solution.py:548
  18.6 35.7 %collective-permute-start.3 = (bf16[1,192,256]{2,1,0:T(8,128)(2,1)S(1)}, bf16[1,192,256]{2,1,0:T(8,128)(2,1)S(1)}, u32[]{:S(2)}, u32[]{:S(2)}) collective-permute-start(bf16[1,192,256]{2,1,0:T(8,128)(2,1)S(1)} %dynamic-slice_bitcast_fusion.1), channel_id=1, source_target_pairs={{0,4},{1,5},{2,6},{3,7},{4,0},{5,1},{6,2},{7,3},{8,12},{9,13},{10,... | collective-permute-start | bytes 294920 | tf_op jit(solution)/shard_map/ppermute | solution.py:548
  54.4 5.7 %collective-permute-start.7 = (bf16[2,192,256]{2,1,0:T(8,128)(2,1)S(1)}, bf16[2,192,256]{2,1,0:T(8,128)(2,1)S(1)}, u32[]{:S(2)}, u32[]{:S(2)}) collective-permute-start(bf16[2,192,256]{2,1,0:T(8,128)(2,1)S(1)} %gate.1), channel_id=1, source_target_pairs={{0,2},{1,3},{2,0},{3,1},{4,6},{5,7},{6,4},{7,5},{8,10},{9,11},{10,... | collective-permute-start | bytes 589832 | tf_op jit(solution)/shard_map/ppermute | solution.py:548
  60.2 9.1 %collective-permute-start.8 = (bf16[4,192,256]{2,1,0:T(8,128)(2,1)S(1)}, bf16[4,192,256]{2,1,0:T(8,128)(2,1)S(1)}, u32[]{:S(2)}, u32[]{:S(2)}) collective-permute-start(bf16[4,192,256]{2,1,0:T(8,128)(2,1)S(1)} %pad_maximum_fusion.1), channel_id=1, source_target_pairs={{0,1},{1,0},{2,3},{3,2},{4,5},{5,4},{6,7},{7,6},{8,9},{9,8},{10,11... | collective-permute-start | bytes 1179656 | tf_op jit(solution)/shard_map/ppermute | solution.py:548
  73.6 33.2 %all-to-all-start.2 = ((bf16[8,3,64,384]{3,2,1,0:T(8,128)(2,1)}), bf16[8,3,64,384]{3,2,1,0:T(8,128)(2,1)S(1)}, u32[]{:S(2)}, u32[]{:S(2)}) async-start(bf16[8,3,64,384]{3,2,1,0:T(8,128)(2,1)} %bitcast.13), calls=%async_computation.2 | async-start | bytes 2359296 | tf_op jit(solution)/shard_map/all_to_all | solution.py:552
  79.6 50.2 %collective-permute-start.10 = (bf16[8,192,256]{2,1,0:T(8,128)(2,1)}, bf16[8,192,256]{2,1,0:T(8,128)(2,1)}, u32[]{:S(2)}, u32[]{:S(2)}) collective-permute-start(bf16[8,192,256]{2,1,0:T(8,128)(2,1)} %pad_maximum_fusion.refs_0_.refs_6_), channel_id=1, source_target_pairs={{0,16},{16,0},{1,17},{17,1},{2,18},{18,2},{3,19},{19,3},{4,20},{20... | collective-permute-start | bytes 2359304 | tf_op jit(solution)/shard_map/ppermute | solution.py:544
  106.8 35.5 %all-to-all-start.1 = ((bf16[8,64,384]{2,1,0:T(8,128)(2,1)}), bf16[8,64,384]{2,1,0:T(8,128)(2,1)}, u32[]{:S(2)}, u32[]{:S(2)}) async-start(bf16[8,64,384]{2,1,0:T(8,128)(2,1)} %copy-done.18), calls=%async_computation.1 | async-start | bytes 786432 | tf_op jit(solution)/shard_map/all_to_all | solution.py:552
  110.9 13.3 %collective-permute-start.16 = (bf16[1,512,256]{2,1,0:T(8,128)(2,1)S(1)}, bf16[1,512,256]{2,1,0:T(8,128)(2,1)S(1)}, u32[]{:S(2)}, u32[]{:S(2)}) collective-permute-start(bf16[1,512,256]{2,1,0:T(8,128)(2,1)S(1)} %copy-done.2), channel_id=1, source_target_pairs={{0,1},{1,0},{2,3},{3,2},{4,5},{5,4},{6,7},{7,6},{8,9},{9,8},{10,11... | collective-permute-start | bytes 786440 | tf_op jit(solution)/shard_map/ppermute | solution.py:548
  112.8 11.6 %collective-permute-start.18 = (bf16[1,512,256]{2,1,0:T(8,128)(2,1)S(1)}, bf16[1,512,256]{2,1,0:T(8,128)(2,1)S(1)}, u32[]{:S(2)}, u32[]{:S(2)}) collective-permute-start(bf16[1,512,256]{2,1,0:T(8,128)(2,1)S(1)} %copy-done.5), channel_id=1, source_target_pairs={{0,16},{16,0},{1,17},{17,1},{2,18},{18,2},{3,19},{19,3},{4,20},{20... | collective-permute-start | bytes 786440 | tf_op jit(solution)/shard_map/ppermute | solution.py:544
  114.3 15.5 %collective-permute-start.15 = (bf16[1,512,256]{2,1,0:T(8,128)(2,1)S(1)}, bf16[1,512,256]{2,1,0:T(8,128)(2,1)S(1)}, u32[]{:S(2)}, u32[]{:S(2)}) collective-permute-start(bf16[1,512,256]{2,1,0:T(8,128)(2,1)S(1)} %copy-done.5), channel_id=1, source_target_pairs={{0,1},{1,0},{2,3},{3,2},{4,5},{5,4},{6,7},{7,6},{8,9},{9,8},{10,11... | collective-permute-start | bytes 786440 | tf_op jit(solution)/shard_map/ppermute | solution.py:548
  114.5 15.8 %collective-permute-start.17 = (bf16[1,512,256]{2,1,0:T(8,128)(2,1)S(1)}, bf16[1,512,256]{2,1,0:T(8,128)(2,1)S(1)}, u32[]{:S(2)}, u32[]{:S(2)}) collective-permute-start(bf16[1,512,256]{2,1,0:T(8,128)(2,1)S(1)} %copy-done.7), channel_id=1, source_target_pairs={{0,16},{16,0},{1,17},{17,1},{2,18},{18,2},{3,19},{19,3},{4,20},{20... | collective-permute-start | bytes 786440 | tf_op jit(solution)/shard_map/ppermute | solution.py:544
  124.1 9.6 %collective-permute-start.13 = (bf16[1,512,256]{2,1,0:T(8,128)(2,1)S(1)}, bf16[1,512,256]{2,1,0:T(8,128)(2,1)S(1)}, u32[]{:S(2)}, u32[]{:S(2)}) collective-permute-start(bf16[1,512,256]{2,1,0:T(8,128)(2,1)S(1)} %copy-done.7), channel_id=1, source_target_pairs={{0,1},{1,0},{2,3},{3,2},{4,5},{5,4},{6,7},{7,6},{8,9},{9,8},{10,11... | collective-permute-start | bytes 786440 | tf_op jit(solution)/shard_map/ppermute | solution.py:548
  124.4 9.4 %collective-permute-start.1 = (bf16[1,512,256]{2,1,0:T(8,128)(2,1)S(1)}, bf16[1,512,256]{2,1,0:T(8,128)(2,1)S(1)}, u32[]{:S(2)}, u32[]{:S(2)}) collective-permute-start(bf16[1,512,256]{2,1,0:T(8,128)(2,1)S(1)} %copy-done.7), channel_id=1, source_target_pairs={{0,2},{1,3},{2,0},{3,1},{4,6},{5,7},{6,4},{7,5},{8,10},{9,11},{10,... | collective-permute-start | bytes 786440 | tf_op jit(solution)/shard_map/ppermute | solution.py:548
  129.8 32.6 %collective-permute-start.9 = (bf16[8,192,256]{2,1,0:T(8,128)(2,1)}, bf16[8,192,256]{2,1,0:T(8,128)(2,1)}, u32[]{:S(2)}, u32[]{:S(2)}) collective-permute-start(bf16[8,192,256]{2,1,0:T(8,128)(2,1)} %pad_maximum_fusion.refs_0_.refs_6_), channel_id=1, source_target_pairs={{0,8},{8,0},{1,9},{9,1},{2,10},{10,2},{3,11},{11,3},{4,12},{12,4},... | collective-permute-start | bytes 2359304 | tf_op jit(solution)/shard_map/ppermute | solution.py:544
  129.8 32.6 %collective-permute-start.11 = (bf16[8,192,256]{2,1,0:T(8,128)(2,1)}, bf16[8,192,256]{2,1,0:T(8,128)(2,1)}, u32[]{:S(2)}, u32[]{:S(2)}) collective-permute-start(bf16[8,192,256]{2,1,0:T(8,128)(2,1)} %collective-permute-done.10.refs_4_.refs_7_), channel_id=1, source_target_pairs={{0,8},{8,0},{1,9},{9,1},{2,10},{10,2},{3,11},{11,3},{4,12},{12,4},... | collective-permute-start | bytes 2359304 | tf_op jit(solution)/shard_map/ppermute | solution.py:544
  142.3 25.6 %all-to-all-start.3 = ((bf16[8,64,384]{2,1,0:T(8,128)(2,1)}), bf16[8,64,384]{2,1,0:T(8,128)(2,1)S(1)}, u32[]{:S(2)}, u32[]{:S(2)}) async-start(bf16[8,64,384]{2,1,0:T(8,128)(2,1)} %copy-done.14), calls=%async_computation.3 | async-start | bytes 786432 | tf_op jit(solution)/shard_map/all_to_all | solution.py:552
  146.8 9.3 %collective-permute-start.14 = (bf16[1,512,256]{2,1,0:T(8,128)(2,1)S(1)}, bf16[1,512,256]{2,1,0:T(8,128)(2,1)S(1)}, u32[]{:S(2)}, u32[]{:S(2)}) collective-permute-start(bf16[1,512,256]{2,1,0:T(8,128)(2,1)S(1)} %collective-permute-done.13.refs_1_.refs_10_), channel_id=1, source_target_pairs={{0,16},{16,0},{1,17},{17,1},{2,18},{18,2},{3,19},{19,3},{4,20},{20... | collective-permute-start | bytes 786440 | tf_op jit(solution)/shard_map/ppermute | solution.py:544
  148.4 11.5 %collective-permute-start.2 = (bf16[1,512,256]{2,1,0:T(8,128)(2,1)}, bf16[1,512,256]{2,1,0:T(8,128)(2,1)S(1)}, u32[]{:S(2)}, u32[]{:S(2)}) collective-permute-start(bf16[1,512,256]{2,1,0:T(8,128)(2,1)} %copy-done.13), channel_id=1, source_target_pairs={{0,1},{1,0},{2,3},{3,2},{4,5},{5,4},{6,7},{7,6},{8,9},{9,8},{10,11... | collective-permute-start | bytes 786440 | tf_op jit(solution)/shard_map/ppermute | solution.py:548
  150.3 12.1 %collective-permute-start.12 = (bf16[1,512,256]{2,1,0:T(8,128)(2,1)}, bf16[1,512,256]{2,1,0:T(8,128)(2,1)S(1)}, u32[]{:S(2)}, u32[]{:S(2)}) collective-permute-start(bf16[1,512,256]{2,1,0:T(8,128)(2,1)} %copy-done.13), channel_id=1, source_target_pairs={{0,16},{16,0},{1,17},{17,1},{2,18},{18,2},{3,19},{19,3},{4,20},{20... | collective-permute-start | bytes 786440 | tf_op jit(solution)/shard_map/ppermute | solution.py:544
  156.1 11.7 %collective-permute-start.20 = (bf16[1,512,256]{2,1,0:T(8,128)(2,1)S(1)}, bf16[1,512,256]{2,1,0:T(8,128)(2,1)S(1)}, u32[]{:S(2)}, u32[]{:S(2)}) collective-permute-start(bf16[1,512,256]{2,1,0:T(8,128)(2,1)S(1)} %collective-permute-done.18.refs_6_.refs_13_), channel_id=1, source_target_pairs={{0,1},{1,0},{2,3},{3,2},{4,5},{5,4},{6,7},{7,6},{8,9},{9,8},{10,11... | collective-permute-start | bytes 786440 | tf_op jit(solution)/shard_map/ppermute | solution.py:548
  159.9 7.9 %collective-permute-start.19 = (bf16[1,512,256]{2,1,0:T(8,128)(2,1)S(1)}, bf16[1,512,256]{2,1,0:T(8,128)(2,1)S(1)}, u32[]{:S(2)}, u32[]{:S(2)}) collective-permute-start(bf16[1,512,256]{2,1,0:T(8,128)(2,1)S(1)} %collective-permute-done.2.refs_0_.refs_12_.refs_18_), channel_id=1, source_target_pairs={{0,16},{16,0},{1,17},{17,1},{2,18},{18,2},{3,19},{19,3},{4,20},{20... | collective-permute-start | bytes 786440 | tf_op jit(solution)/shard_map/ppermute | solution.py:544
  177.5 22.7 %collective-permute-start.21 = (bf16[4,64,1536]{2,1,0:T(8,128)(2,1)}, bf16[4,64,1536]{2,1,0:T(8,128)(2,1)S(1)}, u32[]{:S(2)}, u32[]{:S(2)}) collective-permute-start(bf16[4,64,1536]{2,1,0:T(8,128)(2,1)} %get-tuple-element.6.own_ref), channel_id=1, source_target_pairs={{0,8},{8,0},{1,9},{9,1},{2,10},{10,2},{3,11},{11,3},{4,12},{12,4},... | collective-permute-start | bytes 2359304 | tf_op jit(solution)/shard_map/ppermute | solution.py:544
  177.6 5.9 %collective-permute-start.22 = (bf16[2,256,512]{2,1,0:T(8,128)(2,1)}, bf16[2,256,512]{2,1,0:T(8,128)(2,1)S(1)}, u32[]{:S(2)}, u32[]{:S(2)}) collective-permute-start(bf16[2,256,512]{2,1,0:T(8,128)(2,1)} %get-tuple-element.7.refs_1_), channel_id=1, source_target_pairs={{0,8},{8,0},{1,9},{9,1},{2,10},{10,2},{3,11},{11,3},{4,12},{12,4},... | collective-permute-start | bytes 1572872 | tf_op jit(solution)/shard_map/ppermute | solution.py:544
  189.8 5.7 %collective-permute-start.25 = (f32[8,128]{1,0:T(8,128)}, f32[8,128]{1,0:T(8,128)S(1)}, u32[]{:S(2)}, u32[]{:S(2)}) collective-permute-start(f32[8,128]{1,0:T(8,128)} %reward.3.refs_0_), channel_id=1, source_target_pairs={{0,6},{1,7},{2,4},{3,5},{4,2},{5,3},{6,0},{7,1},{8,14},{9,15},{10,... | collective-permute-start | bytes 12296 | tf_op jit(solution)/shard_map/ppermute | solution.py:548
  192.7 4.7 %collective-permute-start.24 = (f32[8,128]{1,0:T(8,128)}, f32[8,128]{1,0:T(8,128)S(1)}, u32[]{:S(2)}, u32[]{:S(2)}) collective-permute-start(f32[8,128]{1,0:T(8,128)} %reward.3.refs_0_), channel_id=1, source_target_pairs={{0,4},{1,5},{2,6},{3,7},{4,0},{5,1},{6,2},{7,3},{8,12},{9,13},{10,... | collective-permute-start | bytes 12296 | tf_op jit(solution)/shard_map/ppermute | solution.py:548
  193.2 4.2 %collective-permute-start.23 = (f32[8,128]{1,0:T(8,128)}, f32[8,128]{1,0:T(8,128)S(1)}, u32[]{:S(2)}, u32[]{:S(2)}) collective-permute-start(f32[8,128]{1,0:T(8,128)} %reward.3.refs_0_), channel_id=1, source_target_pairs={{0,2},{1,3},{2,0},{3,1},{4,6},{5,7},{6,4},{7,5},{8,10},{9,11},{10,... | collective-permute-start | bytes 12296 | tf_op jit(solution)/shard_map/ppermute | solution.py:548
  198.1 4.2 %collective-permute-start.28 = (f32[8,128]{1,0:T(8,128)S(1)}, f32[8,128]{1,0:T(8,128)S(1)}, u32[]{:S(2)}, u32[]{:S(2)}) collective-permute-start(f32[8,128]{1,0:T(8,128)S(1)} %add_partials.1.refs_0_), channel_id=1, source_target_pairs={{0,8},{8,0},{1,9},{9,1},{2,10},{10,2},{3,11},{11,3},{4,12},{12,4},... | collective-permute-start | bytes 12296 | tf_op jit(solution)/shard_map/ppermute | solution.py:544
  198.1 4.2 %collective-permute-start.27 = (f32[8,128]{1,0:T(8,128)S(1)}, f32[8,128]{1,0:T(8,128)S(1)}, u32[]{:S(2)}, u32[]{:S(2)}) collective-permute-start(f32[8,128]{1,0:T(8,128)S(1)} %add_partials.1.refs_0_), channel_id=1, source_target_pairs={{0,9},{1,8},{2,11},{3,10},{4,13},{5,12},{6,15},{7,14},{8,1},{9,0},... | collective-permute-start | bytes 12296 | tf_op jit(solution)/shard_map/ppermute | solution.py:696
  (31 other events, 355.8 us)

commit v10 on v8

--- a/solution.py
+++ b/solution.py
@@ -52,22 +52,17 @@
     pass
 
 
-def gate(pinned, delayed, after):
-    count = len(pinned) + len(delayed)
-    anywhere = pl.BlockSpec(memory_space=pl.ANY)
-    specs = [pl.BlockSpec(memory_space=pltpu.HBM)] * len(pinned) + [anywhere] * len(delayed)
-    arrays = [*pinned, *delayed]
-    return list(
-        pl.pallas_call(
-            gate_kernel,
-            in_specs=specs + [anywhere] * len(after),
-            out_specs=specs,
-            out_shape=[jax.ShapeDtypeStruct(array.shape, array.dtype) for array in arrays],
-            input_output_aliases={index: index for index in range(count)},
-            compiler_params=pltpu.CompilerParams(vmem_limit_bytes=MIB),
-            name="gate",
-        )(*arrays, *after)
-    )
+def gate(array, after):
+    hbm = pl.BlockSpec(memory_space=pltpu.HBM)
+    return pl.pallas_call(
+        gate_kernel,
+        in_specs=[hbm] + [pl.BlockSpec(memory_space=pl.ANY)] * len(after),
+        out_specs=hbm,
+        out_shape=jax.ShapeDtypeStruct(array.shape, array.dtype),
+        input_output_aliases={0: 0},
+        compiler_params=pltpu.CompilerParams(vmem_limit_bytes=60 * MIB),
+        name="gate",
+    )(array, *after)
 
 
 def attention_kernel(head_width, block_sources, qkv_ref, out_ref):
@@ -371,13 +366,17 @@
     ids_ref, features_ref, head_ref, before_ref = refs[:4]
     weight_refs, (out_ref, weight_vmem, rows_ref, sems) = refs[4:-4], refs[-4:]
     dom, group, seq = ids_ref[0], ids_ref[1], ids_ref[2]
-    shards, depth, columns = weight_refs[0].shape
+    _, depth, columns = weight_refs[0].shape
     rows = features_ref.shape[1]
-    count = shards * len(weight_refs) // parts
+    places = [
+        (pair, shard)
+        for pair in range(len(weight_refs) // parts)
+        for shard in range(weight_refs[pair * parts].shape[0])
+    ]
+    count = len(places)
 
     copies = []
-    for place in range(count):
-        pair, shard = divmod(place, shards)
+    for place, (pair, shard) in enumerate(places):
         lane = place % joined * columns
         for index in range(parts):
             copy = pltpu.make_async_copy(
@@ -400,9 +399,12 @@
         for copy in copies[step * joined * parts : (step + 1) * joined * parts]:
             copy.wait()
         hidden = jnp.dot(rows_ref[...], weight_vmem[step], preferred_element_type=jnp.float32)
-        places = range(step * joined, (step + 1) * joined)
         head = jnp.concatenate(
-            [head_ref[(seq ^ offsets[place]) * doms + dom] for place in places], axis=1
+            [
+                head_ref[(seq ^ offset) * doms + dom]
+                for offset in offsets[step * joined : (step + 1) * joined]
+            ],
+            axis=1,
         )
         scored = jax.nn.gelu(hidden) * head
         totals += jnp.sum(scored.reshape(particles, rows // particles, -1), axis=1)
@@ -424,9 +426,9 @@
 
 
 def reward(ids, features, weights, parts, doms, offsets, head, before, particles, scale):
-    shards, depth, columns = weights[0].shape
+    _, depth, columns = weights[0].shape
     rows = features.shape[1]
-    count = shards * len(weights) // parts
+    count = len(offsets)
     joined = 2 if columns % LANES == 0 and count % 2 == 0 else 1
     smem = pl.BlockSpec(memory_space=pltpu.SMEM)
     vmem = pl.BlockSpec(memory_space=pltpu.VMEM)
@@ -577,50 +579,59 @@
         up_weight, (group * up_depth, dom * up_columns), (up_depth, up_columns)
     )[None]
     bits = [1 << place for place in reversed(range(1, seq_count.bit_length() - 1))]
+    near = [0]
+    for bit in bits[:-2]:
+        embed_share = jnp.concatenate([embed_share, swapped(embed_share, "seq", bit)])
+        up_share = jnp.concatenate([up_share, swapped(up_share, "seq", bit)])
+        near = near + [offset ^ bit for offset in near]
+    high, low = bits[-2:]
+
+    def over_groups(array):
+        return [array] + [shifted(array, "groups", k) for k in range(1, group_count)]
 
     packed = pack(queries, keys, values, chunks, width)
-    near = [0]
-    for bit in bits[:-1]:
+    embed_share = jnp.concatenate([embed_share, swapped(embed_share, "seq", high)])
+    packed[0] = gate(packed[0], [embed_share])
+
+    arrived = [exchange(packed[0])]
+    up_high = swapped(up_share, "seq", high)
+    own_pair, own_groups = swapped(up_share, "seq", 1), over_groups(up_share)
+    for bit in (low, 1):
         embed_share = jnp.concatenate([embed_share, swapped(embed_share, "seq", bit)])
-        near = near + [offset ^ bit for offset in near]
-    far = [offset ^ bits[-1] for offset in near]
-    packed[0], embed_share = gate([packed[0]], [embed_share], [])
-
-    arrived = [exchange(packed[0])]
-    for bit in bits[:-1]:
-        up_share = jnp.concatenate([up_share, swapped(up_share, "seq", bit)])
-    for bit in (bits[-1], 1):
-        embed_share = jnp.concatenate([embed_share, swapped(embed_share, "seq", bit)])
-    *packed[1:], embed_share, up_near = gate(packed[1:], [embed_share, up_share], arrived[:1])
+    after = [arrived[0], embed_share, up_high, own_pair, *own_groups[1:]]
+    packed[1:] = [gate(piece, after) for piece in packed[1:]]
 
     arrived += [exchange(piece) for piece in packed[1:]]
-    up_far = swapped(up_near, "seq", bits[-1])
-    near_pair = swapped(up_near, "seq", 1)
-    near_groups = [up_near] + [shifted(up_near, "groups", k) for k in range(1, group_count)]
-    embed_near = [embed_share] + [shifted(embed_share, "groups", k) for k in range(1, group_count)]
+    up_far = swapped(jnp.concatenate([up_share, up_high]), "seq", low)
+    high_pair, high_groups = swapped(up_high, "seq", 1), over_groups(up_high)
+    own_pairs = [own_pair] + [swapped(piece, "seq", 1) for piece in own_groups[1:]]
+    embed_near = over_groups(embed_share)
     attended = [attention(arrived[0], head_width)]
-    attended[0], up_far, near_pair, *embed_near = gate(
-        attended, [up_far, near_pair, *embed_near], arrived[1:]
-    )
+    after = [up_far, high_pair, *high_groups[1:], *own_pairs[1:], *embed_near[1:]]
+    attended[0] = gate(attended[0], [*after, *arrived[1:]])
 
     returned = [exchange(attended[0])]
-    far_pair = swapped(up_far, "seq", 1)
-    far_groups = [up_far] + [shifted(up_far, "groups", k) for k in range(1, group_count)]
+    far_pair, far_groups = swapped(up_far, "seq", 1), over_groups(up_far)
     embed_parts = embed_near + [
         shifted(piece, "dom", k) for k in range(1, dom_count) for piece in embed_near
     ]
     attended += [attention(piece, head_width) for piece in arrived[1:]]
-    *rest, near_pair, far_pair = gate(
-        attended[1:], [*far_groups[1:], near_pair, far_pair], [returned[0], *embed_parts]
-    )
-    attended[1:], far_groups[1:] = rest[: chunks - 1], rest[chunks - 1 :]
+    after = [returned[0], *far_groups[1:], *embed_parts[group_count:]]
+    attended[1:] = [gate(piece, after) for piece in attended[1:]]
 
     returned += [exchange(piece) for piece in attended[1:]]
-    pair_groups = [near_pair] + [shifted(near_pair, "groups", k) for k in range(1, group_count)]
-    far_pairs = [far_pair] + [swapped(piece, "seq", 1) for piece in far_groups[1:]]
-    up_parts = near_groups + pair_groups + far_groups + far_pairs
-    embed_offsets = near + far + [offset ^ 1 for offset in near + far]
-    up_offsets = near + [offset ^ 1 for offset in near] + far + [offset ^ 1 for offset in far]
+    high_pairs = [high_pair] + [swapped(piece, "seq", 1) for piece in high_groups[1:]]
+    far_pairs = over_groups(far_pair)
+    up_parts = [own_groups, own_pairs, high_groups, high_pairs, far_groups, far_pairs]
+    far = [offset ^ low for offset in near + [offset ^ high for offset in near]]
+    up_offsets = [
+        [offset ^ bit for offset in offsets]
+        for offsets in (near, [offset ^ high for offset in near], far)
+        for bit in (0, 1)
+    ]
+    embed_offsets = near + [offset ^ high for offset in near]
+    for bit in (low, 1):
+        embed_offsets = embed_offsets + [offset ^ bit for offset in embed_offsets]
 
     begun = first_project(latents, out_weight, returned.pop(0), chunks, width) if chunks > 1 else None
     stepped, features = project_embed(
@@ -635,7 +646,7 @@
         embed_parts,
         norm_gain,
         group_count,
-        pair_groups[1:] + far_pairs,
+        [*high_pairs[1:], *far_pairs],
     )
     stepped_other = shifted(stepped, "dom", 1)
     features_other = shifted(features, "dom", 1)
@@ -645,10 +656,10 @@
     score = functools.partial(
         reward,
         ids,
-        weights=up_parts,
+        weights=[piece for pieces in up_parts for piece in pieces],
         parts=group_count,
         doms=dom_count,
-        offsets=up_offsets,
+        offsets=[offset for offsets in up_offsets for offset in offsets],
         head=head,
         particles=particles,
         scale=scale,

time: 198 us -> 176 us (0.89)
  waiting for transfers between devices: 89.2 us -> 59.1 us
  starting transfers between devices: 50.7 us -> 57.1 us
  other arithmetic: 0.78 us -> 5.01 us
  local copies, waits for them, and re-layouts: 14.4 us -> 11.8 us
    ppermute x12 -> x14, waiting for transfers between devices: 69 us -> 37.8 us  [swapped(): lax.ppermute(array, axis, [(i, i ^ bit) for i in range(lax.axis_size(axis...]
    all_to_all x4, starting transfers between devices: 19 us -> 22.6 us  [exchange(): return lax.all_to_all(array, 'seq', 0, 0, tiled=True)]
    concatenate x3 -> x2, other arithmetic: 0.14 us -> 2.81 us  [on_device(): jnp.concatenate([embed_share, swapped(embed_share, 'seq', bit)])]
    unnamed x58 -> x78, local copies, waits for them, and re-layouts: 13.4 us -> 10.8 us
    ppermute x12 -> x14, starting transfers between devices: 23.8 us -> 26.1 us  [swapped(): lax.ppermute(array, axis, [(i, i ^ bit) for i in range(lax.axis_size(axis...]
    ppermute x9 -> x10, waiting for transfers between devices: 20.2 us -> 21 us  [shifted(): lax.ppermute(array, axis, [(i, (i + step) % count) for i in range(count)])]
    ppermute x9 -> x10, starting transfers between devices: 7.91 us -> 8.38 us  [shifted(): lax.ppermute(array, axis, [(i, (i + step) % count) for i in range(count)])]
  transfers between devices with their start and end apart: 26 -> 29, of which waited for: 11 -> 12; matrix products, arithmetic and copies ran while one was open for 0% -> 2% of each run, Pallas kernels for 16% -> 18%
where the time goes in v10:
time: 176 us; the launch traced here: 175 us
  waiting for transfers between devices  59.1 us (34%)
  starting transfers between devices  57.1 us (32%)
  Pallas kernels  40.8 us (23%)
  local copies, waits for them, and re-layouts  11.8 us (7%)
  other arithmetic  5.01 us (3%)
    ppermute x14, waiting for transfers between devices, swapped(): lax.ppermute(array, axis, [(i, i ^ bit) for i in range(lax.axis_size(axis...  37.8 us
    ppermute x14, starting transfers between devices, swapped(): lax.ppermute(array, axis, [(i, i ^ bit) for i in range(lax.axis_size(axis...  26.1 us
    all_to_all x4, starting transfers between devices, exchange(): return lax.all_to_all(array, 'seq', 0, 0, tiled=True)  22.6 us
    ppermute x10, waiting for transfers between devices, shifted(): lax.ppermute(array, axis, [(i, (i + step) % count) for i in range(count)])  21 us
    pallas_call x2, Pallas kernels, attention(): pl.pallas_call(functools.partial(attention_kernel, head_width, block_sour...  13.8 us
    unnamed x78, local copies, waits for them, and re-layouts  10.8 us
    pallas_call x1, Pallas kernels, project_embed(): pl.pallas_call(kernel, in_specs=[smem, hbm, vmem, hbm] + ([] if begun is...  8.84 us
    ppermute x10, starting transfers between devices, shifted(): lax.ppermute(array, axis, [(i, (i + step) % count) for i in range(count)])  8.38 us
  transfers between devices with their start and end apart: 29, of which 12 were waited for; matrix products, arithmetic and copies ran while one was open for 2% of the time, Pallas kernels for 18%

profile of v10, /device:TPU:0, one launch (start us, length us, event | category | flops | bytes accessed | tf_op | source)
XLA Modules:
  0.0 175.4 jit_solution(16880239763633667221)
XLA Ops:
  1.6 4.0 %collective-permute-start = (bf16[1,192,256]{2,1,0:T(8,128)(2,1)S(1)}, bf16[1,192,256]{2,1,0:T(8,128)(2,1)S(1)}, u32[]{:S(2)}, u32[]{:S(2)}) collective-permute-start(bf16[1,192,256]{2,1,0:T(8,128)(2,1)S(1)} %dynamic-slice_bitcast_fusion.1), channel_id=1, source_target_pairs={{0,4},{1,5},{2,6},{3,7},{4,0},{5,1},{6,2},{7,3},{8,12},{9,13},{10,... | collective-permute-start | bytes 294920 | tf_op jit(solution)/shard_map/ppermute | solution.py:537
  5.7 3.3 %pack_heads.1 = (bf16[8,3,64,384]{3,2,1,0:T(8,128)(2,1)}, bf16[8,3,64,384]{3,2,1,0:T(8,128)(2,1)}) custom-call(bf16[4,64,1536]{2,1,0:T(8,128)(2,1)} %q_ref.1, bf16[4,64,1536]{2,1,0:T(8,128)(2,1)} %k_ref.1, bf16[4,64,1536]{2,1,0:T(8,128)(2,1)} %v_ref.1), custom_call_target="tpu_custom_call" | custom-call | tf_op jit(solution)/shard_map/pack_heads/pallas_call | solution.py:40
  8.9 1.6 collective-permute-done
  11.3 5.9 %all-to-all-start = ((bf16[8,3,64,384]{3,2,1,0:T(8,128)(2,1)}), bf16[8,3,64,384]{3,2,1,0:T(8,128)(2,1)S(1)}, u32[]{:S(2)}, u32[]{:S(2)}) async-start(bf16[8,3,64,384]{3,2,1,0:T(8,128)(2,1)} %gate.4), calls=%async_computation | async-start | bytes 2359296 | tf_op jit(solution)/shard_map/all_to_all | solution.py:541
  17.2 2.0 %collective-permute-start.7 = (bf16[2,192,256]{2,1,0:T(8,128)(2,1)S(1)}, bf16[2,192,256]{2,1,0:T(8,128)(2,1)S(1)}, u32[]{:S(2)}, u32[]{:S(2)}) collective-permute-start(bf16[2,192,256]{2,1,0:T(8,128)(2,1)S(1)} %copy-done.37), channel_id=1, source_target_pairs={{0,2},{1,3},{2,0},{3,1},{4,6},{5,7},{6,4},{7,5},{8,10},{9,11},{10,... | collective-permute-start | bytes 589832 | tf_op jit(solution)/shard_map/ppermute | solution.py:537
  19.2 22.1 %collective-permute-done.7 = bf16[2,192,256]{2,1,0:T(8,128)(2,1)S(1)} collective-permute-done((bf16[2,192,256]{2,1,0:T(8,128)(2,1)S(1)}, bf16[2,192,256]{2,1,0:T(8,128)(2,1)S(1)}, u32[]{:S(2)}, u32[]{:S(2)}) %collective-permute-start.7) | collective-permute-done | bytes 196640 | tf_op jit(solution)/shard_map/ppermute | solution.py:537
  43.3 4.4 %collective-permute-start.1 = (bf16[1,512,256]{2,1,0:T(8,128)(2,1)S(1)}, bf16[1,512,256]{2,1,0:T(8,128)(2,1)S(1)}, u32[]{:S(2)}, u32[]{:S(2)}) collective-permute-start(bf16[1,512,256]{2,1,0:T(8,128)(2,1)S(1)} %dynamic-slice_bitcast_fusion.refs_4_), channel_id=1, source_target_pairs={{0,4},{1,5},{2,6},{3,7},{4,0},{5,1},{6,2},{7,3},{8,12},{9,13},{10,... | collective-permute-start | bytes 786440 | tf_op jit(solution)/shard_map/ppermute | solution.py:537
  49.8 4.7 %collective-permute-done.8 = bf16[4,192,256]{2,1,0:T(8,128)(2,1)} collective-permute-done((bf16[4,192,256]{2,1,0:T(8,128)(2,1)}, bf16[4,192,256]{2,1,0:T(8,128)(2,1)}, u32[]{:S(2)}, u32[]{:S(2)}) %collective-permute-start.8) | collective-permute-done | bytes 393248 | tf_op jit(solution)/shard_map/ppermute | solution.py:537
  54.5 2.0 %pad_maximum_fusion.refs_2_.refs_6_ = bf16[8,192,256]{2,1,0:T(8,128)(2,1)} fusion(bf16[4,192,256]{2,1,0:T(8,128)(2,1)} %collective-permute-done.8, bf16[2,192,256]{2,1,0:T(8,128)(2,1)} %copy-done.38, bf16[1,192,256]{2,1,0:T(8,128)(2,1)S(1)} %collective-permute-done, bf16[1,192,256]{2,1,0:T(8,128)(2,1)S(1)} %dynamic-slice_bitcast_fusion.1), kind=kLoop, calls=%fused_computation | loop fusion | flops 1179648 | bytes 1572864 | tf_op jit(solution)/shard_map/concatenate | solution.py:600
  56.5 1.9 %collective-permute-done.1.refs_3_.refs_8_ = bf16[1,512,256]{2,1,0:T(8,128)(2,1)S(1)} collective-permute-done((bf16[1,512,256]{2,1,0:T(8,128)(2,1)S(1)}, bf16[1,512,256]{2,1,0:T(8,128)(2,1)S(1)}, u32[]{:S(2)}, u32[]{:S(2)}) %collective-permute-start.1) | collective-permute-done | bytes 262176 | tf_op jit(solution)/shard_map/ppermute | solution.py:537
  59.8 5.6 %all-to-all-start.1 = ((bf16[8,3,64,384]{3,2,1,0:T(8,128)(2,1)}), bf16[8,3,64,384]{3,2,1,0:T(8,128)(2,1)}, u32[]{:S(2)}, u32[]{:S(2)}) async-start(bf16[8,3,64,384]{3,2,1,0:T(8,128)(2,1)} %gate.5), calls=%async_computation.1 | async-start | bytes 2359296 | tf_op jit(solution)/shard_map/all_to_all | solution.py:541
  65.4 1.6 collective-permute-start.9
  67.8 2.0 %collective-permute-start.2 = (bf16[2,512,256]{2,1,0:T(8,128)(2,1)}, bf16[2,512,256]{2,1,0:T(8,128)(2,1)S(1)}, u32[]{:S(2)}, u32[]{:S(2)}) collective-permute-start(bf16[2,512,256]{2,1,0:T(8,128)(2,1)} %pad_maximum_fusion.1), channel_id=1, source_target_pairs={{0,2},{1,3},{2,0},{3,1},{4,6},{5,7},{6,4},{7,5},{8,10},{9,11},{10,... | collective-permute-start | bytes 1572872 | tf_op jit(solution)/shard_map/ppermute | solution.py:537
  72.3 16.8 %collective-permute-done.4.refs_3_.refs_9_ = bf16[1,512,256]{2,1,0:T(8,128)(2,1)S(1)} collective-permute-done((bf16[1,512,256]{2,1,0:T(8,128)(2,1)S(1)}, bf16[1,512,256]{2,1,0:T(8,128)(2,1)S(1)}, u32[]{:S(2)}, u32[]{:S(2)}) %collective-permute-start.4) | collective-permute-done | bytes 262176 | tf_op jit(solution)/shard_map/ppermute | solution.py:533
  89.7 6.9 %attention.2.refs_0_ = bf16[8,64,384]{2,1,0:T(8,128)(2,1)} custom-call(bf16[8,3,64,384]{3,2,1,0:T(8,128)(2,1)} %copy-done.35), custom_call_target="tpu_custom_call" | custom-call | flops 402653184 | bytes 1572864 | tf_op jit(solution)/shard_map/attention/pallas_call | solution.py:104
  97.7 5.4 %all-to-all-start.2 = ((bf16[8,64,384]{2,1,0:T(8,128)(2,1)}), bf16[8,64,384]{2,1,0:T(8,128)(2,1)}, u32[]{:S(2)}, u32[]{:S(2)}) async-start(bf16[8,64,384]{2,1,0:T(8,128)(2,1)} %gate.6), calls=%async_computation.2 | async-start | bytes 786432 | tf_op jit(solution)/shard_map/all_to_all | solution.py:541
  104.6 2.0 %collective-permute-start.15 = (bf16[2,512,256]{2,1,0:T(8,128)(2,1)}, bf16[2,512,256]{2,1,0:T(8,128)(2,1)S(1)}, u32[]{:S(2)}, u32[]{:S(2)}) collective-permute-start(bf16[2,512,256]{2,1,0:T(8,128)(2,1)} %copy-done.7), channel_id=1, source_target_pairs={{0,1},{1,0},{2,3},{3,2},{4,5},{5,4},{6,7},{7,6},{8,9},{9,8},{10,11... | collective-permute-start | bytes 1572872 | tf_op jit(solution)/shard_map/ppermute | solution.py:537
  106.6 6.9 %attention.3.refs_0_ = bf16[8,64,384]{2,1,0:T(8,128)(2,1)} custom-call(bf16[8,3,64,384]{3,2,1,0:T(8,128)(2,1)} %all-to-all-done.1.refs_6_.qkv_ref), custom_call_target="tpu_custom_call" | custom-call | flops 402653184 | bytes 1572864 | tf_op jit(solution)/shard_map/attention/pallas_call | solution.py:104
  113.5 3.4 %collective-permute-done.11.refs_2_.refs_13_ = bf16[2,512,256]{2,1,0:T(8,128)(2,1)S(1)} collective-permute-done((bf16[2,512,256]{2,1,0:T(8,128)(2,1)}, bf16[2,512,256]{2,1,0:T(8,128)(2,1)S(1)}, u32[]{:S(2)}, u32[]{:S(2)}) %collective-permute-start.11) | collective-permute-done | bytes 524320 | tf_op jit(solution)/shard_map/ppermute | solution.py:533
  117.7 5.7 %all-to-all-start.3 = ((bf16[8,64,384]{2,1,0:T(8,128)(2,1)}), bf16[8,64,384]{2,1,0:T(8,128)(2,1)S(1)}, u32[]{:S(2)}, u32[]{:S(2)}) async-start(bf16[8,64,384]{2,1,0:T(8,128)(2,1)} %gate.7), calls=%async_computation.3 | async-start | bytes 786432 | tf_op jit(solution)/shard_map/all_to_all | solution.py:541
  123.5 1.6 collective-permute-start.16
  125.0 2.0 %collective-permute-start.14 = (bf16[1,512,256]{2,1,0:T(8,128)(2,1)S(1)}, bf16[1,512,256]{2,1,0:T(8,128)(2,1)S(1)}, u32[]{:S(2)}, u32[]{:S(2)}) collective-permute-start(bf16[1,512,256]{2,1,0:T(8,128)(2,1)S(1)} %copy-done.20), channel_id=1, source_target_pairs={{0,1},{1,0},{2,3},{3,2},{4,5},{5,4},{6,7},{7,6},{8,9},{9,8},{10,11... | collective-permute-start | bytes 786440 | tf_op jit(solution)/shard_map/ppermute | solution.py:537
  128.4 4.7 %first_project.1.refs_4_ = f32[256,1536]{1,0:T(8,128)} custom-call(bf16[4,64,1536]{2,1,0:T(8,128)(2,1)} %refs_1_.1, bf16[1536,1536]{1,0:T(8,128)(2,1)} %refs_3_.2, bf16[8,64,384]{2,1,0:T(8,128)(2,1)} %all-to-all-done.2.piece_ref.refs_1_), custom_call_target="tpu_custom_call" | custom-call | flops 603979776 | bytes 5505024 | tf_op jit(solution)/shard_map/first_project/pallas_call | solution.py:181
  133.0 1.9 %collective-permute-done.14.refs_10_.refs_11_ = bf16[1,512,256]{2,1,0:T(8,128)(2,1)S(1)} collective-permute-done((bf16[1,512,256]{2,1,0:T(8,128)(2,1)S(1)}, bf16[1,512,256]{2,1,0:T(8,128)(2,1)S(1)}, u32[]{:S(2)}, u32[]{:S(2)}) %collective-permute-start.14) | collective-permute-done | bytes 262176 | tf_op jit(solution)/shard_map/ppermute | solution.py:537
  136.7 8.8 %project_embed.1 = (bf16[4,64,1536]{2,1,0:T(8,128)(2,1)}, bf16[2,256,512]{2,1,0:T(8,128)(2,1)}) custom-call(s32[4]{0:T(128)} %pad_add_fusion.refs_0_.ids_ref, bf16[4,64,1536]{2,1,0:T(8,128)(2,1)} %refs_1_.1, f32[1,1024]{1,0:T(1,128)} %bitcast.12, bf16[1536,1536]{1,0:T(8,128)(2,1)} %refs_3_.2, f32[256,1536]{1,0:T(8,128)} %first_project.1.refs_4_, ...), custom_call_target="tpu_custom_call" | custom-call | flops 1409286144 | bytes 10223616 | tf_op jit(solution)/shard_map/project_embed/pallas_call | solution.py:331
  153.1 3.5 %reward.2.refs_3_ = f32[8,128]{1,0:T(8,128)S(1)} custom-call(s32[4]{0:T(128)S(1)} %copy-done.31, bf16[2,256,512]{2,1,0:T(8,128)(2,1)S(1)} %copy-done.29, f32[16,1,256]{2,1,0:T(1,128)S(1)} %bitcast.10, f32[4]{0:T(128)S(1)} %copy-done.32, bf16[1,512,256]{2,1,0:T(8,128)(2,1)S(1)} %copy-done.12, bf16[1,512,256]{2,1,0:T(8,128)(2,1)S(1)} %copy-done.15, ...), custom_call_target="tpu_custom_call" | custom-call | flops 1073741824 | bytes 4194304 | tf_op jit(solution)/shard_map/reward/pallas_call | solution.py:435
  156.6 3.5 %reward.3.refs_0_ = f32[8,128]{1,0:T(8,128)S(1)} custom-call(s32[4]{0:T(128)S(1)} %copy-done.31, bf16[2,256,512]{2,1,0:T(8,128)(2,1)S(1)} %collective-permute-done.18.refs_1_, f32[16,1,256]{2,1,0:T(1,128)S(1)} %bitcast.11, f32[8,128]{1,0:T(8,128)S(1)} %reward.2.refs_3_, bf16[1,512,256]{2,1,0:T(8,128)(2,1)S(1)} %copy-done.12, ...), custom_call_target="tpu_custom_call" | custom-call | flops 1073741824 | bytes 4194304 | tf_op jit(solution)/shard_map/reward/pallas_call | solution.py:435
  160.1 1.8 %collective-permute-start.19 = (f32[8,128]{1,0:T(8,128)S(1)}, f32[8,128]{1,0:T(8,128)S(1)}, u32[]{:S(2)}, u32[]{:S(2)}) collective-permute-start(f32[8,128]{1,0:T(8,128)S(1)} %reward.3.refs_0_), channel_id=1, source_target_pairs={{0,2},{1,3},{2,0},{3,1},{4,6},{5,7},{6,4},{7,5},{8,10},{9,11},{10,... | collective-permute-start | bytes 12296 | tf_op jit(solution)/shard_map/ppermute | solution.py:537
  161.9 2.4 %collective-permute-start.20 = (f32[8,128]{1,0:T(8,128)S(1)}, f32[8,128]{1,0:T(8,128)S(1)}, u32[]{:S(2)}, u32[]{:S(2)}) collective-permute-start(f32[8,128]{1,0:T(8,128)S(1)} %reward.3.refs_0_), channel_id=1, source_target_pairs={{0,4},{1,5},{2,6},{3,7},{4,0},{5,1},{6,2},{7,3},{8,12},{9,13},{10,... | collective-permute-start | bytes 12296 | tf_op jit(solution)/shard_map/ppermute | solution.py:537
  164.5 1.9 %collective-permute-done.20.refs_2_ = f32[8,128]{1,0:T(8,128)S(1)} collective-permute-done((f32[8,128]{1,0:T(8,128)S(1)}, f32[8,128]{1,0:T(8,128)S(1)}, u32[]{:S(2)}, u32[]{:S(2)}) %collective-permute-start.20) | collective-permute-done | bytes 4128 | tf_op jit(solution)/shard_map/ppermute | solution.py:537
  166.4 3.2 %collective-permute-done.21.refs_3_ = f32[8,128]{1,0:T(8,128)S(1)} collective-permute-done((f32[8,128]{1,0:T(8,128)S(1)}, f32[8,128]{1,0:T(8,128)S(1)}, u32[]{:S(2)}, u32[]{:S(2)}) %collective-permute-start.21) | collective-permute-done | bytes 4128 | tf_op jit(solution)/shard_map/ppermute | solution.py:537
  171.8 2.0 %resample.1.resampled_ref = bf16[4,64,1536]{2,1,0:T(8,128)(2,1)} custom-call(s32[4]{0:T(128)S(1)} %copy-done.31, s32[4]{0:T(128)S(1)} %copy-done.33, bf16[4,64,1536]{2,1,0:T(8,128)(2,1)S(1)} %copy-done.28, bf16[4,64,1536]{2,1,0:T(8,128)(2,1)S(1)} %collective-permute-done.17.other_ref), custom_call_target="tpu_custom_call" | custom-call | tf_op jit(solution)/shard_map/resample/pallas_call | solution.py:517
  (125 shorter events, 28.2 us)
Async XLA Ops:
  0.6 42.7 %copy-start = (bf16[1024,512]{1,0:T(8,128)(2,1)S(1)}, bf16[1024,512]{1,0:T(8,128)(2,1)}, u32[]{:S(2)}) copy-start(bf16[1024,512]{1,0:T(8,128)(2,1)} %param.20) | copy-start | bytes 3145732
  1.6 8.9 %collective-permute-start = (bf16[1,192,256]{2,1,0:T(8,128)(2,1)S(1)}, bf16[1,192,256]{2,1,0:T(8,128)(2,1)S(1)}, u32[]{:S(2)}, u32[]{:S(2)}) collective-permute-start(bf16[1,192,256]{2,1,0:T(8,128)(2,1)S(1)} %dynamic-slice_bitcast_fusion.1), channel_id=1, source_target_pairs={{0,4},{1,5},{2,6},{3,7},{4,0},{5,1},{6,2},{7,3},{8,12},{9,13},{10,... | collective-permute-start | bytes 294920 | tf_op jit(solution)/shard_map/ppermute | solution.py:537
  11.3 47.2 %all-to-all-start = ((bf16[8,3,64,384]{3,2,1,0:T(8,128)(2,1)}), bf16[8,3,64,384]{3,2,1,0:T(8,128)(2,1)S(1)}, u32[]{:S(2)}, u32[]{:S(2)}) async-start(bf16[8,3,64,384]{3,2,1,0:T(8,128)(2,1)} %gate.4), calls=%async_computation | async-start | bytes 2359296 | tf_op jit(solution)/shard_map/all_to_all | solution.py:541
  17.2 24.2 %collective-permute-start.7 = (bf16[2,192,256]{2,1,0:T(8,128)(2,1)S(1)}, bf16[2,192,256]{2,1,0:T(8,128)(2,1)S(1)}, u32[]{:S(2)}, u32[]{:S(2)}) collective-permute-start(bf16[2,192,256]{2,1,0:T(8,128)(2,1)S(1)} %copy-done.37), channel_id=1, source_target_pairs={{0,2},{1,3},{2,0},{3,1},{4,6},{5,7},{6,4},{7,5},{8,10},{9,11},{10,... | collective-permute-start | bytes 589832 | tf_op jit(solution)/shard_map/ppermute | solution.py:537
  42.2 12.4 %collective-permute-start.8 = (bf16[4,192,256]{2,1,0:T(8,128)(2,1)}, bf16[4,192,256]{2,1,0:T(8,128)(2,1)}, u32[]{:S(2)}, u32[]{:S(2)}) collective-permute-start(bf16[4,192,256]{2,1,0:T(8,128)(2,1)} %pad_maximum_fusion.2), channel_id=1, source_target_pairs={{0,1},{1,0},{2,3},{3,2},{4,5},{5,4},{6,7},{7,6},{8,9},{9,8},{10,11... | collective-permute-start | bytes 1179656 | tf_op jit(solution)/shard_map/ppermute | solution.py:537
  43.3 23.6 %copy-start.11 = (bf16[1,512,256]{2,1,0:T(8,128)(2,1)}, bf16[1,512,256]{2,1,0:T(8,128)(2,1)S(1)}, u32[]{:S(2)}) copy-start(bf16[1,512,256]{2,1,0:T(8,128)(2,1)S(1)} %dynamic-slice_bitcast_fusion.refs_4_) | copy-start | bytes 786436
  43.3 15.1 %collective-permute-start.1 = (bf16[1,512,256]{2,1,0:T(8,128)(2,1)S(1)}, bf16[1,512,256]{2,1,0:T(8,128)(2,1)S(1)}, u32[]{:S(2)}, u32[]{:S(2)}) collective-permute-start(bf16[1,512,256]{2,1,0:T(8,128)(2,1)S(1)} %dynamic-slice_bitcast_fusion.refs_4_), channel_id=1, source_target_pairs={{0,4},{1,5},{2,6},{3,7},{4,0},{5,1},{6,2},{7,3},{8,12},{9,13},{10,... | collective-permute-start | bytes 786440 | tf_op jit(solution)/shard_map/ppermute | solution.py:537
  47.7 10.7 %collective-permute-start.5 = (bf16[1,512,256]{2,1,0:T(8,128)(2,1)S(1)}, bf16[1,512,256]{2,1,0:T(8,128)(2,1)S(1)}, u32[]{:S(2)}, u32[]{:S(2)}) collective-permute-start(bf16[1,512,256]{2,1,0:T(8,128)(2,1)S(1)} %dynamic-slice_bitcast_fusion.refs_4_), channel_id=1, source_target_pairs={{0,16},{16,0},{1,17},{17,1},{2,18},{18,2},{3,19},{19,3},{4,20},{20... | collective-permute-start | bytes 786440 | tf_op jit(solution)/shard_map/ppermute | solution.py:533
  49.2 9.2 %collective-permute-start.10 = (bf16[1,512,256]{2,1,0:T(8,128)(2,1)S(1)}, bf16[1,512,256]{2,1,0:T(8,128)(2,1)S(1)}, u32[]{:S(2)}, u32[]{:S(2)}) collective-permute-start(bf16[1,512,256]{2,1,0:T(8,128)(2,1)S(1)} %dynamic-slice_bitcast_fusion.refs_4_), channel_id=1, source_target_pairs={{0,1},{1,0},{2,3},{3,2},{4,5},{5,4},{6,7},{7,6},{8,9},{9,8},{10,11... | collective-permute-start | bytes 786440 | tf_op jit(solution)/shard_map/ppermute | solution.py:537
  59.8 37.2 %all-to-all-start.1 = ((bf16[8,3,64,384]{3,2,1,0:T(8,128)(2,1)}), bf16[8,3,64,384]{3,2,1,0:T(8,128)(2,1)}, u32[]{:S(2)}, u32[]{:S(2)}) async-start(bf16[8,3,64,384]{3,2,1,0:T(8,128)(2,1)} %gate.5), calls=%async_computation.1 | async-start | bytes 2359296 | tf_op jit(solution)/shard_map/all_to_all | solution.py:541
  65.4 23.8 %collective-permute-start.9 = (bf16[8,192,256]{2,1,0:T(8,128)(2,1)S(1)}, bf16[8,192,256]{2,1,0:T(8,128)(2,1)}, u32[]{:S(2)}, u32[]{:S(2)}) collective-permute-start(bf16[8,192,256]{2,1,0:T(8,128)(2,1)S(1)} %copy-done.34), channel_id=1, source_target_pairs={{0,16},{16,0},{1,17},{17,1},{2,18},{18,2},{3,19},{19,3},{4,20},{20... | collective-permute-start | bytes 2359304 | tf_op jit(solution)/shard_map/ppermute | solution.py:533
  67.8 29.1 %collective-permute-start.2 = (bf16[2,512,256]{2,1,0:T(8,128)(2,1)}, bf16[2,512,256]{2,1,0:T(8,128)(2,1)S(1)}, u32[]{:S(2)}, u32[]{:S(2)}) collective-permute-start(bf16[2,512,256]{2,1,0:T(8,128)(2,1)} %pad_maximum_fusion.1), channel_id=1, source_target_pairs={{0,2},{1,3},{2,0},{3,1},{4,6},{5,7},{6,4},{7,5},{8,10},{9,11},{10,... | collective-permute-start | bytes 1572872 | tf_op jit(solution)/shard_map/ppermute | solution.py:537
  69.8 19.4 %collective-permute-start.4 = (bf16[1,512,256]{2,1,0:T(8,128)(2,1)S(1)}, bf16[1,512,256]{2,1,0:T(8,128)(2,1)S(1)}, u32[]{:S(2)}, u32[]{:S(2)}) collective-permute-start(bf16[1,512,256]{2,1,0:T(8,128)(2,1)S(1)} %copy-done.10), channel_id=1, source_target_pairs={{0,16},{16,0},{1,17},{17,1},{2,18},{18,2},{3,19},{19,3},{4,20},{20... | collective-permute-start | bytes 786440 | tf_op jit(solution)/shard_map/ppermute | solution.py:533
  70.3 26.3 %collective-permute-start.3 = (bf16[1,512,256]{2,1,0:T(8,128)(2,1)S(1)}, bf16[1,512,256]{2,1,0:T(8,128)(2,1)S(1)}, u32[]{:S(2)}, u32[]{:S(2)}) collective-permute-start(bf16[1,512,256]{2,1,0:T(8,128)(2,1)S(1)} %copy-done.10), channel_id=1, source_target_pairs={{0,1},{1,0},{2,3},{3,2},{4,5},{5,4},{6,7},{7,6},{8,9},{9,8},{10,11... | collective-permute-start | bytes 786440 | tf_op jit(solution)/shard_map/ppermute | solution.py:537
  71.8 24.8 %collective-permute-start.6 = (bf16[1,512,256]{2,1,0:T(8,128)(2,1)S(1)}, bf16[1,512,256]{2,1,0:T(8,128)(2,1)S(1)}, u32[]{:S(2)}, u32[]{:S(2)}) collective-permute-start(bf16[1,512,256]{2,1,0:T(8,128)(2,1)S(1)} %copy-done.14), channel_id=1, source_target_pairs={{0,1},{1,0},{2,3},{3,2},{4,5},{5,4},{6,7},{7,6},{8,9},{9,8},{10,11... | collective-permute-start | bytes 786440 | tf_op jit(solution)/shard_map/ppermute | solution.py:537
  89.1 27.8 %collective-permute-start.12 = (bf16[8,192,256]{2,1,0:T(8,128)(2,1)S(1)}, bf16[8,192,256]{2,1,0:T(8,128)(2,1)}, u32[]{:S(2)}, u32[]{:S(2)}) collective-permute-start(bf16[8,192,256]{2,1,0:T(8,128)(2,1)S(1)} %copy-done.34), channel_id=1, source_target_pairs={{0,8},{8,0},{1,9},{9,1},{2,10},{10,2},{3,11},{11,3},{4,12},{12,4},... | collective-permute-start | bytes 2359304 | tf_op jit(solution)/shard_map/ppermute | solution.py:533
  89.2 27.8 %collective-permute-start.13 = (bf16[8,192,256]{2,1,0:T(8,128)(2,1)}, bf16[8,192,256]{2,1,0:T(8,128)(2,1)}, u32[]{:S(2)}, u32[]{:S(2)}) collective-permute-start(bf16[8,192,256]{2,1,0:T(8,128)(2,1)} %collective-permute-done.9.refs_5_.refs_7_), channel_id=1, source_target_pairs={{0,8},{8,0},{1,9},{9,1},{2,10},{10,2},{3,11},{11,3},{4,12},{12,4},... | collective-permute-start | bytes 2359304 | tf_op jit(solution)/shard_map/ppermute | solution.py:533
  97.7 19.2 %all-to-all-start.2 = ((bf16[8,64,384]{2,1,0:T(8,128)(2,1)}), bf16[8,64,384]{2,1,0:T(8,128)(2,1)}, u32[]{:S(2)}, u32[]{:S(2)}) async-start(bf16[8,64,384]{2,1,0:T(8,128)(2,1)} %gate.6), calls=%async_computation.2 | async-start | bytes 786432 | tf_op jit(solution)/shard_map/all_to_all | solution.py:541
  103.1 13.8 %collective-permute-start.11 = (bf16[2,512,256]{2,1,0:T(8,128)(2,1)}, bf16[2,512,256]{2,1,0:T(8,128)(2,1)S(1)}, u32[]{:S(2)}, u32[]{:S(2)}) collective-permute-start(bf16[2,512,256]{2,1,0:T(8,128)(2,1)} %copy-done.7), channel_id=1, source_target_pairs={{0,16},{16,0},{1,17},{17,1},{2,18},{18,2},{3,19},{19,3},{4,20},{20... | collective-permute-start | bytes 1572872 | tf_op jit(solution)/shard_map/ppermute | solution.py:533
  104.6 18.9 %collective-permute-start.15 = (bf16[2,512,256]{2,1,0:T(8,128)(2,1)}, bf16[2,512,256]{2,1,0:T(8,128)(2,1)S(1)}, u32[]{:S(2)}, u32[]{:S(2)}) collective-permute-start(bf16[2,512,256]{2,1,0:T(8,128)(2,1)} %copy-done.7), channel_id=1, source_target_pairs={{0,1},{1,0},{2,3},{3,2},{4,5},{5,4},{6,7},{7,6},{8,9},{9,8},{10,11... | collective-permute-start | bytes 1572872 | tf_op jit(solution)/shard_map/ppermute | solution.py:537
  117.7 17.9 %all-to-all-start.3 = ((bf16[8,64,384]{2,1,0:T(8,128)(2,1)}), bf16[8,64,384]{2,1,0:T(8,128)(2,1)S(1)}, u32[]{:S(2)}, u32[]{:S(2)}) async-start(bf16[8,64,384]{2,1,0:T(8,128)(2,1)} %gate.7), calls=%async_computation.3 | async-start | bytes 786432 | tf_op jit(solution)/shard_map/all_to_all | solution.py:541
  123.5 12.2 %collective-permute-start.16 = (bf16[2,512,256]{2,1,0:T(8,128)(2,1)S(1)}, bf16[2,512,256]{2,1,0:T(8,128)(2,1)S(1)}, u32[]{:S(2)}, u32[]{:S(2)}) collective-permute-start(bf16[2,512,256]{2,1,0:T(8,128)(2,1)S(1)} %collective-permute-done.15.refs_11_.refs_14_), channel_id=1, source_target_pairs={{0,16},{16,0},{1,17},{17,1},{2,18},{18,2},{3,19},{19,3},{4,20},{20... | collective-permute-start | bytes 1572872 | tf_op jit(solution)/shard_map/ppermute | solution.py:533
  125.0 9.9 %collective-permute-start.14 = (bf16[1,512,256]{2,1,0:T(8,128)(2,1)S(1)}, bf16[1,512,256]{2,1,0:T(8,128)(2,1)S(1)}, u32[]{:S(2)}, u32[]{:S(2)}) collective-permute-start(bf16[1,512,256]{2,1,0:T(8,128)(2,1)S(1)} %copy-done.20), channel_id=1, source_target_pairs={{0,1},{1,0},{2,3},{3,2},{4,5},{5,4},{6,7},{7,6},{8,9},{9,8},{10,11... | collective-permute-start | bytes 786440 | tf_op jit(solution)/shard_map/ppermute | solution.py:537
  145.6 26.2 %collective-permute-start.17 = (bf16[4,64,1536]{2,1,0:T(8,128)(2,1)}, bf16[4,64,1536]{2,1,0:T(8,128)(2,1)S(1)}, u32[]{:S(2)}, u32[]{:S(2)}) collective-permute-start(bf16[4,64,1536]{2,1,0:T(8,128)(2,1)} %get-tuple-element.10.own_ref), channel_id=1, source_target_pairs={{0,8},{8,0},{1,9},{9,1},{2,10},{10,2},{3,11},{11,3},{4,12},{12,4},... | collective-permute-start | bytes 2359304 | tf_op jit(solution)/shard_map/ppermute | solution.py:533
  145.7 10.9 %collective-permute-start.18 = (bf16[2,256,512]{2,1,0:T(8,128)(2,1)}, bf16[2,256,512]{2,1,0:T(8,128)(2,1)S(1)}, u32[]{:S(2)}, u32[]{:S(2)}) collective-permute-start(bf16[2,256,512]{2,1,0:T(8,128)(2,1)} %get-tuple-element.11.refs_1_), channel_id=1, source_target_pairs={{0,8},{8,0},{1,9},{9,1},{2,10},{10,2},{3,11},{11,3},{4,12},{12,4},... | collective-permute-start | bytes 1572872 | tf_op jit(solution)/shard_map/ppermute | solution.py:533
  156.5 15.3 %copy-start.28 = (bf16[4,64,1536]{2,1,0:T(8,128)(2,1)S(1)}, bf16[4,64,1536]{2,1,0:T(8,128)(2,1)}, u32[]{:S(2)}) copy-start(bf16[4,64,1536]{2,1,0:T(8,128)(2,1)} %get-tuple-element.10.own_ref) | copy-start | bytes 2359300
  160.1 4.5 %collective-permute-start.19 = (f32[8,128]{1,0:T(8,128)S(1)}, f32[8,128]{1,0:T(8,128)S(1)}, u32[]{:S(2)}, u32[]{:S(2)}) collective-permute-start(f32[8,128]{1,0:T(8,128)S(1)} %reward.3.refs_0_), channel_id=1, source_target_pairs={{0,2},{1,3},{2,0},{3,1},{4,6},{5,7},{6,4},{7,5},{8,10},{9,11},{10,... | collective-permute-start | bytes 12296 | tf_op jit(solution)/shard_map/ppermute | solution.py:537
  161.9 4.5 %collective-permute-start.20 = (f32[8,128]{1,0:T(8,128)S(1)}, f32[8,128]{1,0:T(8,128)S(1)}, u32[]{:S(2)}, u32[]{:S(2)}) collective-permute-start(f32[8,128]{1,0:T(8,128)S(1)} %reward.3.refs_0_), channel_id=1, source_target_pairs={{0,4},{1,5},{2,6},{3,7},{4,0},{5,1},{6,2},{7,3},{8,12},{9,13},{10,... | collective-permute-start | bytes 12296 | tf_op jit(solution)/shard_map/ppermute | solution.py:537
  164.2 5.4 %collective-permute-start.21 = (f32[8,128]{1,0:T(8,128)S(1)}, f32[8,128]{1,0:T(8,128)S(1)}, u32[]{:S(2)}, u32[]{:S(2)}) collective-permute-start(f32[8,128]{1,0:T(8,128)S(1)} %reward.3.refs_0_), channel_id=1, source_target_pairs={{0,6},{1,7},{2,4},{3,5},{4,2},{5,3},{6,0},{7,1},{8,14},{9,15},{10,... | collective-permute-start | bytes 12296 | tf_op jit(solution)/shard_map/ppermute | solution.py:537
  169.7 4.2 %collective-permute-start.22 = (f32[8,128]{1,0:T(8,128)S(1)}, f32[8,128]{1,0:T(8,128)S(1)}, u32[]{:S(2)}, u32[]{:S(2)}) collective-permute-start(f32[8,128]{1,0:T(8,128)S(1)} %add_partials.1.refs_0_), channel_id=1, source_target_pairs={{0,1},{1,0},{2,3},{3,2},{4,5},{5,4},{6,7},{7,6},{8,9},{9,8},{10,11... | collective-permute-start | bytes 12296 | tf_op jit(solution)/shard_map/ppermute | solution.py:537
  171.1 3.0 %collective-permute-start.23 = (f32[8,128]{1,0:T(8,128)S(1)}, f32[8,128]{1,0:T(8,128)S(1)}, u32[]{:S(2)}, u32[]{:S(2)}) collective-permute-start(f32[8,128]{1,0:T(8,128)S(1)} %add_partials.1.refs_0_), channel_id=1, source_target_pairs={{0,9},{1,8},{2,11},{3,10},{4,13},{5,12},{6,15},{7,14},{8,1},{9,0},... | collective-permute-start | bytes 12296 | tf_op jit(solution)/shard_map/ppermute | solution.py:678
  171.1 3.0 %collective-permute-start.24 = (f32[8,128]{1,0:T(8,128)S(1)}, f32[8,128]{1,0:T(8,128)S(1)}, u32[]{:S(2)}, u32[]{:S(2)}) collective-permute-start(f32[8,128]{1,0:T(8,128)S(1)} %add_partials.1.refs_0_), channel_id=1, source_target_pairs={{0,8},{8,0},{1,9},{9,1},{2,10},{10,2},{3,11},{11,3},{4,12},{12,4},... | collective-permute-start | bytes 12296 | tf_op jit(solution)/shard_map/ppermute | solution.py:533
  (36 other events, 172.1 us)

commit v11 on v10

v11 whole, which is shorter than its diff:
```python
import functools
import math

import jax
import jax.numpy as jnp
from jax import lax
from jax.experimental import pallas as pl
from jax.experimental.pallas import tpu as pltpu
from jax.sharding import PartitionSpec as P

HEADS = 24
STEPS = 28
LANES = 128

potential_scale = 4.0
norm_eps = 1e-05
MIB = 1024 * 1024


def pack_kernel(splits, width, q_ref, k_ref, v_ref, *out_refs):
    particles, _, model_width = q_ref.shape
    blocks = model_width // width
    for index, ref in enumerate((q_ref, k_ref, v_ref)):
        for particle in range(particles):
            for block in range(blocks):
                for out_ref, (start, size) in zip(out_refs, splits):
                    first = block * width + start
                    out_ref[particle * blocks + block, index] = ref[
                        particle, :, first : first + size
                    ]


def pack(queries, keys, values, splits, width):
    particles, tokens, model_width = queries.shape
    count = particles * model_width // width
    vmem = pl.BlockSpec(memory_space=pltpu.VMEM)
    return list(
        pl.pallas_call(
            functools.partial(pack_kernel, splits, width),
            in_specs=[vmem] * 3,
            out_specs=[vmem] * len(splits),
            out_shape=[
                jax.ShapeDtypeStruct((count, 3, tokens, size), queries.dtype)
                for _, size in splits
            ],
            compiler_params=pltpu.CompilerParams(vmem_limit_bytes=60 * MIB),
            name="pack_heads",
        )(queries, keys, values)
    )


def gate_kernel(*refs):
    pass


def gate(array, after):
    hbm = pl.BlockSpec(memory_space=pltpu.HBM)
    return pl.pallas_call(
        gate_kernel,
        in_specs=[hbm] + [pl.BlockSpec(memory_space=pl.ANY)] * len(after),
        out_specs=hbm,
        out_shape=jax.ShapeDtypeStruct(array.shape, array.dtype),
        input_output_aliases={0: 0},
        compiler_params=pltpu.CompilerParams(vmem_limit_bytes=60 * MIB),
        name="gate",
    )(array, *after)


def attention_kernel(head_width, block_sources, qkv_ref, *refs):
    out_ref = refs[-1]
    sources, _, tokens, columns = qkv_ref.shape
    total = sources * tokens
    rows = block_sources * tokens
    factor = 1.0 / math.sqrt(head_width) / math.log(2.0)
    k_all = qkv_ref[:, 1].reshape(total, columns)
    v_all = qkv_ref[:, 2].reshape(total, columns)
    for block in range(0, sources, block_sources):
        span = slice(block, block + block_sources)
        q_all = qkv_ref[span, 0].reshape(rows, columns)
        pieces = []
        for head in range(columns // head_width):
            cols = slice(head * head_width, (head + 1) * head_width)
            scores = lax.dot_general(
                q_all[:, cols],
                k_all[:, cols],
                (((1,), (1,)), ((), ())),
                preferred_element_type=jnp.float32,
            )
            highest = jnp.max(scores, axis=1, keepdims=True)
            expanded = jnp.exp2((scores - highest) * factor)
            norm = 1.0 / jnp.sum(expanded, axis=1, keepdims=True)
            weights = (expanded * norm).astype(jnp.bfloat16)
            pieces.append(jnp.dot(weights, v_all[:, cols], preferred_element_type=jnp.float32))
        joined = jnp.concatenate(pieces, axis=1).astype(jnp.bfloat16)
        out_ref[span] = joined.reshape(block_sources, tokens, columns)


def attention(qkv, head_width, width, start, earlier, after):
    sources, _, tokens, columns = qkv.shape
    total = sources * tokens
    block_sources = max(1, min(sources, 512 // tokens))
    while sources % block_sources:
        block_sources -= 1
    step = LANES if columns % LANES == 0 and LANES % head_width == 0 else columns
    first = start // step
    unread = earlier + after
    return pl.pallas_call(
        functools.partial(attention_kernel, head_width, block_sources),
        grid=(columns // step,),
        in_specs=[pl.BlockSpec((sources, 3, tokens, step), lambda i: (0, 0, 0, i))]
        + [pl.BlockSpec(memory_space=pl.ANY)] * len(unread),
        out_specs=pl.BlockSpec((sources, tokens, step), lambda i: (0, 0, first + i)),
        out_shape=jax.ShapeDtypeStruct((sources, tokens, width), jnp.bfloat16),
        input_output_aliases={1: 0} if earlier else {},
        compiler_params=pltpu.CompilerParams(vmem_limit_bytes=60 * MIB),
        cost_estimate=pl.CostEstimate(
            flops=4 * total * total * columns,
            bytes_accessed=8 * total * columns,
            transcendentals=columns // head_width * total * total,
        ),
        name="attention",
    )(qkv, *unread)


def column_block(model_width):
    return 512 if model_width % 512 == 0 else model_width


def project_kernel(parts, offsets, depth_parts, refs_in, refs_out):
    ids_ref, latents_hbm, gain_ref, out_weight_ref, attended_ref = refs_in[:5]
    weight_refs = refs_in[5 : 5 + parts]
    stepped_ref, features_ref = refs_out[:2]
    out_vmem, weight_vmem, rows_ref, clean_ref, embedded_ref, latents_ref = refs_out[2:8]
    out_sems, sems = refs_out[8:]
    dom, group, seq = ids_ref[0], ids_ref[1], ids_ref[2]
    sigma = ids_ref[3].astype(jnp.float32) * (1.0 / STEPS)
    particles, tokens, model_width = latents_ref.shape
    rows = particles * tokens
    shards, depth, columns = weight_refs[0].shape

    block = column_block(model_width)
    first_copies = []
    for index in range(model_width // block):
        cols = slice(index * block, (index + 1) * block)
        first_copies += [
            pltpu.make_async_copy(
                out_weight_ref.at[:, cols], out_vmem.at[:, cols], out_sems.at[0, index]
            ),
            pltpu.make_async_copy(
                latents_hbm.at[:, :, cols], latents_ref.at[:, :, cols], out_sems.at[1, index]
            ),
        ]
    copies = []
    for index in range(parts):
        for shard in range(shards):
            start = pl.multiple_of((seq ^ offsets[shard]) * depth, depth)
            copies.append(
                pltpu.make_async_copy(
                    weight_refs[index].at[shard],
                    weight_vmem.at[index, pl.ds(start, depth)],
                    sems.at[index],
                )
            )
    for copy in first_copies + copies:
        copy.start()

    count, _, width = attended_ref.shape
    blocks = count // particles
    for piece in range(count):
        particle, place = divmod(piece, blocks)
        rows_ref[
            particle * tokens : (particle + 1) * tokens, place * width : (place + 1) * width
        ] = attended_ref[piece]
    for index in range(model_width // block):
        cols = slice(index * block, (index + 1) * block)
        for copy in first_copies[2 * index : 2 * index + 2]:
            copy.wait()
        flat = latents_ref[:, :, cols].reshape(rows, block).astype(jnp.float32)
        velocity = flat + jnp.dot(
            rows_ref[...], out_vmem[:, cols], preferred_element_type=jnp.float32
        )
        clean_ref[:, cols] = (flat - sigma * velocity).astype(jnp.bfloat16)
        stepped_ref[:, :, cols] = (
            (flat - velocity * (1.0 / STEPS)).astype(jnp.bfloat16).reshape(particles, tokens, block)
        )

    for index in range(parts):
        for copy in copies[index * shards : (index + 1) * shards]:
            copy.wait()
        doms = parts // depth_parts
        dom_of = (dom + doms - index // depth_parts) % doms
        group_of = (group + depth_parts - index % depth_parts) % depth_parts
        embedded_ref[dom_of * depth_parts + group_of] = jnp.dot(
            clean_ref[...], weight_vmem[index], preferred_element_type=jnp.float32
        )
    count = parts * columns
    blocks = [embedded_ref[index] for index in range(parts)]
    centre = sum(jnp.sum(piece, axis=1, keepdims=True) for piece in blocks) * (1.0 / count)
    blocks = [piece - centre for piece in blocks]
    variance = sum(jnp.sum(piece * piece, axis=1, keepdims=True) for piece in blocks) * (
        1.0 / count
    )
    inverse = lax.rsqrt(variance + norm_eps)
    share = features_ref.shape[2]
    for index, piece in enumerate(blocks):
        cols = slice(index * columns, (index + 1) * columns)
        feature = jax.nn.gelu(piece * inverse * gain_ref[:, cols]).astype(jnp.bfloat16)
        start = index * columns % share
        features_ref[index * columns // share, :, start : start + columns] = feature


def project_embed(
    ids, offsets, latents, attended, out_weight, weights, gain, depth_parts, after
):
    particles, tokens, model_width = latents.shape
    rows = particles * tokens
    parts = len(weights)
    columns = weights[0].shape[2]
    count = parts * columns
    groups = model_width // column_block(model_width)
    vmem = pl.BlockSpec(memory_space=pltpu.VMEM)
    hbm = pl.BlockSpec(memory_space=pltpu.HBM)
    inputs = 5 + parts + len(after)

    def kernel(*refs):
        project_kernel(parts, offsets, depth_parts, refs[:inputs], refs[inputs:])

    return pl.pallas_call(
        kernel,
        in_specs=[pl.BlockSpec(memory_space=pltpu.SMEM), hbm, vmem, hbm, vmem]
        + [hbm] * parts
        + [pl.BlockSpec(memory_space=pl.ANY)] * len(after),
        out_specs=[vmem, vmem],
        out_shape=[
            jax.ShapeDtypeStruct(latents.shape, jnp.bfloat16),
            jax.ShapeDtypeStruct((depth_parts, rows, count // depth_parts), jnp.bfloat16),
        ],
        scratch_shapes=[
            pltpu.VMEM((model_width, model_width), jnp.bfloat16),
            pltpu.VMEM((parts, model_width, columns), jnp.bfloat16),
            pltpu.VMEM((rows, model_width), jnp.bfloat16),
            pltpu.VMEM((rows, model_width), jnp.bfloat16),
            pltpu.VMEM((parts, rows, columns), jnp.float32),
            pltpu.VMEM(latents.shape, latents.dtype),
            pltpu.SemaphoreType.DMA((2, groups)),
            pltpu.SemaphoreType.DMA((parts,)),
        ],
        compiler_params=pltpu.CompilerParams(vmem_limit_bytes=60 * MIB),
        cost_estimate=pl.CostEstimate(
            flops=2 * rows * model_width * (model_width + count),
            bytes_accessed=2 * model_width * (model_width + count) + 8 * rows * model_width,
            transcendentals=rows * count,
        ),
        name="project_embed",
    )(ids, latents, gain.reshape(1, count), out_weight, attended, *weights, *after)


def reward_kernel(particles, scale, parts, doms, offsets, joined, *refs):
    ids_ref, features_ref, head_ref, before_ref = refs[:4]
    weight_refs, (out_ref, weight_vmem, rows_ref, sems) = refs[4:-4], refs[-4:]
    dom, group, seq = ids_ref[0], ids_ref[1], ids_ref[2]
    _, depth, columns = weight_refs[0].shape
    rows = features_ref.shape[1]
    places = [
        (pair, shard)
        for pair in range(len(weight_refs) // parts)
        for shard in range(weight_refs[pair * parts].shape[0])
    ]
    count = len(places)

    copies = []
    for place, (pair, shard) in enumerate(places):
        lane = place % joined * columns
        for index in range(parts):
            copy = pltpu.make_async_copy(
                weight_refs[pair * parts + index].at[shard],
                weight_vmem.at[
                    place // joined,
                    index * depth : (index + 1) * depth,
                    lane : lane + columns,
                ],
                sems.at[place, index],
            )
            copy.start()
            copies.append(copy)
    for index in range(parts):
        rows_ref[:, index * depth : (index + 1) * depth] = features_ref[
            (group + parts - index) % parts
        ]
    totals = jnp.zeros((particles, joined * columns), jnp.float32)
    for step in range(count // joined):
        for copy in copies[step * joined * parts : (step + 1) * joined * parts]:
            copy.wait()
        hidden = jnp.dot(rows_ref[...], weight_vmem[step], preferred_element_type=jnp.float32)
        head = jnp.concatenate(
            [
                head_ref[(seq ^ offset) * doms + dom]
                for offset in offsets[step * joined : (step + 1) * joined]
            ],
            axis=1,
        )
        scored = jax.nn.gelu(hidden) * head
        totals += jnp.sum(scored.reshape(particles, rows // particles, -1), axis=1)

    sums = jnp.sum(totals, axis=1, keepdims=True) * scale
    first = len(before_ref.shape) == 1
    shape = out_ref.shape[-2:]
    out_rows = lax.broadcasted_iota(jnp.int32, shape, 0)
    lanes = lax.broadcasted_iota(jnp.int32, shape, 1)
    logits = jnp.zeros(shape, jnp.float32) if first else before_ref[...]
    row = dom if first else (dom + 1) % doms
    for particle in range(particles):
        here = jnp.logical_and(out_rows == row, lanes == particle)
        value = sums[particle : particle + 1]
        if first:
            value = value + jnp.where(seq == 0, before_ref[particle], 0.0)
        logits += jnp.where(here, value, 0.0)
    out_ref[...] = jnp.broadcast_to(logits, out_ref.shape)


def reward(ids, features, weights, parts, doms, offsets, head, before, particles, scale, copies):
    _, depth, columns = weights[0].shape
    rows = features.shape[1]
    count = len(offsets)
    joined = 2 if columns % LANES == 0 and count % 2 == 0 else 1
    smem = pl.BlockSpec(memory_space=pltpu.SMEM)
    vmem = pl.BlockSpec(memory_space=pltpu.VMEM)
    return pl.pallas_call(
        functools.partial(reward_kernel, particles, scale, parts, doms, offsets, joined),
        in_specs=[smem, vmem, vmem, smem if before.ndim == 1 else vmem]
        + [pl.BlockSpec(memory_space=pltpu.HBM)] * len(weights),
        out_specs=vmem,
        out_shape=jax.ShapeDtypeStruct((*copies, 8, LANES), jnp.float32),
        scratch_shapes=[
            pltpu.VMEM((count // joined, parts * depth, joined * columns), jnp.bfloat16),
            pltpu.VMEM((rows, parts * depth), jnp.bfloat16),
            pltpu.SemaphoreType.DMA((count, parts)),
        ],
        compiler_params=pltpu.CompilerParams(vmem_limit_bytes=60 * MIB),
        cost_estimate=pl.CostEstimate(
            flops=2 * rows * parts * depth * count * columns,
            bytes_accessed=2 * parts * depth * count * columns,
            transcendentals=rows * count * columns,
        ),
        name="reward",
    )(ids, features, head, before, *weights)


def finish_kernel(particles, doms, ids_ref, resampled_ref, parts_ref, out_ref, same_ref):
    logits = jnp.sum(parts_ref[...], axis=0)
    rows = lax.broadcasted_iota(jnp.int32, logits.shape, 0)
    lanes = lax.broadcasted_iota(jnp.int32, logits.shape, 1)
    valid = jnp.logical_and(rows < doms, lanes < particles)
    highest = jnp.max(jnp.where(valid, logits, -jnp.inf))
    total = jnp.sum(jnp.where(valid, jnp.exp(logits - highest), 0.0), axis=1, keepdims=True)
    log_total = highest + jnp.log(jnp.sum(total, axis=0, keepdims=True))
    own = jnp.sum(jnp.where(rows == ids_ref[0], logits, 0.0), axis=0, keepdims=True)
    out_ref[...] = (own - log_total)[:, :particles]


def finish(ids, parts, resampled, particles, doms):
    vmem = pl.BlockSpec(memory_space=pltpu.VMEM)
    anywhere = pl.BlockSpec(memory_space=pl.ANY)
    log_weights, resampled = pl.pallas_call(
        functools.partial(finish_kernel, particles, doms),
        in_specs=[pl.BlockSpec(memory_space=pltpu.SMEM), anywhere, vmem],
        out_specs=[vmem, anywhere],
        out_shape=[
            jax.ShapeDtypeStruct((1, particles), jnp.float32),
            jax.ShapeDtypeStruct(resampled.shape, resampled.dtype),
        ],
        input_output_aliases={1: 1},
        compiler_params=pltpu.CompilerParams(vmem_limit_bytes=2 * MIB),
        name="log_weights",
    )(ids, resampled, parts)
    return resampled, log_weights.reshape(particles)


def resample_kernel(ids_ref, ancestors_ref, own_ref, other_ref, out_ref):
    index = pl.program_id(0)
    own = ancestors_ref[index] // pl.num_programs(0) == ids_ref[0]

    @pl.when(own)
    def _():
        out_ref[...] = own_ref[...]

    @pl.when(jnp.logical_not(own))
    def _():
        out_ref[...] = other_ref[...]


def resample(ids, ancestors, own, other):
    particles, tokens, columns = own.shape
    block = (1, tokens, columns)
    parent = pl.BlockSpec(block, lambda i, ids, ancestors: (ancestors[i] % particles, 0, 0))
    return pl.pallas_call(
        resample_kernel,
        grid_spec=pltpu.PrefetchScalarGridSpec(
            num_scalar_prefetch=2,
            grid=(particles,),
            in_specs=[parent, parent],
            out_specs=pl.BlockSpec(block, lambda i, ids, ancestors: (i, 0, 0)),
        ),
        out_shape=jax.ShapeDtypeStruct(own.shape, own.dtype),
        compiler_params=pltpu.CompilerParams(vmem_limit_bytes=4 * MIB),
        name="resample",
    )(ids, ancestors, own, other)


def shifted(array, axis, step):
    count = lax.axis_size(axis)
    return lax.ppermute(array, axis, [(i, (i + step) % count) for i in range(count)])


def swapped(array, axis, bit):
    return lax.ppermute(array, axis, [(i, i ^ bit) for i in range(lax.axis_size(axis))])


def exchange(array):
    return lax.all_to_all(array, "seq", 0, 0, tiled=True)


def on_device(
    latents,
    queries,
    keys,
    values,
    out_weight,
    step_index,
    embed_weight,
    norm_gain,
    up_weight,
    head_weight,
    prev_logw,
    ancestors,
):
    seq_count = lax.axis_size("seq")
    group_count = lax.axis_size("groups")
    dom_count = lax.axis_size("dom")
    holders = group_count * dom_count
    dom = lax.axis_index("dom")
    group = lax.axis_index("groups")
    seq = lax.axis_index("seq")
    particles, tokens, model_width = latents.shape
    head_width = model_width // HEADS
    width = particles * model_width // seq_count
    splits = [(0, width)]
    if width % LANES == 0 and width >= 2 * LANES:
        start = -(-2 * width // (3 * LANES)) * LANES
        splits = [(0, start), (start, width - start)]

    ids = jnp.stack([dom, group, seq, step_index[0]]).astype(jnp.int32)

    embed_columns = embed_weight.shape[1] // holders
    embed_share = lax.dynamic_slice_in_dim(
        embed_weight, (dom * group_count + group) * embed_columns, embed_columns, 1
    )[None]
    up_depth = up_weight.shape[0] // group_count
    up_columns = up_weight.shape[1] // dom_count
    up_share = lax.dynamic_slice(
        up_weight, (group * up_depth, dom * up_columns), (up_depth, up_columns)
    )[None]
    bits = [1 << place for place in reversed(range(1, seq_count.bit_length() - 1))]
    near = [0]
    for bit in bits[:-2]:
        embed_share = jnp.concatenate([embed_share, swapped(embed_share, "seq", bit)])
        up_share = jnp.concatenate([up_share, swapped(up_share, "seq", bit)])
        near = near + [offset ^ bit for offset in near]
    high, low = bits[-2:]

    def over_groups(array):
        return [array] + [shifted(array, "groups", k) for k in range(1, group_count)]

    packed = pack(queries, keys, values, splits, width)
    embed_share = jnp.concatenate([embed_share, swapped(embed_share, "seq", high)])
    packed[0] = gate(packed[0], [embed_share])

    arrived = [exchange(packed[0])]
    up_high = swapped(up_share, "seq", high)
    own_pair, own_groups = swapped(up_share, "seq", 1), over_groups(up_share)
    for bit in (low, 1):
        embed_share = jnp.concatenate([embed_share, swapped(embed_share, "seq", bit)])
    after = [arrived[0], embed_share, up_high, own_pair, *own_groups[1:]]
    packed[1:] = [gate(piece, after) for piece in packed[1:]]

    arrived += [exchange(piece) for piece in packed[1:]]
    up_far = swapped(jnp.concatenate([up_share, up_high]), "seq", low)
    high_pair, high_groups = swapped(up_high, "seq", 1), over_groups(up_high)
    own_pairs = [own_pair] + [swapped(piece, "seq", 1) for piece in own_groups[1:]]
    embed_near = over_groups(embed_share)
    after = [up_far, high_pair, *high_groups[1:], *own_pairs[1:], *embed_near[1:]]
    attended = []
    for piece, (start, _) in zip(arrived, splits):
        attended = [
            attention(piece, head_width, width, start, attended, after if attended else [])
        ]

    returned = exchange(attended[0])
    far_pair, far_groups = swapped(up_far, "seq", 1), over_groups(up_far)
    embed_parts = embed_near + [
        shifted(piece, "dom", k) for k in range(1, dom_count) for piece in embed_near
    ]
    high_pairs = [high_pair] + [swapped(piece, "seq", 1) for piece in high_groups[1:]]
    far_pairs = over_groups(far_pair)
    up_parts = [own_groups, own_pairs, high_groups, high_pairs, far_groups, far_pairs]
    far = [offset ^ low for offset in near + [offset ^ high for offset in near]]
    up_offsets = [
        [offset ^ bit for offset in offsets]
        for offsets in (near, [offset ^ high for offset in near], far)
        for bit in (0, 1)
    ]
    embed_offsets = near + [offset ^ high for offset in near]
    for bit in (low, 1):
        embed_offsets = embed_offsets + [offset ^ bit for offset in embed_offsets]

    stepped, features = project_embed(
        ids,
        embed_offsets,
        latents,
        returned,
        out_weight,
        embed_parts,
        norm_gain,
        group_count,
        [*high_pairs[1:], *far_groups[1:], *far_pairs],
    )
    stepped_other = shifted(stepped, "dom", 1)
    features_other = shifted(features, "dom", 1)

    scale = potential_scale / math.sqrt(tokens * seq_count)
    head = head_weight.reshape(seq_count * dom_count, 1, up_columns)
    score = functools.partial(
        reward,
        ids,
        weights=[piece for pieces in up_parts for piece in pieces],
        parts=group_count,
        doms=dom_count,
        offsets=[offset for offsets in up_offsets for offset in offsets],
        head=head,
        particles=particles,
        scale=scale,
    )
    partial_own = score(features, before=prev_logw, copies=())
    partial = score(features_other, before=partial_own, copies=(dom_count * seq_count,))
    logits = lax.all_to_all(partial, ("dom", "seq"), 0, 0, tiled=True)
    resampled = resample(ids, ancestors.astype(jnp.int32), stepped, stepped_other)
    return finish(ids, logits, resampled, particles, dom_count)


def solution(mesh):
    in_specs = (
        P(("groups", "dom"), "seq", None),
        P(("groups", "dom"), "seq", None),
        P(("groups", "dom"), "seq", None),
        P(("groups", "dom"), "seq", None),
        P(),
        P("groups"),
        P("seq", None),
        P(),
        P(None, "seq"),
        P(),
        P(("groups", "dom")),
        P(("groups", "dom")),
    )
    out_specs = (P(("groups", "dom"), "seq", None), P(("groups", "dom")))
    return jax.shard_map(
        on_device, mesh=mesh, in_specs=in_specs, out_specs=out_specs, check_vma=False
    )
```

time: 176 us -> 177 us (level)
  waiting for transfers between devices: 59.1 us -> 77.5 us
  starting transfers between devices: 57.1 us -> 47.2 us
  local copies, waits for them, and re-layouts: 11.8 us -> 4.83 us
    ppermute x14 -> x10, waiting for transfers between devices: 37.8 us -> 60.9 us  [swapped(): lax.ppermute(array, axis, [(i, i ^ bit) for i in range(lax.axis_size(axis...]
    ppermute x10 -> x9, waiting for transfers between devices: 21 us -> 12 us  [shifted(): lax.ppermute(array, axis, [(i, (i + step) % count) for i in range(count)])]
    ppermute x14 -> x10, starting transfers between devices: 26.1 us -> 18.2 us  [swapped(): lax.ppermute(array, axis, [(i, i ^ bit) for i in range(lax.axis_size(axis...]
    unnamed x78 -> x46, local copies, waits for them, and re-layouts: 10.8 us -> 3.83 us
    all_to_all x4 -> x3, starting transfers between devices: 22.6 us -> 15.8 us  [exchange(): return lax.all_to_all(array, 'seq', 0, 0, tiled=True)]
    all_to_all x0 -> x1, starting transfers between devices: none -> 5.47 us  [on_device(): logits = lax.all_to_all(partial, ('dom', 'seq'), 0, 0, tiled=True)]
    all_to_all x0 -> x1, waiting for transfers between devices: none -> 4.69 us  [on_device(): logits = lax.all_to_all(partial, ('dom', 'seq'), 0, 0, tiled=True)]
    pallas_call x4 -> x2, Pallas kernels: 16.8 us -> 12.4 us  [the longest x1 9.23 us: project_embed(): pl.pallas_call(kernel, in_specs=[pl.BlockSpec(memory_space=pltpu.SMEM), h...]
  transfers between devices with their start and end apart: 29 -> 23, of which waited for: 12 -> 10; matrix products, arithmetic and copies ran while one was open for 2% -> 2% of each run, Pallas kernels for 18% -> 14%
where the time goes in v11:
time: 177 us; the launch traced here: 176 us
  waiting for transfers between devices  77.5 us (44%)
  starting transfers between devices  47.2 us (27%)
  Pallas kernels  40.4 us (23%)
  other arithmetic  5.04 us (3%)
  local copies, waits for them, and re-layouts  4.83 us (3%)
    ppermute x10, waiting for transfers between devices, swapped(): lax.ppermute(array, axis, [(i, i ^ bit) for i in range(lax.axis_size(axis...  60.9 us
    ppermute x10, starting transfers between devices, swapped(): lax.ppermute(array, axis, [(i, i ^ bit) for i in range(lax.axis_size(axis...  18.2 us
    all_to_all x3, starting transfers between devices, exchange(): return lax.all_to_all(array, 'seq', 0, 0, tiled=True)  15.8 us
    pallas_call x2, Pallas kernels, attention(): pl.pallas_call(functools.partial(attention_kernel, head_width, block_sour...  13.8 us
    ppermute x9, waiting for transfers between devices, shifted(): lax.ppermute(array, axis, [(i, (i + step) % count) for i in range(count)])  12 us
    pallas_call x2, Pallas kernels, reward(): pl.pallas_call(functools.partial(reward_kernel, particles, scale, parts,...  10.8 us
    pallas_call x1, Pallas kernels, project_embed(): pl.pallas_call(kernel, in_specs=[pl.BlockSpec(memory_space=pltpu.SMEM), h...  9.23 us
    ppermute x9, starting transfers between devices, shifted(): lax.ppermute(array, axis, [(i, (i + step) % count) for i in range(count)])  7.64 us
  transfers between devices with their start and end apart: 23, of which 10 were waited for; matrix products, arithmetic and copies ran while one was open for 2% of the time, Pallas kernels for 14%

profile of v11, /device:TPU:0, one launch (start us, length us, event | category | flops | bytes accessed | tf_op | source)
XLA Modules:
  0.0 176.5 jit_solution(5319176578757573816)
XLA Ops:
  1.6 4.0 %collective-permute-start = (bf16[1,192,256]{2,1,0:T(8,128)(2,1)S(1)}, bf16[1,192,256]{2,1,0:T(8,128)(2,1)S(1)}, u32[]{:S(2)}, u32[]{:S(2)}) collective-permute-start(bf16[1,192,256]{2,1,0:T(8,128)(2,1)S(1)} %dynamic-slice_bitcast_fusion.1), channel_id=1, source_target_pairs={{0,4},{1,5},{2,6},{3,7},{4,0},{5,1},{6,2},{7,3},{8,12},{9,13},{10,... | collective-permute-start | bytes 294920 | tf_op jit(solution)/shard_map/ppermute | solution.py:416
  5.7 3.2 %pack_heads.1 = (bf16[8,3,64,512]{3,2,1,0:T(8,128)(2,1)}, bf16[8,3,64,256]{3,2,1,0:T(8,128)(2,1)}) custom-call(bf16[4,64,1536]{2,1,0:T(8,128)(2,1)} %q_ref.1, bf16[4,64,1536]{2,1,0:T(8,128)(2,1)} %k_ref.1, bf16[4,64,1536]{2,1,0:T(8,128)(2,1)} %v_ref.1), custom_call_target="tpu_custom_call" | custom-call | tf_op jit(solution)/shard_map/pack_heads/pallas_call | solution.py:38
  8.8 1.7 collective-permute-done
  11.3 5.9 %all-to-all-start = ((bf16[8,3,64,512]{3,2,1,0:T(8,128)(2,1)}), bf16[8,3,64,512]{3,2,1,0:T(8,128)(2,1)S(1)}, u32[]{:S(2)}, u32[]{:S(2)}) async-start(bf16[8,3,64,512]{3,2,1,0:T(8,128)(2,1)} %gate.2), calls=%async_computation | async-start | bytes 3145728 | tf_op jit(solution)/shard_map/all_to_all | solution.py:420
  17.2 2.0 %collective-permute-start.1 = (bf16[2,192,256]{2,1,0:T(8,128)(2,1)S(1)}, bf16[2,192,256]{2,1,0:T(8,128)(2,1)S(1)}, u32[]{:S(2)}, u32[]{:S(2)}) collective-permute-start(bf16[2,192,256]{2,1,0:T(8,128)(2,1)S(1)} %copy-done.20), channel_id=1, source_target_pairs={{0,2},{1,3},{2,0},{3,1},{4,6},{5,7},{6,4},{7,5},{8,10},{9,11},{10,... | collective-permute-start | bytes 589832 | tf_op jit(solution)/shard_map/ppermute | solution.py:416
  19.2 28.9 %collective-permute-done.1 = bf16[2,192,256]{2,1,0:T(8,128)(2,1)S(1)} collective-permute-done((bf16[2,192,256]{2,1,0:T(8,128)(2,1)S(1)}, bf16[2,192,256]{2,1,0:T(8,128)(2,1)S(1)}, u32[]{:S(2)}, u32[]{:S(2)}) %collective-permute-start.1) | collective-permute-done | bytes 196640 | tf_op jit(solution)/shard_map/ppermute | solution.py:416
  49.9 4.2 %collective-permute-start.3 = (bf16[1,512,256]{2,1,0:T(8,128)(2,1)S(1)}, bf16[1,512,256]{2,1,0:T(8,128)(2,1)S(1)}, u32[]{:S(2)}, u32[]{:S(2)}) collective-permute-start(bf16[1,512,256]{2,1,0:T(8,128)(2,1)S(1)} %dynamic-slice_bitcast_fusion.refs_4_), channel_id=1, source_target_pairs={{0,4},{1,5},{2,6},{3,7},{4,0},{5,1},{6,2},{7,3},{8,12},{9,13},{10,... | collective-permute-start | bytes 786440 | tf_op jit(solution)/shard_map/ppermute | solution.py:416
  54.1 1.5 collective-permute-start.5
  56.2 5.1 %collective-permute-done.2 = bf16[4,192,256]{2,1,0:T(8,128)(2,1)} collective-permute-done((bf16[4,192,256]{2,1,0:T(8,128)(2,1)}, bf16[4,192,256]{2,1,0:T(8,128)(2,1)}, u32[]{:S(2)}, u32[]{:S(2)}) %collective-permute-start.2) | collective-permute-done | bytes 393248 | tf_op jit(solution)/shard_map/ppermute | solution.py:416
  61.3 2.1 %pad_maximum_fusion.refs_2_.refs_5_ = bf16[8,192,256]{2,1,0:T(8,128)(2,1)} fusion(bf16[4,192,256]{2,1,0:T(8,128)(2,1)} %collective-permute-done.2, bf16[2,192,256]{2,1,0:T(8,128)(2,1)} %copy-done.21, bf16[1,192,256]{2,1,0:T(8,128)(2,1)} %copy-done.19, bf16[1,192,256]{2,1,0:T(8,128)(2,1)S(1)} %dynamic-slice_bitcast_fusion.1), kind=kLoop, calls=%fused_computation | loop fusion | flops 1179648 | bytes 1572864 | tf_op jit(solution)/shard_map/concatenate | solution.py:482
  63.4 2.3 %collective-permute-done.3.refs_3_.refs_8_ = bf16[1,512,256]{2,1,0:T(8,128)(2,1)S(1)} collective-permute-done((bf16[1,512,256]{2,1,0:T(8,128)(2,1)S(1)}, bf16[1,512,256]{2,1,0:T(8,128)(2,1)S(1)}, u32[]{:S(2)}, u32[]{:S(2)}) %collective-permute-start.3) | collective-permute-done | bytes 262176 | tf_op jit(solution)/shard_map/ppermute | solution.py:416
  67.0 4.9 %all-to-all-start.1 = ((bf16[8,3,64,256]{3,2,1,0:T(8,128)(2,1)}), bf16[8,3,64,256]{3,2,1,0:T(8,128)(2,1)S(1)}, u32[]{:S(2)}, u32[]{:S(2)}) async-start(bf16[8,3,64,256]{3,2,1,0:T(8,128)(2,1)} %gate.3), calls=%async_computation.1 | async-start | bytes 1572864 | tf_op jit(solution)/shard_map/all_to_all | solution.py:420
  71.9 1.6 collective-permute-start.10
  74.3 2.0 %collective-permute-start.6 = (bf16[2,512,256]{2,1,0:T(8,128)(2,1)}, bf16[2,512,256]{2,1,0:T(8,128)(2,1)S(1)}, u32[]{:S(2)}, u32[]{:S(2)}) collective-permute-start(bf16[2,512,256]{2,1,0:T(8,128)(2,1)} %pad_maximum_fusion.1), channel_id=1, source_target_pairs={{0,2},{1,3},{2,0},{3,1},{4,6},{5,7},{6,4},{7,5},{8,10},{9,11},{10,... | collective-permute-start | bytes 1572872 | tf_op jit(solution)/shard_map/ppermute | solution.py:416
  76.8 1.5 collective-permute-start.7
  78.8 8.7 %attention.2.refs_0_ = bf16[8,64,768]{2,1,0:T(8,128)(2,1)} custom-call(bf16[8,3,64,512]{3,2,1,0:T(8,128)(2,1)} %copy-done.5), custom_call_target="tpu_custom_call" | custom-call | flops 536870912 | bytes 2097152 | tf_op jit(solution)/shard_map/attention/pallas_call | solution.py:107
  87.5 7.7 %collective-permute-done.8.refs_3_.refs_9_ = bf16[1,512,256]{2,1,0:T(8,128)(2,1)S(1)} collective-permute-done((bf16[1,512,256]{2,1,0:T(8,128)(2,1)S(1)}, bf16[1,512,256]{2,1,0:T(8,128)(2,1)S(1)}, u32[]{:S(2)}, u32[]{:S(2)}) %collective-permute-start.8) | collective-permute-done | bytes 262176 | tf_op jit(solution)/shard_map/ppermute | solution.py:412
  95.2 1.5 collective-permute-done.6.refs_1_.refs_12_
  98.4 5.2 %attention.3 = bf16[8,64,768]{2,1,0:T(8,128)(2,1)} custom-call(bf16[8,3,64,256]{3,2,1,0:T(8,128)(2,1)} %copy-done.13, bf16[8,64,768]{2,1,0:T(8,128)(2,1)} %attention.2.refs_0_, bf16[2,512,256]{2,1,0:T(8,128)(2,1)} %copy-done.6, bf16[1,512,256]{2,1,0:T(8,128)(2,1)} %copy-done.17, bf16[1,512,256]{2,1,0:T(8,128)(2,1)} %copy-done.15, ...), custom_call_target="tpu_custom_call", output_to_operand_aliasing={{}: (1, {})} | custom-call | flops 268435456 | bytes 1048576 | tf_op jit(solution)/shard_map/attention/pallas_call | solution.py:107
  103.6 5.0 %all-to-all-start.2 = ((bf16[8,64,768]{2,1,0:T(8,128)(2,1)}), bf16[8,64,768]{2,1,0:T(8,128)(2,1)}, u32[]{:S(2)}, u32[]{:S(2)}) async-start(bf16[8,64,768]{2,1,0:T(8,128)(2,1)} %attention.3), calls=%async_computation.2 | async-start | bytes 1572864 | tf_op jit(solution)/shard_map/all_to_all | solution.py:420
  108.6 2.0 %collective-permute-start.15 = (bf16[2,512,256]{2,1,0:T(8,128)(2,1)S(1)}, bf16[2,512,256]{2,1,0:T(8,128)(2,1)S(1)}, u32[]{:S(2)}, u32[]{:S(2)}) collective-permute-start(bf16[2,512,256]{2,1,0:T(8,128)(2,1)S(1)} %copy-done.7), channel_id=1, source_target_pairs={{0,1},{1,0},{2,3},{3,2},{4,5},{5,4},{6,7},{7,6},{8,9},{9,8},{10,11... | collective-permute-start | bytes 1572872 | tf_op jit(solution)/shard_map/ppermute | solution.py:416
  111.1 1.5 collective-permute-start.14
  112.6 16.6 %collective-permute-done.15.refs_11_.refs_14_ = bf16[2,512,256]{2,1,0:T(8,128)(2,1)S(1)} collective-permute-done((bf16[2,512,256]{2,1,0:T(8,128)(2,1)S(1)}, bf16[2,512,256]{2,1,0:T(8,128)(2,1)S(1)}, u32[]{:S(2)}, u32[]{:S(2)}) %collective-permute-start.15) | collective-permute-done | bytes 524320 | tf_op jit(solution)/shard_map/ppermute | solution.py:416
  129.3 1.5 collective-permute-start.16
  132.4 4.7 %collective-permute-done.13.refs_9_.refs_11_ = bf16[1,512,256]{2,1,0:T(8,128)(2,1)S(1)} collective-permute-done((bf16[1,512,256]{2,1,0:T(8,128)(2,1)S(1)}, bf16[1,512,256]{2,1,0:T(8,128)(2,1)S(1)}, u32[]{:S(2)}, u32[]{:S(2)}) %collective-permute-start.13) | collective-permute-done | bytes 262176 | tf_op jit(solution)/shard_map/ppermute | solution.py:416
  137.2 4.3 %collective-permute-done.16.refs_12_.refs_15_ = bf16[2,512,256]{2,1,0:T(8,128)(2,1)} collective-permute-done((bf16[2,512,256]{2,1,0:T(8,128)(2,1)S(1)}, bf16[2,512,256]{2,1,0:T(8,128)(2,1)}, u32[]{:S(2)}, u32[]{:S(2)}) %collective-permute-start.16) | collective-permute-done | bytes 524320 | tf_op jit(solution)/shard_map/ppermute | solution.py:412
  141.4 9.2 %project_embed.1 = (bf16[4,64,1536]{2,1,0:T(8,128)(2,1)}, bf16[2,256,512]{2,1,0:T(8,128)(2,1)}) custom-call(s32[4]{0:T(128)} %pad_add_fusion.refs_0_.ids_ref, bf16[4,64,1536]{2,1,0:T(8,128)(2,1)} %refs_1_.1, f32[1,1024]{1,0:T(1,128)} %bitcast.12, bf16[1536,1536]{1,0:T(8,128)(2,1)} %refs_3_.2, bf16[8,64,768]{2,1,0:T(8,128)(2,1)} %all-to-all-done.2.refs_4_, ...), custom_call_target="tpu_custom_call" | custom-call | flops 2013265920 | bytes 11010048 | tf_op jit(solution)/shard_map/project_embed/pallas_call | solution.py:228
  151.2 5.4 %reward.2.refs_3_ = f32[8,128]{1,0:T(8,128)} custom-call(s32[4]{0:T(128)} %pad_add_fusion.refs_0_.ids_ref, bf16[2,256,512]{2,1,0:T(8,128)(2,1)} %get-tuple-element.11.refs_1_, f32[16,1,256]{2,1,0:T(1,128)} %bitcast.10, f32[4]{0:T(128)} %refs_3_.3, bf16[1,512,256]{2,1,0:T(8,128)(2,1)} %copy-done.11, bf16[1,512,256]{2,1,0:T(8,128)(2,1)} %copy-done.14, ...), custom_call_target="tpu_custom_call" | custom-call | flops 1073741824 | bytes 4194304 | tf_op jit(solution)/shard_map/reward/pallas_call | solution.py:328
  157.5 5.4 %reward.3 = f32[16,8,128]{2,1,0:T(8,128)} custom-call(s32[4]{0:T(128)} %pad_add_fusion.refs_0_.ids_ref, bf16[2,256,512]{2,1,0:T(8,128)(2,1)} %copy-done.22, f32[16,1,256]{2,1,0:T(1,128)} %bitcast.11, f32[8,128]{1,0:T(8,128)} %reward.2.refs_3_, bf16[1,512,256]{2,1,0:T(8,128)(2,1)} %copy-done.11, bf16[1,512,256]{2,1,0:T(8,128)(2,1)} %copy-done.14, ...), custom_call_target="tpu_custom_call" | custom-call | flops 1073741824 | bytes 4194304 | tf_op jit(solution)/shard_map/reward/pallas_call | solution.py:328
  162.9 5.5 %all-to-all-start.3 = ((f32[16,8,128]{2,1,0:T(8,128)}), f32[16,8,128]{2,1,0:T(8,128)S(1)}, u32[]{:S(2)}, u32[]{:S(2)}) async-start(f32[16,8,128]{2,1,0:T(8,128)} %reward.3), calls=%async_computation.3 | async-start | bytes 131072 | tf_op jit(solution)/shard_map/all_to_all | solution.py:545
  168.5 2.0 %resample.1.resampled_ref = bf16[4,64,1536]{2,1,0:T(8,128)(2,1)} custom-call(s32[4]{0:T(128)S(1)} %copy-done.2, s32[4]{0:T(128)S(1)} %copy-done.3, bf16[4,64,1536]{2,1,0:T(8,128)(2,1)S(1)} %copy-done.1, bf16[4,64,1536]{2,1,0:T(8,128)(2,1)S(1)} %collective-permute-done.17.other_ref), custom_call_target="tpu_custom_call" | custom-call | tf_op jit(solution)/shard_map/resample/pallas_call | solution.py:396
  170.5 4.7 %all-to-all-done.3.parts_ref = f32[16,8,128]{2,1,0:T(8,128)S(1)} async-done(((f32[16,8,128]{2,1,0:T(8,128)}), f32[16,8,128]{2,1,0:T(8,128)S(1)}, u32[]{:S(2)}, u32[]{:S(2)}) %all-to-all-start.3) | async-done | bytes 65568 | tf_op jit(solution)/shard_map/all_to_all | solution.py:545
  (77 shorter events, 13.2 us)
Async XLA Ops:
  0.6 49.2 %copy-start = (bf16[1024,512]{1,0:T(8,128)(2,1)S(1)}, bf16[1024,512]{1,0:T(8,128)(2,1)}, u32[]{:S(2)}) copy-start(bf16[1024,512]{1,0:T(8,128)(2,1)} %param.20) | copy-start | bytes 3145732
  1.6 8.9 %collective-permute-start = (bf16[1,192,256]{2,1,0:T(8,128)(2,1)S(1)}, bf16[1,192,256]{2,1,0:T(8,128)(2,1)S(1)}, u32[]{:S(2)}, u32[]{:S(2)}) collective-permute-start(bf16[1,192,256]{2,1,0:T(8,128)(2,1)S(1)} %dynamic-slice_bitcast_fusion.1), channel_id=1, source_target_pairs={{0,4},{1,5},{2,6},{3,7},{4,0},{5,1},{6,2},{7,3},{8,12},{9,13},{10,... | collective-permute-start | bytes 294920 | tf_op jit(solution)/shard_map/ppermute | solution.py:416
  10.6 37.5 %copy-start.19 = (bf16[1,192,256]{2,1,0:T(8,128)(2,1)}, bf16[1,192,256]{2,1,0:T(8,128)(2,1)S(1)}, u32[]{:S(2)}) copy-start(bf16[1,192,256]{2,1,0:T(8,128)(2,1)S(1)} %collective-permute-done) | copy-start | bytes 294916
  11.3 54.3 %all-to-all-start = ((bf16[8,3,64,512]{3,2,1,0:T(8,128)(2,1)}), bf16[8,3,64,512]{3,2,1,0:T(8,128)(2,1)S(1)}, u32[]{:S(2)}, u32[]{:S(2)}) async-start(bf16[8,3,64,512]{3,2,1,0:T(8,128)(2,1)} %gate.2), calls=%async_computation | async-start | bytes 3145728 | tf_op jit(solution)/shard_map/all_to_all | solution.py:420
  17.2 30.9 %collective-permute-start.1 = (bf16[2,192,256]{2,1,0:T(8,128)(2,1)S(1)}, bf16[2,192,256]{2,1,0:T(8,128)(2,1)S(1)}, u32[]{:S(2)}, u32[]{:S(2)}) collective-permute-start(bf16[2,192,256]{2,1,0:T(8,128)(2,1)S(1)} %copy-done.20), channel_id=1, source_target_pairs={{0,2},{1,3},{2,0},{3,1},{4,6},{5,7},{6,4},{7,5},{8,10},{9,11},{10,... | collective-permute-start | bytes 589832 | tf_op jit(solution)/shard_map/ppermute | solution.py:416
  48.9 12.4 %collective-permute-start.2 = (bf16[4,192,256]{2,1,0:T(8,128)(2,1)}, bf16[4,192,256]{2,1,0:T(8,128)(2,1)}, u32[]{:S(2)}, u32[]{:S(2)}) collective-permute-start(bf16[4,192,256]{2,1,0:T(8,128)(2,1)} %pad_maximum_fusion.2), channel_id=1, source_target_pairs={{0,1},{1,0},{2,3},{3,2},{4,5},{5,4},{6,7},{7,6},{8,9},{9,8},{10,11... | collective-permute-start | bytes 1179656 | tf_op jit(solution)/shard_map/ppermute | solution.py:416
  49.9 15.8 %copy-start.11 = (bf16[1,512,256]{2,1,0:T(8,128)(2,1)}, bf16[1,512,256]{2,1,0:T(8,128)(2,1)S(1)}, u32[]{:S(2)}) copy-start(bf16[1,512,256]{2,1,0:T(8,128)(2,1)S(1)} %dynamic-slice_bitcast_fusion.refs_4_) | copy-start | bytes 786436
  49.9 15.7 %collective-permute-start.3 = (bf16[1,512,256]{2,1,0:T(8,128)(2,1)S(1)}, bf16[1,512,256]{2,1,0:T(8,128)(2,1)S(1)}, u32[]{:S(2)}, u32[]{:S(2)}) collective-permute-start(bf16[1,512,256]{2,1,0:T(8,128)(2,1)S(1)} %dynamic-slice_bitcast_fusion.refs_4_), channel_id=1, source_target_pairs={{0,4},{1,5},{2,6},{3,7},{4,0},{5,1},{6,2},{7,3},{8,12},{9,13},{10,... | collective-permute-start | bytes 786440 | tf_op jit(solution)/shard_map/ppermute | solution.py:416
  54.1 11.5 %collective-permute-start.5 = (bf16[1,512,256]{2,1,0:T(8,128)(2,1)S(1)}, bf16[1,512,256]{2,1,0:T(8,128)(2,1)S(1)}, u32[]{:S(2)}, u32[]{:S(2)}) collective-permute-start(bf16[1,512,256]{2,1,0:T(8,128)(2,1)S(1)} %dynamic-slice_bitcast_fusion.refs_4_), channel_id=1, source_target_pairs={{0,16},{16,0},{1,17},{17,1},{2,18},{18,2},{3,19},{19,3},{4,20},{20... | collective-permute-start | bytes 786440 | tf_op jit(solution)/shard_map/ppermute | solution.py:412
  55.6 10.0 %collective-permute-start.4 = (bf16[1,512,256]{2,1,0:T(8,128)(2,1)S(1)}, bf16[1,512,256]{2,1,0:T(8,128)(2,1)}, u32[]{:S(2)}, u32[]{:S(2)}) collective-permute-start(bf16[1,512,256]{2,1,0:T(8,128)(2,1)S(1)} %dynamic-slice_bitcast_fusion.refs_4_), channel_id=1, source_target_pairs={{0,1},{1,0},{2,3},{3,2},{4,5},{5,4},{6,7},{7,6},{8,9},{9,8},{10,11... | collective-permute-start | bytes 786440 | tf_op jit(solution)/shard_map/ppermute | solution.py:416
  67.0 6.5 %copy-start.12 = (bf16[1,512,256]{2,1,0:T(8,128)(2,1)S(1)}, bf16[1,512,256]{2,1,0:T(8,128)(2,1)}, u32[]{:S(2)}) copy-start(bf16[1,512,256]{2,1,0:T(8,128)(2,1)} %copy-done.11) | copy-start | bytes 786436
  67.0 29.8 %all-to-all-start.1 = ((bf16[8,3,64,256]{3,2,1,0:T(8,128)(2,1)}), bf16[8,3,64,256]{3,2,1,0:T(8,128)(2,1)S(1)}, u32[]{:S(2)}, u32[]{:S(2)}) async-start(bf16[8,3,64,256]{3,2,1,0:T(8,128)(2,1)} %gate.3), calls=%async_computation.1 | async-start | bytes 1572864 | tf_op jit(solution)/shard_map/all_to_all | solution.py:420
  71.9 24.8 %collective-permute-start.10 = (bf16[8,192,256]{2,1,0:T(8,128)(2,1)S(1)}, bf16[8,192,256]{2,1,0:T(8,128)(2,1)}, u32[]{:S(2)}, u32[]{:S(2)}) collective-permute-start(bf16[8,192,256]{2,1,0:T(8,128)(2,1)S(1)} %copy-done.4), channel_id=1, source_target_pairs={{0,16},{16,0},{1,17},{17,1},{2,18},{18,2},{3,19},{19,3},{4,20},{20... | collective-permute-start | bytes 2359304 | tf_op jit(solution)/shard_map/ppermute | solution.py:412
  74.3 22.4 %collective-permute-start.6 = (bf16[2,512,256]{2,1,0:T(8,128)(2,1)}, bf16[2,512,256]{2,1,0:T(8,128)(2,1)S(1)}, u32[]{:S(2)}, u32[]{:S(2)}) collective-permute-start(bf16[2,512,256]{2,1,0:T(8,128)(2,1)} %pad_maximum_fusion.1), channel_id=1, source_target_pairs={{0,2},{1,3},{2,0},{3,1},{4,6},{5,7},{6,4},{7,5},{8,10},{9,11},{10,... | collective-permute-start | bytes 1572872 | tf_op jit(solution)/shard_map/ppermute | solution.py:416
  76.3 18.9 %collective-permute-start.8 = (bf16[1,512,256]{2,1,0:T(8,128)(2,1)S(1)}, bf16[1,512,256]{2,1,0:T(8,128)(2,1)S(1)}, u32[]{:S(2)}, u32[]{:S(2)}) collective-permute-start(bf16[1,512,256]{2,1,0:T(8,128)(2,1)S(1)} %copy-done.10), channel_id=1, source_target_pairs={{0,16},{16,0},{1,17},{17,1},{2,18},{18,2},{3,19},{19,3},{4,20},{20... | collective-permute-start | bytes 786440 | tf_op jit(solution)/shard_map/ppermute | solution.py:412
  76.8 18.4 %collective-permute-start.7 = (bf16[1,512,256]{2,1,0:T(8,128)(2,1)S(1)}, bf16[1,512,256]{2,1,0:T(8,128)(2,1)S(1)}, u32[]{:S(2)}, u32[]{:S(2)}) collective-permute-start(bf16[1,512,256]{2,1,0:T(8,128)(2,1)S(1)} %copy-done.10), channel_id=1, source_target_pairs={{0,1},{1,0},{2,3},{3,2},{4,5},{5,4},{6,7},{7,6},{8,9},{9,8},{10,11... | collective-permute-start | bytes 786440 | tf_op jit(solution)/shard_map/ppermute | solution.py:416
  78.3 16.9 %collective-permute-start.9 = (bf16[1,512,256]{2,1,0:T(8,128)(2,1)}, bf16[1,512,256]{2,1,0:T(8,128)(2,1)}, u32[]{:S(2)}, u32[]{:S(2)}) collective-permute-start(bf16[1,512,256]{2,1,0:T(8,128)(2,1)} %copy-done.14), channel_id=1, source_target_pairs={{0,1},{1,0},{2,3},{3,2},{4,5},{5,4},{6,7},{7,6},{8,9},{9,8},{10,11... | collective-permute-start | bytes 786440 | tf_op jit(solution)/shard_map/ppermute | solution.py:416
  103.6 27.2 %copy-start.16 = (bf16[1,512,256]{2,1,0:T(8,128)(2,1)S(1)}, bf16[1,512,256]{2,1,0:T(8,128)(2,1)}, u32[]{:S(2)}) copy-start(bf16[1,512,256]{2,1,0:T(8,128)(2,1)} %copy-done.15) | copy-start | bytes 786436
  103.6 37.8 %all-to-all-start.2 = ((bf16[8,64,768]{2,1,0:T(8,128)(2,1)}), bf16[8,64,768]{2,1,0:T(8,128)(2,1)}, u32[]{:S(2)}, u32[]{:S(2)}) async-start(bf16[8,64,768]{2,1,0:T(8,128)(2,1)} %attention.3), calls=%async_computation.2 | async-start | bytes 1572864 | tf_op jit(solution)/shard_map/all_to_all | solution.py:420
  108.6 20.7 %collective-permute-start.15 = (bf16[2,512,256]{2,1,0:T(8,128)(2,1)S(1)}, bf16[2,512,256]{2,1,0:T(8,128)(2,1)S(1)}, u32[]{:S(2)}, u32[]{:S(2)}) collective-permute-start(bf16[2,512,256]{2,1,0:T(8,128)(2,1)S(1)} %copy-done.7), channel_id=1, source_target_pairs={{0,1},{1,0},{2,3},{3,2},{4,5},{5,4},{6,7},{7,6},{8,9},{9,8},{10,11... | collective-permute-start | bytes 1572872 | tf_op jit(solution)/shard_map/ppermute | solution.py:416
  110.6 26.5 %collective-permute-start.11 = (bf16[8,192,256]{2,1,0:T(8,128)(2,1)S(1)}, bf16[8,192,256]{2,1,0:T(8,128)(2,1)}, u32[]{:S(2)}, u32[]{:S(2)}) collective-permute-start(bf16[8,192,256]{2,1,0:T(8,128)(2,1)S(1)} %copy-done.4), channel_id=1, source_target_pairs={{0,8},{8,0},{1,9},{9,1},{2,10},{10,2},{3,11},{11,3},{4,12},{12,4},... | collective-permute-start | bytes 2359304 | tf_op jit(solution)/shard_map/ppermute | solution.py:412
  110.6 30.8 %collective-permute-start.12 = (bf16[8,192,256]{2,1,0:T(8,128)(2,1)}, bf16[8,192,256]{2,1,0:T(8,128)(2,1)}, u32[]{:S(2)}, u32[]{:S(2)}) collective-permute-start(bf16[8,192,256]{2,1,0:T(8,128)(2,1)} %collective-permute-done.10.refs_5_.refs_6_), channel_id=1, source_target_pairs={{0,8},{8,0},{1,9},{9,1},{2,10},{10,2},{3,11},{11,3},{4,12},{12,4},... | collective-permute-start | bytes 2359304 | tf_op jit(solution)/shard_map/ppermute | solution.py:412
  111.1 26.0 %collective-permute-start.14 = (bf16[2,512,256]{2,1,0:T(8,128)(2,1)S(1)}, bf16[2,512,256]{2,1,0:T(8,128)(2,1)}, u32[]{:S(2)}, u32[]{:S(2)}) collective-permute-start(bf16[2,512,256]{2,1,0:T(8,128)(2,1)S(1)} %copy-done.7), channel_id=1, source_target_pairs={{0,16},{16,0},{1,17},{17,1},{2,18},{18,2},{3,19},{19,3},{4,20},{20... | collective-permute-start | bytes 1572872 | tf_op jit(solution)/shard_map/ppermute | solution.py:412
  129.3 12.1 %copy-start.8 = (bf16[2,512,256]{2,1,0:T(8,128)(2,1)}, bf16[2,512,256]{2,1,0:T(8,128)(2,1)S(1)}, u32[]{:S(2)}) copy-start(bf16[2,512,256]{2,1,0:T(8,128)(2,1)S(1)} %collective-permute-done.15.refs_11_.refs_14_) | copy-start | bytes 1572868
  129.3 12.1 %collective-permute-start.16 = (bf16[2,512,256]{2,1,0:T(8,128)(2,1)S(1)}, bf16[2,512,256]{2,1,0:T(8,128)(2,1)}, u32[]{:S(2)}, u32[]{:S(2)}) collective-permute-start(bf16[2,512,256]{2,1,0:T(8,128)(2,1)S(1)} %collective-permute-done.15.refs_11_.refs_14_), channel_id=1, source_target_pairs={{0,16},{16,0},{1,17},{17,1},{2,18},{18,2},{3,19},{19,3},{4,20},{20... | collective-permute-start | bytes 1572872 | tf_op jit(solution)/shard_map/ppermute | solution.py:412
  130.8 6.4 %collective-permute-start.13 = (bf16[1,512,256]{2,1,0:T(8,128)(2,1)S(1)}, bf16[1,512,256]{2,1,0:T(8,128)(2,1)S(1)}, u32[]{:S(2)}, u32[]{:S(2)}) collective-permute-start(bf16[1,512,256]{2,1,0:T(8,128)(2,1)S(1)} %copy-done.16), channel_id=1, source_target_pairs={{0,1},{1,0},{2,3},{3,2},{4,5},{5,4},{6,7},{7,6},{8,9},{9,8},{10,11... | collective-permute-start | bytes 786440 | tf_op jit(solution)/shard_map/ppermute | solution.py:416
  150.7 17.8 %collective-permute-start.17 = (bf16[4,64,1536]{2,1,0:T(8,128)(2,1)}, bf16[4,64,1536]{2,1,0:T(8,128)(2,1)S(1)}, u32[]{:S(2)}, u32[]{:S(2)}) collective-permute-start(bf16[4,64,1536]{2,1,0:T(8,128)(2,1)} %get-tuple-element.10.own_ref), channel_id=1, source_target_pairs={{0,8},{8,0},{1,9},{9,1},{2,10},{10,2},{3,11},{11,3},{4,12},{12,4},... | collective-permute-start | bytes 2359304 | tf_op jit(solution)/shard_map/ppermute | solution.py:412
  150.8 5.9 %collective-permute-start.18 = (bf16[2,256,512]{2,1,0:T(8,128)(2,1)}, bf16[2,256,512]{2,1,0:T(8,128)(2,1)S(1)}, u32[]{:S(2)}, u32[]{:S(2)}) collective-permute-start(bf16[2,256,512]{2,1,0:T(8,128)(2,1)} %get-tuple-element.11.refs_1_), channel_id=1, source_target_pairs={{0,8},{8,0},{1,9},{9,1},{2,10},{10,2},{3,11},{11,3},{4,12},{12,4},... | collective-permute-start | bytes 1572872 | tf_op jit(solution)/shard_map/ppermute | solution.py:412
  156.7 11.8 %copy-start.1 = (bf16[4,64,1536]{2,1,0:T(8,128)(2,1)S(1)}, bf16[4,64,1536]{2,1,0:T(8,128)(2,1)}, u32[]{:S(2)}) copy-start(bf16[4,64,1536]{2,1,0:T(8,128)(2,1)} %get-tuple-element.10.own_ref) | copy-start | bytes 2359300
  156.7 11.8 %copy-start.2 = (s32[4]{0:T(128)S(1)}, s32[4]{0:T(128)}, u32[]{:S(2)}) copy-start(s32[4]{0:T(128)} %pad_add_fusion.refs_0_.ids_ref) | copy-start | bytes 52
  156.7 11.8 %copy-start.3 = (s32[4]{0:T(128)S(1)}, s32[4]{0:T(128)}, u32[]{:S(2)}) copy-start(s32[4]{0:T(128)} %ancestors_ref.1) | copy-start | bytes 52
  162.9 12.2 %all-to-all-start.3 = ((f32[16,8,128]{2,1,0:T(8,128)}), f32[16,8,128]{2,1,0:T(8,128)S(1)}, u32[]{:S(2)}, u32[]{:S(2)}) async-start(f32[16,8,128]{2,1,0:T(8,128)} %reward.3), calls=%async_computation.3 | async-start | bytes 131072 | tf_op jit(solution)/shard_map/all_to_all | solution.py:545
  (14 other events, 36.9 us)

commit v12 on v10

--- a/solution.py
+++ b/solution.py
@@ -87,8 +87,10 @@
             highest = jnp.max(scores, axis=1, keepdims=True)
             expanded = jnp.exp2((scores - highest) * factor)
             norm = 1.0 / jnp.sum(expanded, axis=1, keepdims=True)
-            weights = (expanded * norm).astype(jnp.bfloat16)
-            pieces.append(jnp.dot(weights, v_all[:, cols], preferred_element_type=jnp.float32))
+            weighted = jnp.dot(
+                expanded.astype(jnp.bfloat16), v_all[:, cols], preferred_element_type=jnp.float32
+            )
+            pieces.append(weighted * norm)
         joined = jnp.concatenate(pieces, axis=1).astype(jnp.bfloat16)
         out_ref[span] = joined.reshape(block_sources, tokens, columns)
 
@@ -363,11 +365,12 @@
 
 
 def reward_kernel(particles, scale, parts, doms, offsets, joined, *refs):
-    ids_ref, features_ref, head_ref, before_ref = refs[:4]
-    weight_refs, (out_ref, weight_vmem, rows_ref, sems) = refs[4:-4], refs[-4:]
+    ids_ref, prev_ref, head_ref = refs[:3]
+    features_refs, weight_refs = refs[3 : 3 + doms], refs[3 + doms : -4]
+    out_ref, weight_vmem, rows_ref, sems = refs[-4:]
     dom, group, seq = ids_ref[0], ids_ref[1], ids_ref[2]
     _, depth, columns = weight_refs[0].shape
-    rows = features_ref.shape[1]
+    rows = features_refs[0].shape[1]
     places = [
         (pair, shard)
         for pair in range(len(weight_refs) // parts)
@@ -390,11 +393,12 @@
             )
             copy.start()
             copies.append(copy)
-    for index in range(parts):
-        rows_ref[:, index * depth : (index + 1) * depth] = features_ref[
-            (group + parts - index) % parts
-        ]
-    totals = jnp.zeros((particles, joined * columns), jnp.float32)
+    for step, features_ref in enumerate(features_refs):
+        for index in range(parts):
+            rows_ref[step * rows : (step + 1) * rows, index * depth : (index + 1) * depth] = (
+                features_ref[(group + parts - index) % parts]
+            )
+    totals = jnp.zeros((doms * particles, joined * columns), jnp.float32)
     for step in range(count // joined):
         for copy in copies[step * joined * parts : (step + 1) * joined * parts]:
             copy.wait()
@@ -407,68 +411,54 @@
             axis=1,
         )
         scored = jax.nn.gelu(hidden) * head
-        totals += jnp.sum(scored.reshape(particles, rows // particles, -1), axis=1)
+        totals += jnp.sum(scored.reshape(doms * particles, rows // particles, -1), axis=1)
 
     sums = jnp.sum(totals, axis=1, keepdims=True) * scale
-    first = len(before_ref.shape) == 1
-    shape = out_ref.shape
+    shape = out_ref.shape[1:]
     out_rows = lax.broadcasted_iota(jnp.int32, shape, 0)
     lanes = lax.broadcasted_iota(jnp.int32, shape, 1)
-    logits = jnp.zeros(shape, jnp.float32) if first else before_ref[...]
-    row = dom if first else (dom + 1) % doms
-    for particle in range(particles):
-        here = jnp.logical_and(out_rows == row, lanes == particle)
-        value = sums[particle : particle + 1]
-        if first:
-            value = value + jnp.where(seq == 0, before_ref[particle], 0.0)
+    logits = jnp.zeros(shape, jnp.float32)
+    for index in range(doms * particles):
+        step, particle = divmod(index, particles)
+        value = sums[index : index + 1]
+        if step == 0:
+            value = value + jnp.where(seq == 0, prev_ref[particle], 0.0)
+        here = jnp.logical_and(out_rows == (dom + doms - step) % doms, lanes == particle)
         logits += jnp.where(here, value, 0.0)
-    out_ref[...] = logits
-
-
-def reward(ids, features, weights, parts, doms, offsets, head, before, particles, scale):
+    out_ref[...] = jnp.broadcast_to(logits[None], out_ref.shape)
+
+
+def reward(ids, prev_logw, features, weights, parts, offsets, head, particles, scale, copies):
     _, depth, columns = weights[0].shape
-    rows = features.shape[1]
+    rows, doms = features[0].shape[1], len(features)
     count = len(offsets)
     joined = 2 if columns % LANES == 0 and count % 2 == 0 else 1
     smem = pl.BlockSpec(memory_space=pltpu.SMEM)
     vmem = pl.BlockSpec(memory_space=pltpu.VMEM)
     return pl.pallas_call(
         functools.partial(reward_kernel, particles, scale, parts, doms, offsets, joined),
-        in_specs=[smem, vmem, vmem, smem if before.ndim == 1 else vmem]
+        in_specs=[smem, smem, vmem]
+        + [vmem] * doms
         + [pl.BlockSpec(memory_space=pltpu.HBM)] * len(weights),
         out_specs=vmem,
-        out_shape=jax.ShapeDtypeStruct((8, LANES), jnp.float32),
+        out_shape=jax.ShapeDtypeStruct((copies, 8, LANES), jnp.float32),
         scratch_shapes=[
             pltpu.VMEM((count // joined, parts * depth, joined * columns), jnp.bfloat16),
-            pltpu.VMEM((rows, parts * depth), jnp.bfloat16),
+            pltpu.VMEM((doms * rows, parts * depth), jnp.bfloat16),
             pltpu.SemaphoreType.DMA((count, parts)),
         ],
-        compiler_params=pltpu.CompilerParams(vmem_limit_bytes=20 * MIB),
+        compiler_params=pltpu.CompilerParams(vmem_limit_bytes=60 * MIB),
         cost_estimate=pl.CostEstimate(
-            flops=2 * rows * parts * depth * count * columns,
+            flops=2 * doms * rows * parts * depth * count * columns,
             bytes_accessed=2 * parts * depth * count * columns,
-            transcendentals=rows * count * columns,
+            transcendentals=doms * rows * count * columns,
         ),
         name="reward",
-    )(ids, features, head, before, *weights)
-
-
-def add_kernel(*refs):
-    refs[-1][...] = sum(ref[...] for ref in refs[:-1])
-
-
-def add_parts(parts):
-    return pl.pallas_call(
-        add_kernel,
-        out_shape=jax.ShapeDtypeStruct(parts[0].shape, parts[0].dtype),
-        compiler_params=pltpu.CompilerParams(vmem_limit_bytes=2 * MIB),
-        name="add_partials",
-    )(*parts)
-
-
-def finish_kernel(particles, doms, ids_ref, resampled_ref, *refs):
-    logit_refs, (out_ref, same_ref) = refs[:-2], refs[-2:]
-    logits = sum(ref[...] for ref in logit_refs)
+    )(ids, prev_logw, head, *features, *weights)
+
+
+def finish_kernel(particles, doms, ids_ref, resampled_ref, parts_ref, out_ref, same_ref):
+    logits = jnp.sum(parts_ref[...], axis=0)
     rows = lax.broadcasted_iota(jnp.int32, logits.shape, 0)
     lanes = lax.broadcasted_iota(jnp.int32, logits.shape, 1)
     valid = jnp.logical_and(rows < doms, lanes < particles)
@@ -479,12 +469,12 @@
     out_ref[...] = (own - log_total)[:, :particles]
 
 
-def finish(ids, logits, resampled, particles, doms):
+def finish(ids, parts, resampled, particles, doms):
     vmem = pl.BlockSpec(memory_space=pltpu.VMEM)
     anywhere = pl.BlockSpec(memory_space=pl.ANY)
     log_weights, resampled = pl.pallas_call(
         functools.partial(finish_kernel, particles, doms),
-        in_specs=[pl.BlockSpec(memory_space=pltpu.SMEM), anywhere] + [vmem] * len(logits),
+        in_specs=[pl.BlockSpec(memory_space=pltpu.SMEM), anywhere, vmem],
         out_specs=[vmem, anywhere],
         out_shape=[
             jax.ShapeDtypeStruct((1, particles), jnp.float32),
@@ -493,7 +483,7 @@
         input_output_aliases={1: 1},
         compiler_params=pltpu.CompilerParams(vmem_limit_bytes=2 * MIB),
         name="log_weights",
-    )(ids, resampled, *logits)
+    )(ids, resampled, parts)
     return resampled, log_weights.reshape(particles)
 
 
@@ -594,40 +584,39 @@
     packed[0] = gate(packed[0], [embed_share])
 
     arrived = [exchange(packed[0])]
-    up_high = swapped(up_share, "seq", high)
+    up_high, up_low = swapped(up_share, "seq", high), swapped(up_share, "seq", low)
     own_pair, own_groups = swapped(up_share, "seq", 1), over_groups(up_share)
     for bit in (low, 1):
         embed_share = jnp.concatenate([embed_share, swapped(embed_share, "seq", bit)])
-    after = [arrived[0], embed_share, up_high, own_pair, *own_groups[1:]]
+    after = [arrived[0], embed_share, up_high, up_low, own_pair, *own_groups[1:]]
     packed[1:] = [gate(piece, after) for piece in packed[1:]]
 
     arrived += [exchange(piece) for piece in packed[1:]]
-    up_far = swapped(jnp.concatenate([up_share, up_high]), "seq", low)
+    up_both = swapped(up_high, "seq", low)
     high_pair, high_groups = swapped(up_high, "seq", 1), over_groups(up_high)
-    own_pairs = [own_pair] + [swapped(piece, "seq", 1) for piece in own_groups[1:]]
+    low_pair, low_groups = swapped(up_low, "seq", 1), over_groups(up_low)
     embed_near = over_groups(embed_share)
     attended = [attention(arrived[0], head_width)]
-    after = [up_far, high_pair, *high_groups[1:], *own_pairs[1:], *embed_near[1:]]
+    after = [up_both, high_pair, low_pair, *high_groups[1:], *low_groups[1:], *embed_near[1:]]
     attended[0] = gate(attended[0], [*after, *arrived[1:]])
 
     returned = [exchange(attended[0])]
-    far_pair, far_groups = swapped(up_far, "seq", 1), over_groups(up_far)
+    both_pair, both_groups = swapped(up_both, "seq", 1), over_groups(up_both)
+    high_pairs = over_groups(high_pair)
+    attended += [attention(piece, head_width) for piece in arrived[1:]]
+    after = [returned[0], both_pair, *both_groups[1:], *high_pairs[1:]]
+    attended[1:] = [gate(piece, after) for piece in attended[1:]]
+
+    returned += [exchange(piece) for piece in attended[1:]]
     embed_parts = embed_near + [
         shifted(piece, "dom", k) for k in range(1, dom_count) for piece in embed_near
     ]
-    attended += [attention(piece, head_width) for piece in arrived[1:]]
-    after = [returned[0], *far_groups[1:], *embed_parts[group_count:]]
-    attended[1:] = [gate(piece, after) for piece in attended[1:]]
-
-    returned += [exchange(piece) for piece in attended[1:]]
-    high_pairs = [high_pair] + [swapped(piece, "seq", 1) for piece in high_groups[1:]]
-    far_pairs = over_groups(far_pair)
-    up_parts = [own_groups, own_pairs, high_groups, high_pairs, far_groups, far_pairs]
-    far = [offset ^ low for offset in near + [offset ^ high for offset in near]]
+    own_pairs, both_pairs = over_groups(own_pair), over_groups(both_pair)
+    low_pairs = [low_pair] + [swapped(piece, "seq", 1) for piece in low_groups[1:]]
+    up_parts = own_groups + own_pairs + high_groups + high_pairs
+    up_parts += low_groups + low_pairs + both_groups + both_pairs
     up_offsets = [
-        [offset ^ bit for offset in offsets]
-        for offsets in (near, [offset ^ high for offset in near], far)
-        for bit in (0, 1)
+        offset ^ bit ^ pair for bit in (0, high, low, high ^ low) for pair in (0, 1) for offset in near
     ]
     embed_offsets = near + [offset ^ high for offset in near]
     for bit in (low, 1):
@@ -646,38 +635,26 @@
         embed_parts,
         norm_gain,
         group_count,
-        [*high_pairs[1:], *far_pairs],
+        [*own_pairs[1:], *low_pairs[1:], *both_pairs[1:]],
     )
     stepped_other = shifted(stepped, "dom", 1)
     features_other = shifted(features, "dom", 1)
 
     scale = potential_scale / math.sqrt(tokens * seq_count)
     head = head_weight.reshape(seq_count * dom_count, 1, up_columns)
-    score = functools.partial(
-        reward,
+    partial = reward(
         ids,
-        weights=[piece for pieces in up_parts for piece in pieces],
-        parts=group_count,
-        doms=dom_count,
-        offsets=[offset for offsets in up_offsets for offset in offsets],
-        head=head,
-        particles=particles,
-        scale=scale,
+        prev_logw,
+        [features, features_other],
+        up_parts,
+        group_count,
+        up_offsets,
+        head,
+        particles,
+        scale,
+        dom_count * seq_count,
     )
-    partial_own = score(features, before=prev_logw)
-    partial = score(features_other, before=partial_own)
-    partial = add_parts(
-        [partial] + [swapped(partial, "seq", 2 * k) for k in range(1, seq_count // 2)]
-    )
-    pair = [
-        (d * seq_count + i, (d + k) % dom_count * seq_count + (i ^ 1))
-        for k in range(1, dom_count)
-        for d in range(dom_count)
-        for i in range(seq_count)
-    ]
-    logits = [partial, swapped(partial, "seq", 1), lax.ppermute(partial, ("dom", "seq"), pair)] + [
-        shifted(partial, "dom", k) for k in range(1, dom_count)
-    ]
+    logits = lax.all_to_all(partial, ("dom", "seq"), 0, 0, tiled=True)
     resampled = resample(ids, ancestors.astype(jnp.int32), stepped, stepped_other)
     return finish(ids, logits, resampled, particles, dom_count)
 

time: 176 us -> 170 us (0.966)
  local copies, waits for them, and re-layouts: 11.8 us -> 8.62 us
    ppermute x10 -> x12, waiting for transfers between devices: 21 us -> 2.78 us  [shifted(): lax.ppermute(array, axis, [(i, (i + step) % count) for i in range(count)])]
    ppermute x14 -> x11, waiting for transfers between devices: 37.8 us -> 51 us  [swapped(): lax.ppermute(array, axis, [(i, i ^ bit) for i in range(lax.axis_size(axis...]
    all_to_all x0 -> x1, starting transfers between devices: none -> 5.83 us  [on_device(): logits = lax.all_to_all(partial, ('dom', 'seq'), 0, 0, tiled=True)]
    ppermute x14 -> x11, starting transfers between devices: 26.1 us -> 21.3 us  [swapped(): lax.ppermute(array, axis, [(i, i ^ bit) for i in range(lax.axis_size(axis...]
    all_to_all x0 -> x1, waiting for transfers between devices: none -> 4.69 us  [on_device(): logits = lax.all_to_all(partial, ('dom', 'seq'), 0, 0, tiled=True)]
    unnamed x78 -> x48, local copies, waits for them, and re-layouts: 10.8 us -> 7.61 us
    all_to_all x4, starting transfers between devices: 22.6 us -> 20.4 us  [exchange(): return lax.all_to_all(array, 'seq', 0, 0, tiled=True)]
    ppermute x10 -> x12, starting transfers between devices: 8.38 us -> 10.2 us  [shifted(): lax.ppermute(array, axis, [(i, (i + step) % count) for i in range(count)])]
  transfers between devices with their start and end apart: 29 -> 28, of which waited for: 12 -> 11; matrix products, arithmetic and copies ran while one was open for 2% -> 2% of each run, Pallas kernels for 18% -> 17%
where the time goes in v12:
time: 170 us; the launch traced here: 169 us
  waiting for transfers between devices  58.5 us (34%)
  starting transfers between devices  57.8 us (34%)
  Pallas kernels  39.4 us (23%)
  local copies, waits for them, and re-layouts  8.62 us (5%)
  other arithmetic  3.28 us (2%)
    ppermute x11, waiting for transfers between devices, swapped(): lax.ppermute(array, axis, [(i, i ^ bit) for i in range(lax.axis_size(axis...  51 us
    ppermute x11, starting transfers between devices, swapped(): lax.ppermute(array, axis, [(i, i ^ bit) for i in range(lax.axis_size(axis...  21.3 us
    all_to_all x4, starting transfers between devices, exchange(): return lax.all_to_all(array, 'seq', 0, 0, tiled=True)  20.4 us
    pallas_call x2, Pallas kernels, attention(): pl.pallas_call(functools.partial(attention_kernel, head_width, block_sour...  12.1 us
    ppermute x12, starting transfers between devices, shifted(): lax.ppermute(array, axis, [(i, (i + step) % count) for i in range(count)])  10.2 us
    pallas_call x1, Pallas kernels, project_embed(): pl.pallas_call(kernel, in_specs=[smem, hbm, vmem, hbm] + ([] if begun is...  8.71 us
    unnamed x48, local copies, waits for them, and re-layouts  7.61 us
    pallas_call x1, Pallas kernels, reward(): pl.pallas_call(functools.partial(reward_kernel, particles, scale, parts,...  7.28 us
  transfers between devices with their start and end apart: 28, of which 11 were waited for; matrix products, arithmetic and copies ran while one was open for 2% of the time, Pallas kernels for 17%

profile of v12, /device:TPU:0, one launch (start us, length us, event | category | flops | bytes accessed | tf_op | source)
XLA Modules:
  0.0 169.0 jit_solution(14059238630533331083)
XLA Ops:
  1.6 4.0 %collective-permute-start = (bf16[1,192,256]{2,1,0:T(8,128)(2,1)S(1)}, bf16[1,192,256]{2,1,0:T(8,128)(2,1)S(1)}, u32[]{:S(2)}, u32[]{:S(2)}) collective-permute-start(bf16[1,192,256]{2,1,0:T(8,128)(2,1)S(1)} %dynamic-slice_bitcast_fusion.1), channel_id=1, source_target_pairs={{0,4},{1,5},{2,6},{3,7},{4,0},{5,1},{6,2},{7,3},{8,12},{9,13},{10,... | collective-permute-start | bytes 294920 | tf_op jit(solution)/shard_map/ppermute | solution.py:527
  5.7 3.2 %pack_heads.1 = (bf16[8,3,64,384]{3,2,1,0:T(8,128)(2,1)}, bf16[8,3,64,384]{3,2,1,0:T(8,128)(2,1)}) custom-call(bf16[4,64,1536]{2,1,0:T(8,128)(2,1)} %q_ref.1, bf16[4,64,1536]{2,1,0:T(8,128)(2,1)} %k_ref.1, bf16[4,64,1536]{2,1,0:T(8,128)(2,1)} %v_ref.1), custom_call_target="tpu_custom_call" | custom-call | tf_op jit(solution)/shard_map/pack_heads/pallas_call | solution.py:40
  8.9 1.7 collective-permute-done
  11.3 5.9 %all-to-all-start = ((bf16[8,3,64,384]{3,2,1,0:T(8,128)(2,1)}), bf16[8,3,64,384]{3,2,1,0:T(8,128)(2,1)S(1)}, u32[]{:S(2)}, u32[]{:S(2)}) async-start(bf16[8,3,64,384]{3,2,1,0:T(8,128)(2,1)} %gate.4), calls=%async_computation | async-start | bytes 2359296 | tf_op jit(solution)/shard_map/all_to_all | solution.py:531
  17.2 2.0 %collective-permute-start.8 = (bf16[2,192,256]{2,1,0:T(8,128)(2,1)S(1)}, bf16[2,192,256]{2,1,0:T(8,128)(2,1)S(1)}, u32[]{:S(2)}, u32[]{:S(2)}) collective-permute-start(bf16[2,192,256]{2,1,0:T(8,128)(2,1)S(1)} %copy-done.9), channel_id=1, source_target_pairs={{0,2},{1,3},{2,0},{3,1},{4,6},{5,7},{6,4},{7,5},{8,10},{9,11},{10,... | collective-permute-start | bytes 589832 | tf_op jit(solution)/shard_map/ppermute | solution.py:527
  19.2 22.1 %collective-permute-done.8 = bf16[2,192,256]{2,1,0:T(8,128)(2,1)S(1)} collective-permute-done((bf16[2,192,256]{2,1,0:T(8,128)(2,1)S(1)}, bf16[2,192,256]{2,1,0:T(8,128)(2,1)S(1)}, u32[]{:S(2)}, u32[]{:S(2)}) %collective-permute-start.8) | collective-permute-done | bytes 196640 | tf_op jit(solution)/shard_map/ppermute | solution.py:527
  42.6 4.4 %collective-permute-start.1 = (bf16[1,512,256]{2,1,0:T(8,128)(2,1)S(1)}, bf16[1,512,256]{2,1,0:T(8,128)(2,1)}, u32[]{:S(2)}, u32[]{:S(2)}) collective-permute-start(bf16[1,512,256]{2,1,0:T(8,128)(2,1)S(1)} %dynamic-slice_bitcast_fusion.refs_5_), channel_id=1, source_target_pairs={{0,4},{1,5},{2,6},{3,7},{4,0},{5,1},{6,2},{7,3},{8,12},{9,13},{10,... | collective-permute-start | bytes 786440 | tf_op jit(solution)/shard_map/ppermute | solution.py:527
  47.6 1.5 collective-permute-start.12
  49.1 4.5 %collective-permute-done.9 = bf16[4,192,256]{2,1,0:T(8,128)(2,1)} collective-permute-done((bf16[4,192,256]{2,1,0:T(8,128)(2,1)S(1)}, bf16[4,192,256]{2,1,0:T(8,128)(2,1)}, u32[]{:S(2)}, u32[]{:S(2)}) %collective-permute-start.9) | collective-permute-done | bytes 393248 | tf_op jit(solution)/shard_map/ppermute | solution.py:527
  53.6 2.0 %pad_maximum_fusion.refs_2_.refs_6_ = bf16[8,192,256]{2,1,0:T(8,128)(2,1)} fusion(bf16[4,192,256]{2,1,0:T(8,128)(2,1)} %collective-permute-done.9, bf16[2,192,256]{2,1,0:T(8,128)(2,1)S(1)} %collective-permute-done.8, bf16[1,192,256]{2,1,0:T(8,128)(2,1)S(1)} %collective-permute-done, bf16[1,192,256]{2,1,0:T(8,128)(2,1)S(1)} %dynamic-slice_bitcast_fusion.1), kind=kLoop, calls=%fused_computation | loop fusion | flops 1179648 | bytes 1572864 | tf_op jit(solution)/shard_map/concatenate | solution.py:590
  55.6 2.4 %collective-permute-done.1.refs_3_.refs_9_ = bf16[1,512,256]{2,1,0:T(8,128)(2,1)} collective-permute-done((bf16[1,512,256]{2,1,0:T(8,128)(2,1)S(1)}, bf16[1,512,256]{2,1,0:T(8,128)(2,1)}, u32[]{:S(2)}, u32[]{:S(2)}) %collective-permute-start.1) | collective-permute-done | bytes 262176 | tf_op jit(solution)/shard_map/ppermute | solution.py:527
  60.7 4.4 %all-to-all-start.1 = ((bf16[8,3,64,384]{3,2,1,0:T(8,128)(2,1)}), bf16[8,3,64,384]{3,2,1,0:T(8,128)(2,1)S(1)}, u32[]{:S(2)}, u32[]{:S(2)}) async-start(bf16[8,3,64,384]{3,2,1,0:T(8,128)(2,1)} %gate.5), calls=%async_computation.1 | async-start | bytes 2359296 | tf_op jit(solution)/shard_map/all_to_all | solution.py:531
  65.0 1.6 collective-permute-start.10
  66.6 2.0 %collective-permute-start.2 = (bf16[1,512,256]{2,1,0:T(8,128)(2,1)}, bf16[1,512,256]{2,1,0:T(8,128)(2,1)S(1)}, u32[]{:S(2)}, u32[]{:S(2)}) collective-permute-start(bf16[1,512,256]{2,1,0:T(8,128)(2,1)} %collective-permute-done.1.refs_3_.refs_9_), channel_id=1, source_target_pairs={{0,2},{1,3},{2,0},{3,1},{4,6},{5,7},{6,4},{7,5},{8,10},{9,11},{10,... | collective-permute-start | bytes 786440 | tf_op jit(solution)/shard_map/ppermute | solution.py:527
  70.6 1.5 collective-permute-start.7
  72.0 16.6 %collective-permute-done.2.refs_1_.refs_17_ = bf16[1,512,256]{2,1,0:T(8,128)(2,1)S(1)} collective-permute-done((bf16[1,512,256]{2,1,0:T(8,128)(2,1)}, bf16[1,512,256]{2,1,0:T(8,128)(2,1)S(1)}, u32[]{:S(2)}, u32[]{:S(2)}) %collective-permute-start.2) | collective-permute-done | bytes 262176 | tf_op jit(solution)/shard_map/ppermute | solution.py:527
  88.6 1.6 collective-permute-start.5
  90.2 6.1 %attention.2.refs_0_ = bf16[8,64,384]{2,1,0:T(8,128)(2,1)} custom-call(bf16[8,3,64,384]{3,2,1,0:T(8,128)(2,1)} %copy-done.5), custom_call_target="tpu_custom_call" | custom-call | flops 402653184 | bytes 1572864 | tf_op jit(solution)/shard_map/attention/pallas_call | solution.py:106
  98.3 5.6 %all-to-all-start.2 = ((bf16[8,64,384]{2,1,0:T(8,128)(2,1)}), bf16[8,64,384]{2,1,0:T(8,128)(2,1)S(1)}, u32[]{:S(2)}, u32[]{:S(2)}) async-start(bf16[8,64,384]{2,1,0:T(8,128)(2,1)} %gate.6), calls=%async_computation.2 | async-start | bytes 786432 | tf_op jit(solution)/shard_map/all_to_all | solution.py:531
  103.9 2.0 %collective-permute-start.13 = (bf16[1,512,256]{2,1,0:T(8,128)(2,1)S(1)}, bf16[1,512,256]{2,1,0:T(8,128)(2,1)S(1)}, u32[]{:S(2)}, u32[]{:S(2)}) collective-permute-start(bf16[1,512,256]{2,1,0:T(8,128)(2,1)S(1)} %copy-done.12), channel_id=1, source_target_pairs={{0,1},{1,0},{2,3},{3,2},{4,5},{5,4},{6,7},{7,6},{8,9},{9,8},{10,11... | collective-permute-start | bytes 786440 | tf_op jit(solution)/shard_map/ppermute | solution.py:527
  108.5 6.1 %attention.3.refs_0_ = bf16[8,64,384]{2,1,0:T(8,128)(2,1)} custom-call(bf16[8,3,64,384]{3,2,1,0:T(8,128)(2,1)} %copy-done.6), custom_call_target="tpu_custom_call" | custom-call | flops 402653184 | bytes 1572864 | tf_op jit(solution)/shard_map/attention/pallas_call | solution.py:106
  116.9 4.5 %all-to-all-start.3 = ((bf16[8,64,384]{2,1,0:T(8,128)(2,1)}), bf16[8,64,384]{2,1,0:T(8,128)(2,1)S(1)}, u32[]{:S(2)}, u32[]{:S(2)}) async-start(bf16[8,64,384]{2,1,0:T(8,128)(2,1)} %gate.7), calls=%async_computation.3 | async-start | bytes 786432 | tf_op jit(solution)/shard_map/all_to_all | solution.py:531
  121.4 1.5 collective-permute-start.18
  122.9 2.0 %collective-permute-start.19 = (bf16[1,512,256]{2,1,0:T(8,128)(2,1)S(1)}, bf16[1,512,256]{2,1,0:T(8,128)(2,1)}, u32[]{:S(2)}, u32[]{:S(2)}) collective-permute-start(bf16[1,512,256]{2,1,0:T(8,128)(2,1)S(1)} %copy-done.16), channel_id=1, source_target_pairs={{0,1},{1,0},{2,3},{3,2},{4,5},{5,4},{6,7},{7,6},{8,9},{9,8},{10,11... | collective-permute-start | bytes 786440 | tf_op jit(solution)/shard_map/ppermute | solution.py:527
  126.7 4.7 %first_project.1.refs_4_ = f32[256,1536]{1,0:T(8,128)} custom-call(bf16[4,64,1536]{2,1,0:T(8,128)(2,1)} %refs_1_.2, bf16[1536,1536]{1,0:T(8,128)(2,1)} %refs_3_.1, bf16[8,64,384]{2,1,0:T(8,128)(2,1)} %copy-done.7), custom_call_target="tpu_custom_call" | custom-call | flops 603979776 | bytes 5505024 | tf_op jit(solution)/shard_map/first_project/pallas_call | solution.py:183
  131.4 2.7 %collective-permute-done.19.refs_11_.refs_16_ = bf16[1,512,256]{2,1,0:T(8,128)(2,1)} collective-permute-done((bf16[1,512,256]{2,1,0:T(8,128)(2,1)S(1)}, bf16[1,512,256]{2,1,0:T(8,128)(2,1)}, u32[]{:S(2)}, u32[]{:S(2)}) %collective-permute-start.19) | collective-permute-done | bytes 262176 | tf_op jit(solution)/shard_map/ppermute | solution.py:527
  136.1 8.7 %project_embed.1 = (bf16[4,64,1536]{2,1,0:T(8,128)(2,1)}, bf16[2,256,512]{2,1,0:T(8,128)(2,1)}) custom-call(s32[4]{0:T(128)} %pad_add_fusion.refs_0_.ids_ref, bf16[4,64,1536]{2,1,0:T(8,128)(2,1)} %refs_1_.2, f32[1,1024]{1,0:T(1,128)} %bitcast.10, bf16[1536,1536]{1,0:T(8,128)(2,1)} %refs_3_.1, f32[256,1536]{1,0:T(8,128)} %first_project.1.refs_4_, ...), custom_call_target="tpu_custom_call" | custom-call | flops 1409286144 | bytes 10223616 | tf_op jit(solution)/shard_map/project_embed/pallas_call | solution.py:333
  145.4 1.6 collective-permute-done.22.refs_4_
  147.8 7.3 %reward.1 = f32[16,8,128]{2,1,0:T(8,128)} custom-call(s32[4]{0:T(128)} %pad_add_fusion.refs_0_.ids_ref, f32[4]{0:T(128)} %refs_1_.3, f32[16,1,256]{2,1,0:T(1,128)} %bitcast.11, bf16[2,256,512]{2,1,0:T(8,128)(2,1)} %get-tuple-element.11.refs_3_, bf16[2,256,512]{2,1,0:T(8,128)(2,1)} %copy-done.23, bf16[1,512,256]{2,1,0:T(8,128)(2,1)} %copy-done.20, ...), custom_call_target="tpu_custom_call" | custom-call | flops 2147483648 | bytes 4194304 | tf_op jit(solution)/shard_map/reward/pallas_call | solution.py:438
  155.1 5.8 %all-to-all-start.4 = ((f32[16,8,128]{2,1,0:T(8,128)}), f32[16,8,128]{2,1,0:T(8,128)S(1)}, u32[]{:S(2)}, u32[]{:S(2)}) async-start(f32[16,8,128]{2,1,0:T(8,128)} %reward.1), calls=%async_computation.4 | async-start | bytes 131072 | tf_op jit(solution)/shard_map/all_to_all | solution.py:657
  161.0 2.0 %resample.1.resampled_ref = bf16[4,64,1536]{2,1,0:T(8,128)(2,1)} custom-call(s32[4]{0:T(128)S(1)} %copy-done.2, s32[4]{0:T(128)S(1)} %copy-done.3, bf16[4,64,1536]{2,1,0:T(8,128)(2,1)S(1)} %copy-done.1, bf16[4,64,1536]{2,1,0:T(8,128)(2,1)S(1)} %collective-permute-done.21.other_ref), custom_call_target="tpu_custom_call" | custom-call | tf_op jit(solution)/shard_map/resample/pallas_call | solution.py:507
  163.0 4.7 %all-to-all-done.4.parts_ref = f32[16,8,128]{2,1,0:T(8,128)S(1)} async-done(((f32[16,8,128]{2,1,0:T(8,128)}), f32[16,8,128]{2,1,0:T(8,128)S(1)}, u32[]{:S(2)}, u32[]{:S(2)}) %all-to-all-start.4) | async-done | bytes 65568 | tf_op jit(solution)/shard_map/all_to_all | solution.py:657
  (90 shorter events, 20.8 us)
Async XLA Ops:
  0.6 42.0 %copy-start = (bf16[1024,512]{1,0:T(8,128)(2,1)S(1)}, bf16[1024,512]{1,0:T(8,128)(2,1)}, u32[]{:S(2)}) copy-start(bf16[1024,512]{1,0:T(8,128)(2,1)} %param.20) | copy-start | bytes 3145732
  1.6 8.9 %collective-permute-start = (bf16[1,192,256]{2,1,0:T(8,128)(2,1)S(1)}, bf16[1,192,256]{2,1,0:T(8,128)(2,1)S(1)}, u32[]{:S(2)}, u32[]{:S(2)}) collective-permute-start(bf16[1,192,256]{2,1,0:T(8,128)(2,1)S(1)} %dynamic-slice_bitcast_fusion.1), channel_id=1, source_target_pairs={{0,4},{1,5},{2,6},{3,7},{4,0},{5,1},{6,2},{7,3},{8,12},{9,13},{10,... | collective-permute-start | bytes 294920 | tf_op jit(solution)/shard_map/ppermute | solution.py:527
  11.3 48.4 %all-to-all-start = ((bf16[8,3,64,384]{3,2,1,0:T(8,128)(2,1)}), bf16[8,3,64,384]{3,2,1,0:T(8,128)(2,1)S(1)}, u32[]{:S(2)}, u32[]{:S(2)}) async-start(bf16[8,3,64,384]{3,2,1,0:T(8,128)(2,1)} %gate.4), calls=%async_computation | async-start | bytes 2359296 | tf_op jit(solution)/shard_map/all_to_all | solution.py:531
  17.2 24.2 %collective-permute-start.8 = (bf16[2,192,256]{2,1,0:T(8,128)(2,1)S(1)}, bf16[2,192,256]{2,1,0:T(8,128)(2,1)S(1)}, u32[]{:S(2)}, u32[]{:S(2)}) collective-permute-start(bf16[2,192,256]{2,1,0:T(8,128)(2,1)S(1)} %copy-done.9), channel_id=1, source_target_pairs={{0,2},{1,3},{2,0},{3,1},{4,6},{5,7},{6,4},{7,5},{8,10},{9,11},{10,... | collective-permute-start | bytes 589832 | tf_op jit(solution)/shard_map/ppermute | solution.py:527
  41.4 12.2 %collective-permute-start.9 = (bf16[4,192,256]{2,1,0:T(8,128)(2,1)S(1)}, bf16[4,192,256]{2,1,0:T(8,128)(2,1)}, u32[]{:S(2)}, u32[]{:S(2)}) collective-permute-start(bf16[4,192,256]{2,1,0:T(8,128)(2,1)S(1)} %pad_maximum_fusion.1), channel_id=1, source_target_pairs={{0,1},{1,0},{2,3},{3,2},{4,5},{5,4},{6,7},{7,6},{8,9},{9,8},{10,11... | collective-permute-start | bytes 1179656 | tf_op jit(solution)/shard_map/ppermute | solution.py:527
  42.6 16.3 %copy-start.20 = (bf16[1,512,256]{2,1,0:T(8,128)(2,1)}, bf16[1,512,256]{2,1,0:T(8,128)(2,1)S(1)}, u32[]{:S(2)}) copy-start(bf16[1,512,256]{2,1,0:T(8,128)(2,1)S(1)} %dynamic-slice_bitcast_fusion.refs_5_) | copy-start | bytes 786436
  42.6 15.3 %collective-permute-start.1 = (bf16[1,512,256]{2,1,0:T(8,128)(2,1)S(1)}, bf16[1,512,256]{2,1,0:T(8,128)(2,1)}, u32[]{:S(2)}, u32[]{:S(2)}) collective-permute-start(bf16[1,512,256]{2,1,0:T(8,128)(2,1)S(1)} %dynamic-slice_bitcast_fusion.refs_5_), channel_id=1, source_target_pairs={{0,4},{1,5},{2,6},{3,7},{4,0},{5,1},{6,2},{7,3},{8,12},{9,13},{10,... | collective-permute-start | bytes 786440 | tf_op jit(solution)/shard_map/ppermute | solution.py:527
  47.0 11.9 %collective-permute-start.4 = (bf16[1,512,256]{2,1,0:T(8,128)(2,1)S(1)}, bf16[1,512,256]{2,1,0:T(8,128)(2,1)S(1)}, u32[]{:S(2)}, u32[]{:S(2)}) collective-permute-start(bf16[1,512,256]{2,1,0:T(8,128)(2,1)S(1)} %dynamic-slice_bitcast_fusion.refs_5_), channel_id=1, source_target_pairs={{0,2},{1,3},{2,0},{3,1},{4,6},{5,7},{6,4},{7,5},{8,10},{9,11},{10,... | collective-permute-start | bytes 786440 | tf_op jit(solution)/shard_map/ppermute | solution.py:527
  47.0 11.9 %collective-permute-start.11 = (bf16[1,512,256]{2,1,0:T(8,128)(2,1)S(1)}, bf16[1,512,256]{2,1,0:T(8,128)(2,1)S(1)}, u32[]{:S(2)}, u32[]{:S(2)}) collective-permute-start(bf16[1,512,256]{2,1,0:T(8,128)(2,1)S(1)} %dynamic-slice_bitcast_fusion.refs_5_), channel_id=1, source_target_pairs={{0,1},{1,0},{2,3},{3,2},{4,5},{5,4},{6,7},{7,6},{8,9},{9,8},{10,11... | collective-permute-start | bytes 786440 | tf_op jit(solution)/shard_map/ppermute | solution.py:527
  47.6 12.1 %collective-permute-start.12 = (bf16[1,512,256]{2,1,0:T(8,128)(2,1)S(1)}, bf16[1,512,256]{2,1,0:T(8,128)(2,1)}, u32[]{:S(2)}, u32[]{:S(2)}) collective-permute-start(bf16[1,512,256]{2,1,0:T(8,128)(2,1)S(1)} %dynamic-slice_bitcast_fusion.refs_5_), channel_id=1, source_target_pairs={{0,16},{16,0},{1,17},{17,1},{2,18},{18,2},{3,19},{19,3},{4,20},{20... | collective-permute-start | bytes 786440 | tf_op jit(solution)/shard_map/ppermute | solution.py:523
  60.7 36.5 %all-to-all-start.1 = ((bf16[8,3,64,384]{3,2,1,0:T(8,128)(2,1)}), bf16[8,3,64,384]{3,2,1,0:T(8,128)(2,1)S(1)}, u32[]{:S(2)}, u32[]{:S(2)}) async-start(bf16[8,3,64,384]{3,2,1,0:T(8,128)(2,1)} %gate.5), calls=%async_computation.1 | async-start | bytes 2359296 | tf_op jit(solution)/shard_map/all_to_all | solution.py:531
  65.0 32.1 %collective-permute-start.10 = (bf16[8,192,256]{2,1,0:T(8,128)(2,1)S(1)}, bf16[8,192,256]{2,1,0:T(8,128)(2,1)}, u32[]{:S(2)}, u32[]{:S(2)}) collective-permute-start(bf16[8,192,256]{2,1,0:T(8,128)(2,1)S(1)} %copy-done.4), channel_id=1, source_target_pairs={{0,16},{16,0},{1,17},{17,1},{2,18},{18,2},{3,19},{19,3},{4,20},{20... | collective-permute-start | bytes 2359304 | tf_op jit(solution)/shard_map/ppermute | solution.py:523
  66.6 22.0 %collective-permute-start.2 = (bf16[1,512,256]{2,1,0:T(8,128)(2,1)}, bf16[1,512,256]{2,1,0:T(8,128)(2,1)S(1)}, u32[]{:S(2)}, u32[]{:S(2)}) collective-permute-start(bf16[1,512,256]{2,1,0:T(8,128)(2,1)} %collective-permute-done.1.refs_3_.refs_9_), channel_id=1, source_target_pairs={{0,2},{1,3},{2,0},{3,1},{4,6},{5,7},{6,4},{7,5},{8,10},{9,11},{10,... | collective-permute-start | bytes 786440 | tf_op jit(solution)/shard_map/ppermute | solution.py:527
  68.6 27.7 %collective-permute-start.3 = (bf16[1,512,256]{2,1,0:T(8,128)(2,1)}, bf16[1,512,256]{2,1,0:T(8,128)(2,1)S(1)}, u32[]{:S(2)}, u32[]{:S(2)}) collective-permute-start(bf16[1,512,256]{2,1,0:T(8,128)(2,1)} %collective-permute-done.1.refs_3_.refs_9_), channel_id=1, source_target_pairs={{0,1},{1,0},{2,3},{3,2},{4,5},{5,4},{6,7},{7,6},{8,9},{9,8},{10,11... | collective-permute-start | bytes 786440 | tf_op jit(solution)/shard_map/ppermute | solution.py:527
  70.0 26.3 %collective-permute-start.6 = (bf16[1,512,256]{2,1,0:T(8,128)(2,1)}, bf16[1,512,256]{2,1,0:T(8,128)(2,1)S(1)}, u32[]{:S(2)}, u32[]{:S(2)}) collective-permute-start(bf16[1,512,256]{2,1,0:T(8,128)(2,1)} %collective-permute-done.1.refs_3_.refs_9_), channel_id=1, source_target_pairs={{0,16},{16,0},{1,17},{17,1},{2,18},{18,2},{3,19},{19,3},{4,20},{20... | collective-permute-start | bytes 786440 | tf_op jit(solution)/shard_map/ppermute | solution.py:523
  70.6 25.8 %collective-permute-start.7 = (bf16[1,512,256]{2,1,0:T(8,128)(2,1)}, bf16[1,512,256]{2,1,0:T(8,128)(2,1)S(1)}, u32[]{:S(2)}, u32[]{:S(2)}) collective-permute-start(bf16[1,512,256]{2,1,0:T(8,128)(2,1)} %copy-done.21), channel_id=1, source_target_pairs={{0,16},{16,0},{1,17},{17,1},{2,18},{18,2},{3,19},{19,3},{4,20},{20... | collective-permute-start | bytes 786440 | tf_op jit(solution)/shard_map/ppermute | solution.py:523
  88.6 7.7 %collective-permute-start.5 = (bf16[1,512,256]{2,1,0:T(8,128)(2,1)}, bf16[1,512,256]{2,1,0:T(8,128)(2,1)}, u32[]{:S(2)}, u32[]{:S(2)}) collective-permute-start(bf16[1,512,256]{2,1,0:T(8,128)(2,1)} %copy-done.21), channel_id=1, source_target_pairs={{0,1},{1,0},{2,3},{3,2},{4,5},{5,4},{6,7},{7,6},{8,9},{9,8},{10,11... | collective-permute-start | bytes 786440 | tf_op jit(solution)/shard_map/ppermute | solution.py:527
  98.3 17.9 %all-to-all-start.2 = ((bf16[8,64,384]{2,1,0:T(8,128)(2,1)}), bf16[8,64,384]{2,1,0:T(8,128)(2,1)S(1)}, u32[]{:S(2)}, u32[]{:S(2)}) async-start(bf16[8,64,384]{2,1,0:T(8,128)(2,1)} %gate.6), calls=%async_computation.2 | async-start | bytes 786432 | tf_op jit(solution)/shard_map/all_to_all | solution.py:531
  103.9 10.6 %collective-permute-start.13 = (bf16[1,512,256]{2,1,0:T(8,128)(2,1)S(1)}, bf16[1,512,256]{2,1,0:T(8,128)(2,1)S(1)}, u32[]{:S(2)}, u32[]{:S(2)}) collective-permute-start(bf16[1,512,256]{2,1,0:T(8,128)(2,1)S(1)} %copy-done.12), channel_id=1, source_target_pairs={{0,1},{1,0},{2,3},{3,2},{4,5},{5,4},{6,7},{7,6},{8,9},{9,8},{10,11... | collective-permute-start | bytes 786440 | tf_op jit(solution)/shard_map/ppermute | solution.py:527
  105.9 8.6 %collective-permute-start.14 = (bf16[1,512,256]{2,1,0:T(8,128)(2,1)S(1)}, bf16[1,512,256]{2,1,0:T(8,128)(2,1)S(1)}, u32[]{:S(2)}, u32[]{:S(2)}) collective-permute-start(bf16[1,512,256]{2,1,0:T(8,128)(2,1)S(1)} %copy-done.12), channel_id=1, source_target_pairs={{0,16},{16,0},{1,17},{17,1},{2,18},{18,2},{3,19},{19,3},{4,20},{20... | collective-permute-start | bytes 786440 | tf_op jit(solution)/shard_map/ppermute | solution.py:523
  107.4 8.7 %collective-permute-start.15 = (bf16[1,512,256]{2,1,0:T(8,128)(2,1)}, bf16[1,512,256]{2,1,0:T(8,128)(2,1)}, u32[]{:S(2)}, u32[]{:S(2)}) collective-permute-start(bf16[1,512,256]{2,1,0:T(8,128)(2,1)} %copy-done.13), channel_id=1, source_target_pairs={{0,16},{16,0},{1,17},{17,1},{2,18},{18,2},{3,19},{19,3},{4,20},{20... | collective-permute-start | bytes 786440 | tf_op jit(solution)/shard_map/ppermute | solution.py:523
  108.0 27.1 %collective-permute-start.16 = (bf16[8,192,256]{2,1,0:T(8,128)(2,1)S(1)}, bf16[8,192,256]{2,1,0:T(8,128)(2,1)S(1)}, u32[]{:S(2)}, u32[]{:S(2)}) collective-permute-start(bf16[8,192,256]{2,1,0:T(8,128)(2,1)S(1)} %copy-done.4), channel_id=1, source_target_pairs={{0,8},{8,0},{1,9},{9,1},{2,10},{10,2},{3,11},{11,3},{4,12},{12,4},... | collective-permute-start | bytes 2359304 | tf_op jit(solution)/shard_map/ppermute | solution.py:523
  108.0 27.1 %collective-permute-start.17 = (bf16[8,192,256]{2,1,0:T(8,128)(2,1)}, bf16[8,192,256]{2,1,0:T(8,128)(2,1)}, u32[]{:S(2)}, u32[]{:S(2)}) collective-permute-start(bf16[8,192,256]{2,1,0:T(8,128)(2,1)} %collective-permute-done.10.refs_6_.refs_7_), channel_id=1, source_target_pairs={{0,8},{8,0},{1,9},{9,1},{2,10},{10,2},{3,11},{11,3},{4,12},{12,4},... | collective-permute-start | bytes 2359304 | tf_op jit(solution)/shard_map/ppermute | solution.py:523
  116.9 18.2 %all-to-all-start.3 = ((bf16[8,64,384]{2,1,0:T(8,128)(2,1)}), bf16[8,64,384]{2,1,0:T(8,128)(2,1)S(1)}, u32[]{:S(2)}, u32[]{:S(2)}) async-start(bf16[8,64,384]{2,1,0:T(8,128)(2,1)} %gate.7), calls=%async_computation.3 | async-start | bytes 786432 | tf_op jit(solution)/shard_map/all_to_all | solution.py:531
  121.4 10.0 %collective-permute-start.18 = (bf16[1,512,256]{2,1,0:T(8,128)(2,1)}, bf16[1,512,256]{2,1,0:T(8,128)(2,1)}, u32[]{:S(2)}, u32[]{:S(2)}) collective-permute-start(bf16[1,512,256]{2,1,0:T(8,128)(2,1)} %copy-done.22), channel_id=1, source_target_pairs={{0,16},{16,0},{1,17},{17,1},{2,18},{18,2},{3,19},{19,3},{4,20},{20... | collective-permute-start | bytes 786440 | tf_op jit(solution)/shard_map/ppermute | solution.py:523
  122.9 11.2 %collective-permute-start.19 = (bf16[1,512,256]{2,1,0:T(8,128)(2,1)S(1)}, bf16[1,512,256]{2,1,0:T(8,128)(2,1)}, u32[]{:S(2)}, u32[]{:S(2)}) collective-permute-start(bf16[1,512,256]{2,1,0:T(8,128)(2,1)S(1)} %copy-done.16), channel_id=1, source_target_pairs={{0,1},{1,0},{2,3},{3,2},{4,5},{5,4},{6,7},{7,6},{8,9},{9,8},{10,11... | collective-permute-start | bytes 786440 | tf_op jit(solution)/shard_map/ppermute | solution.py:527
  124.9 10.1 %collective-permute-start.20 = (bf16[1,512,256]{2,1,0:T(8,128)(2,1)S(1)}, bf16[1,512,256]{2,1,0:T(8,128)(2,1)}, u32[]{:S(2)}, u32[]{:S(2)}) collective-permute-start(bf16[1,512,256]{2,1,0:T(8,128)(2,1)S(1)} %copy-done.18), channel_id=1, source_target_pairs={{0,16},{16,0},{1,17},{17,1},{2,18},{18,2},{3,19},{19,3},{4,20},{20... | collective-permute-start | bytes 786440 | tf_op jit(solution)/shard_map/ppermute | solution.py:523
  144.9 2.2 %collective-permute-start.22 = (bf16[2,256,512]{2,1,0:T(8,128)(2,1)}, bf16[2,256,512]{2,1,0:T(8,128)(2,1)S(1)}, u32[]{:S(2)}, u32[]{:S(2)}) collective-permute-start(bf16[2,256,512]{2,1,0:T(8,128)(2,1)} %get-tuple-element.11.refs_3_), channel_id=1, source_target_pairs={{0,8},{8,0},{1,9},{9,1},{2,10},{10,2},{3,11},{11,3},{4,12},{12,4},... | collective-permute-start | bytes 1572872 | tf_op jit(solution)/shard_map/ppermute | solution.py:523
  144.9 16.0 %collective-permute-start.21 = (bf16[4,64,1536]{2,1,0:T(8,128)(2,1)}, bf16[4,64,1536]{2,1,0:T(8,128)(2,1)S(1)}, u32[]{:S(2)}, u32[]{:S(2)}) collective-permute-start(bf16[4,64,1536]{2,1,0:T(8,128)(2,1)} %get-tuple-element.10.own_ref), channel_id=1, source_target_pairs={{0,8},{8,0},{1,9},{9,1},{2,10},{10,2},{3,11},{11,3},{4,12},{12,4},... | collective-permute-start | bytes 2359304 | tf_op jit(solution)/shard_map/ppermute | solution.py:523
  147.8 13.2 %copy-start.2 = (s32[4]{0:T(128)S(1)}, s32[4]{0:T(128)}, u32[]{:S(2)}) copy-start(s32[4]{0:T(128)} %pad_add_fusion.refs_0_.ids_ref) | copy-start | bytes 52
  147.8 13.2 %copy-start.3 = (s32[4]{0:T(128)S(1)}, s32[4]{0:T(128)}, u32[]{:S(2)}) copy-start(s32[4]{0:T(128)} %ancestors_ref.1) | copy-start | bytes 52
  155.1 12.6 %all-to-all-start.4 = ((f32[16,8,128]{2,1,0:T(8,128)}), f32[16,8,128]{2,1,0:T(8,128)S(1)}, u32[]{:S(2)}, u32[]{:S(2)}) async-start(f32[16,8,128]{2,1,0:T(8,128)} %reward.1), calls=%async_computation.4 | async-start | bytes 131072 | tf_op jit(solution)/shard_map/all_to_all | solution.py:657
  (20 other events, 66.7 us)

commit v13 on v12

--- a/solution.py
+++ b/solution.py
@@ -87,10 +87,8 @@
             highest = jnp.max(scores, axis=1, keepdims=True)
             expanded = jnp.exp2((scores - highest) * factor)
             norm = 1.0 / jnp.sum(expanded, axis=1, keepdims=True)
-            weighted = jnp.dot(
-                expanded.astype(jnp.bfloat16), v_all[:, cols], preferred_element_type=jnp.float32
-            )
-            pieces.append(weighted * norm)
+            weights = (expanded * norm).astype(jnp.bfloat16)
+            pieces.append(jnp.dot(weights, v_all[:, cols], preferred_element_type=jnp.float32))
         joined = jnp.concatenate(pieces, axis=1).astype(jnp.bfloat16)
         out_ref[span] = joined.reshape(block_sources, tokens, columns)
 
@@ -202,69 +200,88 @@
     )(latents, out_weight, piece)
 
 
-def project_kernel(chunks, width, pieces, parts, offsets, depth_parts, refs_in, refs_out):
-    ids_ref, latents_hbm, gain_ref, out_weight_ref = refs_in[:4]
-    rest, weight_refs = list(refs_in[4 : 4 + pieces]), refs_in[4 + pieces : 4 + pieces + parts]
-    begun_hbm = rest.pop(0) if chunks > 1 else None
-    stepped_ref, features_ref = refs_out[:2]
+def project_kernel(chunks, width, parts, offsets, depth_parts, refs_in, refs_out):
+    ids_ref, latents_hbm, gain_ref, out_weight_ref, piece_ref = refs_in[:5]
+    weight_refs = refs_in[5 : 5 + parts]
+    begun_hbm = refs_in[5 + parts] if chunks > 1 else None
+    stepped_hbm, features_ref = refs_out[:2]
     out_vmem, weight_vmem, rows_ref, clean_ref, embedded_ref = refs_out[2:7]
-    latents_ref, begun_ref, out_sems, sems, first_sems = refs_out[7:]
+    latents_ref, begun_ref, stepped_ref, piece_vmem = refs_out[7:11]
+    out_sems, sems, first_sems, rows_sem = refs_out[11:]
     dom, group, seq = ids_ref[0], ids_ref[1], ids_ref[2]
     sigma = ids_ref[3].astype(jnp.float32) * (1.0 / STEPS)
     particles, tokens, model_width = latents_ref.shape
     rows = particles * tokens
     shards, depth, columns = weight_refs[0].shape
 
-    wanted = list(range(chunks - len(rest), chunks))
-    block = column_block(model_width)
-    first_copies = []
-    for index in range(model_width // block):
-        cols = slice(index * block, (index + 1) * block)
-        first_copies.append(
-            pltpu.make_async_copy(
-                latents_hbm.at[:, :, cols], latents_ref.at[:, :, cols], first_sems.at[0, index]
+    count, _, part = piece_ref.shape
+    blocks = count // particles
+    row_copies, slots = [], []
+    for piece in range(count):
+        particle, place = divmod(piece, blocks)
+        slots.append(
+            (
+                slice(particle * tokens, (particle + 1) * tokens),
+                slice(place * part, (place + 1) * part),
             )
         )
+        to = rows_ref.at[slots[-1]] if part % LANES == 0 else piece_vmem.at[piece]
+        row_copies.append(pltpu.make_async_copy(piece_ref.at[piece], to, rows_sem.at[piece]))
+    block = column_block(model_width)
+    groups = [slice(i * block, (i + 1) * block) for i in range(model_width // block)]
+    group_copies = []
+    for index, cols in enumerate(groups):
+        begins = [(latents_hbm.at[:, :, cols], latents_ref.at[:, :, cols], 0)]
         if chunks > 1:
-            first_copies.append(
+            begins.append((begun_hbm.at[:, cols], begun_ref.at[:, cols], 1))
+        own = [pltpu.make_async_copy(a, b, first_sems.at[i, index]) for a, b, i in begins]
+        for place in range(blocks):
+            start = place * width + (chunks - 1) * part
+            own.append(
                 pltpu.make_async_copy(
-                    begun_hbm.at[:, cols], begun_ref.at[:, cols], first_sems.at[1, index]
+                    out_weight_ref.at[start : start + part, cols],
+                    out_vmem.at[place * part : (place + 1) * part, cols],
+                    out_sems.at[index, place],
                 )
             )
-    for copy in first_copies[: len(first_copies) // (model_width // block)]:
-        copy.start()
-    out_weights = ProjectionWeights(out_weight_ref, out_vmem, out_sems, chunks, wanted, width)
-    for copy in first_copies[len(first_copies) // (model_width // block) :]:
-        copy.start()
+        group_copies.append(own)
     copies = []
     for index in range(parts):
         for shard in range(shards):
             start = pl.multiple_of((seq ^ offsets[shard]) * depth, depth)
-            copy = pltpu.make_async_copy(
-                weight_refs[index].at[shard],
-                weight_vmem.at[index, pl.ds(start, depth)],
-                sems.at[index],
+            copies.append(
+                pltpu.make_async_copy(
+                    weight_refs[index].at[shard],
+                    weight_vmem.at[index, pl.ds(start, depth)],
+                    sems.at[index],
+                )
             )
-            copy.start()
-            copies.append(copy)
-
-    gather_rows(rest, rows_ref, particles)
-    for index in range(model_width // out_weights.block):
-        cols = out_weights.wait(index)
-        each = len(first_copies) // (model_width // block)
-        for copy in first_copies[index * each : (index + 1) * each]:
+    for copy in row_copies + [copy for own in group_copies for copy in own] + copies:
+        copy.start()
+    stepped_copies = [
+        pltpu.make_async_copy(
+            stepped_ref.at[:, :, cols], stepped_hbm.at[:, :, cols], first_sems.at[2, index]
+        )
+        for index, cols in enumerate(groups)
+    ]
+    for copy in row_copies:
+        copy.wait()
+    if part % LANES:
+        for piece, slot in enumerate(slots):
+            rows_ref[slot] = piece_vmem[piece]
+    for index, cols in enumerate(groups):
+        for copy in group_copies[index]:
             copy.wait()
-        flat = latents_ref[:, :, cols].reshape(rows, out_weights.block).astype(jnp.float32)
+        flat = latents_ref[:, :, cols].reshape(rows, block).astype(jnp.float32)
         begun = begun_ref[:, cols] if chunks > 1 else flat
         velocity = begun + jnp.dot(
             rows_ref[...], out_vmem[:, cols], preferred_element_type=jnp.float32
         )
         clean_ref[:, cols] = (flat - sigma * velocity).astype(jnp.bfloat16)
         stepped_ref[:, :, cols] = (
-            (flat - velocity * (1.0 / STEPS))
-            .astype(jnp.bfloat16)
-            .reshape(particles, tokens, out_weights.block)
+            (flat - velocity * (1.0 / STEPS)).astype(jnp.bfloat16).reshape(particles, tokens, block)
         )
+        stepped_copies[index].start()
 
     for index in range(parts):
         for copy in copies[index * shards : (index + 1) * shards]:
@@ -289,6 +306,8 @@
         feature = jax.nn.gelu(piece * inverse * gain_ref[:, cols]).astype(jnp.bfloat16)
         start = index * columns % share
         features_ref[index * columns // share, :, start : start + columns] = feature
+    for copy in stepped_copies:
+        copy.wait()
 
 
 def project_embed(
@@ -296,7 +315,7 @@
     offsets,
     latents,
     begun,
-    attended,
+    piece,
     chunks,
     width,
     out_weight,
@@ -310,34 +329,23 @@
     parts = len(weights)
     columns = weights[0].shape[2]
     count = parts * columns
-    out_depth = model_width * len(attended) // chunks
-    pieces = ([] if begun is None else [begun]) + attended
+    blocks = model_width // width
+    out_depth = blocks * piece.shape[2]
+    groups = model_width // column_block(model_width)
     vmem = pl.BlockSpec(memory_space=pltpu.VMEM)
-    smem = pl.BlockSpec(memory_space=pltpu.SMEM)
     hbm = pl.BlockSpec(memory_space=pltpu.HBM)
-    inputs = 4 + len(pieces) + parts + len(after)
-    groups = model_width // column_block(model_width)
+    begun = [] if begun is None else [begun]
+    inputs = 5 + parts + len(begun) + len(after)
 
     def kernel(*refs):
-        project_kernel(
-            chunks,
-            width,
-            len(pieces),
-            parts,
-            offsets,
-            depth_parts,
-            refs[:inputs],
-            refs[inputs:],
-        )
+        project_kernel(chunks, width, parts, offsets, depth_parts, refs[:inputs], refs[inputs:])
 
     return pl.pallas_call(
         kernel,
-        in_specs=[smem, hbm, vmem, hbm]
-        + ([] if begun is None else [hbm])
-        + [vmem] * len(attended)
-        + [hbm] * parts
+        in_specs=[pl.BlockSpec(memory_space=pltpu.SMEM), hbm, vmem, hbm, hbm]
+        + [hbm] * (parts + len(begun))
         + [pl.BlockSpec(memory_space=pl.ANY)] * len(after),
-        out_specs=[vmem, vmem],
+        out_specs=[hbm, vmem],
         out_shape=[
             jax.ShapeDtypeStruct(latents.shape, jnp.bfloat16),
             jax.ShapeDtypeStruct((depth_parts, rows, count // depth_parts), jnp.bfloat16),
@@ -350,9 +358,12 @@
             pltpu.VMEM((parts, rows, columns), jnp.float32),
             pltpu.VMEM(latents.shape, latents.dtype),
             pltpu.VMEM((rows, model_width), jnp.float32),
-            pltpu.SemaphoreType.DMA((groups, model_width // width * len(attended))),
+            pltpu.VMEM(latents.shape, latents.dtype),
+            pltpu.VMEM(piece.shape, piece.dtype),
+            pltpu.SemaphoreType.DMA((groups, blocks)),
             pltpu.SemaphoreType.DMA((parts,)),
-            pltpu.SemaphoreType.DMA((2, groups)),
+            pltpu.SemaphoreType.DMA((3, groups)),
+            pltpu.SemaphoreType.DMA((piece.shape[0],)),
         ],
         compiler_params=pltpu.CompilerParams(vmem_limit_bytes=60 * MIB),
         cost_estimate=pl.CostEstimate(
@@ -361,13 +372,22 @@
             transcendentals=rows * count,
         ),
         name="project_embed",
-    )(ids, latents, gain.reshape(1, count), out_weight, *pieces, *weights, *after)
+    )(
+        ids,
+        latents,
+        gain.reshape(1, count),
+        out_weight,
+        piece,
+        *weights,
+        *begun,
+        *after,
+    )
 
 
 def reward_kernel(particles, scale, parts, doms, offsets, joined, *refs):
     ids_ref, prev_ref, head_ref = refs[:3]
-    features_refs, weight_refs = refs[3 : 3 + doms], refs[3 + doms : -4]
-    out_ref, weight_vmem, rows_ref, sems = refs[-4:]
+    features_refs, weight_refs = refs[3 : 3 + doms], refs[3 + doms : -5]
+    out_ref, weight_vmem, rows_ref, sems, row_sems = refs[-5:]
     dom, group, seq = ids_ref[0], ids_ref[1], ids_ref[2]
     _, depth, columns = weight_refs[0].shape
     rows = features_refs[0].shape[1]
@@ -378,6 +398,18 @@
     ]
     count = len(places)
 
+    row_copies = []
+    for step, features_ref in enumerate(features_refs):
+        for index in range(parts):
+            copy = pltpu.make_async_copy(
+                features_ref.at[(group + parts - index) % parts],
+                rows_ref.at[
+                    step * rows : (step + 1) * rows, index * depth : (index + 1) * depth
+                ],
+                row_sems.at[step, index],
+            )
+            copy.start()
+            row_copies.append(copy)
     copies = []
     for place, (pair, shard) in enumerate(places):
         lane = place % joined * columns
@@ -393,11 +425,8 @@
             )
             copy.start()
             copies.append(copy)
-    for step, features_ref in enumerate(features_refs):
-        for index in range(parts):
-            rows_ref[step * rows : (step + 1) * rows, index * depth : (index + 1) * depth] = (
-                features_ref[(group + parts - index) % parts]
-            )
+    for copy in row_copies:
+        copy.wait()
     totals = jnp.zeros((doms * particles, joined * columns), jnp.float32)
     for step in range(count // joined):
         for copy in copies[step * joined * parts : (step + 1) * joined * parts]:
@@ -438,14 +467,14 @@
     return pl.pallas_call(
         functools.partial(reward_kernel, particles, scale, parts, doms, offsets, joined),
         in_specs=[smem, smem, vmem]
-        + [vmem] * doms
-        + [pl.BlockSpec(memory_space=pltpu.HBM)] * len(weights),
+        + [pl.BlockSpec(memory_space=pltpu.HBM)] * (doms + len(weights)),
         out_specs=vmem,
         out_shape=jax.ShapeDtypeStruct((copies, 8, LANES), jnp.float32),
         scratch_shapes=[
             pltpu.VMEM((count // joined, parts * depth, joined * columns), jnp.bfloat16),
             pltpu.VMEM((doms * rows, parts * depth), jnp.bfloat16),
             pltpu.SemaphoreType.DMA((count, parts)),
+            pltpu.SemaphoreType.DMA((doms, parts)),
         ],
         compiler_params=pltpu.CompilerParams(vmem_limit_bytes=60 * MIB),
         cost_estimate=pl.CostEstimate(
@@ -595,24 +624,25 @@
     up_both = swapped(up_high, "seq", low)
     high_pair, high_groups = swapped(up_high, "seq", 1), over_groups(up_high)
     low_pair, low_groups = swapped(up_low, "seq", 1), over_groups(up_low)
+    own_pairs = [own_pair] + [swapped(piece, "seq", 1) for piece in own_groups[1:]]
     embed_near = over_groups(embed_share)
     attended = [attention(arrived[0], head_width)]
     after = [up_both, high_pair, low_pair, *high_groups[1:], *low_groups[1:], *embed_near[1:]]
-    attended[0] = gate(attended[0], [*after, *arrived[1:]])
+    attended[0] = gate(attended[0], [*after, *own_pairs[1:], *arrived[1:]])
 
     returned = [exchange(attended[0])]
     both_pair, both_groups = swapped(up_both, "seq", 1), over_groups(up_both)
     high_pairs = over_groups(high_pair)
+    low_pairs = [low_pair] + [swapped(piece, "seq", 1) for piece in low_groups[1:]]
     attended += [attention(piece, head_width) for piece in arrived[1:]]
-    after = [returned[0], both_pair, *both_groups[1:], *high_pairs[1:]]
+    after = [returned[0], both_pair, *both_groups[1:], *high_pairs[1:], *low_pairs[1:]]
     attended[1:] = [gate(piece, after) for piece in attended[1:]]
 
     returned += [exchange(piece) for piece in attended[1:]]
     embed_parts = embed_near + [
         shifted(piece, "dom", k) for k in range(1, dom_count) for piece in embed_near
     ]
-    own_pairs, both_pairs = over_groups(own_pair), over_groups(both_pair)
-    low_pairs = [low_pair] + [swapped(piece, "seq", 1) for piece in low_groups[1:]]
+    both_pairs = over_groups(both_pair)
     up_parts = own_groups + own_pairs + high_groups + high_pairs
     up_parts += low_groups + low_pairs + both_groups + both_pairs
     up_offsets = [
@@ -628,14 +658,14 @@
         embed_offsets,
         latents,
         begun,
-        returned,
+        returned[0],
         chunks,
         width,
         out_weight,
         embed_parts,
         norm_gain,
         group_count,
-        [*own_pairs[1:], *low_pairs[1:], *both_pairs[1:]],
+        both_pairs[1:],
     )
     stepped_other = shifted(stepped, "dom", 1)
     features_other = shifted(features, "dom", 1)

time: 170 us -> 180 us (1.059)
  waiting for transfers between devices: 58.5 us -> 70.9 us
  starting transfers between devices: 57.8 us -> 53.5 us
  Pallas kernels: 39.4 us -> 42.1 us
    ppermute x11 -> x12, waiting for transfers between devices: 51 us -> 59.8 us  [swapped(): lax.ppermute(array, axis, [(i, i ^ bit) for i in range(lax.axis_size(axis...]
    all_to_all x4, waiting for transfers between devices: 0.01 us -> 3.83 us  [exchange(): return lax.all_to_all(array, 'seq', 0, 0, tiled=True)]
    all_to_all x1, starting transfers between devices: 5.83 us -> 3.75 us  [on_device(): logits = lax.all_to_all(partial, ('dom', 'seq'), 0, 0, tiled=True)]
    ppermute x11 -> x12, starting transfers between devices: 21.3 us -> 19.8 us  [swapped(): lax.ppermute(array, axis, [(i, i ^ bit) for i in range(lax.axis_size(axis...]
    ppermute x12 -> x11, starting transfers between devices: 10.2 us -> 9.23 us  [shifted(): lax.ppermute(array, axis, [(i, (i + step) % count) for i in range(count)])]
    unnamed x48 -> x52, local copies, waits for them, and re-layouts: 7.61 us -> 7.24 us
  transfers between devices with their start and end apart: 28 -> 28, of which waited for: 11 -> 13; matrix products, arithmetic and copies ran while one was open for 2% -> 1% of each run, Pallas kernels for 17% -> 18%
where the time goes in v13:
time: 180 us
  waiting for transfers between devices  70.9 us (39%)
  starting transfers between devices  53.5 us (30%)
  Pallas kernels  42.1 us (23%)
  local copies, waits for them, and re-layouts  8.25 us (5%)
  other arithmetic  3.36 us (2%)
    ppermute x12, waiting for transfers between devices, swapped(): lax.ppermute(array, axis, [(i, i ^ bit) for i in range(lax.axis_size(axis...  59.8 us
    all_to_all x4, starting transfers between devices, exchange(): return lax.all_to_all(array, 'seq', 0, 0, tiled=True)  20.7 us
    ppermute x12, starting transfers between devices, swapped(): lax.ppermute(array, axis, [(i, i ^ bit) for i in range(lax.axis_size(axis...  19.8 us
    pallas_call x2, Pallas kernels, attention(): pl.pallas_call(functools.partial(attention_kernel, head_width, block_sour...  13.8 us
    ppermute x11, starting transfers between devices, shifted(): lax.ppermute(array, axis, [(i, (i + step) % count) for i in range(count)])  9.23 us
    pallas_call x1, Pallas kernels, project_embed(): pl.pallas_call(kernel, in_specs=[pl.BlockSpec(memory_space=pltpu.SMEM), h...  9 us
    pallas_call x1, Pallas kernels, reward(): pl.pallas_call(functools.partial(reward_kernel, particles, scale, parts,...  8.02 us
    unnamed x52, local copies, waits for them, and re-layouts  7.24 us
  transfers between devices with their start and end apart: 28, of which 13 were waited for; matrix products, arithmetic and copies ran while one was open for 1% of the time, Pallas kernels for 18%

profile of v13, /device:TPU:0, one launch (start us, length us, event | category | flops | bytes accessed | tf_op | source)
XLA Modules:
  0.0 179.5 jit_solution(8738539004495039269)
XLA Ops:
  1.6 4.0 %collective-permute-start = (bf16[1,192,256]{2,1,0:T(8,128)(2,1)S(1)}, bf16[1,192,256]{2,1,0:T(8,128)(2,1)S(1)}, u32[]{:S(2)}, u32[]{:S(2)}) collective-permute-start(bf16[1,192,256]{2,1,0:T(8,128)(2,1)S(1)} %dynamic-slice_bitcast_fusion.1), channel_id=1, source_target_pairs={{0,4},{1,5},{2,6},{3,7},{4,0},{5,1},{6,2},{7,3},{8,12},{9,13},{10,... | collective-permute-start | bytes 294920 | tf_op jit(solution)/shard_map/ppermute | solution.py:556
  5.7 3.2 %pack_heads.1 = (bf16[8,3,64,384]{3,2,1,0:T(8,128)(2,1)}, bf16[8,3,64,384]{3,2,1,0:T(8,128)(2,1)}) custom-call(bf16[4,64,1536]{2,1,0:T(8,128)(2,1)} %q_ref.1, bf16[4,64,1536]{2,1,0:T(8,128)(2,1)} %k_ref.1, bf16[4,64,1536]{2,1,0:T(8,128)(2,1)} %v_ref.1), custom_call_target="tpu_custom_call" | custom-call | tf_op jit(solution)/shard_map/pack_heads/pallas_call | solution.py:40
  8.9 1.7 collective-permute-done
  11.3 5.9 %all-to-all-start = ((bf16[8,3,64,384]{3,2,1,0:T(8,128)(2,1)}), bf16[8,3,64,384]{3,2,1,0:T(8,128)(2,1)S(1)}, u32[]{:S(2)}, u32[]{:S(2)}) async-start(bf16[8,3,64,384]{3,2,1,0:T(8,128)(2,1)} %gate.4), calls=%async_computation | async-start | bytes 2359296 | tf_op jit(solution)/shard_map/all_to_all | solution.py:560
  17.2 2.0 %collective-permute-start.1 = (bf16[2,192,256]{2,1,0:T(8,128)(2,1)S(1)}, bf16[2,192,256]{2,1,0:T(8,128)(2,1)S(1)}, u32[]{:S(2)}, u32[]{:S(2)}) collective-permute-start(bf16[2,192,256]{2,1,0:T(8,128)(2,1)S(1)} %copy-done.10), channel_id=1, source_target_pairs={{0,2},{1,3},{2,0},{3,1},{4,6},{5,7},{6,4},{7,5},{8,10},{9,11},{10,... | collective-permute-start | bytes 589832 | tf_op jit(solution)/shard_map/ppermute | solution.py:556
  19.2 22.1 %collective-permute-done.1 = bf16[2,192,256]{2,1,0:T(8,128)(2,1)S(1)} collective-permute-done((bf16[2,192,256]{2,1,0:T(8,128)(2,1)S(1)}, bf16[2,192,256]{2,1,0:T(8,128)(2,1)S(1)}, u32[]{:S(2)}, u32[]{:S(2)}) %collective-permute-start.1) | collective-permute-done | bytes 196640 | tf_op jit(solution)/shard_map/ppermute | solution.py:556
  42.6 4.4 %collective-permute-start.3 = (bf16[1,512,256]{2,1,0:T(8,128)(2,1)S(1)}, bf16[1,512,256]{2,1,0:T(8,128)(2,1)}, u32[]{:S(2)}, u32[]{:S(2)}) collective-permute-start(bf16[1,512,256]{2,1,0:T(8,128)(2,1)S(1)} %dynamic-slice_bitcast_fusion.refs_5_), channel_id=1, source_target_pairs={{0,4},{1,5},{2,6},{3,7},{4,0},{5,1},{6,2},{7,3},{8,12},{9,13},{10,... | collective-permute-start | bytes 786440 | tf_op jit(solution)/shard_map/ppermute | solution.py:556
  49.1 4.5 %collective-permute-done.2 = bf16[4,192,256]{2,1,0:T(8,128)(2,1)} collective-permute-done((bf16[4,192,256]{2,1,0:T(8,128)(2,1)S(1)}, bf16[4,192,256]{2,1,0:T(8,128)(2,1)}, u32[]{:S(2)}, u32[]{:S(2)}) %collective-permute-start.2) | collective-permute-done | bytes 393248 | tf_op jit(solution)/shard_map/ppermute | solution.py:556
  53.6 2.0 %pad_maximum_fusion.refs_2_.refs_5_ = bf16[8,192,256]{2,1,0:T(8,128)(2,1)} fusion(bf16[4,192,256]{2,1,0:T(8,128)(2,1)} %collective-permute-done.2, bf16[2,192,256]{2,1,0:T(8,128)(2,1)S(1)} %collective-permute-done.1, bf16[1,192,256]{2,1,0:T(8,128)(2,1)S(1)} %collective-permute-done, bf16[1,192,256]{2,1,0:T(8,128)(2,1)S(1)} %dynamic-slice_bitcast_fusion.1), kind=kLoop, calls=%fused_computation | loop fusion | flops 1179648 | bytes 1572864 | tf_op jit(solution)/shard_map/concatenate | solution.py:619
  55.6 2.4 %collective-permute-done.3.refs_3_.refs_9_ = bf16[1,512,256]{2,1,0:T(8,128)(2,1)} collective-permute-done((bf16[1,512,256]{2,1,0:T(8,128)(2,1)S(1)}, bf16[1,512,256]{2,1,0:T(8,128)(2,1)}, u32[]{:S(2)}, u32[]{:S(2)}) %collective-permute-start.3) | collective-permute-done | bytes 262176 | tf_op jit(solution)/shard_map/ppermute | solution.py:556
  60.7 3.8 %all-to-all-start.1 = ((bf16[8,3,64,384]{3,2,1,0:T(8,128)(2,1)}), bf16[8,3,64,384]{3,2,1,0:T(8,128)(2,1)S(1)}, u32[]{:S(2)}, u32[]{:S(2)}) async-start(bf16[8,3,64,384]{3,2,1,0:T(8,128)(2,1)} %gate.5), calls=%async_computation.1 | async-start | bytes 2359296 | tf_op jit(solution)/shard_map/all_to_all | solution.py:560
  64.4 1.6 collective-permute-start.12
  66.0 2.0 %collective-permute-start.7 = (bf16[1,512,256]{2,1,0:T(8,128)(2,1)}, bf16[1,512,256]{2,1,0:T(8,128)(2,1)S(1)}, u32[]{:S(2)}, u32[]{:S(2)}) collective-permute-start(bf16[1,512,256]{2,1,0:T(8,128)(2,1)} %collective-permute-done.3.refs_3_.refs_9_), channel_id=1, source_target_pairs={{0,2},{1,3},{2,0},{3,1},{4,6},{5,7},{6,4},{7,5},{8,10},{9,11},{10,... | collective-permute-start | bytes 786440 | tf_op jit(solution)/shard_map/ppermute | solution.py:556
  69.9 1.5 collective-permute-start.11
  71.4 17.0 %collective-permute-done.7.refs_1_.refs_17_ = bf16[1,512,256]{2,1,0:T(8,128)(2,1)S(1)} collective-permute-done((bf16[1,512,256]{2,1,0:T(8,128)(2,1)}, bf16[1,512,256]{2,1,0:T(8,128)(2,1)S(1)}, u32[]{:S(2)}, u32[]{:S(2)}) %collective-permute-start.7) | collective-permute-done | bytes 262176 | tf_op jit(solution)/shard_map/ppermute | solution.py:556
  88.4 1.8 collective-permute-start.9
  90.5 6.9 %attention.3.refs_0_ = bf16[8,64,384]{2,1,0:T(8,128)(2,1)} custom-call(bf16[8,3,64,384]{3,2,1,0:T(8,128)(2,1)} %copy-done.5), custom_call_target="tpu_custom_call" | custom-call | flops 402653184 | bytes 1572864 | tf_op jit(solution)/shard_map/attention/pallas_call | solution.py:104
  97.8 2.8 %collective-permute-done.13.refs_7_.refs_8_ = bf16[1,512,256]{2,1,0:T(8,128)(2,1)} collective-permute-done((bf16[1,512,256]{2,1,0:T(8,128)(2,1)}, bf16[1,512,256]{2,1,0:T(8,128)(2,1)}, u32[]{:S(2)}, u32[]{:S(2)}) %collective-permute-start.13) | collective-permute-done | bytes 262176 | tf_op jit(solution)/shard_map/ppermute | solution.py:556
  101.7 6.5 %all-to-all-start.2 = ((bf16[8,64,384]{2,1,0:T(8,128)(2,1)}), bf16[8,64,384]{2,1,0:T(8,128)(2,1)S(1)}, u32[]{:S(2)}, u32[]{:S(2)}) async-start(bf16[8,64,384]{2,1,0:T(8,128)(2,1)} %gate.6), calls=%async_computation.2 | async-start | bytes 786432 | tf_op jit(solution)/shard_map/all_to_all | solution.py:560
  108.2 2.0 %collective-permute-start.14 = (bf16[1,512,256]{2,1,0:T(8,128)(2,1)S(1)}, bf16[1,512,256]{2,1,0:T(8,128)(2,1)S(1)}, u32[]{:S(2)}, u32[]{:S(2)}) collective-permute-start(bf16[1,512,256]{2,1,0:T(8,128)(2,1)S(1)} %copy-done.12), channel_id=1, source_target_pairs={{0,1},{1,0},{2,3},{3,2},{4,5},{5,4},{6,7},{7,6},{8,9},{9,8},{10,11... | collective-permute-start | bytes 786440 | tf_op jit(solution)/shard_map/ppermute | solution.py:556
  112.4 7.9 %collective-permute-done.14.refs_2_.refs_19_ = bf16[1,512,256]{2,1,0:T(8,128)(2,1)S(1)} collective-permute-done((bf16[1,512,256]{2,1,0:T(8,128)(2,1)S(1)}, bf16[1,512,256]{2,1,0:T(8,128)(2,1)S(1)}, u32[]{:S(2)}, u32[]{:S(2)}) %collective-permute-start.14) | collective-permute-done | bytes 262176 | tf_op jit(solution)/shard_map/ppermute | solution.py:556
  121.0 6.9 %attention.2.refs_0_ = bf16[8,64,384]{2,1,0:T(8,128)(2,1)} custom-call(bf16[8,3,64,384]{3,2,1,0:T(8,128)(2,1)} %copy-done.6), custom_call_target="tpu_custom_call" | custom-call | flops 402653184 | bytes 1572864 | tf_op jit(solution)/shard_map/attention/pallas_call | solution.py:104
  130.1 4.5 %all-to-all-start.3 = ((bf16[8,64,384]{2,1,0:T(8,128)(2,1)}), bf16[8,64,384]{2,1,0:T(8,128)(2,1)S(1)}, u32[]{:S(2)}, u32[]{:S(2)}) async-start(bf16[8,64,384]{2,1,0:T(8,128)(2,1)} %gate.7), calls=%async_computation.3 | async-start | bytes 786432 | tf_op jit(solution)/shard_map/all_to_all | solution.py:560
  134.6 1.6 collective-permute-start.20
  137.5 4.7 %first_project.1.refs_9_ = f32[256,1536]{1,0:T(8,128)} custom-call(bf16[4,64,1536]{2,1,0:T(8,128)(2,1)} %refs_1_.2, bf16[1536,1536]{1,0:T(8,128)(2,1)} %refs_3_.1, bf16[8,64,384]{2,1,0:T(8,128)(2,1)} %copy-done.7), custom_call_target="tpu_custom_call" | custom-call | flops 603979776 | bytes 5505024 | tf_op jit(solution)/shard_map/first_project/pallas_call | solution.py:181
  143.1 3.8 %all-to-all-done.3.refs_4_ = bf16[8,64,384]{2,1,0:T(8,128)(2,1)S(1)} async-done(((bf16[8,64,384]{2,1,0:T(8,128)(2,1)}), bf16[8,64,384]{2,1,0:T(8,128)(2,1)S(1)}, u32[]{:S(2)}, u32[]{:S(2)}) %all-to-all-start.3) | async-done | bytes 393248 | tf_op jit(solution)/shard_map/all_to_all | solution.py:560
  147.7 9.0 %project_embed.1 = (bf16[4,64,1536]{2,1,0:T(8,128)(2,1)}, bf16[2,256,512]{2,1,0:T(8,128)(2,1)}) custom-call(s32[4]{0:T(128)} %pad_add_fusion.refs_0_.ids_ref, bf16[4,64,1536]{2,1,0:T(8,128)(2,1)} %refs_1_.2, f32[1,1024]{1,0:T(1,128)} %bitcast.10, bf16[1536,1536]{1,0:T(8,128)(2,1)} %refs_3_.1, bf16[8,64,384]{2,1,0:T(8,128)(2,1)} %copy-done.8, ...), custom_call_target="tpu_custom_call" | custom-call | flops 1409286144 | bytes 10223616 | tf_op jit(solution)/shard_map/project_embed/pallas_call | solution.py:343
  157.3 1.6 collective-permute-done.22.refs_4_
  159.7 8.0 %reward.1 = f32[16,8,128]{2,1,0:T(8,128)} custom-call(s32[4]{0:T(128)} %pad_add_fusion.refs_0_.ids_ref, f32[4]{0:T(128)} %refs_1_.3, f32[16,1,256]{2,1,0:T(1,128)} %bitcast.11, bf16[2,256,512]{2,1,0:T(8,128)(2,1)} %get-tuple-element.11.refs_3_, bf16[2,256,512]{2,1,0:T(8,128)(2,1)} %copy-done.25, bf16[1,512,256]{2,1,0:T(8,128)(2,1)} %copy-done.22, ...), custom_call_target="tpu_custom_call" | custom-call | flops 2147483648 | bytes 4194304 | tf_op jit(solution)/shard_map/reward/pallas_call | solution.py:467
  167.7 3.8 %all-to-all-start.4 = ((f32[16,8,128]{2,1,0:T(8,128)}), f32[16,8,128]{2,1,0:T(8,128)S(1)}, u32[]{:S(2)}, u32[]{:S(2)}) async-start(f32[16,8,128]{2,1,0:T(8,128)} %reward.1), calls=%async_computation.4 | async-start | bytes 131072 | tf_op jit(solution)/shard_map/all_to_all | solution.py:687
  171.5 2.0 %resample.1.resampled_ref = bf16[4,64,1536]{2,1,0:T(8,128)(2,1)} custom-call(s32[4]{0:T(128)S(1)} %copy-done.2, s32[4]{0:T(128)S(1)} %copy-done.3, bf16[4,64,1536]{2,1,0:T(8,128)(2,1)S(1)} %copy-done.1, bf16[4,64,1536]{2,1,0:T(8,128)(2,1)S(1)} %collective-permute-done.21.other_ref), custom_call_target="tpu_custom_call" | custom-call | tf_op jit(solution)/shard_map/resample/pallas_call | solution.py:536
  173.6 4.7 %all-to-all-done.4.parts_ref = f32[16,8,128]{2,1,0:T(8,128)S(1)} async-done(((f32[16,8,128]{2,1,0:T(8,128)}), f32[16,8,128]{2,1,0:T(8,128)S(1)}, u32[]{:S(2)}, u32[]{:S(2)}) %all-to-all-start.4) | async-done | bytes 65568 | tf_op jit(solution)/shard_map/all_to_all | solution.py:687
  (94 shorter events, 21.5 us)
Async XLA Ops:
  0.6 42.0 %copy-start = (bf16[1024,512]{1,0:T(8,128)(2,1)S(1)}, bf16[1024,512]{1,0:T(8,128)(2,1)}, u32[]{:S(2)}) copy-start(bf16[1024,512]{1,0:T(8,128)(2,1)} %param.20) | copy-start | bytes 3145732
  1.6 8.9 %collective-permute-start = (bf16[1,192,256]{2,1,0:T(8,128)(2,1)S(1)}, bf16[1,192,256]{2,1,0:T(8,128)(2,1)S(1)}, u32[]{:S(2)}, u32[]{:S(2)}) collective-permute-start(bf16[1,192,256]{2,1,0:T(8,128)(2,1)S(1)} %dynamic-slice_bitcast_fusion.1), channel_id=1, source_target_pairs={{0,4},{1,5},{2,6},{3,7},{4,0},{5,1},{6,2},{7,3},{8,12},{9,13},{10,... | collective-permute-start | bytes 294920 | tf_op jit(solution)/shard_map/ppermute | solution.py:556
  11.3 48.4 %all-to-all-start = ((bf16[8,3,64,384]{3,2,1,0:T(8,128)(2,1)}), bf16[8,3,64,384]{3,2,1,0:T(8,128)(2,1)S(1)}, u32[]{:S(2)}, u32[]{:S(2)}) async-start(bf16[8,3,64,384]{3,2,1,0:T(8,128)(2,1)} %gate.4), calls=%async_computation | async-start | bytes 2359296 | tf_op jit(solution)/shard_map/all_to_all | solution.py:560
  17.2 24.2 %collective-permute-start.1 = (bf16[2,192,256]{2,1,0:T(8,128)(2,1)S(1)}, bf16[2,192,256]{2,1,0:T(8,128)(2,1)S(1)}, u32[]{:S(2)}, u32[]{:S(2)}) collective-permute-start(bf16[2,192,256]{2,1,0:T(8,128)(2,1)S(1)} %copy-done.10), channel_id=1, source_target_pairs={{0,2},{1,3},{2,0},{3,1},{4,6},{5,7},{6,4},{7,5},{8,10},{9,11},{10,... | collective-permute-start | bytes 589832 | tf_op jit(solution)/shard_map/ppermute | solution.py:556
  41.4 12.2 %collective-permute-start.2 = (bf16[4,192,256]{2,1,0:T(8,128)(2,1)S(1)}, bf16[4,192,256]{2,1,0:T(8,128)(2,1)}, u32[]{:S(2)}, u32[]{:S(2)}) collective-permute-start(bf16[4,192,256]{2,1,0:T(8,128)(2,1)S(1)} %pad_maximum_fusion.1), channel_id=1, source_target_pairs={{0,1},{1,0},{2,3},{3,2},{4,5},{5,4},{6,7},{7,6},{8,9},{9,8},{10,11... | collective-permute-start | bytes 1179656 | tf_op jit(solution)/shard_map/ppermute | solution.py:556
  42.6 16.3 %copy-start.22 = (bf16[1,512,256]{2,1,0:T(8,128)(2,1)}, bf16[1,512,256]{2,1,0:T(8,128)(2,1)S(1)}, u32[]{:S(2)}) copy-start(bf16[1,512,256]{2,1,0:T(8,128)(2,1)S(1)} %dynamic-slice_bitcast_fusion.refs_5_) | copy-start | bytes 786436
  42.6 15.3 %collective-permute-start.3 = (bf16[1,512,256]{2,1,0:T(8,128)(2,1)S(1)}, bf16[1,512,256]{2,1,0:T(8,128)(2,1)}, u32[]{:S(2)}, u32[]{:S(2)}) collective-permute-start(bf16[1,512,256]{2,1,0:T(8,128)(2,1)S(1)} %dynamic-slice_bitcast_fusion.refs_5_), channel_id=1, source_target_pairs={{0,4},{1,5},{2,6},{3,7},{4,0},{5,1},{6,2},{7,3},{8,12},{9,13},{10,... | collective-permute-start | bytes 786440 | tf_op jit(solution)/shard_map/ppermute | solution.py:556
  47.0 11.9 %collective-permute-start.4 = (bf16[1,512,256]{2,1,0:T(8,128)(2,1)S(1)}, bf16[1,512,256]{2,1,0:T(8,128)(2,1)S(1)}, u32[]{:S(2)}, u32[]{:S(2)}) collective-permute-start(bf16[1,512,256]{2,1,0:T(8,128)(2,1)S(1)} %dynamic-slice_bitcast_fusion.refs_5_), channel_id=1, source_target_pairs={{0,2},{1,3},{2,0},{3,1},{4,6},{5,7},{6,4},{7,5},{8,10},{9,11},{10,... | collective-permute-start | bytes 786440 | tf_op jit(solution)/shard_map/ppermute | solution.py:556
  47.0 11.9 %collective-permute-start.6 = (bf16[1,512,256]{2,1,0:T(8,128)(2,1)S(1)}, bf16[1,512,256]{2,1,0:T(8,128)(2,1)S(1)}, u32[]{:S(2)}, u32[]{:S(2)}) collective-permute-start(bf16[1,512,256]{2,1,0:T(8,128)(2,1)S(1)} %dynamic-slice_bitcast_fusion.refs_5_), channel_id=1, source_target_pairs={{0,16},{16,0},{1,17},{17,1},{2,18},{18,2},{3,19},{19,3},{4,20},{20... | collective-permute-start | bytes 786440 | tf_op jit(solution)/shard_map/ppermute | solution.py:552
  48.5 11.1 %collective-permute-start.5 = (bf16[1,512,256]{2,1,0:T(8,128)(2,1)S(1)}, bf16[1,512,256]{2,1,0:T(8,128)(2,1)}, u32[]{:S(2)}, u32[]{:S(2)}) collective-permute-start(bf16[1,512,256]{2,1,0:T(8,128)(2,1)S(1)} %dynamic-slice_bitcast_fusion.refs_5_), channel_id=1, source_target_pairs={{0,1},{1,0},{2,3},{3,2},{4,5},{5,4},{6,7},{7,6},{8,9},{9,8},{10,11... | collective-permute-start | bytes 786440 | tf_op jit(solution)/shard_map/ppermute | solution.py:556
  60.7 40.0 %all-to-all-start.1 = ((bf16[8,3,64,384]{3,2,1,0:T(8,128)(2,1)}), bf16[8,3,64,384]{3,2,1,0:T(8,128)(2,1)S(1)}, u32[]{:S(2)}, u32[]{:S(2)}) async-start(bf16[8,3,64,384]{3,2,1,0:T(8,128)(2,1)} %gate.5), calls=%async_computation.1 | async-start | bytes 2359296 | tf_op jit(solution)/shard_map/all_to_all | solution.py:560
  64.4 36.2 %collective-permute-start.12 = (bf16[8,192,256]{2,1,0:T(8,128)(2,1)S(1)}, bf16[8,192,256]{2,1,0:T(8,128)(2,1)}, u32[]{:S(2)}, u32[]{:S(2)}) collective-permute-start(bf16[8,192,256]{2,1,0:T(8,128)(2,1)S(1)} %copy-done.4), channel_id=1, source_target_pairs={{0,16},{16,0},{1,17},{17,1},{2,18},{18,2},{3,19},{19,3},{4,20},{20... | collective-permute-start | bytes 2359304 | tf_op jit(solution)/shard_map/ppermute | solution.py:552
  66.0 22.4 %collective-permute-start.7 = (bf16[1,512,256]{2,1,0:T(8,128)(2,1)}, bf16[1,512,256]{2,1,0:T(8,128)(2,1)S(1)}, u32[]{:S(2)}, u32[]{:S(2)}) collective-permute-start(bf16[1,512,256]{2,1,0:T(8,128)(2,1)} %collective-permute-done.3.refs_3_.refs_9_), channel_id=1, source_target_pairs={{0,2},{1,3},{2,0},{3,1},{4,6},{5,7},{6,4},{7,5},{8,10},{9,11},{10,... | collective-permute-start | bytes 786440 | tf_op jit(solution)/shard_map/ppermute | solution.py:556
  67.9 22.3 %collective-permute-start.8 = (bf16[1,512,256]{2,1,0:T(8,128)(2,1)}, bf16[1,512,256]{2,1,0:T(8,128)(2,1)S(1)}, u32[]{:S(2)}, u32[]{:S(2)}) collective-permute-start(bf16[1,512,256]{2,1,0:T(8,128)(2,1)} %collective-permute-done.3.refs_3_.refs_9_), channel_id=1, source_target_pairs={{0,1},{1,0},{2,3},{3,2},{4,5},{5,4},{6,7},{7,6},{8,9},{9,8},{10,11... | collective-permute-start | bytes 786440 | tf_op jit(solution)/shard_map/ppermute | solution.py:556
  69.4 28.0 %collective-permute-start.10 = (bf16[1,512,256]{2,1,0:T(8,128)(2,1)}, bf16[1,512,256]{2,1,0:T(8,128)(2,1)S(1)}, u32[]{:S(2)}, u32[]{:S(2)}) collective-permute-start(bf16[1,512,256]{2,1,0:T(8,128)(2,1)} %collective-permute-done.3.refs_3_.refs_9_), channel_id=1, source_target_pairs={{0,16},{16,0},{1,17},{17,1},{2,18},{18,2},{3,19},{19,3},{4,20},{20... | collective-permute-start | bytes 786440 | tf_op jit(solution)/shard_map/ppermute | solution.py:552
  69.9 27.5 %collective-permute-start.11 = (bf16[1,512,256]{2,1,0:T(8,128)(2,1)}, bf16[1,512,256]{2,1,0:T(8,128)(2,1)S(1)}, u32[]{:S(2)}, u32[]{:S(2)}) collective-permute-start(bf16[1,512,256]{2,1,0:T(8,128)(2,1)} %copy-done.23), channel_id=1, source_target_pairs={{0,16},{16,0},{1,17},{17,1},{2,18},{18,2},{3,19},{19,3},{4,20},{20... | collective-permute-start | bytes 786440 | tf_op jit(solution)/shard_map/ppermute | solution.py:552
  88.4 9.4 %collective-permute-start.9 = (bf16[1,512,256]{2,1,0:T(8,128)(2,1)}, bf16[1,512,256]{2,1,0:T(8,128)(2,1)}, u32[]{:S(2)}, u32[]{:S(2)}) collective-permute-start(bf16[1,512,256]{2,1,0:T(8,128)(2,1)} %copy-done.23), channel_id=1, source_target_pairs={{0,1},{1,0},{2,3},{3,2},{4,5},{5,4},{6,7},{7,6},{8,9},{9,8},{10,11... | collective-permute-start | bytes 786440 | tf_op jit(solution)/shard_map/ppermute | solution.py:556
  90.2 10.4 %collective-permute-start.13 = (bf16[1,512,256]{2,1,0:T(8,128)(2,1)}, bf16[1,512,256]{2,1,0:T(8,128)(2,1)}, u32[]{:S(2)}, u32[]{:S(2)}) collective-permute-start(bf16[1,512,256]{2,1,0:T(8,128)(2,1)} %copy-done.24), channel_id=1, source_target_pairs={{0,1},{1,0},{2,3},{3,2},{4,5},{5,4},{6,7},{7,6},{8,9},{9,8},{10,11... | collective-permute-start | bytes 786440 | tf_op jit(solution)/shard_map/ppermute | solution.py:556
  97.4 14.4 %copy-start.14 = (bf16[1,512,256]{2,1,0:T(8,128)(2,1)S(1)}, bf16[1,512,256]{2,1,0:T(8,128)(2,1)}, u32[]{:S(2)}) copy-start(bf16[1,512,256]{2,1,0:T(8,128)(2,1)} %copy-done.13) | copy-start | bytes 786436
  101.7 27.5 %all-to-all-start.2 = ((bf16[8,64,384]{2,1,0:T(8,128)(2,1)}), bf16[8,64,384]{2,1,0:T(8,128)(2,1)S(1)}, u32[]{:S(2)}, u32[]{:S(2)}) async-start(bf16[8,64,384]{2,1,0:T(8,128)(2,1)} %gate.6), calls=%async_computation.2 | async-start | bytes 786432 | tf_op jit(solution)/shard_map/all_to_all | solution.py:560
  108.2 12.1 %collective-permute-start.14 = (bf16[1,512,256]{2,1,0:T(8,128)(2,1)S(1)}, bf16[1,512,256]{2,1,0:T(8,128)(2,1)S(1)}, u32[]{:S(2)}, u32[]{:S(2)}) collective-permute-start(bf16[1,512,256]{2,1,0:T(8,128)(2,1)S(1)} %copy-done.12), channel_id=1, source_target_pairs={{0,1},{1,0},{2,3},{3,2},{4,5},{5,4},{6,7},{7,6},{8,9},{9,8},{10,11... | collective-permute-start | bytes 786440 | tf_op jit(solution)/shard_map/ppermute | solution.py:556
  110.3 17.6 %collective-permute-start.15 = (bf16[1,512,256]{2,1,0:T(8,128)(2,1)S(1)}, bf16[1,512,256]{2,1,0:T(8,128)(2,1)S(1)}, u32[]{:S(2)}, u32[]{:S(2)}) collective-permute-start(bf16[1,512,256]{2,1,0:T(8,128)(2,1)S(1)} %copy-done.12), channel_id=1, source_target_pairs={{0,16},{16,0},{1,17},{17,1},{2,18},{18,2},{3,19},{19,3},{4,20},{20... | collective-permute-start | bytes 786440 | tf_op jit(solution)/shard_map/ppermute | solution.py:552
  111.8 16.1 %collective-permute-start.16 = (bf16[1,512,256]{2,1,0:T(8,128)(2,1)S(1)}, bf16[1,512,256]{2,1,0:T(8,128)(2,1)S(1)}, u32[]{:S(2)}, u32[]{:S(2)}) collective-permute-start(bf16[1,512,256]{2,1,0:T(8,128)(2,1)S(1)} %copy-done.14), channel_id=1, source_target_pairs={{0,16},{16,0},{1,17},{17,1},{2,18},{18,2},{3,19},{19,3},{4,20},{20... | collective-permute-start | bytes 786440 | tf_op jit(solution)/shard_map/ppermute | solution.py:552
  112.3 17.0 %collective-permute-start.17 = (bf16[1,512,256]{2,1,0:T(8,128)(2,1)}, bf16[1,512,256]{2,1,0:T(8,128)(2,1)}, u32[]{:S(2)}, u32[]{:S(2)}) collective-permute-start(bf16[1,512,256]{2,1,0:T(8,128)(2,1)} %copy-done.16), channel_id=1, source_target_pairs={{0,1},{1,0},{2,3},{3,2},{4,5},{5,4},{6,7},{7,6},{8,9},{9,8},{10,11... | collective-permute-start | bytes 786440 | tf_op jit(solution)/shard_map/ppermute | solution.py:556
  112.4 30.7 %collective-permute-start.18 = (bf16[8,192,256]{2,1,0:T(8,128)(2,1)S(1)}, bf16[8,192,256]{2,1,0:T(8,128)(2,1)S(1)}, u32[]{:S(2)}, u32[]{:S(2)}) collective-permute-start(bf16[8,192,256]{2,1,0:T(8,128)(2,1)S(1)} %copy-done.4), channel_id=1, source_target_pairs={{0,8},{8,0},{1,9},{9,1},{2,10},{10,2},{3,11},{11,3},{4,12},{12,4},... | collective-permute-start | bytes 2359304 | tf_op jit(solution)/shard_map/ppermute | solution.py:552
  121.0 22.1 %collective-permute-start.19 = (bf16[8,192,256]{2,1,0:T(8,128)(2,1)}, bf16[8,192,256]{2,1,0:T(8,128)(2,1)}, u32[]{:S(2)}, u32[]{:S(2)}) collective-permute-start(bf16[8,192,256]{2,1,0:T(8,128)(2,1)} %collective-permute-done.12.refs_6_), channel_id=1, source_target_pairs={{0,8},{8,0},{1,9},{9,1},{2,10},{10,2},{3,11},{11,3},{4,12},{12,4},... | collective-permute-start | bytes 2359304 | tf_op jit(solution)/shard_map/ppermute | solution.py:552
  130.1 16.9 %all-to-all-start.3 = ((bf16[8,64,384]{2,1,0:T(8,128)(2,1)}), bf16[8,64,384]{2,1,0:T(8,128)(2,1)S(1)}, u32[]{:S(2)}, u32[]{:S(2)}) async-start(bf16[8,64,384]{2,1,0:T(8,128)(2,1)} %gate.7), calls=%async_computation.3 | async-start | bytes 786432 | tf_op jit(solution)/shard_map/all_to_all | solution.py:560
  134.6 8.5 %collective-permute-start.20 = (bf16[1,512,256]{2,1,0:T(8,128)(2,1)S(1)}, bf16[1,512,256]{2,1,0:T(8,128)(2,1)S(1)}, u32[]{:S(2)}, u32[]{:S(2)}) collective-permute-start(bf16[1,512,256]{2,1,0:T(8,128)(2,1)S(1)} %copy-done.18), channel_id=1, source_target_pairs={{0,16},{16,0},{1,17},{17,1},{2,18},{18,2},{3,19},{19,3},{4,20},{20... | collective-permute-start | bytes 786440 | tf_op jit(solution)/shard_map/ppermute | solution.py:552
  156.7 2.2 %collective-permute-start.22 = (bf16[2,256,512]{2,1,0:T(8,128)(2,1)}, bf16[2,256,512]{2,1,0:T(8,128)(2,1)S(1)}, u32[]{:S(2)}, u32[]{:S(2)}) collective-permute-start(bf16[2,256,512]{2,1,0:T(8,128)(2,1)} %get-tuple-element.11.refs_3_), channel_id=1, source_target_pairs={{0,8},{8,0},{1,9},{9,1},{2,10},{10,2},{3,11},{11,3},{4,12},{12,4},... | collective-permute-start | bytes 1572872 | tf_op jit(solution)/shard_map/ppermute | solution.py:552
  156.8 14.7 %collective-permute-start.21 = (bf16[4,64,1536]{2,1,0:T(8,128)(2,1)}, bf16[4,64,1536]{2,1,0:T(8,128)(2,1)S(1)}, u32[]{:S(2)}, u32[]{:S(2)}) collective-permute-start(bf16[4,64,1536]{2,1,0:T(8,128)(2,1)} %get-tuple-element.10.own_ref), channel_id=1, source_target_pairs={{0,8},{8,0},{1,9},{9,1},{2,10},{10,2},{3,11},{11,3},{4,12},{12,4},... | collective-permute-start | bytes 2359304 | tf_op jit(solution)/shard_map/ppermute | solution.py:552
  159.7 11.8 %copy-start.3 = (s32[4]{0:T(128)S(1)}, s32[4]{0:T(128)}, u32[]{:S(2)}) copy-start(s32[4]{0:T(128)} %ancestors_ref.1) | copy-start | bytes 52
  167.7 10.5 %all-to-all-start.4 = ((f32[16,8,128]{2,1,0:T(8,128)}), f32[16,8,128]{2,1,0:T(8,128)S(1)}, u32[]{:S(2)}, u32[]{:S(2)}) async-start(f32[16,8,128]{2,1,0:T(8,128)} %reward.1), calls=%async_computation.4 | async-start | bytes 131072 | tf_op jit(solution)/shard_map/all_to_all | solution.py:687
  (22 other events, 89.1 us)

commit v14 on v12

--- a/solution.py
+++ b/solution.py
@@ -87,10 +87,8 @@
             highest = jnp.max(scores, axis=1, keepdims=True)
             expanded = jnp.exp2((scores - highest) * factor)
             norm = 1.0 / jnp.sum(expanded, axis=1, keepdims=True)
-            weighted = jnp.dot(
-                expanded.astype(jnp.bfloat16), v_all[:, cols], preferred_element_type=jnp.float32
-            )
-            pieces.append(weighted * norm)
+            weights = (expanded * norm).astype(jnp.bfloat16)
+            pieces.append(jnp.dot(weights, v_all[:, cols], preferred_element_type=jnp.float32))
         joined = jnp.concatenate(pieces, axis=1).astype(jnp.bfloat16)
         out_ref[span] = joined.reshape(block_sources, tokens, columns)
 
@@ -109,7 +107,7 @@
         in_specs=[pl.BlockSpec((sources, 3, tokens, step), lambda i: (0, 0, 0, i))],
         out_specs=pl.BlockSpec((sources, tokens, step), lambda i: (0, 0, i)),
         out_shape=jax.ShapeDtypeStruct((sources, tokens, columns), jnp.bfloat16),
-        compiler_params=pltpu.CompilerParams(vmem_limit_bytes=60 * MIB),
+        compiler_params=pltpu.CompilerParams(vmem_limit_bytes=8 * MIB + 6 * scores_bytes),
         cost_estimate=pl.CostEstimate(
             flops=4 * total * total * columns,
             bytes_accessed=8 * total * columns,
@@ -588,35 +586,38 @@
     own_pair, own_groups = swapped(up_share, "seq", 1), over_groups(up_share)
     for bit in (low, 1):
         embed_share = jnp.concatenate([embed_share, swapped(embed_share, "seq", bit)])
-    after = [arrived[0], embed_share, up_high, up_low, own_pair, *own_groups[1:]]
+    after = [embed_share, up_high, up_low, own_pair, *own_groups[1:]]
     packed[1:] = [gate(piece, after) for piece in packed[1:]]
 
     arrived += [exchange(piece) for piece in packed[1:]]
     up_both = swapped(up_high, "seq", low)
-    high_pair, high_groups = swapped(up_high, "seq", 1), over_groups(up_high)
-    low_pair, low_groups = swapped(up_low, "seq", 1), over_groups(up_low)
+    up_next = jnp.concatenate([up_high, up_low])
+    next_pair, next_groups = swapped(up_next, "seq", 1), over_groups(up_next)
     embed_near = over_groups(embed_share)
     attended = [attention(arrived[0], head_width)]
-    after = [up_both, high_pair, low_pair, *high_groups[1:], *low_groups[1:], *embed_near[1:]]
-    attended[0] = gate(attended[0], [*after, *arrived[1:]])
+    after = [up_both, next_pair, *next_groups[1:], *embed_near[1:]]
+    attended[0] = gate(attended[0], after)
 
     returned = [exchange(attended[0])]
     both_pair, both_groups = swapped(up_both, "seq", 1), over_groups(up_both)
-    high_pairs = over_groups(high_pair)
+    own_pairs = over_groups(own_pair)
     attended += [attention(piece, head_width) for piece in arrived[1:]]
-    after = [returned[0], both_pair, *both_groups[1:], *high_pairs[1:]]
+    after = [both_pair, *both_groups[1:], *own_pairs[1:]]
     attended[1:] = [gate(piece, after) for piece in attended[1:]]
 
     returned += [exchange(piece) for piece in attended[1:]]
     embed_parts = embed_near + [
         shifted(piece, "dom", k) for k in range(1, dom_count) for piece in embed_near
     ]
-    own_pairs, both_pairs = over_groups(own_pair), over_groups(both_pair)
-    low_pairs = [low_pair] + [swapped(piece, "seq", 1) for piece in low_groups[1:]]
-    up_parts = own_groups + own_pairs + high_groups + high_pairs
-    up_parts += low_groups + low_pairs + both_groups + both_pairs
+    next_pairs = over_groups(next_pair)
+    both_pairs = [both_pair] + [swapped(piece, "seq", 1) for piece in both_groups[1:]]
+    up_parts = own_groups + own_pairs + next_groups + next_pairs + both_groups + both_pairs
     up_offsets = [
-        offset ^ bit ^ pair for bit in (0, high, low, high ^ low) for pair in (0, 1) for offset in near
+        offset ^ bit ^ pair
+        for bits in ((0,), (high, low), (high ^ low,))
+        for pair in (0, 1)
+        for bit in bits
+        for offset in near
     ]
     embed_offsets = near + [offset ^ high for offset in near]
     for bit in (low, 1):
@@ -635,7 +636,7 @@
         embed_parts,
         norm_gain,
         group_count,
-        [*own_pairs[1:], *low_pairs[1:], *both_pairs[1:]],
+        [*next_pairs[1:], *both_pairs[1:]],
     )
     stepped_other = shifted(stepped, "dom", 1)
     features_other = shifted(features, "dom", 1)

time: 170 us -> 164 us (0.965)
  starting transfers between devices: 57.8 us -> 53.2 us
    ppermute x12 -> x10, waiting for transfers between devices: 2.78 us -> 7.15 us  [shifted(): lax.ppermute(array, axis, [(i, (i + step) % count) for i in range(count)])]
    ppermute x11 -> x10, waiting for transfers between devices: 51 us -> 47.4 us  [swapped(): lax.ppermute(array, axis, [(i, i ^ bit) for i in range(lax.axis_size(axis...]
    ppermute x12 -> x10, starting transfers between devices: 10.2 us -> 7.02 us  [shifted(): lax.ppermute(array, axis, [(i, (i + step) % count) for i in range(count)])]
    unnamed x48 -> x41, local copies, waits for them, and re-layouts: 7.61 us -> 5.59 us
    ppermute x11 -> x10, starting transfers between devices: 21.3 us -> 19.8 us  [swapped(): lax.ppermute(array, axis, [(i, i ^ bit) for i in range(lax.axis_size(axis...]
  transfers between devices with their start and end apart: 28 -> 25, of which waited for: 11 -> 12; matrix products, arithmetic and copies ran while one was open for 2% -> 3% of each run, Pallas kernels for 17% -> 17%
where the time goes in v14:
time: 164 us; the launch traced here: 163 us
  waiting for transfers between devices  59.3 us (36%)
  starting transfers between devices  53.2 us (32%)
  Pallas kernels  38.2 us (23%)
  local copies, waits for them, and re-layouts  7.57 us (5%)
  other arithmetic  3.3 us (2%)
    ppermute x10, waiting for transfers between devices, swapped(): lax.ppermute(array, axis, [(i, i ^ bit) for i in range(lax.axis_size(axis...  47.4 us
    all_to_all x4, starting transfers between devices, exchange(): return lax.all_to_all(array, 'seq', 0, 0, tiled=True)  20.6 us
    ppermute x10, starting transfers between devices, swapped(): lax.ppermute(array, axis, [(i, i ^ bit) for i in range(lax.axis_size(axis...  19.8 us
    pallas_call x2, Pallas kernels, attention(): pl.pallas_call(functools.partial(attention_kernel, head_width, block_sour...  11 us
    pallas_call x1, Pallas kernels, project_embed(): pl.pallas_call(kernel, in_specs=[smem, hbm, vmem, hbm] + ([] if begun is...  8.72 us
    pallas_call x1, Pallas kernels, reward(): pl.pallas_call(functools.partial(reward_kernel, particles, scale, parts,...  7.28 us
    ppermute x10, waiting for transfers between devices, shifted(): lax.ppermute(array, axis, [(i, (i + step) % count) for i in range(count)])  7.15 us
    ppermute x10, starting transfers between devices, shifted(): lax.ppermute(array, axis, [(i, (i + step) % count) for i in range(count)])  7.02 us
  transfers between devices with their start and end apart: 25, of which 12 were waited for; matrix products, arithmetic and copies ran while one was open for 3% of the time, Pallas kernels for 17%

profile of v14, /device:TPU:0, one launch (start us, length us, event | category | flops | bytes accessed | tf_op | source)
XLA Modules:
  0.0 163.1 jit_solution(10426735925481935034)
XLA Ops:
  1.6 4.0 %collective-permute-start = (bf16[1,192,256]{2,1,0:T(8,128)(2,1)S(1)}, bf16[1,192,256]{2,1,0:T(8,128)(2,1)S(1)}, u32[]{:S(2)}, u32[]{:S(2)}) collective-permute-start(bf16[1,192,256]{2,1,0:T(8,128)(2,1)S(1)} %dynamic-slice_bitcast_fusion.1), channel_id=1, source_target_pairs={{0,4},{1,5},{2,6},{3,7},{4,0},{5,1},{6,2},{7,3},{8,12},{9,13},{10,... | collective-permute-start | bytes 294920 | tf_op jit(solution)/shard_map/ppermute | solution.py:525
  5.7 3.2 %pack_heads.1 = (bf16[8,3,64,384]{3,2,1,0:T(8,128)(2,1)}, bf16[8,3,64,384]{3,2,1,0:T(8,128)(2,1)}) custom-call(bf16[4,64,1536]{2,1,0:T(8,128)(2,1)} %q_ref.1, bf16[4,64,1536]{2,1,0:T(8,128)(2,1)} %k_ref.1, bf16[4,64,1536]{2,1,0:T(8,128)(2,1)} %v_ref.1), custom_call_target="tpu_custom_call" | custom-call | tf_op jit(solution)/shard_map/pack_heads/pallas_call | solution.py:40
  8.9 1.7 %collective-permute-done = bf16[1,192,256]{2,1,0:T(8,128)(2,1)S(1)} collective-permute-done((bf16[1,192,256]{2,1,0:T(8,128)(2,1)S(1)}, bf16[1,192,256]{2,1,0:T(8,128)(2,1)S(1)}, u32[]{:S(2)}, u32[]{:S(2)}) %collective-permute-start) | collective-permute-done | bytes 98336 | tf_op jit(solution)/shard_map/ppermute | solution.py:525
  11.3 5.9 %all-to-all-start = ((bf16[8,3,64,384]{3,2,1,0:T(8,128)(2,1)}), bf16[8,3,64,384]{3,2,1,0:T(8,128)(2,1)S(1)}, u32[]{:S(2)}, u32[]{:S(2)}) async-start(bf16[8,3,64,384]{3,2,1,0:T(8,128)(2,1)} %gate.4), calls=%async_computation | async-start | bytes 2359296 | tf_op jit(solution)/shard_map/all_to_all | solution.py:529
  17.2 2.0 %collective-permute-start.6 = (bf16[2,192,256]{2,1,0:T(8,128)(2,1)S(1)}, bf16[2,192,256]{2,1,0:T(8,128)(2,1)S(1)}, u32[]{:S(2)}, u32[]{:S(2)}) collective-permute-start(bf16[2,192,256]{2,1,0:T(8,128)(2,1)S(1)} %copy-done.10), channel_id=1, source_target_pairs={{0,2},{1,3},{2,0},{3,1},{4,6},{5,7},{6,4},{7,5},{8,10},{9,11},{10,... | collective-permute-start | bytes 589832 | tf_op jit(solution)/shard_map/ppermute | solution.py:525
  19.2 22.1 %collective-permute-done.6 = bf16[2,192,256]{2,1,0:T(8,128)(2,1)S(1)} collective-permute-done((bf16[2,192,256]{2,1,0:T(8,128)(2,1)S(1)}, bf16[2,192,256]{2,1,0:T(8,128)(2,1)S(1)}, u32[]{:S(2)}, u32[]{:S(2)}) %collective-permute-start.6) | collective-permute-done | bytes 196640 | tf_op jit(solution)/shard_map/ppermute | solution.py:525
  42.6 4.4 %collective-permute-start.1 = (bf16[1,512,256]{2,1,0:T(8,128)(2,1)S(1)}, bf16[1,512,256]{2,1,0:T(8,128)(2,1)S(1)}, u32[]{:S(2)}, u32[]{:S(2)}) collective-permute-start(bf16[1,512,256]{2,1,0:T(8,128)(2,1)S(1)} %dynamic-slice_bitcast_fusion.refs_5_), channel_id=1, source_target_pairs={{0,4},{1,5},{2,6},{3,7},{4,0},{5,1},{6,2},{7,3},{8,12},{9,13},{10,... | collective-permute-start | bytes 786440 | tf_op jit(solution)/shard_map/ppermute | solution.py:525
  47.6 1.5 collective-permute-start.10
  49.1 4.5 %collective-permute-done.7 = bf16[4,192,256]{2,1,0:T(8,128)(2,1)} collective-permute-done((bf16[4,192,256]{2,1,0:T(8,128)(2,1)S(1)}, bf16[4,192,256]{2,1,0:T(8,128)(2,1)}, u32[]{:S(2)}, u32[]{:S(2)}) %collective-permute-start.7) | collective-permute-done | bytes 393248 | tf_op jit(solution)/shard_map/ppermute | solution.py:525
  53.6 2.0 %pad_maximum_fusion.refs_1_.refs_6_ = bf16[8,192,256]{2,1,0:T(8,128)(2,1)} fusion(bf16[4,192,256]{2,1,0:T(8,128)(2,1)} %collective-permute-done.7, bf16[2,192,256]{2,1,0:T(8,128)(2,1)S(1)} %collective-permute-done.6, bf16[1,192,256]{2,1,0:T(8,128)(2,1)S(1)} %collective-permute-done, bf16[1,192,256]{2,1,0:T(8,128)(2,1)S(1)} %dynamic-slice_bitcast_fusion.1), kind=kLoop, calls=%fused_computation | loop fusion | flops 1179648 | bytes 1572864 | tf_op jit(solution)/shard_map/concatenate | solution.py:588
  55.6 2.3 %collective-permute-done.1.refs_2_ = bf16[1,512,256]{2,1,0:T(8,128)(2,1)S(1)} collective-permute-done((bf16[1,512,256]{2,1,0:T(8,128)(2,1)S(1)}, bf16[1,512,256]{2,1,0:T(8,128)(2,1)S(1)}, u32[]{:S(2)}, u32[]{:S(2)}) %collective-permute-start.1) | collective-permute-done | bytes 262176 | tf_op jit(solution)/shard_map/ppermute | solution.py:525
  57.9 2.6 %collective-permute-done.3.refs_3_ = bf16[1,512,256]{2,1,0:T(8,128)(2,1)S(1)} collective-permute-done((bf16[1,512,256]{2,1,0:T(8,128)(2,1)S(1)}, bf16[1,512,256]{2,1,0:T(8,128)(2,1)S(1)}, u32[]{:S(2)}, u32[]{:S(2)}) %collective-permute-start.3) | collective-permute-done | bytes 262176 | tf_op jit(solution)/shard_map/ppermute | solution.py:525
  61.1 3.6 %all-to-all-start.2 = ((bf16[8,3,64,384]{3,2,1,0:T(8,128)(2,1)}), bf16[8,3,64,384]{3,2,1,0:T(8,128)(2,1)S(1)}, u32[]{:S(2)}, u32[]{:S(2)}) async-start(bf16[8,3,64,384]{3,2,1,0:T(8,128)(2,1)} %gate.6), calls=%async_computation.2 | async-start | bytes 2359296 | tf_op jit(solution)/shard_map/all_to_all | solution.py:529
  67.6 2.1 %collective-permute-start.4 = (bf16[2,512,256]{2,1,0:T(8,128)(2,1)S(1)}, bf16[2,512,256]{2,1,0:T(8,128)(2,1)S(1)}, u32[]{:S(2)}, u32[]{:S(2)}) collective-permute-start(bf16[2,512,256]{2,1,0:T(8,128)(2,1)S(1)} %constant_dynamic-update-slice_fusion.refs_9_), channel_id=1, source_target_pairs={{0,1},{1,0},{2,3},{3,2},{4,5},{5,4},{6,7},{7,6},{8,9},{9,8},{10,11... | collective-permute-start | bytes 1572872 | tf_op jit(solution)/shard_map/ppermute | solution.py:525
  70.7 1.5 collective-permute-start.2
  72.1 5.5 %attention.2.refs_0_ = bf16[8,64,384]{2,1,0:T(8,128)(2,1)S(1)} custom-call(bf16[8,3,64,384]{3,2,1,0:T(8,128)(2,1)S(1)} %all-to-all-done.qkv_ref), custom_call_target="tpu_custom_call" | custom-call | flops 402653184 | bytes 1572864 | tf_op jit(solution)/shard_map/attention/pallas_call | solution.py:104
  78.4 9.8 %collective-permute-done.2.refs_1_.refs_13_ = bf16[1,512,256]{2,1,0:T(8,128)(2,1)} collective-permute-done((bf16[1,512,256]{2,1,0:T(8,128)(2,1)}, bf16[1,512,256]{2,1,0:T(8,128)(2,1)}, u32[]{:S(2)}, u32[]{:S(2)}) %collective-permute-start.2) | collective-permute-done | bytes 262176 | tf_op jit(solution)/shard_map/ppermute | solution.py:525
  88.2 1.6 collective-permute-done.4.refs_2_.refs_11_
  89.8 4.1 %collective-permute-done.5.refs_3_.refs_10_ = bf16[2,512,256]{2,1,0:T(8,128)(2,1)} collective-permute-done((bf16[2,512,256]{2,1,0:T(8,128)(2,1)S(1)}, bf16[2,512,256]{2,1,0:T(8,128)(2,1)}, u32[]{:S(2)}, u32[]{:S(2)}) %collective-permute-start.5) | collective-permute-done | bytes 524320 | tf_op jit(solution)/shard_map/ppermute | solution.py:521
  94.0 5.6 %all-to-all-start.1 = ((bf16[8,64,384]{2,1,0:T(8,128)(2,1)}), bf16[8,64,384]{2,1,0:T(8,128)(2,1)}, u32[]{:S(2)}, u32[]{:S(2)}) async-start(bf16[8,64,384]{2,1,0:T(8,128)(2,1)} %gate.5), calls=%async_computation.1 | async-start | bytes 786432 | tf_op jit(solution)/shard_map/all_to_all | solution.py:529
  101.6 2.0 %collective-permute-start.11 = (bf16[1,512,256]{2,1,0:T(8,128)(2,1)}, bf16[1,512,256]{2,1,0:T(8,128)(2,1)}, u32[]{:S(2)}, u32[]{:S(2)}) collective-permute-start(bf16[1,512,256]{2,1,0:T(8,128)(2,1)} %collective-permute-done.2.refs_1_.refs_13_), channel_id=1, source_target_pairs={{0,1},{1,0},{2,3},{3,2},{4,5},{5,4},{6,7},{7,6},{8,9},{9,8},{10,11... | collective-permute-start | bytes 786440 | tf_op jit(solution)/shard_map/ppermute | solution.py:525
  104.1 5.5 %attention.3.refs_0_ = bf16[8,64,384]{2,1,0:T(8,128)(2,1)S(1)} custom-call(bf16[8,3,64,384]{3,2,1,0:T(8,128)(2,1)S(1)} %all-to-all-done.2.qkv_ref), custom_call_target="tpu_custom_call" | custom-call | flops 402653184 | bytes 1572864 | tf_op jit(solution)/shard_map/attention/pallas_call | solution.py:104
  111.2 5.6 %all-to-all-start.3 = ((bf16[8,64,384]{2,1,0:T(8,128)(2,1)}), bf16[8,64,384]{2,1,0:T(8,128)(2,1)S(1)}, u32[]{:S(2)}, u32[]{:S(2)}) async-start(bf16[8,64,384]{2,1,0:T(8,128)(2,1)} %gate.7), calls=%async_computation.3 | async-start | bytes 786432 | tf_op jit(solution)/shard_map/all_to_all | solution.py:529
  117.2 2.0 %collective-permute-start.17 = (bf16[1,512,256]{2,1,0:T(8,128)(2,1)}, bf16[1,512,256]{2,1,0:T(8,128)(2,1)S(1)}, u32[]{:S(2)}, u32[]{:S(2)}) collective-permute-start(bf16[1,512,256]{2,1,0:T(8,128)(2,1)} %copy-done.17), channel_id=1, source_target_pairs={{0,1},{1,0},{2,3},{3,2},{4,5},{5,4},{6,7},{7,6},{8,9},{9,8},{10,11... | collective-permute-start | bytes 786440 | tf_op jit(solution)/shard_map/ppermute | solution.py:525
  120.5 4.7 %first_project.1.refs_4_ = f32[256,1536]{1,0:T(8,128)} custom-call(bf16[4,64,1536]{2,1,0:T(8,128)(2,1)} %refs_1_.2, bf16[1536,1536]{1,0:T(8,128)(2,1)} %refs_3_.1, bf16[8,64,384]{2,1,0:T(8,128)(2,1)} %all-to-all-done.1.piece_ref), custom_call_target="tpu_custom_call" | custom-call | flops 603979776 | bytes 5505024 | tf_op jit(solution)/shard_map/first_project/pallas_call | solution.py:181
  125.2 2.9 %collective-permute-done.17.refs_11_.refs_16_ = bf16[1,512,256]{2,1,0:T(8,128)(2,1)S(1)} collective-permute-done((bf16[1,512,256]{2,1,0:T(8,128)(2,1)}, bf16[1,512,256]{2,1,0:T(8,128)(2,1)S(1)}, u32[]{:S(2)}, u32[]{:S(2)}) %collective-permute-start.17) | collective-permute-done | bytes 262176 | tf_op jit(solution)/shard_map/ppermute | solution.py:525
  130.3 8.7 %project_embed.1 = (bf16[4,64,1536]{2,1,0:T(8,128)(2,1)}, bf16[2,256,512]{2,1,0:T(8,128)(2,1)}) custom-call(s32[4]{0:T(128)} %pad_add_fusion.refs_0_.ids_ref, bf16[4,64,1536]{2,1,0:T(8,128)(2,1)} %refs_1_.2, f32[1,1024]{1,0:T(1,128)} %bitcast.10, bf16[1536,1536]{1,0:T(8,128)(2,1)} %refs_3_.1, f32[256,1536]{1,0:T(8,128)} %first_project.1.refs_4_, ...), custom_call_target="tpu_custom_call" | custom-call | flops 1409286144 | bytes 10223616 | tf_op jit(solution)/shard_map/project_embed/pallas_call | solution.py:331
  139.6 1.6 collective-permute-done.19.refs_4_
  142.0 7.3 %reward.1 = f32[16,8,128]{2,1,0:T(8,128)} custom-call(s32[4]{0:T(128)} %pad_add_fusion.refs_0_.ids_ref, f32[4]{0:T(128)} %refs_1_.3, f32[16,1,256]{2,1,0:T(1,128)} %bitcast.11, bf16[2,256,512]{2,1,0:T(8,128)(2,1)} %get-tuple-element.11.refs_3_, bf16[2,256,512]{2,1,0:T(8,128)(2,1)} %copy-done.19, bf16[1,512,256]{2,1,0:T(8,128)(2,1)} %copy-done.15, ...), custom_call_target="tpu_custom_call" | custom-call | flops 2147483648 | bytes 4194304 | tf_op jit(solution)/shard_map/reward/pallas_call | solution.py:436
  149.3 5.8 %all-to-all-start.4 = ((f32[16,8,128]{2,1,0:T(8,128)}), f32[16,8,128]{2,1,0:T(8,128)S(1)}, u32[]{:S(2)}, u32[]{:S(2)}) async-start(f32[16,8,128]{2,1,0:T(8,128)} %reward.1), calls=%async_computation.4 | async-start | bytes 131072 | tf_op jit(solution)/shard_map/all_to_all | solution.py:658
  155.1 2.0 %resample.1.resampled_ref = bf16[4,64,1536]{2,1,0:T(8,128)(2,1)} custom-call(s32[4]{0:T(128)S(1)} %copy-done.4, s32[4]{0:T(128)S(1)} %copy-done.5, bf16[4,64,1536]{2,1,0:T(8,128)(2,1)S(1)} %copy-done.3, bf16[4,64,1536]{2,1,0:T(8,128)(2,1)S(1)} %collective-permute-done.18.other_ref), custom_call_target="tpu_custom_call" | custom-call | tf_op jit(solution)/shard_map/resample/pallas_call | solution.py:505
  157.1 4.7 %all-to-all-done.4.parts_ref = f32[16,8,128]{2,1,0:T(8,128)S(1)} async-done(((f32[16,8,128]{2,1,0:T(8,128)}), f32[16,8,128]{2,1,0:T(8,128)S(1)}, u32[]{:S(2)}, u32[]{:S(2)}) %all-to-all-start.4) | async-done | bytes 65568 | tf_op jit(solution)/shard_map/all_to_all | solution.py:658
  (78 shorter events, 18.9 us)
Async XLA Ops:
  0.6 42.0 %copy-start = (bf16[1024,512]{1,0:T(8,128)(2,1)S(1)}, bf16[1024,512]{1,0:T(8,128)(2,1)}, u32[]{:S(2)}) copy-start(bf16[1024,512]{1,0:T(8,128)(2,1)} %param.20) | copy-start | bytes 3145732
  1.6 8.9 %collective-permute-start = (bf16[1,192,256]{2,1,0:T(8,128)(2,1)S(1)}, bf16[1,192,256]{2,1,0:T(8,128)(2,1)S(1)}, u32[]{:S(2)}, u32[]{:S(2)}) collective-permute-start(bf16[1,192,256]{2,1,0:T(8,128)(2,1)S(1)} %dynamic-slice_bitcast_fusion.1), channel_id=1, source_target_pairs={{0,4},{1,5},{2,6},{3,7},{4,0},{5,1},{6,2},{7,3},{8,12},{9,13},{10,... | collective-permute-start | bytes 294920 | tf_op jit(solution)/shard_map/ppermute | solution.py:525
  11.3 49.9 %all-to-all-start = ((bf16[8,3,64,384]{3,2,1,0:T(8,128)(2,1)}), bf16[8,3,64,384]{3,2,1,0:T(8,128)(2,1)S(1)}, u32[]{:S(2)}, u32[]{:S(2)}) async-start(bf16[8,3,64,384]{3,2,1,0:T(8,128)(2,1)} %gate.4), calls=%async_computation | async-start | bytes 2359296 | tf_op jit(solution)/shard_map/all_to_all | solution.py:529
  17.2 24.2 %collective-permute-start.6 = (bf16[2,192,256]{2,1,0:T(8,128)(2,1)S(1)}, bf16[2,192,256]{2,1,0:T(8,128)(2,1)S(1)}, u32[]{:S(2)}, u32[]{:S(2)}) collective-permute-start(bf16[2,192,256]{2,1,0:T(8,128)(2,1)S(1)} %copy-done.10), channel_id=1, source_target_pairs={{0,2},{1,3},{2,0},{3,1},{4,6},{5,7},{6,4},{7,5},{8,10},{9,11},{10,... | collective-permute-start | bytes 589832 | tf_op jit(solution)/shard_map/ppermute | solution.py:525
  41.4 12.2 %collective-permute-start.7 = (bf16[4,192,256]{2,1,0:T(8,128)(2,1)S(1)}, bf16[4,192,256]{2,1,0:T(8,128)(2,1)}, u32[]{:S(2)}, u32[]{:S(2)}) collective-permute-start(bf16[4,192,256]{2,1,0:T(8,128)(2,1)S(1)} %pad_maximum_fusion.1), channel_id=1, source_target_pairs={{0,1},{1,0},{2,3},{3,2},{4,5},{5,4},{6,7},{7,6},{8,9},{9,8},{10,11... | collective-permute-start | bytes 1179656 | tf_op jit(solution)/shard_map/ppermute | solution.py:525
  42.6 17.8 %copy-start.15 = (bf16[1,512,256]{2,1,0:T(8,128)(2,1)}, bf16[1,512,256]{2,1,0:T(8,128)(2,1)S(1)}, u32[]{:S(2)}) copy-start(bf16[1,512,256]{2,1,0:T(8,128)(2,1)S(1)} %dynamic-slice_bitcast_fusion.refs_5_) | copy-start | bytes 786436
  42.6 15.2 %collective-permute-start.1 = (bf16[1,512,256]{2,1,0:T(8,128)(2,1)S(1)}, bf16[1,512,256]{2,1,0:T(8,128)(2,1)S(1)}, u32[]{:S(2)}, u32[]{:S(2)}) collective-permute-start(bf16[1,512,256]{2,1,0:T(8,128)(2,1)S(1)} %dynamic-slice_bitcast_fusion.refs_5_), channel_id=1, source_target_pairs={{0,4},{1,5},{2,6},{3,7},{4,0},{5,1},{6,2},{7,3},{8,12},{9,13},{10,... | collective-permute-start | bytes 786440 | tf_op jit(solution)/shard_map/ppermute | solution.py:525
  47.0 10.8 %collective-permute-start.9 = (bf16[1,512,256]{2,1,0:T(8,128)(2,1)S(1)}, bf16[1,512,256]{2,1,0:T(8,128)(2,1)}, u32[]{:S(2)}, u32[]{:S(2)}) collective-permute-start(bf16[1,512,256]{2,1,0:T(8,128)(2,1)S(1)} %dynamic-slice_bitcast_fusion.refs_5_), channel_id=1, source_target_pairs={{0,1},{1,0},{2,3},{3,2},{4,5},{5,4},{6,7},{7,6},{8,9},{9,8},{10,11... | collective-permute-start | bytes 786440 | tf_op jit(solution)/shard_map/ppermute | solution.py:525
  47.6 10.2 %collective-permute-start.10 = (bf16[1,512,256]{2,1,0:T(8,128)(2,1)S(1)}, bf16[1,512,256]{2,1,0:T(8,128)(2,1)S(1)}, u32[]{:S(2)}, u32[]{:S(2)}) collective-permute-start(bf16[1,512,256]{2,1,0:T(8,128)(2,1)S(1)} %dynamic-slice_bitcast_fusion.refs_5_), channel_id=1, source_target_pairs={{0,16},{16,0},{1,17},{17,1},{2,18},{18,2},{3,19},{19,3},{4,20},{20... | collective-permute-start | bytes 786440 | tf_op jit(solution)/shard_map/ppermute | solution.py:521
  49.1 11.3 %collective-permute-start.3 = (bf16[1,512,256]{2,1,0:T(8,128)(2,1)S(1)}, bf16[1,512,256]{2,1,0:T(8,128)(2,1)S(1)}, u32[]{:S(2)}, u32[]{:S(2)}) collective-permute-start(bf16[1,512,256]{2,1,0:T(8,128)(2,1)S(1)} %dynamic-slice_bitcast_fusion.refs_5_), channel_id=1, source_target_pairs={{0,2},{1,3},{2,0},{3,1},{4,6},{5,7},{6,4},{7,5},{8,10},{9,11},{10,... | collective-permute-start | bytes 786440 | tf_op jit(solution)/shard_map/ppermute | solution.py:525
  61.1 32.8 %all-to-all-start.2 = ((bf16[8,3,64,384]{3,2,1,0:T(8,128)(2,1)}), bf16[8,3,64,384]{3,2,1,0:T(8,128)(2,1)S(1)}, u32[]{:S(2)}, u32[]{:S(2)}) async-start(bf16[8,3,64,384]{3,2,1,0:T(8,128)(2,1)} %gate.6), calls=%async_computation.2 | async-start | bytes 2359296 | tf_op jit(solution)/shard_map/all_to_all | solution.py:529
  64.7 29.2 %collective-permute-start.8 = (bf16[8,192,256]{2,1,0:T(8,128)(2,1)}, bf16[8,192,256]{2,1,0:T(8,128)(2,1)}, u32[]{:S(2)}, u32[]{:S(2)}) collective-permute-start(bf16[8,192,256]{2,1,0:T(8,128)(2,1)} %pad_maximum_fusion.refs_1_.refs_6_), channel_id=1, source_target_pairs={{0,16},{16,0},{1,17},{17,1},{2,18},{18,2},{3,19},{19,3},{4,20},{20... | collective-permute-start | bytes 2359304 | tf_op jit(solution)/shard_map/ppermute | solution.py:521
  67.5 10.1 %copy-start.18 = (bf16[2,512,256]{2,1,0:T(8,128)(2,1)}, bf16[2,512,256]{2,1,0:T(8,128)(2,1)S(1)}, u32[]{:S(2)}) copy-start(bf16[2,512,256]{2,1,0:T(8,128)(2,1)S(1)} %constant_dynamic-update-slice_fusion.refs_9_) | copy-start | bytes 1572868
  67.6 22.2 %collective-permute-start.4 = (bf16[2,512,256]{2,1,0:T(8,128)(2,1)S(1)}, bf16[2,512,256]{2,1,0:T(8,128)(2,1)S(1)}, u32[]{:S(2)}, u32[]{:S(2)}) collective-permute-start(bf16[2,512,256]{2,1,0:T(8,128)(2,1)S(1)} %constant_dynamic-update-slice_fusion.refs_9_), channel_id=1, source_target_pairs={{0,1},{1,0},{2,3},{3,2},{4,5},{5,4},{6,7},{7,6},{8,9},{9,8},{10,11... | collective-permute-start | bytes 1572872 | tf_op jit(solution)/shard_map/ppermute | solution.py:525
  69.6 24.3 %collective-permute-start.5 = (bf16[2,512,256]{2,1,0:T(8,128)(2,1)S(1)}, bf16[2,512,256]{2,1,0:T(8,128)(2,1)}, u32[]{:S(2)}, u32[]{:S(2)}) collective-permute-start(bf16[2,512,256]{2,1,0:T(8,128)(2,1)S(1)} %constant_dynamic-update-slice_fusion.refs_9_), channel_id=1, source_target_pairs={{0,16},{16,0},{1,17},{17,1},{2,18},{18,2},{3,19},{19,3},{4,20},{20... | collective-permute-start | bytes 1572872 | tf_op jit(solution)/shard_map/ppermute | solution.py:521
  70.7 17.6 %collective-permute-start.2 = (bf16[1,512,256]{2,1,0:T(8,128)(2,1)}, bf16[1,512,256]{2,1,0:T(8,128)(2,1)}, u32[]{:S(2)}, u32[]{:S(2)}) collective-permute-start(bf16[1,512,256]{2,1,0:T(8,128)(2,1)} %copy-done.8), channel_id=1, source_target_pairs={{0,2},{1,3},{2,0},{3,1},{4,6},{5,7},{6,4},{7,5},{8,10},{9,11},{10,... | collective-permute-start | bytes 786440 | tf_op jit(solution)/shard_map/ppermute | solution.py:525
  78.4 25.2 %copy-start.6 = (bf16[8,192,256]{2,1,0:T(8,128)(2,1)S(1)}, bf16[8,192,256]{2,1,0:T(8,128)(2,1)}, u32[]{:S(2)}) copy-start(bf16[8,192,256]{2,1,0:T(8,128)(2,1)} %pad_maximum_fusion.refs_1_.refs_6_) | copy-start | bytes 2359300
  94.0 17.2 %all-to-all-start.1 = ((bf16[8,64,384]{2,1,0:T(8,128)(2,1)}), bf16[8,64,384]{2,1,0:T(8,128)(2,1)}, u32[]{:S(2)}, u32[]{:S(2)}) async-start(bf16[8,64,384]{2,1,0:T(8,128)(2,1)} %gate.5), calls=%async_computation.1 | async-start | bytes 786432 | tf_op jit(solution)/shard_map/all_to_all | solution.py:529
  99.6 10.8 %collective-permute-start.13 = (bf16[1,512,256]{2,1,0:T(8,128)(2,1)}, bf16[1,512,256]{2,1,0:T(8,128)(2,1)S(1)}, u32[]{:S(2)}, u32[]{:S(2)}) collective-permute-start(bf16[1,512,256]{2,1,0:T(8,128)(2,1)} %collective-permute-done.9.refs_4_.refs_7_), channel_id=1, source_target_pairs={{0,16},{16,0},{1,17},{17,1},{2,18},{18,2},{3,19},{19,3},{4,20},{20... | collective-permute-start | bytes 786440 | tf_op jit(solution)/shard_map/ppermute | solution.py:521
  100.3 10.1 %collective-permute-start.12 = (bf16[1,512,256]{2,1,0:T(8,128)(2,1)}, bf16[1,512,256]{2,1,0:T(8,128)(2,1)S(1)}, u32[]{:S(2)}, u32[]{:S(2)}) collective-permute-start(bf16[1,512,256]{2,1,0:T(8,128)(2,1)} %collective-permute-done.2.refs_1_.refs_13_), channel_id=1, source_target_pairs={{0,16},{16,0},{1,17},{17,1},{2,18},{18,2},{3,19},{19,3},{4,20},{20... | collective-permute-start | bytes 786440 | tf_op jit(solution)/shard_map/ppermute | solution.py:521
  101.6 8.8 %collective-permute-start.11 = (bf16[1,512,256]{2,1,0:T(8,128)(2,1)}, bf16[1,512,256]{2,1,0:T(8,128)(2,1)}, u32[]{:S(2)}, u32[]{:S(2)}) collective-permute-start(bf16[1,512,256]{2,1,0:T(8,128)(2,1)} %collective-permute-done.2.refs_1_.refs_13_), channel_id=1, source_target_pairs={{0,1},{1,0},{2,3},{3,2},{4,5},{5,4},{6,7},{7,6},{8,9},{9,8},{10,11... | collective-permute-start | bytes 786440 | tf_op jit(solution)/shard_map/ppermute | solution.py:525
  103.6 25.8 %collective-permute-start.14 = (bf16[8,192,256]{2,1,0:T(8,128)(2,1)S(1)}, bf16[8,192,256]{2,1,0:T(8,128)(2,1)}, u32[]{:S(2)}, u32[]{:S(2)}) collective-permute-start(bf16[8,192,256]{2,1,0:T(8,128)(2,1)S(1)} %copy-done.6), channel_id=1, source_target_pairs={{0,8},{8,0},{1,9},{9,1},{2,10},{10,2},{3,11},{11,3},{4,12},{12,4},... | collective-permute-start | bytes 2359304 | tf_op jit(solution)/shard_map/ppermute | solution.py:521
  103.6 25.8 %collective-permute-start.15 = (bf16[8,192,256]{2,1,0:T(8,128)(2,1)}, bf16[8,192,256]{2,1,0:T(8,128)(2,1)}, u32[]{:S(2)}, u32[]{:S(2)}) collective-permute-start(bf16[8,192,256]{2,1,0:T(8,128)(2,1)} %collective-permute-done.8.refs_4_.refs_7_), channel_id=1, source_target_pairs={{0,8},{8,0},{1,9},{9,1},{2,10},{10,2},{3,11},{11,3},{4,12},{12,4},... | collective-permute-start | bytes 2359304 | tf_op jit(solution)/shard_map/ppermute | solution.py:521
  111.2 18.3 %all-to-all-start.3 = ((bf16[8,64,384]{2,1,0:T(8,128)(2,1)}), bf16[8,64,384]{2,1,0:T(8,128)(2,1)S(1)}, u32[]{:S(2)}, u32[]{:S(2)}) async-start(bf16[8,64,384]{2,1,0:T(8,128)(2,1)} %gate.7), calls=%async_computation.3 | async-start | bytes 786432 | tf_op jit(solution)/shard_map/all_to_all | solution.py:529
  116.7 12.7 %collective-permute-start.16 = (bf16[2,512,256]{2,1,0:T(8,128)(2,1)S(1)}, bf16[2,512,256]{2,1,0:T(8,128)(2,1)}, u32[]{:S(2)}, u32[]{:S(2)}) collective-permute-start(bf16[2,512,256]{2,1,0:T(8,128)(2,1)S(1)} %copy-done.12), channel_id=1, source_target_pairs={{0,16},{16,0},{1,17},{17,1},{2,18},{18,2},{3,19},{19,3},{4,20},{20... | collective-permute-start | bytes 1572872 | tf_op jit(solution)/shard_map/ppermute | solution.py:521
  117.2 10.8 %collective-permute-start.17 = (bf16[1,512,256]{2,1,0:T(8,128)(2,1)}, bf16[1,512,256]{2,1,0:T(8,128)(2,1)S(1)}, u32[]{:S(2)}, u32[]{:S(2)}) collective-permute-start(bf16[1,512,256]{2,1,0:T(8,128)(2,1)} %copy-done.17), channel_id=1, source_target_pairs={{0,1},{1,0},{2,3},{3,2},{4,5},{5,4},{6,7},{7,6},{8,9},{9,8},{10,11... | collective-permute-start | bytes 786440 | tf_op jit(solution)/shard_map/ppermute | solution.py:525
  139.0 2.2 %collective-permute-start.19 = (bf16[2,256,512]{2,1,0:T(8,128)(2,1)}, bf16[2,256,512]{2,1,0:T(8,128)(2,1)S(1)}, u32[]{:S(2)}, u32[]{:S(2)}) collective-permute-start(bf16[2,256,512]{2,1,0:T(8,128)(2,1)} %get-tuple-element.11.refs_3_), channel_id=1, source_target_pairs={{0,8},{8,0},{1,9},{9,1},{2,10},{10,2},{3,11},{11,3},{4,12},{12,4},... | collective-permute-start | bytes 1572872 | tf_op jit(solution)/shard_map/ppermute | solution.py:521
  139.1 16.0 %collective-permute-start.18 = (bf16[4,64,1536]{2,1,0:T(8,128)(2,1)}, bf16[4,64,1536]{2,1,0:T(8,128)(2,1)S(1)}, u32[]{:S(2)}, u32[]{:S(2)}) collective-permute-start(bf16[4,64,1536]{2,1,0:T(8,128)(2,1)} %get-tuple-element.10.own_ref), channel_id=1, source_target_pairs={{0,8},{8,0},{1,9},{9,1},{2,10},{10,2},{3,11},{11,3},{4,12},{12,4},... | collective-permute-start | bytes 2359304 | tf_op jit(solution)/shard_map/ppermute | solution.py:521
  142.0 13.1 %copy-start.3 = (bf16[4,64,1536]{2,1,0:T(8,128)(2,1)S(1)}, bf16[4,64,1536]{2,1,0:T(8,128)(2,1)}, u32[]{:S(2)}) copy-start(bf16[4,64,1536]{2,1,0:T(8,128)(2,1)} %get-tuple-element.10.own_ref) | copy-start | bytes 2359300
  142.0 13.1 %copy-start.4 = (s32[4]{0:T(128)S(1)}, s32[4]{0:T(128)}, u32[]{:S(2)}) copy-start(s32[4]{0:T(128)} %pad_add_fusion.refs_0_.ids_ref) | copy-start | bytes 52
  142.0 13.1 %copy-start.5 = (s32[4]{0:T(128)S(1)}, s32[4]{0:T(128)}, u32[]{:S(2)}) copy-start(s32[4]{0:T(128)} %ancestors_ref.1) | copy-start | bytes 52
  149.3 12.5 %all-to-all-start.4 = ((f32[16,8,128]{2,1,0:T(8,128)}), f32[16,8,128]{2,1,0:T(8,128)S(1)}, u32[]{:S(2)}, u32[]{:S(2)}) async-start(f32[16,8,128]{2,1,0:T(8,128)} %reward.1), calls=%async_computation.4 | async-start | bytes 131072 | tf_op jit(solution)/shard_map/all_to_all | solution.py:658
  (13 other events, 28.4 us)

commit v15 on v11

--- a/solution.py
+++ b/solution.py
@@ -17,32 +17,31 @@
 MIB = 1024 * 1024
 
 
-def pack_kernel(splits, width, q_ref, k_ref, v_ref, *out_refs):
+def pack_kernel(chunks, width, q_ref, k_ref, v_ref, *out_refs):
     particles, _, model_width = q_ref.shape
     blocks = model_width // width
+    part = width // chunks
     for index, ref in enumerate((q_ref, k_ref, v_ref)):
         for particle in range(particles):
             for block in range(blocks):
-                for out_ref, (start, size) in zip(out_refs, splits):
-                    first = block * width + start
-                    out_ref[particle * blocks + block, index] = ref[
-                        particle, :, first : first + size
+                for chunk in range(chunks):
+                    start = block * width + chunk * part
+                    out_refs[chunk][particle * blocks + block, index] = ref[
+                        particle, :, start : start + part
                     ]
 
 
-def pack(queries, keys, values, splits, width):
+def pack(queries, keys, values, chunks, width):
     particles, tokens, model_width = queries.shape
     count = particles * model_width // width
     vmem = pl.BlockSpec(memory_space=pltpu.VMEM)
+    shape = jax.ShapeDtypeStruct((count, 3, tokens, width // chunks), queries.dtype)
     return list(
         pl.pallas_call(
-            functools.partial(pack_kernel, splits, width),
+            functools.partial(pack_kernel, chunks, width),
             in_specs=[vmem] * 3,
-            out_specs=[vmem] * len(splits),
-            out_shape=[
-                jax.ShapeDtypeStruct((count, 3, tokens, size), queries.dtype)
-                for _, size in splits
-            ],
+            out_specs=[vmem] * chunks,
+            out_shape=[shape] * chunks,
             compiler_params=pltpu.CompilerParams(vmem_limit_bytes=60 * MIB),
             name="pack_heads",
         )(queries, keys, values)
@@ -102,6 +101,7 @@
     while sources % block_sources:
         block_sources -= 1
     step = LANES if columns % LANES == 0 and LANES % head_width == 0 else columns
+    scores_bytes = 4 * block_sources * tokens * total
     first = start // step
     unread = earlier + after
     return pl.pallas_call(
@@ -112,7 +112,7 @@
         out_specs=pl.BlockSpec((sources, tokens, step), lambda i: (0, 0, first + i)),
         out_shape=jax.ShapeDtypeStruct((sources, tokens, width), jnp.bfloat16),
         input_output_aliases={1: 0} if earlier else {},
-        compiler_params=pltpu.CompilerParams(vmem_limit_bytes=60 * MIB),
+        compiler_params=pltpu.CompilerParams(vmem_limit_bytes=8 * MIB + 6 * scores_bytes),
         cost_estimate=pl.CostEstimate(
             flops=4 * total * total * columns,
             bytes_accessed=8 * total * columns,
@@ -256,11 +256,12 @@
 
 
 def reward_kernel(particles, scale, parts, doms, offsets, joined, *refs):
-    ids_ref, features_ref, head_ref, before_ref = refs[:4]
-    weight_refs, (out_ref, weight_vmem, rows_ref, sems) = refs[4:-4], refs[-4:]
+    ids_ref, prev_ref, head_ref = refs[:3]
+    features_refs, weight_refs = refs[3 : 3 + doms], refs[3 + doms : -4]
+    out_ref, weight_vmem, rows_ref, sems = refs[-4:]
     dom, group, seq = ids_ref[0], ids_ref[1], ids_ref[2]
     _, depth, columns = weight_refs[0].shape
-    rows = features_ref.shape[1]
+    rows = features_refs[0].shape[1]
     places = [
         (pair, shard)
         for pair in range(len(weight_refs) // parts)
@@ -283,11 +284,12 @@
             )
             copy.start()
             copies.append(copy)
-    for index in range(parts):
-        rows_ref[:, index * depth : (index + 1) * depth] = features_ref[
-            (group + parts - index) % parts
-        ]
-    totals = jnp.zeros((particles, joined * columns), jnp.float32)
+    for step, features_ref in enumerate(features_refs):
+        for index in range(parts):
+            rows_ref[step * rows : (step + 1) * rows, index * depth : (index + 1) * depth] = (
+                features_ref[(group + parts - index) % parts]
+            )
+    totals = jnp.zeros((doms * particles, joined * columns), jnp.float32)
     for step in range(count // joined):
         for copy in copies[step * joined * parts : (step + 1) * joined * parts]:
             copy.wait()
@@ -300,50 +302,50 @@
             axis=1,
         )
         scored = jax.nn.gelu(hidden) * head
-        totals += jnp.sum(scored.reshape(particles, rows // particles, -1), axis=1)
+        totals += jnp.sum(scored.reshape(doms * particles, rows // particles, -1), axis=1)
 
     sums = jnp.sum(totals, axis=1, keepdims=True) * scale
-    first = len(before_ref.shape) == 1
-    shape = out_ref.shape[-2:]
+    shape = out_ref.shape[1:]
     out_rows = lax.broadcasted_iota(jnp.int32, shape, 0)
     lanes = lax.broadcasted_iota(jnp.int32, shape, 1)
-    logits = jnp.zeros(shape, jnp.float32) if first else before_ref[...]
-    row = dom if first else (dom + 1) % doms
-    for particle in range(particles):
-        here = jnp.logical_and(out_rows == row, lanes == particle)
-        value = sums[particle : particle + 1]
-        if first:
-            value = value + jnp.where(seq == 0, before_ref[particle], 0.0)
+    logits = jnp.zeros(shape, jnp.float32)
+    for index in range(doms * particles):
+        step, particle = divmod(index, particles)
+        value = sums[index : index + 1]
+        if step == 0:
+            value = value + jnp.where(seq == 0, prev_ref[particle], 0.0)
+        here = jnp.logical_and(out_rows == (dom + doms - step) % doms, lanes == particle)
         logits += jnp.where(here, value, 0.0)
-    out_ref[...] = jnp.broadcast_to(logits, out_ref.shape)
-
-
-def reward(ids, features, weights, parts, doms, offsets, head, before, particles, scale, copies):
+    out_ref[...] = jnp.broadcast_to(logits[None], out_ref.shape)
+
+
+def reward(ids, prev_logw, features, weights, parts, offsets, head, particles, scale, copies):
     _, depth, columns = weights[0].shape
-    rows = features.shape[1]
+    rows, doms = features[0].shape[1], len(features)
     count = len(offsets)
     joined = 2 if columns % LANES == 0 and count % 2 == 0 else 1
     smem = pl.BlockSpec(memory_space=pltpu.SMEM)
     vmem = pl.BlockSpec(memory_space=pltpu.VMEM)
     return pl.pallas_call(
         functools.partial(reward_kernel, particles, scale, parts, doms, offsets, joined),
-        in_specs=[smem, vmem, vmem, smem if before.ndim == 1 else vmem]
+        in_specs=[smem, smem, vmem]
+        + [vmem] * doms
         + [pl.BlockSpec(memory_space=pltpu.HBM)] * len(weights),
         out_specs=vmem,
-        out_shape=jax.ShapeDtypeStruct((*copies, 8, LANES), jnp.float32),
+        out_shape=jax.ShapeDtypeStruct((copies, 8, LANES), jnp.float32),
         scratch_shapes=[
             pltpu.VMEM((count // joined, parts * depth, joined * columns), jnp.bfloat16),
-            pltpu.VMEM((rows, parts * depth), jnp.bfloat16),
+            pltpu.VMEM((doms * rows, parts * depth), jnp.bfloat16),
             pltpu.SemaphoreType.DMA((count, parts)),
         ],
         compiler_params=pltpu.CompilerParams(vmem_limit_bytes=60 * MIB),
         cost_estimate=pl.CostEstimate(
-            flops=2 * rows * parts * depth * count * columns,
+            flops=2 * doms * rows * parts * depth * count * columns,
             bytes_accessed=2 * parts * depth * count * columns,
-            transcendentals=rows * count * columns,
+            transcendentals=doms * rows * count * columns,
         ),
         name="reward",
-    )(ids, features, head, before, *weights)
+    )(ids, prev_logw, head, *features, *weights)
 
 
 def finish_kernel(particles, doms, ids_ref, resampled_ref, parts_ref, out_ref, same_ref):
@@ -444,10 +446,7 @@
     particles, tokens, model_width = latents.shape
     head_width = model_width // HEADS
     width = particles * model_width // seq_count
-    splits = [(0, width)]
-    if width % LANES == 0 and width >= 2 * LANES:
-        start = -(-2 * width // (3 * LANES)) * LANES
-        splits = [(0, start), (start, width - start)]
+    chunks = 2 if width % (2 * LANES) == 0 else 1
 
     ids = jnp.stack([dom, group, seq, step_index[0]]).astype(jnp.int32)
 
@@ -471,43 +470,46 @@
     def over_groups(array):
         return [array] + [shifted(array, "groups", k) for k in range(1, group_count)]
 
-    packed = pack(queries, keys, values, splits, width)
+    packed = pack(queries, keys, values, chunks, width)
     embed_share = jnp.concatenate([embed_share, swapped(embed_share, "seq", high)])
     packed[0] = gate(packed[0], [embed_share])
 
     arrived = [exchange(packed[0])]
-    up_high = swapped(up_share, "seq", high)
+    up_high, up_low = swapped(up_share, "seq", high), swapped(up_share, "seq", low)
     own_pair, own_groups = swapped(up_share, "seq", 1), over_groups(up_share)
     for bit in (low, 1):
         embed_share = jnp.concatenate([embed_share, swapped(embed_share, "seq", bit)])
-    after = [arrived[0], embed_share, up_high, own_pair, *own_groups[1:]]
+    after = [embed_share, up_high, up_low, own_pair, *own_groups[1:]]
     packed[1:] = [gate(piece, after) for piece in packed[1:]]
 
     arrived += [exchange(piece) for piece in packed[1:]]
-    up_far = swapped(jnp.concatenate([up_share, up_high]), "seq", low)
-    high_pair, high_groups = swapped(up_high, "seq", 1), over_groups(up_high)
-    own_pairs = [own_pair] + [swapped(piece, "seq", 1) for piece in own_groups[1:]]
+    up_both = swapped(up_high, "seq", low)
+    up_next = jnp.concatenate([up_high, up_low])
+    next_pair, next_groups = swapped(up_next, "seq", 1), over_groups(up_next)
     embed_near = over_groups(embed_share)
-    after = [up_far, high_pair, *high_groups[1:], *own_pairs[1:], *embed_near[1:]]
+    after = [up_both, next_pair, *next_groups[1:], *embed_near[1:]]
     attended = []
-    for piece, (start, _) in zip(arrived, splits):
+    for index, piece in enumerate(arrived):
+        start = index * (width // chunks)
         attended = [
-            attention(piece, head_width, width, start, attended, after if attended else [])
+            attention(piece, head_width, width, start, attended, after if index else [])
         ]
 
     returned = exchange(attended[0])
-    far_pair, far_groups = swapped(up_far, "seq", 1), over_groups(up_far)
+    both_pair, both_groups = swapped(up_both, "seq", 1), over_groups(up_both)
+    own_pairs = over_groups(own_pair)
     embed_parts = embed_near + [
         shifted(piece, "dom", k) for k in range(1, dom_count) for piece in embed_near
     ]
-    high_pairs = [high_pair] + [swapped(piece, "seq", 1) for piece in high_groups[1:]]
-    far_pairs = over_groups(far_pair)
-    up_parts = [own_groups, own_pairs, high_groups, high_pairs, far_groups, far_pairs]
-    far = [offset ^ low for offset in near + [offset ^ high for offset in near]]
+    next_pairs = over_groups(next_pair)
+    both_pairs = [both_pair] + [swapped(piece, "seq", 1) for piece in both_groups[1:]]
+    up_parts = own_groups + own_pairs + next_groups + next_pairs + both_groups + both_pairs
     up_offsets = [
-        [offset ^ bit for offset in offsets]
-        for offsets in (near, [offset ^ high for offset in near], far)
-        for bit in (0, 1)
+        offset ^ bit ^ pair
+        for bits in ((0,), (high, low), (high ^ low,))
+        for pair in (0, 1)
+        for bit in bits
+        for offset in near
     ]
     embed_offsets = near + [offset ^ high for offset in near]
     for bit in (low, 1):
@@ -522,26 +524,25 @@
         embed_parts,
         norm_gain,
         group_count,
-        [*high_pairs[1:], *far_groups[1:], *far_pairs],
+        [*own_pairs[1:], *next_pairs[1:], *both_groups[1:], *both_pairs],
     )
     stepped_other = shifted(stepped, "dom", 1)
     features_other = shifted(features, "dom", 1)
 
     scale = potential_scale / math.sqrt(tokens * seq_count)
     head = head_weight.reshape(seq_count * dom_count, 1, up_columns)
-    score = functools.partial(
-        reward,
+    partial = reward(
         ids,
-        weights=[piece for pieces in up_parts for piece in pieces],
-        parts=group_count,
-        doms=dom_count,
-        offsets=[offset for offsets in up_offsets for offset in offsets],
-        head=head,
-        particles=particles,
-        scale=scale,
+        prev_logw,
+        [features, features_other],
+        up_parts,
+        group_count,
+        up_offsets,
+        head,
+        particles,
+        scale,
+        dom_count * seq_count,
     )
-    partial_own = score(features, before=prev_logw, copies=())
-    partial = score(features_other, before=partial_own, copies=(dom_count * seq_count,))
     logits = lax.all_to_all(partial, ("dom", "seq"), 0, 0, tiled=True)
     resampled = resample(ids, ancestors.astype(jnp.int32), stepped, stepped_other)
     return finish(ids, logits, resampled, particles, dom_count)

time: 177 us -> 171 us (0.966)
  waiting for transfers between devices: 77.5 us -> 70.1 us
  local copies, waits for them, and re-layouts: 4.83 us -> 11.6 us
  Pallas kernels: 40.4 us -> 34 us
  starting transfers between devices: 47.2 us -> 49.7 us
    ppermute x10, waiting for transfers between devices: 60.9 us -> 47.5 us  [swapped(): lax.ppermute(array, axis, [(i, i ^ bit) for i in range(lax.axis_size(axis...]
    unnamed x46 -> x55, local copies, waits for them, and re-layouts: 3.83 us -> 10.6 us
    ppermute x9 -> x10, waiting for transfers between devices: 12 us -> 17.9 us  [shifted(): lax.ppermute(array, axis, [(i, (i + step) % count) for i in range(count)])]
    pallas_call x2 -> x1, Pallas kernels: 10.8 us -> 7.29 us  [reward(): pl.pallas_call(functools.partial(reward_kernel, particles, scale, parts,...]
    pallas_call x2, Pallas kernels: 13.8 us -> 11 us  [attention(): pl.pallas_call(functools.partial(attention_kernel, head_width, block_sour...]
    ppermute x9 -> x10, starting transfers between devices: 7.64 us -> 8.17 us  [shifted(): lax.ppermute(array, axis, [(i, (i + step) % count) for i in range(count)])]
  transfers between devices with their start and end apart: 23 -> 24, of which waited for: 10 -> 15; matrix products, arithmetic and copies ran while one was open for 2% -> 2% of each run, Pallas kernels for 14% -> 11%
where the time goes in v15:
time: 171 us; the launch traced here: 170 us
  waiting for transfers between devices  70.1 us (41%)
  starting transfers between devices  49.7 us (29%)
  Pallas kernels  34 us (20%)
  local copies, waits for them, and re-layouts  11.6 us (7%)
  other arithmetic  3.29 us (2%)
    ppermute x10, waiting for transfers between devices, swapped(): lax.ppermute(array, axis, [(i, i ^ bit) for i in range(lax.axis_size(axis...  47.5 us
    ppermute x10, starting transfers between devices, swapped(): lax.ppermute(array, axis, [(i, i ^ bit) for i in range(lax.axis_size(axis...  19.7 us
    ppermute x10, waiting for transfers between devices, shifted(): lax.ppermute(array, axis, [(i, (i + step) % count) for i in range(count)])  17.9 us
    all_to_all x3, starting transfers between devices, exchange(): return lax.all_to_all(array, 'seq', 0, 0, tiled=True)  15.8 us
    pallas_call x2, Pallas kernels, attention(): pl.pallas_call(functools.partial(attention_kernel, head_width, block_sour...  11 us
    unnamed x55, local copies, waits for them, and re-layouts  10.6 us
    pallas_call x1, Pallas kernels, project_embed(): pl.pallas_call(kernel, in_specs=[pl.BlockSpec(memory_space=pltpu.SMEM), h...  9.21 us
    ppermute x10, starting transfers between devices, shifted(): lax.ppermute(array, axis, [(i, (i + step) % count) for i in range(count)])  8.17 us
  transfers between devices with their start and end apart: 24, of which 15 were waited for; matrix products, arithmetic and copies ran while one was open for 2% of the time, Pallas kernels for 11%

profile of v15, /device:TPU:0, one launch (start us, length us, event | category | flops | bytes accessed | tf_op | source)
XLA Modules:
  0.0 170.2 jit_solution(4313016237146151405)
XLA Ops:
  1.6 4.0 %collective-permute-start = (bf16[1,192,256]{2,1,0:T(8,128)(2,1)S(1)}, bf16[1,192,256]{2,1,0:T(8,128)(2,1)S(1)}, u32[]{:S(2)}, u32[]{:S(2)}) collective-permute-start(bf16[1,192,256]{2,1,0:T(8,128)(2,1)S(1)} %dynamic-slice_bitcast_fusion.1), channel_id=1, source_target_pairs={{0,4},{1,5},{2,6},{3,7},{4,0},{5,1},{6,2},{7,3},{8,12},{9,13},{10,... | collective-permute-start | bytes 294920 | tf_op jit(solution)/shard_map/ppermute | solution.py:418
  5.7 3.2 %pack_heads.1 = (bf16[8,3,64,384]{3,2,1,0:T(8,128)(2,1)}, bf16[8,3,64,384]{3,2,1,0:T(8,128)(2,1)}) custom-call(bf16[4,64,1536]{2,1,0:T(8,128)(2,1)} %q_ref.1, bf16[4,64,1536]{2,1,0:T(8,128)(2,1)} %k_ref.1, bf16[4,64,1536]{2,1,0:T(8,128)(2,1)} %v_ref.1), custom_call_target="tpu_custom_call" | custom-call | tf_op jit(solution)/shard_map/pack_heads/pallas_call | solution.py:40
  8.9 1.7 collective-permute-done
  11.3 5.9 %all-to-all-start.1 = ((bf16[8,3,64,384]{3,2,1,0:T(8,128)(2,1)}), bf16[8,3,64,384]{3,2,1,0:T(8,128)(2,1)S(1)}, u32[]{:S(2)}, u32[]{:S(2)}) async-start(bf16[8,3,64,384]{3,2,1,0:T(8,128)(2,1)} %gate.3), calls=%async_computation.1 | async-start | bytes 2359296 | tf_op jit(solution)/shard_map/all_to_all | solution.py:422
  17.2 2.0 %collective-permute-start.1 = (bf16[2,192,256]{2,1,0:T(8,128)(2,1)S(1)}, bf16[2,192,256]{2,1,0:T(8,128)(2,1)S(1)}, u32[]{:S(2)}, u32[]{:S(2)}) collective-permute-start(bf16[2,192,256]{2,1,0:T(8,128)(2,1)S(1)} %copy-done.21), channel_id=1, source_target_pairs={{0,2},{1,3},{2,0},{3,1},{4,6},{5,7},{6,4},{7,5},{8,10},{9,11},{10,... | collective-permute-start | bytes 589832 | tf_op jit(solution)/shard_map/ppermute | solution.py:418
  19.2 22.1 %collective-permute-done.1 = bf16[2,192,256]{2,1,0:T(8,128)(2,1)S(1)} collective-permute-done((bf16[2,192,256]{2,1,0:T(8,128)(2,1)S(1)}, bf16[2,192,256]{2,1,0:T(8,128)(2,1)S(1)}, u32[]{:S(2)}, u32[]{:S(2)}) %collective-permute-start.1) | collective-permute-done | bytes 196640 | tf_op jit(solution)/shard_map/ppermute | solution.py:418
  42.6 4.4 %collective-permute-start.3 = (bf16[1,512,256]{2,1,0:T(8,128)(2,1)S(1)}, bf16[1,512,256]{2,1,0:T(8,128)(2,1)S(1)}, u32[]{:S(2)}, u32[]{:S(2)}) collective-permute-start(bf16[1,512,256]{2,1,0:T(8,128)(2,1)S(1)} %dynamic-slice_bitcast_fusion.refs_5_), channel_id=1, source_target_pairs={{0,4},{1,5},{2,6},{3,7},{4,0},{5,1},{6,2},{7,3},{8,12},{9,13},{10,... | collective-permute-start | bytes 786440 | tf_op jit(solution)/shard_map/ppermute | solution.py:418
  49.1 4.5 %collective-permute-done.2 = bf16[4,192,256]{2,1,0:T(8,128)(2,1)} collective-permute-done((bf16[4,192,256]{2,1,0:T(8,128)(2,1)S(1)}, bf16[4,192,256]{2,1,0:T(8,128)(2,1)}, u32[]{:S(2)}, u32[]{:S(2)}) %collective-permute-start.2) | collective-permute-done | bytes 393248 | tf_op jit(solution)/shard_map/ppermute | solution.py:418
  53.6 2.0 %pad_maximum_fusion.refs_1_.refs_5_ = bf16[8,192,256]{2,1,0:T(8,128)(2,1)} fusion(bf16[4,192,256]{2,1,0:T(8,128)(2,1)} %collective-permute-done.2, bf16[2,192,256]{2,1,0:T(8,128)(2,1)S(1)} %collective-permute-done.1, bf16[1,192,256]{2,1,0:T(8,128)(2,1)S(1)} %collective-permute-done, bf16[1,192,256]{2,1,0:T(8,128)(2,1)S(1)} %dynamic-slice_bitcast_fusion.1), kind=kLoop, calls=%fused_computation | loop fusion | flops 1179648 | bytes 1572864 | tf_op jit(solution)/shard_map/concatenate | solution.py:481
  55.6 2.3 %collective-permute-done.3.refs_2_ = bf16[1,512,256]{2,1,0:T(8,128)(2,1)S(1)} collective-permute-done((bf16[1,512,256]{2,1,0:T(8,128)(2,1)S(1)}, bf16[1,512,256]{2,1,0:T(8,128)(2,1)S(1)}, u32[]{:S(2)}, u32[]{:S(2)}) %collective-permute-start.3) | collective-permute-done | bytes 262176 | tf_op jit(solution)/shard_map/ppermute | solution.py:418
  61.0 4.2 %all-to-all-start = ((bf16[8,3,64,384]{3,2,1,0:T(8,128)(2,1)}), bf16[8,3,64,384]{3,2,1,0:T(8,128)(2,1)S(1)}, u32[]{:S(2)}, u32[]{:S(2)}) async-start(bf16[8,3,64,384]{3,2,1,0:T(8,128)(2,1)} %gate.2), calls=%async_computation | async-start | bytes 2359296 | tf_op jit(solution)/shard_map/all_to_all | solution.py:422
  65.2 1.5 collective-permute-start.10
  66.7 2.1 %collective-permute-start.8 = (bf16[2,512,256]{2,1,0:T(8,128)(2,1)S(1)}, bf16[2,512,256]{2,1,0:T(8,128)(2,1)S(1)}, u32[]{:S(2)}, u32[]{:S(2)}) collective-permute-start(bf16[2,512,256]{2,1,0:T(8,128)(2,1)S(1)} %constant_dynamic-update-slice_fusion.refs_9_), channel_id=1, source_target_pairs={{0,1},{1,0},{2,3},{3,2},{4,5},{5,4},{6,7},{7,6},{8,9},{9,8},{10,11... | collective-permute-start | bytes 1572872 | tf_op jit(solution)/shard_map/ppermute | solution.py:418
  72.1 5.5 %attention.2.refs_0_ = bf16[8,64,768]{2,1,0:T(8,128)(2,1)S(1)} custom-call(bf16[8,3,64,384]{3,2,1,0:T(8,128)(2,1)S(1)} %copy-done.6), custom_call_target="tpu_custom_call" | custom-call | flops 402653184 | bytes 1572864 | tf_op jit(solution)/shard_map/attention/pallas_call | solution.py:107
  78.5 10.2 %collective-permute-done.7.refs_1_.refs_13_ = bf16[1,512,256]{2,1,0:T(8,128)(2,1)S(1)} collective-permute-done((bf16[1,512,256]{2,1,0:T(8,128)(2,1)}, bf16[1,512,256]{2,1,0:T(8,128)(2,1)S(1)}, u32[]{:S(2)}, u32[]{:S(2)}) %collective-permute-start.7) | collective-permute-done | bytes 262176 | tf_op jit(solution)/shard_map/ppermute | solution.py:418
  89.8 4.4 %collective-permute-done.9.refs_3_.refs_10_ = bf16[2,512,256]{2,1,0:T(8,128)(2,1)S(1)} collective-permute-done((bf16[2,512,256]{2,1,0:T(8,128)(2,1)S(1)}, bf16[2,512,256]{2,1,0:T(8,128)(2,1)S(1)}, u32[]{:S(2)}, u32[]{:S(2)}) %collective-permute-start.9) | collective-permute-done | bytes 524320 | tf_op jit(solution)/shard_map/ppermute | solution.py:414
  98.4 5.5 %attention.3 = bf16[8,64,768]{2,1,0:T(8,128)(2,1)S(1)} custom-call(bf16[8,3,64,384]{3,2,1,0:T(8,128)(2,1)S(1)} %all-to-all-done.qkv_ref, bf16[8,64,768]{2,1,0:T(8,128)(2,1)S(1)} %copy-done.3, bf16[1,512,256]{2,1,0:T(8,128)(2,1)S(1)} %copy-done.12, bf16[2,512,256]{2,1,0:T(8,128)(2,1)S(1)} %collective-permute-done.8.refs_2_.refs_11_, ...), custom_call_target="tpu_custom_call", output_to_operand_aliasing={{}: (1, {})} | custom-call | flops 402653184 | bytes 1572864 | tf_op jit(solution)/shard_map/attention/pallas_call | solution.py:107
  104.9 5.7 %all-to-all-start.2 = ((bf16[8,64,768]{2,1,0:T(8,128)(2,1)}), bf16[8,64,768]{2,1,0:T(8,128)(2,1)}, u32[]{:S(2)}, u32[]{:S(2)}) async-start(bf16[8,64,768]{2,1,0:T(8,128)(2,1)} %copy-done.4), calls=%async_computation.2 | async-start | bytes 1572864 | tf_op jit(solution)/shard_map/all_to_all | solution.py:422
  111.2 1.5 collective-permute-start.13
  113.2 1.5 collective-permute-start.14
  114.7 5.8 %collective-permute-done.13.refs_9_.refs_8_ = bf16[1,512,256]{2,1,0:T(8,128)(2,1)S(1)} collective-permute-done((bf16[1,512,256]{2,1,0:T(8,128)(2,1)}, bf16[1,512,256]{2,1,0:T(8,128)(2,1)S(1)}, u32[]{:S(2)}, u32[]{:S(2)}) %collective-permute-start.13) | collective-permute-done | bytes 262176 | tf_op jit(solution)/shard_map/ppermute | solution.py:414
  120.5 2.0 %collective-permute-start.16 = (bf16[1,512,256]{2,1,0:T(8,128)(2,1)S(1)}, bf16[1,512,256]{2,1,0:T(8,128)(2,1)}, u32[]{:S(2)}, u32[]{:S(2)}) collective-permute-start(bf16[1,512,256]{2,1,0:T(8,128)(2,1)S(1)} %copy-done.13), channel_id=1, source_target_pairs={{0,1},{1,0},{2,3},{3,2},{4,5},{5,4},{6,7},{7,6},{8,9},{9,8},{10,11... | collective-permute-start | bytes 786440 | tf_op jit(solution)/shard_map/ppermute | solution.py:418
  122.5 3.8 %collective-permute-done.15.refs_11_.refs_14_ = bf16[1,512,256]{2,1,0:T(8,128)(2,1)} collective-permute-done((bf16[1,512,256]{2,1,0:T(8,128)(2,1)S(1)}, bf16[1,512,256]{2,1,0:T(8,128)(2,1)}, u32[]{:S(2)}, u32[]{:S(2)}) %collective-permute-start.15) | collective-permute-done | bytes 262176 | tf_op jit(solution)/shard_map/ppermute | solution.py:414
  126.3 2.0 %collective-permute-start.17 = (bf16[1,512,256]{2,1,0:T(8,128)(2,1)}, bf16[1,512,256]{2,1,0:T(8,128)(2,1)}, u32[]{:S(2)}, u32[]{:S(2)}) collective-permute-start(bf16[1,512,256]{2,1,0:T(8,128)(2,1)} %collective-permute-done.15.refs_11_.refs_14_), channel_id=1, source_target_pairs={{0,1},{1,0},{2,3},{3,2},{4,5},{5,4},{6,7},{7,6},{8,9},{9,8},{10,11... | collective-permute-start | bytes 786440 | tf_op jit(solution)/shard_map/ppermute | solution.py:418
  129.7 4.7 %collective-permute-done.17.refs_13_.refs_16_ = bf16[1,512,256]{2,1,0:T(8,128)(2,1)} collective-permute-done((bf16[1,512,256]{2,1,0:T(8,128)(2,1)}, bf16[1,512,256]{2,1,0:T(8,128)(2,1)}, u32[]{:S(2)}, u32[]{:S(2)}) %collective-permute-start.17) | collective-permute-done | bytes 262176 | tf_op jit(solution)/shard_map/ppermute | solution.py:418
  134.4 2.3 %collective-permute-done.14.refs_10_.refs_12_ = bf16[2,512,256]{2,1,0:T(8,128)(2,1)} collective-permute-done((bf16[2,512,256]{2,1,0:T(8,128)(2,1)S(1)}, bf16[2,512,256]{2,1,0:T(8,128)(2,1)}, u32[]{:S(2)}, u32[]{:S(2)}) %collective-permute-start.14) | collective-permute-done | bytes 524320 | tf_op jit(solution)/shard_map/ppermute | solution.py:414
  136.6 9.2 %project_embed.1 = (bf16[4,64,1536]{2,1,0:T(8,128)(2,1)}, bf16[2,256,512]{2,1,0:T(8,128)(2,1)}) custom-call(s32[4]{0:T(128)} %pad_add_fusion.refs_0_.ids_ref, bf16[4,64,1536]{2,1,0:T(8,128)(2,1)} %refs_1_.2, f32[1,1024]{1,0:T(1,128)} %bitcast.10, bf16[1536,1536]{1,0:T(8,128)(2,1)} %refs_3_.1, bf16[8,64,768]{2,1,0:T(8,128)(2,1)} %all-to-all-done.2.refs_4_, ...), custom_call_target="tpu_custom_call" | custom-call | flops 2013265920 | bytes 11010048 | tf_op jit(solution)/shard_map/project_embed/pallas_call | solution.py:228
  146.4 1.6 collective-permute-done.19.refs_4_
  148.9 7.3 %reward.1 = f32[16,8,128]{2,1,0:T(8,128)} custom-call(s32[4]{0:T(128)} %pad_add_fusion.refs_0_.ids_ref, f32[4]{0:T(128)} %refs_1_.3, f32[16,1,256]{2,1,0:T(1,128)} %bitcast.11, bf16[2,256,512]{2,1,0:T(8,128)(2,1)} %get-tuple-element.11.refs_3_, bf16[2,256,512]{2,1,0:T(8,128)(2,1)} %copy-done.26, bf16[1,512,256]{2,1,0:T(8,128)(2,1)} %copy-done.24, ...), custom_call_target="tpu_custom_call" | custom-call | flops 2147483648 | bytes 4194304 | tf_op jit(solution)/shard_map/reward/pallas_call | solution.py:329
  156.1 6.0 %all-to-all-start.3 = ((f32[16,8,128]{2,1,0:T(8,128)}), f32[16,8,128]{2,1,0:T(8,128)S(1)}, u32[]{:S(2)}, u32[]{:S(2)}) async-start(f32[16,8,128]{2,1,0:T(8,128)} %reward.1), calls=%async_computation.3 | async-start | bytes 131072 | tf_op jit(solution)/shard_map/all_to_all | solution.py:546
  162.2 2.0 %resample.1.resampled_ref = bf16[4,64,1536]{2,1,0:T(8,128)(2,1)} custom-call(s32[4]{0:T(128)S(1)} %copy-done.14, s32[4]{0:T(128)S(1)} %copy-done.15, bf16[4,64,1536]{2,1,0:T(8,128)(2,1)S(1)} %copy-done.7, bf16[4,64,1536]{2,1,0:T(8,128)(2,1)S(1)} %collective-permute-done.18.other_ref), custom_call_target="tpu_custom_call" | custom-call | tf_op jit(solution)/shard_map/resample/pallas_call | solution.py:398
  164.3 4.7 %all-to-all-done.3.parts_ref = f32[16,8,128]{2,1,0:T(8,128)S(1)} async-done(((f32[16,8,128]{2,1,0:T(8,128)}), f32[16,8,128]{2,1,0:T(8,128)S(1)}, u32[]{:S(2)}, u32[]{:S(2)}) %all-to-all-start.3) | async-done | bytes 65568 | tf_op jit(solution)/shard_map/all_to_all | solution.py:546
  (87 shorter events, 23.1 us)
Async XLA Ops:
  0.6 42.0 %copy-start = (bf16[1024,512]{1,0:T(8,128)(2,1)S(1)}, bf16[1024,512]{1,0:T(8,128)(2,1)}, u32[]{:S(2)}) copy-start(bf16[1024,512]{1,0:T(8,128)(2,1)} %param.20) | copy-start | bytes 3145732
  1.6 8.9 %collective-permute-start = (bf16[1,192,256]{2,1,0:T(8,128)(2,1)S(1)}, bf16[1,192,256]{2,1,0:T(8,128)(2,1)S(1)}, u32[]{:S(2)}, u32[]{:S(2)}) collective-permute-start(bf16[1,192,256]{2,1,0:T(8,128)(2,1)S(1)} %dynamic-slice_bitcast_fusion.1), channel_id=1, source_target_pairs={{0,4},{1,5},{2,6},{3,7},{4,0},{5,1},{6,2},{7,3},{8,12},{9,13},{10,... | collective-permute-start | bytes 294920 | tf_op jit(solution)/shard_map/ppermute | solution.py:418
  11.3 48.6 %all-to-all-start.1 = ((bf16[8,3,64,384]{3,2,1,0:T(8,128)(2,1)}), bf16[8,3,64,384]{3,2,1,0:T(8,128)(2,1)S(1)}, u32[]{:S(2)}, u32[]{:S(2)}) async-start(bf16[8,3,64,384]{3,2,1,0:T(8,128)(2,1)} %gate.3), calls=%async_computation.1 | async-start | bytes 2359296 | tf_op jit(solution)/shard_map/all_to_all | solution.py:422
  17.2 24.2 %collective-permute-start.1 = (bf16[2,192,256]{2,1,0:T(8,128)(2,1)S(1)}, bf16[2,192,256]{2,1,0:T(8,128)(2,1)S(1)}, u32[]{:S(2)}, u32[]{:S(2)}) collective-permute-start(bf16[2,192,256]{2,1,0:T(8,128)(2,1)S(1)} %copy-done.21), channel_id=1, source_target_pairs={{0,2},{1,3},{2,0},{3,1},{4,6},{5,7},{6,4},{7,5},{8,10},{9,11},{10,... | collective-permute-start | bytes 589832 | tf_op jit(solution)/shard_map/ppermute | solution.py:418
  41.4 12.2 %collective-permute-start.2 = (bf16[4,192,256]{2,1,0:T(8,128)(2,1)S(1)}, bf16[4,192,256]{2,1,0:T(8,128)(2,1)}, u32[]{:S(2)}, u32[]{:S(2)}) collective-permute-start(bf16[4,192,256]{2,1,0:T(8,128)(2,1)S(1)} %pad_maximum_fusion.1), channel_id=1, source_target_pairs={{0,1},{1,0},{2,3},{3,2},{4,5},{5,4},{6,7},{7,6},{8,9},{9,8},{10,11... | collective-permute-start | bytes 1179656 | tf_op jit(solution)/shard_map/ppermute | solution.py:418
  42.6 16.6 %copy-start.24 = (bf16[1,512,256]{2,1,0:T(8,128)(2,1)}, bf16[1,512,256]{2,1,0:T(8,128)(2,1)S(1)}, u32[]{:S(2)}) copy-start(bf16[1,512,256]{2,1,0:T(8,128)(2,1)S(1)} %dynamic-slice_bitcast_fusion.refs_5_) | copy-start | bytes 786436
  42.6 15.2 %collective-permute-start.3 = (bf16[1,512,256]{2,1,0:T(8,128)(2,1)S(1)}, bf16[1,512,256]{2,1,0:T(8,128)(2,1)S(1)}, u32[]{:S(2)}, u32[]{:S(2)}) collective-permute-start(bf16[1,512,256]{2,1,0:T(8,128)(2,1)S(1)} %dynamic-slice_bitcast_fusion.refs_5_), channel_id=1, source_target_pairs={{0,4},{1,5},{2,6},{3,7},{4,0},{5,1},{6,2},{7,3},{8,12},{9,13},{10,... | collective-permute-start | bytes 786440 | tf_op jit(solution)/shard_map/ppermute | solution.py:418
  47.0 10.8 %collective-permute-start.5 = (bf16[1,512,256]{2,1,0:T(8,128)(2,1)S(1)}, bf16[1,512,256]{2,1,0:T(8,128)(2,1)S(1)}, u32[]{:S(2)}, u32[]{:S(2)}) collective-permute-start(bf16[1,512,256]{2,1,0:T(8,128)(2,1)S(1)} %dynamic-slice_bitcast_fusion.refs_5_), channel_id=1, source_target_pairs={{0,1},{1,0},{2,3},{3,2},{4,5},{5,4},{6,7},{7,6},{8,9},{9,8},{10,11... | collective-permute-start | bytes 786440 | tf_op jit(solution)/shard_map/ppermute | solution.py:418
  47.6 11.6 %collective-permute-start.4 = (bf16[1,512,256]{2,1,0:T(8,128)(2,1)S(1)}, bf16[1,512,256]{2,1,0:T(8,128)(2,1)S(1)}, u32[]{:S(2)}, u32[]{:S(2)}) collective-permute-start(bf16[1,512,256]{2,1,0:T(8,128)(2,1)S(1)} %dynamic-slice_bitcast_fusion.refs_5_), channel_id=1, source_target_pairs={{0,2},{1,3},{2,0},{3,1},{4,6},{5,7},{6,4},{7,5},{8,10},{9,11},{10,... | collective-permute-start | bytes 786440 | tf_op jit(solution)/shard_map/ppermute | solution.py:418
  47.6 11.6 %collective-permute-start.6 = (bf16[1,512,256]{2,1,0:T(8,128)(2,1)S(1)}, bf16[1,512,256]{2,1,0:T(8,128)(2,1)}, u32[]{:S(2)}, u32[]{:S(2)}) collective-permute-start(bf16[1,512,256]{2,1,0:T(8,128)(2,1)S(1)} %dynamic-slice_bitcast_fusion.refs_5_), channel_id=1, source_target_pairs={{0,16},{16,0},{1,17},{17,1},{2,18},{18,2},{3,19},{19,3},{4,20},{20... | collective-permute-start | bytes 786440 | tf_op jit(solution)/shard_map/ppermute | solution.py:414
  61.0 34.1 %all-to-all-start = ((bf16[8,3,64,384]{3,2,1,0:T(8,128)(2,1)}), bf16[8,3,64,384]{3,2,1,0:T(8,128)(2,1)S(1)}, u32[]{:S(2)}, u32[]{:S(2)}) async-start(bf16[8,3,64,384]{3,2,1,0:T(8,128)(2,1)} %gate.2), calls=%async_computation | async-start | bytes 2359296 | tf_op jit(solution)/shard_map/all_to_all | solution.py:422
  65.2 29.9 %collective-permute-start.10 = (bf16[8,192,256]{2,1,0:T(8,128)(2,1)}, bf16[8,192,256]{2,1,0:T(8,128)(2,1)S(1)}, u32[]{:S(2)}, u32[]{:S(2)}) collective-permute-start(bf16[8,192,256]{2,1,0:T(8,128)(2,1)} %pad_maximum_fusion.refs_1_.refs_5_), channel_id=1, source_target_pairs={{0,16},{16,0},{1,17},{17,1},{2,18},{18,2},{3,19},{19,3},{4,20},{20... | collective-permute-start | bytes 2359304 | tf_op jit(solution)/shard_map/ppermute | solution.py:414
  66.7 10.9 %copy-start.25 = (bf16[2,512,256]{2,1,0:T(8,128)(2,1)}, bf16[2,512,256]{2,1,0:T(8,128)(2,1)S(1)}, u32[]{:S(2)}) copy-start(bf16[2,512,256]{2,1,0:T(8,128)(2,1)S(1)} %constant_dynamic-update-slice_fusion.refs_9_) | copy-start | bytes 1572868
  66.7 23.1 %collective-permute-start.8 = (bf16[2,512,256]{2,1,0:T(8,128)(2,1)S(1)}, bf16[2,512,256]{2,1,0:T(8,128)(2,1)S(1)}, u32[]{:S(2)}, u32[]{:S(2)}) collective-permute-start(bf16[2,512,256]{2,1,0:T(8,128)(2,1)S(1)} %constant_dynamic-update-slice_fusion.refs_9_), channel_id=1, source_target_pairs={{0,1},{1,0},{2,3},{3,2},{4,5},{5,4},{6,7},{7,6},{8,9},{9,8},{10,11... | collective-permute-start | bytes 1572872 | tf_op jit(solution)/shard_map/ppermute | solution.py:418
  68.8 25.4 %collective-permute-start.9 = (bf16[2,512,256]{2,1,0:T(8,128)(2,1)S(1)}, bf16[2,512,256]{2,1,0:T(8,128)(2,1)S(1)}, u32[]{:S(2)}, u32[]{:S(2)}) collective-permute-start(bf16[2,512,256]{2,1,0:T(8,128)(2,1)S(1)} %constant_dynamic-update-slice_fusion.refs_9_), channel_id=1, source_target_pairs={{0,16},{16,0},{1,17},{17,1},{2,18},{18,2},{3,19},{19,3},{4,20},{20... | collective-permute-start | bytes 1572872 | tf_op jit(solution)/shard_map/ppermute | solution.py:414
  69.3 19.4 %collective-permute-start.7 = (bf16[1,512,256]{2,1,0:T(8,128)(2,1)}, bf16[1,512,256]{2,1,0:T(8,128)(2,1)S(1)}, u32[]{:S(2)}, u32[]{:S(2)}) collective-permute-start(bf16[1,512,256]{2,1,0:T(8,128)(2,1)} %copy-done.17), channel_id=1, source_target_pairs={{0,2},{1,3},{2,0},{3,1},{4,6},{5,7},{6,4},{7,5},{8,10},{9,11},{10,... | collective-permute-start | bytes 786440 | tf_op jit(solution)/shard_map/ppermute | solution.py:418
  89.8 23.4 %copy-start.8 = (bf16[2,512,256]{2,1,0:T(8,128)(2,1)}, bf16[2,512,256]{2,1,0:T(8,128)(2,1)S(1)}, u32[]{:S(2)}) copy-start(bf16[2,512,256]{2,1,0:T(8,128)(2,1)S(1)} %collective-permute-done.8.refs_2_.refs_11_) | copy-start | bytes 1572868
  95.0 15.7 %copy-start.1 = (bf16[8,192,256]{2,1,0:T(8,128)(2,1)}, bf16[8,192,256]{2,1,0:T(8,128)(2,1)S(1)}, u32[]{:S(2)}) copy-start(bf16[8,192,256]{2,1,0:T(8,128)(2,1)S(1)} %collective-permute-done.10.refs_4_.refs_6_) | copy-start | bytes 2359300
  104.9 31.8 %all-to-all-start.2 = ((bf16[8,64,768]{2,1,0:T(8,128)(2,1)}), bf16[8,64,768]{2,1,0:T(8,128)(2,1)}, u32[]{:S(2)}, u32[]{:S(2)}) async-start(bf16[8,64,768]{2,1,0:T(8,128)(2,1)} %copy-done.4), calls=%async_computation.2 | async-start | bytes 1572864 | tf_op jit(solution)/shard_map/all_to_all | solution.py:422
  110.6 26.0 %collective-permute-start.11 = (bf16[8,192,256]{2,1,0:T(8,128)(2,1)S(1)}, bf16[8,192,256]{2,1,0:T(8,128)(2,1)}, u32[]{:S(2)}, u32[]{:S(2)}) collective-permute-start(bf16[8,192,256]{2,1,0:T(8,128)(2,1)S(1)} %copy-done.16), channel_id=1, source_target_pairs={{0,8},{8,0},{1,9},{9,1},{2,10},{10,2},{3,11},{11,3},{4,12},{12,4},... | collective-permute-start | bytes 2359304 | tf_op jit(solution)/shard_map/ppermute | solution.py:414
  110.7 26.0 %collective-permute-start.12 = (bf16[8,192,256]{2,1,0:T(8,128)(2,1)S(1)}, bf16[8,192,256]{2,1,0:T(8,128)(2,1)}, u32[]{:S(2)}, u32[]{:S(2)}) collective-permute-start(bf16[8,192,256]{2,1,0:T(8,128)(2,1)S(1)} %collective-permute-done.10.refs_4_.refs_6_), channel_id=1, source_target_pairs={{0,8},{8,0},{1,9},{9,1},{2,10},{10,2},{3,11},{11,3},{4,12},{12,4},... | collective-permute-start | bytes 2359304 | tf_op jit(solution)/shard_map/ppermute | solution.py:414
  111.2 9.4 %collective-permute-start.13 = (bf16[1,512,256]{2,1,0:T(8,128)(2,1)}, bf16[1,512,256]{2,1,0:T(8,128)(2,1)S(1)}, u32[]{:S(2)}, u32[]{:S(2)}) collective-permute-start(bf16[1,512,256]{2,1,0:T(8,128)(2,1)} %copy-done.22), channel_id=1, source_target_pairs={{0,16},{16,0},{1,17},{17,1},{2,18},{18,2},{3,19},{19,3},{4,20},{20... | collective-permute-start | bytes 786440 | tf_op jit(solution)/shard_map/ppermute | solution.py:414
  112.7 13.6 %collective-permute-start.15 = (bf16[1,512,256]{2,1,0:T(8,128)(2,1)S(1)}, bf16[1,512,256]{2,1,0:T(8,128)(2,1)}, u32[]{:S(2)}, u32[]{:S(2)}) collective-permute-start(bf16[1,512,256]{2,1,0:T(8,128)(2,1)S(1)} %copy-done.13), channel_id=1, source_target_pairs={{0,16},{16,0},{1,17},{17,1},{2,18},{18,2},{3,19},{19,3},{4,20},{20... | collective-permute-start | bytes 786440 | tf_op jit(solution)/shard_map/ppermute | solution.py:414
  113.2 23.4 %collective-permute-start.14 = (bf16[2,512,256]{2,1,0:T(8,128)(2,1)S(1)}, bf16[2,512,256]{2,1,0:T(8,128)(2,1)}, u32[]{:S(2)}, u32[]{:S(2)}) collective-permute-start(bf16[2,512,256]{2,1,0:T(8,128)(2,1)S(1)} %collective-permute-done.8.refs_2_.refs_11_), channel_id=1, source_target_pairs={{0,16},{16,0},{1,17},{17,1},{2,18},{18,2},{3,19},{19,3},{4,20},{20... | collective-permute-start | bytes 1572872 | tf_op jit(solution)/shard_map/ppermute | solution.py:414
  120.5 9.1 %collective-permute-start.16 = (bf16[1,512,256]{2,1,0:T(8,128)(2,1)S(1)}, bf16[1,512,256]{2,1,0:T(8,128)(2,1)}, u32[]{:S(2)}, u32[]{:S(2)}) collective-permute-start(bf16[1,512,256]{2,1,0:T(8,128)(2,1)S(1)} %copy-done.13), channel_id=1, source_target_pairs={{0,1},{1,0},{2,3},{3,2},{4,5},{5,4},{6,7},{7,6},{8,9},{9,8},{10,11... | collective-permute-start | bytes 786440 | tf_op jit(solution)/shard_map/ppermute | solution.py:418
  126.3 8.1 %collective-permute-start.17 = (bf16[1,512,256]{2,1,0:T(8,128)(2,1)}, bf16[1,512,256]{2,1,0:T(8,128)(2,1)}, u32[]{:S(2)}, u32[]{:S(2)}) collective-permute-start(bf16[1,512,256]{2,1,0:T(8,128)(2,1)} %collective-permute-done.15.refs_11_.refs_14_), channel_id=1, source_target_pairs={{0,1},{1,0},{2,3},{3,2},{4,5},{5,4},{6,7},{7,6},{8,9},{9,8},{10,11... | collective-permute-start | bytes 786440 | tf_op jit(solution)/shard_map/ppermute | solution.py:418
  145.9 2.2 %collective-permute-start.19 = (bf16[2,256,512]{2,1,0:T(8,128)(2,1)}, bf16[2,256,512]{2,1,0:T(8,128)(2,1)S(1)}, u32[]{:S(2)}, u32[]{:S(2)}) collective-permute-start(bf16[2,256,512]{2,1,0:T(8,128)(2,1)} %get-tuple-element.11.refs_3_), channel_id=1, source_target_pairs={{0,8},{8,0},{1,9},{9,1},{2,10},{10,2},{3,11},{11,3},{4,12},{12,4},... | collective-permute-start | bytes 1572872 | tf_op jit(solution)/shard_map/ppermute | solution.py:414
  145.9 16.3 %collective-permute-start.18 = (bf16[4,64,1536]{2,1,0:T(8,128)(2,1)}, bf16[4,64,1536]{2,1,0:T(8,128)(2,1)S(1)}, u32[]{:S(2)}, u32[]{:S(2)}) collective-permute-start(bf16[4,64,1536]{2,1,0:T(8,128)(2,1)} %get-tuple-element.10.own_ref), channel_id=1, source_target_pairs={{0,8},{8,0},{1,9},{9,1},{2,10},{10,2},{3,11},{11,3},{4,12},{12,4},... | collective-permute-start | bytes 2359304 | tf_op jit(solution)/shard_map/ppermute | solution.py:414
  148.8 13.4 %copy-start.7 = (bf16[4,64,1536]{2,1,0:T(8,128)(2,1)S(1)}, bf16[4,64,1536]{2,1,0:T(8,128)(2,1)}, u32[]{:S(2)}) copy-start(bf16[4,64,1536]{2,1,0:T(8,128)(2,1)} %get-tuple-element.10.own_ref) | copy-start | bytes 2359300
  148.8 13.4 %copy-start.14 = (s32[4]{0:T(128)S(1)}, s32[4]{0:T(128)}, u32[]{:S(2)}) copy-start(s32[4]{0:T(128)} %pad_add_fusion.refs_0_.ids_ref) | copy-start | bytes 52
  148.8 13.4 %copy-start.15 = (s32[4]{0:T(128)S(1)}, s32[4]{0:T(128)}, u32[]{:S(2)}) copy-start(s32[4]{0:T(128)} %ancestors_ref.1) | copy-start | bytes 52
  156.1 12.8 %all-to-all-start.3 = ((f32[16,8,128]{2,1,0:T(8,128)}), f32[16,8,128]{2,1,0:T(8,128)S(1)}, u32[]{:S(2)}, u32[]{:S(2)}) async-start(f32[16,8,128]{2,1,0:T(8,128)} %reward.1), calls=%async_computation.3 | async-start | bytes 131072 | tf_op jit(solution)/shard_map/all_to_all | solution.py:546
  (19 other events, 49.9 us)

commit v16 on v14

--- a/solution.py
+++ b/solution.py
@@ -247,21 +247,24 @@
             copies.append(copy)
 
     gather_rows(rest, rows_ref, particles)
-    for index in range(model_width // out_weights.block):
+    each = len(first_copies) // (model_width // block)
+
+    def product(index):
         cols = out_weights.wait(index)
-        each = len(first_copies) // (model_width // block)
         for copy in first_copies[index * each : (index + 1) * each]:
             copy.wait()
-        flat = latents_ref[:, :, cols].reshape(rows, out_weights.block).astype(jnp.float32)
-        begun = begun_ref[:, cols] if chunks > 1 else flat
-        velocity = begun + jnp.dot(
-            rows_ref[...], out_vmem[:, cols], preferred_element_type=jnp.float32
-        )
+        return jnp.dot(rows_ref[...], out_vmem[:, cols], preferred_element_type=jnp.float32)
+
+    following = product(0)
+    for index in range(model_width // block):
+        cols, projected = slice(index * block, (index + 1) * block), following
+        if index + 1 < model_width // block:
+            following = product(index + 1)
+        flat = latents_ref[:, :, cols].reshape(rows, block).astype(jnp.float32)
+        velocity = (begun_ref[:, cols] if chunks > 1 else flat) + projected
         clean_ref[:, cols] = (flat - sigma * velocity).astype(jnp.bfloat16)
         stepped_ref[:, :, cols] = (
-            (flat - velocity * (1.0 / STEPS))
-            .astype(jnp.bfloat16)
-            .reshape(particles, tokens, out_weights.block)
+            (flat - velocity * (1.0 / STEPS)).astype(jnp.bfloat16).reshape(particles, tokens, block)
         )
 
     for index in range(parts):
@@ -396,19 +399,27 @@
             rows_ref[step * rows : (step + 1) * rows, index * depth : (index + 1) * depth] = (
                 features_ref[(group + parts - index) % parts]
             )
-    totals = jnp.zeros((doms * particles, joined * columns), jnp.float32)
-    for step in range(count // joined):
+    def product(step):
         for copy in copies[step * joined * parts : (step + 1) * joined * parts]:
             copy.wait()
-        hidden = jnp.dot(rows_ref[...], weight_vmem[step], preferred_element_type=jnp.float32)
-        head = jnp.concatenate(
+        return jnp.dot(rows_ref[...], weight_vmem[step], preferred_element_type=jnp.float32)
+
+    linear, cubic = math.sqrt(2.0 / math.pi), math.sqrt(2.0 / math.pi) * 0.044715
+    totals = jnp.zeros((doms * particles, joined * columns), jnp.float32)
+    following = product(0)
+    for step in range(count // joined):
+        hidden = following
+        if step + 1 < count // joined:
+            following = product(step + 1)
+        half_head = 0.5 * jnp.concatenate(
             [
                 head_ref[(seq ^ offset) * doms + dom]
                 for offset in offsets[step * joined : (step + 1) * joined]
             ],
             axis=1,
         )
-        scored = jax.nn.gelu(hidden) * head
+        bent = jnp.tanh(hidden * (linear + cubic * (hidden * hidden)))
+        scored = (hidden + hidden * bent) * half_head
         totals += jnp.sum(scored.reshape(doms * particles, rows // particles, -1), axis=1)
 
     sums = jnp.sum(totals, axis=1, keepdims=True) * scale

time: 164 us -> 164 us (level)
  no operation moved by 1% of the time
where the time goes in v16:
time: 164 us; the launch traced here: 163 us
  waiting for transfers between devices  59.3 us (36%)
  starting transfers between devices  53.2 us (32%)
  Pallas kernels  38.5 us (23%)
  local copies, waits for them, and re-layouts  7.57 us (5%)
  other arithmetic  3.3 us (2%)
    ppermute x10, waiting for transfers between devices, swapped(): lax.ppermute(array, axis, [(i, i ^ bit) for i in range(lax.axis_size(axis...  47.4 us
    all_to_all x4, starting transfers between devices, exchange(): return lax.all_to_all(array, 'seq', 0, 0, tiled=True)  20.6 us
    ppermute x10, starting transfers between devices, swapped(): lax.ppermute(array, axis, [(i, i ^ bit) for i in range(lax.axis_size(axis...  19.8 us
    pallas_call x2, Pallas kernels, attention(): pl.pallas_call(functools.partial(attention_kernel, head_width, block_sour...  11 us
    pallas_call x1, Pallas kernels, project_embed(): pl.pallas_call(kernel, in_specs=[smem, hbm, vmem, hbm] + ([] if begun is...  8.86 us
    pallas_call x1, Pallas kernels, reward(): pl.pallas_call(functools.partial(reward_kernel, particles, scale, parts,...  7.42 us
    ppermute x10, waiting for transfers between devices, shifted(): lax.ppermute(array, axis, [(i, (i + step) % count) for i in range(count)])  7.15 us
    ppermute x10, starting transfers between devices, shifted(): lax.ppermute(array, axis, [(i, (i + step) % count) for i in range(count)])  7.02 us
  transfers between devices with their start and end apart: 25, of which 12 were waited for; matrix products, arithmetic and copies ran while one was open for 3% of the time, Pallas kernels for 17%

profile of v16, /device:TPU:0, one launch (start us, length us, event | category | flops | bytes accessed | tf_op | source)
XLA Modules:
  0.0 163.4 jit_solution(5783295774430507832)
XLA Ops:
  1.6 4.0 %collective-permute-start = (bf16[1,192,256]{2,1,0:T(8,128)(2,1)S(1)}, bf16[1,192,256]{2,1,0:T(8,128)(2,1)S(1)}, u32[]{:S(2)}, u32[]{:S(2)}) collective-permute-start(bf16[1,192,256]{2,1,0:T(8,128)(2,1)S(1)} %dynamic-slice_bitcast_fusion.1), channel_id=1, source_target_pairs={{0,4},{1,5},{2,6},{3,7},{4,0},{5,1},{6,2},{7,3},{8,12},{9,13},{10,... | collective-permute-start | bytes 294920 | tf_op jit(solution)/shard_map/ppermute | solution.py:536
  5.7 3.2 %pack_heads.1 = (bf16[8,3,64,384]{3,2,1,0:T(8,128)(2,1)}, bf16[8,3,64,384]{3,2,1,0:T(8,128)(2,1)}) custom-call(bf16[4,64,1536]{2,1,0:T(8,128)(2,1)} %q_ref.1, bf16[4,64,1536]{2,1,0:T(8,128)(2,1)} %k_ref.1, bf16[4,64,1536]{2,1,0:T(8,128)(2,1)} %v_ref.1), custom_call_target="tpu_custom_call" | custom-call | tf_op jit(solution)/shard_map/pack_heads/pallas_call | solution.py:40
  8.9 1.7 %collective-permute-done = bf16[1,192,256]{2,1,0:T(8,128)(2,1)S(1)} collective-permute-done((bf16[1,192,256]{2,1,0:T(8,128)(2,1)S(1)}, bf16[1,192,256]{2,1,0:T(8,128)(2,1)S(1)}, u32[]{:S(2)}, u32[]{:S(2)}) %collective-permute-start) | collective-permute-done | bytes 98336 | tf_op jit(solution)/shard_map/ppermute | solution.py:536
  11.3 5.9 %all-to-all-start = ((bf16[8,3,64,384]{3,2,1,0:T(8,128)(2,1)}), bf16[8,3,64,384]{3,2,1,0:T(8,128)(2,1)S(1)}, u32[]{:S(2)}, u32[]{:S(2)}) async-start(bf16[8,3,64,384]{3,2,1,0:T(8,128)(2,1)} %gate.4), calls=%async_computation | async-start | bytes 2359296 | tf_op jit(solution)/shard_map/all_to_all | solution.py:540
  17.2 2.0 %collective-permute-start.6 = (bf16[2,192,256]{2,1,0:T(8,128)(2,1)S(1)}, bf16[2,192,256]{2,1,0:T(8,128)(2,1)S(1)}, u32[]{:S(2)}, u32[]{:S(2)}) collective-permute-start(bf16[2,192,256]{2,1,0:T(8,128)(2,1)S(1)} %copy-done.10), channel_id=1, source_target_pairs={{0,2},{1,3},{2,0},{3,1},{4,6},{5,7},{6,4},{7,5},{8,10},{9,11},{10,... | collective-permute-start | bytes 589832 | tf_op jit(solution)/shard_map/ppermute | solution.py:536
  19.2 22.1 %collective-permute-done.6 = bf16[2,192,256]{2,1,0:T(8,128)(2,1)S(1)} collective-permute-done((bf16[2,192,256]{2,1,0:T(8,128)(2,1)S(1)}, bf16[2,192,256]{2,1,0:T(8,128)(2,1)S(1)}, u32[]{:S(2)}, u32[]{:S(2)}) %collective-permute-start.6) | collective-permute-done | bytes 196640 | tf_op jit(solution)/shard_map/ppermute | solution.py:536
  42.6 4.4 %collective-permute-start.1 = (bf16[1,512,256]{2,1,0:T(8,128)(2,1)S(1)}, bf16[1,512,256]{2,1,0:T(8,128)(2,1)S(1)}, u32[]{:S(2)}, u32[]{:S(2)}) collective-permute-start(bf16[1,512,256]{2,1,0:T(8,128)(2,1)S(1)} %dynamic-slice_bitcast_fusion.refs_5_), channel_id=1, source_target_pairs={{0,4},{1,5},{2,6},{3,7},{4,0},{5,1},{6,2},{7,3},{8,12},{9,13},{10,... | collective-permute-start | bytes 786440 | tf_op jit(solution)/shard_map/ppermute | solution.py:536
  47.6 1.5 collective-permute-start.10
  49.1 4.5 %collective-permute-done.7 = bf16[4,192,256]{2,1,0:T(8,128)(2,1)} collective-permute-done((bf16[4,192,256]{2,1,0:T(8,128)(2,1)S(1)}, bf16[4,192,256]{2,1,0:T(8,128)(2,1)}, u32[]{:S(2)}, u32[]{:S(2)}) %collective-permute-start.7) | collective-permute-done | bytes 393248 | tf_op jit(solution)/shard_map/ppermute | solution.py:536
  53.6 2.0 %pad_maximum_fusion.refs_1_.refs_6_ = bf16[8,192,256]{2,1,0:T(8,128)(2,1)} fusion(bf16[4,192,256]{2,1,0:T(8,128)(2,1)} %collective-permute-done.7, bf16[2,192,256]{2,1,0:T(8,128)(2,1)S(1)} %collective-permute-done.6, bf16[1,192,256]{2,1,0:T(8,128)(2,1)S(1)} %collective-permute-done, bf16[1,192,256]{2,1,0:T(8,128)(2,1)S(1)} %dynamic-slice_bitcast_fusion.1), kind=kLoop, calls=%fused_computation | loop fusion | flops 1179648 | bytes 1572864 | tf_op jit(solution)/shard_map/concatenate | solution.py:599
  55.6 2.3 %collective-permute-done.1.refs_2_ = bf16[1,512,256]{2,1,0:T(8,128)(2,1)S(1)} collective-permute-done((bf16[1,512,256]{2,1,0:T(8,128)(2,1)S(1)}, bf16[1,512,256]{2,1,0:T(8,128)(2,1)S(1)}, u32[]{:S(2)}, u32[]{:S(2)}) %collective-permute-start.1) | collective-permute-done | bytes 262176 | tf_op jit(solution)/shard_map/ppermute | solution.py:536
  57.9 2.6 %collective-permute-done.3.refs_3_ = bf16[1,512,256]{2,1,0:T(8,128)(2,1)S(1)} collective-permute-done((bf16[1,512,256]{2,1,0:T(8,128)(2,1)S(1)}, bf16[1,512,256]{2,1,0:T(8,128)(2,1)S(1)}, u32[]{:S(2)}, u32[]{:S(2)}) %collective-permute-start.3) | collective-permute-done | bytes 262176 | tf_op jit(solution)/shard_map/ppermute | solution.py:536
  61.1 3.6 %all-to-all-start.2 = ((bf16[8,3,64,384]{3,2,1,0:T(8,128)(2,1)}), bf16[8,3,64,384]{3,2,1,0:T(8,128)(2,1)S(1)}, u32[]{:S(2)}, u32[]{:S(2)}) async-start(bf16[8,3,64,384]{3,2,1,0:T(8,128)(2,1)} %gate.6), calls=%async_computation.2 | async-start | bytes 2359296 | tf_op jit(solution)/shard_map/all_to_all | solution.py:540
  67.6 2.1 %collective-permute-start.4 = (bf16[2,512,256]{2,1,0:T(8,128)(2,1)S(1)}, bf16[2,512,256]{2,1,0:T(8,128)(2,1)S(1)}, u32[]{:S(2)}, u32[]{:S(2)}) collective-permute-start(bf16[2,512,256]{2,1,0:T(8,128)(2,1)S(1)} %constant_dynamic-update-slice_fusion.refs_9_), channel_id=1, source_target_pairs={{0,1},{1,0},{2,3},{3,2},{4,5},{5,4},{6,7},{7,6},{8,9},{9,8},{10,11... | collective-permute-start | bytes 1572872 | tf_op jit(solution)/shard_map/ppermute | solution.py:536
  70.7 1.5 collective-permute-start.2
  72.1 5.5 %attention.2.refs_0_ = bf16[8,64,384]{2,1,0:T(8,128)(2,1)S(1)} custom-call(bf16[8,3,64,384]{3,2,1,0:T(8,128)(2,1)S(1)} %all-to-all-done.qkv_ref), custom_call_target="tpu_custom_call" | custom-call | flops 402653184 | bytes 1572864 | tf_op jit(solution)/shard_map/attention/pallas_call | solution.py:104
  78.4 9.8 %collective-permute-done.2.refs_1_.refs_13_ = bf16[1,512,256]{2,1,0:T(8,128)(2,1)} collective-permute-done((bf16[1,512,256]{2,1,0:T(8,128)(2,1)}, bf16[1,512,256]{2,1,0:T(8,128)(2,1)}, u32[]{:S(2)}, u32[]{:S(2)}) %collective-permute-start.2) | collective-permute-done | bytes 262176 | tf_op jit(solution)/shard_map/ppermute | solution.py:536
  88.2 1.6 collective-permute-done.4.refs_2_.refs_11_
  89.8 4.1 %collective-permute-done.5.refs_3_.refs_10_ = bf16[2,512,256]{2,1,0:T(8,128)(2,1)} collective-permute-done((bf16[2,512,256]{2,1,0:T(8,128)(2,1)S(1)}, bf16[2,512,256]{2,1,0:T(8,128)(2,1)}, u32[]{:S(2)}, u32[]{:S(2)}) %collective-permute-start.5) | collective-permute-done | bytes 524320 | tf_op jit(solution)/shard_map/ppermute | solution.py:532
  94.0 5.6 %all-to-all-start.1 = ((bf16[8,64,384]{2,1,0:T(8,128)(2,1)}), bf16[8,64,384]{2,1,0:T(8,128)(2,1)}, u32[]{:S(2)}, u32[]{:S(2)}) async-start(bf16[8,64,384]{2,1,0:T(8,128)(2,1)} %gate.5), calls=%async_computation.1 | async-start | bytes 786432 | tf_op jit(solution)/shard_map/all_to_all | solution.py:540
  101.6 2.0 %collective-permute-start.11 = (bf16[1,512,256]{2,1,0:T(8,128)(2,1)}, bf16[1,512,256]{2,1,0:T(8,128)(2,1)}, u32[]{:S(2)}, u32[]{:S(2)}) collective-permute-start(bf16[1,512,256]{2,1,0:T(8,128)(2,1)} %collective-permute-done.2.refs_1_.refs_13_), channel_id=1, source_target_pairs={{0,1},{1,0},{2,3},{3,2},{4,5},{5,4},{6,7},{7,6},{8,9},{9,8},{10,11... | collective-permute-start | bytes 786440 | tf_op jit(solution)/shard_map/ppermute | solution.py:536
  104.1 5.5 %attention.3.refs_0_ = bf16[8,64,384]{2,1,0:T(8,128)(2,1)S(1)} custom-call(bf16[8,3,64,384]{3,2,1,0:T(8,128)(2,1)S(1)} %all-to-all-done.2.qkv_ref), custom_call_target="tpu_custom_call" | custom-call | flops 402653184 | bytes 1572864 | tf_op jit(solution)/shard_map/attention/pallas_call | solution.py:104
  111.2 5.6 %all-to-all-start.3 = ((bf16[8,64,384]{2,1,0:T(8,128)(2,1)}), bf16[8,64,384]{2,1,0:T(8,128)(2,1)S(1)}, u32[]{:S(2)}, u32[]{:S(2)}) async-start(bf16[8,64,384]{2,1,0:T(8,128)(2,1)} %gate.7), calls=%async_computation.3 | async-start | bytes 786432 | tf_op jit(solution)/shard_map/all_to_all | solution.py:540
  117.2 2.0 %collective-permute-start.17 = (bf16[1,512,256]{2,1,0:T(8,128)(2,1)}, bf16[1,512,256]{2,1,0:T(8,128)(2,1)S(1)}, u32[]{:S(2)}, u32[]{:S(2)}) collective-permute-start(bf16[1,512,256]{2,1,0:T(8,128)(2,1)} %copy-done.17), channel_id=1, source_target_pairs={{0,1},{1,0},{2,3},{3,2},{4,5},{5,4},{6,7},{7,6},{8,9},{9,8},{10,11... | collective-permute-start | bytes 786440 | tf_op jit(solution)/shard_map/ppermute | solution.py:536
  120.5 4.7 %first_project.1.refs_4_ = f32[256,1536]{1,0:T(8,128)} custom-call(bf16[4,64,1536]{2,1,0:T(8,128)(2,1)} %refs_1_.2, bf16[1536,1536]{1,0:T(8,128)(2,1)} %refs_3_.1, bf16[8,64,384]{2,1,0:T(8,128)(2,1)} %all-to-all-done.1.piece_ref), custom_call_target="tpu_custom_call" | custom-call | flops 603979776 | bytes 5505024 | tf_op jit(solution)/shard_map/first_project/pallas_call | solution.py:181
  125.2 2.9 %collective-permute-done.17.refs_11_.refs_16_ = bf16[1,512,256]{2,1,0:T(8,128)(2,1)S(1)} collective-permute-done((bf16[1,512,256]{2,1,0:T(8,128)(2,1)}, bf16[1,512,256]{2,1,0:T(8,128)(2,1)S(1)}, u32[]{:S(2)}, u32[]{:S(2)}) %collective-permute-start.17) | collective-permute-done | bytes 262176 | tf_op jit(solution)/shard_map/ppermute | solution.py:536
  130.3 8.9 %project_embed.1 = (bf16[4,64,1536]{2,1,0:T(8,128)(2,1)}, bf16[2,256,512]{2,1,0:T(8,128)(2,1)}) custom-call(s32[4]{0:T(128)} %pad_add_fusion.refs_0_.ids_ref, bf16[4,64,1536]{2,1,0:T(8,128)(2,1)} %refs_1_.2, f32[1,1024]{1,0:T(1,128)} %bitcast.10, bf16[1536,1536]{1,0:T(8,128)(2,1)} %refs_3_.1, f32[256,1536]{1,0:T(8,128)} %first_project.1.refs_4_, ...), custom_call_target="tpu_custom_call" | custom-call | flops 1409286144 | bytes 10223616 | tf_op jit(solution)/shard_map/project_embed/pallas_call | solution.py:334
  139.7 1.6 collective-permute-done.19.refs_4_
  142.1 7.4 %reward.1 = f32[16,8,128]{2,1,0:T(8,128)} custom-call(s32[4]{0:T(128)} %pad_add_fusion.refs_0_.ids_ref, f32[4]{0:T(128)} %refs_1_.3, f32[16,1,256]{2,1,0:T(1,128)} %bitcast.11, bf16[2,256,512]{2,1,0:T(8,128)(2,1)} %get-tuple-element.11.refs_3_, bf16[2,256,512]{2,1,0:T(8,128)(2,1)} %copy-done.19, bf16[1,512,256]{2,1,0:T(8,128)(2,1)} %copy-done.15, ...), custom_call_target="tpu_custom_call" | custom-call | flops 2147483648 | bytes 4194304 | tf_op jit(solution)/shard_map/reward/pallas_call | solution.py:447
  149.5 5.8 %all-to-all-start.4 = ((f32[16,8,128]{2,1,0:T(8,128)}), f32[16,8,128]{2,1,0:T(8,128)S(1)}, u32[]{:S(2)}, u32[]{:S(2)}) async-start(f32[16,8,128]{2,1,0:T(8,128)} %reward.1), calls=%async_computation.4 | async-start | bytes 131072 | tf_op jit(solution)/shard_map/all_to_all | solution.py:669
  155.4 2.0 %resample.1.resampled_ref = bf16[4,64,1536]{2,1,0:T(8,128)(2,1)} custom-call(s32[4]{0:T(128)S(1)} %copy-done.4, s32[4]{0:T(128)S(1)} %copy-done.5, bf16[4,64,1536]{2,1,0:T(8,128)(2,1)S(1)} %copy-done.3, bf16[4,64,1536]{2,1,0:T(8,128)(2,1)S(1)} %collective-permute-done.18.other_ref), custom_call_target="tpu_custom_call" | custom-call | tf_op jit(solution)/shard_map/resample/pallas_call | solution.py:516
  157.4 4.7 %all-to-all-done.4.parts_ref = f32[16,8,128]{2,1,0:T(8,128)S(1)} async-done(((f32[16,8,128]{2,1,0:T(8,128)}), f32[16,8,128]{2,1,0:T(8,128)S(1)}, u32[]{:S(2)}, u32[]{:S(2)}) %all-to-all-start.4) | async-done | bytes 65568 | tf_op jit(solution)/shard_map/all_to_all | solution.py:669
  (78 shorter events, 18.9 us)
Async XLA Ops:
  0.6 42.0 %copy-start = (bf16[1024,512]{1,0:T(8,128)(2,1)S(1)}, bf16[1024,512]{1,0:T(8,128)(2,1)}, u32[]{:S(2)}) copy-start(bf16[1024,512]{1,0:T(8,128)(2,1)} %param.20) | copy-start | bytes 3145732
  1.6 8.9 %collective-permute-start = (bf16[1,192,256]{2,1,0:T(8,128)(2,1)S(1)}, bf16[1,192,256]{2,1,0:T(8,128)(2,1)S(1)}, u32[]{:S(2)}, u32[]{:S(2)}) collective-permute-start(bf16[1,192,256]{2,1,0:T(8,128)(2,1)S(1)} %dynamic-slice_bitcast_fusion.1), channel_id=1, source_target_pairs={{0,4},{1,5},{2,6},{3,7},{4,0},{5,1},{6,2},{7,3},{8,12},{9,13},{10,... | collective-permute-start | bytes 294920 | tf_op jit(solution)/shard_map/ppermute | solution.py:536
  11.3 49.9 %all-to-all-start = ((bf16[8,3,64,384]{3,2,1,0:T(8,128)(2,1)}), bf16[8,3,64,384]{3,2,1,0:T(8,128)(2,1)S(1)}, u32[]{:S(2)}, u32[]{:S(2)}) async-start(bf16[8,3,64,384]{3,2,1,0:T(8,128)(2,1)} %gate.4), calls=%async_computation | async-start | bytes 2359296 | tf_op jit(solution)/shard_map/all_to_all | solution.py:540
  17.2 24.2 %collective-permute-start.6 = (bf16[2,192,256]{2,1,0:T(8,128)(2,1)S(1)}, bf16[2,192,256]{2,1,0:T(8,128)(2,1)S(1)}, u32[]{:S(2)}, u32[]{:S(2)}) collective-permute-start(bf16[2,192,256]{2,1,0:T(8,128)(2,1)S(1)} %copy-done.10), channel_id=1, source_target_pairs={{0,2},{1,3},{2,0},{3,1},{4,6},{5,7},{6,4},{7,5},{8,10},{9,11},{10,... | collective-permute-start | bytes 589832 | tf_op jit(solution)/shard_map/ppermute | solution.py:536
  41.4 12.2 %collective-permute-start.7 = (bf16[4,192,256]{2,1,0:T(8,128)(2,1)S(1)}, bf16[4,192,256]{2,1,0:T(8,128)(2,1)}, u32[]{:S(2)}, u32[]{:S(2)}) collective-permute-start(bf16[4,192,256]{2,1,0:T(8,128)(2,1)S(1)} %pad_maximum_fusion.1), channel_id=1, source_target_pairs={{0,1},{1,0},{2,3},{3,2},{4,5},{5,4},{6,7},{7,6},{8,9},{9,8},{10,11... | collective-permute-start | bytes 1179656 | tf_op jit(solution)/shard_map/ppermute | solution.py:536
  42.6 17.8 %copy-start.15 = (bf16[1,512,256]{2,1,0:T(8,128)(2,1)}, bf16[1,512,256]{2,1,0:T(8,128)(2,1)S(1)}, u32[]{:S(2)}) copy-start(bf16[1,512,256]{2,1,0:T(8,128)(2,1)S(1)} %dynamic-slice_bitcast_fusion.refs_5_) | copy-start | bytes 786436
  42.6 15.2 %collective-permute-start.1 = (bf16[1,512,256]{2,1,0:T(8,128)(2,1)S(1)}, bf16[1,512,256]{2,1,0:T(8,128)(2,1)S(1)}, u32[]{:S(2)}, u32[]{:S(2)}) collective-permute-start(bf16[1,512,256]{2,1,0:T(8,128)(2,1)S(1)} %dynamic-slice_bitcast_fusion.refs_5_), channel_id=1, source_target_pairs={{0,4},{1,5},{2,6},{3,7},{4,0},{5,1},{6,2},{7,3},{8,12},{9,13},{10,... | collective-permute-start | bytes 786440 | tf_op jit(solution)/shard_map/ppermute | solution.py:536
  47.0 10.8 %collective-permute-start.9 = (bf16[1,512,256]{2,1,0:T(8,128)(2,1)S(1)}, bf16[1,512,256]{2,1,0:T(8,128)(2,1)}, u32[]{:S(2)}, u32[]{:S(2)}) collective-permute-start(bf16[1,512,256]{2,1,0:T(8,128)(2,1)S(1)} %dynamic-slice_bitcast_fusion.refs_5_), channel_id=1, source_target_pairs={{0,1},{1,0},{2,3},{3,2},{4,5},{5,4},{6,7},{7,6},{8,9},{9,8},{10,11... | collective-permute-start | bytes 786440 | tf_op jit(solution)/shard_map/ppermute | solution.py:536
  47.6 10.2 %collective-permute-start.10 = (bf16[1,512,256]{2,1,0:T(8,128)(2,1)S(1)}, bf16[1,512,256]{2,1,0:T(8,128)(2,1)S(1)}, u32[]{:S(2)}, u32[]{:S(2)}) collective-permute-start(bf16[1,512,256]{2,1,0:T(8,128)(2,1)S(1)} %dynamic-slice_bitcast_fusion.refs_5_), channel_id=1, source_target_pairs={{0,16},{16,0},{1,17},{17,1},{2,18},{18,2},{3,19},{19,3},{4,20},{20... | collective-permute-start | bytes 786440 | tf_op jit(solution)/shard_map/ppermute | solution.py:532
  49.1 11.3 %collective-permute-start.3 = (bf16[1,512,256]{2,1,0:T(8,128)(2,1)S(1)}, bf16[1,512,256]{2,1,0:T(8,128)(2,1)S(1)}, u32[]{:S(2)}, u32[]{:S(2)}) collective-permute-start(bf16[1,512,256]{2,1,0:T(8,128)(2,1)S(1)} %dynamic-slice_bitcast_fusion.refs_5_), channel_id=1, source_target_pairs={{0,2},{1,3},{2,0},{3,1},{4,6},{5,7},{6,4},{7,5},{8,10},{9,11},{10,... | collective-permute-start | bytes 786440 | tf_op jit(solution)/shard_map/ppermute | solution.py:536
  61.1 32.8 %all-to-all-start.2 = ((bf16[8,3,64,384]{3,2,1,0:T(8,128)(2,1)}), bf16[8,3,64,384]{3,2,1,0:T(8,128)(2,1)S(1)}, u32[]{:S(2)}, u32[]{:S(2)}) async-start(bf16[8,3,64,384]{3,2,1,0:T(8,128)(2,1)} %gate.6), calls=%async_computation.2 | async-start | bytes 2359296 | tf_op jit(solution)/shard_map/all_to_all | solution.py:540
  64.7 29.2 %collective-permute-start.8 = (bf16[8,192,256]{2,1,0:T(8,128)(2,1)}, bf16[8,192,256]{2,1,0:T(8,128)(2,1)}, u32[]{:S(2)}, u32[]{:S(2)}) collective-permute-start(bf16[8,192,256]{2,1,0:T(8,128)(2,1)} %pad_maximum_fusion.refs_1_.refs_6_), channel_id=1, source_target_pairs={{0,16},{16,0},{1,17},{17,1},{2,18},{18,2},{3,19},{19,3},{4,20},{20... | collective-permute-start | bytes 2359304 | tf_op jit(solution)/shard_map/ppermute | solution.py:532
  67.5 10.1 %copy-start.18 = (bf16[2,512,256]{2,1,0:T(8,128)(2,1)}, bf16[2,512,256]{2,1,0:T(8,128)(2,1)S(1)}, u32[]{:S(2)}) copy-start(bf16[2,512,256]{2,1,0:T(8,128)(2,1)S(1)} %constant_dynamic-update-slice_fusion.refs_9_) | copy-start | bytes 1572868
  67.6 22.2 %collective-permute-start.4 = (bf16[2,512,256]{2,1,0:T(8,128)(2,1)S(1)}, bf16[2,512,256]{2,1,0:T(8,128)(2,1)S(1)}, u32[]{:S(2)}, u32[]{:S(2)}) collective-permute-start(bf16[2,512,256]{2,1,0:T(8,128)(2,1)S(1)} %constant_dynamic-update-slice_fusion.refs_9_), channel_id=1, source_target_pairs={{0,1},{1,0},{2,3},{3,2},{4,5},{5,4},{6,7},{7,6},{8,9},{9,8},{10,11... | collective-permute-start | bytes 1572872 | tf_op jit(solution)/shard_map/ppermute | solution.py:536
  69.6 24.3 %collective-permute-start.5 = (bf16[2,512,256]{2,1,0:T(8,128)(2,1)S(1)}, bf16[2,512,256]{2,1,0:T(8,128)(2,1)}, u32[]{:S(2)}, u32[]{:S(2)}) collective-permute-start(bf16[2,512,256]{2,1,0:T(8,128)(2,1)S(1)} %constant_dynamic-update-slice_fusion.refs_9_), channel_id=1, source_target_pairs={{0,16},{16,0},{1,17},{17,1},{2,18},{18,2},{3,19},{19,3},{4,20},{20... | collective-permute-start | bytes 1572872 | tf_op jit(solution)/shard_map/ppermute | solution.py:532
  70.7 17.6 %collective-permute-start.2 = (bf16[1,512,256]{2,1,0:T(8,128)(2,1)}, bf16[1,512,256]{2,1,0:T(8,128)(2,1)}, u32[]{:S(2)}, u32[]{:S(2)}) collective-permute-start(bf16[1,512,256]{2,1,0:T(8,128)(2,1)} %copy-done.8), channel_id=1, source_target_pairs={{0,2},{1,3},{2,0},{3,1},{4,6},{5,7},{6,4},{7,5},{8,10},{9,11},{10,... | collective-permute-start | bytes 786440 | tf_op jit(solution)/shard_map/ppermute | solution.py:536
  78.4 25.2 %copy-start.6 = (bf16[8,192,256]{2,1,0:T(8,128)(2,1)S(1)}, bf16[8,192,256]{2,1,0:T(8,128)(2,1)}, u32[]{:S(2)}) copy-start(bf16[8,192,256]{2,1,0:T(8,128)(2,1)} %pad_maximum_fusion.refs_1_.refs_6_) | copy-start | bytes 2359300
  94.0 17.2 %all-to-all-start.1 = ((bf16[8,64,384]{2,1,0:T(8,128)(2,1)}), bf16[8,64,384]{2,1,0:T(8,128)(2,1)}, u32[]{:S(2)}, u32[]{:S(2)}) async-start(bf16[8,64,384]{2,1,0:T(8,128)(2,1)} %gate.5), calls=%async_computation.1 | async-start | bytes 786432 | tf_op jit(solution)/shard_map/all_to_all | solution.py:540
  99.6 10.8 %collective-permute-start.13 = (bf16[1,512,256]{2,1,0:T(8,128)(2,1)}, bf16[1,512,256]{2,1,0:T(8,128)(2,1)S(1)}, u32[]{:S(2)}, u32[]{:S(2)}) collective-permute-start(bf16[1,512,256]{2,1,0:T(8,128)(2,1)} %collective-permute-done.9.refs_4_.refs_7_), channel_id=1, source_target_pairs={{0,16},{16,0},{1,17},{17,1},{2,18},{18,2},{3,19},{19,3},{4,20},{20... | collective-permute-start | bytes 786440 | tf_op jit(solution)/shard_map/ppermute | solution.py:532
  100.3 10.1 %collective-permute-start.12 = (bf16[1,512,256]{2,1,0:T(8,128)(2,1)}, bf16[1,512,256]{2,1,0:T(8,128)(2,1)S(1)}, u32[]{:S(2)}, u32[]{:S(2)}) collective-permute-start(bf16[1,512,256]{2,1,0:T(8,128)(2,1)} %collective-permute-done.2.refs_1_.refs_13_), channel_id=1, source_target_pairs={{0,16},{16,0},{1,17},{17,1},{2,18},{18,2},{3,19},{19,3},{4,20},{20... | collective-permute-start | bytes 786440 | tf_op jit(solution)/shard_map/ppermute | solution.py:532
  101.6 8.8 %collective-permute-start.11 = (bf16[1,512,256]{2,1,0:T(8,128)(2,1)}, bf16[1,512,256]{2,1,0:T(8,128)(2,1)}, u32[]{:S(2)}, u32[]{:S(2)}) collective-permute-start(bf16[1,512,256]{2,1,0:T(8,128)(2,1)} %collective-permute-done.2.refs_1_.refs_13_), channel_id=1, source_target_pairs={{0,1},{1,0},{2,3},{3,2},{4,5},{5,4},{6,7},{7,6},{8,9},{9,8},{10,11... | collective-permute-start | bytes 786440 | tf_op jit(solution)/shard_map/ppermute | solution.py:536
  103.6 25.8 %collective-permute-start.14 = (bf16[8,192,256]{2,1,0:T(8,128)(2,1)S(1)}, bf16[8,192,256]{2,1,0:T(8,128)(2,1)}, u32[]{:S(2)}, u32[]{:S(2)}) collective-permute-start(bf16[8,192,256]{2,1,0:T(8,128)(2,1)S(1)} %copy-done.6), channel_id=1, source_target_pairs={{0,8},{8,0},{1,9},{9,1},{2,10},{10,2},{3,11},{11,3},{4,12},{12,4},... | collective-permute-start | bytes 2359304 | tf_op jit(solution)/shard_map/ppermute | solution.py:532
  103.6 25.8 %collective-permute-start.15 = (bf16[8,192,256]{2,1,0:T(8,128)(2,1)}, bf16[8,192,256]{2,1,0:T(8,128)(2,1)}, u32[]{:S(2)}, u32[]{:S(2)}) collective-permute-start(bf16[8,192,256]{2,1,0:T(8,128)(2,1)} %collective-permute-done.8.refs_4_.refs_7_), channel_id=1, source_target_pairs={{0,8},{8,0},{1,9},{9,1},{2,10},{10,2},{3,11},{11,3},{4,12},{12,4},... | collective-permute-start | bytes 2359304 | tf_op jit(solution)/shard_map/ppermute | solution.py:532
  111.2 18.3 %all-to-all-start.3 = ((bf16[8,64,384]{2,1,0:T(8,128)(2,1)}), bf16[8,64,384]{2,1,0:T(8,128)(2,1)S(1)}, u32[]{:S(2)}, u32[]{:S(2)}) async-start(bf16[8,64,384]{2,1,0:T(8,128)(2,1)} %gate.7), calls=%async_computation.3 | async-start | bytes 786432 | tf_op jit(solution)/shard_map/all_to_all | solution.py:540
  116.7 12.7 %collective-permute-start.16 = (bf16[2,512,256]{2,1,0:T(8,128)(2,1)S(1)}, bf16[2,512,256]{2,1,0:T(8,128)(2,1)}, u32[]{:S(2)}, u32[]{:S(2)}) collective-permute-start(bf16[2,512,256]{2,1,0:T(8,128)(2,1)S(1)} %copy-done.12), channel_id=1, source_target_pairs={{0,16},{16,0},{1,17},{17,1},{2,18},{18,2},{3,19},{19,3},{4,20},{20... | collective-permute-start | bytes 1572872 | tf_op jit(solution)/shard_map/ppermute | solution.py:532
  117.2 10.8 %collective-permute-start.17 = (bf16[1,512,256]{2,1,0:T(8,128)(2,1)}, bf16[1,512,256]{2,1,0:T(8,128)(2,1)S(1)}, u32[]{:S(2)}, u32[]{:S(2)}) collective-permute-start(bf16[1,512,256]{2,1,0:T(8,128)(2,1)} %copy-done.17), channel_id=1, source_target_pairs={{0,1},{1,0},{2,3},{3,2},{4,5},{5,4},{6,7},{7,6},{8,9},{9,8},{10,11... | collective-permute-start | bytes 786440 | tf_op jit(solution)/shard_map/ppermute | solution.py:536
  139.1 2.2 %collective-permute-start.19 = (bf16[2,256,512]{2,1,0:T(8,128)(2,1)}, bf16[2,256,512]{2,1,0:T(8,128)(2,1)S(1)}, u32[]{:S(2)}, u32[]{:S(2)}) collective-permute-start(bf16[2,256,512]{2,1,0:T(8,128)(2,1)} %get-tuple-element.11.refs_3_), channel_id=1, source_target_pairs={{0,8},{8,0},{1,9},{9,1},{2,10},{10,2},{3,11},{11,3},{4,12},{12,4},... | collective-permute-start | bytes 1572872 | tf_op jit(solution)/shard_map/ppermute | solution.py:532
  139.2 16.1 %collective-permute-start.18 = (bf16[4,64,1536]{2,1,0:T(8,128)(2,1)}, bf16[4,64,1536]{2,1,0:T(8,128)(2,1)S(1)}, u32[]{:S(2)}, u32[]{:S(2)}) collective-permute-start(bf16[4,64,1536]{2,1,0:T(8,128)(2,1)} %get-tuple-element.10.own_ref), channel_id=1, source_target_pairs={{0,8},{8,0},{1,9},{9,1},{2,10},{10,2},{3,11},{11,3},{4,12},{12,4},... | collective-permute-start | bytes 2359304 | tf_op jit(solution)/shard_map/ppermute | solution.py:532
  142.1 13.2 %copy-start.3 = (bf16[4,64,1536]{2,1,0:T(8,128)(2,1)S(1)}, bf16[4,64,1536]{2,1,0:T(8,128)(2,1)}, u32[]{:S(2)}) copy-start(bf16[4,64,1536]{2,1,0:T(8,128)(2,1)} %get-tuple-element.10.own_ref) | copy-start | bytes 2359300
  142.1 13.2 %copy-start.4 = (s32[4]{0:T(128)S(1)}, s32[4]{0:T(128)}, u32[]{:S(2)}) copy-start(s32[4]{0:T(128)} %pad_add_fusion.refs_0_.ids_ref) | copy-start | bytes 52
  142.1 13.2 %copy-start.5 = (s32[4]{0:T(128)S(1)}, s32[4]{0:T(128)}, u32[]{:S(2)}) copy-start(s32[4]{0:T(128)} %ancestors_ref.1) | copy-start | bytes 52
  149.5 12.5 %all-to-all-start.4 = ((f32[16,8,128]{2,1,0:T(8,128)}), f32[16,8,128]{2,1,0:T(8,128)S(1)}, u32[]{:S(2)}, u32[]{:S(2)}) async-start(f32[16,8,128]{2,1,0:T(8,128)} %reward.1), calls=%async_computation.4 | async-start | bytes 131072 | tf_op jit(solution)/shard_map/all_to_all | solution.py:669
  (13 other events, 28.4 us)

commit v17 on v14

--- a/solution.py
+++ b/solution.py
@@ -430,7 +430,7 @@
     _, depth, columns = weights[0].shape
     rows, doms = features[0].shape[1], len(features)
     count = len(offsets)
-    joined = 2 if columns % LANES == 0 and count % 2 == 0 else 1
+    joined = 1
     smem = pl.BlockSpec(memory_space=pltpu.SMEM)
     vmem = pl.BlockSpec(memory_space=pltpu.VMEM)
     return pl.pallas_call(

time: 164 us -> 166 us (1.012)
  Pallas kernels: 38.2 us -> 40.3 us
    pallas_call x1, Pallas kernels: 7.28 us -> 9.38 us  [reward(): pl.pallas_call(functools.partial(reward_kernel, particles, scale, parts,...]
  transfers between devices with their start and end apart: 25 -> 25, of which waited for: 12 -> 12; matrix products, arithmetic and copies ran while one was open for 3% -> 3% of each run, Pallas kernels for 17% -> 18%
where the time goes in v17:
time: 166 us; the launch traced here: 165 us
  waiting for transfers between devices  59.3 us (36%)
  starting transfers between devices  53.2 us (32%)
  Pallas kernels  40.3 us (24%)
  local copies, waits for them, and re-layouts  7.57 us (5%)
  other arithmetic  3.3 us (2%)
    ppermute x10, waiting for transfers between devices, swapped(): lax.ppermute(array, axis, [(i, i ^ bit) for i in range(lax.axis_size(axis...  47.4 us
    all_to_all x4, starting transfers between devices, exchange(): return lax.all_to_all(array, 'seq', 0, 0, tiled=True)  20.6 us
    ppermute x10, starting transfers between devices, swapped(): lax.ppermute(array, axis, [(i, i ^ bit) for i in range(lax.axis_size(axis...  19.8 us
    pallas_call x2, Pallas kernels, attention(): pl.pallas_call(functools.partial(attention_kernel, head_width, block_sour...  11 us
    pallas_call x1, Pallas kernels, reward(): pl.pallas_call(functools.partial(reward_kernel, particles, scale, parts,...  9.38 us
    pallas_call x1, Pallas kernels, project_embed(): pl.pallas_call(kernel, in_specs=[smem, hbm, vmem, hbm] + ([] if begun is...  8.72 us
    ppermute x10, waiting for transfers between devices, shifted(): lax.ppermute(array, axis, [(i, (i + step) % count) for i in range(count)])  7.15 us
    ppermute x10, starting transfers between devices, shifted(): lax.ppermute(array, axis, [(i, (i + step) % count) for i in range(count)])  7.02 us
  transfers between devices with their start and end apart: 25, of which 12 were waited for; matrix products, arithmetic and copies ran while one was open for 3% of the time, Pallas kernels for 18%

profile of v17, /device:TPU:0, one launch (start us, length us, event | category | flops | bytes accessed | tf_op | source)
XLA Modules:
  0.0 165.2 jit_solution(4677327873092601625)
XLA Ops:
  1.6 4.0 %collective-permute-start = (bf16[1,192,256]{2,1,0:T(8,128)(2,1)S(1)}, bf16[1,192,256]{2,1,0:T(8,128)(2,1)S(1)}, u32[]{:S(2)}, u32[]{:S(2)}) collective-permute-start(bf16[1,192,256]{2,1,0:T(8,128)(2,1)S(1)} %dynamic-slice_bitcast_fusion.1), channel_id=1, source_target_pairs={{0,4},{1,5},{2,6},{3,7},{4,0},{5,1},{6,2},{7,3},{8,12},{9,13},{10,... | collective-permute-start | bytes 294920 | tf_op jit(solution)/shard_map/ppermute | solution.py:525
  5.7 3.2 %pack_heads.1 = (bf16[8,3,64,384]{3,2,1,0:T(8,128)(2,1)}, bf16[8,3,64,384]{3,2,1,0:T(8,128)(2,1)}) custom-call(bf16[4,64,1536]{2,1,0:T(8,128)(2,1)} %q_ref.1, bf16[4,64,1536]{2,1,0:T(8,128)(2,1)} %k_ref.1, bf16[4,64,1536]{2,1,0:T(8,128)(2,1)} %v_ref.1), custom_call_target="tpu_custom_call" | custom-call | tf_op jit(solution)/shard_map/pack_heads/pallas_call | solution.py:40
  8.9 1.7 %collective-permute-done = bf16[1,192,256]{2,1,0:T(8,128)(2,1)S(1)} collective-permute-done((bf16[1,192,256]{2,1,0:T(8,128)(2,1)S(1)}, bf16[1,192,256]{2,1,0:T(8,128)(2,1)S(1)}, u32[]{:S(2)}, u32[]{:S(2)}) %collective-permute-start) | collective-permute-done | bytes 98336 | tf_op jit(solution)/shard_map/ppermute | solution.py:525
  11.3 5.9 %all-to-all-start = ((bf16[8,3,64,384]{3,2,1,0:T(8,128)(2,1)}), bf16[8,3,64,384]{3,2,1,0:T(8,128)(2,1)S(1)}, u32[]{:S(2)}, u32[]{:S(2)}) async-start(bf16[8,3,64,384]{3,2,1,0:T(8,128)(2,1)} %gate.4), calls=%async_computation | async-start | bytes 2359296 | tf_op jit(solution)/shard_map/all_to_all | solution.py:529
  17.2 2.0 %collective-permute-start.6 = (bf16[2,192,256]{2,1,0:T(8,128)(2,1)S(1)}, bf16[2,192,256]{2,1,0:T(8,128)(2,1)S(1)}, u32[]{:S(2)}, u32[]{:S(2)}) collective-permute-start(bf16[2,192,256]{2,1,0:T(8,128)(2,1)S(1)} %copy-done.10), channel_id=1, source_target_pairs={{0,2},{1,3},{2,0},{3,1},{4,6},{5,7},{6,4},{7,5},{8,10},{9,11},{10,... | collective-permute-start | bytes 589832 | tf_op jit(solution)/shard_map/ppermute | solution.py:525
  19.2 22.1 %collective-permute-done.6 = bf16[2,192,256]{2,1,0:T(8,128)(2,1)S(1)} collective-permute-done((bf16[2,192,256]{2,1,0:T(8,128)(2,1)S(1)}, bf16[2,192,256]{2,1,0:T(8,128)(2,1)S(1)}, u32[]{:S(2)}, u32[]{:S(2)}) %collective-permute-start.6) | collective-permute-done | bytes 196640 | tf_op jit(solution)/shard_map/ppermute | solution.py:525
  42.6 4.4 %collective-permute-start.1 = (bf16[1,512,256]{2,1,0:T(8,128)(2,1)S(1)}, bf16[1,512,256]{2,1,0:T(8,128)(2,1)S(1)}, u32[]{:S(2)}, u32[]{:S(2)}) collective-permute-start(bf16[1,512,256]{2,1,0:T(8,128)(2,1)S(1)} %dynamic-slice_bitcast_fusion.refs_5_), channel_id=1, source_target_pairs={{0,4},{1,5},{2,6},{3,7},{4,0},{5,1},{6,2},{7,3},{8,12},{9,13},{10,... | collective-permute-start | bytes 786440 | tf_op jit(solution)/shard_map/ppermute | solution.py:525
  47.6 1.5 collective-permute-start.10
  49.1 4.5 %collective-permute-done.7 = bf16[4,192,256]{2,1,0:T(8,128)(2,1)} collective-permute-done((bf16[4,192,256]{2,1,0:T(8,128)(2,1)S(1)}, bf16[4,192,256]{2,1,0:T(8,128)(2,1)}, u32[]{:S(2)}, u32[]{:S(2)}) %collective-permute-start.7) | collective-permute-done | bytes 393248 | tf_op jit(solution)/shard_map/ppermute | solution.py:525
  53.6 2.0 %pad_maximum_fusion.refs_1_.refs_6_ = bf16[8,192,256]{2,1,0:T(8,128)(2,1)} fusion(bf16[4,192,256]{2,1,0:T(8,128)(2,1)} %collective-permute-done.7, bf16[2,192,256]{2,1,0:T(8,128)(2,1)S(1)} %collective-permute-done.6, bf16[1,192,256]{2,1,0:T(8,128)(2,1)S(1)} %collective-permute-done, bf16[1,192,256]{2,1,0:T(8,128)(2,1)S(1)} %dynamic-slice_bitcast_fusion.1), kind=kLoop, calls=%fused_computation | loop fusion | flops 1179648 | bytes 1572864 | tf_op jit(solution)/shard_map/concatenate | solution.py:588
  55.6 2.3 %collective-permute-done.1.refs_2_ = bf16[1,512,256]{2,1,0:T(8,128)(2,1)S(1)} collective-permute-done((bf16[1,512,256]{2,1,0:T(8,128)(2,1)S(1)}, bf16[1,512,256]{2,1,0:T(8,128)(2,1)S(1)}, u32[]{:S(2)}, u32[]{:S(2)}) %collective-permute-start.1) | collective-permute-done | bytes 262176 | tf_op jit(solution)/shard_map/ppermute | solution.py:525
  57.9 2.6 %collective-permute-done.3.refs_3_ = bf16[1,512,256]{2,1,0:T(8,128)(2,1)S(1)} collective-permute-done((bf16[1,512,256]{2,1,0:T(8,128)(2,1)S(1)}, bf16[1,512,256]{2,1,0:T(8,128)(2,1)S(1)}, u32[]{:S(2)}, u32[]{:S(2)}) %collective-permute-start.3) | collective-permute-done | bytes 262176 | tf_op jit(solution)/shard_map/ppermute | solution.py:525
  61.1 3.6 %all-to-all-start.2 = ((bf16[8,3,64,384]{3,2,1,0:T(8,128)(2,1)}), bf16[8,3,64,384]{3,2,1,0:T(8,128)(2,1)S(1)}, u32[]{:S(2)}, u32[]{:S(2)}) async-start(bf16[8,3,64,384]{3,2,1,0:T(8,128)(2,1)} %gate.6), calls=%async_computation.2 | async-start | bytes 2359296 | tf_op jit(solution)/shard_map/all_to_all | solution.py:529
  67.6 2.1 %collective-permute-start.4 = (bf16[2,512,256]{2,1,0:T(8,128)(2,1)S(1)}, bf16[2,512,256]{2,1,0:T(8,128)(2,1)S(1)}, u32[]{:S(2)}, u32[]{:S(2)}) collective-permute-start(bf16[2,512,256]{2,1,0:T(8,128)(2,1)S(1)} %constant_dynamic-update-slice_fusion.refs_9_), channel_id=1, source_target_pairs={{0,1},{1,0},{2,3},{3,2},{4,5},{5,4},{6,7},{7,6},{8,9},{9,8},{10,11... | collective-permute-start | bytes 1572872 | tf_op jit(solution)/shard_map/ppermute | solution.py:525
  70.7 1.5 collective-permute-start.2
  72.1 5.5 %attention.2.refs_0_ = bf16[8,64,384]{2,1,0:T(8,128)(2,1)S(1)} custom-call(bf16[8,3,64,384]{3,2,1,0:T(8,128)(2,1)S(1)} %all-to-all-done.qkv_ref), custom_call_target="tpu_custom_call" | custom-call | flops 402653184 | bytes 1572864 | tf_op jit(solution)/shard_map/attention/pallas_call | solution.py:104
  78.4 9.8 %collective-permute-done.2.refs_1_.refs_13_ = bf16[1,512,256]{2,1,0:T(8,128)(2,1)} collective-permute-done((bf16[1,512,256]{2,1,0:T(8,128)(2,1)}, bf16[1,512,256]{2,1,0:T(8,128)(2,1)}, u32[]{:S(2)}, u32[]{:S(2)}) %collective-permute-start.2) | collective-permute-done | bytes 262176 | tf_op jit(solution)/shard_map/ppermute | solution.py:525
  88.2 1.6 collective-permute-done.4.refs_2_.refs_11_
  89.8 4.1 %collective-permute-done.5.refs_3_.refs_10_ = bf16[2,512,256]{2,1,0:T(8,128)(2,1)} collective-permute-done((bf16[2,512,256]{2,1,0:T(8,128)(2,1)S(1)}, bf16[2,512,256]{2,1,0:T(8,128)(2,1)}, u32[]{:S(2)}, u32[]{:S(2)}) %collective-permute-start.5) | collective-permute-done | bytes 524320 | tf_op jit(solution)/shard_map/ppermute | solution.py:521
  94.0 5.6 %all-to-all-start.1 = ((bf16[8,64,384]{2,1,0:T(8,128)(2,1)}), bf16[8,64,384]{2,1,0:T(8,128)(2,1)}, u32[]{:S(2)}, u32[]{:S(2)}) async-start(bf16[8,64,384]{2,1,0:T(8,128)(2,1)} %gate.5), calls=%async_computation.1 | async-start | bytes 786432 | tf_op jit(solution)/shard_map/all_to_all | solution.py:529
  101.6 2.0 %collective-permute-start.11 = (bf16[1,512,256]{2,1,0:T(8,128)(2,1)}, bf16[1,512,256]{2,1,0:T(8,128)(2,1)}, u32[]{:S(2)}, u32[]{:S(2)}) collective-permute-start(bf16[1,512,256]{2,1,0:T(8,128)(2,1)} %collective-permute-done.2.refs_1_.refs_13_), channel_id=1, source_target_pairs={{0,1},{1,0},{2,3},{3,2},{4,5},{5,4},{6,7},{7,6},{8,9},{9,8},{10,11... | collective-permute-start | bytes 786440 | tf_op jit(solution)/shard_map/ppermute | solution.py:525
  104.1 5.5 %attention.3.refs_0_ = bf16[8,64,384]{2,1,0:T(8,128)(2,1)S(1)} custom-call(bf16[8,3,64,384]{3,2,1,0:T(8,128)(2,1)S(1)} %all-to-all-done.2.qkv_ref), custom_call_target="tpu_custom_call" | custom-call | flops 402653184 | bytes 1572864 | tf_op jit(solution)/shard_map/attention/pallas_call | solution.py:104
  111.2 5.6 %all-to-all-start.3 = ((bf16[8,64,384]{2,1,0:T(8,128)(2,1)}), bf16[8,64,384]{2,1,0:T(8,128)(2,1)S(1)}, u32[]{:S(2)}, u32[]{:S(2)}) async-start(bf16[8,64,384]{2,1,0:T(8,128)(2,1)} %gate.7), calls=%async_computation.3 | async-start | bytes 786432 | tf_op jit(solution)/shard_map/all_to_all | solution.py:529
  117.2 2.0 %collective-permute-start.17 = (bf16[1,512,256]{2,1,0:T(8,128)(2,1)}, bf16[1,512,256]{2,1,0:T(8,128)(2,1)S(1)}, u32[]{:S(2)}, u32[]{:S(2)}) collective-permute-start(bf16[1,512,256]{2,1,0:T(8,128)(2,1)} %copy-done.17), channel_id=1, source_target_pairs={{0,1},{1,0},{2,3},{3,2},{4,5},{5,4},{6,7},{7,6},{8,9},{9,8},{10,11... | collective-permute-start | bytes 786440 | tf_op jit(solution)/shard_map/ppermute | solution.py:525
  120.5 4.7 %first_project.1.refs_4_ = f32[256,1536]{1,0:T(8,128)} custom-call(bf16[4,64,1536]{2,1,0:T(8,128)(2,1)} %refs_1_.2, bf16[1536,1536]{1,0:T(8,128)(2,1)} %refs_3_.1, bf16[8,64,384]{2,1,0:T(8,128)(2,1)} %all-to-all-done.1.piece_ref), custom_call_target="tpu_custom_call" | custom-call | flops 603979776 | bytes 5505024 | tf_op jit(solution)/shard_map/first_project/pallas_call | solution.py:181
  125.2 2.9 %collective-permute-done.17.refs_11_.refs_16_ = bf16[1,512,256]{2,1,0:T(8,128)(2,1)S(1)} collective-permute-done((bf16[1,512,256]{2,1,0:T(8,128)(2,1)}, bf16[1,512,256]{2,1,0:T(8,128)(2,1)S(1)}, u32[]{:S(2)}, u32[]{:S(2)}) %collective-permute-start.17) | collective-permute-done | bytes 262176 | tf_op jit(solution)/shard_map/ppermute | solution.py:525
  130.3 8.7 %project_embed.1 = (bf16[4,64,1536]{2,1,0:T(8,128)(2,1)}, bf16[2,256,512]{2,1,0:T(8,128)(2,1)}) custom-call(s32[4]{0:T(128)} %pad_add_fusion.refs_0_.ids_ref, bf16[4,64,1536]{2,1,0:T(8,128)(2,1)} %refs_1_.2, f32[1,1024]{1,0:T(1,128)} %bitcast.10, bf16[1536,1536]{1,0:T(8,128)(2,1)} %refs_3_.1, f32[256,1536]{1,0:T(8,128)} %first_project.1.refs_4_, ...), custom_call_target="tpu_custom_call" | custom-call | flops 1409286144 | bytes 10223616 | tf_op jit(solution)/shard_map/project_embed/pallas_call | solution.py:331
  139.6 1.6 collective-permute-done.19.refs_4_
  142.0 9.4 %reward.1 = f32[16,8,128]{2,1,0:T(8,128)} custom-call(s32[4]{0:T(128)} %pad_add_fusion.refs_0_.ids_ref, f32[4]{0:T(128)} %refs_1_.3, f32[16,1,256]{2,1,0:T(1,128)} %bitcast.11, bf16[2,256,512]{2,1,0:T(8,128)(2,1)} %get-tuple-element.11.refs_3_, bf16[2,256,512]{2,1,0:T(8,128)(2,1)} %copy-done.19, bf16[1,512,256]{2,1,0:T(8,128)(2,1)} %copy-done.15, ...), custom_call_target="tpu_custom_call" | custom-call | flops 2147483648 | bytes 4194304 | tf_op jit(solution)/shard_map/reward/pallas_call | solution.py:436
  151.4 5.8 %all-to-all-start.4 = ((f32[16,8,128]{2,1,0:T(8,128)}), f32[16,8,128]{2,1,0:T(8,128)S(1)}, u32[]{:S(2)}, u32[]{:S(2)}) async-start(f32[16,8,128]{2,1,0:T(8,128)} %reward.1), calls=%async_computation.4 | async-start | bytes 131072 | tf_op jit(solution)/shard_map/all_to_all | solution.py:658
  157.2 2.0 %resample.1.resampled_ref = bf16[4,64,1536]{2,1,0:T(8,128)(2,1)} custom-call(s32[4]{0:T(128)S(1)} %copy-done.4, s32[4]{0:T(128)S(1)} %copy-done.5, bf16[4,64,1536]{2,1,0:T(8,128)(2,1)S(1)} %copy-done.3, bf16[4,64,1536]{2,1,0:T(8,128)(2,1)S(1)} %collective-permute-done.18.other_ref), custom_call_target="tpu_custom_call" | custom-call | tf_op jit(solution)/shard_map/resample/pallas_call | solution.py:505
  159.2 4.7 %all-to-all-done.4.parts_ref = f32[16,8,128]{2,1,0:T(8,128)S(1)} async-done(((f32[16,8,128]{2,1,0:T(8,128)}), f32[16,8,128]{2,1,0:T(8,128)S(1)}, u32[]{:S(2)}, u32[]{:S(2)}) %all-to-all-start.4) | async-done | bytes 65568 | tf_op jit(solution)/shard_map/all_to_all | solution.py:658
  (78 shorter events, 18.9 us)
Async XLA Ops:
  0.6 42.0 %copy-start = (bf16[1024,512]{1,0:T(8,128)(2,1)S(1)}, bf16[1024,512]{1,0:T(8,128)(2,1)}, u32[]{:S(2)}) copy-start(bf16[1024,512]{1,0:T(8,128)(2,1)} %param.20) | copy-start | bytes 3145732
  1.6 8.9 %collective-permute-start = (bf16[1,192,256]{2,1,0:T(8,128)(2,1)S(1)}, bf16[1,192,256]{2,1,0:T(8,128)(2,1)S(1)}, u32[]{:S(2)}, u32[]{:S(2)}) collective-permute-start(bf16[1,192,256]{2,1,0:T(8,128)(2,1)S(1)} %dynamic-slice_bitcast_fusion.1), channel_id=1, source_target_pairs={{0,4},{1,5},{2,6},{3,7},{4,0},{5,1},{6,2},{7,3},{8,12},{9,13},{10,... | collective-permute-start | bytes 294920 | tf_op jit(solution)/shard_map/ppermute | solution.py:525
  11.3 49.9 %all-to-all-start = ((bf16[8,3,64,384]{3,2,1,0:T(8,128)(2,1)}), bf16[8,3,64,384]{3,2,1,0:T(8,128)(2,1)S(1)}, u32[]{:S(2)}, u32[]{:S(2)}) async-start(bf16[8,3,64,384]{3,2,1,0:T(8,128)(2,1)} %gate.4), calls=%async_computation | async-start | bytes 2359296 | tf_op jit(solution)/shard_map/all_to_all | solution.py:529
  17.2 24.2 %collective-permute-start.6 = (bf16[2,192,256]{2,1,0:T(8,128)(2,1)S(1)}, bf16[2,192,256]{2,1,0:T(8,128)(2,1)S(1)}, u32[]{:S(2)}, u32[]{:S(2)}) collective-permute-start(bf16[2,192,256]{2,1,0:T(8,128)(2,1)S(1)} %copy-done.10), channel_id=1, source_target_pairs={{0,2},{1,3},{2,0},{3,1},{4,6},{5,7},{6,4},{7,5},{8,10},{9,11},{10,... | collective-permute-start | bytes 589832 | tf_op jit(solution)/shard_map/ppermute | solution.py:525
  41.4 12.2 %collective-permute-start.7 = (bf16[4,192,256]{2,1,0:T(8,128)(2,1)S(1)}, bf16[4,192,256]{2,1,0:T(8,128)(2,1)}, u32[]{:S(2)}, u32[]{:S(2)}) collective-permute-start(bf16[4,192,256]{2,1,0:T(8,128)(2,1)S(1)} %pad_maximum_fusion.1), channel_id=1, source_target_pairs={{0,1},{1,0},{2,3},{3,2},{4,5},{5,4},{6,7},{7,6},{8,9},{9,8},{10,11... | collective-permute-start | bytes 1179656 | tf_op jit(solution)/shard_map/ppermute | solution.py:525
  42.6 17.8 %copy-start.15 = (bf16[1,512,256]{2,1,0:T(8,128)(2,1)}, bf16[1,512,256]{2,1,0:T(8,128)(2,1)S(1)}, u32[]{:S(2)}) copy-start(bf16[1,512,256]{2,1,0:T(8,128)(2,1)S(1)} %dynamic-slice_bitcast_fusion.refs_5_) | copy-start | bytes 786436
  42.6 15.2 %collective-permute-start.1 = (bf16[1,512,256]{2,1,0:T(8,128)(2,1)S(1)}, bf16[1,512,256]{2,1,0:T(8,128)(2,1)S(1)}, u32[]{:S(2)}, u32[]{:S(2)}) collective-permute-start(bf16[1,512,256]{2,1,0:T(8,128)(2,1)S(1)} %dynamic-slice_bitcast_fusion.refs_5_), channel_id=1, source_target_pairs={{0,4},{1,5},{2,6},{3,7},{4,0},{5,1},{6,2},{7,3},{8,12},{9,13},{10,... | collective-permute-start | bytes 786440 | tf_op jit(solution)/shard_map/ppermute | solution.py:525
  47.0 10.8 %collective-permute-start.9 = (bf16[1,512,256]{2,1,0:T(8,128)(2,1)S(1)}, bf16[1,512,256]{2,1,0:T(8,128)(2,1)}, u32[]{:S(2)}, u32[]{:S(2)}) collective-permute-start(bf16[1,512,256]{2,1,0:T(8,128)(2,1)S(1)} %dynamic-slice_bitcast_fusion.refs_5_), channel_id=1, source_target_pairs={{0,1},{1,0},{2,3},{3,2},{4,5},{5,4},{6,7},{7,6},{8,9},{9,8},{10,11... | collective-permute-start | bytes 786440 | tf_op jit(solution)/shard_map/ppermute | solution.py:525
  47.6 10.2 %collective-permute-start.10 = (bf16[1,512,256]{2,1,0:T(8,128)(2,1)S(1)}, bf16[1,512,256]{2,1,0:T(8,128)(2,1)S(1)}, u32[]{:S(2)}, u32[]{:S(2)}) collective-permute-start(bf16[1,512,256]{2,1,0:T(8,128)(2,1)S(1)} %dynamic-slice_bitcast_fusion.refs_5_), channel_id=1, source_target_pairs={{0,16},{16,0},{1,17},{17,1},{2,18},{18,2},{3,19},{19,3},{4,20},{20... | collective-permute-start | bytes 786440 | tf_op jit(solution)/shard_map/ppermute | solution.py:521
  49.1 11.3 %collective-permute-start.3 = (bf16[1,512,256]{2,1,0:T(8,128)(2,1)S(1)}, bf16[1,512,256]{2,1,0:T(8,128)(2,1)S(1)}, u32[]{:S(2)}, u32[]{:S(2)}) collective-permute-start(bf16[1,512,256]{2,1,0:T(8,128)(2,1)S(1)} %dynamic-slice_bitcast_fusion.refs_5_), channel_id=1, source_target_pairs={{0,2},{1,3},{2,0},{3,1},{4,6},{5,7},{6,4},{7,5},{8,10},{9,11},{10,... | collective-permute-start | bytes 786440 | tf_op jit(solution)/shard_map/ppermute | solution.py:525
  61.1 32.8 %all-to-all-start.2 = ((bf16[8,3,64,384]{3,2,1,0:T(8,128)(2,1)}), bf16[8,3,64,384]{3,2,1,0:T(8,128)(2,1)S(1)}, u32[]{:S(2)}, u32[]{:S(2)}) async-start(bf16[8,3,64,384]{3,2,1,0:T(8,128)(2,1)} %gate.6), calls=%async_computation.2 | async-start | bytes 2359296 | tf_op jit(solution)/shard_map/all_to_all | solution.py:529
  64.7 29.2 %collective-permute-start.8 = (bf16[8,192,256]{2,1,0:T(8,128)(2,1)}, bf16[8,192,256]{2,1,0:T(8,128)(2,1)}, u32[]{:S(2)}, u32[]{:S(2)}) collective-permute-start(bf16[8,192,256]{2,1,0:T(8,128)(2,1)} %pad_maximum_fusion.refs_1_.refs_6_), channel_id=1, source_target_pairs={{0,16},{16,0},{1,17},{17,1},{2,18},{18,2},{3,19},{19,3},{4,20},{20... | collective-permute-start | bytes 2359304 | tf_op jit(solution)/shard_map/ppermute | solution.py:521
  67.5 10.1 %copy-start.18 = (bf16[2,512,256]{2,1,0:T(8,128)(2,1)}, bf16[2,512,256]{2,1,0:T(8,128)(2,1)S(1)}, u32[]{:S(2)}) copy-start(bf16[2,512,256]{2,1,0:T(8,128)(2,1)S(1)} %constant_dynamic-update-slice_fusion.refs_9_) | copy-start | bytes 1572868
  67.6 22.2 %collective-permute-start.4 = (bf16[2,512,256]{2,1,0:T(8,128)(2,1)S(1)}, bf16[2,512,256]{2,1,0:T(8,128)(2,1)S(1)}, u32[]{:S(2)}, u32[]{:S(2)}) collective-permute-start(bf16[2,512,256]{2,1,0:T(8,128)(2,1)S(1)} %constant_dynamic-update-slice_fusion.refs_9_), channel_id=1, source_target_pairs={{0,1},{1,0},{2,3},{3,2},{4,5},{5,4},{6,7},{7,6},{8,9},{9,8},{10,11... | collective-permute-start | bytes 1572872 | tf_op jit(solution)/shard_map/ppermute | solution.py:525
  69.6 24.3 %collective-permute-start.5 = (bf16[2,512,256]{2,1,0:T(8,128)(2,1)S(1)}, bf16[2,512,256]{2,1,0:T(8,128)(2,1)}, u32[]{:S(2)}, u32[]{:S(2)}) collective-permute-start(bf16[2,512,256]{2,1,0:T(8,128)(2,1)S(1)} %constant_dynamic-update-slice_fusion.refs_9_), channel_id=1, source_target_pairs={{0,16},{16,0},{1,17},{17,1},{2,18},{18,2},{3,19},{19,3},{4,20},{20... | collective-permute-start | bytes 1572872 | tf_op jit(solution)/shard_map/ppermute | solution.py:521
  70.7 17.6 %collective-permute-start.2 = (bf16[1,512,256]{2,1,0:T(8,128)(2,1)}, bf16[1,512,256]{2,1,0:T(8,128)(2,1)}, u32[]{:S(2)}, u32[]{:S(2)}) collective-permute-start(bf16[1,512,256]{2,1,0:T(8,128)(2,1)} %copy-done.8), channel_id=1, source_target_pairs={{0,2},{1,3},{2,0},{3,1},{4,6},{5,7},{6,4},{7,5},{8,10},{9,11},{10,... | collective-permute-start | bytes 786440 | tf_op jit(solution)/shard_map/ppermute | solution.py:525
  78.4 25.2 %copy-start.6 = (bf16[8,192,256]{2,1,0:T(8,128)(2,1)S(1)}, bf16[8,192,256]{2,1,0:T(8,128)(2,1)}, u32[]{:S(2)}) copy-start(bf16[8,192,256]{2,1,0:T(8,128)(2,1)} %pad_maximum_fusion.refs_1_.refs_6_) | copy-start | bytes 2359300
  94.0 17.2 %all-to-all-start.1 = ((bf16[8,64,384]{2,1,0:T(8,128)(2,1)}), bf16[8,64,384]{2,1,0:T(8,128)(2,1)}, u32[]{:S(2)}, u32[]{:S(2)}) async-start(bf16[8,64,384]{2,1,0:T(8,128)(2,1)} %gate.5), calls=%async_computation.1 | async-start | bytes 786432 | tf_op jit(solution)/shard_map/all_to_all | solution.py:529
  99.6 10.8 %collective-permute-start.13 = (bf16[1,512,256]{2,1,0:T(8,128)(2,1)}, bf16[1,512,256]{2,1,0:T(8,128)(2,1)S(1)}, u32[]{:S(2)}, u32[]{:S(2)}) collective-permute-start(bf16[1,512,256]{2,1,0:T(8,128)(2,1)} %collective-permute-done.9.refs_4_.refs_7_), channel_id=1, source_target_pairs={{0,16},{16,0},{1,17},{17,1},{2,18},{18,2},{3,19},{19,3},{4,20},{20... | collective-permute-start | bytes 786440 | tf_op jit(solution)/shard_map/ppermute | solution.py:521
  100.3 10.1 %collective-permute-start.12 = (bf16[1,512,256]{2,1,0:T(8,128)(2,1)}, bf16[1,512,256]{2,1,0:T(8,128)(2,1)S(1)}, u32[]{:S(2)}, u32[]{:S(2)}) collective-permute-start(bf16[1,512,256]{2,1,0:T(8,128)(2,1)} %collective-permute-done.2.refs_1_.refs_13_), channel_id=1, source_target_pairs={{0,16},{16,0},{1,17},{17,1},{2,18},{18,2},{3,19},{19,3},{4,20},{20... | collective-permute-start | bytes 786440 | tf_op jit(solution)/shard_map/ppermute | solution.py:521
  101.6 8.8 %collective-permute-start.11 = (bf16[1,512,256]{2,1,0:T(8,128)(2,1)}, bf16[1,512,256]{2,1,0:T(8,128)(2,1)}, u32[]{:S(2)}, u32[]{:S(2)}) collective-permute-start(bf16[1,512,256]{2,1,0:T(8,128)(2,1)} %collective-permute-done.2.refs_1_.refs_13_), channel_id=1, source_target_pairs={{0,1},{1,0},{2,3},{3,2},{4,5},{5,4},{6,7},{7,6},{8,9},{9,8},{10,11... | collective-permute-start | bytes 786440 | tf_op jit(solution)/shard_map/ppermute | solution.py:525
  103.6 25.8 %collective-permute-start.14 = (bf16[8,192,256]{2,1,0:T(8,128)(2,1)S(1)}, bf16[8,192,256]{2,1,0:T(8,128)(2,1)}, u32[]{:S(2)}, u32[]{:S(2)}) collective-permute-start(bf16[8,192,256]{2,1,0:T(8,128)(2,1)S(1)} %copy-done.6), channel_id=1, source_target_pairs={{0,8},{8,0},{1,9},{9,1},{2,10},{10,2},{3,11},{11,3},{4,12},{12,4},... | collective-permute-start | bytes 2359304 | tf_op jit(solution)/shard_map/ppermute | solution.py:521
  103.6 25.8 %collective-permute-start.15 = (bf16[8,192,256]{2,1,0:T(8,128)(2,1)}, bf16[8,192,256]{2,1,0:T(8,128)(2,1)}, u32[]{:S(2)}, u32[]{:S(2)}) collective-permute-start(bf16[8,192,256]{2,1,0:T(8,128)(2,1)} %collective-permute-done.8.refs_4_.refs_7_), channel_id=1, source_target_pairs={{0,8},{8,0},{1,9},{9,1},{2,10},{10,2},{3,11},{11,3},{4,12},{12,4},... | collective-permute-start | bytes 2359304 | tf_op jit(solution)/shard_map/ppermute | solution.py:521
  111.2 18.3 %all-to-all-start.3 = ((bf16[8,64,384]{2,1,0:T(8,128)(2,1)}), bf16[8,64,384]{2,1,0:T(8,128)(2,1)S(1)}, u32[]{:S(2)}, u32[]{:S(2)}) async-start(bf16[8,64,384]{2,1,0:T(8,128)(2,1)} %gate.7), calls=%async_computation.3 | async-start | bytes 786432 | tf_op jit(solution)/shard_map/all_to_all | solution.py:529
  116.7 12.7 %collective-permute-start.16 = (bf16[2,512,256]{2,1,0:T(8,128)(2,1)S(1)}, bf16[2,512,256]{2,1,0:T(8,128)(2,1)}, u32[]{:S(2)}, u32[]{:S(2)}) collective-permute-start(bf16[2,512,256]{2,1,0:T(8,128)(2,1)S(1)} %copy-done.12), channel_id=1, source_target_pairs={{0,16},{16,0},{1,17},{17,1},{2,18},{18,2},{3,19},{19,3},{4,20},{20... | collective-permute-start | bytes 1572872 | tf_op jit(solution)/shard_map/ppermute | solution.py:521
  117.2 10.8 %collective-permute-start.17 = (bf16[1,512,256]{2,1,0:T(8,128)(2,1)}, bf16[1,512,256]{2,1,0:T(8,128)(2,1)S(1)}, u32[]{:S(2)}, u32[]{:S(2)}) collective-permute-start(bf16[1,512,256]{2,1,0:T(8,128)(2,1)} %copy-done.17), channel_id=1, source_target_pairs={{0,1},{1,0},{2,3},{3,2},{4,5},{5,4},{6,7},{7,6},{8,9},{9,8},{10,11... | collective-permute-start | bytes 786440 | tf_op jit(solution)/shard_map/ppermute | solution.py:525
  139.0 2.2 %collective-permute-start.19 = (bf16[2,256,512]{2,1,0:T(8,128)(2,1)}, bf16[2,256,512]{2,1,0:T(8,128)(2,1)S(1)}, u32[]{:S(2)}, u32[]{:S(2)}) collective-permute-start(bf16[2,256,512]{2,1,0:T(8,128)(2,1)} %get-tuple-element.11.refs_3_), channel_id=1, source_target_pairs={{0,8},{8,0},{1,9},{9,1},{2,10},{10,2},{3,11},{11,3},{4,12},{12,4},... | collective-permute-start | bytes 1572872 | tf_op jit(solution)/shard_map/ppermute | solution.py:521
  139.1 18.1 %collective-permute-start.18 = (bf16[4,64,1536]{2,1,0:T(8,128)(2,1)}, bf16[4,64,1536]{2,1,0:T(8,128)(2,1)S(1)}, u32[]{:S(2)}, u32[]{:S(2)}) collective-permute-start(bf16[4,64,1536]{2,1,0:T(8,128)(2,1)} %get-tuple-element.10.own_ref), channel_id=1, source_target_pairs={{0,8},{8,0},{1,9},{9,1},{2,10},{10,2},{3,11},{11,3},{4,12},{12,4},... | collective-permute-start | bytes 2359304 | tf_op jit(solution)/shard_map/ppermute | solution.py:521
  142.0 15.2 %copy-start.3 = (bf16[4,64,1536]{2,1,0:T(8,128)(2,1)S(1)}, bf16[4,64,1536]{2,1,0:T(8,128)(2,1)}, u32[]{:S(2)}) copy-start(bf16[4,64,1536]{2,1,0:T(8,128)(2,1)} %get-tuple-element.10.own_ref) | copy-start | bytes 2359300
  142.0 15.2 %copy-start.4 = (s32[4]{0:T(128)S(1)}, s32[4]{0:T(128)}, u32[]{:S(2)}) copy-start(s32[4]{0:T(128)} %pad_add_fusion.refs_0_.ids_ref) | copy-start | bytes 52
  142.0 15.2 %copy-start.5 = (s32[4]{0:T(128)S(1)}, s32[4]{0:T(128)}, u32[]{:S(2)}) copy-start(s32[4]{0:T(128)} %ancestors_ref.1) | copy-start | bytes 52
  151.4 12.5 %all-to-all-start.4 = ((f32[16,8,128]{2,1,0:T(8,128)}), f32[16,8,128]{2,1,0:T(8,128)S(1)}, u32[]{:S(2)}, u32[]{:S(2)}) async-start(f32[16,8,128]{2,1,0:T(8,128)} %reward.1), calls=%async_computation.4 | async-start | bytes 131072 | tf_op jit(solution)/shard_map/all_to_all | solution.py:658
  (13 other events, 28.4 us)

commit v18 on v17

--- a/solution.py
+++ b/solution.py
@@ -212,6 +212,7 @@
     particles, tokens, model_width = latents_ref.shape
     rows = particles * tokens
     shards, depth, columns = weight_refs[0].shape
+    joined = parts // weight_vmem.shape[0]
 
     wanted = list(range(chunks - len(rest), chunks))
     block = column_block(model_width)
@@ -240,7 +241,11 @@
             start = pl.multiple_of((seq ^ offsets[shard]) * depth, depth)
             copy = pltpu.make_async_copy(
                 weight_refs[index].at[shard],
-                weight_vmem.at[index, pl.ds(start, depth)],
+                weight_vmem.at[
+                    index // joined,
+                    pl.ds(start, depth),
+                    index % joined * columns : (index % joined + 1) * columns,
+                ],
                 sems.at[index],
             )
             copy.start()
@@ -264,15 +269,18 @@
             .reshape(particles, tokens, out_weights.block)
         )
 
-    for index in range(parts):
-        for copy in copies[index * shards : (index + 1) * shards]:
+    doms = parts // depth_parts
+    for step in range(parts // joined):
+        for copy in copies[step * joined * shards : (step + 1) * joined * shards]:
             copy.wait()
-        doms = parts // depth_parts
-        dom_of = (dom + doms - index // depth_parts) % doms
-        group_of = (group + depth_parts - index % depth_parts) % depth_parts
-        embedded_ref[dom_of * depth_parts + group_of] = jnp.dot(
-            clean_ref[...], weight_vmem[index], preferred_element_type=jnp.float32
-        )
+        product = jnp.dot(clean_ref[...], weight_vmem[step], preferred_element_type=jnp.float32)
+        for lane in range(joined):
+            index = step * joined + lane
+            dom_of = (dom + doms - index // depth_parts) % doms
+            group_of = (group + depth_parts - index % depth_parts) % depth_parts
+            embedded_ref[dom_of * depth_parts + group_of] = product[
+                :, lane * columns : (lane + 1) * columns
+            ]
     count = parts * columns
     blocks = [embedded_ref[index] for index in range(parts)]
     centre = sum(jnp.sum(piece, axis=1, keepdims=True) for piece in blocks) * (1.0 / count)
@@ -310,6 +318,7 @@
     count = parts * columns
     out_depth = model_width * len(attended) // chunks
     pieces = ([] if begun is None else [begun]) + attended
+    joined = 2 if columns % LANES == 0 and parts % 2 == 0 else 1
     vmem = pl.BlockSpec(memory_space=pltpu.VMEM)
     smem = pl.BlockSpec(memory_space=pltpu.SMEM)
     hbm = pl.BlockSpec(memory_space=pltpu.HBM)
@@ -342,7 +351,7 @@
         ],
         scratch_shapes=[
             pltpu.VMEM((out_depth, model_width), jnp.bfloat16),
-            pltpu.VMEM((parts, model_width, columns), jnp.bfloat16),
+            pltpu.VMEM((parts // joined, model_width, joined * columns), jnp.bfloat16),
             pltpu.VMEM((rows, out_depth), jnp.bfloat16),
             pltpu.VMEM((rows, model_width), jnp.bfloat16),
             pltpu.VMEM((parts, rows, columns), jnp.float32),
@@ -430,7 +439,7 @@
     _, depth, columns = weights[0].shape
     rows, doms = features[0].shape[1], len(features)
     count = len(offsets)
-    joined = 1
+    joined = next(n for n in (4, 2, 1) if n == 1 or columns % LANES == 0 == count % n)
     smem = pl.BlockSpec(memory_space=pltpu.SMEM)
     vmem = pl.BlockSpec(memory_space=pltpu.VMEM)
     return pl.pallas_call(

time: 166 us -> 163 us (0.982)
  Pallas kernels: 40.3 us -> 37.1 us
    pallas_call x1, Pallas kernels: 9.38 us -> 7.24 us  [reward(): pl.pallas_call(functools.partial(reward_kernel, particles, scale, parts,...]
  transfers between devices with their start and end apart: 25 -> 25, of which waited for: 12 -> 12; matrix products, arithmetic and copies ran while one was open for 3% -> 3% of each run, Pallas kernels for 18% -> 17%
where the time goes in v18:
time: 163 us; the launch traced here: 162 us
  waiting for transfers between devices  59.3 us (36%)
  starting transfers between devices  53.2 us (33%)
  Pallas kernels  37.1 us (23%)
  local copies, waits for them, and re-layouts  7.57 us (5%)
  other arithmetic  3.3 us (2%)
    ppermute x10, waiting for transfers between devices, swapped(): lax.ppermute(array, axis, [(i, i ^ bit) for i in range(lax.axis_size(axis...  47.4 us
    all_to_all x4, starting transfers between devices, exchange(): return lax.all_to_all(array, 'seq', 0, 0, tiled=True)  20.6 us
    ppermute x10, starting transfers between devices, swapped(): lax.ppermute(array, axis, [(i, i ^ bit) for i in range(lax.axis_size(axis...  19.8 us
    pallas_call x2, Pallas kernels, attention(): pl.pallas_call(functools.partial(attention_kernel, head_width, block_sour...  11 us
    pallas_call x1, Pallas kernels, project_embed(): pl.pallas_call(kernel, in_specs=[smem, hbm, vmem, hbm] + ([] if begun is...  7.7 us
    pallas_call x1, Pallas kernels, reward(): pl.pallas_call(functools.partial(reward_kernel, particles, scale, parts,...  7.24 us
    ppermute x10, waiting for transfers between devices, shifted(): lax.ppermute(array, axis, [(i, (i + step) % count) for i in range(count)])  7.15 us
    ppermute x10, starting transfers between devices, shifted(): lax.ppermute(array, axis, [(i, (i + step) % count) for i in range(count)])  7.02 us
  transfers between devices with their start and end apart: 25, of which 12 were waited for; matrix products, arithmetic and copies ran while one was open for 3% of the time, Pallas kernels for 17%

profile of v18, /device:TPU:0, one launch (start us, length us, event | category | flops | bytes accessed | tf_op | source)
XLA Modules:
  0.0 162.0 jit_solution(2031031287079922007)
XLA Ops:
  1.6 4.0 %collective-permute-start = (bf16[1,192,256]{2,1,0:T(8,128)(2,1)S(1)}, bf16[1,192,256]{2,1,0:T(8,128)(2,1)S(1)}, u32[]{:S(2)}, u32[]{:S(2)}) collective-permute-start(bf16[1,192,256]{2,1,0:T(8,128)(2,1)S(1)} %dynamic-slice_bitcast_fusion.1), channel_id=1, source_target_pairs={{0,4},{1,5},{2,6},{3,7},{4,0},{5,1},{6,2},{7,3},{8,12},{9,13},{10,... | collective-permute-start | bytes 294920 | tf_op jit(solution)/shard_map/ppermute | solution.py:534
  5.7 3.2 %pack_heads.1 = (bf16[8,3,64,384]{3,2,1,0:T(8,128)(2,1)}, bf16[8,3,64,384]{3,2,1,0:T(8,128)(2,1)}) custom-call(bf16[4,64,1536]{2,1,0:T(8,128)(2,1)} %q_ref.1, bf16[4,64,1536]{2,1,0:T(8,128)(2,1)} %k_ref.1, bf16[4,64,1536]{2,1,0:T(8,128)(2,1)} %v_ref.1), custom_call_target="tpu_custom_call" | custom-call | tf_op jit(solution)/shard_map/pack_heads/pallas_call | solution.py:40
  8.9 1.7 %collective-permute-done = bf16[1,192,256]{2,1,0:T(8,128)(2,1)S(1)} collective-permute-done((bf16[1,192,256]{2,1,0:T(8,128)(2,1)S(1)}, bf16[1,192,256]{2,1,0:T(8,128)(2,1)S(1)}, u32[]{:S(2)}, u32[]{:S(2)}) %collective-permute-start) | collective-permute-done | bytes 98336 | tf_op jit(solution)/shard_map/ppermute | solution.py:534
  11.3 5.9 %all-to-all-start = ((bf16[8,3,64,384]{3,2,1,0:T(8,128)(2,1)}), bf16[8,3,64,384]{3,2,1,0:T(8,128)(2,1)S(1)}, u32[]{:S(2)}, u32[]{:S(2)}) async-start(bf16[8,3,64,384]{3,2,1,0:T(8,128)(2,1)} %gate.4), calls=%async_computation | async-start | bytes 2359296 | tf_op jit(solution)/shard_map/all_to_all | solution.py:538
  17.2 2.0 %collective-permute-start.6 = (bf16[2,192,256]{2,1,0:T(8,128)(2,1)S(1)}, bf16[2,192,256]{2,1,0:T(8,128)(2,1)S(1)}, u32[]{:S(2)}, u32[]{:S(2)}) collective-permute-start(bf16[2,192,256]{2,1,0:T(8,128)(2,1)S(1)} %copy-done.10), channel_id=1, source_target_pairs={{0,2},{1,3},{2,0},{3,1},{4,6},{5,7},{6,4},{7,5},{8,10},{9,11},{10,... | collective-permute-start | bytes 589832 | tf_op jit(solution)/shard_map/ppermute | solution.py:534
  19.2 22.1 %collective-permute-done.6 = bf16[2,192,256]{2,1,0:T(8,128)(2,1)S(1)} collective-permute-done((bf16[2,192,256]{2,1,0:T(8,128)(2,1)S(1)}, bf16[2,192,256]{2,1,0:T(8,128)(2,1)S(1)}, u32[]{:S(2)}, u32[]{:S(2)}) %collective-permute-start.6) | collective-permute-done | bytes 196640 | tf_op jit(solution)/shard_map/ppermute | solution.py:534
  42.6 4.4 %collective-permute-start.1 = (bf16[1,512,256]{2,1,0:T(8,128)(2,1)S(1)}, bf16[1,512,256]{2,1,0:T(8,128)(2,1)S(1)}, u32[]{:S(2)}, u32[]{:S(2)}) collective-permute-start(bf16[1,512,256]{2,1,0:T(8,128)(2,1)S(1)} %dynamic-slice_bitcast_fusion.refs_5_), channel_id=1, source_target_pairs={{0,4},{1,5},{2,6},{3,7},{4,0},{5,1},{6,2},{7,3},{8,12},{9,13},{10,... | collective-permute-start | bytes 786440 | tf_op jit(solution)/shard_map/ppermute | solution.py:534
  47.6 1.5 collective-permute-start.10
  49.1 4.5 %collective-permute-done.7 = bf16[4,192,256]{2,1,0:T(8,128)(2,1)} collective-permute-done((bf16[4,192,256]{2,1,0:T(8,128)(2,1)S(1)}, bf16[4,192,256]{2,1,0:T(8,128)(2,1)}, u32[]{:S(2)}, u32[]{:S(2)}) %collective-permute-start.7) | collective-permute-done | bytes 393248 | tf_op jit(solution)/shard_map/ppermute | solution.py:534
  53.6 2.0 %pad_maximum_fusion.refs_1_.refs_6_ = bf16[8,192,256]{2,1,0:T(8,128)(2,1)} fusion(bf16[4,192,256]{2,1,0:T(8,128)(2,1)} %collective-permute-done.7, bf16[2,192,256]{2,1,0:T(8,128)(2,1)S(1)} %collective-permute-done.6, bf16[1,192,256]{2,1,0:T(8,128)(2,1)S(1)} %collective-permute-done, bf16[1,192,256]{2,1,0:T(8,128)(2,1)S(1)} %dynamic-slice_bitcast_fusion.1), kind=kLoop, calls=%fused_computation | loop fusion | flops 1179648 | bytes 1572864 | tf_op jit(solution)/shard_map/concatenate | solution.py:597
  55.6 2.3 %collective-permute-done.1.refs_2_ = bf16[1,512,256]{2,1,0:T(8,128)(2,1)S(1)} collective-permute-done((bf16[1,512,256]{2,1,0:T(8,128)(2,1)S(1)}, bf16[1,512,256]{2,1,0:T(8,128)(2,1)S(1)}, u32[]{:S(2)}, u32[]{:S(2)}) %collective-permute-start.1) | collective-permute-done | bytes 262176 | tf_op jit(solution)/shard_map/ppermute | solution.py:534
  57.9 2.6 %collective-permute-done.3.refs_3_ = bf16[1,512,256]{2,1,0:T(8,128)(2,1)S(1)} collective-permute-done((bf16[1,512,256]{2,1,0:T(8,128)(2,1)S(1)}, bf16[1,512,256]{2,1,0:T(8,128)(2,1)S(1)}, u32[]{:S(2)}, u32[]{:S(2)}) %collective-permute-start.3) | collective-permute-done | bytes 262176 | tf_op jit(solution)/shard_map/ppermute | solution.py:534
  61.1 3.6 %all-to-all-start.2 = ((bf16[8,3,64,384]{3,2,1,0:T(8,128)(2,1)}), bf16[8,3,64,384]{3,2,1,0:T(8,128)(2,1)S(1)}, u32[]{:S(2)}, u32[]{:S(2)}) async-start(bf16[8,3,64,384]{3,2,1,0:T(8,128)(2,1)} %gate.6), calls=%async_computation.2 | async-start | bytes 2359296 | tf_op jit(solution)/shard_map/all_to_all | solution.py:538
  67.6 2.1 %collective-permute-start.4 = (bf16[2,512,256]{2,1,0:T(8,128)(2,1)S(1)}, bf16[2,512,256]{2,1,0:T(8,128)(2,1)S(1)}, u32[]{:S(2)}, u32[]{:S(2)}) collective-permute-start(bf16[2,512,256]{2,1,0:T(8,128)(2,1)S(1)} %constant_dynamic-update-slice_fusion.refs_9_), channel_id=1, source_target_pairs={{0,1},{1,0},{2,3},{3,2},{4,5},{5,4},{6,7},{7,6},{8,9},{9,8},{10,11... | collective-permute-start | bytes 1572872 | tf_op jit(solution)/shard_map/ppermute | solution.py:534
  70.7 1.5 collective-permute-start.2
  72.1 5.5 %attention.2.refs_0_ = bf16[8,64,384]{2,1,0:T(8,128)(2,1)S(1)} custom-call(bf16[8,3,64,384]{3,2,1,0:T(8,128)(2,1)S(1)} %all-to-all-done.qkv_ref), custom_call_target="tpu_custom_call" | custom-call | flops 402653184 | bytes 1572864 | tf_op jit(solution)/shard_map/attention/pallas_call | solution.py:104
  78.4 9.8 %collective-permute-done.2.refs_1_.refs_13_ = bf16[1,512,256]{2,1,0:T(8,128)(2,1)} collective-permute-done((bf16[1,512,256]{2,1,0:T(8,128)(2,1)}, bf16[1,512,256]{2,1,0:T(8,128)(2,1)}, u32[]{:S(2)}, u32[]{:S(2)}) %collective-permute-start.2) | collective-permute-done | bytes 262176 | tf_op jit(solution)/shard_map/ppermute | solution.py:534
  88.2 1.6 collective-permute-done.4.refs_2_.refs_11_
  89.8 4.1 %collective-permute-done.5.refs_3_.refs_10_ = bf16[2,512,256]{2,1,0:T(8,128)(2,1)} collective-permute-done((bf16[2,512,256]{2,1,0:T(8,128)(2,1)S(1)}, bf16[2,512,256]{2,1,0:T(8,128)(2,1)}, u32[]{:S(2)}, u32[]{:S(2)}) %collective-permute-start.5) | collective-permute-done | bytes 524320 | tf_op jit(solution)/shard_map/ppermute | solution.py:530
  94.0 5.6 %all-to-all-start.1 = ((bf16[8,64,384]{2,1,0:T(8,128)(2,1)}), bf16[8,64,384]{2,1,0:T(8,128)(2,1)}, u32[]{:S(2)}, u32[]{:S(2)}) async-start(bf16[8,64,384]{2,1,0:T(8,128)(2,1)} %gate.5), calls=%async_computation.1 | async-start | bytes 786432 | tf_op jit(solution)/shard_map/all_to_all | solution.py:538
  101.6 2.0 %collective-permute-start.11 = (bf16[1,512,256]{2,1,0:T(8,128)(2,1)}, bf16[1,512,256]{2,1,0:T(8,128)(2,1)}, u32[]{:S(2)}, u32[]{:S(2)}) collective-permute-start(bf16[1,512,256]{2,1,0:T(8,128)(2,1)} %collective-permute-done.2.refs_1_.refs_13_), channel_id=1, source_target_pairs={{0,1},{1,0},{2,3},{3,2},{4,5},{5,4},{6,7},{7,6},{8,9},{9,8},{10,11... | collective-permute-start | bytes 786440 | tf_op jit(solution)/shard_map/ppermute | solution.py:534
  104.1 5.5 %attention.3.refs_0_ = bf16[8,64,384]{2,1,0:T(8,128)(2,1)S(1)} custom-call(bf16[8,3,64,384]{3,2,1,0:T(8,128)(2,1)S(1)} %all-to-all-done.2.qkv_ref), custom_call_target="tpu_custom_call" | custom-call | flops 402653184 | bytes 1572864 | tf_op jit(solution)/shard_map/attention/pallas_call | solution.py:104
  111.2 5.6 %all-to-all-start.3 = ((bf16[8,64,384]{2,1,0:T(8,128)(2,1)}), bf16[8,64,384]{2,1,0:T(8,128)(2,1)S(1)}, u32[]{:S(2)}, u32[]{:S(2)}) async-start(bf16[8,64,384]{2,1,0:T(8,128)(2,1)} %gate.7), calls=%async_computation.3 | async-start | bytes 786432 | tf_op jit(solution)/shard_map/all_to_all | solution.py:538
  117.2 2.0 %collective-permute-start.17 = (bf16[1,512,256]{2,1,0:T(8,128)(2,1)}, bf16[1,512,256]{2,1,0:T(8,128)(2,1)S(1)}, u32[]{:S(2)}, u32[]{:S(2)}) collective-permute-start(bf16[1,512,256]{2,1,0:T(8,128)(2,1)} %copy-done.17), channel_id=1, source_target_pairs={{0,1},{1,0},{2,3},{3,2},{4,5},{5,4},{6,7},{7,6},{8,9},{9,8},{10,11... | collective-permute-start | bytes 786440 | tf_op jit(solution)/shard_map/ppermute | solution.py:534
  120.5 4.7 %first_project.1.refs_4_ = f32[256,1536]{1,0:T(8,128)} custom-call(bf16[4,64,1536]{2,1,0:T(8,128)(2,1)} %refs_1_.2, bf16[1536,1536]{1,0:T(8,128)(2,1)} %refs_3_.1, bf16[8,64,384]{2,1,0:T(8,128)(2,1)} %all-to-all-done.1.piece_ref), custom_call_target="tpu_custom_call" | custom-call | flops 603979776 | bytes 5505024 | tf_op jit(solution)/shard_map/first_project/pallas_call | solution.py:181
  125.2 2.9 %collective-permute-done.17.refs_11_.refs_16_ = bf16[1,512,256]{2,1,0:T(8,128)(2,1)S(1)} collective-permute-done((bf16[1,512,256]{2,1,0:T(8,128)(2,1)}, bf16[1,512,256]{2,1,0:T(8,128)(2,1)S(1)}, u32[]{:S(2)}, u32[]{:S(2)}) %collective-permute-start.17) | collective-permute-done | bytes 262176 | tf_op jit(solution)/shard_map/ppermute | solution.py:534
  130.3 7.7 %project_embed.1 = (bf16[4,64,1536]{2,1,0:T(8,128)(2,1)}, bf16[2,256,512]{2,1,0:T(8,128)(2,1)}) custom-call(s32[4]{0:T(128)} %pad_add_fusion.refs_0_.ids_ref, bf16[4,64,1536]{2,1,0:T(8,128)(2,1)} %refs_1_.2, f32[1,1024]{1,0:T(1,128)} %bitcast.10, bf16[1536,1536]{1,0:T(8,128)(2,1)} %refs_3_.1, f32[256,1536]{1,0:T(8,128)} %first_project.1.refs_4_, ...), custom_call_target="tpu_custom_call" | custom-call | flops 1409286144 | bytes 10223616 | tf_op jit(solution)/shard_map/project_embed/pallas_call | solution.py:340
  138.5 1.6 collective-permute-done.19.refs_4_
  141.0 7.2 %reward.1 = f32[16,8,128]{2,1,0:T(8,128)} custom-call(s32[4]{0:T(128)} %pad_add_fusion.refs_0_.ids_ref, f32[4]{0:T(128)} %refs_1_.3, f32[16,1,256]{2,1,0:T(1,128)} %bitcast.11, bf16[2,256,512]{2,1,0:T(8,128)(2,1)} %get-tuple-element.11.refs_3_, bf16[2,256,512]{2,1,0:T(8,128)(2,1)} %copy-done.19, bf16[1,512,256]{2,1,0:T(8,128)(2,1)} %copy-done.15, ...), custom_call_target="tpu_custom_call" | custom-call | flops 2147483648 | bytes 4194304 | tf_op jit(solution)/shard_map/reward/pallas_call | solution.py:445
  148.2 5.8 %all-to-all-start.4 = ((f32[16,8,128]{2,1,0:T(8,128)}), f32[16,8,128]{2,1,0:T(8,128)S(1)}, u32[]{:S(2)}, u32[]{:S(2)}) async-start(f32[16,8,128]{2,1,0:T(8,128)} %reward.1), calls=%async_computation.4 | async-start | bytes 131072 | tf_op jit(solution)/shard_map/all_to_all | solution.py:667
  154.0 2.0 %resample.1.resampled_ref = bf16[4,64,1536]{2,1,0:T(8,128)(2,1)} custom-call(s32[4]{0:T(128)S(1)} %copy-done.4, s32[4]{0:T(128)S(1)} %copy-done.5, bf16[4,64,1536]{2,1,0:T(8,128)(2,1)S(1)} %copy-done.3, bf16[4,64,1536]{2,1,0:T(8,128)(2,1)S(1)} %collective-permute-done.18.other_ref), custom_call_target="tpu_custom_call" | custom-call | tf_op jit(solution)/shard_map/resample/pallas_call | solution.py:514
  156.0 4.7 %all-to-all-done.4.parts_ref = f32[16,8,128]{2,1,0:T(8,128)S(1)} async-done(((f32[16,8,128]{2,1,0:T(8,128)}), f32[16,8,128]{2,1,0:T(8,128)S(1)}, u32[]{:S(2)}, u32[]{:S(2)}) %all-to-all-start.4) | async-done | bytes 65568 | tf_op jit(solution)/shard_map/all_to_all | solution.py:667
  (78 shorter events, 18.9 us)
Async XLA Ops:
  0.6 42.0 %copy-start = (bf16[1024,512]{1,0:T(8,128)(2,1)S(1)}, bf16[1024,512]{1,0:T(8,128)(2,1)}, u32[]{:S(2)}) copy-start(bf16[1024,512]{1,0:T(8,128)(2,1)} %param.20) | copy-start | bytes 3145732
  1.6 8.9 %collective-permute-start = (bf16[1,192,256]{2,1,0:T(8,128)(2,1)S(1)}, bf16[1,192,256]{2,1,0:T(8,128)(2,1)S(1)}, u32[]{:S(2)}, u32[]{:S(2)}) collective-permute-start(bf16[1,192,256]{2,1,0:T(8,128)(2,1)S(1)} %dynamic-slice_bitcast_fusion.1), channel_id=1, source_target_pairs={{0,4},{1,5},{2,6},{3,7},{4,0},{5,1},{6,2},{7,3},{8,12},{9,13},{10,... | collective-permute-start | bytes 294920 | tf_op jit(solution)/shard_map/ppermute | solution.py:534
  11.3 49.9 %all-to-all-start = ((bf16[8,3,64,384]{3,2,1,0:T(8,128)(2,1)}), bf16[8,3,64,384]{3,2,1,0:T(8,128)(2,1)S(1)}, u32[]{:S(2)}, u32[]{:S(2)}) async-start(bf16[8,3,64,384]{3,2,1,0:T(8,128)(2,1)} %gate.4), calls=%async_computation | async-start | bytes 2359296 | tf_op jit(solution)/shard_map/all_to_all | solution.py:538
  17.2 24.2 %collective-permute-start.6 = (bf16[2,192,256]{2,1,0:T(8,128)(2,1)S(1)}, bf16[2,192,256]{2,1,0:T(8,128)(2,1)S(1)}, u32[]{:S(2)}, u32[]{:S(2)}) collective-permute-start(bf16[2,192,256]{2,1,0:T(8,128)(2,1)S(1)} %copy-done.10), channel_id=1, source_target_pairs={{0,2},{1,3},{2,0},{3,1},{4,6},{5,7},{6,4},{7,5},{8,10},{9,11},{10,... | collective-permute-start | bytes 589832 | tf_op jit(solution)/shard_map/ppermute | solution.py:534
  41.4 12.2 %collective-permute-start.7 = (bf16[4,192,256]{2,1,0:T(8,128)(2,1)S(1)}, bf16[4,192,256]{2,1,0:T(8,128)(2,1)}, u32[]{:S(2)}, u32[]{:S(2)}) collective-permute-start(bf16[4,192,256]{2,1,0:T(8,128)(2,1)S(1)} %pad_maximum_fusion.1), channel_id=1, source_target_pairs={{0,1},{1,0},{2,3},{3,2},{4,5},{5,4},{6,7},{7,6},{8,9},{9,8},{10,11... | collective-permute-start | bytes 1179656 | tf_op jit(solution)/shard_map/ppermute | solution.py:534
  42.6 17.8 %copy-start.15 = (bf16[1,512,256]{2,1,0:T(8,128)(2,1)}, bf16[1,512,256]{2,1,0:T(8,128)(2,1)S(1)}, u32[]{:S(2)}) copy-start(bf16[1,512,256]{2,1,0:T(8,128)(2,1)S(1)} %dynamic-slice_bitcast_fusion.refs_5_) | copy-start | bytes 786436
  42.6 15.2 %collective-permute-start.1 = (bf16[1,512,256]{2,1,0:T(8,128)(2,1)S(1)}, bf16[1,512,256]{2,1,0:T(8,128)(2,1)S(1)}, u32[]{:S(2)}, u32[]{:S(2)}) collective-permute-start(bf16[1,512,256]{2,1,0:T(8,128)(2,1)S(1)} %dynamic-slice_bitcast_fusion.refs_5_), channel_id=1, source_target_pairs={{0,4},{1,5},{2,6},{3,7},{4,0},{5,1},{6,2},{7,3},{8,12},{9,13},{10,... | collective-permute-start | bytes 786440 | tf_op jit(solution)/shard_map/ppermute | solution.py:534
  47.0 10.8 %collective-permute-start.9 = (bf16[1,512,256]{2,1,0:T(8,128)(2,1)S(1)}, bf16[1,512,256]{2,1,0:T(8,128)(2,1)}, u32[]{:S(2)}, u32[]{:S(2)}) collective-permute-start(bf16[1,512,256]{2,1,0:T(8,128)(2,1)S(1)} %dynamic-slice_bitcast_fusion.refs_5_), channel_id=1, source_target_pairs={{0,1},{1,0},{2,3},{3,2},{4,5},{5,4},{6,7},{7,6},{8,9},{9,8},{10,11... | collective-permute-start | bytes 786440 | tf_op jit(solution)/shard_map/ppermute | solution.py:534
  47.6 10.2 %collective-permute-start.10 = (bf16[1,512,256]{2,1,0:T(8,128)(2,1)S(1)}, bf16[1,512,256]{2,1,0:T(8,128)(2,1)S(1)}, u32[]{:S(2)}, u32[]{:S(2)}) collective-permute-start(bf16[1,512,256]{2,1,0:T(8,128)(2,1)S(1)} %dynamic-slice_bitcast_fusion.refs_5_), channel_id=1, source_target_pairs={{0,16},{16,0},{1,17},{17,1},{2,18},{18,2},{3,19},{19,3},{4,20},{20... | collective-permute-start | bytes 786440 | tf_op jit(solution)/shard_map/ppermute | solution.py:530
  49.1 11.3 %collective-permute-start.3 = (bf16[1,512,256]{2,1,0:T(8,128)(2,1)S(1)}, bf16[1,512,256]{2,1,0:T(8,128)(2,1)S(1)}, u32[]{:S(2)}, u32[]{:S(2)}) collective-permute-start(bf16[1,512,256]{2,1,0:T(8,128)(2,1)S(1)} %dynamic-slice_bitcast_fusion.refs_5_), channel_id=1, source_target_pairs={{0,2},{1,3},{2,0},{3,1},{4,6},{5,7},{6,4},{7,5},{8,10},{9,11},{10,... | collective-permute-start | bytes 786440 | tf_op jit(solution)/shard_map/ppermute | solution.py:534
  61.1 32.8 %all-to-all-start.2 = ((bf16[8,3,64,384]{3,2,1,0:T(8,128)(2,1)}), bf16[8,3,64,384]{3,2,1,0:T(8,128)(2,1)S(1)}, u32[]{:S(2)}, u32[]{:S(2)}) async-start(bf16[8,3,64,384]{3,2,1,0:T(8,128)(2,1)} %gate.6), calls=%async_computation.2 | async-start | bytes 2359296 | tf_op jit(solution)/shard_map/all_to_all | solution.py:538
  64.7 29.2 %collective-permute-start.8 = (bf16[8,192,256]{2,1,0:T(8,128)(2,1)}, bf16[8,192,256]{2,1,0:T(8,128)(2,1)}, u32[]{:S(2)}, u32[]{:S(2)}) collective-permute-start(bf16[8,192,256]{2,1,0:T(8,128)(2,1)} %pad_maximum_fusion.refs_1_.refs_6_), channel_id=1, source_target_pairs={{0,16},{16,0},{1,17},{17,1},{2,18},{18,2},{3,19},{19,3},{4,20},{20... | collective-permute-start | bytes 2359304 | tf_op jit(solution)/shard_map/ppermute | solution.py:530
  67.5 10.1 %copy-start.18 = (bf16[2,512,256]{2,1,0:T(8,128)(2,1)}, bf16[2,512,256]{2,1,0:T(8,128)(2,1)S(1)}, u32[]{:S(2)}) copy-start(bf16[2,512,256]{2,1,0:T(8,128)(2,1)S(1)} %constant_dynamic-update-slice_fusion.refs_9_) | copy-start | bytes 1572868
  67.6 22.2 %collective-permute-start.4 = (bf16[2,512,256]{2,1,0:T(8,128)(2,1)S(1)}, bf16[2,512,256]{2,1,0:T(8,128)(2,1)S(1)}, u32[]{:S(2)}, u32[]{:S(2)}) collective-permute-start(bf16[2,512,256]{2,1,0:T(8,128)(2,1)S(1)} %constant_dynamic-update-slice_fusion.refs_9_), channel_id=1, source_target_pairs={{0,1},{1,0},{2,3},{3,2},{4,5},{5,4},{6,7},{7,6},{8,9},{9,8},{10,11... | collective-permute-start | bytes 1572872 | tf_op jit(solution)/shard_map/ppermute | solution.py:534
  69.6 24.3 %collective-permute-start.5 = (bf16[2,512,256]{2,1,0:T(8,128)(2,1)S(1)}, bf16[2,512,256]{2,1,0:T(8,128)(2,1)}, u32[]{:S(2)}, u32[]{:S(2)}) collective-permute-start(bf16[2,512,256]{2,1,0:T(8,128)(2,1)S(1)} %constant_dynamic-update-slice_fusion.refs_9_), channel_id=1, source_target_pairs={{0,16},{16,0},{1,17},{17,1},{2,18},{18,2},{3,19},{19,3},{4,20},{20... | collective-permute-start | bytes 1572872 | tf_op jit(solution)/shard_map/ppermute | solution.py:530
  70.7 17.6 %collective-permute-start.2 = (bf16[1,512,256]{2,1,0:T(8,128)(2,1)}, bf16[1,512,256]{2,1,0:T(8,128)(2,1)}, u32[]{:S(2)}, u32[]{:S(2)}) collective-permute-start(bf16[1,512,256]{2,1,0:T(8,128)(2,1)} %copy-done.8), channel_id=1, source_target_pairs={{0,2},{1,3},{2,0},{3,1},{4,6},{5,7},{6,4},{7,5},{8,10},{9,11},{10,... | collective-permute-start | bytes 786440 | tf_op jit(solution)/shard_map/ppermute | solution.py:534
  78.4 25.2 %copy-start.6 = (bf16[8,192,256]{2,1,0:T(8,128)(2,1)S(1)}, bf16[8,192,256]{2,1,0:T(8,128)(2,1)}, u32[]{:S(2)}) copy-start(bf16[8,192,256]{2,1,0:T(8,128)(2,1)} %pad_maximum_fusion.refs_1_.refs_6_) | copy-start | bytes 2359300
  94.0 17.2 %all-to-all-start.1 = ((bf16[8,64,384]{2,1,0:T(8,128)(2,1)}), bf16[8,64,384]{2,1,0:T(8,128)(2,1)}, u32[]{:S(2)}, u32[]{:S(2)}) async-start(bf16[8,64,384]{2,1,0:T(8,128)(2,1)} %gate.5), calls=%async_computation.1 | async-start | bytes 786432 | tf_op jit(solution)/shard_map/all_to_all | solution.py:538
  99.6 10.8 %collective-permute-start.13 = (bf16[1,512,256]{2,1,0:T(8,128)(2,1)}, bf16[1,512,256]{2,1,0:T(8,128)(2,1)S(1)}, u32[]{:S(2)}, u32[]{:S(2)}) collective-permute-start(bf16[1,512,256]{2,1,0:T(8,128)(2,1)} %collective-permute-done.9.refs_4_.refs_7_), channel_id=1, source_target_pairs={{0,16},{16,0},{1,17},{17,1},{2,18},{18,2},{3,19},{19,3},{4,20},{20... | collective-permute-start | bytes 786440 | tf_op jit(solution)/shard_map/ppermute | solution.py:530
  100.3 10.1 %collective-permute-start.12 = (bf16[1,512,256]{2,1,0:T(8,128)(2,1)}, bf16[1,512,256]{2,1,0:T(8,128)(2,1)S(1)}, u32[]{:S(2)}, u32[]{:S(2)}) collective-permute-start(bf16[1,512,256]{2,1,0:T(8,128)(2,1)} %collective-permute-done.2.refs_1_.refs_13_), channel_id=1, source_target_pairs={{0,16},{16,0},{1,17},{17,1},{2,18},{18,2},{3,19},{19,3},{4,20},{20... | collective-permute-start | bytes 786440 | tf_op jit(solution)/shard_map/ppermute | solution.py:530
  101.6 8.8 %collective-permute-start.11 = (bf16[1,512,256]{2,1,0:T(8,128)(2,1)}, bf16[1,512,256]{2,1,0:T(8,128)(2,1)}, u32[]{:S(2)}, u32[]{:S(2)}) collective-permute-start(bf16[1,512,256]{2,1,0:T(8,128)(2,1)} %collective-permute-done.2.refs_1_.refs_13_), channel_id=1, source_target_pairs={{0,1},{1,0},{2,3},{3,2},{4,5},{5,4},{6,7},{7,6},{8,9},{9,8},{10,11... | collective-permute-start | bytes 786440 | tf_op jit(solution)/shard_map/ppermute | solution.py:534
  103.6 25.8 %collective-permute-start.14 = (bf16[8,192,256]{2,1,0:T(8,128)(2,1)S(1)}, bf16[8,192,256]{2,1,0:T(8,128)(2,1)}, u32[]{:S(2)}, u32[]{:S(2)}) collective-permute-start(bf16[8,192,256]{2,1,0:T(8,128)(2,1)S(1)} %copy-done.6), channel_id=1, source_target_pairs={{0,8},{8,0},{1,9},{9,1},{2,10},{10,2},{3,11},{11,3},{4,12},{12,4},... | collective-permute-start | bytes 2359304 | tf_op jit(solution)/shard_map/ppermute | solution.py:530
  103.6 25.8 %collective-permute-start.15 = (bf16[8,192,256]{2,1,0:T(8,128)(2,1)}, bf16[8,192,256]{2,1,0:T(8,128)(2,1)}, u32[]{:S(2)}, u32[]{:S(2)}) collective-permute-start(bf16[8,192,256]{2,1,0:T(8,128)(2,1)} %collective-permute-done.8.refs_4_.refs_7_), channel_id=1, source_target_pairs={{0,8},{8,0},{1,9},{9,1},{2,10},{10,2},{3,11},{11,3},{4,12},{12,4},... | collective-permute-start | bytes 2359304 | tf_op jit(solution)/shard_map/ppermute | solution.py:530
  111.2 18.3 %all-to-all-start.3 = ((bf16[8,64,384]{2,1,0:T(8,128)(2,1)}), bf16[8,64,384]{2,1,0:T(8,128)(2,1)S(1)}, u32[]{:S(2)}, u32[]{:S(2)}) async-start(bf16[8,64,384]{2,1,0:T(8,128)(2,1)} %gate.7), calls=%async_computation.3 | async-start | bytes 786432 | tf_op jit(solution)/shard_map/all_to_all | solution.py:538
  116.7 12.7 %collective-permute-start.16 = (bf16[2,512,256]{2,1,0:T(8,128)(2,1)S(1)}, bf16[2,512,256]{2,1,0:T(8,128)(2,1)}, u32[]{:S(2)}, u32[]{:S(2)}) collective-permute-start(bf16[2,512,256]{2,1,0:T(8,128)(2,1)S(1)} %copy-done.12), channel_id=1, source_target_pairs={{0,16},{16,0},{1,17},{17,1},{2,18},{18,2},{3,19},{19,3},{4,20},{20... | collective-permute-start | bytes 1572872 | tf_op jit(solution)/shard_map/ppermute | solution.py:530
  117.2 10.8 %collective-permute-start.17 = (bf16[1,512,256]{2,1,0:T(8,128)(2,1)}, bf16[1,512,256]{2,1,0:T(8,128)(2,1)S(1)}, u32[]{:S(2)}, u32[]{:S(2)}) collective-permute-start(bf16[1,512,256]{2,1,0:T(8,128)(2,1)} %copy-done.17), channel_id=1, source_target_pairs={{0,1},{1,0},{2,3},{3,2},{4,5},{5,4},{6,7},{7,6},{8,9},{9,8},{10,11... | collective-permute-start | bytes 786440 | tf_op jit(solution)/shard_map/ppermute | solution.py:534
  138.0 2.2 %collective-permute-start.19 = (bf16[2,256,512]{2,1,0:T(8,128)(2,1)}, bf16[2,256,512]{2,1,0:T(8,128)(2,1)S(1)}, u32[]{:S(2)}, u32[]{:S(2)}) collective-permute-start(bf16[2,256,512]{2,1,0:T(8,128)(2,1)} %get-tuple-element.11.refs_3_), channel_id=1, source_target_pairs={{0,8},{8,0},{1,9},{9,1},{2,10},{10,2},{3,11},{11,3},{4,12},{12,4},... | collective-permute-start | bytes 1572872 | tf_op jit(solution)/shard_map/ppermute | solution.py:530
  138.0 15.9 %collective-permute-start.18 = (bf16[4,64,1536]{2,1,0:T(8,128)(2,1)}, bf16[4,64,1536]{2,1,0:T(8,128)(2,1)S(1)}, u32[]{:S(2)}, u32[]{:S(2)}) collective-permute-start(bf16[4,64,1536]{2,1,0:T(8,128)(2,1)} %get-tuple-element.10.own_ref), channel_id=1, source_target_pairs={{0,8},{8,0},{1,9},{9,1},{2,10},{10,2},{3,11},{11,3},{4,12},{12,4},... | collective-permute-start | bytes 2359304 | tf_op jit(solution)/shard_map/ppermute | solution.py:530
  140.9 13.0 %copy-start.3 = (bf16[4,64,1536]{2,1,0:T(8,128)(2,1)S(1)}, bf16[4,64,1536]{2,1,0:T(8,128)(2,1)}, u32[]{:S(2)}) copy-start(bf16[4,64,1536]{2,1,0:T(8,128)(2,1)} %get-tuple-element.10.own_ref) | copy-start | bytes 2359300
  140.9 13.0 %copy-start.4 = (s32[4]{0:T(128)S(1)}, s32[4]{0:T(128)}, u32[]{:S(2)}) copy-start(s32[4]{0:T(128)} %pad_add_fusion.refs_0_.ids_ref) | copy-start | bytes 52
  141.0 13.1 %copy-start.5 = (s32[4]{0:T(128)S(1)}, s32[4]{0:T(128)}, u32[]{:S(2)}) copy-start(s32[4]{0:T(128)} %ancestors_ref.1) | copy-start | bytes 52
  148.2 12.5 %all-to-all-start.4 = ((f32[16,8,128]{2,1,0:T(8,128)}), f32[16,8,128]{2,1,0:T(8,128)S(1)}, u32[]{:S(2)}, u32[]{:S(2)}) async-start(f32[16,8,128]{2,1,0:T(8,128)} %reward.1), calls=%async_computation.4 | async-start | bytes 131072 | tf_op jit(solution)/shard_map/all_to_all | solution.py:667
  (13 other events, 28.4 us)

commit v19 on v18

--- a/solution.py
+++ b/solution.py
@@ -318,7 +318,7 @@
     count = parts * columns
     out_depth = model_width * len(attended) // chunks
     pieces = ([] if begun is None else [begun]) + attended
-    joined = 2 if columns % LANES == 0 and parts % 2 == 0 else 1
+    joined = next(n for n in (4, 2, 1) if n == 1 or columns % LANES == 0 == parts % n)
     vmem = pl.BlockSpec(memory_space=pltpu.VMEM)
     smem = pl.BlockSpec(memory_space=pltpu.SMEM)
     hbm = pl.BlockSpec(memory_space=pltpu.HBM)

time: 163 us -> 163 us (level)
  no operation moved by 1% of the time
where the time goes in v19:
time: 163 us; the launch traced here: 162 us
  waiting for transfers between devices  59.3 us (36%)
  starting transfers between devices  53.2 us (33%)
  Pallas kernels  36.9 us (23%)
  local copies, waits for them, and re-layouts  7.57 us (5%)
  other arithmetic  3.3 us (2%)
    ppermute x10, waiting for transfers between devices, swapped(): lax.ppermute(array, axis, [(i, i ^ bit) for i in range(lax.axis_size(axis...  47.4 us
    all_to_all x4, starting transfers between devices, exchange(): return lax.all_to_all(array, 'seq', 0, 0, tiled=True)  20.6 us
    ppermute x10, starting transfers between devices, swapped(): lax.ppermute(array, axis, [(i, i ^ bit) for i in range(lax.axis_size(axis...  19.8 us
    pallas_call x2, Pallas kernels, attention(): pl.pallas_call(functools.partial(attention_kernel, head_width, block_sour...  11 us
    pallas_call x1, Pallas kernels, project_embed(): pl.pallas_call(kernel, in_specs=[smem, hbm, vmem, hbm] + ([] if begun is...  7.52 us
    pallas_call x1, Pallas kernels, reward(): pl.pallas_call(functools.partial(reward_kernel, particles, scale, parts,...  7.23 us
    ppermute x10, waiting for transfers between devices, shifted(): lax.ppermute(array, axis, [(i, (i + step) % count) for i in range(count)])  7.15 us
    ppermute x10, starting transfers between devices, shifted(): lax.ppermute(array, axis, [(i, (i + step) % count) for i in range(count)])  7.02 us
  transfers between devices with their start and end apart: 25, of which 12 were waited for; matrix products, arithmetic and copies ran while one was open for 3% of the time, Pallas kernels for 17%

profile of v19, /device:TPU:0, one launch (start us, length us, event | category | flops | bytes accessed | tf_op | source)
XLA Modules:
  0.0 161.8 jit_solution(6132924119527046019)
XLA Ops:
  1.6 4.0 %collective-permute-start = (bf16[1,192,256]{2,1,0:T(8,128)(2,1)S(1)}, bf16[1,192,256]{2,1,0:T(8,128)(2,1)S(1)}, u32[]{:S(2)}, u32[]{:S(2)}) collective-permute-start(bf16[1,192,256]{2,1,0:T(8,128)(2,1)S(1)} %dynamic-slice_bitcast_fusion.1), channel_id=1, source_target_pairs={{0,4},{1,5},{2,6},{3,7},{4,0},{5,1},{6,2},{7,3},{8,12},{9,13},{10,... | collective-permute-start | bytes 294920 | tf_op jit(solution)/shard_map/ppermute | solution.py:534
  5.7 3.2 %pack_heads.1 = (bf16[8,3,64,384]{3,2,1,0:T(8,128)(2,1)}, bf16[8,3,64,384]{3,2,1,0:T(8,128)(2,1)}) custom-call(bf16[4,64,1536]{2,1,0:T(8,128)(2,1)} %q_ref.1, bf16[4,64,1536]{2,1,0:T(8,128)(2,1)} %k_ref.1, bf16[4,64,1536]{2,1,0:T(8,128)(2,1)} %v_ref.1), custom_call_target="tpu_custom_call" | custom-call | tf_op jit(solution)/shard_map/pack_heads/pallas_call | solution.py:40
  8.9 1.7 %collective-permute-done = bf16[1,192,256]{2,1,0:T(8,128)(2,1)S(1)} collective-permute-done((bf16[1,192,256]{2,1,0:T(8,128)(2,1)S(1)}, bf16[1,192,256]{2,1,0:T(8,128)(2,1)S(1)}, u32[]{:S(2)}, u32[]{:S(2)}) %collective-permute-start) | collective-permute-done | bytes 98336 | tf_op jit(solution)/shard_map/ppermute | solution.py:534
  11.3 5.9 %all-to-all-start = ((bf16[8,3,64,384]{3,2,1,0:T(8,128)(2,1)}), bf16[8,3,64,384]{3,2,1,0:T(8,128)(2,1)S(1)}, u32[]{:S(2)}, u32[]{:S(2)}) async-start(bf16[8,3,64,384]{3,2,1,0:T(8,128)(2,1)} %gate.4), calls=%async_computation | async-start | bytes 2359296 | tf_op jit(solution)/shard_map/all_to_all | solution.py:538
  17.2 2.0 %collective-permute-start.6 = (bf16[2,192,256]{2,1,0:T(8,128)(2,1)S(1)}, bf16[2,192,256]{2,1,0:T(8,128)(2,1)S(1)}, u32[]{:S(2)}, u32[]{:S(2)}) collective-permute-start(bf16[2,192,256]{2,1,0:T(8,128)(2,1)S(1)} %copy-done.10), channel_id=1, source_target_pairs={{0,2},{1,3},{2,0},{3,1},{4,6},{5,7},{6,4},{7,5},{8,10},{9,11},{10,... | collective-permute-start | bytes 589832 | tf_op jit(solution)/shard_map/ppermute | solution.py:534
  19.2 22.1 %collective-permute-done.6 = bf16[2,192,256]{2,1,0:T(8,128)(2,1)S(1)} collective-permute-done((bf16[2,192,256]{2,1,0:T(8,128)(2,1)S(1)}, bf16[2,192,256]{2,1,0:T(8,128)(2,1)S(1)}, u32[]{:S(2)}, u32[]{:S(2)}) %collective-permute-start.6) | collective-permute-done | bytes 196640 | tf_op jit(solution)/shard_map/ppermute | solution.py:534
  42.6 4.4 %collective-permute-start.1 = (bf16[1,512,256]{2,1,0:T(8,128)(2,1)S(1)}, bf16[1,512,256]{2,1,0:T(8,128)(2,1)S(1)}, u32[]{:S(2)}, u32[]{:S(2)}) collective-permute-start(bf16[1,512,256]{2,1,0:T(8,128)(2,1)S(1)} %dynamic-slice_bitcast_fusion.refs_5_), channel_id=1, source_target_pairs={{0,4},{1,5},{2,6},{3,7},{4,0},{5,1},{6,2},{7,3},{8,12},{9,13},{10,... | collective-permute-start | bytes 786440 | tf_op jit(solution)/shard_map/ppermute | solution.py:534
  47.6 1.5 collective-permute-start.10
  49.1 4.5 %collective-permute-done.7 = bf16[4,192,256]{2,1,0:T(8,128)(2,1)} collective-permute-done((bf16[4,192,256]{2,1,0:T(8,128)(2,1)S(1)}, bf16[4,192,256]{2,1,0:T(8,128)(2,1)}, u32[]{:S(2)}, u32[]{:S(2)}) %collective-permute-start.7) | collective-permute-done | bytes 393248 | tf_op jit(solution)/shard_map/ppermute | solution.py:534
  53.6 2.0 %pad_maximum_fusion.refs_1_.refs_6_ = bf16[8,192,256]{2,1,0:T(8,128)(2,1)} fusion(bf16[4,192,256]{2,1,0:T(8,128)(2,1)} %collective-permute-done.7, bf16[2,192,256]{2,1,0:T(8,128)(2,1)S(1)} %collective-permute-done.6, bf16[1,192,256]{2,1,0:T(8,128)(2,1)S(1)} %collective-permute-done, bf16[1,192,256]{2,1,0:T(8,128)(2,1)S(1)} %dynamic-slice_bitcast_fusion.1), kind=kLoop, calls=%fused_computation | loop fusion | flops 1179648 | bytes 1572864 | tf_op jit(solution)/shard_map/concatenate | solution.py:597
  55.6 2.3 %collective-permute-done.1.refs_2_ = bf16[1,512,256]{2,1,0:T(8,128)(2,1)S(1)} collective-permute-done((bf16[1,512,256]{2,1,0:T(8,128)(2,1)S(1)}, bf16[1,512,256]{2,1,0:T(8,128)(2,1)S(1)}, u32[]{:S(2)}, u32[]{:S(2)}) %collective-permute-start.1) | collective-permute-done | bytes 262176 | tf_op jit(solution)/shard_map/ppermute | solution.py:534
  57.9 2.6 %collective-permute-done.3.refs_3_ = bf16[1,512,256]{2,1,0:T(8,128)(2,1)S(1)} collective-permute-done((bf16[1,512,256]{2,1,0:T(8,128)(2,1)S(1)}, bf16[1,512,256]{2,1,0:T(8,128)(2,1)S(1)}, u32[]{:S(2)}, u32[]{:S(2)}) %collective-permute-start.3) | collective-permute-done | bytes 262176 | tf_op jit(solution)/shard_map/ppermute | solution.py:534
  61.1 3.6 %all-to-all-start.2 = ((bf16[8,3,64,384]{3,2,1,0:T(8,128)(2,1)}), bf16[8,3,64,384]{3,2,1,0:T(8,128)(2,1)S(1)}, u32[]{:S(2)}, u32[]{:S(2)}) async-start(bf16[8,3,64,384]{3,2,1,0:T(8,128)(2,1)} %gate.6), calls=%async_computation.2 | async-start | bytes 2359296 | tf_op jit(solution)/shard_map/all_to_all | solution.py:538
  67.6 2.1 %collective-permute-start.4 = (bf16[2,512,256]{2,1,0:T(8,128)(2,1)S(1)}, bf16[2,512,256]{2,1,0:T(8,128)(2,1)S(1)}, u32[]{:S(2)}, u32[]{:S(2)}) collective-permute-start(bf16[2,512,256]{2,1,0:T(8,128)(2,1)S(1)} %constant_dynamic-update-slice_fusion.refs_9_), channel_id=1, source_target_pairs={{0,1},{1,0},{2,3},{3,2},{4,5},{5,4},{6,7},{7,6},{8,9},{9,8},{10,11... | collective-permute-start | bytes 1572872 | tf_op jit(solution)/shard_map/ppermute | solution.py:534
  70.7 1.5 collective-permute-start.2
  72.1 5.5 %attention.2.refs_0_ = bf16[8,64,384]{2,1,0:T(8,128)(2,1)S(1)} custom-call(bf16[8,3,64,384]{3,2,1,0:T(8,128)(2,1)S(1)} %all-to-all-done.qkv_ref), custom_call_target="tpu_custom_call" | custom-call | flops 402653184 | bytes 1572864 | tf_op jit(solution)/shard_map/attention/pallas_call | solution.py:104
  78.4 9.8 %collective-permute-done.2.refs_1_.refs_13_ = bf16[1,512,256]{2,1,0:T(8,128)(2,1)} collective-permute-done((bf16[1,512,256]{2,1,0:T(8,128)(2,1)}, bf16[1,512,256]{2,1,0:T(8,128)(2,1)}, u32[]{:S(2)}, u32[]{:S(2)}) %collective-permute-start.2) | collective-permute-done | bytes 262176 | tf_op jit(solution)/shard_map/ppermute | solution.py:534
  88.2 1.6 collective-permute-done.4.refs_2_.refs_11_
  89.8 4.1 %collective-permute-done.5.refs_3_.refs_10_ = bf16[2,512,256]{2,1,0:T(8,128)(2,1)} collective-permute-done((bf16[2,512,256]{2,1,0:T(8,128)(2,1)S(1)}, bf16[2,512,256]{2,1,0:T(8,128)(2,1)}, u32[]{:S(2)}, u32[]{:S(2)}) %collective-permute-start.5) | collective-permute-done | bytes 524320 | tf_op jit(solution)/shard_map/ppermute | solution.py:530
  94.0 5.6 %all-to-all-start.1 = ((bf16[8,64,384]{2,1,0:T(8,128)(2,1)}), bf16[8,64,384]{2,1,0:T(8,128)(2,1)}, u32[]{:S(2)}, u32[]{:S(2)}) async-start(bf16[8,64,384]{2,1,0:T(8,128)(2,1)} %gate.5), calls=%async_computation.1 | async-start | bytes 786432 | tf_op jit(solution)/shard_map/all_to_all | solution.py:538
  101.6 2.0 %collective-permute-start.11 = (bf16[1,512,256]{2,1,0:T(8,128)(2,1)}, bf16[1,512,256]{2,1,0:T(8,128)(2,1)}, u32[]{:S(2)}, u32[]{:S(2)}) collective-permute-start(bf16[1,512,256]{2,1,0:T(8,128)(2,1)} %collective-permute-done.2.refs_1_.refs_13_), channel_id=1, source_target_pairs={{0,1},{1,0},{2,3},{3,2},{4,5},{5,4},{6,7},{7,6},{8,9},{9,8},{10,11... | collective-permute-start | bytes 786440 | tf_op jit(solution)/shard_map/ppermute | solution.py:534
  104.1 5.5 %attention.3.refs_0_ = bf16[8,64,384]{2,1,0:T(8,128)(2,1)S(1)} custom-call(bf16[8,3,64,384]{3,2,1,0:T(8,128)(2,1)S(1)} %all-to-all-done.2.qkv_ref), custom_call_target="tpu_custom_call" | custom-call | flops 402653184 | bytes 1572864 | tf_op jit(solution)/shard_map/attention/pallas_call | solution.py:104
  111.2 5.6 %all-to-all-start.3 = ((bf16[8,64,384]{2,1,0:T(8,128)(2,1)}), bf16[8,64,384]{2,1,0:T(8,128)(2,1)S(1)}, u32[]{:S(2)}, u32[]{:S(2)}) async-start(bf16[8,64,384]{2,1,0:T(8,128)(2,1)} %gate.7), calls=%async_computation.3 | async-start | bytes 786432 | tf_op jit(solution)/shard_map/all_to_all | solution.py:538
  117.2 2.0 %collective-permute-start.17 = (bf16[1,512,256]{2,1,0:T(8,128)(2,1)}, bf16[1,512,256]{2,1,0:T(8,128)(2,1)S(1)}, u32[]{:S(2)}, u32[]{:S(2)}) collective-permute-start(bf16[1,512,256]{2,1,0:T(8,128)(2,1)} %copy-done.17), channel_id=1, source_target_pairs={{0,1},{1,0},{2,3},{3,2},{4,5},{5,4},{6,7},{7,6},{8,9},{9,8},{10,11... | collective-permute-start | bytes 786440 | tf_op jit(solution)/shard_map/ppermute | solution.py:534
  120.5 4.7 %first_project.1.refs_4_ = f32[256,1536]{1,0:T(8,128)} custom-call(bf16[4,64,1536]{2,1,0:T(8,128)(2,1)} %refs_1_.2, bf16[1536,1536]{1,0:T(8,128)(2,1)} %refs_3_.1, bf16[8,64,384]{2,1,0:T(8,128)(2,1)} %all-to-all-done.1.piece_ref), custom_call_target="tpu_custom_call" | custom-call | flops 603979776 | bytes 5505024 | tf_op jit(solution)/shard_map/first_project/pallas_call | solution.py:181
  125.2 2.9 %collective-permute-done.17.refs_11_.refs_16_ = bf16[1,512,256]{2,1,0:T(8,128)(2,1)S(1)} collective-permute-done((bf16[1,512,256]{2,1,0:T(8,128)(2,1)}, bf16[1,512,256]{2,1,0:T(8,128)(2,1)S(1)}, u32[]{:S(2)}, u32[]{:S(2)}) %collective-permute-start.17) | collective-permute-done | bytes 262176 | tf_op jit(solution)/shard_map/ppermute | solution.py:534
  130.3 7.5 %project_embed.1 = (bf16[4,64,1536]{2,1,0:T(8,128)(2,1)}, bf16[2,256,512]{2,1,0:T(8,128)(2,1)}) custom-call(s32[4]{0:T(128)} %pad_add_fusion.refs_0_.ids_ref, bf16[4,64,1536]{2,1,0:T(8,128)(2,1)} %refs_1_.2, f32[1,1024]{1,0:T(1,128)} %bitcast.10, bf16[1536,1536]{1,0:T(8,128)(2,1)} %refs_3_.1, f32[256,1536]{1,0:T(8,128)} %first_project.1.refs_4_, ...), custom_call_target="tpu_custom_call" | custom-call | flops 1409286144 | bytes 10223616 | tf_op jit(solution)/shard_map/project_embed/pallas_call | solution.py:340
  138.4 1.6 collective-permute-done.19.refs_4_
  140.8 7.2 %reward.1 = f32[16,8,128]{2,1,0:T(8,128)} custom-call(s32[4]{0:T(128)} %pad_add_fusion.refs_0_.ids_ref, f32[4]{0:T(128)} %refs_1_.3, f32[16,1,256]{2,1,0:T(1,128)} %bitcast.11, bf16[2,256,512]{2,1,0:T(8,128)(2,1)} %get-tuple-element.11.refs_3_, bf16[2,256,512]{2,1,0:T(8,128)(2,1)} %copy-done.19, bf16[1,512,256]{2,1,0:T(8,128)(2,1)} %copy-done.15, ...), custom_call_target="tpu_custom_call" | custom-call | flops 2147483648 | bytes 4194304 | tf_op jit(solution)/shard_map/reward/pallas_call | solution.py:445
  148.0 5.8 %all-to-all-start.4 = ((f32[16,8,128]{2,1,0:T(8,128)}), f32[16,8,128]{2,1,0:T(8,128)S(1)}, u32[]{:S(2)}, u32[]{:S(2)}) async-start(f32[16,8,128]{2,1,0:T(8,128)} %reward.1), calls=%async_computation.4 | async-start | bytes 131072 | tf_op jit(solution)/shard_map/all_to_all | solution.py:667
  153.8 2.0 %resample.1.resampled_ref = bf16[4,64,1536]{2,1,0:T(8,128)(2,1)} custom-call(s32[4]{0:T(128)S(1)} %copy-done.4, s32[4]{0:T(128)S(1)} %copy-done.5, bf16[4,64,1536]{2,1,0:T(8,128)(2,1)S(1)} %copy-done.3, bf16[4,64,1536]{2,1,0:T(8,128)(2,1)S(1)} %collective-permute-done.18.other_ref), custom_call_target="tpu_custom_call" | custom-call | tf_op jit(solution)/shard_map/resample/pallas_call | solution.py:514
  155.9 4.7 %all-to-all-done.4.parts_ref = f32[16,8,128]{2,1,0:T(8,128)S(1)} async-done(((f32[16,8,128]{2,1,0:T(8,128)}), f32[16,8,128]{2,1,0:T(8,128)S(1)}, u32[]{:S(2)}, u32[]{:S(2)}) %all-to-all-start.4) | async-done | bytes 65568 | tf_op jit(solution)/shard_map/all_to_all | solution.py:667
  (78 shorter events, 18.9 us)
Async XLA Ops:
  0.6 42.0 %copy-start = (bf16[1024,512]{1,0:T(8,128)(2,1)S(1)}, bf16[1024,512]{1,0:T(8,128)(2,1)}, u32[]{:S(2)}) copy-start(bf16[1024,512]{1,0:T(8,128)(2,1)} %param.20) | copy-start | bytes 3145732
  1.6 8.9 %collective-permute-start = (bf16[1,192,256]{2,1,0:T(8,128)(2,1)S(1)}, bf16[1,192,256]{2,1,0:T(8,128)(2,1)S(1)}, u32[]{:S(2)}, u32[]{:S(2)}) collective-permute-start(bf16[1,192,256]{2,1,0:T(8,128)(2,1)S(1)} %dynamic-slice_bitcast_fusion.1), channel_id=1, source_target_pairs={{0,4},{1,5},{2,6},{3,7},{4,0},{5,1},{6,2},{7,3},{8,12},{9,13},{10,... | collective-permute-start | bytes 294920 | tf_op jit(solution)/shard_map/ppermute | solution.py:534
  11.3 49.9 %all-to-all-start = ((bf16[8,3,64,384]{3,2,1,0:T(8,128)(2,1)}), bf16[8,3,64,384]{3,2,1,0:T(8,128)(2,1)S(1)}, u32[]{:S(2)}, u32[]{:S(2)}) async-start(bf16[8,3,64,384]{3,2,1,0:T(8,128)(2,1)} %gate.4), calls=%async_computation | async-start | bytes 2359296 | tf_op jit(solution)/shard_map/all_to_all | solution.py:538
  17.2 24.2 %collective-permute-start.6 = (bf16[2,192,256]{2,1,0:T(8,128)(2,1)S(1)}, bf16[2,192,256]{2,1,0:T(8,128)(2,1)S(1)}, u32[]{:S(2)}, u32[]{:S(2)}) collective-permute-start(bf16[2,192,256]{2,1,0:T(8,128)(2,1)S(1)} %copy-done.10), channel_id=1, source_target_pairs={{0,2},{1,3},{2,0},{3,1},{4,6},{5,7},{6,4},{7,5},{8,10},{9,11},{10,... | collective-permute-start | bytes 589832 | tf_op jit(solution)/shard_map/ppermute | solution.py:534
  41.4 12.2 %collective-permute-start.7 = (bf16[4,192,256]{2,1,0:T(8,128)(2,1)S(1)}, bf16[4,192,256]{2,1,0:T(8,128)(2,1)}, u32[]{:S(2)}, u32[]{:S(2)}) collective-permute-start(bf16[4,192,256]{2,1,0:T(8,128)(2,1)S(1)} %pad_maximum_fusion.1), channel_id=1, source_target_pairs={{0,1},{1,0},{2,3},{3,2},{4,5},{5,4},{6,7},{7,6},{8,9},{9,8},{10,11... | collective-permute-start | bytes 1179656 | tf_op jit(solution)/shard_map/ppermute | solution.py:534
  42.6 17.8 %copy-start.15 = (bf16[1,512,256]{2,1,0:T(8,128)(2,1)}, bf16[1,512,256]{2,1,0:T(8,128)(2,1)S(1)}, u32[]{:S(2)}) copy-start(bf16[1,512,256]{2,1,0:T(8,128)(2,1)S(1)} %dynamic-slice_bitcast_fusion.refs_5_) | copy-start | bytes 786436
  42.6 15.2 %collective-permute-start.1 = (bf16[1,512,256]{2,1,0:T(8,128)(2,1)S(1)}, bf16[1,512,256]{2,1,0:T(8,128)(2,1)S(1)}, u32[]{:S(2)}, u32[]{:S(2)}) collective-permute-start(bf16[1,512,256]{2,1,0:T(8,128)(2,1)S(1)} %dynamic-slice_bitcast_fusion.refs_5_), channel_id=1, source_target_pairs={{0,4},{1,5},{2,6},{3,7},{4,0},{5,1},{6,2},{7,3},{8,12},{9,13},{10,... | collective-permute-start | bytes 786440 | tf_op jit(solution)/shard_map/ppermute | solution.py:534
  47.0 10.8 %collective-permute-start.9 = (bf16[1,512,256]{2,1,0:T(8,128)(2,1)S(1)}, bf16[1,512,256]{2,1,0:T(8,128)(2,1)}, u32[]{:S(2)}, u32[]{:S(2)}) collective-permute-start(bf16[1,512,256]{2,1,0:T(8,128)(2,1)S(1)} %dynamic-slice_bitcast_fusion.refs_5_), channel_id=1, source_target_pairs={{0,1},{1,0},{2,3},{3,2},{4,5},{5,4},{6,7},{7,6},{8,9},{9,8},{10,11... | collective-permute-start | bytes 786440 | tf_op jit(solution)/shard_map/ppermute | solution.py:534
  47.6 10.2 %collective-permute-start.10 = (bf16[1,512,256]{2,1,0:T(8,128)(2,1)S(1)}, bf16[1,512,256]{2,1,0:T(8,128)(2,1)S(1)}, u32[]{:S(2)}, u32[]{:S(2)}) collective-permute-start(bf16[1,512,256]{2,1,0:T(8,128)(2,1)S(1)} %dynamic-slice_bitcast_fusion.refs_5_), channel_id=1, source_target_pairs={{0,16},{16,0},{1,17},{17,1},{2,18},{18,2},{3,19},{19,3},{4,20},{20... | collective-permute-start | bytes 786440 | tf_op jit(solution)/shard_map/ppermute | solution.py:530
  49.1 11.3 %collective-permute-start.3 = (bf16[1,512,256]{2,1,0:T(8,128)(2,1)S(1)}, bf16[1,512,256]{2,1,0:T(8,128)(2,1)S(1)}, u32[]{:S(2)}, u32[]{:S(2)}) collective-permute-start(bf16[1,512,256]{2,1,0:T(8,128)(2,1)S(1)} %dynamic-slice_bitcast_fusion.refs_5_), channel_id=1, source_target_pairs={{0,2},{1,3},{2,0},{3,1},{4,6},{5,7},{6,4},{7,5},{8,10},{9,11},{10,... | collective-permute-start | bytes 786440 | tf_op jit(solution)/shard_map/ppermute | solution.py:534
  61.1 32.8 %all-to-all-start.2 = ((bf16[8,3,64,384]{3,2,1,0:T(8,128)(2,1)}), bf16[8,3,64,384]{3,2,1,0:T(8,128)(2,1)S(1)}, u32[]{:S(2)}, u32[]{:S(2)}) async-start(bf16[8,3,64,384]{3,2,1,0:T(8,128)(2,1)} %gate.6), calls=%async_computation.2 | async-start | bytes 2359296 | tf_op jit(solution)/shard_map/all_to_all | solution.py:538
  64.7 29.2 %collective-permute-start.8 = (bf16[8,192,256]{2,1,0:T(8,128)(2,1)}, bf16[8,192,256]{2,1,0:T(8,128)(2,1)}, u32[]{:S(2)}, u32[]{:S(2)}) collective-permute-start(bf16[8,192,256]{2,1,0:T(8,128)(2,1)} %pad_maximum_fusion.refs_1_.refs_6_), channel_id=1, source_target_pairs={{0,16},{16,0},{1,17},{17,1},{2,18},{18,2},{3,19},{19,3},{4,20},{20... | collective-permute-start | bytes 2359304 | tf_op jit(solution)/shard_map/ppermute | solution.py:530
  67.5 10.1 %copy-start.18 = (bf16[2,512,256]{2,1,0:T(8,128)(2,1)}, bf16[2,512,256]{2,1,0:T(8,128)(2,1)S(1)}, u32[]{:S(2)}) copy-start(bf16[2,512,256]{2,1,0:T(8,128)(2,1)S(1)} %constant_dynamic-update-slice_fusion.refs_9_) | copy-start | bytes 1572868
  67.6 22.2 %collective-permute-start.4 = (bf16[2,512,256]{2,1,0:T(8,128)(2,1)S(1)}, bf16[2,512,256]{2,1,0:T(8,128)(2,1)S(1)}, u32[]{:S(2)}, u32[]{:S(2)}) collective-permute-start(bf16[2,512,256]{2,1,0:T(8,128)(2,1)S(1)} %constant_dynamic-update-slice_fusion.refs_9_), channel_id=1, source_target_pairs={{0,1},{1,0},{2,3},{3,2},{4,5},{5,4},{6,7},{7,6},{8,9},{9,8},{10,11... | collective-permute-start | bytes 1572872 | tf_op jit(solution)/shard_map/ppermute | solution.py:534
  69.6 24.3 %collective-permute-start.5 = (bf16[2,512,256]{2,1,0:T(8,128)(2,1)S(1)}, bf16[2,512,256]{2,1,0:T(8,128)(2,1)}, u32[]{:S(2)}, u32[]{:S(2)}) collective-permute-start(bf16[2,512,256]{2,1,0:T(8,128)(2,1)S(1)} %constant_dynamic-update-slice_fusion.refs_9_), channel_id=1, source_target_pairs={{0,16},{16,0},{1,17},{17,1},{2,18},{18,2},{3,19},{19,3},{4,20},{20... | collective-permute-start | bytes 1572872 | tf_op jit(solution)/shard_map/ppermute | solution.py:530
  70.7 17.6 %collective-permute-start.2 = (bf16[1,512,256]{2,1,0:T(8,128)(2,1)}, bf16[1,512,256]{2,1,0:T(8,128)(2,1)}, u32[]{:S(2)}, u32[]{:S(2)}) collective-permute-start(bf16[1,512,256]{2,1,0:T(8,128)(2,1)} %copy-done.8), channel_id=1, source_target_pairs={{0,2},{1,3},{2,0},{3,1},{4,6},{5,7},{6,4},{7,5},{8,10},{9,11},{10,... | collective-permute-start | bytes 786440 | tf_op jit(solution)/shard_map/ppermute | solution.py:534
  78.4 25.2 %copy-start.6 = (bf16[8,192,256]{2,1,0:T(8,128)(2,1)S(1)}, bf16[8,192,256]{2,1,0:T(8,128)(2,1)}, u32[]{:S(2)}) copy-start(bf16[8,192,256]{2,1,0:T(8,128)(2,1)} %pad_maximum_fusion.refs_1_.refs_6_) | copy-start | bytes 2359300
  94.0 17.2 %all-to-all-start.1 = ((bf16[8,64,384]{2,1,0:T(8,128)(2,1)}), bf16[8,64,384]{2,1,0:T(8,128)(2,1)}, u32[]{:S(2)}, u32[]{:S(2)}) async-start(bf16[8,64,384]{2,1,0:T(8,128)(2,1)} %gate.5), calls=%async_computation.1 | async-start | bytes 786432 | tf_op jit(solution)/shard_map/all_to_all | solution.py:538
  99.6 10.8 %collective-permute-start.13 = (bf16[1,512,256]{2,1,0:T(8,128)(2,1)}, bf16[1,512,256]{2,1,0:T(8,128)(2,1)S(1)}, u32[]{:S(2)}, u32[]{:S(2)}) collective-permute-start(bf16[1,512,256]{2,1,0:T(8,128)(2,1)} %collective-permute-done.9.refs_4_.refs_7_), channel_id=1, source_target_pairs={{0,16},{16,0},{1,17},{17,1},{2,18},{18,2},{3,19},{19,3},{4,20},{20... | collective-permute-start | bytes 786440 | tf_op jit(solution)/shard_map/ppermute | solution.py:530
  100.3 10.1 %collective-permute-start.12 = (bf16[1,512,256]{2,1,0:T(8,128)(2,1)}, bf16[1,512,256]{2,1,0:T(8,128)(2,1)S(1)}, u32[]{:S(2)}, u32[]{:S(2)}) collective-permute-start(bf16[1,512,256]{2,1,0:T(8,128)(2,1)} %collective-permute-done.2.refs_1_.refs_13_), channel_id=1, source_target_pairs={{0,16},{16,0},{1,17},{17,1},{2,18},{18,2},{3,19},{19,3},{4,20},{20... | collective-permute-start | bytes 786440 | tf_op jit(solution)/shard_map/ppermute | solution.py:530
  101.6 8.8 %collective-permute-start.11 = (bf16[1,512,256]{2,1,0:T(8,128)(2,1)}, bf16[1,512,256]{2,1,0:T(8,128)(2,1)}, u32[]{:S(2)}, u32[]{:S(2)}) collective-permute-start(bf16[1,512,256]{2,1,0:T(8,128)(2,1)} %collective-permute-done.2.refs_1_.refs_13_), channel_id=1, source_target_pairs={{0,1},{1,0},{2,3},{3,2},{4,5},{5,4},{6,7},{7,6},{8,9},{9,8},{10,11... | collective-permute-start | bytes 786440 | tf_op jit(solution)/shard_map/ppermute | solution.py:534
  103.6 25.8 %collective-permute-start.14 = (bf16[8,192,256]{2,1,0:T(8,128)(2,1)S(1)}, bf16[8,192,256]{2,1,0:T(8,128)(2,1)}, u32[]{:S(2)}, u32[]{:S(2)}) collective-permute-start(bf16[8,192,256]{2,1,0:T(8,128)(2,1)S(1)} %copy-done.6), channel_id=1, source_target_pairs={{0,8},{8,0},{1,9},{9,1},{2,10},{10,2},{3,11},{11,3},{4,12},{12,4},... | collective-permute-start | bytes 2359304 | tf_op jit(solution)/shard_map/ppermute | solution.py:530
  103.6 25.8 %collective-permute-start.15 = (bf16[8,192,256]{2,1,0:T(8,128)(2,1)}, bf16[8,192,256]{2,1,0:T(8,128)(2,1)}, u32[]{:S(2)}, u32[]{:S(2)}) collective-permute-start(bf16[8,192,256]{2,1,0:T(8,128)(2,1)} %collective-permute-done.8.refs_4_.refs_7_), channel_id=1, source_target_pairs={{0,8},{8,0},{1,9},{9,1},{2,10},{10,2},{3,11},{11,3},{4,12},{12,4},... | collective-permute-start | bytes 2359304 | tf_op jit(solution)/shard_map/ppermute | solution.py:530
  111.2 18.3 %all-to-all-start.3 = ((bf16[8,64,384]{2,1,0:T(8,128)(2,1)}), bf16[8,64,384]{2,1,0:T(8,128)(2,1)S(1)}, u32[]{:S(2)}, u32[]{:S(2)}) async-start(bf16[8,64,384]{2,1,0:T(8,128)(2,1)} %gate.7), calls=%async_computation.3 | async-start | bytes 786432 | tf_op jit(solution)/shard_map/all_to_all | solution.py:538
  116.7 12.7 %collective-permute-start.16 = (bf16[2,512,256]{2,1,0:T(8,128)(2,1)S(1)}, bf16[2,512,256]{2,1,0:T(8,128)(2,1)}, u32[]{:S(2)}, u32[]{:S(2)}) collective-permute-start(bf16[2,512,256]{2,1,0:T(8,128)(2,1)S(1)} %copy-done.12), channel_id=1, source_target_pairs={{0,16},{16,0},{1,17},{17,1},{2,18},{18,2},{3,19},{19,3},{4,20},{20... | collective-permute-start | bytes 1572872 | tf_op jit(solution)/shard_map/ppermute | solution.py:530
  117.2 10.8 %collective-permute-start.17 = (bf16[1,512,256]{2,1,0:T(8,128)(2,1)}, bf16[1,512,256]{2,1,0:T(8,128)(2,1)S(1)}, u32[]{:S(2)}, u32[]{:S(2)}) collective-permute-start(bf16[1,512,256]{2,1,0:T(8,128)(2,1)} %copy-done.17), channel_id=1, source_target_pairs={{0,1},{1,0},{2,3},{3,2},{4,5},{5,4},{6,7},{7,6},{8,9},{9,8},{10,11... | collective-permute-start | bytes 786440 | tf_op jit(solution)/shard_map/ppermute | solution.py:534
  137.8 2.2 %collective-permute-start.19 = (bf16[2,256,512]{2,1,0:T(8,128)(2,1)}, bf16[2,256,512]{2,1,0:T(8,128)(2,1)S(1)}, u32[]{:S(2)}, u32[]{:S(2)}) collective-permute-start(bf16[2,256,512]{2,1,0:T(8,128)(2,1)} %get-tuple-element.11.refs_3_), channel_id=1, source_target_pairs={{0,8},{8,0},{1,9},{9,1},{2,10},{10,2},{3,11},{11,3},{4,12},{12,4},... | collective-permute-start | bytes 1572872 | tf_op jit(solution)/shard_map/ppermute | solution.py:530
  137.9 15.9 %collective-permute-start.18 = (bf16[4,64,1536]{2,1,0:T(8,128)(2,1)}, bf16[4,64,1536]{2,1,0:T(8,128)(2,1)S(1)}, u32[]{:S(2)}, u32[]{:S(2)}) collective-permute-start(bf16[4,64,1536]{2,1,0:T(8,128)(2,1)} %get-tuple-element.10.own_ref), channel_id=1, source_target_pairs={{0,8},{8,0},{1,9},{9,1},{2,10},{10,2},{3,11},{11,3},{4,12},{12,4},... | collective-permute-start | bytes 2359304 | tf_op jit(solution)/shard_map/ppermute | solution.py:530
  140.8 13.1 %copy-start.3 = (bf16[4,64,1536]{2,1,0:T(8,128)(2,1)S(1)}, bf16[4,64,1536]{2,1,0:T(8,128)(2,1)}, u32[]{:S(2)}) copy-start(bf16[4,64,1536]{2,1,0:T(8,128)(2,1)} %get-tuple-element.10.own_ref) | copy-start | bytes 2359300
  140.8 13.1 %copy-start.4 = (s32[4]{0:T(128)S(1)}, s32[4]{0:T(128)}, u32[]{:S(2)}) copy-start(s32[4]{0:T(128)} %pad_add_fusion.refs_0_.ids_ref) | copy-start | bytes 52
  140.8 13.1 %copy-start.5 = (s32[4]{0:T(128)S(1)}, s32[4]{0:T(128)}, u32[]{:S(2)}) copy-start(s32[4]{0:T(128)} %ancestors_ref.1) | copy-start | bytes 52
  148.0 12.6 %all-to-all-start.4 = ((f32[16,8,128]{2,1,0:T(8,128)}), f32[16,8,128]{2,1,0:T(8,128)S(1)}, u32[]{:S(2)}, u32[]{:S(2)}) async-start(f32[16,8,128]{2,1,0:T(8,128)} %reward.1), calls=%async_computation.4 | async-start | bytes 131072 | tf_op jit(solution)/shard_map/all_to_all | solution.py:667
  (13 other events, 28.4 us)
